TPU v7x, 32 devices: a whole 2x2x4 slice. The times are simulated.
32 devices in a mesh: groups: 1, chan: 16 (over z, y, x), quarter: 2 (over core).
Axes of the slice: x: 2, y: 2, z: 4, core: 2. Of those that a mesh axis runs over, the one named last changes fastest.
Arguments:
- pair: bfloat16 [384, 384, 128], P(('groups', 'chan', 'quarter')), may hold values from -6 to 6
- norm_gain: float32 [128], replicated, may hold values from 0.25 to 1.75
- norm_shift: float32 [128], replicated, may hold values from -3 to 3
- factor_weight: bfloat16 [128, 512], replicated, may hold values from -0.5 to 0.5
- factor_bias: float32 [512], replicated, may hold values from -3 to 3
- gate_weight: bfloat16 [128, 128], replicated, may hold values from -0.5 to 0.5
- gate_bias: float32 [128], replicated, may hold values from -3 to 3
- center_gain: float32 [128], replicated, may hold values from 0.25 to 1.75
- center_shift: float32 [128], replicated, may hold values from -3 to 3
- out_weight: bfloat16 [128, 128], replicated, may hold values from -0.5 to 0.5
- out_bias: float32 [128], replicated, may hold values from -3 to 3
Outputs:
- update: bfloat16 [384, 384, 128], P(('groups', 'chan', 'quarter'))
All inputs are finite; a program needn't handle non-finite values.
Results may differ from a plain program's by a relative error of at most 0.0057.
Values may be sent and summed in bfloat16 or wider, within the bound.
No kernel may reach another device: no remote copies, remote signals or barrier semaphores. Data moves between devices by JAX's collectives and lax.ppermute only.
A program may use at most 128 MiB of HBM per device.

v0:
```python
import jax
import jax.numpy as jnp
from jax import lax
from jax.sharding import PartitionSpec as P

epsilon = 1e-05


def normalize(values, gain, shift, axis):
    average = jnp.mean(values, axis=axis, keepdims=True)
    centered = values - average
    variance = jnp.mean(centered * centered, axis=axis, keepdims=True)
    return centered * lax.rsqrt(variance + epsilon) * gain + shift


def channel_products(left, piece):
    return jnp.einsum("cik,cjk->cij", left, piece, preferred_element_type=jnp.float32).astype(
        jnp.bfloat16
    )


def shards(
    pair,
    norm_gain,
    norm_shift,
    factor_weight,
    factor_bias,
    gate_weight,
    gate_bias,
    center_gain,
    center_shift,
    out_weight,
    out_bias,
):
    width = out_weight.shape[0]
    normed = normalize(pair.astype(jnp.float32), norm_gain, norm_shift, 2).astype(jnp.bfloat16)
    projected = (
        jnp.einsum("rjc,cf->rjf", normed, factor_weight, preferred_element_type=jnp.float32)
        + factor_bias
    )
    left = jax.nn.sigmoid(projected[:, :, :width]) * projected[:, :, width : 2 * width]
    right = jax.nn.sigmoid(projected[:, :, 2 * width : 3 * width]) * projected[:, :, 3 * width :]
    left = jnp.transpose(left, (2, 0, 1)).astype(jnp.bfloat16)
    right = jnp.transpose(right, (2, 0, 1)).astype(jnp.bfloat16)
    left_mine, right_mine = (
        lax.all_to_all(left, ("chan", "quarter"), split_axis=0, concat_axis=1, tiled=True),
        lax.all_to_all(right, ("chan", "quarter"), split_axis=0, concat_axis=1, tiled=True),
    )
    product = channel_products(left_mine, right_mine)
    returned = lax.all_to_all(product, ("chan", "quarter"), split_axis=1, concat_axis=0, tiled=True)
    gate = jax.nn.sigmoid(
        jnp.einsum("rjc,cd->rjd", normed, gate_weight, preferred_element_type=jnp.float32)
        + gate_bias
    )
    centered = normalize(
        returned.astype(jnp.float32), center_gain[:, None, None], center_shift[:, None, None], 0
    ).astype(jnp.bfloat16)
    outward = (
        jnp.einsum("crj,cd->rjd", centered, out_weight, preferred_element_type=jnp.float32)
        + out_bias
    )
    return (gate * outward).astype(jnp.bfloat16)


def solution(mesh):
    placed = (
        P(("groups", "chan", "quarter"), None, None),
        P(),
        P(),
        P(),
        P(),
        P(),
        P(),
        P(),
        P(),
        P(),
        P(),
    )
    return jax.shard_map(
        shards,
        mesh=mesh,
        in_specs=placed,
        out_specs=P(("groups", "chan", "quarter"), None, None),
        check_vma=False,
    )
```

profile of v0, /device:TPU:0, one launch (start us, length us, event | category | flops | bytes accessed | tf_op | source)
XLA Modules:
  0.0 143.0 jit_solution(15635873845326757957)
XLA Ops:
  0.0 0.0 copy-start
  0.0 0.0 copy-start.1
  0.0 0.0 copy-start.6
  0.0 0.0 copy-start.5
  0.0 0.0 copy-start.4
  0.0 1.8 %convert_reduce_fusion = f32[12,384]{1,0:T(8,128)S(1)} fusion(bf16[12,384,128]{2,1,0:T(8,128)(2,1)} %param.11), kind=kLoop, calls=%fused_computation.2 | loop fusion | flops 1175040 | bytes 1198080 | tf_op jit(solution)/shard_map/reduce_sum | solution.py:10
  1.8 2.5 %fusion.2 = f32[12,384]{1,0:T(8,128)S(1)} fusion(bf16[12,384,128]{2,1,0:T(8,128)(2,1)} %param.11, f32[12,384]{1,0:T(8,128)S(1)} %broadcast_multiply_fusion.1), kind=kLoop, calls=%fused_computation.5 | loop fusion | flops 2354688 | bytes 1216512 | tf_op jit(solution)/shard_map/reduce_sum | solution.py:12
  4.3 0.0 copy-done
  4.3 0.0 copy-done.1
  4.3 0.0 copy-done.6
  4.3 0.0 copy-done.5
  4.4 0.0 copy-done.4
  4.4 1.4 %broadcast_add_fusion = f32[12,384,512]{2,1,0:T(8,128)S(1)} fusion(f32[512]{0:T(512)S(1)} %copy-done.4, bf16[12,384,128]{2,1,0:T(8,128)(2,1)S(1)} %copy-done.1, f32[128]{0:T(128)S(1)} %copy-done.5, f32[128]{0:T(128)S(1)} %copy-done.6, f32[12,384]{1,0:T(8,128)S(1)} %add_rsqrt_fusion.1, f32[12,384]{1,0:T(8,128)S(1)} %broadcast_multiply_fusion.1, ...), kind=kOutput, calls=%fused_computation | convolution fusion | flops 609878016 | bytes 10787840 | tf_op jit(solution)/shard_map/rjc,cf->rjf/dot_general | solution.py:38
  5.8 2.2 %fusion.21 = (bf16[128,12,384]{0,2,1:T(8,128)(2,1)}, bf16[128,12,384]{0,2,1:T(8,128)(2,1)S(1)}) fusion(f32[12,384,512]{2,1,0:T(8,128)S(1)} %broadcast_add_fusion), kind=kLoop, calls=%fused_computation.33 | loop fusion | flops 5898240 | bytes 11796480 | tf_op jit(solution)/shard_map/convert_element_type | solution.py:43
  8.1 2.1 %copy.27 = bf16[128,12,384]{2,1,0:T(8,128)(2,1)} copy(bf16[128,12,384]{0,2,1:T(8,128)(2,1)S(1)} %get-tuple-element.6) | data formatting | bytes 2359296 | tf_op jit(solution)/shard_map/convert_element_type | solution.py:44
  10.1 7.3 %all-to-all-start.1 = ((bf16[128,12,384]{2,1,0:T(8,128)(2,1)}), bf16[128,12,384]{2,1,0:T(8,128)(2,1)S(1)}, u32[]{:S(2)}, u32[]{:S(2)}) async-start(bf16[128,12,384]{2,1,0:T(8,128)(2,1)} %copy.27), calls=%async_computation.1 | async-start | bytes 3145728 | tf_op jit(solution)/shard_map/all_to_all | solution.py:47
  17.4 3.0 %copy.24 = bf16[128,12,384]{2,1,0:T(8,128)(2,1)} copy(bf16[128,12,384]{0,2,1:T(8,128)(2,1)} %get-tuple-element.5) | data formatting | bytes 2359296 | tf_op jit(solution)/shard_map/convert_element_type | solution.py:43
  20.4 34.8 %all-to-all-done.1 = bf16[128,12,384]{2,1,0:T(8,128)(2,1)S(1)} async-done(((bf16[128,12,384]{2,1,0:T(8,128)(2,1)}), bf16[128,12,384]{2,1,0:T(8,128)(2,1)S(1)}, u32[]{:S(2)}, u32[]{:S(2)}) %all-to-all-start.1) | async-done | bytes 1179680 | tf_op jit(solution)/shard_map/all_to_all | solution.py:47
  55.2 3.9 %all-to-all-start = ((bf16[128,12,384]{2,1,0:T(8,128)(2,1)}), bf16[128,12,384]{2,1,0:T(8,128)(2,1)}, u32[]{:S(2)}, u32[]{:S(2)}) async-start(bf16[128,12,384]{2,1,0:T(8,128)(2,1)} %copy.24), calls=%async_computation | async-start | bytes 3145728 | tf_op jit(solution)/shard_map/all_to_all | solution.py:46
  59.1 1.5 %copy.39 = bf16[32,4,12,384]{3,1,2,0:T(4,128)(2,1)} copy(bf16[32,4,12,384]{3,2,1,0:T(8,128)(2,1)S(1)} %bitcast.36) | data formatting | bytes 2359296 | tf_op jit(solution)/shard_map/all_to_all | solution.py:47
  60.5 0.0 copy-start.2
  60.5 36.3 %all-to-all-done = bf16[128,12,384]{2,1,0:T(8,128)(2,1)} async-done(((bf16[128,12,384]{2,1,0:T(8,128)(2,1)}), bf16[128,12,384]{2,1,0:T(8,128)(2,1)}, u32[]{:S(2)}, u32[]{:S(2)}) %all-to-all-start) | async-done | bytes 1179680 | tf_op jit(solution)/shard_map/all_to_all | solution.py:46
  96.8 1.9 %copy.37 = bf16[32,4,12,384]{3,1,2,0:T(4,128)(2,1)S(1)} copy(bf16[32,4,12,384]{3,2,1,0:T(8,128)(2,1)} %bitcast.3) | data formatting | bytes 2359296 | tf_op jit(solution)/shard_map/all_to_all | solution.py:46
  98.7 0.0 copy-done.2
  98.7 0.9 convolution_convert_fusion
  99.6 0.0 copy-start.3
  99.6 1.9 %copy.32 = bf16[4,384,384]{2,0,1:T(4,128)(2,1)} copy(bf16[4,384,384]{2,1,0:T(8,128)(2,1)S(1)} %convolution_convert_fusion) | data formatting | bytes 2359296 | tf_op jit(solution)/shard_map/convert_element_type | solution.py:17
  101.6 3.9 %all-to-all-start.2 = ((bf16[4,384,384]{2,0,1:T(4,128)(2,1)}), bf16[4,384,384]{2,0,1:T(4,128)(2,1)S(1)}, u32[]{:S(2)}, u32[]{:S(2)}) async-start(bf16[4,384,384]{2,0,1:T(4,128)(2,1)} %copy.32), calls=%async_computation.2 | async-start | bytes 2359296 | tf_op jit(solution)/shard_map/all_to_all | solution.py:50
  105.5 0.0 copy-done.3
  105.5 3.0 %fusion.24 = f32[12,384,128]{2,1,0:T(8,128)} fusion(bf16[12,384,128]{2,1,0:T(8,128)(2,1)S(1)} %copy-done.1, f32[128]{0:T(128)S(1)} %copy-done.5, f32[128]{0:T(128)S(1)} %copy-done.6, f32[12,384]{1,0:T(8,128)S(1)} %add_rsqrt_fusion.1, f32[12,384]{1,0:T(8,128)S(1)} %broadcast_multiply_fusion.1, bf16[128,128]{1,0:T(8,128)(2,1)S(1)} %copy-done.3), kind=kOutput, calls=%fused_computation.35 | convolution fusion | flops 154533888 | bytes 3609600 | tf_op jit(solution)/shard_map/rjc,cd->rjd/dot_general | solution.py:52
  108.6 25.9 %all-to-all-done.2 = bf16[4,384,384]{2,0,1:T(4,128)(2,1)S(1)} async-done(((bf16[4,384,384]{2,0,1:T(4,128)(2,1)}), bf16[4,384,384]{2,0,1:T(4,128)(2,1)S(1)}, u32[]{:S(2)}, u32[]{:S(2)}) %all-to-all-start.2) | async-done | bytes 1179680 | tf_op jit(solution)/shard_map/all_to_all | solution.py:50
  134.4 0.5 fusion.14
  134.9 0.3 convert_bitcast_fusion
  135.2 0.8 multiply_reduce_fusion
  136.1 0.5 copy.33
  136.6 0.0 copy-start.7
  136.6 0.0 copy-start.8
  136.6 0.0 copy-start.9
  136.6 0.0 copy-start.10
  136.7 0.0 copy-start.11
  136.7 1.9 %reshape.37 = f32[128,12,384]{2,0,1:T(8,128)} reshape(f32[32,4,12,384]{3,1,0,2:T(4,128)S(1)} %copy.33) | data formatting | bytes 4718592 | tf_op jit(solution)/shard_map/convert_element_type | solution.py:56
  138.5 0.0 copy-done.7
  138.6 0.0 copy-done.8
  138.6 0.0 copy-done.9
  138.6 0.0 copy-done.10
  138.6 0.0 copy-done.11
  138.6 4.5 %multiply_convert_fusion = bf16[12,384,128]{2,1,0:T(8,128)(2,1)} fusion(f32[12,384,128]{2,1,0:T(8,128)} %fusion.24, f32[128,12,384]{2,0,1:T(8,128)} %reshape.37, f32[128]{0:T(128)S(1)} %copy-done.8, f32[128]{0:T(128)S(1)} %copy-done.9, f32[128]{0:T(128)S(1)} %copy-done.10, f32[12,384]{1,0:T(8,128)S(1)} %add_rsqrt_fusion, ...), kind=kOutput, calls=%fused_computation.22 | convolution fusion | flops 158072832 | bytes 5969920 | tf_op jit(solution)/shard_map/crj,cd->rjd/dot_general | solution.py:59
  (4 shorter events, 0.0 us)
Async XLA Ops:
  0.0 4.3 %copy-start = (bf16[128,512]{1,0:T(8,128)(2,1)S(1)}, bf16[128,512]{1,0:T(8,128)(2,1)}, u32[]{:S(2)}) copy-start(bf16[128,512]{1,0:T(8,128)(2,1)} %param.14) | copy-start | bytes 393220
  0.0 4.3 %copy-start.1 = (bf16[12,384,128]{2,1,0:T(8,128)(2,1)S(1)}, bf16[12,384,128]{2,1,0:T(8,128)(2,1)}, u32[]{:S(2)}) copy-start(bf16[12,384,128]{2,1,0:T(8,128)(2,1)} %param.11) | copy-start | bytes 3538948
  0.0 4.3 %copy-start.6 = (f32[128]{0:T(128)S(1)}, f32[128]{0:T(128)}, u32[]{:S(2)}) copy-start(f32[128]{0:T(128)} %param.12) | copy-start | bytes 1540
  0.0 4.3 %copy-start.5 = (f32[128]{0:T(128)S(1)}, f32[128]{0:T(128)}, u32[]{:S(2)}) copy-start(f32[128]{0:T(128)} %param.13) | copy-start | bytes 1540
  0.0 4.3 %copy-start.4 = (f32[512]{0:T(512)S(1)}, f32[512]{0:T(512)}, u32[]{:S(2)}) copy-start(f32[512]{0:T(512)} %param.15) | copy-start | bytes 6148
  10.1 45.1 %all-to-all-start.1 = ((bf16[128,12,384]{2,1,0:T(8,128)(2,1)}), bf16[128,12,384]{2,1,0:T(8,128)(2,1)S(1)}, u32[]{:S(2)}, u32[]{:S(2)}) async-start(bf16[128,12,384]{2,1,0:T(8,128)(2,1)} %copy.27), calls=%async_computation.1 | async-start | bytes 3145728 | tf_op jit(solution)/shard_map/all_to_all | solution.py:47
  55.2 41.6 %all-to-all-start = ((bf16[128,12,384]{2,1,0:T(8,128)(2,1)}), bf16[128,12,384]{2,1,0:T(8,128)(2,1)}, u32[]{:S(2)}, u32[]{:S(2)}) async-start(bf16[128,12,384]{2,1,0:T(8,128)(2,1)} %copy.24), calls=%async_computation | async-start | bytes 3145728 | tf_op jit(solution)/shard_map/all_to_all | solution.py:46
  60.5 38.1 %copy-start.2 = (bf16[32,4,12,384]{3,1,2,0:T(4,128)(2,1)S(1)}, bf16[32,4,12,384]{3,1,2,0:T(4,128)(2,1)}, u32[]{:S(2)}) copy-start(bf16[32,4,12,384]{3,1,2,0:T(4,128)(2,1)} %copy.39) | copy-start | bytes 3538948
  99.6 5.9 %copy-start.3 = (bf16[128,128]{1,0:T(8,128)(2,1)S(1)}, bf16[128,128]{1,0:T(8,128)(2,1)}, u32[]{:S(2)}) copy-start(bf16[128,128]{1,0:T(8,128)(2,1)} %param.16) | copy-start | bytes 98308
  101.6 32.9 %all-to-all-start.2 = ((bf16[4,384,384]{2,0,1:T(4,128)(2,1)}), bf16[4,384,384]{2,0,1:T(4,128)(2,1)S(1)}, u32[]{:S(2)}, u32[]{:S(2)}) async-start(bf16[4,384,384]{2,0,1:T(4,128)(2,1)} %copy.32), calls=%async_computation.2 | async-start | bytes 2359296 | tf_op jit(solution)/shard_map/all_to_all | solution.py:50
  136.6 1.9 %copy-start.7 = (bf16[128,128]{1,0:T(8,128)(2,1)S(1)}, bf16[128,128]{1,0:T(8,128)(2,1)}, u32[]{:S(2)}) copy-start(bf16[128,128]{1,0:T(8,128)(2,1)} %param.20) | copy-start | bytes 98308
  136.6 1.9 %copy-start.8 = (f32[128]{0:T(128)S(1)}, f32[128]{0:T(128)}, u32[]{:S(2)}) copy-start(f32[128]{0:T(128)} %param.21) | copy-start | bytes 1540
  136.6 1.9 %copy-start.9 = (f32[128]{0:T(128)S(1)}, f32[128]{0:T(128)}, u32[]{:S(2)}) copy-start(f32[128]{0:T(128)} %param.19) | copy-start | bytes 1540
  136.6 1.9 %copy-start.10 = (f32[128]{0:T(128)S(1)}, f32[128]{0:T(128)}, u32[]{:S(2)}) copy-start(f32[128]{0:T(128)} %param.18) | copy-start | bytes 1540
  136.7 1.9 %copy-start.11 = (f32[128]{0:T(128)S(1)}, f32[128]{0:T(128)}, u32[]{:S(2)}) copy-start(f32[128]{0:T(128)} %param.17) | copy-start | bytes 1540
where the time goes:
time: 143 us
  waiting for transfers between devices  96.9 us (68%)
  starting transfers between devices  15.1 us (11%)
  local copies, waits for them, and re-layouts  12.8 us (9%)
  matrix products  9.87 us (7%)
  other arithmetic  8.11 us (6%)
    all_to_all x1, waiting for transfers between devices, shards(): lax.all_to_all(left, ('chan', 'quarter'), split_axis=0, concat_axis=1, ti...  36.3 us
    all_to_all x1, waiting for transfers between devices, shards(): lax.all_to_all(right, ('chan', 'quarter'), split_axis=0, concat_axis=1, t...  34.8 us
    all_to_all x1, waiting for transfers between devices, shards(): lax.all_to_all(product, ('chan', 'quarter'), split_axis=1, concat_axis=0,...  25.9 us
    all_to_all x1, starting transfers between devices, shards(): lax.all_to_all(right, ('chan', 'quarter'), split_axis=0, concat_axis=1, t...  7.31 us
    dot_general x1, matrix products, shards(): jnp.einsum('crj,cd->rjd', centered, out_weight, preferred_element_type=jn...  4.45 us
    all_to_all x1, starting transfers between devices, shards(): lax.all_to_all(product, ('chan', 'quarter'), split_axis=1, concat_axis=0,...  3.95 us
    all_to_all x1, starting transfers between devices, shards(): lax.all_to_all(left, ('chan', 'quarter'), split_axis=0, concat_axis=1, ti...  3.89 us
    reduce_sum x2, other arithmetic, normalize(): variance = jnp.mean(centered * centered, axis=axis, keepdims=True)  3.29 us
  transfers between devices with their start and end apart: 3, of which 3 were waited for; matrix products, arithmetic and copies ran while one was open for 5% of the time, Pallas kernels for 0%

commit v1 on v0

v1 whole, which is shorter than its diff:
```python
import functools

import jax
import jax.numpy as jnp
from jax import lax
from jax.experimental import pallas as pl
from jax.experimental.pallas import tpu as pltpu
from jax.sharding import Mesh
from jax.sharding import PartitionSpec as P

epsilon = 1e-05
BLOCK = 8
PAIRED = 2
LANES = 128
VMEM = 48 * 1024 * 1024

f32, bf16 = jnp.float32, jnp.bfloat16


def sigmoid(x):
    return 0.5 * jnp.tanh(0.5 * x) + 0.5


def dot(a, b):
    return jnp.dot(a, b, preferred_element_type=f32)


def dot_nt(a, b):
    return lax.dot_general(a, b, (((1,), (1,)), ((), ())), preferred_element_type=f32)


def column(row):
    blocks = [
        jnp.broadcast_to(row[:, k : k + LANES], (LANES, LANES)).T
        for k in range(0, row.shape[1], LANES)
    ]
    return jnp.concatenate(blocks, axis=0) if len(blocks) > 1 else blocks[0]


def widen(col, width):
    return jnp.concatenate([col] * (width // LANES), axis=1)


def shuffle(groups, size):
    n = groups * size
    out = lax.broadcasted_iota(jnp.int32, (n, n), 0)
    row = lax.broadcasted_iota(jnp.int32, (n, n), 1)
    want = (out % size) * groups + out // size
    return jnp.where(want == row, 1.0, 0.0).astype(bf16)


def factor(normed, wt, bias):
    width = wt.shape[0] // 2
    lanes = normed.shape[0]
    gate = dot_nt(wt[:width], normed) + widen(bias[:width], lanes)
    value = dot_nt(wt[width:], normed) + widen(bias[width:], lanes)
    return sigmoid(gate) * value


def as_rows(values, k):
    hosts = values.shape[0] // BLOCK
    return jnp.concatenate(
        [values[:, r * k : (r + 1) * k].reshape(hosts, BLOCK, k) for r in range(PAIRED)], axis=1
    )


def right_kernel(pair_ref, gain_ref, shift_ref, w_ref, b_ref, right_ref, normed_ref, wt, bt):
    @pl.when(pl.program_id(0) == 0)
    def _():
        wt[...] = w_ref[...].T
        bt[...] = column(b_ref[...])

    k, width = pair_ref.shape[1:]
    x = pair_ref[...].astype(f32).reshape(PAIRED * k, width)
    centered = x - jnp.mean(x, axis=1, keepdims=True)
    variance = jnp.mean(centered * centered, axis=1, keepdims=True)
    normed = centered * lax.rsqrt(variance + epsilon) * gain_ref[...] + shift_ref[...]
    normed = normed.astype(bf16)
    normed_ref[...] = normed.reshape(PAIRED, k, width)
    out = as_rows(factor(normed, wt[...], bt[...]), k).astype(bf16)
    for p in range(right_ref.shape[0]):
        right_ref[p] = out


def left_kernel(normed_ref, w_ref, b_ref, gw_ref, gb_ref, left_ref, gate_ref, wt, bt):
    @pl.when(pl.program_id(0) == 0)
    def _():
        wt[...] = w_ref[...].T
        bt[...] = column(b_ref[...])

    k, width = normed_ref.shape[1:]
    normed = normed_ref[...].reshape(PAIRED * k, width)
    left_ref[...] = as_rows(factor(normed, wt[...], bt[...]), k).astype(bf16)
    gate = sigmoid(dot(normed, gw_ref[...]) + gb_ref[...])
    gate_ref[...] = gate.reshape(gate_ref.shape).astype(gate_ref.dtype)


def regroup(source, target, matrix, size):
    for s in range(source.shape[0] // (BLOCK * size)):
        rows = source[s * BLOCK * size : (s + 1) * BLOCK * size, :]
        moved = dot(matrix, rows).astype(bf16)
        for c in range(BLOCK):
            target[c, s * size : (s + 1) * size, :] = moved[c * size : (c + 1) * size]


def product_kernel(left_ref, right_ref, out_ref, left, right, held):
    size = 32
    matrix = shuffle(BLOCK, size)
    back = shuffle(size, BLOCK)

    @pl.when(pl.program_id(0) == 0)
    def _():
        regroup(left_ref, left, matrix, size)

    regroup(right_ref, right, matrix, size)
    for c in range(BLOCK):
        held[c] = dot_nt(left[c], right[c]).astype(bf16)
    for s in range(left.shape[1] // size):
        rows = jnp.concatenate([held[c, s * size : (s + 1) * size, :] for c in range(BLOCK)], axis=0)
        out_ref[s * BLOCK * size : (s + 1) * BLOCK * size, :] = dot(back, rows).astype(bf16)


def final_kernel(x_ref, gate_ref, g_ref, s_ref, w_ref, b_ref, out_ref, gt, st):
    @pl.when(pl.program_id(0) == 0)
    def _():
        gt[...] = column(g_ref[...])
        st[...] = column(s_ref[...])

    hosts, _, j = x_ref.shape
    width = hosts * BLOCK
    for r in range(PAIRED):
        x = x_ref[...].astype(f32)[:, r * BLOCK : (r + 1) * BLOCK].reshape(width, j)
        centered = x - jnp.mean(x, axis=0, keepdims=True)
        variance = jnp.mean(centered * centered, axis=0, keepdims=True)
        normed = centered * lax.rsqrt(variance + epsilon) * widen(gt[...], j) + widen(st[...], j)
        outward = dot(normed.T.astype(bf16), w_ref[...]) + b_ref[...]
        out_ref[r] = (gate_ref[r].astype(f32) * outward).astype(bf16)


def whole(shape):
    return pl.BlockSpec(shape, lambda s: (0,) * len(shape))


def params():
    return pltpu.CompilerParams(vmem_limit_bytes=VMEM)


def shards(parts, pair, norm_gain, norm_shift, factor_weight, factor_bias, gate_weight, gate_bias,
           center_gain, center_shift, out_weight, out_bias):
    rows, k, width = pair.shape
    hidden = out_weight.shape[0]
    hosts = hidden // BLOCK
    steps = rows // PAIRED
    tall = PAIRED * BLOCK
    in_part = ("chan", "quarter")
    row = lambda v: v.reshape(1, -1)
    row_block = pl.BlockSpec((PAIRED, k, width), lambda s: (s, 0, 0))

    right, normed = pl.pallas_call(
        right_kernel,
        grid=(steps,),
        in_specs=[
            row_block,
            whole((1, width)),
            whole((1, width)),
            pl.BlockSpec((width, 2 * hidden), lambda s: (0, 1)),
            pl.BlockSpec((1, 2 * hidden), lambda s: (0, 1)),
        ],
        out_specs=[
            pl.BlockSpec((parts, hosts, tall, k), lambda s: (0, 0, s, 0)),
            row_block,
        ],
        out_shape=[
            jax.ShapeDtypeStruct((parts, hosts, rows * BLOCK, k), bf16),
            jax.ShapeDtypeStruct(pair.shape, bf16),
        ],
        scratch_shapes=[pltpu.VMEM((2 * hidden, width), bf16), pltpu.VMEM((2 * hidden, LANES), f32)],
        compiler_params=params(),
        name="right_factor",
    )(pair, row(norm_gain), row(norm_shift), factor_weight, row(factor_bias))
    right = lax.all_to_all(
        right.reshape(parts * hosts, rows * BLOCK, k), ("part",) + in_part, 0, 0, tiled=True
    )

    left, gate = pl.pallas_call(
        left_kernel,
        grid=(steps,),
        in_specs=[
            row_block,
            pl.BlockSpec((width, 2 * hidden), lambda s: (0, 0)),
            pl.BlockSpec((1, 2 * hidden), lambda s: (0, 0)),
            whole((width, width)),
            whole((1, width)),
        ],
        out_specs=[pl.BlockSpec((hosts, tall, k), lambda s: (0, s, 0)), row_block],
        out_shape=[
            jax.ShapeDtypeStruct((hosts, rows * BLOCK, k), bf16),
            jax.ShapeDtypeStruct(pair.shape, bf16),
        ],
        scratch_shapes=[pltpu.VMEM((2 * hidden, width), bf16), pltpu.VMEM((2 * hidden, LANES), f32)],
        compiler_params=params(),
        name="left_factor",
    )(normed, factor_weight, row(factor_bias), gate_weight, row(gate_bias))
    left = lax.all_to_all(left, in_part, 0, 0, tiled=True)

    mine = hosts * rows
    full = parts * mine
    product = pl.pallas_call(
        product_kernel,
        grid=(full // LANES,),
        in_specs=[
            whole((mine * BLOCK, k)),
            pl.BlockSpec((LANES * BLOCK, k), lambda s: (s, 0)),
        ],
        out_specs=pl.BlockSpec((mine * BLOCK, LANES), lambda s: (0, s)),
        out_shape=jax.ShapeDtypeStruct((mine * BLOCK, full), bf16),
        scratch_shapes=[
            pltpu.VMEM((BLOCK, mine, k), bf16),
            pltpu.VMEM((BLOCK, LANES, k), bf16),
            pltpu.VMEM((BLOCK, mine, LANES), bf16),
        ],
        compiler_params=params(),
        name="products",
    )(left.reshape(mine * BLOCK, k), right.reshape(full * BLOCK, k))
    product = lax.all_to_all(product.reshape(hosts, rows * BLOCK, full), in_part, 0, 0, tiled=True)

    return pl.pallas_call(
        final_kernel,
        grid=(steps,),
        in_specs=[
            pl.BlockSpec((hosts, tall, full), lambda s: (0, s, 0)),
            row_block,
            whole((1, hidden)),
            whole((1, hidden)),
            whole((hidden, width)),
            whole((1, width)),
        ],
        out_specs=row_block,
        out_shape=jax.ShapeDtypeStruct(pair.shape, bf16),
        scratch_shapes=[pltpu.VMEM((hidden, LANES), f32), pltpu.VMEM((hidden, LANES), f32)],
        compiler_params=params(),
        name="update",
    )(product, gate, row(center_gain), row(center_shift), out_weight, row(out_bias))


def solution(mesh):
    groups, chan, quarter = (mesh.shape[a] for a in ("groups", "chan", "quarter"))
    near = 128 // BLOCK // quarter
    parts = chan // near
    split = Mesh(
        mesh.devices.reshape(groups, parts, near, quarter), ("groups", "part", "chan", "quarter")
    )
    rows = P(("groups", "part", "chan", "quarter"), None, None)
    return jax.shard_map(
        functools.partial(shards, parts),
        mesh=split,
        in_specs=(rows,) + (P(),) * 10,
        out_specs=rows,
        check_vma=False,
    )
```

time: 143 us -> 121 us (0.85)
  blocking collectives: 0 us -> 102 us
  waiting for transfers between devices: 96.9 us -> 0 us
  starting transfers between devices: 15.1 us -> 0 us
  Pallas kernels: 0 us -> 14.4 us
  matrix products: 9.87 us -> 0 us
  local copies, waits for them, and re-layouts: 12.8 us -> 4.21 us
  other arithmetic: 8.11 us -> 0 us
    all_to_all x0 -> x3, blocking collectives: none -> 102 us  [the longest x1 58.5 us: shards(): lax.all_to_all(right.reshape(parts * hosts, rows * BLOCK, k), ('part',) +...]
    all_to_all x3 -> x0, waiting for transfers between devices: 96.9 us -> none  [the longest x1 36.3 us: shards(): lax.all_to_all(left, ('chan', 'quarter'), split_axis=0, concat_axis=1, ti...]
    all_to_all x3 -> x0, starting transfers between devices: 15.1 us -> none  [the longest x1 7.31 us: shards(): lax.all_to_all(right, ('chan', 'quarter'), split_axis=0, concat_axis=1, t...]
    pallas_call x0 -> x4, Pallas kernels: none -> 14.4 us  [the longest x1 4.51 us: shards(): pl.pallas_call(product_kernel, grid=(full // LANES,), in_specs=[whole((mi...]
    dot_general x4 -> x0, matrix products: 9.87 us -> none  [the longest x1 4.45 us: shards(): jnp.einsum('crj,cd->rjd', centered, out_weight, preferred_element_type=jn...]
    convert_element_type x5 -> x0, local copies, waits for them, and re-layouts: 9.38 us -> none  [the longest x1 2.96 us: shards(): left = jnp.transpose(left, (2, 0, 1)).astype(jnp.bfloat16)]
    reduce_sum x4 -> x0, other arithmetic: 5.53 us -> none  [the longest x2 3.29 us: normalize(): variance = jnp.mean(centered * centered, axis=axis, keepdims=True)]
    unnamed x24, local copies, waits for them, and re-layouts: 0.06 us -> 4.21 us
  transfers between devices with their start and end apart: 3 -> 0, of which waited for: 3 -> 0; matrix products, arithmetic and copies ran while one was open for 5% -> 0% of each run, Pallas kernels for 0% -> 0%
where the time goes in v1:
time: 121 us
  blocking collectives  102 us (84%)
  Pallas kernels  14.4 us (12%)
  local copies, waits for them, and re-layouts  4.21 us (3%)
    all_to_all x1, blocking collectives, shards(): lax.all_to_all(right.reshape(parts * hosts, rows * BLOCK, k), ('part',) +...  58.5 us
    all_to_all x1, blocking collectives, shards(): left = lax.all_to_all(left, in_part, 0, 0, tiled=True)  23.7 us
    all_to_all x1, blocking collectives, shards(): lax.all_to_all(product.reshape(hosts, rows * BLOCK, full), in_part, 0, 0,...  20.3 us
    pallas_call x1, Pallas kernels, shards(): pl.pallas_call(product_kernel, grid=(full // LANES,), in_specs=[whole((mi...  4.51 us
    unnamed x24, local copies, waits for them, and re-layouts  4.21 us
    pallas_call x1, Pallas kernels, shards(): pl.pallas_call(final_kernel, grid=(steps,), in_specs=[pl.BlockSpec((hosts...  3.79 us
    pallas_call x1, Pallas kernels, shards(): pl.pallas_call(right_kernel, grid=(steps,), in_specs=[row_block, whole((1...  3.62 us
    pallas_call x1, Pallas kernels, shards(): pl.pallas_call(left_kernel, grid=(steps,), in_specs=[row_block, pl.BlockS...  2.45 us

profile of v1, /device:TPU:0, one launch (start us, length us, event | category | flops | bytes accessed | tf_op | source)
XLA Modules:
  0.0 121.1 jit_solution(11045399722503156249)
XLA Ops:
  0.0 0.0 copy-start.6
  0.0 0.0 copy-start
  0.0 1.3 %copy-done = bf16[12,384,128]{2,1,0:T(8,128)(2,1)S(1)} copy-done((bf16[12,384,128]{2,1,0:T(8,128)(2,1)S(1)}, bf16[12,384,128]{2,1,0:T(8,128)(2,1)}, u32[]{:S(2)}) %copy-start) | copy-done | bytes 1179672
  1.3 0.0 copy-start.1
  1.3 0.9 copy-done.1
  2.2 0.0 copy-start.5
  2.2 0.7 copy-done.5
  2.9 0.0 copy-start.7
  2.9 0.7 copy-done.7
  3.5 0.0 copy-start.8
  3.5 0.7 copy-done.8
  4.2 0.0 copy-start.2
  4.2 0.0 copy-start.4
  4.2 3.6 %right_factor.1 = (bf16[2,16,96,384]{3,2,1,0:T(8,128)(2,1)S(1)}, bf16[12,384,128]{2,1,0:T(8,128)(2,1)S(1)}) custom-call(bf16[12,384,128]{2,1,0:T(8,128)(2,1)S(1)} %copy-done, f32[1,128]{1,0:T(1,128)S(1)} %bitcast.18, f32[1,128]{1,0:T(1,128)S(1)} %bitcast.19, bf16[128,512]{1,0:T(8,128)(2,1)S(1)} %copy-done.1, f32[1,512]{1,0:T(1,128)S(1)} %bitcast.15), custom_call_target="tpu_custom_call" | custom-call | tf_op jit(solution)/shard_map/right_factor/pallas_call | solution.py:159
  7.8 0.0 copy-done.6
  7.8 0.0 copy-done.2
  7.8 0.0 copy-done.4
  7.8 2.5 %left_factor.1 = (bf16[16,96,384]{2,1,0:T(8,128)(2,1)S(1)}, bf16[12,384,128]{2,1,0:T(8,128)(2,1)S(1)}) custom-call(bf16[12,384,128]{2,1,0:T(8,128)(2,1)S(1)} %get-tuple-element.9.normed_ref, bf16[128,512]{1,0:T(8,128)(2,1)S(1)} %copy-done.2, f32[1,512]{1,0:T(1,128)S(1)} %bitcast.16, bf16[128,128]{1,0:T(8,128)(2,1)S(1)} %copy-done.4, f32[1,128]{1,0:T(1,128)S(1)} %bitcast.17), custom_call_target="tpu_custom_call" | custom-call | tf_op jit(solution)/shard_map/left_factor/pallas_call | solution.py:185
  10.3 23.7 %all_to_all.15 = bf16[16,96,384]{2,1,0:T(8,128)(2,1)S(1)} all-to-all(bf16[16,96,384]{2,1,0:T(8,128)(2,1)S(1)} %get-tuple-element.10), channel_id=1, replica_groups=mesh['groups'=1,'part'=2,'chan'=8,'quarter'=2] {'chan','quarter'}, dimensions={0} | all-to-all | bytes 2359296 | tf_op jit(solution)/shard_map/all_to_all | solution.py:204
  34.0 58.5 %all_to_all.16 = bf16[32,96,384]{2,1,0:T(8,128)(2,1)S(1)} all-to-all(bf16[32,96,384]{2,1,0:T(8,128)(2,1)S(1)} %bitcast.14), channel_id=1, replica_groups=mesh['groups'=1,'part'=2,'chan'=8,'quarter'=2] {'part','chan','quarter'}, dimensions={0} | all-to-all | bytes 4718592 | tf_op jit(solution)/shard_map/all_to_all | solution.py:181
  92.4 4.5 %products.1 = bf16[1536,384]{1,0:T(8,128)(2,1)S(1)} custom-call(bf16[1536,384]{1,0:T(8,128)(2,1)S(1)} %bitcast.12, bf16[3072,384]{1,0:T(8,128)(2,1)S(1)} %bitcast.11), custom_call_target="tpu_custom_call" | custom-call | tf_op jit(solution)/shard_map/products/pallas_call | solution.py:208
  97.0 0.0 copy-start.3
  97.0 0.0 copy-start.9
  97.0 0.0 copy-start.10
  97.0 0.0 copy-start.11
  97.0 20.3 %all_to_all.17.x_ref = bf16[16,96,384]{2,1,0:T(8,128)(2,1)S(1)} all-to-all(bf16[16,96,384]{2,1,0:T(8,128)(2,1)S(1)} %bitcast.13), channel_id=1, replica_groups=mesh['groups'=1,'part'=2,'chan'=8,'quarter'=2] {'chan','quarter'}, dimensions={0} | all-to-all | bytes 2359296 | tf_op jit(solution)/shard_map/all_to_all | solution.py:225
  117.3 0.0 copy-done.3
  117.3 0.0 copy-done.9
  117.3 0.0 copy-done.10
  117.3 0.0 copy-done.11
  117.3 3.8 %update.1 = bf16[12,384,128]{2,1,0:T(8,128)(2,1)} custom-call(bf16[16,96,384]{2,1,0:T(8,128)(2,1)S(1)} %all_to_all.17.x_ref, bf16[12,384,128]{2,1,0:T(8,128)(2,1)S(1)} %get-tuple-element.12.gate_ref, f32[1,128]{1,0:T(1,128)S(1)} %bitcast.20, f32[1,128]{1,0:T(1,128)S(1)} %bitcast.21, bf16[128,128]{1,0:T(8,128)(2,1)S(1)} %copy-done.3, f32[1,128]{1,0:T(1,128)S(1)} %bitcast.22), custom_call_target="tpu_custom_call" | custom-call | tf_op jit(solution)/shard_map/update/pallas_call | solution.py:227
Async XLA Ops:
  0.0 7.8 %copy-start.6 = (f32[128]{0:T(128)S(1)}, f32[128]{0:T(128)}, u32[]{:S(2)}) copy-start(f32[128]{0:T(128)} %param.17) | copy-start | bytes 1540
  0.0 1.3 %copy-start = (bf16[12,384,128]{2,1,0:T(8,128)(2,1)S(1)}, bf16[12,384,128]{2,1,0:T(8,128)(2,1)}, u32[]{:S(2)}) copy-start(bf16[12,384,128]{2,1,0:T(8,128)(2,1)} %pair_ref.1) | copy-start | bytes 3538948
  1.3 0.9 copy-start.1
  2.2 0.7 copy-start.5
  2.9 0.7 copy-start.7
  3.5 0.7 copy-start.8
  4.2 3.6 %copy-start.2 = (bf16[128,512]{1,0:T(8,128)(2,1)S(1)}, bf16[128,512]{1,0:T(8,128)(2,1)}, u32[]{:S(2)}) copy-start(bf16[128,512]{1,0:T(8,128)(2,1)} %w_ref.4) | copy-start | bytes 393220
  4.2 3.7 %copy-start.4 = (bf16[128,128]{1,0:T(8,128)(2,1)S(1)}, bf16[128,128]{1,0:T(8,128)(2,1)}, u32[]{:S(2)}) copy-start(bf16[128,128]{1,0:T(8,128)(2,1)} %gw_ref.1) | copy-start | bytes 98308
  97.0 20.3 %copy-start.3 = (bf16[128,128]{1,0:T(8,128)(2,1)S(1)}, bf16[128,128]{1,0:T(8,128)(2,1)}, u32[]{:S(2)}) copy-start(bf16[128,128]{1,0:T(8,128)(2,1)} %w_ref.5) | copy-start | bytes 98308
  97.0 20.3 %copy-start.9 = (f32[128]{0:T(128)S(1)}, f32[128]{0:T(128)}, u32[]{:S(2)}) copy-start(f32[128]{0:T(128)} %param.18) | copy-start | bytes 1540
  97.0 20.3 %copy-start.10 = (f32[128]{0:T(128)S(1)}, f32[128]{0:T(128)}, u32[]{:S(2)}) copy-start(f32[128]{0:T(128)} %param.19) | copy-start | bytes 1540
  97.0 20.3 %copy-start.11 = (f32[128]{0:T(128)S(1)}, f32[128]{0:T(128)}, u32[]{:S(2)}) copy-start(f32[128]{0:T(128)} %param.21) | copy-start | bytes 1540

commit v2 on v1

v2 whole, which is shorter than its diff:
```python
import functools

import jax
import jax.numpy as jnp
from jax import lax
from jax.experimental import pallas as pl
from jax.experimental.pallas import tpu as pltpu
from jax.sharding import Mesh
from jax.sharding import PartitionSpec as P

epsilon = 1e-05
CHANNELS = 128
BLOCK = 8
STEP = 4
SIZE = 32
LANES = 128
TAIL = 64
MIB = 1024 * 1024

f32, bf16 = jnp.float32, jnp.bfloat16


def sigmoid(x):
    return 0.5 * jnp.tanh(0.5 * x) + 0.5


def dot(a, b):
    return jnp.dot(a, b, preferred_element_type=f32)


def dot_nt(a, b):
    return lax.dot_general(a, b, (((1,), (1,)), ((), ())), preferred_element_type=f32)


def column(row):
    blocks = [
        jnp.broadcast_to(row[:, k : k + LANES], (LANES, LANES)).T
        for k in range(0, row.shape[1], LANES)
    ]
    return jnp.concatenate(blocks, axis=0)


def widen(col, width):
    return jnp.concatenate([col] * (width // LANES), axis=1)


def shuffle(groups, size):
    n = groups * size
    out = lax.broadcasted_iota(jnp.int32, (n, n), 0)
    row = lax.broadcasted_iota(jnp.int32, (n, n), 1)
    want = (out % size) * groups + out // size
    return jnp.where(want == row, 1.0, 0.0).astype(bf16)


def normalize(x, gain, shift):
    centered = x - jnp.mean(x, axis=1, keepdims=True)
    variance = jnp.mean(centered * centered, axis=1, keepdims=True)
    return (centered * lax.rsqrt(variance + epsilon) * gain + shift).astype(bf16)


def factor(normed, wt, bias):
    width = wt.shape[0] // 2
    lanes = normed.shape[0]
    gate = dot_nt(wt[:width], normed) + widen(bias[:width], lanes)
    value = dot_nt(wt[width:], normed) + widen(bias[width:], lanes)
    return sigmoid(gate) * value


def as_rows(values, k):
    hosts = values.shape[0] // BLOCK
    return jnp.concatenate(
        [values[:, r * k : (r + 1) * k].reshape(hosts, BLOCK, k) for r in range(STEP)], axis=1
    )


def right_kernel(pair_ref, gain_ref, shift_ref, w_ref, b_ref, *refs):
    wf, bf, wt, bt = refs[-4:]
    normed_ref = refs[-5]
    outs = refs[:-5]
    k, width = pair_ref.shape[1:]
    hidden = w_ref.shape[1] // 2

    @pl.when(pl.program_id(0) == 0)
    def _():
        wf[...] = w_ref[...].astype(f32).T
        bf[...] = column(b_ref[...])
        host = lax.axis_index(("chan", "quarter"))
        for half in range(2):
            for b in range(0, len(outs), 2):
                source = [
                    pl.ds(pl.multiple_of(half * hidden + (host ^ (b + n)) * BLOCK, BLOCK), BLOCK)
                    for n in range(2)
                ]
                target = slice(half * hidden + b * BLOCK, half * hidden + (b + 2) * BLOCK)
                wt[target] = jnp.concatenate([wf[s] for s in source], axis=0).astype(bf16)
                bt[target] = jnp.concatenate([bf[s] for s in source], axis=0)

    x = pair_ref[...].astype(f32).reshape(STEP * k, width)
    normed = normalize(x, gain_ref[...], shift_ref[...])
    normed_ref[...] = normed.reshape(STEP, k, width)
    rows = as_rows(factor(normed, wt[...], bt[...]), k).astype(bf16)
    for b, out in enumerate(outs):
        out[...] = rows[b]


def left_kernel(normed_ref, w_ref, b_ref, left_ref, wt, bt):
    @pl.when(pl.program_id(0) == 0)
    def _():
        wt[...] = w_ref[...].astype(f32).T.astype(bf16)
        bt[...] = column(b_ref[...])

    k, width = normed_ref.shape[1:]
    normed = normed_ref[...].reshape(STEP * k, width)
    left_ref[...] = as_rows(factor(normed, wt[...], bt[...]), k).astype(bf16)


def gate_kernel(normed_ref, gw_ref, gb_ref, gate_ref):
    k, width = normed_ref.shape[1:]
    normed = normed_ref[...].reshape(STEP * k, width)
    gate = sigmoid(dot(normed, gw_ref[...]) + gb_ref[...])
    gate_ref[...] = gate.reshape(gate_ref.shape).astype(gate_ref.dtype)


def regroup(source, target, matrix):
    for s in range(source.shape[0] // (BLOCK * SIZE)):
        rows = source[s * BLOCK * SIZE : (s + 1) * BLOCK * SIZE, :]
        moved = dot(matrix, rows).astype(bf16)
        for c in range(BLOCK):
            target[c, s * SIZE : (s + 1) * SIZE, :] = moved[c * SIZE : (c + 1) * SIZE]


def product_kernel(hosts, left_ref, *refs):
    rights = refs[:hosts]
    out_ref, arrived, left, right, held, sems = refs[hosts:]
    tall = rights[0].shape[0]
    rows = tall // BLOCK
    host = lax.axis_index(("chan", "quarter"))
    copies = []
    for b, ref in enumerate(rights):
        start = pl.multiple_of((host ^ b) * tall, 16)
        copies.append(pltpu.make_async_copy(ref, arrived.at[pl.ds(start, tall)], sems.at[b]))
        copies[-1].start()
    matrix = shuffle(BLOCK, SIZE)
    back = shuffle(SIZE, BLOCK)
    regroup(left_ref, left, matrix)
    for copy in copies:
        copy.wait()
    regroup(arrived, right, matrix)
    for c in range(BLOCK):
        held[c] = dot_nt(left[c], right[c]).astype(bf16)
    span = held.shape[2]
    main = span - TAIL
    for s in range(left.shape[1] // SIZE):
        parts = jnp.concatenate([held[c, s * SIZE : (s + 1) * SIZE, :] for c in range(BLOCK)], axis=0)
        moved = dot(back, parts)
        ends = moved[:, main:].reshape(SIZE // 2, 2, BLOCK, TAIL)
        ends = jnp.concatenate([ends[:, 0], ends[:, 1]], axis=2).reshape(SIZE * BLOCK // 2, LANES)
        moved, ends = moved[:, :main].astype(bf16), ends.astype(bf16)
        for i in range(0, SIZE, STEP):
            to, at = divmod(s * SIZE + i, rows)
            out_ref[to, at * BLOCK : (at + STEP) * BLOCK, :] = moved[i * BLOCK : (i + STEP) * BLOCK]
            low = tall + at * BLOCK // 2
            out_ref[to, low : low + STEP * BLOCK // 2, :] = ends[
                i * BLOCK // 2 : (i + STEP) * BLOCK // 2
            ]


def final_kernel(parts, *refs):
    products = refs[:parts]
    gate_ref, g_ref, s_ref, w_ref, b_ref, out_ref, gt, st = refs[parts:]
    step = pl.program_id(0)

    @pl.when(step == 0)
    def _():
        gt[...] = column(g_ref[...])
        st[...] = column(s_ref[...])

    part = lax.axis_index("part")
    hosts, tall, _ = products[0].shape
    tall = tall * 2 // 3
    span = gate_ref.shape[1] // parts
    main = span - TAIL
    width = hosts * BLOCK
    for a, ref in enumerate(products):
        first = pl.multiple_of(lax.rem(part + parts - a, parts) * span, 16)
        whole = ref[:, pl.ds(pl.multiple_of(step * STEP * BLOCK, 16), STEP * BLOCK), :].astype(f32)
        low = pl.multiple_of(tall + step * (STEP * BLOCK // 2), 16)
        ends = ref[:, pl.ds(low, STEP * BLOCK // 2), :].astype(f32)
        blocks = [whole[:, r * BLOCK : (r + 1) * BLOCK].reshape(width, LANES) for r in range(STEP)]
        blocks += [
            ends[:, r * BLOCK : (r + 1) * BLOCK].reshape(width, LANES) for r in range(STEP // 2)
        ]
        x = jnp.concatenate(blocks, axis=1)
        centered = x - jnp.mean(x, axis=0, keepdims=True)
        variance = jnp.mean(centered * centered, axis=0, keepdims=True)
        normed = centered * lax.rsqrt(variance + epsilon)
        normed = normed * widen(gt[...], x.shape[1]) + widen(st[...], x.shape[1])
        outward = dot(normed.T.astype(bf16), w_ref[...]) + b_ref[...]
        for r in range(STEP):
            at = pl.ds(first, main)
            value = outward[r * LANES : (r + 1) * LANES]
            out_ref[r, at, :] = (gate_ref[r, at, :].astype(f32) * value).astype(bf16)
            at = pl.ds(pl.multiple_of(first + main, 16), TAIL)
            low = STEP * LANES + r * TAIL
            value = outward[low : low + TAIL]
            out_ref[r, at, :] = (gate_ref[r, at, :].astype(f32) * value).astype(bf16)


def whole(shape):
    return pl.BlockSpec(shape, lambda s: (0,) * len(shape))


def cost(flops, size):
    return pl.CostEstimate(flops=flops, bytes_accessed=size, transcendentals=0)


def params(mib=32):
    return pltpu.CompilerParams(vmem_limit_bytes=mib * MIB)


def shards(parts, pair, norm_gain, norm_shift, factor_weight, factor_bias, gate_weight, gate_bias,
           center_gain, center_shift, out_weight, out_bias):
    rows, k, width = pair.shape
    hidden = out_weight.shape[0]
    hosts = hidden // BLOCK
    steps = rows // STEP
    tall = rows * BLOCK
    mine = hosts * rows
    in_part = ("chan", "quarter")
    everywhere = ("part",) + in_part
    row = lambda v: v.reshape(1, -1)
    row_block = pl.BlockSpec((STEP, k, width), lambda s: (s, 0, 0))
    factor_block = lambda n: [
        pl.BlockSpec((width, 2 * hidden), lambda s: (0, n)),
        pl.BlockSpec((1, 2 * hidden), lambda s: (0, n)),
    ]
    work = rows * k * width

    *rights, normed = pl.pallas_call(
        right_kernel,
        grid=(steps,),
        in_specs=[row_block, whole((1, width)), whole((1, width))] + factor_block(1),
        out_specs=[pl.BlockSpec((STEP * BLOCK, k), lambda s: (s, 0))] * hosts + [row_block],
        out_shape=[jax.ShapeDtypeStruct((tall, k), bf16)] * hosts
        + [jax.ShapeDtypeStruct(pair.shape, bf16)],
        scratch_shapes=[
            pltpu.VMEM((2 * hidden, width), f32),
            pltpu.VMEM((2 * hidden, LANES), f32),
            pltpu.VMEM((2 * hidden, width), bf16),
            pltpu.VMEM((2 * hidden, LANES), f32),
        ],
        compiler_params=params(60),
        cost_estimate=cost(4 * work * hidden, 6 * work),
        name="right_factor",
    )(pair, row(norm_gain), row(norm_shift), factor_weight, row(factor_bias))

    def send(a, b):
        if a == 0 and b == 0:
            return rights[0]
        pairs = [
            (p * hosts + h, (p + a) % parts * hosts + (h ^ b))
            for p in range(parts)
            for h in range(hosts)
        ]
        return lax.ppermute(rights[b], everywhere, pairs)

    arrived = {}
    order = [(a, b) for b in range(hosts) for a in range(parts)]
    for a, b in order:
        arrived[a, b] = send(a, b)

    left = pl.pallas_call(
        left_kernel,
        grid=(steps,),
        in_specs=[row_block] + factor_block(0),
        out_specs=pl.BlockSpec((hosts, STEP * BLOCK, k), lambda s: (0, s, 0)),
        out_shape=jax.ShapeDtypeStruct((hosts, tall, k), bf16),
        scratch_shapes=[pltpu.VMEM((2 * hidden, width), bf16), pltpu.VMEM((2 * hidden, LANES), f32)],
        compiler_params=params(),
        cost_estimate=cost(4 * work * hidden, 4 * work),
        name="left_factor",
    )(normed, factor_weight, row(factor_bias))
    left = lax.all_to_all(left, in_part, 0, 0, tiled=True).reshape(mine * BLOCK, k)

    gate = pl.pallas_call(
        gate_kernel,
        grid=(steps,),
        in_specs=[row_block, whole((width, width)), whole((1, width))],
        out_specs=row_block,
        out_shape=jax.ShapeDtypeStruct(pair.shape, bf16),
        compiler_params=params(),
        cost_estimate=cost(2 * work * width, 4 * work),
        name="gate",
    )(normed, gate_weight, row(gate_bias))

    products = []
    for a in range(parts):
        product = pl.pallas_call(
            functools.partial(product_kernel, hosts),
            in_specs=[pl.BlockSpec(memory_space=pltpu.VMEM)]
            + [pl.BlockSpec(memory_space=pl.ANY)] * hosts,
            out_specs=pl.BlockSpec(memory_space=pltpu.VMEM),
            out_shape=jax.ShapeDtypeStruct((hosts, tall * 3 // 2, LANES), bf16),
            scratch_shapes=[
                pltpu.VMEM((mine * BLOCK, k), bf16),
                pltpu.VMEM((BLOCK, mine, k), bf16),
                pltpu.VMEM((BLOCK, mine, k), bf16),
                pltpu.VMEM((BLOCK, mine, mine), bf16),
                pltpu.SemaphoreType.DMA((hosts,)),
            ],
            compiler_params=params(),
            cost_estimate=cost(2 * BLOCK * mine * mine * k, 6 * BLOCK * mine * k),
            name="products",
        )(left, *[arrived[a, b] for b in range(hosts)])
        products.append(lax.all_to_all(product, in_part, 0, 0, tiled=True))

    return pl.pallas_call(
        functools.partial(final_kernel, parts),
        grid=(steps,),
        in_specs=[whole(products[0].shape)] * parts
        + [row_block, whole((1, hidden)), whole((1, hidden)), whole((hidden, width)), whole((1, width))],
        out_specs=row_block,
        out_shape=jax.ShapeDtypeStruct(pair.shape, bf16),
        scratch_shapes=[pltpu.VMEM((hidden, LANES), f32), pltpu.VMEM((hidden, LANES), f32)],
        compiler_params=params(),
        cost_estimate=cost(2 * work * width, 6 * work),
        name="update",
    )(*products, gate, row(center_gain), row(center_shift), out_weight, row(out_bias))


def solution(mesh):
    groups, chan, quarter = (mesh.shape[a] for a in ("groups", "chan", "quarter"))
    near = CHANNELS // BLOCK // quarter
    parts = chan // near
    split = Mesh(
        mesh.devices.reshape(groups, parts, near, quarter), ("groups", "part", "chan", "quarter")
    )
    rows = P(("groups", "part", "chan", "quarter"), None, None)
    return jax.shard_map(
        functools.partial(shards, parts),
        mesh=split,
        in_specs=(rows,) + (P(),) * 10,
        out_specs=rows,
        check_vma=False,
    )
```

time: 121 us -> 141 us (1.17)
  blocking collectives: 102 us -> 0 us
  starting transfers between devices: 0 us -> 77.8 us
  waiting for transfers between devices: 0 us -> 38.6 us
  Pallas kernels: 14.4 us -> 20.3 us
    all_to_all x3 -> x0, blocking collectives: 102 us -> none  [the longest x1 58.5 us: shards(): lax.all_to_all(right.reshape(parts * hosts, rows * BLOCK, k), ('part',) +...]
    ppermute x0 -> x31, starting transfers between devices: none -> 59.6 us  [send(): return lax.ppermute(rights[b], everywhere, pairs)]
    ppermute x0 -> x31, waiting for transfers between devices: none -> 29.1 us  [send(): return lax.ppermute(rights[b], everywhere, pairs)]
    all_to_all x0 -> x3, starting transfers between devices: none -> 18.2 us  [the longest x2 11.7 us: shards(): products.append(lax.all_to_all(product, in_part, 0, 0, tiled=True))]
    all_to_all x0 -> x3, waiting for transfers between devices: none -> 9.55 us  [the longest x2 9.55 us: shards(): products.append(lax.all_to_all(product, in_part, 0, 0, tiled=True))]
    pallas_call x3 -> x5, Pallas kernels: 10.8 us -> 15.4 us  [the longest x2 9.28 us: shards(): pl.pallas_call(functools.partial(product_kernel, hosts), in_specs=[pl.Blo...]
    unnamed x24 -> x66, local copies, waits for them, and re-layouts: 4.21 us -> 2.9 us
  transfers between devices with their start and end apart: 0 -> 34, of which waited for: 0 -> 11; matrix products, arithmetic and copies ran while one was open for 0% -> 0% of each run, Pallas kernels for 0% -> 4%
where the time goes in v2:
time: 141 us; the launch traced here: 140 us
  starting transfers between devices  77.8 us (55%)
  waiting for transfers between devices  38.6 us (27%)
  Pallas kernels  20.3 us (14%)
  local copies, waits for them, and re-layouts  2.9 us (2%)
    ppermute x31, starting transfers between devices, send(): return lax.ppermute(rights[b], everywhere, pairs)  59.6 us
    ppermute x31, waiting for transfers between devices, send(): return lax.ppermute(rights[b], everywhere, pairs)  29.1 us
    all_to_all x2, starting transfers between devices, shards(): products.append(lax.all_to_all(product, in_part, 0, 0, tiled=True))  11.7 us
    all_to_all x2, waiting for transfers between devices, shards(): products.append(lax.all_to_all(product, in_part, 0, 0, tiled=True))  9.55 us
    pallas_call x2, Pallas kernels, shards(): pl.pallas_call(functools.partial(product_kernel, hosts), in_specs=[pl.Blo...  9.28 us
    all_to_all x1, starting transfers between devices, shards(): lax.all_to_all(left, in_part, 0, 0, tiled=True).reshape(mine * BLOCK, k)  6.42 us
    pallas_call x1, Pallas kernels, shards(): pl.pallas_call(right_kernel, grid=(steps,), in_specs=[row_block, whole((1...  4.98 us
    unnamed x66, local copies, waits for them, and re-layouts  2.9 us
  transfers between devices with their start and end apart: 34, of which 11 were waited for; matrix products, arithmetic and copies ran while one was open for 0% of the time, Pallas kernels for 4%

profile of v2, /device:TPU:0, one launch (start us, length us, event | category | flops | bytes accessed | tf_op | source)
XLA Modules:
  0.0 140.0 jit_solution(13384375103484011090)
XLA Ops:
  0.0 5.0 %right_factor.1 = (bf16[96,384]{1,0:T(8,128)(2,1)}, bf16[96,384]{1,0:T(8,128)(2,1)}, bf16[96,384]{1,0:T(8,128)(2,1)}, bf16[96,384]{1,0:T(8,128)(2,1)}, bf16[96,3...) custom-call(bf16[12,384,128]{2,1,0:T(8,128)(2,1)} %pair_ref.1, ...), custom_call_target="tpu_custom_call" | custom-call | flops 301989888 | bytes 3538944 | tf_op jit(solution)/shard_map/right_factor/pallas_call | solution.py:239
  5.0 1.3 copy-done
  6.3 2.5 %left_factor.1 = bf16[16,96,384]{2,1,0:T(8,128)(2,1)} custom-call(bf16[12,384,128]{2,1,0:T(8,128)(2,1)S(1)} %copy-done, bf16[128,512]{1,0:T(8,128)(2,1)S(1)} %copy-done.2, f32[1,512]{1,0:T(1,128)S(1)} %bitcast.11), custom_call_target="tpu_custom_call" | custom-call | flops 301989888 | bytes 2359296 | tf_op jit(solution)/shard_map/left_factor/pallas_call | solution.py:272
  8.9 6.4 %all-to-all-start = ((bf16[16,96,384]{2,1,0:T(8,128)(2,1)}), bf16[16,96,384]{2,1,0:T(8,128)(2,1)S(1)}, u32[]{:S(2)}, u32[]{:S(2)}) async-start(bf16[16,96,384]{2,1,0:T(8,128)(2,1)} %left_factor.1), calls=%async_computation | async-start | bytes 2359296 | tf_op jit(solution)/shard_map/all_to_all | solution.py:283
  15.4 0.5 collective-permute-start
  15.8 1.7 %collective-permute-start.1 = (bf16[96,384]{1,0:T(8,128)(2,1)S(1)}, bf16[96,384]{1,0:T(8,128)(2,1)S(1)}, u32[]{:S(2)}, u32[]{:S(2)}) collective-permute-start(bf16[96,384]{1,0:T(8,128)(2,1)S(1)} %copy-done.29), channel_id=1, source_target_pairs={{0,2},{1,3},{2,0},{3,1},{4,6},{5,7},{6,4},{7,5},{8,10},{9,11},{10,... | collective-permute-start | bytes 221192 | tf_op jit(solution)/shard_map/ppermute | solution.py:265
  17.5 1.7 %collective-permute-start.3 = (bf16[96,384]{1,0:T(8,128)(2,1)S(1)}, bf16[96,384]{1,0:T(8,128)(2,1)S(1)}, u32[]{:S(2)}, u32[]{:S(2)}) collective-permute-start(bf16[96,384]{1,0:T(8,128)(2,1)S(1)} %copy-done.25), channel_id=1, source_target_pairs={{0,4},{1,5},{2,6},{3,7},{4,0},{5,1},{6,2},{7,3},{8,12},{9,13},{10,... | collective-permute-start | bytes 221192 | tf_op jit(solution)/shard_map/ppermute | solution.py:265
  19.3 2.6 %collective-permute-start.5 = (bf16[96,384]{1,0:T(8,128)(2,1)S(1)}, bf16[96,384]{1,0:T(8,128)(2,1)S(1)}, u32[]{:S(2)}, u32[]{:S(2)}) collective-permute-start(bf16[96,384]{1,0:T(8,128)(2,1)S(1)} %copy-done.21), channel_id=1, source_target_pairs={{0,6},{1,7},{2,4},{3,5},{4,2},{5,3},{6,0},{7,1},{8,14},{9,15},{10,... | collective-permute-start | bytes 221192 | tf_op jit(solution)/shard_map/ppermute | solution.py:265
  21.9 12.8 %collective-permute-done.1.refs_2_ = bf16[96,384]{1,0:T(8,128)(2,1)S(1)} collective-permute-done((bf16[96,384]{1,0:T(8,128)(2,1)S(1)}, bf16[96,384]{1,0:T(8,128)(2,1)S(1)}, u32[]{:S(2)}, u32[]{:S(2)}) %collective-permute-start.1) | collective-permute-done | bytes 73760 | tf_op jit(solution)/shard_map/ppermute | solution.py:265
  34.7 0.6 collective-permute-done.2.refs_3_
  35.3 1.5 %collective-permute-start.7 = (bf16[96,384]{1,0:T(8,128)(2,1)S(1)}, bf16[96,384]{1,0:T(8,128)(2,1)S(1)}, u32[]{:S(2)}, u32[]{:S(2)}) collective-permute-start(bf16[96,384]{1,0:T(8,128)(2,1)S(1)} %copy-done.18), channel_id=1, source_target_pairs={{0,8},{1,9},{2,10},{3,11},{4,12},{5,13},{6,14},{7,15},{8,0},{9,1},... | collective-permute-start | bytes 221192 | tf_op jit(solution)/shard_map/ppermute | solution.py:265
  36.8 1.0 collective-permute-start.8
  37.9 1.2 collective-permute-start.9
  39.0 1.2 collective-permute-start.10
  40.2 1.3 collective-permute-start.11
  41.6 1.6 %collective-permute-start.12 = (bf16[96,384]{1,0:T(8,128)(2,1)S(1)}, bf16[96,384]{1,0:T(8,128)(2,1)S(1)}, u32[]{:S(2)}, u32[]{:S(2)}) collective-permute-start(bf16[96,384]{1,0:T(8,128)(2,1)S(1)} %copy-done.13), channel_id=1, source_target_pairs={{0,13},{1,12},{2,15},{3,14},{4,9},{5,8},{6,11},{7,10},{8,5},{9,4},... | collective-permute-start | bytes 221192 | tf_op jit(solution)/shard_map/ppermute | solution.py:265
  43.2 2.4 %collective-permute-start.13 = (bf16[96,384]{1,0:T(8,128)(2,1)S(1)}, bf16[96,384]{1,0:T(8,128)(2,1)S(1)}, u32[]{:S(2)}, u32[]{:S(2)}) collective-permute-start(bf16[96,384]{1,0:T(8,128)(2,1)S(1)} %copy-done.12), channel_id=1, source_target_pairs={{0,14},{1,15},{2,12},{3,13},{4,10},{5,11},{6,8},{7,9},{8,6},{9,7},... | collective-permute-start | bytes 221192 | tf_op jit(solution)/shard_map/ppermute | solution.py:265
  45.7 0.8 collective-permute-start.14
  46.9 0.8 collective-permute-done.12.refs_13_
  47.7 3.1 %collective-permute-done.13.refs_14_ = bf16[96,384]{1,0:T(8,128)(2,1)S(1)} collective-permute-done((bf16[96,384]{1,0:T(8,128)(2,1)S(1)}, bf16[96,384]{1,0:T(8,128)(2,1)S(1)}, u32[]{:S(2)}, u32[]{:S(2)}) %collective-permute-start.13) | collective-permute-done | bytes 73760 | tf_op jit(solution)/shard_map/ppermute | solution.py:265
  50.8 1.4 %collective-permute-done.14.refs_15_ = bf16[96,384]{1,0:T(8,128)(2,1)S(1)} collective-permute-done((bf16[96,384]{1,0:T(8,128)(2,1)S(1)}, bf16[96,384]{1,0:T(8,128)(2,1)S(1)}, u32[]{:S(2)}, u32[]{:S(2)}) %collective-permute-start.14) | collective-permute-done | bytes 73760 | tf_op jit(solution)/shard_map/ppermute | solution.py:265
  52.2 4.7 %products.2 = bf16[16,144,128]{2,1,0:T(8,128)(2,1)} custom-call(bf16[1536,384]{1,0:T(8,128)(2,1)S(1)} %bitcast.8, bf16[96,384]{1,0:T(8,128)(2,1)S(1)} %copy-done.3, bf16[96,384]{1,0:T(8,128)(2,1)S(1)} %collective-permute-done.refs_1_, bf16[96,384]{1,0:T(8,128)(2,1)S(1)} %collective-permute-done.1.refs_2_, ...), custom_call_target="tpu_custom_call" | custom-call | flops 226492416 | bytes 3538944 | tf_op jit(solution)/shard_map/products/pallas_call | solution.py:298
  57.0 4.1 %all-to-all-start.1 = ((bf16[16,144,128]{2,1,0:T(8,128)(2,1)}), bf16[16,144,128]{2,1,0:T(8,128)(2,1)S(1)}, u32[]{:S(2)}, u32[]{:S(2)}) async-start(bf16[16,144,128]{2,1,0:T(8,128)(2,1)} %products.2), calls=%async_computation.1 | async-start | bytes 1179648 | tf_op jit(solution)/shard_map/all_to_all | solution.py:315
  61.1 2.7 %collective-permute-start.15 = (bf16[96,384]{1,0:T(8,128)(2,1)S(1)}, bf16[96,384]{1,0:T(8,128)(2,1)S(1)}, u32[]{:S(2)}, u32[]{:S(2)}) collective-permute-start(bf16[96,384]{1,0:T(8,128)(2,1)S(1)} %copy-done.3), channel_id=1, source_target_pairs={{0,16},{1,17},{2,18},{3,19},{4,20},{5,21},{6,22},{7,23},{8,24},{9,... | collective-permute-start | bytes 221192 | tf_op jit(solution)/shard_map/ppermute | solution.py:265
  63.8 3.7 %collective-permute-start.17 = (bf16[96,384]{1,0:T(8,128)(2,1)S(1)}, bf16[96,384]{1,0:T(8,128)(2,1)S(1)}, u32[]{:S(2)}, u32[]{:S(2)}) collective-permute-start(bf16[96,384]{1,0:T(8,128)(2,1)S(1)} %copy-done.30), channel_id=1, source_target_pairs={{0,18},{1,19},{2,16},{3,17},{4,22},{5,23},{6,20},{7,21},{8,26},{9,... | collective-permute-start | bytes 221192 | tf_op jit(solution)/shard_map/ppermute | solution.py:265
  67.8 3.5 %collective-permute-start.19 = (bf16[96,384]{1,0:T(8,128)(2,1)S(1)}, bf16[96,384]{1,0:T(8,128)(2,1)S(1)}, u32[]{:S(2)}, u32[]{:S(2)}) collective-permute-start(bf16[96,384]{1,0:T(8,128)(2,1)S(1)} %copy-done.26), channel_id=1, source_target_pairs={{0,20},{1,21},{2,22},{3,23},{4,16},{5,17},{6,18},{7,19},{8,28},{9,... | collective-permute-start | bytes 221192 | tf_op jit(solution)/shard_map/ppermute | solution.py:265
  71.3 2.5 %collective-permute-start.20 = (bf16[96,384]{1,0:T(8,128)(2,1)S(1)}, bf16[96,384]{1,0:T(8,128)(2,1)S(1)}, u32[]{:S(2)}, u32[]{:S(2)}) collective-permute-start(bf16[96,384]{1,0:T(8,128)(2,1)S(1)} %copy-done.24), channel_id=1, source_target_pairs={{0,21},{1,20},{2,23},{3,22},{4,17},{5,16},{6,19},{7,18},{8,29},{9,... | collective-permute-start | bytes 221192 | tf_op jit(solution)/shard_map/ppermute | solution.py:265
  73.8 2.9 %collective-permute-start.21 = (bf16[96,384]{1,0:T(8,128)(2,1)S(1)}, bf16[96,384]{1,0:T(8,128)(2,1)S(1)}, u32[]{:S(2)}, u32[]{:S(2)}) collective-permute-start(bf16[96,384]{1,0:T(8,128)(2,1)S(1)} %copy-done.22), channel_id=1, source_target_pairs={{0,22},{1,23},{2,20},{3,21},{4,18},{5,19},{6,16},{7,17},{8,30},{9,... | collective-permute-start | bytes 221192 | tf_op jit(solution)/shard_map/ppermute | solution.py:265
  76.6 2.6 %collective-permute-start.22 = (bf16[96,384]{1,0:T(8,128)(2,1)S(1)}, bf16[96,384]{1,0:T(8,128)(2,1)S(1)}, u32[]{:S(2)}, u32[]{:S(2)}) collective-permute-start(bf16[96,384]{1,0:T(8,128)(2,1)S(1)} %copy-done.20), channel_id=1, source_target_pairs={{0,23},{1,22},{2,21},{3,20},{4,19},{5,18},{6,17},{7,16},{8,31},{9,... | collective-permute-start | bytes 221192 | tf_op jit(solution)/shard_map/ppermute | solution.py:265
  79.3 9.1 %collective-permute-start.23 = (bf16[96,384]{1,0:T(8,128)(2,1)S(1)}, bf16[96,384]{1,0:T(8,128)(2,1)S(1)}, u32[]{:S(2)}, u32[]{:S(2)}) collective-permute-start(bf16[96,384]{1,0:T(8,128)(2,1)S(1)} %copy-done.18), channel_id=1, source_target_pairs={{0,24},{1,25},{2,26},{3,27},{4,28},{5,29},{6,30},{7,31},{8,16},{9,... | collective-permute-start | bytes 221192 | tf_op jit(solution)/shard_map/ppermute | solution.py:265
  88.4 1.9 %collective-permute-start.24 = (bf16[96,384]{1,0:T(8,128)(2,1)S(1)}, bf16[96,384]{1,0:T(8,128)(2,1)S(1)}, u32[]{:S(2)}, u32[]{:S(2)}) collective-permute-start(bf16[96,384]{1,0:T(8,128)(2,1)S(1)} %copy-done.17), channel_id=1, source_target_pairs={{0,25},{1,24},{2,27},{3,26},{4,29},{5,28},{6,31},{7,30},{8,17},{9,... | collective-permute-start | bytes 221192 | tf_op jit(solution)/shard_map/ppermute | solution.py:265
  90.3 2.1 %collective-permute-start.25 = (bf16[96,384]{1,0:T(8,128)(2,1)S(1)}, bf16[96,384]{1,0:T(8,128)(2,1)S(1)}, u32[]{:S(2)}, u32[]{:S(2)}) collective-permute-start(bf16[96,384]{1,0:T(8,128)(2,1)S(1)} %copy-done.16), channel_id=1, source_target_pairs={{0,26},{1,27},{2,24},{3,25},{4,30},{5,31},{6,28},{7,29},{8,18},{9,... | collective-permute-start | bytes 221192 | tf_op jit(solution)/shard_map/ppermute | solution.py:265
  92.4 1.7 %collective-permute-done.21.refs_6_ = bf16[96,384]{1,0:T(8,128)(2,1)S(1)} collective-permute-done((bf16[96,384]{1,0:T(8,128)(2,1)S(1)}, bf16[96,384]{1,0:T(8,128)(2,1)S(1)}, u32[]{:S(2)}, u32[]{:S(2)}) %collective-permute-start.21) | collective-permute-done | bytes 73760 | tf_op jit(solution)/shard_map/ppermute | solution.py:265
  94.2 0.9 collective-permute-start.26
  95.1 2.9 %collective-permute-done.22.refs_7_ = bf16[96,384]{1,0:T(8,128)(2,1)S(1)} collective-permute-done((bf16[96,384]{1,0:T(8,128)(2,1)S(1)}, bf16[96,384]{1,0:T(8,128)(2,1)S(1)}, u32[]{:S(2)}, u32[]{:S(2)}) %collective-permute-start.22) | collective-permute-done | bytes 73760 | tf_op jit(solution)/shard_map/ppermute | solution.py:265
  98.0 2.3 %collective-permute-start.27 = (bf16[96,384]{1,0:T(8,128)(2,1)S(1)}, bf16[96,384]{1,0:T(8,128)(2,1)S(1)}, u32[]{:S(2)}, u32[]{:S(2)}) collective-permute-start(bf16[96,384]{1,0:T(8,128)(2,1)S(1)} %copy-done.14), channel_id=1, source_target_pairs={{0,28},{1,29},{2,30},{3,31},{4,24},{5,25},{6,26},{7,27},{8,20},{9,... | collective-permute-start | bytes 221192 | tf_op jit(solution)/shard_map/ppermute | solution.py:265
  100.3 2.5 %collective-permute-start.28 = (bf16[96,384]{1,0:T(8,128)(2,1)S(1)}, bf16[96,384]{1,0:T(8,128)(2,1)S(1)}, u32[]{:S(2)}, u32[]{:S(2)}) collective-permute-start(bf16[96,384]{1,0:T(8,128)(2,1)S(1)} %copy-done.13), channel_id=1, source_target_pairs={{0,29},{1,28},{2,31},{3,30},{4,25},{5,24},{6,27},{7,26},{8,21},{9,... | collective-permute-start | bytes 221192 | tf_op jit(solution)/shard_map/ppermute | solution.py:265
  102.8 2.4 %collective-permute-start.29 = (bf16[96,384]{1,0:T(8,128)(2,1)S(1)}, bf16[96,384]{1,0:T(8,128)(2,1)S(1)}, u32[]{:S(2)}, u32[]{:S(2)}) collective-permute-start(bf16[96,384]{1,0:T(8,128)(2,1)S(1)} %copy-done.12), channel_id=1, source_target_pairs={{0,30},{1,31},{2,28},{3,29},{4,26},{5,27},{6,24},{7,25},{8,22},{9,... | collective-permute-start | bytes 221192 | tf_op jit(solution)/shard_map/ppermute | solution.py:265
  105.2 2.6 %collective-permute-start.30 = (bf16[96,384]{1,0:T(8,128)(2,1)S(1)}, bf16[96,384]{1,0:T(8,128)(2,1)S(1)}, u32[]{:S(2)}, u32[]{:S(2)}) collective-permute-start(bf16[96,384]{1,0:T(8,128)(2,1)S(1)} %copy-done.11), channel_id=1, source_target_pairs={{0,31},{1,30},{2,29},{3,28},{4,27},{5,26},{6,25},{7,24},{8,23},{9,... | collective-permute-start | bytes 221192 | tf_op jit(solution)/shard_map/ppermute | solution.py:265
  107.8 2.9 %collective-permute-done.29.refs_14_ = bf16[96,384]{1,0:T(8,128)(2,1)S(1)} collective-permute-done((bf16[96,384]{1,0:T(8,128)(2,1)S(1)}, bf16[96,384]{1,0:T(8,128)(2,1)S(1)}, u32[]{:S(2)}, u32[]{:S(2)}) %collective-permute-start.29) | collective-permute-done | bytes 73760 | tf_op jit(solution)/shard_map/ppermute | solution.py:265
  110.8 2.3 %collective-permute-done.30.refs_15_ = bf16[96,384]{1,0:T(8,128)(2,1)S(1)} collective-permute-done((bf16[96,384]{1,0:T(8,128)(2,1)S(1)}, bf16[96,384]{1,0:T(8,128)(2,1)S(1)}, u32[]{:S(2)}, u32[]{:S(2)}) %collective-permute-start.30) | collective-permute-done | bytes 73760 | tf_op jit(solution)/shard_map/ppermute | solution.py:265
  113.0 4.6 %products.3 = bf16[16,144,128]{2,1,0:T(8,128)(2,1)} custom-call(bf16[1536,384]{1,0:T(8,128)(2,1)S(1)} %bitcast.9, bf16[96,384]{1,0:T(8,128)(2,1)S(1)} %collective-permute-done.15.refs_0_, bf16[96,384]{1,0:T(8,128)(2,1)S(1)} %collective-permute-done.16.refs_1_, bf16[96,384]{1,0:T(8,128)(2,1)S(1)} %collective-permute-done.17.refs_2_, ...), custom_call_target="tpu_custom_call" | custom-call | flops 226492416 | bytes 3538944 | tf_op jit(solution)/shard_map/products/pallas_call | solution.py:298
  117.7 7.6 %all-to-all-start.2 = ((bf16[16,144,128]{2,1,0:T(8,128)(2,1)}), bf16[16,144,128]{2,1,0:T(8,128)(2,1)S(1)}, u32[]{:S(2)}, u32[]{:S(2)}) async-start(bf16[16,144,128]{2,1,0:T(8,128)(2,1)} %products.3), calls=%async_computation.2 | async-start | bytes 1179648 | tf_op jit(solution)/shard_map/all_to_all | solution.py:315
  125.3 0.7 copy-done.5
  126.1 0.9 gate.1.refs_2_
  127.0 9.5 %all-to-all-done.2.refs_1_ = bf16[16,144,128]{2,1,0:T(8,128)(2,1)S(1)} async-done(((bf16[16,144,128]{2,1,0:T(8,128)(2,1)}), bf16[16,144,128]{2,1,0:T(8,128)(2,1)S(1)}, u32[]{:S(2)}, u32[]{:S(2)}) %all-to-all-start.2) | async-done | bytes 589856 | tf_op jit(solution)/shard_map/all_to_all | solution.py:315
  136.6 0.7 copy-done.4
  137.3 2.7 %update.1 = bf16[12,384,128]{2,1,0:T(8,128)(2,1)} custom-call(bf16[16,144,128]{2,1,0:T(8,128)(2,1)S(1)} %all-to-all-done.1.refs_0_, bf16[16,144,128]{2,1,0:T(8,128)(2,1)S(1)} %all-to-all-done.2.refs_1_, bf16[12,384,128]{2,1,0:T(8,128)(2,1)S(1)} %gate.1.refs_2_, f32[1,128]{1,0:T(1,128)S(1)} %bitcast.12, f32[1,128]{1,0:T(1,128)S(1)} %bitcast.13, ...), custom_call_target="tpu_custom_call" | custom-call | flops 150994944 | bytes 3538944 | tf_op jit(solution)/shard_map/update/pallas_call | solution.py:317
  (92 shorter events, 1.1 us)
Async XLA Ops:
  8.8 25.9 %copy-start.19 = (bf16[96,384]{1,0:T(8,128)(2,1)S(1)}, bf16[96,384]{1,0:T(8,128)(2,1)}, u32[]{:S(2)}) copy-start(bf16[96,384]{1,0:T(8,128)(2,1)} %get-tuple-element.30) | copy-start | bytes 221188
  8.8 26.5 %copy-start.18 = (bf16[96,384]{1,0:T(8,128)(2,1)S(1)}, bf16[96,384]{1,0:T(8,128)(2,1)}, u32[]{:S(2)}) copy-start(bf16[96,384]{1,0:T(8,128)(2,1)} %get-tuple-element.31) | copy-start | bytes 221188
  8.8 28.0 %copy-start.17 = (bf16[96,384]{1,0:T(8,128)(2,1)S(1)}, bf16[96,384]{1,0:T(8,128)(2,1)}, u32[]{:S(2)}) copy-start(bf16[96,384]{1,0:T(8,128)(2,1)} %get-tuple-element.32) | copy-start | bytes 221188
  8.8 29.0 %copy-start.16 = (bf16[96,384]{1,0:T(8,128)(2,1)S(1)}, bf16[96,384]{1,0:T(8,128)(2,1)}, u32[]{:S(2)}) copy-start(bf16[96,384]{1,0:T(8,128)(2,1)} %get-tuple-element.33) | copy-start | bytes 221188
  8.9 30.2 %copy-start.15 = (bf16[96,384]{1,0:T(8,128)(2,1)S(1)}, bf16[96,384]{1,0:T(8,128)(2,1)}, u32[]{:S(2)}) copy-start(bf16[96,384]{1,0:T(8,128)(2,1)} %get-tuple-element.34) | copy-start | bytes 221188
  8.9 31.4 %copy-start.14 = (bf16[96,384]{1,0:T(8,128)(2,1)S(1)}, bf16[96,384]{1,0:T(8,128)(2,1)}, u32[]{:S(2)}) copy-start(bf16[96,384]{1,0:T(8,128)(2,1)} %get-tuple-element.35) | copy-start | bytes 221188
  8.9 32.7 %copy-start.13 = (bf16[96,384]{1,0:T(8,128)(2,1)S(1)}, bf16[96,384]{1,0:T(8,128)(2,1)}, u32[]{:S(2)}) copy-start(bf16[96,384]{1,0:T(8,128)(2,1)} %get-tuple-element.36) | copy-start | bytes 221188
  8.9 34.3 %copy-start.12 = (bf16[96,384]{1,0:T(8,128)(2,1)S(1)}, bf16[96,384]{1,0:T(8,128)(2,1)}, u32[]{:S(2)}) copy-start(bf16[96,384]{1,0:T(8,128)(2,1)} %get-tuple-element.37) | copy-start | bytes 221188
  8.9 36.8 %copy-start.11 = (bf16[96,384]{1,0:T(8,128)(2,1)S(1)}, bf16[96,384]{1,0:T(8,128)(2,1)}, u32[]{:S(2)}) copy-start(bf16[96,384]{1,0:T(8,128)(2,1)} %get-tuple-element.38) | copy-start | bytes 221188
  8.9 43.3 %copy-start.3 = (bf16[96,384]{1,0:T(8,128)(2,1)S(1)}, bf16[96,384]{1,0:T(8,128)(2,1)}, u32[]{:S(2)}) copy-start(bf16[96,384]{1,0:T(8,128)(2,1)} %get-tuple-element.23.refs_0_) | copy-start | bytes 221188
  8.9 43.3 %all-to-all-start = ((bf16[16,96,384]{2,1,0:T(8,128)(2,1)}), bf16[16,96,384]{2,1,0:T(8,128)(2,1)S(1)}, u32[]{:S(2)}, u32[]{:S(2)}) async-start(bf16[16,96,384]{2,1,0:T(8,128)(2,1)} %left_factor.1), calls=%async_computation | async-start | bytes 2359296 | tf_op jit(solution)/shard_map/all_to_all | solution.py:283
  15.4 4.0 %collective-permute-start = (bf16[96,384]{1,0:T(8,128)(2,1)S(1)}, bf16[96,384]{1,0:T(8,128)(2,1)S(1)}, u32[]{:S(2)}, u32[]{:S(2)}) collective-permute-start(bf16[96,384]{1,0:T(8,128)(2,1)S(1)} %copy-done.31), channel_id=1, source_target_pairs={{0,1},{1,0},{2,3},{3,2},{4,5},{5,4},{6,7},{7,6},{8,9},{9,8},{10,11... | collective-permute-start | bytes 221192 | tf_op jit(solution)/shard_map/ppermute | solution.py:265
  15.8 18.9 %collective-permute-start.1 = (bf16[96,384]{1,0:T(8,128)(2,1)S(1)}, bf16[96,384]{1,0:T(8,128)(2,1)S(1)}, u32[]{:S(2)}, u32[]{:S(2)}) collective-permute-start(bf16[96,384]{1,0:T(8,128)(2,1)S(1)} %copy-done.29), channel_id=1, source_target_pairs={{0,2},{1,3},{2,0},{3,1},{4,6},{5,7},{6,4},{7,5},{8,10},{9,11},{10,... | collective-permute-start | bytes 221192 | tf_op jit(solution)/shard_map/ppermute | solution.py:265
  17.5 17.8 %collective-permute-start.2 = (bf16[96,384]{1,0:T(8,128)(2,1)S(1)}, bf16[96,384]{1,0:T(8,128)(2,1)S(1)}, u32[]{:S(2)}, u32[]{:S(2)}) collective-permute-start(bf16[96,384]{1,0:T(8,128)(2,1)S(1)} %copy-done.27), channel_id=1, source_target_pairs={{0,3},{1,2},{2,1},{3,0},{4,7},{5,6},{6,5},{7,4},{8,11},{9,10},{10,... | collective-permute-start | bytes 221192 | tf_op jit(solution)/shard_map/ppermute | solution.py:265
  17.5 19.3 %collective-permute-start.3 = (bf16[96,384]{1,0:T(8,128)(2,1)S(1)}, bf16[96,384]{1,0:T(8,128)(2,1)S(1)}, u32[]{:S(2)}, u32[]{:S(2)}) collective-permute-start(bf16[96,384]{1,0:T(8,128)(2,1)S(1)} %copy-done.25), channel_id=1, source_target_pairs={{0,4},{1,5},{2,6},{3,7},{4,0},{5,1},{6,2},{7,3},{8,12},{9,13},{10,... | collective-permute-start | bytes 221192 | tf_op jit(solution)/shard_map/ppermute | solution.py:265
  19.2 18.6 %collective-permute-start.4 = (bf16[96,384]{1,0:T(8,128)(2,1)S(1)}, bf16[96,384]{1,0:T(8,128)(2,1)S(1)}, u32[]{:S(2)}, u32[]{:S(2)}) collective-permute-start(bf16[96,384]{1,0:T(8,128)(2,1)S(1)} %copy-done.23), channel_id=1, source_target_pairs={{0,5},{1,4},{2,7},{3,6},{4,1},{5,0},{6,3},{7,2},{8,13},{9,12},{10,... | collective-permute-start | bytes 221192 | tf_op jit(solution)/shard_map/ppermute | solution.py:265
  19.3 19.7 %collective-permute-start.5 = (bf16[96,384]{1,0:T(8,128)(2,1)S(1)}, bf16[96,384]{1,0:T(8,128)(2,1)S(1)}, u32[]{:S(2)}, u32[]{:S(2)}) collective-permute-start(bf16[96,384]{1,0:T(8,128)(2,1)S(1)} %copy-done.21), channel_id=1, source_target_pairs={{0,6},{1,7},{2,4},{3,5},{4,2},{5,3},{6,0},{7,1},{8,14},{9,15},{10,... | collective-permute-start | bytes 221192 | tf_op jit(solution)/shard_map/ppermute | solution.py:265
  34.7 5.5 %collective-permute-start.6 = (bf16[96,384]{1,0:T(8,128)(2,1)S(1)}, bf16[96,384]{1,0:T(8,128)(2,1)S(1)}, u32[]{:S(2)}, u32[]{:S(2)}) collective-permute-start(bf16[96,384]{1,0:T(8,128)(2,1)S(1)} %copy-done.19), channel_id=1, source_target_pairs={{0,7},{1,6},{2,5},{3,4},{4,3},{5,2},{6,1},{7,0},{8,15},{9,14},{10,... | collective-permute-start | bytes 221192 | tf_op jit(solution)/shard_map/ppermute | solution.py:265
  35.3 6.2 %collective-permute-start.7 = (bf16[96,384]{1,0:T(8,128)(2,1)S(1)}, bf16[96,384]{1,0:T(8,128)(2,1)S(1)}, u32[]{:S(2)}, u32[]{:S(2)}) collective-permute-start(bf16[96,384]{1,0:T(8,128)(2,1)S(1)} %copy-done.18), channel_id=1, source_target_pairs={{0,8},{1,9},{2,10},{3,11},{4,12},{5,13},{6,14},{7,15},{8,0},{9,1},... | collective-permute-start | bytes 221192 | tf_op jit(solution)/shard_map/ppermute | solution.py:265
  36.8 6.4 %collective-permute-start.8 = (bf16[96,384]{1,0:T(8,128)(2,1)S(1)}, bf16[96,384]{1,0:T(8,128)(2,1)S(1)}, u32[]{:S(2)}, u32[]{:S(2)}) collective-permute-start(bf16[96,384]{1,0:T(8,128)(2,1)S(1)} %copy-done.17), channel_id=1, source_target_pairs={{0,9},{1,8},{2,11},{3,10},{4,13},{5,12},{6,15},{7,14},{8,1},{9,0},... | collective-permute-start | bytes 221192 | tf_op jit(solution)/shard_map/ppermute | solution.py:265
  37.9 7.8 %collective-permute-start.9 = (bf16[96,384]{1,0:T(8,128)(2,1)S(1)}, bf16[96,384]{1,0:T(8,128)(2,1)S(1)}, u32[]{:S(2)}, u32[]{:S(2)}) collective-permute-start(bf16[96,384]{1,0:T(8,128)(2,1)S(1)} %copy-done.16), channel_id=1, source_target_pairs={{0,10},{1,11},{2,8},{3,9},{4,14},{5,15},{6,12},{7,13},{8,2},{9,3},... | collective-permute-start | bytes 221192 | tf_op jit(solution)/shard_map/ppermute | solution.py:265
  39.0 7.4 %collective-permute-start.10 = (bf16[96,384]{1,0:T(8,128)(2,1)S(1)}, bf16[96,384]{1,0:T(8,128)(2,1)S(1)}, u32[]{:S(2)}, u32[]{:S(2)}) collective-permute-start(bf16[96,384]{1,0:T(8,128)(2,1)S(1)} %copy-done.15), channel_id=1, source_target_pairs={{0,11},{1,10},{2,9},{3,8},{4,15},{5,14},{6,13},{7,12},{8,3},{9,2},... | collective-permute-start | bytes 221192 | tf_op jit(solution)/shard_map/ppermute | solution.py:265
  40.2 6.6 %collective-permute-start.11 = (bf16[96,384]{1,0:T(8,128)(2,1)S(1)}, bf16[96,384]{1,0:T(8,128)(2,1)S(1)}, u32[]{:S(2)}, u32[]{:S(2)}) collective-permute-start(bf16[96,384]{1,0:T(8,128)(2,1)S(1)} %copy-done.14), channel_id=1, source_target_pairs={{0,12},{1,13},{2,14},{3,15},{4,8},{5,9},{6,10},{7,11},{8,4},{9,5},... | collective-permute-start | bytes 221192 | tf_op jit(solution)/shard_map/ppermute | solution.py:265
  41.6 6.2 %collective-permute-start.12 = (bf16[96,384]{1,0:T(8,128)(2,1)S(1)}, bf16[96,384]{1,0:T(8,128)(2,1)S(1)}, u32[]{:S(2)}, u32[]{:S(2)}) collective-permute-start(bf16[96,384]{1,0:T(8,128)(2,1)S(1)} %copy-done.13), channel_id=1, source_target_pairs={{0,13},{1,12},{2,15},{3,14},{4,9},{5,8},{6,11},{7,10},{8,5},{9,4},... | collective-permute-start | bytes 221192 | tf_op jit(solution)/shard_map/ppermute | solution.py:265
  43.2 7.6 %collective-permute-start.13 = (bf16[96,384]{1,0:T(8,128)(2,1)S(1)}, bf16[96,384]{1,0:T(8,128)(2,1)S(1)}, u32[]{:S(2)}, u32[]{:S(2)}) collective-permute-start(bf16[96,384]{1,0:T(8,128)(2,1)S(1)} %copy-done.12), channel_id=1, source_target_pairs={{0,14},{1,15},{2,12},{3,13},{4,10},{5,11},{6,8},{7,9},{8,6},{9,7},... | collective-permute-start | bytes 221192 | tf_op jit(solution)/shard_map/ppermute | solution.py:265
  45.7 6.5 %collective-permute-start.14 = (bf16[96,384]{1,0:T(8,128)(2,1)S(1)}, bf16[96,384]{1,0:T(8,128)(2,1)S(1)}, u32[]{:S(2)}, u32[]{:S(2)}) collective-permute-start(bf16[96,384]{1,0:T(8,128)(2,1)S(1)} %copy-done.11), channel_id=1, source_target_pairs={{0,15},{1,14},{2,13},{3,12},{4,11},{5,10},{6,9},{7,8},{8,7},{9,6},... | collective-permute-start | bytes 221192 | tf_op jit(solution)/shard_map/ppermute | solution.py:265
  56.9 10.9 %copy-start.26 = (bf16[96,384]{1,0:T(8,128)(2,1)S(1)}, bf16[96,384]{1,0:T(8,128)(2,1)}, u32[]{:S(2)}) copy-start(bf16[96,384]{1,0:T(8,128)(2,1)} %get-tuple-element.27) | copy-start | bytes 221188
  56.9 14.3 %copy-start.24 = (bf16[96,384]{1,0:T(8,128)(2,1)S(1)}, bf16[96,384]{1,0:T(8,128)(2,1)}, u32[]{:S(2)}) copy-start(bf16[96,384]{1,0:T(8,128)(2,1)} %get-tuple-element.28) | copy-start | bytes 221188
  56.9 16.8 %copy-start.22 = (bf16[96,384]{1,0:T(8,128)(2,1)S(1)}, bf16[96,384]{1,0:T(8,128)(2,1)}, u32[]{:S(2)}) copy-start(bf16[96,384]{1,0:T(8,128)(2,1)} %get-tuple-element.29) | copy-start | bytes 221188
  57.0 19.7 %copy-start.20 = (bf16[96,384]{1,0:T(8,128)(2,1)S(1)}, bf16[96,384]{1,0:T(8,128)(2,1)}, u32[]{:S(2)}) copy-start(bf16[96,384]{1,0:T(8,128)(2,1)} %get-tuple-element.30) | copy-start | bytes 221188
  57.0 60.7 %all-to-all-start.1 = ((bf16[16,144,128]{2,1,0:T(8,128)(2,1)}), bf16[16,144,128]{2,1,0:T(8,128)(2,1)S(1)}, u32[]{:S(2)}, u32[]{:S(2)}) async-start(bf16[16,144,128]{2,1,0:T(8,128)(2,1)} %products.2), calls=%async_computation.1 | async-start | bytes 1179648 | tf_op jit(solution)/shard_map/all_to_all | solution.py:315
  61.1 10.2 %collective-permute-start.15 = (bf16[96,384]{1,0:T(8,128)(2,1)S(1)}, bf16[96,384]{1,0:T(8,128)(2,1)S(1)}, u32[]{:S(2)}, u32[]{:S(2)}) collective-permute-start(bf16[96,384]{1,0:T(8,128)(2,1)S(1)} %copy-done.3), channel_id=1, source_target_pairs={{0,16},{1,17},{2,18},{3,19},{4,20},{5,21},{6,22},{7,23},{8,24},{9,... | collective-permute-start | bytes 221192 | tf_op jit(solution)/shard_map/ppermute | solution.py:265
  63.8 10.0 %collective-permute-start.16 = (bf16[96,384]{1,0:T(8,128)(2,1)S(1)}, bf16[96,384]{1,0:T(8,128)(2,1)S(1)}, u32[]{:S(2)}, u32[]{:S(2)}) collective-permute-start(bf16[96,384]{1,0:T(8,128)(2,1)S(1)} %copy-done.32), channel_id=1, source_target_pairs={{0,17},{1,16},{2,19},{3,18},{4,21},{5,20},{6,23},{7,22},{8,25},{9,... | collective-permute-start | bytes 221192 | tf_op jit(solution)/shard_map/ppermute | solution.py:265
  63.8 12.8 %collective-permute-start.17 = (bf16[96,384]{1,0:T(8,128)(2,1)S(1)}, bf16[96,384]{1,0:T(8,128)(2,1)S(1)}, u32[]{:S(2)}, u32[]{:S(2)}) collective-permute-start(bf16[96,384]{1,0:T(8,128)(2,1)S(1)} %copy-done.30), channel_id=1, source_target_pairs={{0,18},{1,19},{2,16},{3,17},{4,22},{5,23},{6,20},{7,21},{8,26},{9,... | collective-permute-start | bytes 221192 | tf_op jit(solution)/shard_map/ppermute | solution.py:265
  67.5 11.8 %collective-permute-start.18 = (bf16[96,384]{1,0:T(8,128)(2,1)S(1)}, bf16[96,384]{1,0:T(8,128)(2,1)S(1)}, u32[]{:S(2)}, u32[]{:S(2)}) collective-permute-start(bf16[96,384]{1,0:T(8,128)(2,1)S(1)} %copy-done.28), channel_id=1, source_target_pairs={{0,19},{1,18},{2,17},{3,16},{4,23},{5,22},{6,21},{7,20},{8,27},{9,... | collective-permute-start | bytes 221192 | tf_op jit(solution)/shard_map/ppermute | solution.py:265
  67.8 20.6 %collective-permute-start.19 = (bf16[96,384]{1,0:T(8,128)(2,1)S(1)}, bf16[96,384]{1,0:T(8,128)(2,1)S(1)}, u32[]{:S(2)}, u32[]{:S(2)}) collective-permute-start(bf16[96,384]{1,0:T(8,128)(2,1)S(1)} %copy-done.26), channel_id=1, source_target_pairs={{0,20},{1,21},{2,22},{3,23},{4,16},{5,17},{6,18},{7,19},{8,28},{9,... | collective-permute-start | bytes 221192 | tf_op jit(solution)/shard_map/ppermute | solution.py:265
  71.3 19.0 %collective-permute-start.20 = (bf16[96,384]{1,0:T(8,128)(2,1)S(1)}, bf16[96,384]{1,0:T(8,128)(2,1)S(1)}, u32[]{:S(2)}, u32[]{:S(2)}) collective-permute-start(bf16[96,384]{1,0:T(8,128)(2,1)S(1)} %copy-done.24), channel_id=1, source_target_pairs={{0,21},{1,20},{2,23},{3,22},{4,17},{5,16},{6,19},{7,18},{8,29},{9,... | collective-permute-start | bytes 221192 | tf_op jit(solution)/shard_map/ppermute | solution.py:265
  73.8 20.4 %collective-permute-start.21 = (bf16[96,384]{1,0:T(8,128)(2,1)S(1)}, bf16[96,384]{1,0:T(8,128)(2,1)S(1)}, u32[]{:S(2)}, u32[]{:S(2)}) collective-permute-start(bf16[96,384]{1,0:T(8,128)(2,1)S(1)} %copy-done.22), channel_id=1, source_target_pairs={{0,22},{1,23},{2,20},{3,21},{4,18},{5,19},{6,16},{7,17},{8,30},{9,... | collective-permute-start | bytes 221192 | tf_op jit(solution)/shard_map/ppermute | solution.py:265
  76.6 21.4 %collective-permute-start.22 = (bf16[96,384]{1,0:T(8,128)(2,1)S(1)}, bf16[96,384]{1,0:T(8,128)(2,1)S(1)}, u32[]{:S(2)}, u32[]{:S(2)}) collective-permute-start(bf16[96,384]{1,0:T(8,128)(2,1)S(1)} %copy-done.20), channel_id=1, source_target_pairs={{0,23},{1,22},{2,21},{3,20},{4,19},{5,18},{6,17},{7,16},{8,31},{9,... | collective-permute-start | bytes 221192 | tf_op jit(solution)/shard_map/ppermute | solution.py:265
  79.3 21.1 %collective-permute-start.23 = (bf16[96,384]{1,0:T(8,128)(2,1)S(1)}, bf16[96,384]{1,0:T(8,128)(2,1)S(1)}, u32[]{:S(2)}, u32[]{:S(2)}) collective-permute-start(bf16[96,384]{1,0:T(8,128)(2,1)S(1)} %copy-done.18), channel_id=1, source_target_pairs={{0,24},{1,25},{2,26},{3,27},{4,28},{5,29},{6,30},{7,31},{8,16},{9,... | collective-permute-start | bytes 221192 | tf_op jit(solution)/shard_map/ppermute | solution.py:265
  88.4 14.4 %collective-permute-start.24 = (bf16[96,384]{1,0:T(8,128)(2,1)S(1)}, bf16[96,384]{1,0:T(8,128)(2,1)S(1)}, u32[]{:S(2)}, u32[]{:S(2)}) collective-permute-start(bf16[96,384]{1,0:T(8,128)(2,1)S(1)} %copy-done.17), channel_id=1, source_target_pairs={{0,25},{1,24},{2,27},{3,26},{4,29},{5,28},{6,31},{7,30},{8,17},{9,... | collective-permute-start | bytes 221192 | tf_op jit(solution)/shard_map/ppermute | solution.py:265
  90.3 14.9 %collective-permute-start.25 = (bf16[96,384]{1,0:T(8,128)(2,1)S(1)}, bf16[96,384]{1,0:T(8,128)(2,1)S(1)}, u32[]{:S(2)}, u32[]{:S(2)}) collective-permute-start(bf16[96,384]{1,0:T(8,128)(2,1)S(1)} %copy-done.16), channel_id=1, source_target_pairs={{0,26},{1,27},{2,24},{3,25},{4,30},{5,31},{6,28},{7,29},{8,18},{9,... | collective-permute-start | bytes 221192 | tf_op jit(solution)/shard_map/ppermute | solution.py:265
  94.2 13.6 %collective-permute-start.26 = (bf16[96,384]{1,0:T(8,128)(2,1)S(1)}, bf16[96,384]{1,0:T(8,128)(2,1)S(1)}, u32[]{:S(2)}, u32[]{:S(2)}) collective-permute-start(bf16[96,384]{1,0:T(8,128)(2,1)S(1)} %copy-done.15), channel_id=1, source_target_pairs={{0,27},{1,26},{2,25},{3,24},{4,31},{5,30},{6,29},{7,28},{8,19},{9,... | collective-permute-start | bytes 221192 | tf_op jit(solution)/shard_map/ppermute | solution.py:265
  98.0 9.8 %collective-permute-start.27 = (bf16[96,384]{1,0:T(8,128)(2,1)S(1)}, bf16[96,384]{1,0:T(8,128)(2,1)S(1)}, u32[]{:S(2)}, u32[]{:S(2)}) collective-permute-start(bf16[96,384]{1,0:T(8,128)(2,1)S(1)} %copy-done.14), channel_id=1, source_target_pairs={{0,28},{1,29},{2,30},{3,31},{4,24},{5,25},{6,26},{7,27},{8,20},{9,... | collective-permute-start | bytes 221192 | tf_op jit(solution)/shard_map/ppermute | solution.py:265
  100.3 7.5 %collective-permute-start.28 = (bf16[96,384]{1,0:T(8,128)(2,1)S(1)}, bf16[96,384]{1,0:T(8,128)(2,1)S(1)}, u32[]{:S(2)}, u32[]{:S(2)}) collective-permute-start(bf16[96,384]{1,0:T(8,128)(2,1)S(1)} %copy-done.13), channel_id=1, source_target_pairs={{0,29},{1,28},{2,31},{3,30},{4,25},{5,24},{6,27},{7,26},{8,21},{9,... | collective-permute-start | bytes 221192 | tf_op jit(solution)/shard_map/ppermute | solution.py:265
  102.8 8.0 %collective-permute-start.29 = (bf16[96,384]{1,0:T(8,128)(2,1)S(1)}, bf16[96,384]{1,0:T(8,128)(2,1)S(1)}, u32[]{:S(2)}, u32[]{:S(2)}) collective-permute-start(bf16[96,384]{1,0:T(8,128)(2,1)S(1)} %copy-done.12), channel_id=1, source_target_pairs={{0,30},{1,31},{2,28},{3,29},{4,26},{5,27},{6,24},{7,25},{8,22},{9,... | collective-permute-start | bytes 221192 | tf_op jit(solution)/shard_map/ppermute | solution.py:265
  105.2 7.8 %collective-permute-start.30 = (bf16[96,384]{1,0:T(8,128)(2,1)S(1)}, bf16[96,384]{1,0:T(8,128)(2,1)S(1)}, u32[]{:S(2)}, u32[]{:S(2)}) collective-permute-start(bf16[96,384]{1,0:T(8,128)(2,1)S(1)} %copy-done.11), channel_id=1, source_target_pairs={{0,31},{1,30},{2,29},{3,28},{4,27},{5,26},{6,25},{7,24},{8,23},{9,... | collective-permute-start | bytes 221192 | tf_op jit(solution)/shard_map/ppermute | solution.py:265
  117.7 18.8 %all-to-all-start.2 = ((bf16[16,144,128]{2,1,0:T(8,128)(2,1)}), bf16[16,144,128]{2,1,0:T(8,128)(2,1)S(1)}, u32[]{:S(2)}, u32[]{:S(2)}) async-start(bf16[16,144,128]{2,1,0:T(8,128)(2,1)} %products.3), calls=%async_computation.2 | async-start | bytes 1179648 | tf_op jit(solution)/shard_map/all_to_all | solution.py:315
  (19 other events, 135.9 us)

commit v3 on v2

v3 whole, which is shorter than its diff:
```python
import functools

import jax
import jax.numpy as jnp
from jax import lax
from jax.experimental import pallas as pl
from jax.experimental.pallas import tpu as pltpu
from jax.sharding import Mesh
from jax.sharding import PartitionSpec as P

epsilon = 1e-05
CHANNELS = 128
BLOCK = 8
STEP = 4
SIZE = 32
LANES = 128
EARLY = 8
GATHER = 32
MIB = 1024 * 1024

f32, bf16 = jnp.float32, jnp.bfloat16


def sigmoid(x):
    return 0.5 * jnp.tanh(0.5 * x) + 0.5


def dot(a, b):
    return jnp.dot(a, b, preferred_element_type=f32)


def dot_nt(a, b):
    return lax.dot_general(a, b, (((1,), (1,)), ((), ())), preferred_element_type=f32)


def column(row):
    blocks = [
        jnp.broadcast_to(row[:, k : k + LANES], (LANES, LANES)).T
        for k in range(0, row.shape[1], LANES)
    ]
    return jnp.concatenate(blocks, axis=0)


def widen(col, width):
    return jnp.concatenate([col] * (width // LANES), axis=1)


def shuffle(groups, size):
    n = groups * size
    out = lax.broadcasted_iota(jnp.int32, (n, n), 0)
    row = lax.broadcasted_iota(jnp.int32, (n, n), 1)
    want = (out % size) * groups + out // size
    return jnp.where(want == row, 1.0, 0.0).astype(bf16)


def normalize(x, gain, shift):
    centered = x - jnp.mean(x, axis=1, keepdims=True)
    variance = jnp.mean(centered * centered, axis=1, keepdims=True)
    return (centered * lax.rsqrt(variance + epsilon) * gain + shift).astype(bf16)


def factor(normed, wt, bias):
    width = wt.shape[0] // 2
    lanes = normed.shape[0]
    gate = dot_nt(wt[:width], normed) + widen(bias[:width], lanes)
    value = dot_nt(wt[width:], normed) + widen(bias[width:], lanes)
    return sigmoid(gate) * value


def as_rows(values, k):
    hosts = values.shape[0] // BLOCK
    return jnp.concatenate(
        [values[:, r * k : (r + 1) * k].reshape(hosts, BLOCK, k) for r in range(STEP)], axis=1
    )


def early_kernel(pair_ref, gain_ref, shift_ref, w_ref, b_ref, out_ref, wt, bt):
    @pl.when(pl.program_id(0) == 0)
    def _():
        wt[...] = w_ref[...].astype(f32).T.astype(bf16)
        bt[...] = column(b_ref[...])

    k, width = pair_ref.shape[1:]
    x = pair_ref[...].astype(f32).reshape(STEP * k, width)
    normed = normalize(x, gain_ref[...], shift_ref[...])
    out = as_rows(factor(normed, wt[...], bt[...]), k).astype(bf16)
    for p in range(out_ref.shape[0]):
        out_ref[p] = out


def left_kernel(pair_ref, gain_ref, shift_ref, w_ref, b_ref, *refs):
    wf, bf, wt, bt = refs[-4:]
    normed_ref = refs[-5]
    outs = refs[:-5]
    k, width = pair_ref.shape[1:]
    hidden = w_ref.shape[1] // 2

    @pl.when(pl.program_id(0) == 0)
    def _():
        wf[...] = w_ref[...].astype(f32).T
        bf[...] = column(b_ref[...])
        host = lax.axis_index(("chan", "quarter"))
        for half in range(2):
            for b in range(0, len(outs), 2):
                source = [
                    pl.ds(pl.multiple_of(half * hidden + (host ^ (b + n)) * BLOCK, BLOCK), BLOCK)
                    for n in range(2)
                ]
                target = slice(half * hidden + b * BLOCK, half * hidden + (b + 2) * BLOCK)
                wt[target] = jnp.concatenate([wf[s] for s in source], axis=0).astype(bf16)
                bt[target] = jnp.concatenate([bf[s] for s in source], axis=0)

    x = pair_ref[...].astype(f32).reshape(STEP * k, width)
    normed = normalize(x, gain_ref[...], shift_ref[...])
    normed_ref[...] = normed.reshape(STEP, k, width)
    rows = as_rows(factor(normed, wt[...], bt[...]), k).astype(bf16)
    for b, out in enumerate(outs):
        out[...] = rows[b]


def late_kernel(normed_ref, w_ref, b_ref, *refs):
    out_ref = refs[-1]
    k, width = normed_ref.shape[1:]
    normed = normed_ref[...].reshape(STEP * k, width)
    wt = w_ref[...].astype(f32).T.astype(bf16)
    out = as_rows(factor(normed, wt, column(b_ref[...])), k).astype(bf16)
    for p in range(out_ref.shape[0]):
        out_ref[p] = out


def gate_kernel(normed_ref, gw_ref, gb_ref, gate_ref):
    k, width = normed_ref.shape[1:]
    normed = normed_ref[...].reshape(STEP * k, width)
    gate = sigmoid(dot(normed, gw_ref[...]) + gb_ref[...])
    gate_ref[...] = gate.reshape(gate_ref.shape).astype(gate_ref.dtype)


def regroup(pieces, target, matrix):
    many = SIZE // STEP
    for s in range(len(pieces) // many):
        rows = jnp.concatenate([piece() for piece in pieces[s * many : (s + 1) * many]], axis=0)
        moved = dot(matrix, rows).astype(bf16)
        for c in range(BLOCK):
            target[c, s * SIZE : (s + 1) * SIZE, :] = moved[c * SIZE : (c + 1) * SIZE]


def slices(refs):
    tall = STEP * BLOCK
    return [
        functools.partial(lambda ref, at: ref[at : at + tall, :], ref, at)
        for ref in refs
        for at in range(0, ref.shape[0], tall)
    ]


def multiply(left, right_ref, right, held, store):
    regroup(slices([right_ref]), right, shuffle(BLOCK, SIZE))
    back = shuffle(SIZE, BLOCK)
    for c in range(BLOCK):
        held[c] = dot_nt(left[c], right[c]).astype(bf16)
    for s in range(left.shape[1] // SIZE):
        parts = jnp.concatenate([held[c, s * SIZE : (s + 1) * SIZE, :] for c in range(BLOCK)], axis=0)
        moved = dot(back, parts).astype(bf16)
        for i in range(0, SIZE, STEP):
            store(s * SIZE + i, moved[i * BLOCK : (i + STEP) * BLOCK])


def first_kernel(hosts, right_ref, *refs):
    lefts, outs = refs[:hosts], refs[hosts : 2 * hosts]
    left, right, held = refs[2 * hosts :]

    @pl.when(pl.program_id(0) == 0)
    def _():
        regroup(slices(lefts), left, shuffle(BLOCK, SIZE))

    rows = left.shape[1] // hosts

    def store(i, values):
        to, at = divmod(i, rows)
        outs[to][at * BLOCK : (at + STEP) * BLOCK, :] = values

    multiply(left, right_ref, right, held, store)


def second_kernel(right_ref, left, *refs):
    out_ref, right, held = refs[-3:]
    rows = left.shape[1] // out_ref.shape[0]
    host = lax.axis_index(("chan", "quarter"))

    def store(i, values):
        to, at = divmod(i, rows)
        out_ref[host ^ to, at * BLOCK : (at + STEP) * BLOCK, :] = values

    multiply(left, right_ref, right, held, store)


def collect_kernel(*refs):
    host = lax.axis_index(("chan", "quarter"))
    for b, ref in enumerate(refs[:-1]):
        refs[-1][host ^ b] = ref[...]


def final_kernel(first_ref, second_ref, gate_ref, g_ref, s_ref, w_ref, b_ref, out_ref, gt, st, order):
    rows = out_ref.shape[1] * GATHER // (first_ref.shape[2] // EARLY)
    early = GATHER * EARLY

    @pl.when(pl.program_id(0) == 0)
    def _():
        gt[...] = column(g_ref[...])
        st[...] = column(s_ref[...])
        each = rows // GATHER
        out = lax.broadcasted_iota(jnp.int32, (rows, rows), 0)
        lane = lax.broadcasted_iota(jnp.int32, (rows, rows), 1)
        device, at = out // each, out % each
        want = jnp.where(
            at < EARLY, device * EARLY + at, early + device * (each - EARLY) + at - EARLY
        )
        order[...] = jnp.where(want == lane, 1.0, 0.0).astype(bf16)

    width = w_ref.shape[0]
    late = rows - early
    for g in range(out_ref.shape[1] // rows):
        x = jnp.concatenate(
            [
                first_ref[:, :, g * early : (g + 1) * early].astype(f32),
                second_ref[:, :, g * late : (g + 1) * late].astype(f32),
            ],
            axis=2,
        )
        for r in range(STEP):
            one = x[:, r * BLOCK : (r + 1) * BLOCK].reshape(width, rows)
            centered = one - jnp.mean(one, axis=0, keepdims=True)
            variance = jnp.mean(centered * centered, axis=0, keepdims=True)
            normed = centered * lax.rsqrt(variance + epsilon)
            normed = normed * widen(gt[...], rows) + widen(st[...], rows)
            turned = dot_nt(order[...], normed.astype(bf16)).astype(bf16)
            outward = dot(turned, w_ref[...]) + b_ref[...]
            at = slice(g * rows, (g + 1) * rows)
            out_ref[r, at, :] = (gate_ref[r, at, :].astype(f32) * outward).astype(bf16)


def whole(shape):
    return pl.BlockSpec(shape, lambda s: (0,) * len(shape))


def cost(flops, size):
    return pl.CostEstimate(flops=flops, bytes_accessed=size, transcendentals=0)


def params(mib=32):
    return pltpu.CompilerParams(vmem_limit_bytes=mib * MIB)


def shards(parts, pair, norm_gain, norm_shift, factor_weight, factor_bias, gate_weight, gate_bias,
           center_gain, center_shift, out_weight, out_bias):
    rows, k, width = pair.shape
    hidden = out_weight.shape[0]
    hosts = hidden // BLOCK
    steps = rows // STEP
    late = rows - EARLY
    tall = rows * BLOCK
    mine = hosts * rows
    devices = parts * hosts
    gathers = devices // GATHER
    in_part = ("chan", "quarter")
    everywhere = ("part",) + in_part
    row = lambda v: v.reshape(1, -1)
    row_block = pl.BlockSpec((STEP, k, width), lambda s: (s, 0, 0))
    work = rows * k * width
    bfloat = lambda *shape: jax.ShapeDtypeStruct(shape, bf16)

    early_right = pl.pallas_call(
        early_kernel,
        grid=(EARLY // STEP,),
        in_specs=[
            row_block,
            whole((1, width)),
            whole((1, width)),
            pl.BlockSpec((width, 2 * hidden), lambda s: (0, 1)),
            pl.BlockSpec((1, 2 * hidden), lambda s: (0, 1)),
        ],
        out_specs=pl.BlockSpec((parts, hosts, STEP * BLOCK, k), lambda s: (0, 0, s, 0)),
        out_shape=bfloat(parts, hosts, EARLY * BLOCK, k),
        scratch_shapes=[pltpu.VMEM((2 * hidden, width), bf16), pltpu.VMEM((2 * hidden, LANES), f32)],
        compiler_params=params(60),
        cost_estimate=cost(4 * work * hidden, 6 * work),
        name="early_right",
    )(pair, row(norm_gain), row(norm_shift), factor_weight, row(factor_bias))
    early_right = lax.all_to_all(
        early_right.reshape(devices, EARLY * BLOCK, k), everywhere, 0, 0, tiled=True
    )

    def send(values, b):
        if b == 0:
            return values
        pairs = [(p * hosts + h, p * hosts + (h ^ b)) for p in range(parts) for h in range(hosts)]
        return lax.ppermute(values, everywhere, pairs)

    *lefts, normed = pl.pallas_call(
        left_kernel,
        grid=(steps,),
        in_specs=[
            row_block,
            whole((1, width)),
            whole((1, width)),
            whole((width, 2 * hidden)),
            whole((1, 2 * hidden)),
        ],
        out_specs=[pl.BlockSpec((STEP * BLOCK, k), lambda s: (s, 0))] * hosts + [row_block],
        out_shape=[bfloat(tall, k)] * hosts + [bfloat(*pair.shape)],
        scratch_shapes=[
            pltpu.VMEM((2 * hidden, width), f32),
            pltpu.VMEM((2 * hidden, LANES), f32),
            pltpu.VMEM((2 * hidden, width), bf16),
            pltpu.VMEM((2 * hidden, LANES), f32),
        ],
        compiler_params=params(60),
        cost_estimate=cost(4 * work * hidden, 6 * work),
        name="left_factor",
    )(pair, row(norm_gain), row(norm_shift), factor_weight, row(factor_bias))
    lefts = [send(values, b) for b, values in enumerate(lefts)]

    late_right = pl.pallas_call(
        late_kernel,
        grid=(late // STEP,),
        in_specs=[
            pl.BlockSpec((STEP, k, width), lambda s: (s + EARLY // STEP, 0, 0)),
            pl.BlockSpec((width, 2 * hidden), lambda s: (0, 1)),
            pl.BlockSpec((1, 2 * hidden), lambda s: (0, 1)),
        ]
        + [pl.BlockSpec(memory_space=pl.ANY)] * (hosts - 1),
        out_specs=pl.BlockSpec((parts, hosts, STEP * BLOCK, k), lambda s: (0, 0, s, 0)),
        out_shape=bfloat(parts, hosts, late * BLOCK, k),
        compiler_params=params(60),
        cost_estimate=cost(2 * work * hidden, 2 * work),
        name="late_right",
    )(normed, factor_weight, row(factor_bias), *lefts[1:])
    late_right = lax.all_to_all(
        late_right.reshape(devices, late * BLOCK, k), everywhere, 0, 0, tiled=True
    )

    gate = pl.pallas_call(
        gate_kernel,
        grid=(steps,),
        in_specs=[row_block, whole((width, width)), whole((1, width))],
        out_specs=row_block,
        out_shape=bfloat(*pair.shape),
        compiler_params=params(60),
        cost_estimate=cost(2 * work * width, 4 * work),
        name="gate",
    )(normed, gate_weight, row(gate_bias))

    first = GATHER * EARLY
    second = GATHER * late
    spent = cost(2 * BLOCK * mine * mine * k, 6 * BLOCK * mine * k)
    *firsts, left = pl.pallas_call(
        functools.partial(first_kernel, hosts),
        grid=(gathers,),
        in_specs=[pl.BlockSpec((first * BLOCK, k), lambda s: (s, 0))] + [whole((tall, k))] * hosts,
        out_specs=[pl.BlockSpec((tall, first), lambda s: (0, s))] * hosts + [whole((BLOCK, mine, k))],
        out_shape=[bfloat(tall, gathers * first)] * hosts + [bfloat(BLOCK, mine, k)],
        scratch_shapes=[pltpu.VMEM((BLOCK, first, k), bf16), pltpu.VMEM((BLOCK, mine, first), bf16)],
        compiler_params=params(),
        cost_estimate=spent,
        name="first_products",
    )(early_right.reshape(devices * EARLY * BLOCK, k), *lefts)
    firsts = [send(values, b) for b, values in enumerate(firsts)]

    forced = firsts[1 : 1 + hosts * 3 // 4]
    seconds = pl.pallas_call(
        second_kernel,
        grid=(gathers,),
        in_specs=[pl.BlockSpec((second * BLOCK, k), lambda s: (s, 0)), whole((BLOCK, mine, k))]
        + [pl.BlockSpec(memory_space=pl.ANY)] * len(forced),
        out_specs=pl.BlockSpec((hosts, tall, second), lambda s: (0, 0, s)),
        out_shape=bfloat(hosts, tall, gathers * second),
        scratch_shapes=[pltpu.VMEM((BLOCK, second, k), bf16), pltpu.VMEM((BLOCK, mine, second), bf16)],
        compiler_params=params(),
        cost_estimate=spent,
        name="second_products",
    )(late_right.reshape(devices * late * BLOCK, k), left, *forced)
    seconds = lax.all_to_all(seconds, in_part, 0, 0, tiled=True)

    vmem = pl.BlockSpec(memory_space=pltpu.VMEM)
    firsts = pl.pallas_call(
        collect_kernel,
        in_specs=[vmem] * hosts,
        out_specs=vmem,
        out_shape=bfloat(hosts, tall, gathers * first),
        compiler_params=params(),
        cost_estimate=cost(0, 4 * work),
        name="collect",
    )(*firsts)

    return pl.pallas_call(
        final_kernel,
        grid=(steps,),
        in_specs=[
            pl.BlockSpec((hosts, STEP * BLOCK, gathers * first), lambda s: (0, s, 0)),
            pl.BlockSpec((hosts, STEP * BLOCK, gathers * second), lambda s: (0, s, 0)),
            row_block,
            whole((1, hidden)),
            whole((1, hidden)),
            whole((hidden, width)),
            whole((1, width)),
        ],
        out_specs=row_block,
        out_shape=bfloat(*pair.shape),
        scratch_shapes=[
            pltpu.VMEM((hidden, LANES), f32),
            pltpu.VMEM((hidden, LANES), f32),
            pltpu.VMEM((GATHER * rows, GATHER * rows), bf16),
        ],
        compiler_params=params(),
        cost_estimate=cost(2 * work * width, 6 * work),
        name="update",
    )(firsts, seconds, gate, row(center_gain), row(center_shift), out_weight, row(out_bias))


def solution(mesh):
    groups, chan, quarter = (mesh.shape[a] for a in ("groups", "chan", "quarter"))
    near = CHANNELS // BLOCK // quarter
    parts = chan // near
    split = Mesh(
        mesh.devices.reshape(groups, parts, near, quarter), ("groups", "part", "chan", "quarter")
    )
    rows = P(("groups", "part", "chan", "quarter"), None, None)
    return jax.shard_map(
        functools.partial(shards, parts),
        mesh=split,
        in_specs=(rows,) + (P(),) * 10,
        out_specs=rows,
        check_vma=False,
    )
```

time: 141 us -> 120 us (0.85)
  starting transfers between devices: 77.8 us -> 55 us
  waiting for transfers between devices: 38.6 us -> 22.9 us
  local copies, waits for them, and re-layouts: 2.9 us -> 17.3 us
  Pallas kernels: 20.3 us -> 23.5 us
    ppermute x31 -> x30, starting transfers between devices: 59.6 us -> 41 us  [send(): return lax.ppermute(values, everywhere, pairs)]
    unnamed x66 -> x136, local copies, waits for them, and re-layouts: 2.9 us -> 17.3 us
    all_to_all x3, waiting for transfers between devices: 9.55 us -> 0.01 us  [the longest x1 0.01 us: shards(): lax.all_to_all(early_right.reshape(devices, EARLY * BLOCK, k), everywhere...]
    ppermute x31 -> x30, waiting for transfers between devices: 29.1 us -> 22.9 us  [send(): return lax.ppermute(values, everywhere, pairs)]
    all_to_all x3, starting transfers between devices: 18.2 us -> 13.9 us  [the longest x1 7.3 us: shards(): lax.all_to_all(early_right.reshape(devices, EARLY * BLOCK, k), everywhere...]
    pallas_call x1, Pallas kernels: 0.91 us -> 3.65 us  [shards(): pl.pallas_call(gate_kernel, grid=(steps,), in_specs=[row_block, whole((wi...]
    pallas_call x5 -> x7, Pallas kernels: 19.4 us -> 19.8 us  [the longest x1 4.96 us: shards(): pl.pallas_call(left_kernel, grid=(steps,), in_specs=[row_block, whole((1,...]
  transfers between devices with their start and end apart: 34 -> 33, of which waited for: 11 -> 15; matrix products, arithmetic and copies ran while one was open for 0% -> 0% of each run, Pallas kernels for 4% -> 11%
where the time goes in v3:
time: 120 us; the launch traced here: 119 us
  starting transfers between devices  55 us (46%)
  Pallas kernels  23.5 us (20%)
  waiting for transfers between devices  22.9 us (19%)
  local copies, waits for them, and re-layouts  17.3 us (14%)
    ppermute x30, starting transfers between devices, send(): return lax.ppermute(values, everywhere, pairs)  41 us
    ppermute x30, waiting for transfers between devices, send(): return lax.ppermute(values, everywhere, pairs)  22.9 us
    unnamed x136, local copies, waits for them, and re-layouts  17.3 us
    all_to_all x1, starting transfers between devices, shards(): lax.all_to_all(early_right.reshape(devices, EARLY * BLOCK, k), everywhere...  7.3 us
    pallas_call x1, Pallas kernels, shards(): pl.pallas_call(left_kernel, grid=(steps,), in_specs=[row_block, whole((1,...  4.96 us
    pallas_call x1, Pallas kernels, shards(): pl.pallas_call(final_kernel, grid=(steps,), in_specs=[pl.BlockSpec((hosts...  4.15 us
    all_to_all x1, starting transfers between devices, shards(): seconds = lax.all_to_all(seconds, in_part, 0, 0, tiled=True)  3.9 us
    pallas_call x1, Pallas kernels, shards(): pl.pallas_call(early_kernel, grid=(EARLY // STEP,), in_specs=[row_block,...  3.75 us
  transfers between devices with their start and end apart: 33, of which 15 were waited for; matrix products, arithmetic and copies ran while one was open for 0% of the time, Pallas kernels for 11%

profile of v3, /device:TPU:0, one launch (start us, length us, event | category | flops | bytes accessed | tf_op | source)
XLA Modules:
  0.0 119.2 jit_solution(18030075567785583134)
XLA Ops:
  0.0 3.7 %early_right.1 = bf16[2,16,64,384]{3,2,1,0:T(8,128)(2,1)} custom-call(bf16[12,384,128]{2,1,0:T(8,128)(2,1)} %pair_ref.3, f32[1,128]{1,0:T(1,128)} %bitcast.21, f32[1,128]{1,0:T(1,128)} %bitcast.23, bf16[128,512]{1,0:T(8,128)(2,1)} %w_ref.6, f32[1,512]{1,0:T(1,128)} %bitcast.18), custom_call_target="tpu_custom_call" | custom-call | flops 301989888 | bytes 3538944 | tf_op jit(solution)/shard_map/early_right/pallas_call | solution.py:272
  3.7 7.3 %all-to-all-start = ((bf16[32,64,384]{2,1,0:T(8,128)(2,1)}), bf16[32,64,384]{2,1,0:T(8,128)(2,1)S(1)}, u32[]{:S(2)}, u32[]{:S(2)}) async-start(bf16[32,64,384]{2,1,0:T(8,128)(2,1)} %bitcast.16), calls=%async_computation | async-start | bytes 3145728 | tf_op jit(solution)/shard_map/all_to_all | solution.py:289
  11.1 5.0 %left_factor.1 = (bf16[96,384]{1,0:T(8,128)(2,1)}, bf16[96,384]{1,0:T(8,128)(2,1)}, bf16[96,384]{1,0:T(8,128)(2,1)}, bf16[96,384]{1,0:T(8,128)(2,1)}, bf16[96,38...) custom-call(bf16[12,384,128]{2,1,0:T(8,128)(2,1)} %pair_ref.3, ...), custom_call_target="tpu_custom_call" | custom-call | flops 301989888 | bytes 3538944 | tf_op jit(solution)/shard_map/left_factor/pallas_call | solution.py:299
  16.3 1.7 %collective-permute-start.1 = (bf16[96,384]{1,0:T(8,128)(2,1)}, bf16[96,384]{1,0:T(8,128)(2,1)S(1)}, u32[]{:S(2)}, u32[]{:S(2)}) collective-permute-start(bf16[96,384]{1,0:T(8,128)(2,1)} %get-tuple-element.41), channel_id=1, source_target_pairs={{0,2},{1,3},{2,0},{3,1},{4,6},{5,7},{6,4},{7,5},{8,10},{9,11},{10,... | collective-permute-start | bytes 221192 | tf_op jit(solution)/shard_map/ppermute | solution.py:297
  18.0 1.7 %collective-permute-start.3 = (bf16[96,384]{1,0:T(8,128)(2,1)}, bf16[96,384]{1,0:T(8,128)(2,1)S(1)}, u32[]{:S(2)}, u32[]{:S(2)}) collective-permute-start(bf16[96,384]{1,0:T(8,128)(2,1)} %get-tuple-element.43), channel_id=1, source_target_pairs={{0,4},{1,5},{2,6},{3,7},{4,0},{5,1},{6,2},{7,3},{8,12},{9,13},{10,... | collective-permute-start | bytes 221192 | tf_op jit(solution)/shard_map/ppermute | solution.py:297
  19.8 2.6 %collective-permute-start.5 = (bf16[96,384]{1,0:T(8,128)(2,1)}, bf16[96,384]{1,0:T(8,128)(2,1)S(1)}, u32[]{:S(2)}, u32[]{:S(2)}) collective-permute-start(bf16[96,384]{1,0:T(8,128)(2,1)} %get-tuple-element.45), channel_id=1, source_target_pairs={{0,6},{1,7},{2,4},{3,5},{4,2},{5,3},{6,0},{7,1},{8,14},{9,15},{10,... | collective-permute-start | bytes 221192 | tf_op jit(solution)/shard_map/ppermute | solution.py:297
  22.4 3.1 %collective-permute-done.1.refs_2_.refs_1_ = bf16[96,384]{1,0:T(8,128)(2,1)S(1)} collective-permute-done((bf16[96,384]{1,0:T(8,128)(2,1)}, bf16[96,384]{1,0:T(8,128)(2,1)S(1)}, u32[]{:S(2)}, u32[]{:S(2)}) %collective-permute-start.1) | collective-permute-done | bytes 73760 | tf_op jit(solution)/shard_map/ppermute | solution.py:297
  27.4 1.8 %collective-permute-start.8 = (bf16[96,384]{1,0:T(8,128)(2,1)}, bf16[96,384]{1,0:T(8,128)(2,1)S(1)}, u32[]{:S(2)}, u32[]{:S(2)}) collective-permute-start(bf16[96,384]{1,0:T(8,128)(2,1)} %get-tuple-element.48), channel_id=1, source_target_pairs={{0,9},{1,8},{2,11},{3,10},{4,13},{5,12},{6,15},{7,14},{8,1},{9,0},... | collective-permute-start | bytes 221192 | tf_op jit(solution)/shard_map/ppermute | solution.py:297
  29.3 1.0 collective-permute-done.4.refs_5_.refs_4_
  30.3 3.9 %collective-permute-start.9 = (bf16[96,384]{1,0:T(8,128)(2,1)}, bf16[96,384]{1,0:T(8,128)(2,1)S(1)}, u32[]{:S(2)}, u32[]{:S(2)}) collective-permute-start(bf16[96,384]{1,0:T(8,128)(2,1)} %get-tuple-element.49), channel_id=1, source_target_pairs={{0,10},{1,11},{2,8},{3,9},{4,14},{5,15},{6,12},{7,13},{8,2},{9,3},... | collective-permute-start | bytes 221192 | tf_op jit(solution)/shard_map/ppermute | solution.py:297
  35.0 1.6 %collective-permute-start.11 = (bf16[96,384]{1,0:T(8,128)(2,1)}, bf16[96,384]{1,0:T(8,128)(2,1)S(1)}, u32[]{:S(2)}, u32[]{:S(2)}) collective-permute-start(bf16[96,384]{1,0:T(8,128)(2,1)} %get-tuple-element.51), channel_id=1, source_target_pairs={{0,12},{1,13},{2,14},{3,15},{4,8},{5,9},{6,10},{7,11},{8,4},{9,5},... | collective-permute-start | bytes 221192 | tf_op jit(solution)/shard_map/ppermute | solution.py:297
  36.7 2.9 %collective-permute-done.7.refs_8_.refs_7_ = bf16[96,384]{1,0:T(8,128)(2,1)S(1)} collective-permute-done((bf16[96,384]{1,0:T(8,128)(2,1)}, bf16[96,384]{1,0:T(8,128)(2,1)S(1)}, u32[]{:S(2)}, u32[]{:S(2)}) %collective-permute-start.7) | collective-permute-done | bytes 73760 | tf_op jit(solution)/shard_map/ppermute | solution.py:297
  39.5 2.1 %collective-permute-start.12 = (bf16[96,384]{1,0:T(8,128)(2,1)}, bf16[96,384]{1,0:T(8,128)(2,1)S(1)}, u32[]{:S(2)}, u32[]{:S(2)}) collective-permute-start(bf16[96,384]{1,0:T(8,128)(2,1)} %get-tuple-element.52), channel_id=1, source_target_pairs={{0,13},{1,12},{2,15},{3,14},{4,9},{5,8},{6,11},{7,10},{8,5},{9,4},... | collective-permute-start | bytes 221192 | tf_op jit(solution)/shard_map/ppermute | solution.py:297
  41.6 2.7 %collective-permute-start.13 = (bf16[96,384]{1,0:T(8,128)(2,1)}, bf16[96,384]{1,0:T(8,128)(2,1)S(1)}, u32[]{:S(2)}, u32[]{:S(2)}) collective-permute-start(bf16[96,384]{1,0:T(8,128)(2,1)} %get-tuple-element.53), channel_id=1, source_target_pairs={{0,14},{1,15},{2,12},{3,13},{4,10},{5,11},{6,8},{7,9},{8,6},{9,7},... | collective-permute-start | bytes 221192 | tf_op jit(solution)/shard_map/ppermute | solution.py:297
  44.3 1.8 %collective-permute-start.14 = (bf16[96,384]{1,0:T(8,128)(2,1)}, bf16[96,384]{1,0:T(8,128)(2,1)S(1)}, u32[]{:S(2)}, u32[]{:S(2)}) collective-permute-start(bf16[96,384]{1,0:T(8,128)(2,1)} %get-tuple-element.54), channel_id=1, source_target_pairs={{0,15},{1,14},{2,13},{3,12},{4,11},{5,10},{6,9},{7,8},{8,7},{9,6},... | collective-permute-start | bytes 221192 | tf_op jit(solution)/shard_map/ppermute | solution.py:297
  46.1 1.5 %collective-permute-done.11.refs_12_.refs_11_ = bf16[96,384]{1,0:T(8,128)(2,1)S(1)} collective-permute-done((bf16[96,384]{1,0:T(8,128)(2,1)}, bf16[96,384]{1,0:T(8,128)(2,1)S(1)}, u32[]{:S(2)}, u32[]{:S(2)}) %collective-permute-start.11) | collective-permute-done | bytes 73760 | tf_op jit(solution)/shard_map/ppermute | solution.py:297
  47.6 3.0 %collective-permute-done.12.refs_13_.refs_12_ = bf16[96,384]{1,0:T(8,128)(2,1)S(1)} collective-permute-done((bf16[96,384]{1,0:T(8,128)(2,1)}, bf16[96,384]{1,0:T(8,128)(2,1)S(1)}, u32[]{:S(2)}, u32[]{:S(2)}) %collective-permute-start.12) | collective-permute-done | bytes 73760 | tf_op jit(solution)/shard_map/ppermute | solution.py:297
  50.6 2.7 %collective-permute-done.13.refs_14_.refs_13_ = bf16[96,384]{1,0:T(8,128)(2,1)S(1)} collective-permute-done((bf16[96,384]{1,0:T(8,128)(2,1)}, bf16[96,384]{1,0:T(8,128)(2,1)S(1)}, u32[]{:S(2)}, u32[]{:S(2)}) %collective-permute-start.13) | collective-permute-done | bytes 73760 | tf_op jit(solution)/shard_map/ppermute | solution.py:297
  53.3 1.8 %collective-permute-done.14.refs_15_.refs_14_ = bf16[96,384]{1,0:T(8,128)(2,1)S(1)} collective-permute-done((bf16[96,384]{1,0:T(8,128)(2,1)}, bf16[96,384]{1,0:T(8,128)(2,1)S(1)}, u32[]{:S(2)}, u32[]{:S(2)}) %collective-permute-start.14) | collective-permute-done | bytes 73760 | tf_op jit(solution)/shard_map/ppermute | solution.py:297
  55.7 2.4 %late_right.1 = bf16[2,16,32,384]{3,2,1,0:T(8,128)(2,1)} custom-call(bf16[12,384,128]{2,1,0:T(8,128)(2,1)} %get-tuple-element.71.normed_ref, bf16[128,512]{1,0:T(8,128)(2,1)} %w_ref.6, f32[1,512]{1,0:T(1,128)} %bitcast.20, bf16[96,384]{1,0:T(8,128)(2,1)} %copy-done.1, bf16[96,384]{1,0:T(8,128)(2,1)} %copy-done.3, bf16[96,384]{1,0:T(8,128)(2,1)} %copy-done.5, ...), custom_call_target="tpu_custom_call" | custom-call | flops 150994944 | bytes 1179648 | tf_op jit(solution)/shard_map/late_right/pallas_call | solution.py:323
  58.0 2.7 %all-to-all-start.1 = ((bf16[32,32,384]{2,1,0:T(8,128)(2,1)}), bf16[32,32,384]{2,1,0:T(8,128)(2,1)S(1)}, u32[]{:S(2)}, u32[]{:S(2)}) async-start(bf16[32,32,384]{2,1,0:T(8,128)(2,1)} %bitcast.17), calls=%async_computation.1 | async-start | bytes 1572864 | tf_op jit(solution)/shard_map/all_to_all | solution.py:338
  61.7 0.9 copy-done.4
  62.6 0.9 copy-done.6
  63.5 0.9 copy-done.8
  64.3 0.9 copy-done.10
  65.2 0.9 copy-done.12
  66.1 0.9 copy-done.14
  67.0 0.9 copy-done.16
  67.9 0.9 copy-done.18
  72.3 0.9 copy-done.28
  73.2 0.9 copy-done.30
  75.0 2.6 %first_products.1 = (bf16[96,256]{1,0:T(8,128)(2,1)S(1)}, bf16[96,256]{1,0:T(8,128)(2,1)S(1)}, bf16[96,256]{1,0:T(8,128)(2,1)S(1)}, bf16[96,256]{1,0:T(8,128)(2,...) custom-call(bf16[2048,384]{1,0:T(8,128)(2,1)S(1)} %bitcast.11, ...), custom_call_target="tpu_custom_call" | custom-call | flops 226492416 | bytes 3538944 | tf_op jit(solution)/shard_map/first_products/pallas_call | solution.py:356
  80.3 1.7 %collective-permute-start.16 = (bf16[96,256]{1,0:T(8,128)(2,1)S(1)}, bf16[96,256]{1,0:T(8,128)(2,1)S(1)}, u32[]{:S(2)}, u32[]{:S(2)}) collective-permute-start(bf16[96,256]{1,0:T(8,128)(2,1)S(1)} %get-tuple-element.57), channel_id=1, source_target_pairs={{0,2},{1,3},{2,0},{3,1},{4,6},{5,7},{6,4},{7,5},{8,10},{9,11},{10,... | collective-permute-start | bytes 147464 | tf_op jit(solution)/shard_map/ppermute | solution.py:297
  82.0 1.7 %collective-permute-start.18 = (bf16[96,256]{1,0:T(8,128)(2,1)S(1)}, bf16[96,256]{1,0:T(8,128)(2,1)S(1)}, u32[]{:S(2)}, u32[]{:S(2)}) collective-permute-start(bf16[96,256]{1,0:T(8,128)(2,1)S(1)} %get-tuple-element.59), channel_id=1, source_target_pairs={{0,4},{1,5},{2,6},{3,7},{4,0},{5,1},{6,2},{7,3},{8,12},{9,13},{10,... | collective-permute-start | bytes 147464 | tf_op jit(solution)/shard_map/ppermute | solution.py:297
  83.8 2.6 %collective-permute-start.20 = (bf16[96,256]{1,0:T(8,128)(2,1)S(1)}, bf16[96,256]{1,0:T(8,128)(2,1)S(1)}, u32[]{:S(2)}, u32[]{:S(2)}) collective-permute-start(bf16[96,256]{1,0:T(8,128)(2,1)S(1)} %get-tuple-element.61), channel_id=1, source_target_pairs={{0,6},{1,7},{2,4},{3,5},{4,2},{5,3},{6,0},{7,1},{8,14},{9,15},{10,... | collective-permute-start | bytes 147464 | tf_op jit(solution)/shard_map/ppermute | solution.py:297
  86.4 1.7 %collective-permute-start.22 = (bf16[96,256]{1,0:T(8,128)(2,1)}, bf16[96,256]{1,0:T(8,128)(2,1)S(1)}, u32[]{:S(2)}, u32[]{:S(2)}) collective-permute-start(bf16[96,256]{1,0:T(8,128)(2,1)} %get-tuple-element.63), channel_id=1, source_target_pairs={{0,8},{1,9},{2,10},{3,11},{4,12},{5,13},{6,14},{7,15},{8,0},{9,1},... | collective-permute-start | bytes 147464 | tf_op jit(solution)/shard_map/ppermute | solution.py:297
  89.0 1.8 %collective-permute-start.24 = (bf16[96,256]{1,0:T(8,128)(2,1)}, bf16[96,256]{1,0:T(8,128)(2,1)S(1)}, u32[]{:S(2)}, u32[]{:S(2)}) collective-permute-start(bf16[96,256]{1,0:T(8,128)(2,1)} %get-tuple-element.65), channel_id=1, source_target_pairs={{0,10},{1,11},{2,8},{3,9},{4,14},{5,15},{6,12},{7,13},{8,2},{9,3},... | collective-permute-start | bytes 147464 | tf_op jit(solution)/shard_map/ppermute | solution.py:297
  91.1 2.3 %collective-permute-start.26 = (bf16[96,256]{1,0:T(8,128)(2,1)}, bf16[96,256]{1,0:T(8,128)(2,1)S(1)}, u32[]{:S(2)}, u32[]{:S(2)}) collective-permute-start(bf16[96,256]{1,0:T(8,128)(2,1)} %get-tuple-element.67), channel_id=1, source_target_pairs={{0,12},{1,13},{2,14},{3,15},{4,8},{5,9},{6,10},{7,11},{8,4},{9,5},... | collective-permute-start | bytes 147464 | tf_op jit(solution)/shard_map/ppermute | solution.py:297
  94.3 1.4 %collective-permute-done.25.refs_11_.refs_10_ = bf16[96,256]{1,0:T(8,128)(2,1)S(1)} collective-permute-done((bf16[96,256]{1,0:T(8,128)(2,1)}, bf16[96,256]{1,0:T(8,128)(2,1)S(1)}, u32[]{:S(2)}, u32[]{:S(2)}) %collective-permute-start.25) | collective-permute-done | bytes 49184 | tf_op jit(solution)/shard_map/ppermute | solution.py:297
  95.7 1.3 %collective-permute-done.26.refs_12_.refs_11_ = bf16[96,256]{1,0:T(8,128)(2,1)S(1)} collective-permute-done((bf16[96,256]{1,0:T(8,128)(2,1)}, bf16[96,256]{1,0:T(8,128)(2,1)S(1)}, u32[]{:S(2)}, u32[]{:S(2)}) %collective-permute-start.26) | collective-permute-done | bytes 49184 | tf_op jit(solution)/shard_map/ppermute | solution.py:297
  97.0 1.9 %second_products.1 = bf16[16,96,128]{2,1,0:T(8,128)(2,1)} custom-call(bf16[1024,384]{1,0:T(8,128)(2,1)S(1)} %bitcast.12, bf16[8,192,384]{2,1,0:T(8,128)(2,1)S(1)} %get-tuple-element.72.left, bf16[96,256]{1,0:T(8,128)(2,1)S(1)} %collective-permute-done.15.refs_1_.refs_0_, bf16[96,256]{1,0:T(8,128)(2,1)S(1)} %collective-permute-done.16.refs_2_.refs_1_, ...), custom_call_target="tpu_custom_call" | custom-call | flops 226492416 | bytes 3538944 | tf_op jit(solution)/shard_map/second_products/pallas_call | solution.py:370
  99.1 3.9 %all-to-all-start.2 = ((bf16[16,96,128]{2,1,0:T(8,128)(2,1)}), bf16[16,96,128]{2,1,0:T(8,128)(2,1)S(1)}, u32[]{:S(2)}, u32[]{:S(2)}) async-start(bf16[16,96,128]{2,1,0:T(8,128)(2,1)} %second_products.1), calls=%async_computation.2 | async-start | bytes 786432 | tf_op jit(solution)/shard_map/all_to_all | solution.py:382
  103.0 2.6 %collective-permute-start.27 = (bf16[96,256]{1,0:T(8,128)(2,1)S(1)}, bf16[96,256]{1,0:T(8,128)(2,1)S(1)}, u32[]{:S(2)}, u32[]{:S(2)}) collective-permute-start(bf16[96,256]{1,0:T(8,128)(2,1)S(1)} %copy-done.67), channel_id=1, source_target_pairs={{0,13},{1,12},{2,15},{3,14},{4,9},{5,8},{6,11},{7,10},{8,5},{9,4},... | collective-permute-start | bytes 147464 | tf_op jit(solution)/shard_map/ppermute | solution.py:297
  105.6 1.5 %collective-permute-start.28 = (bf16[96,256]{1,0:T(8,128)(2,1)S(1)}, bf16[96,256]{1,0:T(8,128)(2,1)S(1)}, u32[]{:S(2)}, u32[]{:S(2)}) collective-permute-start(bf16[96,256]{1,0:T(8,128)(2,1)S(1)} %copy-done.65), channel_id=1, source_target_pairs={{0,14},{1,15},{2,12},{3,13},{4,10},{5,11},{6,8},{7,9},{8,6},{9,7},... | collective-permute-start | bytes 147464 | tf_op jit(solution)/shard_map/ppermute | solution.py:297
  107.1 2.0 %collective-permute-start.29 = (bf16[96,256]{1,0:T(8,128)(2,1)S(1)}, bf16[96,256]{1,0:T(8,128)(2,1)S(1)}, u32[]{:S(2)}, u32[]{:S(2)}) collective-permute-start(bf16[96,256]{1,0:T(8,128)(2,1)S(1)} %copy-done.63), channel_id=1, source_target_pairs={{0,15},{1,14},{2,13},{3,12},{4,11},{5,10},{6,9},{7,8},{8,7},{9,6},... | collective-permute-start | bytes 147464 | tf_op jit(solution)/shard_map/ppermute | solution.py:297
  109.2 3.7 %gate.1.gate_ref = bf16[12,384,128]{2,1,0:T(8,128)(2,1)} custom-call(bf16[12,384,128]{2,1,0:T(8,128)(2,1)} %get-tuple-element.71.normed_ref, bf16[128,128]{1,0:T(8,128)(2,1)} %gw_ref.1, f32[1,128]{1,0:T(1,128)} %bitcast.25), custom_call_target="tpu_custom_call" | custom-call | flops 150994944 | bytes 2359296 | tf_op jit(solution)/shard_map/gate/pallas_call | solution.py:342
  112.9 1.8 %collective-permute-done.28.refs_14_ = bf16[96,256]{1,0:T(8,128)(2,1)S(1)} collective-permute-done((bf16[96,256]{1,0:T(8,128)(2,1)S(1)}, bf16[96,256]{1,0:T(8,128)(2,1)S(1)}, u32[]{:S(2)}, u32[]{:S(2)}) %collective-permute-start.28) | collective-permute-done | bytes 49184 | tf_op jit(solution)/shard_map/ppermute | solution.py:297
  115.0 4.2 %update.1 = bf16[12,384,128]{2,1,0:T(8,128)(2,1)} custom-call(bf16[16,96,256]{2,1,0:T(8,128)(2,1)S(1)} %collect.1.first_ref, bf16[16,96,128]{2,1,0:T(8,128)(2,1)S(1)} %all-to-all-done.2.second_ref, bf16[12,384,128]{2,1,0:T(8,128)(2,1)S(1)} %copy-done, f32[1,128]{1,0:T(1,128)S(1)} %bitcast.13, f32[1,128]{1,0:T(1,128)S(1)} %bitcast.14, ...), custom_call_target="tpu_custom_call" | custom-call | flops 150994944 | bytes 3538944 | tf_op jit(solution)/shard_map/update/pallas_call | solution.py:395
  (162 shorter events, 14.3 us)
Async XLA Ops:
  3.7 54.3 %all-to-all-start = ((bf16[32,64,384]{2,1,0:T(8,128)(2,1)}), bf16[32,64,384]{2,1,0:T(8,128)(2,1)S(1)}, u32[]{:S(2)}, u32[]{:S(2)}) async-start(bf16[32,64,384]{2,1,0:T(8,128)(2,1)} %bitcast.16), calls=%async_computation | async-start | bytes 3145728 | tf_op jit(solution)/shard_map/all_to_all | solution.py:289
  16.0 3.8 %collective-permute-start = (bf16[96,384]{1,0:T(8,128)(2,1)}, bf16[96,384]{1,0:T(8,128)(2,1)S(1)}, u32[]{:S(2)}, u32[]{:S(2)}) collective-permute-start(bf16[96,384]{1,0:T(8,128)(2,1)} %get-tuple-element.40), channel_id=1, source_target_pairs={{0,1},{1,0},{2,3},{3,2},{4,5},{5,4},{6,7},{7,6},{8,9},{9,8},{10,11... | collective-permute-start | bytes 221192 | tf_op jit(solution)/shard_map/ppermute | solution.py:297
  16.3 9.2 %collective-permute-start.1 = (bf16[96,384]{1,0:T(8,128)(2,1)}, bf16[96,384]{1,0:T(8,128)(2,1)S(1)}, u32[]{:S(2)}, u32[]{:S(2)}) collective-permute-start(bf16[96,384]{1,0:T(8,128)(2,1)} %get-tuple-element.41), channel_id=1, source_target_pairs={{0,2},{1,3},{2,0},{3,1},{4,6},{5,7},{6,4},{7,5},{8,10},{9,11},{10,... | collective-permute-start | bytes 221192 | tf_op jit(solution)/shard_map/ppermute | solution.py:297
  18.0 8.8 %collective-permute-start.2 = (bf16[96,384]{1,0:T(8,128)(2,1)}, bf16[96,384]{1,0:T(8,128)(2,1)S(1)}, u32[]{:S(2)}, u32[]{:S(2)}) collective-permute-start(bf16[96,384]{1,0:T(8,128)(2,1)} %get-tuple-element.42), channel_id=1, source_target_pairs={{0,3},{1,2},{2,1},{3,0},{4,7},{5,6},{6,5},{7,4},{8,11},{9,10},{10,... | collective-permute-start | bytes 221192 | tf_op jit(solution)/shard_map/ppermute | solution.py:297
  18.0 9.4 %collective-permute-start.3 = (bf16[96,384]{1,0:T(8,128)(2,1)}, bf16[96,384]{1,0:T(8,128)(2,1)S(1)}, u32[]{:S(2)}, u32[]{:S(2)}) collective-permute-start(bf16[96,384]{1,0:T(8,128)(2,1)} %get-tuple-element.43), channel_id=1, source_target_pairs={{0,4},{1,5},{2,6},{3,7},{4,0},{5,1},{6,2},{7,3},{8,12},{9,13},{10,... | collective-permute-start | bytes 221192 | tf_op jit(solution)/shard_map/ppermute | solution.py:297
  19.7 10.6 %collective-permute-start.4 = (bf16[96,384]{1,0:T(8,128)(2,1)}, bf16[96,384]{1,0:T(8,128)(2,1)S(1)}, u32[]{:S(2)}, u32[]{:S(2)}) collective-permute-start(bf16[96,384]{1,0:T(8,128)(2,1)} %get-tuple-element.44), channel_id=1, source_target_pairs={{0,5},{1,4},{2,7},{3,6},{4,1},{5,0},{6,3},{7,2},{8,13},{9,12},{10,... | collective-permute-start | bytes 221192 | tf_op jit(solution)/shard_map/ppermute | solution.py:297
  19.8 35.2 %copy-start.1 = (bf16[96,384]{1,0:T(8,128)(2,1)}, bf16[96,384]{1,0:T(8,128)(2,1)S(1)}, u32[]{:S(2)}) copy-start(bf16[96,384]{1,0:T(8,128)(2,1)S(1)} %collective-permute-done.refs_1_.refs_0_) | copy-start | bytes 221188
  19.8 14.4 %collective-permute-start.5 = (bf16[96,384]{1,0:T(8,128)(2,1)}, bf16[96,384]{1,0:T(8,128)(2,1)S(1)}, u32[]{:S(2)}, u32[]{:S(2)}) collective-permute-start(bf16[96,384]{1,0:T(8,128)(2,1)} %get-tuple-element.45), channel_id=1, source_target_pairs={{0,6},{1,7},{2,4},{3,5},{4,2},{5,3},{6,0},{7,1},{8,14},{9,15},{10,... | collective-permute-start | bytes 221192 | tf_op jit(solution)/shard_map/ppermute | solution.py:297
  25.5 29.5 %copy-start.3 = (bf16[96,384]{1,0:T(8,128)(2,1)}, bf16[96,384]{1,0:T(8,128)(2,1)S(1)}, u32[]{:S(2)}) copy-start(bf16[96,384]{1,0:T(8,128)(2,1)S(1)} %collective-permute-done.1.refs_2_.refs_1_) | copy-start | bytes 221188
  25.6 9.5 %collective-permute-start.6 = (bf16[96,384]{1,0:T(8,128)(2,1)}, bf16[96,384]{1,0:T(8,128)(2,1)S(1)}, u32[]{:S(2)}, u32[]{:S(2)}) collective-permute-start(bf16[96,384]{1,0:T(8,128)(2,1)} %get-tuple-element.46), channel_id=1, source_target_pairs={{0,7},{1,6},{2,5},{3,4},{4,3},{5,2},{6,1},{7,0},{8,15},{9,14},{10,... | collective-permute-start | bytes 221192 | tf_op jit(solution)/shard_map/ppermute | solution.py:297
  26.8 28.2 %copy-start.5 = (bf16[96,384]{1,0:T(8,128)(2,1)}, bf16[96,384]{1,0:T(8,128)(2,1)S(1)}, u32[]{:S(2)}) copy-start(bf16[96,384]{1,0:T(8,128)(2,1)S(1)} %collective-permute-done.2.refs_3_.refs_2_) | copy-start | bytes 221188
  26.8 12.7 %collective-permute-start.7 = (bf16[96,384]{1,0:T(8,128)(2,1)}, bf16[96,384]{1,0:T(8,128)(2,1)S(1)}, u32[]{:S(2)}, u32[]{:S(2)}) collective-permute-start(bf16[96,384]{1,0:T(8,128)(2,1)} %get-tuple-element.47), channel_id=1, source_target_pairs={{0,8},{1,9},{2,10},{3,11},{4,12},{5,13},{6,14},{7,15},{8,0},{9,1},... | collective-permute-start | bytes 221192 | tf_op jit(solution)/shard_map/ppermute | solution.py:297
  27.4 27.6 %copy-start.7 = (bf16[96,384]{1,0:T(8,128)(2,1)}, bf16[96,384]{1,0:T(8,128)(2,1)S(1)}, u32[]{:S(2)}) copy-start(bf16[96,384]{1,0:T(8,128)(2,1)S(1)} %collective-permute-done.3.refs_4_.refs_3_) | copy-start | bytes 221188
  27.4 14.2 %collective-permute-start.8 = (bf16[96,384]{1,0:T(8,128)(2,1)}, bf16[96,384]{1,0:T(8,128)(2,1)S(1)}, u32[]{:S(2)}, u32[]{:S(2)}) collective-permute-start(bf16[96,384]{1,0:T(8,128)(2,1)} %get-tuple-element.48), channel_id=1, source_target_pairs={{0,9},{1,8},{2,11},{3,10},{4,13},{5,12},{6,15},{7,14},{8,1},{9,0},... | collective-permute-start | bytes 221192 | tf_op jit(solution)/shard_map/ppermute | solution.py:297
  30.3 24.8 %copy-start.9 = (bf16[96,384]{1,0:T(8,128)(2,1)}, bf16[96,384]{1,0:T(8,128)(2,1)S(1)}, u32[]{:S(2)}) copy-start(bf16[96,384]{1,0:T(8,128)(2,1)S(1)} %collective-permute-done.4.refs_5_.refs_4_) | copy-start | bytes 221188
  30.3 14.0 %collective-permute-start.9 = (bf16[96,384]{1,0:T(8,128)(2,1)}, bf16[96,384]{1,0:T(8,128)(2,1)S(1)}, u32[]{:S(2)}, u32[]{:S(2)}) collective-permute-start(bf16[96,384]{1,0:T(8,128)(2,1)} %get-tuple-element.49), channel_id=1, source_target_pairs={{0,10},{1,11},{2,8},{3,9},{4,14},{5,15},{6,12},{7,13},{8,2},{9,3},... | collective-permute-start | bytes 221192 | tf_op jit(solution)/shard_map/ppermute | solution.py:297
  34.2 20.9 %copy-start.11 = (bf16[96,384]{1,0:T(8,128)(2,1)}, bf16[96,384]{1,0:T(8,128)(2,1)S(1)}, u32[]{:S(2)}) copy-start(bf16[96,384]{1,0:T(8,128)(2,1)S(1)} %collective-permute-done.5.refs_6_.refs_5_) | copy-start | bytes 221188
  34.2 11.9 %collective-permute-start.10 = (bf16[96,384]{1,0:T(8,128)(2,1)}, bf16[96,384]{1,0:T(8,128)(2,1)S(1)}, u32[]{:S(2)}, u32[]{:S(2)}) collective-permute-start(bf16[96,384]{1,0:T(8,128)(2,1)} %get-tuple-element.50), channel_id=1, source_target_pairs={{0,11},{1,10},{2,9},{3,8},{4,15},{5,14},{6,13},{7,12},{8,3},{9,2},... | collective-permute-start | bytes 221192 | tf_op jit(solution)/shard_map/ppermute | solution.py:297
  35.0 20.1 %copy-start.13 = (bf16[96,384]{1,0:T(8,128)(2,1)}, bf16[96,384]{1,0:T(8,128)(2,1)S(1)}, u32[]{:S(2)}) copy-start(bf16[96,384]{1,0:T(8,128)(2,1)S(1)} %collective-permute-done.6.refs_7_.refs_6_) | copy-start | bytes 221188
  35.0 12.6 %collective-permute-start.11 = (bf16[96,384]{1,0:T(8,128)(2,1)}, bf16[96,384]{1,0:T(8,128)(2,1)S(1)}, u32[]{:S(2)}, u32[]{:S(2)}) collective-permute-start(bf16[96,384]{1,0:T(8,128)(2,1)} %get-tuple-element.51), channel_id=1, source_target_pairs={{0,12},{1,13},{2,14},{3,15},{4,8},{5,9},{6,10},{7,11},{8,4},{9,5},... | collective-permute-start | bytes 221192 | tf_op jit(solution)/shard_map/ppermute | solution.py:297
  39.5 15.6 %copy-start.15 = (bf16[96,384]{1,0:T(8,128)(2,1)}, bf16[96,384]{1,0:T(8,128)(2,1)S(1)}, u32[]{:S(2)}) copy-start(bf16[96,384]{1,0:T(8,128)(2,1)S(1)} %collective-permute-done.7.refs_8_.refs_7_) | copy-start | bytes 221188
  39.5 11.0 %collective-permute-start.12 = (bf16[96,384]{1,0:T(8,128)(2,1)}, bf16[96,384]{1,0:T(8,128)(2,1)S(1)}, u32[]{:S(2)}, u32[]{:S(2)}) collective-permute-start(bf16[96,384]{1,0:T(8,128)(2,1)} %get-tuple-element.52), channel_id=1, source_target_pairs={{0,13},{1,12},{2,15},{3,14},{4,9},{5,8},{6,11},{7,10},{8,5},{9,4},... | collective-permute-start | bytes 221192 | tf_op jit(solution)/shard_map/ppermute | solution.py:297
  41.6 13.5 %copy-start.17 = (bf16[96,384]{1,0:T(8,128)(2,1)}, bf16[96,384]{1,0:T(8,128)(2,1)S(1)}, u32[]{:S(2)}) copy-start(bf16[96,384]{1,0:T(8,128)(2,1)S(1)} %collective-permute-done.8.refs_9_.refs_8_) | copy-start | bytes 221188
  41.6 11.7 %collective-permute-start.13 = (bf16[96,384]{1,0:T(8,128)(2,1)}, bf16[96,384]{1,0:T(8,128)(2,1)S(1)}, u32[]{:S(2)}, u32[]{:S(2)}) collective-permute-start(bf16[96,384]{1,0:T(8,128)(2,1)} %get-tuple-element.53), channel_id=1, source_target_pairs={{0,14},{1,15},{2,12},{3,13},{4,10},{5,11},{6,8},{7,9},{8,6},{9,7},... | collective-permute-start | bytes 221192 | tf_op jit(solution)/shard_map/ppermute | solution.py:297
  44.3 10.8 %copy-start.19 = (bf16[96,384]{1,0:T(8,128)(2,1)}, bf16[96,384]{1,0:T(8,128)(2,1)S(1)}, u32[]{:S(2)}) copy-start(bf16[96,384]{1,0:T(8,128)(2,1)S(1)} %collective-permute-done.9.refs_10_.refs_9_) | copy-start | bytes 221188
  44.3 10.8 %collective-permute-start.14 = (bf16[96,384]{1,0:T(8,128)(2,1)}, bf16[96,384]{1,0:T(8,128)(2,1)S(1)}, u32[]{:S(2)}, u32[]{:S(2)}) collective-permute-start(bf16[96,384]{1,0:T(8,128)(2,1)} %get-tuple-element.54), channel_id=1, source_target_pairs={{0,15},{1,14},{2,13},{3,12},{4,11},{5,10},{6,9},{7,8},{8,7},{9,6},... | collective-permute-start | bytes 221192 | tf_op jit(solution)/shard_map/ppermute | solution.py:297
  58.0 35.4 %all-to-all-start.1 = ((bf16[32,32,384]{2,1,0:T(8,128)(2,1)}), bf16[32,32,384]{2,1,0:T(8,128)(2,1)S(1)}, u32[]{:S(2)}, u32[]{:S(2)}) async-start(bf16[32,32,384]{2,1,0:T(8,128)(2,1)} %bitcast.17), calls=%async_computation.1 | async-start | bytes 1572864 | tf_op jit(solution)/shard_map/all_to_all | solution.py:338
  80.0 3.8 %collective-permute-start.15 = (bf16[96,256]{1,0:T(8,128)(2,1)S(1)}, bf16[96,256]{1,0:T(8,128)(2,1)S(1)}, u32[]{:S(2)}, u32[]{:S(2)}) collective-permute-start(bf16[96,256]{1,0:T(8,128)(2,1)S(1)} %get-tuple-element.56), channel_id=1, source_target_pairs={{0,1},{1,0},{2,3},{3,2},{4,5},{5,4},{6,7},{7,6},{8,9},{9,8},{10,11... | collective-permute-start | bytes 147464 | tf_op jit(solution)/shard_map/ppermute | solution.py:297
  80.3 6.1 %collective-permute-start.16 = (bf16[96,256]{1,0:T(8,128)(2,1)S(1)}, bf16[96,256]{1,0:T(8,128)(2,1)S(1)}, u32[]{:S(2)}, u32[]{:S(2)}) collective-permute-start(bf16[96,256]{1,0:T(8,128)(2,1)S(1)} %get-tuple-element.57), channel_id=1, source_target_pairs={{0,2},{1,3},{2,0},{3,1},{4,6},{5,7},{6,4},{7,5},{8,10},{9,11},{10,... | collective-permute-start | bytes 147464 | tf_op jit(solution)/shard_map/ppermute | solution.py:297
  82.0 4.4 %collective-permute-start.17 = (bf16[96,256]{1,0:T(8,128)(2,1)S(1)}, bf16[96,256]{1,0:T(8,128)(2,1)S(1)}, u32[]{:S(2)}, u32[]{:S(2)}) collective-permute-start(bf16[96,256]{1,0:T(8,128)(2,1)S(1)} %get-tuple-element.58), channel_id=1, source_target_pairs={{0,3},{1,2},{2,1},{3,0},{4,7},{5,6},{6,5},{7,4},{8,11},{9,10},{10,... | collective-permute-start | bytes 147464 | tf_op jit(solution)/shard_map/ppermute | solution.py:297
  82.0 6.1 %collective-permute-start.18 = (bf16[96,256]{1,0:T(8,128)(2,1)S(1)}, bf16[96,256]{1,0:T(8,128)(2,1)S(1)}, u32[]{:S(2)}, u32[]{:S(2)}) collective-permute-start(bf16[96,256]{1,0:T(8,128)(2,1)S(1)} %get-tuple-element.59), channel_id=1, source_target_pairs={{0,4},{1,5},{2,6},{3,7},{4,0},{5,1},{6,2},{7,3},{8,12},{9,13},{10,... | collective-permute-start | bytes 147464 | tf_op jit(solution)/shard_map/ppermute | solution.py:297
  83.7 5.3 %collective-permute-start.19 = (bf16[96,256]{1,0:T(8,128)(2,1)S(1)}, bf16[96,256]{1,0:T(8,128)(2,1)S(1)}, u32[]{:S(2)}, u32[]{:S(2)}) collective-permute-start(bf16[96,256]{1,0:T(8,128)(2,1)S(1)} %get-tuple-element.60), channel_id=1, source_target_pairs={{0,5},{1,4},{2,7},{3,6},{4,1},{5,0},{6,3},{7,2},{8,13},{9,12},{10,... | collective-permute-start | bytes 147464 | tf_op jit(solution)/shard_map/ppermute | solution.py:297
  83.8 15.2 %copy-start.31 = (bf16[96,256]{1,0:T(8,128)(2,1)}, bf16[96,256]{1,0:T(8,128)(2,1)S(1)}, u32[]{:S(2)}) copy-start(bf16[96,256]{1,0:T(8,128)(2,1)S(1)} %collective-permute-done.15.refs_1_.refs_0_) | copy-start | bytes 147460
  83.8 7.0 %collective-permute-start.20 = (bf16[96,256]{1,0:T(8,128)(2,1)S(1)}, bf16[96,256]{1,0:T(8,128)(2,1)S(1)}, u32[]{:S(2)}, u32[]{:S(2)}) collective-permute-start(bf16[96,256]{1,0:T(8,128)(2,1)S(1)} %get-tuple-element.61), channel_id=1, source_target_pairs={{0,6},{1,7},{2,4},{3,5},{4,2},{5,3},{6,0},{7,1},{8,14},{9,15},{10,... | collective-permute-start | bytes 147464 | tf_op jit(solution)/shard_map/ppermute | solution.py:297
  86.4 12.6 %copy-start.33 = (bf16[96,256]{1,0:T(8,128)(2,1)}, bf16[96,256]{1,0:T(8,128)(2,1)S(1)}, u32[]{:S(2)}) copy-start(bf16[96,256]{1,0:T(8,128)(2,1)S(1)} %collective-permute-done.16.refs_2_.refs_1_) | copy-start | bytes 147460
  86.4 4.8 %collective-permute-start.21 = (bf16[96,256]{1,0:T(8,128)(2,1)S(1)}, bf16[96,256]{1,0:T(8,128)(2,1)S(1)}, u32[]{:S(2)}, u32[]{:S(2)}) collective-permute-start(bf16[96,256]{1,0:T(8,128)(2,1)S(1)} %get-tuple-element.62), channel_id=1, source_target_pairs={{0,7},{1,6},{2,5},{3,4},{4,3},{5,2},{6,1},{7,0},{8,15},{9,14},{10,... | collective-permute-start | bytes 147464 | tf_op jit(solution)/shard_map/ppermute | solution.py:297
  86.4 12.5 %copy-start.35 = (bf16[96,256]{1,0:T(8,128)(2,1)}, bf16[96,256]{1,0:T(8,128)(2,1)S(1)}, u32[]{:S(2)}) copy-start(bf16[96,256]{1,0:T(8,128)(2,1)S(1)} %collective-permute-done.17.refs_3_.refs_2_) | copy-start | bytes 147460
  86.4 7.0 %collective-permute-start.22 = (bf16[96,256]{1,0:T(8,128)(2,1)}, bf16[96,256]{1,0:T(8,128)(2,1)S(1)}, u32[]{:S(2)}, u32[]{:S(2)}) collective-permute-start(bf16[96,256]{1,0:T(8,128)(2,1)} %get-tuple-element.63), channel_id=1, source_target_pairs={{0,8},{1,9},{2,10},{3,11},{4,12},{5,13},{6,14},{7,15},{8,0},{9,1},... | collective-permute-start | bytes 147464 | tf_op jit(solution)/shard_map/ppermute | solution.py:297
  88.1 10.9 %copy-start.37 = (bf16[96,256]{1,0:T(8,128)(2,1)}, bf16[96,256]{1,0:T(8,128)(2,1)S(1)}, u32[]{:S(2)}) copy-start(bf16[96,256]{1,0:T(8,128)(2,1)S(1)} %collective-permute-done.18.refs_4_.refs_3_) | copy-start | bytes 147460
  88.1 5.3 %collective-permute-start.23 = (bf16[96,256]{1,0:T(8,128)(2,1)}, bf16[96,256]{1,0:T(8,128)(2,1)S(1)}, u32[]{:S(2)}, u32[]{:S(2)}) collective-permute-start(bf16[96,256]{1,0:T(8,128)(2,1)} %get-tuple-element.64), channel_id=1, source_target_pairs={{0,9},{1,8},{2,11},{3,10},{4,13},{5,12},{6,15},{7,14},{8,1},{9,0},... | collective-permute-start | bytes 147464 | tf_op jit(solution)/shard_map/ppermute | solution.py:297
  89.0 5.3 %collective-permute-start.24 = (bf16[96,256]{1,0:T(8,128)(2,1)}, bf16[96,256]{1,0:T(8,128)(2,1)S(1)}, u32[]{:S(2)}, u32[]{:S(2)}) collective-permute-start(bf16[96,256]{1,0:T(8,128)(2,1)} %get-tuple-element.65), channel_id=1, source_target_pairs={{0,10},{1,11},{2,8},{3,9},{4,14},{5,15},{6,12},{7,13},{8,2},{9,3},... | collective-permute-start | bytes 147464 | tf_op jit(solution)/shard_map/ppermute | solution.py:297
  90.8 4.9 %collective-permute-start.25 = (bf16[96,256]{1,0:T(8,128)(2,1)}, bf16[96,256]{1,0:T(8,128)(2,1)S(1)}, u32[]{:S(2)}, u32[]{:S(2)}) collective-permute-start(bf16[96,256]{1,0:T(8,128)(2,1)} %get-tuple-element.66), channel_id=1, source_target_pairs={{0,11},{1,10},{2,9},{3,8},{4,15},{5,14},{6,13},{7,12},{8,3},{9,2},... | collective-permute-start | bytes 147464 | tf_op jit(solution)/shard_map/ppermute | solution.py:297
  91.1 5.9 %collective-permute-start.26 = (bf16[96,256]{1,0:T(8,128)(2,1)}, bf16[96,256]{1,0:T(8,128)(2,1)S(1)}, u32[]{:S(2)}, u32[]{:S(2)}) collective-permute-start(bf16[96,256]{1,0:T(8,128)(2,1)} %get-tuple-element.67), channel_id=1, source_target_pairs={{0,12},{1,13},{2,14},{3,15},{4,8},{5,9},{6,10},{7,11},{8,4},{9,5},... | collective-permute-start | bytes 147464 | tf_op jit(solution)/shard_map/ppermute | solution.py:297
  97.0 10.1 %copy-start.63 = (bf16[96,256]{1,0:T(8,128)(2,1)S(1)}, bf16[96,256]{1,0:T(8,128)(2,1)}, u32[]{:S(2)}) copy-start(bf16[96,256]{1,0:T(8,128)(2,1)} %copy-done.62) | copy-start | bytes 147460
  99.1 15.9 %all-to-all-start.2 = ((bf16[16,96,128]{2,1,0:T(8,128)(2,1)}), bf16[16,96,128]{2,1,0:T(8,128)(2,1)S(1)}, u32[]{:S(2)}, u32[]{:S(2)}) async-start(bf16[16,96,128]{2,1,0:T(8,128)(2,1)} %second_products.1), calls=%async_computation.2 | async-start | bytes 786432 | tf_op jit(solution)/shard_map/all_to_all | solution.py:382
  103.0 10.0 %collective-permute-start.27 = (bf16[96,256]{1,0:T(8,128)(2,1)S(1)}, bf16[96,256]{1,0:T(8,128)(2,1)S(1)}, u32[]{:S(2)}, u32[]{:S(2)}) collective-permute-start(bf16[96,256]{1,0:T(8,128)(2,1)S(1)} %copy-done.67), channel_id=1, source_target_pairs={{0,13},{1,12},{2,15},{3,14},{4,9},{5,8},{6,11},{7,10},{8,5},{9,4},... | collective-permute-start | bytes 147464 | tf_op jit(solution)/shard_map/ppermute | solution.py:297
  105.6 9.1 %collective-permute-start.28 = (bf16[96,256]{1,0:T(8,128)(2,1)S(1)}, bf16[96,256]{1,0:T(8,128)(2,1)S(1)}, u32[]{:S(2)}, u32[]{:S(2)}) collective-permute-start(bf16[96,256]{1,0:T(8,128)(2,1)S(1)} %copy-done.65), channel_id=1, source_target_pairs={{0,14},{1,15},{2,12},{3,13},{4,10},{5,11},{6,8},{7,9},{8,6},{9,7},... | collective-permute-start | bytes 147464 | tf_op jit(solution)/shard_map/ppermute | solution.py:297
  107.1 7.7 %collective-permute-start.29 = (bf16[96,256]{1,0:T(8,128)(2,1)S(1)}, bf16[96,256]{1,0:T(8,128)(2,1)S(1)}, u32[]{:S(2)}, u32[]{:S(2)}) collective-permute-start(bf16[96,256]{1,0:T(8,128)(2,1)S(1)} %copy-done.63), channel_id=1, source_target_pairs={{0,15},{1,14},{2,13},{3,12},{4,11},{5,10},{6,9},{7,8},{8,7},{9,6},... | collective-permute-start | bytes 147464 | tf_op jit(solution)/shard_map/ppermute | solution.py:297
  (53 other events, 186.4 us)

commit v4 on v3

v4 whole, which is shorter than its diff:
```python
import functools

import jax
import jax.numpy as jnp
from jax import lax
from jax.experimental import pallas as pl
from jax.experimental.pallas import tpu as pltpu
from jax.sharding import Mesh
from jax.sharding import PartitionSpec as P

epsilon = 1e-05
CHANNELS = 128
BLOCK = 8
STEP = 4
SIZE = 32
LANES = 128
GATHER = 32
MIB = 1024 * 1024

f32, bf16 = jnp.float32, jnp.bfloat16


def sigmoid(x):
    return 0.5 * jnp.tanh(0.5 * x) + 0.5


def dot(a, b):
    return jnp.dot(a, b, preferred_element_type=f32)


def dot_nt(a, b):
    return lax.dot_general(a, b, (((1,), (1,)), ((), ())), preferred_element_type=f32)


def column(row):
    blocks = [
        jnp.broadcast_to(row[:, k : k + LANES], (LANES, LANES)).T
        for k in range(0, row.shape[1], LANES)
    ]
    return jnp.concatenate(blocks, axis=0)


def widen(col, width):
    return jnp.concatenate([col] * (width // LANES), axis=1)


def shuffle(groups, size):
    n = groups * size
    out = lax.broadcasted_iota(jnp.int32, (n, n), 0)
    row = lax.broadcasted_iota(jnp.int32, (n, n), 1)
    want = (out % size) * groups + out // size
    return jnp.where(want == row, 1.0, 0.0).astype(bf16)


def normalize(x, gain, shift):
    centered = x - jnp.mean(x, axis=1, keepdims=True)
    variance = jnp.mean(centered * centered, axis=1, keepdims=True)
    return (centered * lax.rsqrt(variance + epsilon) * gain + shift).astype(bf16)


def factor(normed, wt, bias):
    width = wt.shape[0] // 2
    lanes = normed.shape[0]
    gate = dot_nt(wt[:width], normed) + widen(bias[:width], lanes)
    value = dot_nt(wt[width:], normed) + widen(bias[width:], lanes)
    return sigmoid(gate) * value


def as_rows(values, k):
    hosts = values.shape[0] // BLOCK
    return jnp.concatenate(
        [values[:, r * k : (r + 1) * k].reshape(hosts, BLOCK, k) for r in range(STEP)], axis=1
    )


def right_kernel(pair_ref, gain_ref, shift_ref, w_ref, b_ref, out_ref, wt, bt):
    @pl.when(pl.program_id(0) == 0)
    def _():
        wt[...] = w_ref[...].astype(f32).T.astype(bf16)
        bt[...] = column(b_ref[...])

    k, width = pair_ref.shape[1:]
    x = pair_ref[...].astype(f32).reshape(STEP * k, width)
    normed = normalize(x, gain_ref[...], shift_ref[...])
    out = as_rows(factor(normed, wt[...], bt[...]), k).astype(bf16)
    for p in range(out_ref.shape[0]):
        out_ref[p] = out


def left_kernel(pair_ref, gain_ref, shift_ref, w_ref, b_ref, *refs):
    wf, bf, wt, bt = refs[-4:]
    normed_ref = refs[-5]
    outs = refs[:-5]
    k, width = pair_ref.shape[1:]
    hidden = w_ref.shape[1] // 2

    @pl.when(pl.program_id(0) == 0)
    def _():
        wf[...] = w_ref[...].astype(f32).T
        bf[...] = column(b_ref[...])
        host = lax.axis_index(("chan", "quarter"))
        for half in range(2):
            for b in range(0, len(outs), 2):
                source = [
                    pl.ds(pl.multiple_of(half * hidden + (host ^ (b + n)) * BLOCK, BLOCK), BLOCK)
                    for n in range(2)
                ]
                target = slice(half * hidden + b * BLOCK, half * hidden + (b + 2) * BLOCK)
                wt[target] = jnp.concatenate([wf[s] for s in source], axis=0).astype(bf16)
                bt[target] = jnp.concatenate([bf[s] for s in source], axis=0)

    x = pair_ref[...].astype(f32).reshape(STEP * k, width)
    normed = normalize(x, gain_ref[...], shift_ref[...])
    normed_ref[...] = normed.reshape(STEP, k, width)
    rows = as_rows(factor(normed, wt[...], bt[...]), k).astype(bf16)
    for b, out in enumerate(outs):
        out[...] = rows[b]


def gate_kernel(normed_ref, gw_ref, gb_ref, gate_ref):
    k, width = normed_ref.shape[1:]
    normed = normed_ref[...].reshape(STEP * k, width)
    gate = sigmoid(dot(normed, gw_ref[...]) + gb_ref[...])
    gate_ref[...] = gate.reshape(gate_ref.shape).astype(gate_ref.dtype)


def regroup(pieces, target, matrix):
    many = SIZE // STEP
    for s in range(len(pieces) // many):
        rows = jnp.concatenate([piece() for piece in pieces[s * many : (s + 1) * many]], axis=0)
        moved = dot(matrix, rows).astype(bf16)
        for c in range(BLOCK):
            target[c, s * SIZE : (s + 1) * SIZE, :] = moved[c * SIZE : (c + 1) * SIZE]


def slices(refs):
    tall = STEP * BLOCK
    return [
        functools.partial(lambda ref, at: ref[at : at + tall, :], ref, at)
        for ref in refs
        for at in range(0, ref.shape[0], tall)
    ]


def multiply(left, right_ref, right, held, store):
    regroup(slices([right_ref]), right, shuffle(BLOCK, SIZE))
    back = shuffle(SIZE, BLOCK)
    for c in range(BLOCK):
        held[c] = dot_nt(left[c], right[c]).astype(bf16)
    for s in range(left.shape[1] // SIZE):
        parts = jnp.concatenate([held[c, s * SIZE : (s + 1) * SIZE, :] for c in range(BLOCK)], axis=0)
        moved = dot(back, parts).astype(bf16)
        for i in range(0, SIZE, STEP):
            store(s * SIZE + i, moved[i * BLOCK : (i + STEP) * BLOCK])


def gather_kernel(*refs):
    regroup(slices(refs[:-1]), refs[-1], shuffle(BLOCK, SIZE))


def product_kernel(right_ref, left, out_ref, right, held):
    rows = left.shape[1] // out_ref.shape[0]
    host = lax.axis_index(("chan", "quarter"))

    def store(i, values):
        to, at = divmod(i, rows)
        out_ref[host ^ to, at * BLOCK : (at + STEP) * BLOCK, :] = values

    multiply(left, right_ref, right, held, store)


def final_kernel(x_ref, gate_ref, g_ref, s_ref, w_ref, b_ref, out_ref, gt, st):
    @pl.when(pl.program_id(0) == 0)
    def _():
        gt[...] = column(g_ref[...])
        st[...] = column(s_ref[...])

    hosts, _, j = x_ref.shape
    width = hosts * BLOCK
    for r in range(0, STEP, 2):
        pair = x_ref[:, r * BLOCK : (r + 2) * BLOCK].astype(f32)
        for n in range(2):
            x = pair[:, n * BLOCK : (n + 1) * BLOCK].reshape(width, j)
            centered = x - jnp.mean(x, axis=0, keepdims=True)
            variance = jnp.mean(centered * centered, axis=0, keepdims=True)
            normed = centered * lax.rsqrt(variance + epsilon)
            normed = normed * widen(gt[...], j) + widen(st[...], j)
            outward = dot(normed.T.astype(bf16), w_ref[...]) + b_ref[...]
            out_ref[r + n] = (gate_ref[r + n].astype(f32) * outward).astype(bf16)


def whole(shape):
    return pl.BlockSpec(shape, lambda s: (0,) * len(shape))


def cost(flops, size):
    return pl.CostEstimate(flops=flops, bytes_accessed=size, transcendentals=0)


def params(mib=32):
    return pltpu.CompilerParams(vmem_limit_bytes=mib * MIB)


def shards(parts, pair, norm_gain, norm_shift, factor_weight, factor_bias, gate_weight, gate_bias,
           center_gain, center_shift, out_weight, out_bias):
    rows, k, width = pair.shape
    hidden = out_weight.shape[0]
    hosts = hidden // BLOCK
    steps = rows // STEP
    tall = rows * BLOCK
    mine = hosts * rows
    devices = parts * hosts
    in_part = ("chan", "quarter")
    everywhere = ("part",) + in_part
    row = lambda v: v.reshape(1, -1)
    row_block = pl.BlockSpec((STEP, k, width), lambda s: (s, 0, 0))
    work = rows * k * width
    bfloat = lambda *shape: jax.ShapeDtypeStruct(shape, bf16)

    right = pl.pallas_call(
        right_kernel,
        grid=(steps,),
        in_specs=[
            row_block,
            whole((1, width)),
            whole((1, width)),
            pl.BlockSpec((width, 2 * hidden), lambda s: (0, 1)),
            pl.BlockSpec((1, 2 * hidden), lambda s: (0, 1)),
        ],
        out_specs=pl.BlockSpec((parts, hosts, STEP * BLOCK, k), lambda s: (0, 0, s, 0)),
        out_shape=bfloat(parts, hosts, tall, k),
        scratch_shapes=[pltpu.VMEM((2 * hidden, width), bf16), pltpu.VMEM((2 * hidden, LANES), f32)],
        compiler_params=params(60),
        cost_estimate=cost(4 * work * hidden, 6 * work),
        name="right_factor",
    )(pair, row(norm_gain), row(norm_shift), factor_weight, row(factor_bias))
    right = lax.all_to_all(right.reshape(devices, tall, k), everywhere, 0, 0, tiled=True)

    def send(values, b):
        if b == 0:
            return values
        pairs = [(p * hosts + h, p * hosts + (h ^ b)) for p in range(parts) for h in range(hosts)]
        return lax.ppermute(values, everywhere, pairs)

    *lefts, normed = pl.pallas_call(
        left_kernel,
        grid=(steps,),
        in_specs=[
            row_block,
            whole((1, width)),
            whole((1, width)),
            whole((width, 2 * hidden)),
            whole((1, 2 * hidden)),
        ],
        out_specs=[pl.BlockSpec((STEP * BLOCK, k), lambda s: (s, 0))] * hosts + [row_block],
        out_shape=[bfloat(tall, k)] * hosts + [bfloat(*pair.shape)],
        scratch_shapes=[
            pltpu.VMEM((2 * hidden, width), f32),
            pltpu.VMEM((2 * hidden, LANES), f32),
            pltpu.VMEM((2 * hidden, width), bf16),
            pltpu.VMEM((2 * hidden, LANES), f32),
        ],
        compiler_params=params(),
        cost_estimate=cost(4 * work * hidden, 6 * work),
        name="left_factor",
    )(pair, row(norm_gain), row(norm_shift), factor_weight, row(factor_bias))
    lefts = [send(values, b) for b, values in enumerate(lefts)]

    vmem = pl.BlockSpec(memory_space=pltpu.VMEM)
    left = pl.pallas_call(
        gather_kernel,
        in_specs=[vmem] * hosts,
        out_specs=vmem,
        out_shape=bfloat(BLOCK, mine, k),
        compiler_params=params(),
        cost_estimate=cost(2 * work * BLOCK * SIZE, 4 * work),
        name="gather_left",
    )(*lefts)

    gate = pl.pallas_call(
        gate_kernel,
        grid=(steps,),
        in_specs=[row_block, whole((width, width)), whole((1, width))],
        out_specs=row_block,
        out_shape=bfloat(*pair.shape),
        compiler_params=params(),
        cost_estimate=cost(2 * work * width, 4 * work),
        name="gate",
    )(normed, gate_weight, row(gate_bias))

    span = GATHER * rows
    product = pl.pallas_call(
        product_kernel,
        grid=(devices // GATHER,),
        in_specs=[pl.BlockSpec((span * BLOCK, k), lambda s: (s, 0)), whole((BLOCK, mine, k))],
        out_specs=pl.BlockSpec((hosts, tall, span), lambda s: (0, 0, s)),
        out_shape=bfloat(hosts, tall, devices * rows),
        scratch_shapes=[pltpu.VMEM((BLOCK, span, k), bf16), pltpu.VMEM((BLOCK, mine, span), bf16)],
        compiler_params=params(40),
        cost_estimate=cost(2 * BLOCK * mine * mine * k, 6 * BLOCK * mine * k),
        name="products",
    )(right.reshape(devices * tall, k), left)
    product = lax.all_to_all(product, in_part, 0, 0, tiled=True)

    return pl.pallas_call(
        final_kernel,
        grid=(steps,),
        in_specs=[
            pl.BlockSpec((hosts, STEP * BLOCK, devices * rows), lambda s: (0, s, 0)),
            row_block,
            whole((1, hidden)),
            whole((1, hidden)),
            whole((hidden, width)),
            whole((1, width)),
        ],
        out_specs=row_block,
        out_shape=bfloat(*pair.shape),
        scratch_shapes=[pltpu.VMEM((hidden, LANES), f32), pltpu.VMEM((hidden, LANES), f32)],
        compiler_params=params(),
        cost_estimate=cost(2 * work * width, 6 * work),
        name="update",
    )(product, gate, row(center_gain), row(center_shift), out_weight, row(out_bias))


def solution(mesh):
    groups, chan, quarter = (mesh.shape[a] for a in ("groups", "chan", "quarter"))
    near = CHANNELS // BLOCK // quarter
    parts = chan // near
    split = Mesh(
        mesh.devices.reshape(groups, parts, near, quarter), ("groups", "part", "chan", "quarter")
    )
    rows = P(("groups", "part", "chan", "quarter"), None, None)
    return jax.shard_map(
        functools.partial(shards, parts),
        mesh=split,
        in_specs=(rows,) + (P(),) * 10,
        out_specs=rows,
        check_vma=False,
    )
```

time: 120 us -> 97.4 us (0.81)
  starting transfers between devices: 55 us -> 31 us
  waiting for transfers between devices: 22.9 us -> 46.9 us
  local copies, waits for them, and re-layouts: 17.3 us -> 4.47 us
  Pallas kernels: 23.5 us -> 14.4 us
    ppermute x30 -> x15, starting transfers between devices: 41 us -> 19.2 us  [send(): return lax.ppermute(values, everywhere, pairs)]
    all_to_all x3 -> x2, waiting for transfers between devices: 0.01 us -> 16.1 us  [the longest x1 16.1 us: shards(): product = lax.all_to_all(product, in_part, 0, 0, tiled=True)]
    unnamed x136 -> x28, local copies, waits for them, and re-layouts: 17.3 us -> 4.47 us
    ppermute x30 -> x15, waiting for transfers between devices: 22.9 us -> 30.8 us  [send(): return lax.ppermute(values, everywhere, pairs)]
    pallas_call x1, Pallas kernels: 3.65 us -> 0.9 us  [shards(): pl.pallas_call(gate_kernel, grid=(steps,), in_specs=[row_block, whole((wi...]
    pallas_call x5 -> x3, Pallas kernels: 10.7 us -> 8 us  [the longest x1 5.03 us: shards(): pl.pallas_call(right_kernel, grid=(steps,), in_specs=[row_block, whole((1...]
    pallas_call x1, Pallas kernels: 4.96 us -> 2.71 us  [shards(): pl.pallas_call(left_kernel, grid=(steps,), in_specs=[row_block, whole((1,...]
    all_to_all x3 -> x2, starting transfers between devices: 13.9 us -> 11.7 us  [the longest x1 7.3 us: shards(): lax.all_to_all(right.reshape(devices, tall, k), everywhere, 0, 0, tiled=T...]
  transfers between devices with their start and end apart: 33 -> 17, of which waited for: 15 -> 9; matrix products, arithmetic and copies ran while one was open for 0% -> 0% of each run, Pallas kernels for 11% -> 4%
where the time goes in v4:
time: 97.4 us; the launch traced here: 96.9 us
  waiting for transfers between devices  46.9 us (48%)
  starting transfers between devices  31 us (32%)
  Pallas kernels  14.4 us (15%)
  local copies, waits for them, and re-layouts  4.47 us (5%)
    ppermute x15, waiting for transfers between devices, send(): return lax.ppermute(values, everywhere, pairs)  30.8 us
    ppermute x15, starting transfers between devices, send(): return lax.ppermute(values, everywhere, pairs)  19.2 us
    all_to_all x1, waiting for transfers between devices, shards(): product = lax.all_to_all(product, in_part, 0, 0, tiled=True)  16.1 us
    all_to_all x1, starting transfers between devices, shards(): lax.all_to_all(right.reshape(devices, tall, k), everywhere, 0, 0, tiled=T...  7.3 us
    pallas_call x1, Pallas kernels, shards(): pl.pallas_call(right_kernel, grid=(steps,), in_specs=[row_block, whole((1...  5.03 us
    unnamed x28, local copies, waits for them, and re-layouts  4.47 us
    all_to_all x1, starting transfers between devices, shards(): product = lax.all_to_all(product, in_part, 0, 0, tiled=True)  4.42 us
    pallas_call x1, Pallas kernels, shards(): pl.pallas_call(final_kernel, grid=(steps,), in_specs=[pl.BlockSpec((hosts...  2.78 us
  transfers between devices with their start and end apart: 17, of which 9 were waited for; matrix products, arithmetic and copies ran while one was open for 0% of the time, Pallas kernels for 4%

profile of v4, /device:TPU:0, one launch (start us, length us, event | category | flops | bytes accessed | tf_op | source)
XLA Modules:
  0.0 96.9 jit_solution(6776841673656010537)
XLA Ops:
  0.0 5.0 %right_factor.1 = bf16[2,16,96,384]{3,2,1,0:T(8,128)(2,1)} custom-call(bf16[12,384,128]{2,1,0:T(8,128)(2,1)} %pair_ref.3, f32[1,128]{1,0:T(1,128)} %bitcast.12, f32[1,128]{1,0:T(1,128)} %bitcast.14, bf16[128,512]{1,0:T(8,128)(2,1)} %w_ref.4, f32[1,512]{1,0:T(1,128)} %bitcast.10), custom_call_target="tpu_custom_call" | custom-call | flops 301989888 | bytes 3538944 | tf_op jit(solution)/shard_map/right_factor/pallas_call | solution.py:220
  5.0 0.0 copy-start.9
  5.1 7.3 %all-to-all-start = ((bf16[32,96,384]{2,1,0:T(8,128)(2,1)}), bf16[32,96,384]{2,1,0:T(8,128)(2,1)S(1)}, u32[]{:S(2)}, u32[]{:S(2)}) async-start(bf16[32,96,384]{2,1,0:T(8,128)(2,1)} %bitcast.20), calls=%async_computation | async-start | bytes 4718592 | tf_op jit(solution)/shard_map/all_to_all | solution.py:237
  12.4 0.0 copy-start.4
  12.4 0.9 copy-done.4
  13.3 2.7 %left_factor.1 = (bf16[96,384]{1,0:T(8,128)(2,1)S(1)}, bf16[96,384]{1,0:T(8,128)(2,1)S(1)}, bf16[96,384]{1,0:T(8,128)(2,1)S(1)}, bf16[96,384]{1,0:T(8,128)(2,1)S...) custom-call(bf16[12,384,128]{2,1,0:T(8,128)(2,1)S(1)} %copy-done, ...), custom_call_target="tpu_custom_call" | custom-call | flops 301989888 | bytes 3538944 | tf_op jit(solution)/shard_map/left_factor/pallas_call | solution.py:245
  16.0 1.0 %copy-done.2 = bf16[12,384,128]{2,1,0:T(8,128)(2,1)} copy-done((bf16[12,384,128]{2,1,0:T(8,128)(2,1)}, bf16[12,384,128]{2,1,0:T(8,128)(2,1)S(1)}, u32[]{:S(2)}) %copy-start.2) | copy-done | bytes 1179672
  17.1 0.2 collective-permute-start
  17.3 1.7 %collective-permute-start.1 = (bf16[96,384]{1,0:T(8,128)(2,1)S(1)}, bf16[96,384]{1,0:T(8,128)(2,1)S(1)}, u32[]{:S(2)}, u32[]{:S(2)}) collective-permute-start(bf16[96,384]{1,0:T(8,128)(2,1)S(1)} %get-tuple-element.24), channel_id=1, source_target_pairs={{0,2},{1,3},{2,0},{3,1},{4,6},{5,7},{6,4},{7,5},{8,10},{9,11},{10,... | collective-permute-start | bytes 221192 | tf_op jit(solution)/shard_map/ppermute | solution.py:243
  19.0 0.0 collective-permute-start.2
  19.0 1.7 %collective-permute-start.3 = (bf16[96,384]{1,0:T(8,128)(2,1)S(1)}, bf16[96,384]{1,0:T(8,128)(2,1)S(1)}, u32[]{:S(2)}, u32[]{:S(2)}) collective-permute-start(bf16[96,384]{1,0:T(8,128)(2,1)S(1)} %get-tuple-element.26), channel_id=1, source_target_pairs={{0,4},{1,5},{2,6},{3,7},{4,0},{5,1},{6,2},{7,3},{8,12},{9,13},{10,... | collective-permute-start | bytes 221192 | tf_op jit(solution)/shard_map/ppermute | solution.py:243
  20.7 0.1 collective-permute-start.4
  20.8 0.0 collective-permute-done.refs_1_
  20.8 2.6 %collective-permute-start.5 = (bf16[96,384]{1,0:T(8,128)(2,1)S(1)}, bf16[96,384]{1,0:T(8,128)(2,1)S(1)}, u32[]{:S(2)}, u32[]{:S(2)}) collective-permute-start(bf16[96,384]{1,0:T(8,128)(2,1)S(1)} %get-tuple-element.28), channel_id=1, source_target_pairs={{0,6},{1,7},{2,4},{3,5},{4,2},{5,3},{6,0},{7,1},{8,14},{9,15},{10,... | collective-permute-start | bytes 221192 | tf_op jit(solution)/shard_map/ppermute | solution.py:243
  23.4 8.5 %collective-permute-done.1.refs_2_ = bf16[96,384]{1,0:T(8,128)(2,1)S(1)} collective-permute-done((bf16[96,384]{1,0:T(8,128)(2,1)S(1)}, bf16[96,384]{1,0:T(8,128)(2,1)S(1)}, u32[]{:S(2)}, u32[]{:S(2)}) %collective-permute-start.1) | collective-permute-done | bytes 73760 | tf_op jit(solution)/shard_map/ppermute | solution.py:243
  31.9 0.6 collective-permute-start.6
  32.5 0.2 collective-permute-done.2.refs_3_
  32.7 0.3 collective-permute-start.7
  33.0 0.0 collective-permute-done.3.refs_4_
  33.0 2.3 %collective-permute-start.8 = (bf16[96,384]{1,0:T(8,128)(2,1)S(1)}, bf16[96,384]{1,0:T(8,128)(2,1)S(1)}, u32[]{:S(2)}, u32[]{:S(2)}) collective-permute-start(bf16[96,384]{1,0:T(8,128)(2,1)S(1)} %get-tuple-element.31), channel_id=1, source_target_pairs={{0,9},{1,8},{2,11},{3,10},{4,13},{5,12},{6,15},{7,14},{8,1},{9,0},... | collective-permute-start | bytes 221192 | tf_op jit(solution)/shard_map/ppermute | solution.py:243
  35.3 0.0 collective-permute-done.4.refs_5_
  35.3 3.3 %collective-permute-start.9 = (bf16[96,384]{1,0:T(8,128)(2,1)S(1)}, bf16[96,384]{1,0:T(8,128)(2,1)S(1)}, u32[]{:S(2)}, u32[]{:S(2)}) collective-permute-start(bf16[96,384]{1,0:T(8,128)(2,1)S(1)} %get-tuple-element.32), channel_id=1, source_target_pairs={{0,10},{1,11},{2,8},{3,9},{4,14},{5,15},{6,12},{7,13},{8,2},{9,3},... | collective-permute-start | bytes 221192 | tf_op jit(solution)/shard_map/ppermute | solution.py:243
  38.6 3.8 %collective-permute-done.5.refs_6_ = bf16[96,384]{1,0:T(8,128)(2,1)S(1)} collective-permute-done((bf16[96,384]{1,0:T(8,128)(2,1)S(1)}, bf16[96,384]{1,0:T(8,128)(2,1)S(1)}, u32[]{:S(2)}, u32[]{:S(2)}) %collective-permute-start.5) | collective-permute-done | bytes 73760 | tf_op jit(solution)/shard_map/ppermute | solution.py:243
  42.4 0.0 collective-permute-start.10
  42.4 0.8 collective-permute-done.6.refs_7_
  43.2 0.0 collective-permute-start.11
  43.2 10.3 %collective-permute-done.7.refs_8_ = bf16[96,384]{1,0:T(8,128)(2,1)S(1)} collective-permute-done((bf16[96,384]{1,0:T(8,128)(2,1)S(1)}, bf16[96,384]{1,0:T(8,128)(2,1)S(1)}, u32[]{:S(2)}, u32[]{:S(2)}) %collective-permute-start.7) | collective-permute-done | bytes 73760 | tf_op jit(solution)/shard_map/ppermute | solution.py:243
  53.6 2.0 %collective-permute-start.12 = (bf16[96,384]{1,0:T(8,128)(2,1)S(1)}, bf16[96,384]{1,0:T(8,128)(2,1)S(1)}, u32[]{:S(2)}, u32[]{:S(2)}) collective-permute-start(bf16[96,384]{1,0:T(8,128)(2,1)S(1)} %get-tuple-element.35), channel_id=1, source_target_pairs={{0,13},{1,12},{2,15},{3,14},{4,9},{5,8},{6,11},{7,10},{8,5},{9,4},... | collective-permute-start | bytes 221192 | tf_op jit(solution)/shard_map/ppermute | solution.py:243
  55.6 0.0 collective-permute-done.8.refs_9_
  55.6 2.8 %collective-permute-start.13 = (bf16[96,384]{1,0:T(8,128)(2,1)S(1)}, bf16[96,384]{1,0:T(8,128)(2,1)S(1)}, u32[]{:S(2)}, u32[]{:S(2)}) collective-permute-start(bf16[96,384]{1,0:T(8,128)(2,1)S(1)} %get-tuple-element.36), channel_id=1, source_target_pairs={{0,14},{1,15},{2,12},{3,13},{4,10},{5,11},{6,8},{7,9},{8,6},{9,7},... | collective-permute-start | bytes 221192 | tf_op jit(solution)/shard_map/ppermute | solution.py:243
  58.4 0.0 collective-permute-done.9.refs_10_
  58.4 1.7 %collective-permute-start.14 = (bf16[96,384]{1,0:T(8,128)(2,1)S(1)}, bf16[96,384]{1,0:T(8,128)(2,1)S(1)}, u32[]{:S(2)}, u32[]{:S(2)}) collective-permute-start(bf16[96,384]{1,0:T(8,128)(2,1)S(1)} %get-tuple-element.37), channel_id=1, source_target_pairs={{0,15},{1,14},{2,13},{3,12},{4,11},{5,10},{6,9},{7,8},{8,7},{9,6},... | collective-permute-start | bytes 221192 | tf_op jit(solution)/shard_map/ppermute | solution.py:243
  60.1 1.4 %collective-permute-done.12.refs_13_ = bf16[96,384]{1,0:T(8,128)(2,1)S(1)} collective-permute-done((bf16[96,384]{1,0:T(8,128)(2,1)S(1)}, bf16[96,384]{1,0:T(8,128)(2,1)S(1)}, u32[]{:S(2)}, u32[]{:S(2)}) %collective-permute-start.12) | collective-permute-done | bytes 73760 | tf_op jit(solution)/shard_map/ppermute | solution.py:243
  61.5 3.0 %collective-permute-done.13.refs_14_ = bf16[96,384]{1,0:T(8,128)(2,1)S(1)} collective-permute-done((bf16[96,384]{1,0:T(8,128)(2,1)S(1)}, bf16[96,384]{1,0:T(8,128)(2,1)S(1)}, u32[]{:S(2)}, u32[]{:S(2)}) %collective-permute-start.13) | collective-permute-done | bytes 73760 | tf_op jit(solution)/shard_map/ppermute | solution.py:243
  64.5 2.7 %collective-permute-done.14.refs_15_ = bf16[96,384]{1,0:T(8,128)(2,1)S(1)} collective-permute-done((bf16[96,384]{1,0:T(8,128)(2,1)S(1)}, bf16[96,384]{1,0:T(8,128)(2,1)S(1)}, u32[]{:S(2)}, u32[]{:S(2)}) %collective-permute-start.14) | collective-permute-done | bytes 73760 | tf_op jit(solution)/shard_map/ppermute | solution.py:243
  67.2 0.6 gather_left.1.left
  67.7 0.0 all-to-all-done
  67.7 2.4 %products.1 = bf16[16,96,384]{2,1,0:T(8,128)(2,1)S(1)} custom-call(bf16[3072,384]{1,0:T(8,128)(2,1)S(1)} %bitcast.9, bf16[8,192,384]{2,1,0:T(8,128)(2,1)S(1)} %gather_left.1.left), custom_call_target="tpu_custom_call" | custom-call | flops 226492416 | bytes 3538944 | tf_op jit(solution)/shard_map/products/pallas_call | solution.py:292
  70.2 0.0 copy-start.1
  70.2 1.0 %copy-done.1 = bf16[16,96,384]{2,1,0:T(8,128)(2,1)} copy-done((bf16[16,96,384]{2,1,0:T(8,128)(2,1)}, bf16[16,96,384]{2,1,0:T(8,128)(2,1)S(1)}, u32[]{:S(2)}) %copy-start.1) | copy-done | bytes 1179672
  71.2 4.4 %all-to-all-start.1 = ((bf16[16,96,384]{2,1,0:T(8,128)(2,1)}), bf16[16,96,384]{2,1,0:T(8,128)(2,1)S(1)}, u32[]{:S(2)}, u32[]{:S(2)}) async-start(bf16[16,96,384]{2,1,0:T(8,128)(2,1)} %copy-done.1), calls=%async_computation.1 | async-start | bytes 2359296 | tf_op jit(solution)/shard_map/all_to_all | solution.py:303
  75.6 0.0 copy-start.6
  75.6 0.7 copy-done.6
  76.4 0.9 gate.1.gate_ref
  77.3 16.1 %all-to-all-done.1.x_ref = bf16[16,96,384]{2,1,0:T(8,128)(2,1)S(1)} async-done(((bf16[16,96,384]{2,1,0:T(8,128)(2,1)}), bf16[16,96,384]{2,1,0:T(8,128)(2,1)S(1)}, u32[]{:S(2)}, u32[]{:S(2)}) %all-to-all-start.1) | async-done | bytes 1179680 | tf_op jit(solution)/shard_map/all_to_all | solution.py:303
  93.4 0.0 copy-start.5
  93.4 0.7 copy-done.5
  94.1 2.8 %update.1 = bf16[12,384,128]{2,1,0:T(8,128)(2,1)} custom-call(bf16[16,96,384]{2,1,0:T(8,128)(2,1)S(1)} %all-to-all-done.1.x_ref, bf16[12,384,128]{2,1,0:T(8,128)(2,1)S(1)} %gate.1.gate_ref, f32[1,128]{1,0:T(1,128)S(1)} %bitcast.16, f32[1,128]{1,0:T(1,128)S(1)} %bitcast.17, bf16[128,128]{1,0:T(8,128)(2,1)S(1)} %copy-done.5, f32[1,128]{1,0:T(1,128)S(1)} %bitcast.18), custom_call_target="tpu_custom_call" | custom-call | flops 150994944 | bytes 3538944 | tf_op jit(solution)/shard_map/update/pallas_call | solution.py:305
  (20 shorter events, 0.0 us)
Async XLA Ops:
  5.0 7.3 %copy-start = (bf16[12,384,128]{2,1,0:T(8,128)(2,1)S(1)}, bf16[12,384,128]{2,1,0:T(8,128)(2,1)}, u32[]{:S(2)}) copy-start(bf16[12,384,128]{2,1,0:T(8,128)(2,1)} %pair_ref.3) | copy-start | bytes 3538948
  5.0 7.3 %copy-start.7 = (f32[512]{0:T(512)S(1)}, f32[512]{0:T(512)}, u32[]{:S(2)}) copy-start(f32[512]{0:T(512)} %param.15) | copy-start | bytes 6148
  5.0 7.4 %copy-start.8 = (f32[128]{0:T(128)S(1)}, f32[128]{0:T(128)}, u32[]{:S(2)}) copy-start(f32[128]{0:T(128)} %param.12) | copy-start | bytes 1540
  5.0 7.4 %copy-start.9 = (f32[128]{0:T(128)S(1)}, f32[128]{0:T(128)}, u32[]{:S(2)}) copy-start(f32[128]{0:T(128)} %param.13) | copy-start | bytes 1540
  5.1 62.7 %all-to-all-start = ((bf16[32,96,384]{2,1,0:T(8,128)(2,1)}), bf16[32,96,384]{2,1,0:T(8,128)(2,1)S(1)}, u32[]{:S(2)}, u32[]{:S(2)}) async-start(bf16[32,96,384]{2,1,0:T(8,128)(2,1)} %bitcast.20), calls=%async_computation | async-start | bytes 4718592 | tf_op jit(solution)/shard_map/all_to_all | solution.py:237
  12.4 0.9 copy-start.4
  16.0 1.0 %copy-start.2 = (bf16[12,384,128]{2,1,0:T(8,128)(2,1)}, bf16[12,384,128]{2,1,0:T(8,128)(2,1)S(1)}, u32[]{:S(2)}) copy-start(bf16[12,384,128]{2,1,0:T(8,128)(2,1)S(1)} %get-tuple-element.38.normed_ref) | copy-start | bytes 3538948
  17.1 3.7 %collective-permute-start = (bf16[96,384]{1,0:T(8,128)(2,1)S(1)}, bf16[96,384]{1,0:T(8,128)(2,1)S(1)}, u32[]{:S(2)}, u32[]{:S(2)}) collective-permute-start(bf16[96,384]{1,0:T(8,128)(2,1)S(1)} %get-tuple-element.23), channel_id=1, source_target_pairs={{0,1},{1,0},{2,3},{3,2},{4,5},{5,4},{6,7},{7,6},{8,9},{9,8},{10,11... | collective-permute-start | bytes 221192 | tf_op jit(solution)/shard_map/ppermute | solution.py:243
  17.3 14.6 %collective-permute-start.1 = (bf16[96,384]{1,0:T(8,128)(2,1)S(1)}, bf16[96,384]{1,0:T(8,128)(2,1)S(1)}, u32[]{:S(2)}, u32[]{:S(2)}) collective-permute-start(bf16[96,384]{1,0:T(8,128)(2,1)S(1)} %get-tuple-element.24), channel_id=1, source_target_pairs={{0,2},{1,3},{2,0},{3,1},{4,6},{5,7},{6,4},{7,5},{8,10},{9,11},{10,... | collective-permute-start | bytes 221192 | tf_op jit(solution)/shard_map/ppermute | solution.py:243
  19.0 13.8 %collective-permute-start.2 = (bf16[96,384]{1,0:T(8,128)(2,1)S(1)}, bf16[96,384]{1,0:T(8,128)(2,1)S(1)}, u32[]{:S(2)}, u32[]{:S(2)}) collective-permute-start(bf16[96,384]{1,0:T(8,128)(2,1)S(1)} %get-tuple-element.25), channel_id=1, source_target_pairs={{0,3},{1,2},{2,1},{3,0},{4,7},{5,6},{6,5},{7,4},{8,11},{9,10},{10,... | collective-permute-start | bytes 221192 | tf_op jit(solution)/shard_map/ppermute | solution.py:243
  19.0 14.0 %collective-permute-start.3 = (bf16[96,384]{1,0:T(8,128)(2,1)S(1)}, bf16[96,384]{1,0:T(8,128)(2,1)S(1)}, u32[]{:S(2)}, u32[]{:S(2)}) collective-permute-start(bf16[96,384]{1,0:T(8,128)(2,1)S(1)} %get-tuple-element.26), channel_id=1, source_target_pairs={{0,4},{1,5},{2,6},{3,7},{4,0},{5,1},{6,2},{7,3},{8,12},{9,13},{10,... | collective-permute-start | bytes 221192 | tf_op jit(solution)/shard_map/ppermute | solution.py:243
  20.7 14.6 %collective-permute-start.4 = (bf16[96,384]{1,0:T(8,128)(2,1)S(1)}, bf16[96,384]{1,0:T(8,128)(2,1)S(1)}, u32[]{:S(2)}, u32[]{:S(2)}) collective-permute-start(bf16[96,384]{1,0:T(8,128)(2,1)S(1)} %get-tuple-element.27), channel_id=1, source_target_pairs={{0,5},{1,4},{2,7},{3,6},{4,1},{5,0},{6,3},{7,2},{8,13},{9,12},{10,... | collective-permute-start | bytes 221192 | tf_op jit(solution)/shard_map/ppermute | solution.py:243
  20.8 21.6 %collective-permute-start.5 = (bf16[96,384]{1,0:T(8,128)(2,1)S(1)}, bf16[96,384]{1,0:T(8,128)(2,1)S(1)}, u32[]{:S(2)}, u32[]{:S(2)}) collective-permute-start(bf16[96,384]{1,0:T(8,128)(2,1)S(1)} %get-tuple-element.28), channel_id=1, source_target_pairs={{0,6},{1,7},{2,4},{3,5},{4,2},{5,3},{6,0},{7,1},{8,14},{9,15},{10,... | collective-permute-start | bytes 221192 | tf_op jit(solution)/shard_map/ppermute | solution.py:243
  31.9 11.3 %collective-permute-start.6 = (bf16[96,384]{1,0:T(8,128)(2,1)S(1)}, bf16[96,384]{1,0:T(8,128)(2,1)S(1)}, u32[]{:S(2)}, u32[]{:S(2)}) collective-permute-start(bf16[96,384]{1,0:T(8,128)(2,1)S(1)} %get-tuple-element.29), channel_id=1, source_target_pairs={{0,7},{1,6},{2,5},{3,4},{4,3},{5,2},{6,1},{7,0},{8,15},{9,14},{10,... | collective-permute-start | bytes 221192 | tf_op jit(solution)/shard_map/ppermute | solution.py:243
  32.7 20.8 %collective-permute-start.7 = (bf16[96,384]{1,0:T(8,128)(2,1)S(1)}, bf16[96,384]{1,0:T(8,128)(2,1)S(1)}, u32[]{:S(2)}, u32[]{:S(2)}) collective-permute-start(bf16[96,384]{1,0:T(8,128)(2,1)S(1)} %get-tuple-element.30), channel_id=1, source_target_pairs={{0,8},{1,9},{2,10},{3,11},{4,12},{5,13},{6,14},{7,15},{8,0},{9,1},... | collective-permute-start | bytes 221192 | tf_op jit(solution)/shard_map/ppermute | solution.py:243
  33.0 22.6 %collective-permute-start.8 = (bf16[96,384]{1,0:T(8,128)(2,1)S(1)}, bf16[96,384]{1,0:T(8,128)(2,1)S(1)}, u32[]{:S(2)}, u32[]{:S(2)}) collective-permute-start(bf16[96,384]{1,0:T(8,128)(2,1)S(1)} %get-tuple-element.31), channel_id=1, source_target_pairs={{0,9},{1,8},{2,11},{3,10},{4,13},{5,12},{6,15},{7,14},{8,1},{9,0},... | collective-permute-start | bytes 221192 | tf_op jit(solution)/shard_map/ppermute | solution.py:243
  35.3 23.1 %collective-permute-start.9 = (bf16[96,384]{1,0:T(8,128)(2,1)S(1)}, bf16[96,384]{1,0:T(8,128)(2,1)S(1)}, u32[]{:S(2)}, u32[]{:S(2)}) collective-permute-start(bf16[96,384]{1,0:T(8,128)(2,1)S(1)} %get-tuple-element.32), channel_id=1, source_target_pairs={{0,10},{1,11},{2,8},{3,9},{4,14},{5,15},{6,12},{7,13},{8,2},{9,3},... | collective-permute-start | bytes 221192 | tf_op jit(solution)/shard_map/ppermute | solution.py:243
  42.4 17.7 %collective-permute-start.10 = (bf16[96,384]{1,0:T(8,128)(2,1)S(1)}, bf16[96,384]{1,0:T(8,128)(2,1)S(1)}, u32[]{:S(2)}, u32[]{:S(2)}) collective-permute-start(bf16[96,384]{1,0:T(8,128)(2,1)S(1)} %get-tuple-element.33), channel_id=1, source_target_pairs={{0,11},{1,10},{2,9},{3,8},{4,15},{5,14},{6,13},{7,12},{8,3},{9,2},... | collective-permute-start | bytes 221192 | tf_op jit(solution)/shard_map/ppermute | solution.py:243
  43.2 16.9 %collective-permute-start.11 = (bf16[96,384]{1,0:T(8,128)(2,1)S(1)}, bf16[96,384]{1,0:T(8,128)(2,1)S(1)}, u32[]{:S(2)}, u32[]{:S(2)}) collective-permute-start(bf16[96,384]{1,0:T(8,128)(2,1)S(1)} %get-tuple-element.34), channel_id=1, source_target_pairs={{0,12},{1,13},{2,14},{3,15},{4,8},{5,9},{6,10},{7,11},{8,4},{9,5},... | collective-permute-start | bytes 221192 | tf_op jit(solution)/shard_map/ppermute | solution.py:243
  53.6 7.9 %collective-permute-start.12 = (bf16[96,384]{1,0:T(8,128)(2,1)S(1)}, bf16[96,384]{1,0:T(8,128)(2,1)S(1)}, u32[]{:S(2)}, u32[]{:S(2)}) collective-permute-start(bf16[96,384]{1,0:T(8,128)(2,1)S(1)} %get-tuple-element.35), channel_id=1, source_target_pairs={{0,13},{1,12},{2,15},{3,14},{4,9},{5,8},{6,11},{7,10},{8,5},{9,4},... | collective-permute-start | bytes 221192 | tf_op jit(solution)/shard_map/ppermute | solution.py:243
  55.6 8.9 %collective-permute-start.13 = (bf16[96,384]{1,0:T(8,128)(2,1)S(1)}, bf16[96,384]{1,0:T(8,128)(2,1)S(1)}, u32[]{:S(2)}, u32[]{:S(2)}) collective-permute-start(bf16[96,384]{1,0:T(8,128)(2,1)S(1)} %get-tuple-element.36), channel_id=1, source_target_pairs={{0,14},{1,15},{2,12},{3,13},{4,10},{5,11},{6,8},{7,9},{8,6},{9,7},... | collective-permute-start | bytes 221192 | tf_op jit(solution)/shard_map/ppermute | solution.py:243
  58.4 8.8 %collective-permute-start.14 = (bf16[96,384]{1,0:T(8,128)(2,1)S(1)}, bf16[96,384]{1,0:T(8,128)(2,1)S(1)}, u32[]{:S(2)}, u32[]{:S(2)}) collective-permute-start(bf16[96,384]{1,0:T(8,128)(2,1)S(1)} %get-tuple-element.37), channel_id=1, source_target_pairs={{0,15},{1,14},{2,13},{3,12},{4,11},{5,10},{6,9},{7,8},{8,7},{9,6},... | collective-permute-start | bytes 221192 | tf_op jit(solution)/shard_map/ppermute | solution.py:243
  70.2 1.0 %copy-start.1 = (bf16[16,96,384]{2,1,0:T(8,128)(2,1)}, bf16[16,96,384]{2,1,0:T(8,128)(2,1)S(1)}, u32[]{:S(2)}) copy-start(bf16[16,96,384]{2,1,0:T(8,128)(2,1)S(1)} %products.1) | copy-start | bytes 3538948
  71.2 4.4 %copy-start.3 = (bf16[12,384,128]{2,1,0:T(8,128)(2,1)S(1)}, bf16[12,384,128]{2,1,0:T(8,128)(2,1)}, u32[]{:S(2)}) copy-start(bf16[12,384,128]{2,1,0:T(8,128)(2,1)} %copy-done.2) | copy-start | bytes 3538948
  71.2 4.4 %copy-start.13 = (f32[128]{0:T(128)S(1)}, f32[128]{0:T(128)}, u32[]{:S(2)}) copy-start(f32[128]{0:T(128)} %param.17) | copy-start | bytes 1540
  71.2 22.2 %all-to-all-start.1 = ((bf16[16,96,384]{2,1,0:T(8,128)(2,1)}), bf16[16,96,384]{2,1,0:T(8,128)(2,1)S(1)}, u32[]{:S(2)}, u32[]{:S(2)}) async-start(bf16[16,96,384]{2,1,0:T(8,128)(2,1)} %copy-done.1), calls=%async_computation.1 | async-start | bytes 2359296 | tf_op jit(solution)/shard_map/all_to_all | solution.py:303
  75.6 0.8 copy-start.6
  76.4 17.0 %copy-start.10 = (f32[128]{0:T(128)S(1)}, f32[128]{0:T(128)}, u32[]{:S(2)}) copy-start(f32[128]{0:T(128)} %param.18) | copy-start | bytes 1540
  76.4 17.0 %copy-start.11 = (f32[128]{0:T(128)S(1)}, f32[128]{0:T(128)}, u32[]{:S(2)}) copy-start(f32[128]{0:T(128)} %param.19) | copy-start | bytes 1540
  76.4 17.0 %copy-start.12 = (f32[128]{0:T(128)S(1)}, f32[128]{0:T(128)}, u32[]{:S(2)}) copy-start(f32[128]{0:T(128)} %param.21) | copy-start | bytes 1540
  93.4 0.8 copy-start.5

commit v5 on v4

--- a/solution.py
+++ b/solution.py
@@ -87,39 +87,42 @@
         out_ref[p] = out
 
 
-def left_kernel(pair_ref, gain_ref, shift_ref, w_ref, b_ref, *refs):
+def left_kernel(own_ref, other_ref, gain_ref, shift_ref, w_ref, b_ref, *refs):
     wf, bf, wt, bt = refs[-4:]
-    normed_ref = refs[-5]
-    outs = refs[:-5]
-    k, width = pair_ref.shape[1:]
+    outs = refs[:-4]
+    k, width = own_ref.shape[1:]
     hidden = w_ref.shape[1] // 2
-
-    @pl.when(pl.program_id(0) == 0)
+    near = len(outs) * BLOCK
+    step = pl.program_id(0)
+
+    @pl.when(step == 0)
     def _():
         wf[...] = w_ref[...].astype(f32).T
         bf[...] = column(b_ref[...])
         host = lax.axis_index(("chan", "quarter"))
         for half in range(2):
-            for b in range(0, len(outs), 2):
+            for m in range(0, len(outs), 2):
                 source = [
-                    pl.ds(pl.multiple_of(half * hidden + (host ^ (b + n)) * BLOCK, BLOCK), BLOCK)
+                    pl.ds(
+                        pl.multiple_of(half * hidden + (host ^ (2 * (m + n))) * BLOCK, BLOCK), BLOCK
+                    )
                     for n in range(2)
                 ]
-                target = slice(half * hidden + b * BLOCK, half * hidden + (b + 2) * BLOCK)
+                target = slice(half * near + m * BLOCK, half * near + (m + 2) * BLOCK)
                 wt[target] = jnp.concatenate([wf[s] for s in source], axis=0).astype(bf16)
                 bt[target] = jnp.concatenate([bf[s] for s in source], axis=0)
 
+    pair = jnp.where(step < pl.num_programs(0) // 2, own_ref[...], other_ref[...])
+    normed = normalize(pair.astype(f32).reshape(STEP * k, width), gain_ref[...], shift_ref[...])
+    rows = as_rows(factor(normed, wt[...], bt[...]), k).astype(bf16)
+    for m, out in enumerate(outs):
+        out[...] = rows[m]
+
+
+def gate_kernel(pair_ref, gain_ref, shift_ref, gw_ref, gb_ref, gate_ref):
+    k, width = pair_ref.shape[1:]
     x = pair_ref[...].astype(f32).reshape(STEP * k, width)
     normed = normalize(x, gain_ref[...], shift_ref[...])
-    normed_ref[...] = normed.reshape(STEP, k, width)
-    rows = as_rows(factor(normed, wt[...], bt[...]), k).astype(bf16)
-    for b, out in enumerate(outs):
-        out[...] = rows[b]
-
-
-def gate_kernel(normed_ref, gw_ref, gb_ref, gate_ref):
-    k, width = normed_ref.shape[1:]
-    normed = normed_ref[...].reshape(STEP * k, width)
     gate = sigmoid(dot(normed, gw_ref[...]) + gb_ref[...])
     gate_ref[...] = gate.reshape(gate_ref.shape).astype(gate_ref.dtype)
 
@@ -142,9 +145,10 @@
     ]
 
 
-def multiply(left, right_ref, right, held, store):
+def multiply(left, right_ref, right, held, arrive, store):
     regroup(slices([right_ref]), right, shuffle(BLOCK, SIZE))
     back = shuffle(SIZE, BLOCK)
+    arrive()
     for c in range(BLOCK):
         held[c] = dot_nt(left[c], right[c]).astype(bf16)
     for s in range(left.shape[1] // SIZE):
@@ -158,22 +162,48 @@
     regroup(slices(refs[:-1]), refs[-1], shuffle(BLOCK, SIZE))
 
 
-def product_kernel(right_ref, left, out_ref, right, held):
-    rows = left.shape[1] // out_ref.shape[0]
+def product_kernel(right_ref, left_ref, out_ref, left, right, held, made, sems, sem):
+    copy = pltpu.make_async_copy(left_ref, left, sem)
+
+    @pl.when(pl.program_id(0) == 0)
+    def _():
+        copy.start()
+
+    def arrive():
+        @pl.when(pl.program_id(0) == 0)
+        def _():
+            copy.wait()
+
+    hosts = out_ref.shape[0]
+    rows = left.shape[1] // hosts
+    span = made.shape[2]
     host = lax.axis_index(("chan", "quarter"))
+    lanes = pl.ds(pl.multiple_of(pl.program_id(0) * span, LANES), span)
+    copies = [
+        pltpu.make_async_copy(made.at[b], out_ref.at[host ^ b, :, lanes], sems.at[b])
+        for b in range(hosts)
+    ]
 
     def store(i, values):
         to, at = divmod(i, rows)
-        out_ref[host ^ to, at * BLOCK : (at + STEP) * BLOCK, :] = values
-
-    multiply(left, right_ref, right, held, store)
-
-
-def final_kernel(x_ref, gate_ref, g_ref, s_ref, w_ref, b_ref, out_ref, gt, st):
+        made[to, at * BLOCK : (at + STEP) * BLOCK, :] = values
+        if at + STEP == rows:
+            copies[to].start()
+
+    multiply(left, right_ref, right, held, arrive, store)
+    for copy in copies:
+        copy.wait()
+
+
+def final_kernel(x_ref, gate_ref, g_ref, s_ref, w_ref, b_ref, out_ref, gt, st, wt, sem):
+    copy = pltpu.make_async_copy(w_ref, wt, sem)
+
     @pl.when(pl.program_id(0) == 0)
     def _():
+        copy.start()
         gt[...] = column(g_ref[...])
         st[...] = column(s_ref[...])
+        copy.wait()
 
     hosts, _, j = x_ref.shape
     width = hosts * BLOCK
@@ -185,7 +215,7 @@
             variance = jnp.mean(centered * centered, axis=0, keepdims=True)
             normed = centered * lax.rsqrt(variance + epsilon)
             normed = normed * widen(gt[...], j) + widen(st[...], j)
-            outward = dot(normed.T.astype(bf16), w_ref[...]) + b_ref[...]
+            outward = dot(normed.astype(bf16).T, wt[...]) + b_ref[...]
             out_ref[r + n] = (gate_ref[r + n].astype(f32) * outward).astype(bf16)
 
 
@@ -199,6 +229,10 @@
 
 def params(mib=32):
     return pltpu.CompilerParams(vmem_limit_bytes=mib * MIB)
+
+
+def held_in_hbm(x):
+    return pltpu.with_memory_space_constraint(x, pltpu.HBM)
 
 
 def shards(parts, pair, norm_gain, norm_shift, factor_weight, factor_bias, gate_weight, gate_bias,
@@ -212,10 +246,14 @@
     devices = parts * hosts
     in_part = ("chan", "quarter")
     everywhere = ("part",) + in_part
-    row = lambda v: v.reshape(1, -1)
+    row = lambda v: held_in_hbm(v.reshape(1, -1))
     row_block = pl.BlockSpec((STEP, k, width), lambda s: (s, 0, 0))
     work = rows * k * width
-    bfloat = lambda *shape: jax.ShapeDtypeStruct(shape, bf16)
+    bfloat = lambda *shape: pltpu.HBM(shape, bf16)
+    factor_weight, gate_weight, out_weight = map(
+        held_in_hbm, (factor_weight, gate_weight, out_weight)
+    )
+    kept = held_in_hbm(pair)
 
     right = pl.pallas_call(
         right_kernel,
@@ -230,46 +268,51 @@
         out_specs=pl.BlockSpec((parts, hosts, STEP * BLOCK, k), lambda s: (0, 0, s, 0)),
         out_shape=bfloat(parts, hosts, tall, k),
         scratch_shapes=[pltpu.VMEM((2 * hidden, width), bf16), pltpu.VMEM((2 * hidden, LANES), f32)],
-        compiler_params=params(60),
+        compiler_params=params(),
         cost_estimate=cost(4 * work * hidden, 6 * work),
         name="right_factor",
-    )(pair, row(norm_gain), row(norm_shift), factor_weight, row(factor_bias))
+    )(kept, row(norm_gain), row(norm_shift), factor_weight, row(factor_bias))
     right = lax.all_to_all(right.reshape(devices, tall, k), everywhere, 0, 0, tiled=True)
 
-    def send(values, b):
-        if b == 0:
-            return values
-        pairs = [(p * hosts + h, p * hosts + (h ^ b)) for p in range(parts) for h in range(hosts)]
-        return lax.ppermute(values, everywhere, pairs)
-
-    *lefts, normed = pl.pallas_call(
+    chips = hosts // 2
+    other = lax.ppermute(pair, "quarter", [(0, 1), (1, 0)])
+    *lefts, = pl.pallas_call(
         left_kernel,
-        grid=(steps,),
+        grid=(2 * steps,),
         in_specs=[
-            row_block,
+            pl.BlockSpec((STEP, k, width), lambda s: (jnp.minimum(s, steps - 1), 0, 0)),
+            pl.BlockSpec((STEP, k, width), lambda s: (jnp.maximum(s - steps, 0), 0, 0)),
             whole((1, width)),
             whole((1, width)),
             whole((width, 2 * hidden)),
             whole((1, 2 * hidden)),
         ],
-        out_specs=[pl.BlockSpec((STEP * BLOCK, k), lambda s: (s, 0))] * hosts + [row_block],
-        out_shape=[bfloat(tall, k)] * hosts + [bfloat(*pair.shape)],
+        out_specs=[pl.BlockSpec((STEP * BLOCK, k), lambda s: (s, 0))] * chips,
+        out_shape=[bfloat(2 * tall, k)] * chips,
         scratch_shapes=[
             pltpu.VMEM((2 * hidden, width), f32),
             pltpu.VMEM((2 * hidden, LANES), f32),
-            pltpu.VMEM((2 * hidden, width), bf16),
-            pltpu.VMEM((2 * hidden, LANES), f32),
+            pltpu.VMEM((hidden, width), bf16),
+            pltpu.VMEM((hidden, LANES), f32),
         ],
         compiler_params=params(),
         cost_estimate=cost(4 * work * hidden, 6 * work),
         name="left_factor",
-    )(pair, row(norm_gain), row(norm_shift), factor_weight, row(factor_bias))
-    lefts = [send(values, b) for b, values in enumerate(lefts)]
+    )(kept, other, row(norm_gain), row(norm_shift), factor_weight, row(factor_bias))
+
+    def send(values, m):
+        pairs = [
+            (p * hosts + h, p * hosts + (h ^ (2 * m))) for p in range(parts) for h in range(hosts)
+        ]
+        return lax.ppermute(values, everywhere, pairs)
+
+    for m in reversed(range(1, chips)):
+        lefts[m] = send(lefts[m], m)
 
     vmem = pl.BlockSpec(memory_space=pltpu.VMEM)
     left = pl.pallas_call(
         gather_kernel,
-        in_specs=[vmem] * hosts,
+        in_specs=[vmem] * chips,
         out_specs=vmem,
         out_shape=bfloat(BLOCK, mine, k),
         compiler_params=params(),
@@ -280,26 +323,40 @@
     gate = pl.pallas_call(
         gate_kernel,
         grid=(steps,),
-        in_specs=[row_block, whole((width, width)), whole((1, width))],
+        in_specs=[
+            row_block,
+            whole((1, width)),
+            whole((1, width)),
+            whole((width, width)),
+            whole((1, width)),
+        ],
         out_specs=row_block,
         out_shape=bfloat(*pair.shape),
         compiler_params=params(),
         cost_estimate=cost(2 * work * width, 4 * work),
         name="gate",
-    )(normed, gate_weight, row(gate_bias))
+    )(kept, row(norm_gain), row(norm_shift), gate_weight, row(gate_bias))
 
     span = GATHER * rows
+    hbm = pl.BlockSpec(memory_space=pltpu.HBM)
     product = pl.pallas_call(
         product_kernel,
         grid=(devices // GATHER,),
-        in_specs=[pl.BlockSpec((span * BLOCK, k), lambda s: (s, 0)), whole((BLOCK, mine, k))],
-        out_specs=pl.BlockSpec((hosts, tall, span), lambda s: (0, 0, s)),
+        in_specs=[pl.BlockSpec((span * BLOCK, k), lambda s: (s, 0)), hbm],
+        out_specs=hbm,
         out_shape=bfloat(hosts, tall, devices * rows),
-        scratch_shapes=[pltpu.VMEM((BLOCK, span, k), bf16), pltpu.VMEM((BLOCK, mine, span), bf16)],
+        scratch_shapes=[
+            pltpu.VMEM((BLOCK, mine, k), bf16),
+            pltpu.VMEM((BLOCK, span, k), bf16),
+            pltpu.VMEM((BLOCK, mine, span), bf16),
+            pltpu.VMEM((hosts, tall, span), bf16),
+            pltpu.SemaphoreType.DMA((hosts,)),
+            pltpu.SemaphoreType.DMA,
+        ],
         compiler_params=params(40),
         cost_estimate=cost(2 * BLOCK * mine * mine * k, 6 * BLOCK * mine * k),
         name="products",
-    )(right.reshape(devices * tall, k), left)
+    )(right.reshape(devices * tall, k), held_in_hbm(left))
     product = lax.all_to_all(product, in_part, 0, 0, tiled=True)
 
     return pl.pallas_call(
@@ -310,16 +367,21 @@
             row_block,
             whole((1, hidden)),
             whole((1, hidden)),
-            whole((hidden, width)),
+            hbm,
             whole((1, width)),
         ],
         out_specs=row_block,
         out_shape=bfloat(*pair.shape),
-        scratch_shapes=[pltpu.VMEM((hidden, LANES), f32), pltpu.VMEM((hidden, LANES), f32)],
+        scratch_shapes=[
+            pltpu.VMEM((hidden, LANES), f32),
+            pltpu.VMEM((hidden, LANES), f32),
+            pltpu.VMEM((hidden, width), bf16),
+            pltpu.SemaphoreType.DMA,
+        ],
         compiler_params=params(),
         cost_estimate=cost(2 * work * width, 6 * work),
         name="update",
-    )(product, gate, row(center_gain), row(center_shift), out_weight, row(out_bias))
+    )(product, held_in_hbm(gate), row(center_gain), row(center_shift), out_weight, row(out_bias))
 
 
 def solution(mesh):

time: 97.4 us -> 102 us (1.047)
  Pallas kernels: 14.4 us -> 27.2 us
  starting transfers between devices: 31 us -> 24.7 us
  local copies, waits for them, and re-layouts: 4.47 us -> 0.91 us
  waiting for transfers between devices: 46.9 us -> 48.5 us
    pallas_call x3, Pallas kernels: 4.17 us -> 13 us  [the longest x1 7.06 us: shards(): pl.pallas_call(left_kernel, grid=(2 * steps,), in_specs=[pl.BlockSpec((ST...]
    ppermute x15 -> x7, starting transfers between devices: 19.2 us -> 11.3 us  [send(): return lax.ppermute(values, everywhere, pairs)]
    unnamed x28 -> x4, local copies, waits for them, and re-layouts: 4.47 us -> 0.91 us
    all_to_all x1, waiting for transfers between devices: 16.1 us -> 13.4 us  [shards(): product = lax.all_to_all(product, in_part, 0, 0, tiled=True)]
    ppermute x0 -> x1, waiting for transfers between devices: none -> 2.6 us  [shards(): other = lax.ppermute(pair, 'quarter', [(0, 1), (1, 0)])]
    pallas_call x1, Pallas kernels: 2.78 us -> 4.79 us  [shards(): pl.pallas_call(final_kernel, grid=(steps,), in_specs=[pl.BlockSpec((hosts...]
    pallas_call x1, Pallas kernels: 2.41 us -> 4.38 us  [shards(): pl.pallas_call(product_kernel, grid=(devices // GATHER,), in_specs=[pl.Bl...]
    ppermute x15 -> x7, waiting for transfers between devices: 30.8 us -> 32.5 us  [send(): return lax.ppermute(values, everywhere, pairs)]
  transfers between devices with their start and end apart: 17 -> 10, of which waited for: 9 -> 9; matrix products, arithmetic and copies ran while one was open for 0% -> 0% of each run, Pallas kernels for 4% -> 13%
where the time goes in v5:
time: 102 us; the launch traced here: 101 us
  waiting for transfers between devices  48.5 us (48%)
  Pallas kernels  27.2 us (27%)
  starting transfers between devices  24.7 us (24%)
    ppermute x7, waiting for transfers between devices, send(): return lax.ppermute(values, everywhere, pairs)  32.5 us
    all_to_all x1, waiting for transfers between devices, shards(): product = lax.all_to_all(product, in_part, 0, 0, tiled=True)  13.4 us
    ppermute x7, starting transfers between devices, send(): return lax.ppermute(values, everywhere, pairs)  11.3 us
    all_to_all x1, starting transfers between devices, shards(): lax.all_to_all(right.reshape(devices, tall, k), everywhere, 0, 0, tiled=T...  7.29 us
    pallas_call x1, Pallas kernels, shards(): pl.pallas_call(left_kernel, grid=(2 * steps,), in_specs=[pl.BlockSpec((ST...  7.06 us
    all_to_all x1, starting transfers between devices, shards(): product = lax.all_to_all(product, in_part, 0, 0, tiled=True)  5.71 us
    pallas_call x1, Pallas kernels, shards(): pl.pallas_call(right_kernel, grid=(steps,), in_specs=[row_block, whole((1...  5.05 us
    pallas_call x1, Pallas kernels, shards(): pl.pallas_call(final_kernel, grid=(steps,), in_specs=[pl.BlockSpec((hosts...  4.79 us
  transfers between devices with their start and end apart: 10, of which 9 were waited for; matrix products, arithmetic and copies ran while one was open for 0% of the time, Pallas kernels for 13%

profile of v5, /device:TPU:0, one launch (start us, length us, event | category | flops | bytes accessed | tf_op | source)
XLA Modules:
  0.0 101.3 jit_solution(3484421897842328862)
XLA Ops:
  0.0 5.1 %right_factor.1 = bf16[2,16,96,384]{3,2,1,0:T(8,128)(2,1)} custom-call(bf16[12,384,128]{2,1,0:T(8,128)(2,1)} %pair_ref.3, f32[1,128]{1,0:T(1,128)} %bitcast.13, f32[1,128]{1,0:T(1,128)} %bitcast.16, bf16[128,512]{1,0:T(8,128)(2,1)} %w_ref.4, f32[1,512]{1,0:T(1,128)} %bitcast.11), custom_call_target="tpu_custom_call" | custom-call | flops 301989888 | bytes 3538944 | tf_op jit(solution)/shard_map/right_factor/pallas_call | solution.py:258
  5.1 0.0 copy-start.1
  5.1 7.3 %all-to-all-start = ((bf16[32,96,384]{2,1,0:T(8,128)(2,1)}), bf16[32,96,384]{2,1,0:T(8,128)(2,1)S(1)}, u32[]{:S(2)}, u32[]{:S(2)}) async-start(bf16[32,96,384]{2,1,0:T(8,128)(2,1)} %bitcast.10), calls=%async_computation | async-start | bytes 4718592 | tf_op jit(solution)/shard_map/all_to_all | solution.py:275
  12.4 0.0 copy-done.1
  12.4 0.3 collective-permute-start
  12.7 2.6 %collective-permute-done.other_ref = bf16[12,384,128]{2,1,0:T(8,128)(2,1)S(1)} collective-permute-done((bf16[12,384,128]{2,1,0:T(8,128)(2,1)S(1)}, bf16[12,384,128]{2,1,0:T(8,128)(2,1)S(1)}, u32[]{:S(2)}, u32[]{:S(2)}) %collective-permute-start) | collective-permute-done | bytes 1179680 | tf_op jit(solution)/shard_map/ppermute | solution.py:278
  15.3 7.1 %left_factor.1 = (bf16[192,384]{1,0:T(8,128)(2,1)}, bf16[192,384]{1,0:T(8,128)(2,1)}, bf16[192,384]{1,0:T(8,128)(2,1)}, bf16[192,384]{1,0:T(8,128)(2,1)}, bf16[1...) custom-call(bf16[12,384,128]{2,1,0:T(8,128)(2,1)} %pair_ref.3, ...), custom_call_target="tpu_custom_call" | custom-call | flops 301989888 | bytes 3538944 | tf_op jit(solution)/shard_map/left_factor/pallas_call | solution.py:279
  22.3 1.8 %collective-permute-start.1 = (bf16[192,384]{1,0:T(8,128)(2,1)}, bf16[192,384]{1,0:T(8,128)(2,1)S(1)}, u32[]{:S(2)}, u32[]{:S(2)}) collective-permute-start(bf16[192,384]{1,0:T(8,128)(2,1)} %get-tuple-element.14), channel_id=1, source_target_pairs={{0,2},{1,3},{2,0},{3,1},{4,6},{5,7},{6,4},{7,5},{8,10},{9,11},{10,... | collective-permute-start | bytes 442376 | tf_op jit(solution)/shard_map/ppermute | solution.py:307
  24.2 1.5 %collective-permute-start.2 = (bf16[192,384]{1,0:T(8,128)(2,1)}, bf16[192,384]{1,0:T(8,128)(2,1)S(1)}, u32[]{:S(2)}, u32[]{:S(2)}) collective-permute-start(bf16[192,384]{1,0:T(8,128)(2,1)} %get-tuple-element.15), channel_id=1, source_target_pairs={{0,4},{1,5},{2,6},{3,7},{4,0},{5,1},{6,2},{7,3},{8,12},{9,13},{10,... | collective-permute-start | bytes 442376 | tf_op jit(solution)/shard_map/ppermute | solution.py:307
  25.6 0.3 collective-permute-start.3
  25.9 1.8 %collective-permute-start.4 = (bf16[192,384]{1,0:T(8,128)(2,1)}, bf16[192,384]{1,0:T(8,128)(2,1)S(1)}, u32[]{:S(2)}, u32[]{:S(2)}) collective-permute-start(bf16[192,384]{1,0:T(8,128)(2,1)} %get-tuple-element.17), channel_id=1, source_target_pairs={{0,8},{1,9},{2,10},{3,11},{4,12},{5,13},{6,14},{7,15},{8,0},{9,1},... | collective-permute-start | bytes 442376 | tf_op jit(solution)/shard_map/ppermute | solution.py:307
  27.7 1.5 %collective-permute-start.5 = (bf16[192,384]{1,0:T(8,128)(2,1)}, bf16[192,384]{1,0:T(8,128)(2,1)S(1)}, u32[]{:S(2)}, u32[]{:S(2)}) collective-permute-start(bf16[192,384]{1,0:T(8,128)(2,1)} %get-tuple-element.18), channel_id=1, source_target_pairs={{0,10},{1,11},{2,8},{3,9},{4,14},{5,15},{6,12},{7,13},{8,2},{9,3},... | collective-permute-start | bytes 442376 | tf_op jit(solution)/shard_map/ppermute | solution.py:307
  29.1 4.5 %collective-permute-done.1.refs_1_ = bf16[192,384]{1,0:T(8,128)(2,1)S(1)} collective-permute-done((bf16[192,384]{1,0:T(8,128)(2,1)}, bf16[192,384]{1,0:T(8,128)(2,1)S(1)}, u32[]{:S(2)}, u32[]{:S(2)}) %collective-permute-start.1) | collective-permute-done | bytes 147488 | tf_op jit(solution)/shard_map/ppermute | solution.py:307
  33.6 0.2 collective-permute-start.6
  33.9 3.4 %collective-permute-done.2.refs_2_ = bf16[192,384]{1,0:T(8,128)(2,1)S(1)} collective-permute-done((bf16[192,384]{1,0:T(8,128)(2,1)}, bf16[192,384]{1,0:T(8,128)(2,1)S(1)}, u32[]{:S(2)}, u32[]{:S(2)}) %collective-permute-start.2) | collective-permute-done | bytes 147488 | tf_op jit(solution)/shard_map/ppermute | solution.py:307
  37.3 4.3 %collective-permute-start.7 = (bf16[192,384]{1,0:T(8,128)(2,1)}, bf16[192,384]{1,0:T(8,128)(2,1)S(1)}, u32[]{:S(2)}, u32[]{:S(2)}) collective-permute-start(bf16[192,384]{1,0:T(8,128)(2,1)} %get-tuple-element.20), channel_id=1, source_target_pairs={{0,14},{1,15},{2,12},{3,13},{4,10},{5,11},{6,8},{7,9},{8,6},{9,7},... | collective-permute-start | bytes 442376 | tf_op jit(solution)/shard_map/ppermute | solution.py:307
  41.6 2.3 %collective-permute-done.3.refs_3_ = bf16[192,384]{1,0:T(8,128)(2,1)S(1)} collective-permute-done((bf16[192,384]{1,0:T(8,128)(2,1)}, bf16[192,384]{1,0:T(8,128)(2,1)S(1)}, u32[]{:S(2)}, u32[]{:S(2)}) %collective-permute-start.3) | collective-permute-done | bytes 147488 | tf_op jit(solution)/shard_map/ppermute | solution.py:307
  43.9 11.6 %collective-permute-done.4.refs_4_ = bf16[192,384]{1,0:T(8,128)(2,1)S(1)} collective-permute-done((bf16[192,384]{1,0:T(8,128)(2,1)}, bf16[192,384]{1,0:T(8,128)(2,1)S(1)}, u32[]{:S(2)}, u32[]{:S(2)}) %collective-permute-start.4) | collective-permute-done | bytes 147488 | tf_op jit(solution)/shard_map/ppermute | solution.py:307
  55.4 3.2 %collective-permute-done.5.refs_5_ = bf16[192,384]{1,0:T(8,128)(2,1)S(1)} collective-permute-done((bf16[192,384]{1,0:T(8,128)(2,1)}, bf16[192,384]{1,0:T(8,128)(2,1)S(1)}, u32[]{:S(2)}, u32[]{:S(2)}) %collective-permute-start.5) | collective-permute-done | bytes 147488 | tf_op jit(solution)/shard_map/ppermute | solution.py:307
  58.6 3.2 %collective-permute-done.6.refs_6_ = bf16[192,384]{1,0:T(8,128)(2,1)S(1)} collective-permute-done((bf16[192,384]{1,0:T(8,128)(2,1)}, bf16[192,384]{1,0:T(8,128)(2,1)S(1)}, u32[]{:S(2)}, u32[]{:S(2)}) %collective-permute-start.6) | collective-permute-done | bytes 147488 | tf_op jit(solution)/shard_map/ppermute | solution.py:307
  61.7 4.4 %collective-permute-done.7.refs_7_ = bf16[192,384]{1,0:T(8,128)(2,1)S(1)} collective-permute-done((bf16[192,384]{1,0:T(8,128)(2,1)}, bf16[192,384]{1,0:T(8,128)(2,1)S(1)}, u32[]{:S(2)}, u32[]{:S(2)}) %collective-permute-start.7) | collective-permute-done | bytes 147488 | tf_op jit(solution)/shard_map/ppermute | solution.py:307
  66.2 0.0 copy-start
  66.2 0.9 copy-done
  67.1 1.6 %gather_left.1.left_ref = bf16[8,192,384]{2,1,0:T(8,128)(2,1)} custom-call(bf16[192,384]{1,0:T(8,128)(2,1)S(1)} %copy-done, bf16[192,384]{1,0:T(8,128)(2,1)S(1)} %collective-permute-done.1.refs_1_, bf16[192,384]{1,0:T(8,128)(2,1)S(1)} %collective-permute-done.2.refs_2_, bf16[192,384]{1,0:T(8,128)(2,1)S(1)} %collective-permute-done.3.refs_3_, ...), custom_call_target="tpu_custom_call" | custom-call | flops 301989888 | bytes 2359296 | tf_op jit(solution)/shard_map/gather_left/pallas_call | solution.py:313
  68.6 0.0 all-to-all-done
  68.6 4.4 %products.1 = bf16[16,96,384]{2,1,0:T(8,128)(2,1)} custom-call(bf16[3072,384]{1,0:T(8,128)(2,1)S(1)} %bitcast.9, bf16[8,192,384]{2,1,0:T(8,128)(2,1)} %gather_left.1.left_ref), custom_call_target="tpu_custom_call" | custom-call | flops 226492416 | bytes 3538944 | tf_op jit(solution)/shard_map/products/pallas_call | solution.py:342
  73.0 5.7 %all-to-all-start.1 = ((bf16[16,96,384]{2,1,0:T(8,128)(2,1)}), bf16[16,96,384]{2,1,0:T(8,128)(2,1)S(1)}, u32[]{:S(2)}, u32[]{:S(2)}) async-start(bf16[16,96,384]{2,1,0:T(8,128)(2,1)} %products.1), calls=%async_computation.1 | async-start | bytes 2359296 | tf_op jit(solution)/shard_map/all_to_all | solution.py:360
  78.7 4.3 %gate.1.gate_ref = bf16[12,384,128]{2,1,0:T(8,128)(2,1)} custom-call(bf16[12,384,128]{2,1,0:T(8,128)(2,1)} %pair_ref.3, f32[1,128]{1,0:T(1,128)} %bitcast.15, f32[1,128]{1,0:T(1,128)} %bitcast.18, bf16[128,128]{1,0:T(8,128)(2,1)} %gw_ref.1, f32[1,128]{1,0:T(1,128)} %bitcast.19), custom_call_target="tpu_custom_call" | custom-call | flops 150994944 | bytes 2359296 | tf_op jit(solution)/shard_map/gate/pallas_call | solution.py:323
  83.1 13.4 %all-to-all-done.1.x_ref = bf16[16,96,384]{2,1,0:T(8,128)(2,1)S(1)} async-done(((bf16[16,96,384]{2,1,0:T(8,128)(2,1)}), bf16[16,96,384]{2,1,0:T(8,128)(2,1)S(1)}, u32[]{:S(2)}, u32[]{:S(2)}) %all-to-all-start.1) | async-done | bytes 1179680 | tf_op jit(solution)/shard_map/all_to_all | solution.py:360
  96.5 4.8 %update.1 = bf16[12,384,128]{2,1,0:T(8,128)(2,1)} custom-call(bf16[16,96,384]{2,1,0:T(8,128)(2,1)S(1)} %all-to-all-done.1.x_ref, bf16[12,384,128]{2,1,0:T(8,128)(2,1)} %gate.1.gate_ref, f32[1,128]{1,0:T(1,128)} %bitcast.20, f32[1,128]{1,0:T(1,128)} %bitcast.21, bf16[128,128]{1,0:T(8,128)(2,1)} %w_ref.5, f32[1,128]{1,0:T(1,128)} %bitcast.22), custom_call_target="tpu_custom_call" | custom-call | flops 150994944 | bytes 3538944 | tf_op jit(solution)/shard_map/update/pallas_call | solution.py:362
Async XLA Ops:
  5.1 7.3 %copy-start.1 = (bf16[12,384,128]{2,1,0:T(8,128)(2,1)S(1)}, bf16[12,384,128]{2,1,0:T(8,128)(2,1)}, u32[]{:S(2)}) copy-start(bf16[12,384,128]{2,1,0:T(8,128)(2,1)} %pair_ref.3) | copy-start | bytes 3538948
  5.1 63.6 %all-to-all-start = ((bf16[32,96,384]{2,1,0:T(8,128)(2,1)}), bf16[32,96,384]{2,1,0:T(8,128)(2,1)S(1)}, u32[]{:S(2)}, u32[]{:S(2)}) async-start(bf16[32,96,384]{2,1,0:T(8,128)(2,1)} %bitcast.10), calls=%async_computation | async-start | bytes 4718592 | tf_op jit(solution)/shard_map/all_to_all | solution.py:275
  12.4 2.9 %collective-permute-start = (bf16[12,384,128]{2,1,0:T(8,128)(2,1)S(1)}, bf16[12,384,128]{2,1,0:T(8,128)(2,1)S(1)}, u32[]{:S(2)}, u32[]{:S(2)}) collective-permute-start(bf16[12,384,128]{2,1,0:T(8,128)(2,1)S(1)} %copy-done.1), channel_id=1, source_target_pairs={{0,1},{1,0},{2,3},{3,2},{4,5},{5,4},{6,7},{7,6},{8,9},{9,8},{10,11... | collective-permute-start | bytes 3538952 | tf_op jit(solution)/shard_map/ppermute | solution.py:278
  22.3 11.3 %collective-permute-start.1 = (bf16[192,384]{1,0:T(8,128)(2,1)}, bf16[192,384]{1,0:T(8,128)(2,1)S(1)}, u32[]{:S(2)}, u32[]{:S(2)}) collective-permute-start(bf16[192,384]{1,0:T(8,128)(2,1)} %get-tuple-element.14), channel_id=1, source_target_pairs={{0,2},{1,3},{2,0},{3,1},{4,6},{5,7},{6,4},{7,5},{8,10},{9,11},{10,... | collective-permute-start | bytes 442376 | tf_op jit(solution)/shard_map/ppermute | solution.py:307
  24.2 13.1 %collective-permute-start.2 = (bf16[192,384]{1,0:T(8,128)(2,1)}, bf16[192,384]{1,0:T(8,128)(2,1)S(1)}, u32[]{:S(2)}, u32[]{:S(2)}) collective-permute-start(bf16[192,384]{1,0:T(8,128)(2,1)} %get-tuple-element.15), channel_id=1, source_target_pairs={{0,4},{1,5},{2,6},{3,7},{4,0},{5,1},{6,2},{7,3},{8,12},{9,13},{10,... | collective-permute-start | bytes 442376 | tf_op jit(solution)/shard_map/ppermute | solution.py:307
  25.6 18.2 %collective-permute-start.3 = (bf16[192,384]{1,0:T(8,128)(2,1)}, bf16[192,384]{1,0:T(8,128)(2,1)S(1)}, u32[]{:S(2)}, u32[]{:S(2)}) collective-permute-start(bf16[192,384]{1,0:T(8,128)(2,1)} %get-tuple-element.16), channel_id=1, source_target_pairs={{0,6},{1,7},{2,4},{3,5},{4,2},{5,3},{6,0},{7,1},{8,14},{9,15},{10,... | collective-permute-start | bytes 442376 | tf_op jit(solution)/shard_map/ppermute | solution.py:307
  25.9 29.5 %collective-permute-start.4 = (bf16[192,384]{1,0:T(8,128)(2,1)}, bf16[192,384]{1,0:T(8,128)(2,1)S(1)}, u32[]{:S(2)}, u32[]{:S(2)}) collective-permute-start(bf16[192,384]{1,0:T(8,128)(2,1)} %get-tuple-element.17), channel_id=1, source_target_pairs={{0,8},{1,9},{2,10},{3,11},{4,12},{5,13},{6,14},{7,15},{8,0},{9,1},... | collective-permute-start | bytes 442376 | tf_op jit(solution)/shard_map/ppermute | solution.py:307
  27.7 30.9 %collective-permute-start.5 = (bf16[192,384]{1,0:T(8,128)(2,1)}, bf16[192,384]{1,0:T(8,128)(2,1)S(1)}, u32[]{:S(2)}, u32[]{:S(2)}) collective-permute-start(bf16[192,384]{1,0:T(8,128)(2,1)} %get-tuple-element.18), channel_id=1, source_target_pairs={{0,10},{1,11},{2,8},{3,9},{4,14},{5,15},{6,12},{7,13},{8,2},{9,3},... | collective-permute-start | bytes 442376 | tf_op jit(solution)/shard_map/ppermute | solution.py:307
  33.6 28.1 %collective-permute-start.6 = (bf16[192,384]{1,0:T(8,128)(2,1)}, bf16[192,384]{1,0:T(8,128)(2,1)S(1)}, u32[]{:S(2)}, u32[]{:S(2)}) collective-permute-start(bf16[192,384]{1,0:T(8,128)(2,1)} %get-tuple-element.19), channel_id=1, source_target_pairs={{0,12},{1,13},{2,14},{3,15},{4,8},{5,9},{6,10},{7,11},{8,4},{9,5},... | collective-permute-start | bytes 442376 | tf_op jit(solution)/shard_map/ppermute | solution.py:307
  37.3 28.9 %collective-permute-start.7 = (bf16[192,384]{1,0:T(8,128)(2,1)}, bf16[192,384]{1,0:T(8,128)(2,1)S(1)}, u32[]{:S(2)}, u32[]{:S(2)}) collective-permute-start(bf16[192,384]{1,0:T(8,128)(2,1)} %get-tuple-element.20), channel_id=1, source_target_pairs={{0,14},{1,15},{2,12},{3,13},{4,10},{5,11},{6,8},{7,9},{8,6},{9,7},... | collective-permute-start | bytes 442376 | tf_op jit(solution)/shard_map/ppermute | solution.py:307
  66.2 0.9 copy-start
  73.0 23.5 %all-to-all-start.1 = ((bf16[16,96,384]{2,1,0:T(8,128)(2,1)}), bf16[16,96,384]{2,1,0:T(8,128)(2,1)S(1)}, u32[]{:S(2)}, u32[]{:S(2)}) async-start(bf16[16,96,384]{2,1,0:T(8,128)(2,1)} %products.1), calls=%async_computation.1 | async-start | bytes 2359296 | tf_op jit(solution)/shard_map/all_to_all | solution.py:360

commit v6 on v2

v6 whole, which is shorter than its diff:
```python
import functools

import jax
import jax.numpy as jnp
from jax import lax
from jax.experimental import pallas as pl
from jax.experimental.pallas import tpu as pltpu
from jax.sharding import Mesh
from jax.sharding import PartitionSpec as P

epsilon = 1e-05
CHANNELS = 128
BLOCK = 8
STEP = 4
SIZE = 32
LANES = 128
TAIL = 64
MIB = 1024 * 1024

f32, bf16 = jnp.float32, jnp.bfloat16


def sigmoid(x):
    return 0.5 * jnp.tanh(0.5 * x) + 0.5


def dot(a, b):
    return jnp.dot(a, b, preferred_element_type=f32)


def dot_nt(a, b):
    return lax.dot_general(a, b, (((1,), (1,)), ((), ())), preferred_element_type=f32)


def column(row):
    blocks = [
        jnp.broadcast_to(row[:, k : k + LANES], (LANES, LANES)).T
        for k in range(0, row.shape[1], LANES)
    ]
    return jnp.concatenate(blocks, axis=0)


def widen(col, width):
    return jnp.concatenate([col] * (width // LANES), axis=1)


def shuffle(groups, size):
    n = groups * size
    out = lax.broadcasted_iota(jnp.int32, (n, n), 0)
    row = lax.broadcasted_iota(jnp.int32, (n, n), 1)
    want = (out % size) * groups + out // size
    return jnp.where(want == row, 1.0, 0.0).astype(bf16)


def normalize(x, gain, shift):
    centered = x - jnp.mean(x, axis=1, keepdims=True)
    variance = jnp.mean(centered * centered, axis=1, keepdims=True)
    return (centered * lax.rsqrt(variance + epsilon) * gain + shift).astype(bf16)


def factor(normed, wt, bias):
    width = wt.shape[0] // 2
    lanes = normed.shape[0]
    gate = dot_nt(wt[:width], normed) + widen(bias[:width], lanes)
    value = dot_nt(wt[width:], normed) + widen(bias[width:], lanes)
    return sigmoid(gate) * value


def as_rows(values, k):
    hosts = values.shape[0] // BLOCK
    return jnp.concatenate(
        [values[:, r * k : (r + 1) * k].reshape(hosts, BLOCK, k) for r in range(STEP)], axis=1
    )


def factor_kernel(pair_ref, gain_ref, shift_ref, w_ref, b_ref, out_ref, *refs):
    wt, bt = refs[-2:]
    rights = refs[:-2]

    @pl.when(pl.program_id(0) == 0)
    def _():
        wt[...] = w_ref[...].astype(f32).T.astype(bf16)
        bt[...] = column(b_ref[...])

    k, width = pair_ref.shape[1:]
    half = wt.shape[0] // 2
    x = pair_ref[...].astype(f32).reshape(STEP * k, width)
    normed = normalize(x, gain_ref[...], shift_ref[...])
    for n in range(2):
        rows = slice((1 - n) * half, (2 - n) * half)
        values = factor(normed, wt[rows], bt[rows])
        out_ref[:, n] = as_rows(values, k).astype(bf16)
    host = lax.axis_index(("chan", "quarter"))
    for b, right in enumerate(rights):
        right[...] = out_ref[host ^ b, 0]


def gate_kernel(pair_ref, gain_ref, shift_ref, gw_ref, gb_ref, gate_ref):
    k, width = pair_ref.shape[1:]
    x = pair_ref[...].astype(f32).reshape(STEP * k, width)
    normed = normalize(x, gain_ref[...], shift_ref[...])
    gate = sigmoid(dot(normed, gw_ref[...]) + gb_ref[...])
    gate_ref[...] = gate.reshape(gate_ref.shape).astype(gate_ref.dtype)


def regroup(pieces, target, matrix):
    many = SIZE // STEP
    for s in range(len(pieces) // many):
        rows = jnp.concatenate([piece() for piece in pieces[s * many : (s + 1) * many]], axis=0)
        moved = dot(matrix, rows).astype(bf16)
        for c in range(BLOCK):
            target[c, s * SIZE : (s + 1) * SIZE, :] = moved[c * SIZE : (c + 1) * SIZE]


def multiply(left, right, held, out_ref):
    rows = left.shape[1] // out_ref.shape[0]
    tall = rows * BLOCK
    back = shuffle(SIZE, BLOCK)
    for c in range(BLOCK):
        held[c] = dot_nt(left[c], right[c]).astype(bf16)
    main = held.shape[2] - TAIL
    for s in range(left.shape[1] // SIZE):
        parts = jnp.concatenate([held[c, s * SIZE : (s + 1) * SIZE, :] for c in range(BLOCK)], axis=0)
        moved = dot(back, parts)
        ends = moved[:, main:].reshape(SIZE // 2, 2, BLOCK, TAIL)
        ends = jnp.concatenate([ends[:, 0], ends[:, 1]], axis=2).reshape(SIZE * BLOCK // 2, LANES)
        moved, ends = moved[:, :main].astype(bf16), ends.astype(bf16)
        for i in range(0, SIZE, STEP):
            to, at = divmod(s * SIZE + i, rows)
            out_ref[to, at * BLOCK : (at + STEP) * BLOCK, :] = moved[i * BLOCK : (i + STEP) * BLOCK]
            low = tall + at * BLOCK // 2
            out_ref[to, low : low + STEP * BLOCK // 2, :] = ends[
                i * BLOCK // 2 : (i + STEP) * BLOCK // 2
            ]


def near_kernel(factors_ref, left, out_ref, right, held):
    matrix = shuffle(BLOCK, SIZE)
    tall = factors_ref.shape[1] // 2
    step = STEP * BLOCK

    def pieces(n):
        return [
            functools.partial(lambda h, at: factors_ref[h, at : at + step, :], h, at)
            for h in range(factors_ref.shape[0])
            for at in range(n * tall, (n + 1) * tall, step)
        ]

    regroup(pieces(0), right, matrix)
    regroup(pieces(1), left, matrix)
    multiply(left, right, held, out_ref)


def far_kernel(hosts, left_ref, *refs):
    rights = refs[:hosts]
    out_ref, left, arrived, right, held, sems = refs[-6:]
    tall = rights[0].shape[0]
    host = lax.axis_index(("chan", "quarter"))
    copies = []
    for b, ref in enumerate(rights):
        to = arrived.at[pl.ds(pl.multiple_of((host ^ b) * tall, 16), tall)]
        copies.append(pltpu.make_async_copy(ref, to, sems.at[b]))
    copies.append(pltpu.make_async_copy(left_ref, left, sems.at[hosts]))
    for copy in copies:
        copy.start()
    for copy in copies[:-1]:
        copy.wait()
    step = STEP * BLOCK
    pieces = [
        functools.partial(lambda at: arrived[at : at + step, :], at)
        for at in range(0, arrived.shape[0], step)
    ]
    regroup(pieces, right, shuffle(BLOCK, SIZE))
    copies[-1].wait()
    multiply(left, right, held, out_ref)


def final_kernel(parts, *refs):
    products = refs[:parts]
    gate_ref, g_ref, s_ref, w_ref, b_ref, out_ref, gt, st = refs[parts:]
    step = pl.program_id(0)

    @pl.when(step == 0)
    def _():
        gt[...] = column(g_ref[...])
        st[...] = column(s_ref[...])

    part = lax.axis_index("part")
    hosts, tall, _ = products[0].shape
    tall = tall * 2 // 3
    span = gate_ref.shape[1] // parts
    main = span - TAIL
    width = hosts * BLOCK
    for a, ref in enumerate(products):
        first = pl.multiple_of(lax.rem(part + parts - a, parts) * span, 16)
        whole = ref[:, pl.ds(pl.multiple_of(step * STEP * BLOCK, 16), STEP * BLOCK), :].astype(f32)
        low = pl.multiple_of(tall + step * (STEP * BLOCK // 2), 16)
        ends = ref[:, pl.ds(low, STEP * BLOCK // 2), :].astype(f32)
        blocks = [whole[:, r * BLOCK : (r + 1) * BLOCK].reshape(width, LANES) for r in range(STEP)]
        blocks += [
            ends[:, r * BLOCK : (r + 1) * BLOCK].reshape(width, LANES) for r in range(STEP // 2)
        ]
        x = jnp.concatenate(blocks, axis=1)
        centered = x - jnp.mean(x, axis=0, keepdims=True)
        variance = jnp.mean(centered * centered, axis=0, keepdims=True)
        normed = centered * lax.rsqrt(variance + epsilon)
        normed = normed * widen(gt[...], x.shape[1]) + widen(st[...], x.shape[1])
        outward = dot(normed.T.astype(bf16), w_ref[...]) + b_ref[...]
        for r in range(STEP):
            at = pl.ds(first, main)
            value = outward[r * LANES : (r + 1) * LANES]
            out_ref[r, at, :] = (gate_ref[r, at, :].astype(f32) * value).astype(bf16)
            at = pl.ds(pl.multiple_of(first + main, 16), TAIL)
            low = STEP * LANES + r * TAIL
            value = outward[low : low + TAIL]
            out_ref[r, at, :] = (gate_ref[r, at, :].astype(f32) * value).astype(bf16)


def whole(shape):
    return pl.BlockSpec(shape, lambda s: (0,) * len(shape))


def cost(flops, size):
    return pl.CostEstimate(flops=flops, bytes_accessed=size, transcendentals=0)


def params(mib=32):
    return pltpu.CompilerParams(vmem_limit_bytes=mib * MIB)


def in_hbm(x):
    return pltpu.with_memory_space_constraint(x, pltpu.HBM)


def shards(parts, pair, norm_gain, norm_shift, factor_weight, factor_bias, gate_weight, gate_bias,
           center_gain, center_shift, out_weight, out_bias):
    rows, k, width = pair.shape
    hidden = out_weight.shape[0]
    hosts = hidden // BLOCK
    steps = rows // STEP
    tall = rows * BLOCK
    mine = hosts * rows
    in_part = ("chan", "quarter")
    everywhere = ("part",) + in_part
    row = lambda v: in_hbm(v.reshape(1, -1))
    row_block = pl.BlockSpec((STEP, k, width), lambda s: (s, 0, 0))
    work = rows * k * width

    anywhere = pl.BlockSpec(memory_space=pl.ANY)
    bfloat = lambda *shape: jax.ShapeDtypeStruct(shape, bf16)
    bfloat_hbm = lambda *shape: pltpu.HBM(shape, bf16)
    kept = in_hbm(pair)
    factors, *rights = pl.pallas_call(
        factor_kernel,
        grid=(steps,),
        in_specs=[
            row_block,
            whole((1, width)),
            whole((1, width)),
            whole((width, 4 * hidden)),
            whole((1, 4 * hidden)),
        ],
        out_specs=[pl.BlockSpec((hosts, 2, STEP * BLOCK, k), lambda s: (0, 0, s, 0))]
        + [pl.BlockSpec((STEP * BLOCK, k), lambda s: (s, 0))] * hosts,
        out_shape=[bfloat_hbm(hosts, 2, tall, k)] + [bfloat_hbm(tall, k)] * hosts,
        scratch_shapes=[pltpu.VMEM((4 * hidden, width), bf16), pltpu.VMEM((4 * hidden, LANES), f32)],
        compiler_params=params(60),
        cost_estimate=cost(8 * work * hidden, 8 * work),
        name="factors",
    )(kept, row(norm_gain), row(norm_shift), factor_weight, row(factor_bias))

    def send(a, b):
        pairs = [
            (p * hosts + h, (p + a) % parts * hosts + (h ^ b))
            for p in range(parts)
            for h in range(hosts)
        ]
        return lax.ppermute(rights[b], everywhere, pairs)

    arrived = [[send(a, b) for b in range(hosts)] for a in range(1, parts)]

    factors = factors.reshape(hosts, 2 * tall, k)
    factors = lax.all_to_all(factors, in_part, 0, 0, tiled=True)

    gate = pl.pallas_call(
        gate_kernel,
        grid=(steps,),
        in_specs=[
            row_block,
            whole((1, width)),
            whole((1, width)),
            whole((width, width)),
            whole((1, width)),
        ],
        out_specs=row_block,
        out_shape=bfloat_hbm(*pair.shape),
        compiler_params=params(),
        cost_estimate=cost(1 << 37, 4 * work),
        name="gate",
    )(kept, row(norm_gain), row(norm_shift), in_hbm(gate_weight), row(gate_bias))

    vmem = pl.BlockSpec(memory_space=pltpu.VMEM)
    anywhere = pl.BlockSpec(memory_space=pl.ANY)
    grouped = (BLOCK, mine, k)
    spent = cost(2 * BLOCK * mine * mine * k, 6 * BLOCK * mine * k)
    left, product = pl.pallas_call(
        near_kernel,
        in_specs=[vmem],
        out_specs=[vmem, vmem],
        out_shape=[bfloat_hbm(*grouped), bfloat_hbm(hosts, tall * 3 // 2, LANES)],
        scratch_shapes=[pltpu.VMEM(grouped, bf16), pltpu.VMEM((BLOCK, mine, mine), bf16)],
        compiler_params=params(),
        cost_estimate=spent,
        name="near_products",
    )(factors)
    products = [lax.all_to_all(product, in_part, 0, 0, tiled=True)]
    for rest in arrived:
        product = pl.pallas_call(
            functools.partial(far_kernel, hosts),
            in_specs=[anywhere] * (3 + hosts),
            out_specs=vmem,
            out_shape=bfloat_hbm(hosts, tall * 3 // 2, LANES),
            scratch_shapes=[
                pltpu.VMEM(grouped, bf16),
                pltpu.VMEM((mine * BLOCK, k), bf16),
                pltpu.VMEM(grouped, bf16),
                pltpu.VMEM((BLOCK, mine, mine), bf16),
                pltpu.SemaphoreType.DMA((1 + hosts,)),
            ],
            compiler_params=params(),
            cost_estimate=spent,
            name="far_products",
        )(in_hbm(left), *map(in_hbm, rest), in_hbm(products[-1]), in_hbm(gate))
        products.append(lax.all_to_all(product, in_part, 0, 0, tiled=True))

    return pl.pallas_call(
        functools.partial(final_kernel, parts),
        grid=(steps,),
        in_specs=[whole(products[0].shape)] * parts
        + [row_block, whole((1, hidden)), whole((1, hidden)), whole((hidden, width)), whole((1, width))],
        out_specs=row_block,
        out_shape=bfloat(*pair.shape),
        scratch_shapes=[pltpu.VMEM((hidden, LANES), f32), pltpu.VMEM((hidden, LANES), f32)],
        compiler_params=params(),
        cost_estimate=cost(2 * work * width, 6 * work),
        name="update",
    )(
        *map(in_hbm, products[:-1]),
        products[-1],
        in_hbm(gate),
        row(center_gain),
        row(center_shift),
        in_hbm(out_weight),
        row(out_bias),
    )


def solution(mesh):
    groups, chan, quarter = (mesh.shape[a] for a in ("groups", "chan", "quarter"))
    near = CHANNELS // BLOCK // quarter
    parts = chan // near
    split = Mesh(
        mesh.devices.reshape(groups, parts, near, quarter), ("groups", "part", "chan", "quarter")
    )
    rows = P(("groups", "part", "chan", "quarter"), None, None)
    return jax.shard_map(
        functools.partial(shards, parts),
        mesh=split,
        in_specs=(rows,) + (P(),) * 10,
        out_specs=rows,
        check_vma=False,
    )
```

time: 141 us -> 120 us (0.85)
  starting transfers between devices: 77.8 us -> 56.8 us
  blocking collectives: 0 us -> 18 us
  waiting for transfers between devices: 38.6 us -> 22.1 us
  local copies, waits for them, and re-layouts: 2.9 us -> 0.92 us
    all_to_all x0 -> x1, blocking collectives: none -> 18 us  [shards(): products.append(lax.all_to_all(product, in_part, 0, 0, tiled=True))]
    ppermute x31 -> x16, starting transfers between devices: 59.6 us -> 46.7 us  [send(): return lax.ppermute(rights[b], everywhere, pairs)]
    all_to_all x3 -> x2, waiting for transfers between devices: 9.55 us -> 0.01 us  [the longest x1 0.01 us: shards(): products = [lax.all_to_all(product, in_part, 0, 0, tiled=True)]]
    all_to_all x3 -> x2, starting transfers between devices: 18.2 us -> 10.2 us  [the longest x1 6.43 us: shards(): factors = lax.all_to_all(factors, in_part, 0, 0, tiled=True)]
    ppermute x31 -> x16, waiting for transfers between devices: 29.1 us -> 22.1 us  [send(): return lax.ppermute(rights[b], everywhere, pairs)]
    unnamed x66, local copies, waits for them, and re-layouts: 2.9 us -> 0.92 us
    pallas_call x1, Pallas kernels: 2.67 us -> 4.3 us  [shards(): pl.pallas_call(functools.partial(final_kernel, parts), grid=(steps,), in_...]
    pallas_call x5 -> x4, Pallas kernels: 17.7 us -> 16.6 us  [the longest x1 5.8 us: shards(): pl.pallas_call(factor_kernel, grid=(steps,), in_specs=[row_block, whole((...]
  transfers between devices with their start and end apart: 34 -> 18, of which waited for: 11 -> 4; matrix products, arithmetic and copies ran while one was open for 0% -> 0% of each run, Pallas kernels for 4% -> 6%
where the time goes in v6:
time: 120 us; the launch traced here: 119 us
  starting transfers between devices  56.8 us (47%)
  waiting for transfers between devices  22.1 us (18%)
  Pallas kernels  20.9 us (17%)
  blocking collectives  18 us (15%)
    ppermute x16, starting transfers between devices, send(): return lax.ppermute(rights[b], everywhere, pairs)  46.7 us
    ppermute x16, waiting for transfers between devices, send(): return lax.ppermute(rights[b], everywhere, pairs)  22.1 us
    all_to_all x1, blocking collectives, shards(): products.append(lax.all_to_all(product, in_part, 0, 0, tiled=True))  18 us
    all_to_all x1, starting transfers between devices, shards(): factors = lax.all_to_all(factors, in_part, 0, 0, tiled=True)  6.43 us
    pallas_call x1, Pallas kernels, shards(): pl.pallas_call(factor_kernel, grid=(steps,), in_specs=[row_block, whole((...  5.8 us
    pallas_call x1, Pallas kernels, shards(): pl.pallas_call(gate_kernel, grid=(steps,), in_specs=[row_block, whole((1,...  4.32 us
    pallas_call x1, Pallas kernels, shards(): pl.pallas_call(functools.partial(final_kernel, parts), grid=(steps,), in_...  4.3 us
    pallas_call x1, Pallas kernels, shards(): pl.pallas_call(functools.partial(far_kernel, hosts), in_specs=[anywhere]...  3.86 us
  transfers between devices with their start and end apart: 18, of which 4 were waited for; matrix products, arithmetic and copies ran while one was open for 0% of the time, Pallas kernels for 6%

profile of v6, /device:TPU:0, one launch (start us, length us, event | category | flops | bytes accessed | tf_op | source)
XLA Modules:
  0.0 119.1 jit_solution(7881556631143572833)
XLA Ops:
  0.0 5.8 %factors.1 = (bf16[16,2,96,384]{3,2,1,0:T(8,128)(2,1)}, bf16[96,384]{1,0:T(8,128)(2,1)}, bf16[96,384]{1,0:T(8,128)(2,1)}, bf16[96,384]{1,0:T(8,128)(2,1)}, bf16[...) custom-call(bf16[12,384,128]{2,1,0:T(8,128)(2,1)} %pair_ref.3, ...), custom_call_target="tpu_custom_call" | custom-call | flops 603979776 | bytes 4718592 | tf_op jit(solution)/shard_map/factors/pallas_call | solution.py:253
  5.8 0.0 copy-start.32
  5.9 6.4 %all-to-all-start = ((bf16[16,192,384]{2,1,0:T(8,128)(2,1)}), bf16[16,192,384]{2,1,0:T(8,128)(2,1)S(1)}, u32[]{:S(2)}, u32[]{:S(2)}) async-start(bf16[16,192,384]{2,1,0:T(8,128)(2,1)} %bitcast.8), calls=%async_computation | async-start | bytes 4718592 | tf_op jit(solution)/shard_map/all_to_all | solution.py:283
  12.4 0.0 copy-done.32
  12.4 2.7 %collective-permute-start = (bf16[96,384]{1,0:T(8,128)(2,1)S(1)}, bf16[96,384]{1,0:T(8,128)(2,1)S(1)}, u32[]{:S(2)}, u32[]{:S(2)}) collective-permute-start(bf16[96,384]{1,0:T(8,128)(2,1)S(1)} %copy-done.32), channel_id=1, source_target_pairs={{0,16},{1,17},{2,18},{3,19},{4,20},{5,21},{6,22},{7,23},{8,24},{9,... | collective-permute-start | bytes 221192 | tf_op jit(solution)/shard_map/ppermute | solution.py:278
  15.0 0.1 collective-permute-start.1
  15.1 4.6 %collective-permute-start.10 = (bf16[96,384]{1,0:T(8,128)(2,1)S(1)}, bf16[96,384]{1,0:T(8,128)(2,1)S(1)}, u32[]{:S(2)}, u32[]{:S(2)}) collective-permute-start(bf16[96,384]{1,0:T(8,128)(2,1)S(1)} %copy-done.30), channel_id=1, source_target_pairs={{0,26},{1,27},{2,24},{3,25},{4,30},{5,31},{6,28},{7,29},{8,18},{9,... | collective-permute-start | bytes 221192 | tf_op jit(solution)/shard_map/ppermute | solution.py:278
  19.7 0.0 copy-done.29
  19.7 0.3 collective-permute-start.11
  20.0 0.0 copy-done.28
  20.0 4.4 %collective-permute-start.12 = (bf16[96,384]{1,0:T(8,128)(2,1)S(1)}, bf16[96,384]{1,0:T(8,128)(2,1)S(1)}, u32[]{:S(2)}, u32[]{:S(2)}) collective-permute-start(bf16[96,384]{1,0:T(8,128)(2,1)S(1)} %copy-done.28), channel_id=1, source_target_pairs={{0,28},{1,29},{2,30},{3,31},{4,24},{5,25},{6,26},{7,27},{8,20},{9,... | collective-permute-start | bytes 221192 | tf_op jit(solution)/shard_map/ppermute | solution.py:278
  24.4 18.4 %collective-permute-done.refs_0_ = bf16[96,384]{1,0:T(8,128)(2,1)S(1)} collective-permute-done((bf16[96,384]{1,0:T(8,128)(2,1)S(1)}, bf16[96,384]{1,0:T(8,128)(2,1)S(1)}, u32[]{:S(2)}, u32[]{:S(2)}) %collective-permute-start) | collective-permute-done | bytes 73760 | tf_op jit(solution)/shard_map/ppermute | solution.py:278
  42.8 6.9 %collective-permute-start.13 = (bf16[96,384]{1,0:T(8,128)(2,1)S(1)}, bf16[96,384]{1,0:T(8,128)(2,1)S(1)}, u32[]{:S(2)}, u32[]{:S(2)}) collective-permute-start(bf16[96,384]{1,0:T(8,128)(2,1)S(1)} %copy-done.27), channel_id=1, source_target_pairs={{0,29},{1,28},{2,31},{3,30},{4,25},{5,24},{6,27},{7,26},{8,21},{9,... | collective-permute-start | bytes 221192 | tf_op jit(solution)/shard_map/ppermute | solution.py:278
  49.7 0.0 collective-permute-done.1.refs_1_
  49.7 2.6 %collective-permute-start.14 = (bf16[96,384]{1,0:T(8,128)(2,1)S(1)}, bf16[96,384]{1,0:T(8,128)(2,1)S(1)}, u32[]{:S(2)}, u32[]{:S(2)}) collective-permute-start(bf16[96,384]{1,0:T(8,128)(2,1)S(1)} %copy-done.26), channel_id=1, source_target_pairs={{0,30},{1,31},{2,28},{3,29},{4,26},{5,27},{6,24},{7,25},{8,22},{9,... | collective-permute-start | bytes 221192 | tf_op jit(solution)/shard_map/ppermute | solution.py:278
  52.3 0.0 collective-permute-done.10.refs_10_
  52.3 3.8 %collective-permute-start.15 = (bf16[96,384]{1,0:T(8,128)(2,1)S(1)}, bf16[96,384]{1,0:T(8,128)(2,1)S(1)}, u32[]{:S(2)}, u32[]{:S(2)}) collective-permute-start(bf16[96,384]{1,0:T(8,128)(2,1)S(1)} %copy-done.25), channel_id=1, source_target_pairs={{0,31},{1,30},{2,29},{3,28},{4,27},{5,26},{6,25},{7,24},{8,23},{9,... | collective-permute-start | bytes 221192 | tf_op jit(solution)/shard_map/ppermute | solution.py:278
  56.1 0.0 collective-permute-done.11.refs_11_
  56.1 0.5 collective-permute-start.2
  56.6 1.2 collective-permute-done.12.refs_12_
  57.8 1.1 collective-permute-start.3
  58.9 0.0 collective-permute-done.13.refs_13_
  58.9 7.3 %collective-permute-start.4 = (bf16[96,384]{1,0:T(8,128)(2,1)S(1)}, bf16[96,384]{1,0:T(8,128)(2,1)S(1)}, u32[]{:S(2)}, u32[]{:S(2)}) collective-permute-start(bf16[96,384]{1,0:T(8,128)(2,1)S(1)} %copy-done.22), channel_id=1, source_target_pairs={{0,20},{1,21},{2,22},{3,23},{4,16},{5,17},{6,18},{7,19},{8,28},{9,... | collective-permute-start | bytes 221192 | tf_op jit(solution)/shard_map/ppermute | solution.py:278
  66.2 0.0 all-to-all-done.factors_ref
  66.2 2.6 %near_products.1 = (bf16[8,192,384]{2,1,0:T(8,128)(2,1)}, bf16[16,144,128]{2,1,0:T(8,128)(2,1)}) custom-call(bf16[16,192,384]{2,1,0:T(8,128)(2,1)S(1)} %all-to-all-done.factors_ref), custom_call_target="tpu_custom_call" | custom-call | flops 226492416 | bytes 3538944 | tf_op jit(solution)/shard_map/near_products/pallas_call | solution.py:306
  68.9 3.7 %all-to-all-start.1 = ((bf16[16,144,128]{2,1,0:T(8,128)(2,1)}), bf16[16,144,128]{2,1,0:T(8,128)(2,1)S(1)}, u32[]{:S(2)}, u32[]{:S(2)}) async-start(bf16[16,144,128]{2,1,0:T(8,128)(2,1)} %get-tuple-element.25), calls=%async_computation.1 | async-start | bytes 1179648 | tf_op jit(solution)/shard_map/all_to_all | solution.py:316
  72.6 0.0 collective-permute-done.14.refs_14_
  72.6 4.2 %collective-permute-start.5 = (bf16[96,384]{1,0:T(8,128)(2,1)S(1)}, bf16[96,384]{1,0:T(8,128)(2,1)S(1)}, u32[]{:S(2)}, u32[]{:S(2)}) collective-permute-start(bf16[96,384]{1,0:T(8,128)(2,1)S(1)} %copy-done.21), channel_id=1, source_target_pairs={{0,21},{1,20},{2,23},{3,22},{4,17},{5,16},{6,19},{7,18},{8,29},{9,... | collective-permute-start | bytes 221192 | tf_op jit(solution)/shard_map/ppermute | solution.py:278
  76.8 0.0 collective-permute-done.15.refs_15_
  76.8 1.2 %collective-permute-start.6 = (bf16[96,384]{1,0:T(8,128)(2,1)S(1)}, bf16[96,384]{1,0:T(8,128)(2,1)S(1)}, u32[]{:S(2)}, u32[]{:S(2)}) collective-permute-start(bf16[96,384]{1,0:T(8,128)(2,1)S(1)} %copy-done.20), channel_id=1, source_target_pairs={{0,22},{1,23},{2,20},{3,21},{4,18},{5,19},{6,16},{7,17},{8,30},{9,... | collective-permute-start | bytes 221192 | tf_op jit(solution)/shard_map/ppermute | solution.py:278
  78.1 0.0 collective-permute-done.2.refs_2_
  78.1 3.3 %collective-permute-start.7 = (bf16[96,384]{1,0:T(8,128)(2,1)S(1)}, bf16[96,384]{1,0:T(8,128)(2,1)S(1)}, u32[]{:S(2)}, u32[]{:S(2)}) collective-permute-start(bf16[96,384]{1,0:T(8,128)(2,1)S(1)} %copy-done.19), channel_id=1, source_target_pairs={{0,23},{1,22},{2,21},{3,20},{4,19},{5,18},{6,17},{7,16},{8,31},{9,... | collective-permute-start | bytes 221192 | tf_op jit(solution)/shard_map/ppermute | solution.py:278
  81.4 0.0 collective-permute-done.3.refs_3_
  81.4 0.8 collective-permute-start.8
  82.2 0.0 collective-permute-done.4.refs_4_
  82.2 2.9 %collective-permute-start.9 = (bf16[96,384]{1,0:T(8,128)(2,1)S(1)}, bf16[96,384]{1,0:T(8,128)(2,1)S(1)}, u32[]{:S(2)}, u32[]{:S(2)}) collective-permute-start(bf16[96,384]{1,0:T(8,128)(2,1)S(1)} %copy-done.17), channel_id=1, source_target_pairs={{0,25},{1,24},{2,27},{3,26},{4,29},{5,28},{6,31},{7,30},{8,17},{9,... | collective-permute-start | bytes 221192 | tf_op jit(solution)/shard_map/ppermute | solution.py:278
  85.1 4.3 %gate.1.refs_17_.refs_2_ = bf16[12,384,128]{2,1,0:T(8,128)(2,1)} custom-call(bf16[12,384,128]{2,1,0:T(8,128)(2,1)} %pair_ref.3, f32[1,128]{1,0:T(1,128)} %bitcast.14, f32[1,128]{1,0:T(1,128)} %bitcast.16, bf16[128,128]{1,0:T(8,128)(2,1)} %gw_ref.1, f32[1,128]{1,0:T(1,128)} %bitcast.17), custom_call_target="tpu_custom_call" | custom-call | flops 137438953472 | bytes 2359296 | tf_op jit(solution)/shard_map/gate/pallas_call | solution.py:285
  89.5 0.0 collective-permute-done.5.refs_5_
  89.5 0.0 collective-permute-done.6.refs_6_
  89.5 0.0 collective-permute-done.7.refs_7_
  89.5 1.9 %collective-permute-done.8.refs_8_ = bf16[96,384]{1,0:T(8,128)(2,1)S(1)} collective-permute-done((bf16[96,384]{1,0:T(8,128)(2,1)S(1)}, bf16[96,384]{1,0:T(8,128)(2,1)S(1)}, u32[]{:S(2)}, u32[]{:S(2)}) %collective-permute-start.8) | collective-permute-done | bytes 73760 | tf_op jit(solution)/shard_map/ppermute | solution.py:278
  91.4 0.6 collective-permute-done.9.refs_9_
  92.0 0.0 all-to-all-done.1.refs_16_.refs_0_
  92.1 0.6 copy-done.16
  92.7 0.2 copy-done
  92.9 3.9 %far_products.1 = bf16[16,144,128]{2,1,0:T(8,128)(2,1)} custom-call(bf16[8,192,384]{2,1,0:T(8,128)(2,1)} %get-tuple-element.26.left_ref, bf16[96,384]{1,0:T(8,128)(2,1)} %copy-done.1, bf16[96,384]{1,0:T(8,128)(2,1)} %copy-done.2, bf16[96,384]{1,0:T(8,128)(2,1)} %copy-done.9, bf16[96,384]{1,0:T(8,128)(2,1)} %copy-done.10, bf16[96,384]{1,0:T(8,128)(2,1)} %copy-done.11, ...), custom_call_target="tpu_custom_call" | custom-call | flops 226492416 | bytes 3538944 | tf_op jit(solution)/shard_map/far_products/pallas_call | solution.py:318
  96.7 18.0 %all_to_all.15.refs_1_ = bf16[16,144,128]{2,1,0:T(8,128)(2,1)S(1)} all-to-all(bf16[16,144,128]{2,1,0:T(8,128)(2,1)} %far_products.1), channel_id=1, replica_groups=mesh['groups'=1,'part'=2,'chan'=8,'quarter'=2] {'chan','quarter'}, dimensions={0} | all-to-all | bytes 1179648 | tf_op jit(solution)/shard_map/all_to_all | solution.py:334
  114.8 4.3 %update.1 = bf16[12,384,128]{2,1,0:T(8,128)(2,1)} custom-call(bf16[16,144,128]{2,1,0:T(8,128)(2,1)} %copy-done, bf16[16,144,128]{2,1,0:T(8,128)(2,1)S(1)} %all_to_all.15.refs_1_, bf16[12,384,128]{2,1,0:T(8,128)(2,1)} %gate.1.refs_17_.refs_2_, f32[1,128]{1,0:T(1,128)} %bitcast.9, f32[1,128]{1,0:T(1,128)} %bitcast.10, bf16[128,128]{1,0:T(8,128)(2,1)} %refs_5_.1, ...), custom_call_target="tpu_custom_call" | custom-call | flops 150994944 | bytes 3538944 | tf_op jit(solution)/shard_map/update/pallas_call | solution.py:336
  (60 shorter events, 0.1 us)
Async XLA Ops:
  5.8 6.6 %copy-start.32 = (bf16[96,384]{1,0:T(8,128)(2,1)S(1)}, bf16[96,384]{1,0:T(8,128)(2,1)}, u32[]{:S(2)}) copy-start(bf16[96,384]{1,0:T(8,128)(2,1)} %get-tuple-element.27) | copy-start | bytes 221188
  5.8 9.2 %copy-start.31 = (bf16[96,384]{1,0:T(8,128)(2,1)S(1)}, bf16[96,384]{1,0:T(8,128)(2,1)}, u32[]{:S(2)}) copy-start(bf16[96,384]{1,0:T(8,128)(2,1)} %get-tuple-element.28) | copy-start | bytes 221188
  5.8 9.3 %copy-start.30 = (bf16[96,384]{1,0:T(8,128)(2,1)S(1)}, bf16[96,384]{1,0:T(8,128)(2,1)}, u32[]{:S(2)}) copy-start(bf16[96,384]{1,0:T(8,128)(2,1)} %get-tuple-element.37) | copy-start | bytes 221188
  5.8 13.9 %copy-start.29 = (bf16[96,384]{1,0:T(8,128)(2,1)S(1)}, bf16[96,384]{1,0:T(8,128)(2,1)}, u32[]{:S(2)}) copy-start(bf16[96,384]{1,0:T(8,128)(2,1)} %get-tuple-element.38) | copy-start | bytes 221188
  5.8 14.2 %copy-start.28 = (bf16[96,384]{1,0:T(8,128)(2,1)S(1)}, bf16[96,384]{1,0:T(8,128)(2,1)}, u32[]{:S(2)}) copy-start(bf16[96,384]{1,0:T(8,128)(2,1)} %get-tuple-element.39) | copy-start | bytes 221188
  5.9 36.9 %copy-start.27 = (bf16[96,384]{1,0:T(8,128)(2,1)S(1)}, bf16[96,384]{1,0:T(8,128)(2,1)}, u32[]{:S(2)}) copy-start(bf16[96,384]{1,0:T(8,128)(2,1)} %get-tuple-element.40) | copy-start | bytes 221188
  5.9 43.8 %copy-start.26 = (bf16[96,384]{1,0:T(8,128)(2,1)S(1)}, bf16[96,384]{1,0:T(8,128)(2,1)}, u32[]{:S(2)}) copy-start(bf16[96,384]{1,0:T(8,128)(2,1)} %get-tuple-element.41) | copy-start | bytes 221188
  5.9 46.4 %copy-start.25 = (bf16[96,384]{1,0:T(8,128)(2,1)S(1)}, bf16[96,384]{1,0:T(8,128)(2,1)}, u32[]{:S(2)}) copy-start(bf16[96,384]{1,0:T(8,128)(2,1)} %get-tuple-element.42) | copy-start | bytes 221188
  5.9 50.2 %copy-start.24 = (bf16[96,384]{1,0:T(8,128)(2,1)S(1)}, bf16[96,384]{1,0:T(8,128)(2,1)}, u32[]{:S(2)}) copy-start(bf16[96,384]{1,0:T(8,128)(2,1)} %get-tuple-element.29) | copy-start | bytes 221188
  5.9 51.9 %copy-start.23 = (bf16[96,384]{1,0:T(8,128)(2,1)S(1)}, bf16[96,384]{1,0:T(8,128)(2,1)}, u32[]{:S(2)}) copy-start(bf16[96,384]{1,0:T(8,128)(2,1)} %get-tuple-element.30) | copy-start | bytes 221188
  5.9 53.0 %copy-start.22 = (bf16[96,384]{1,0:T(8,128)(2,1)S(1)}, bf16[96,384]{1,0:T(8,128)(2,1)}, u32[]{:S(2)}) copy-start(bf16[96,384]{1,0:T(8,128)(2,1)} %get-tuple-element.31) | copy-start | bytes 221188
  5.9 60.3 %all-to-all-start = ((bf16[16,192,384]{2,1,0:T(8,128)(2,1)}), bf16[16,192,384]{2,1,0:T(8,128)(2,1)S(1)}, u32[]{:S(2)}, u32[]{:S(2)}) async-start(bf16[16,192,384]{2,1,0:T(8,128)(2,1)} %bitcast.8), calls=%async_computation | async-start | bytes 4718592 | tf_op jit(solution)/shard_map/all_to_all | solution.py:283
  12.4 30.4 %collective-permute-start = (bf16[96,384]{1,0:T(8,128)(2,1)S(1)}, bf16[96,384]{1,0:T(8,128)(2,1)S(1)}, u32[]{:S(2)}, u32[]{:S(2)}) collective-permute-start(bf16[96,384]{1,0:T(8,128)(2,1)S(1)} %copy-done.32), channel_id=1, source_target_pairs={{0,16},{1,17},{2,18},{3,19},{4,20},{5,21},{6,22},{7,23},{8,24},{9,... | collective-permute-start | bytes 221192 | tf_op jit(solution)/shard_map/ppermute | solution.py:278
  15.0 34.7 %collective-permute-start.1 = (bf16[96,384]{1,0:T(8,128)(2,1)S(1)}, bf16[96,384]{1,0:T(8,128)(2,1)S(1)}, u32[]{:S(2)}, u32[]{:S(2)}) collective-permute-start(bf16[96,384]{1,0:T(8,128)(2,1)S(1)} %copy-done.31), channel_id=1, source_target_pairs={{0,17},{1,16},{2,19},{3,18},{4,21},{5,20},{6,23},{7,22},{8,25},{9,... | collective-permute-start | bytes 221192 | tf_op jit(solution)/shard_map/ppermute | solution.py:278
  15.1 37.2 %collective-permute-start.10 = (bf16[96,384]{1,0:T(8,128)(2,1)S(1)}, bf16[96,384]{1,0:T(8,128)(2,1)S(1)}, u32[]{:S(2)}, u32[]{:S(2)}) collective-permute-start(bf16[96,384]{1,0:T(8,128)(2,1)S(1)} %copy-done.30), channel_id=1, source_target_pairs={{0,26},{1,27},{2,24},{3,25},{4,30},{5,31},{6,28},{7,29},{8,18},{9,... | collective-permute-start | bytes 221192 | tf_op jit(solution)/shard_map/ppermute | solution.py:278
  19.7 36.4 %collective-permute-start.11 = (bf16[96,384]{1,0:T(8,128)(2,1)S(1)}, bf16[96,384]{1,0:T(8,128)(2,1)S(1)}, u32[]{:S(2)}, u32[]{:S(2)}) collective-permute-start(bf16[96,384]{1,0:T(8,128)(2,1)S(1)} %copy-done.29), channel_id=1, source_target_pairs={{0,27},{1,26},{2,25},{3,24},{4,31},{5,30},{6,29},{7,28},{8,19},{9,... | collective-permute-start | bytes 221192 | tf_op jit(solution)/shard_map/ppermute | solution.py:278
  20.0 37.8 %collective-permute-start.12 = (bf16[96,384]{1,0:T(8,128)(2,1)S(1)}, bf16[96,384]{1,0:T(8,128)(2,1)S(1)}, u32[]{:S(2)}, u32[]{:S(2)}) collective-permute-start(bf16[96,384]{1,0:T(8,128)(2,1)S(1)} %copy-done.28), channel_id=1, source_target_pairs={{0,28},{1,29},{2,30},{3,31},{4,24},{5,25},{6,26},{7,27},{8,20},{9,... | collective-permute-start | bytes 221192 | tf_op jit(solution)/shard_map/ppermute | solution.py:278
  42.8 26.0 %copy-start.1 = (bf16[96,384]{1,0:T(8,128)(2,1)}, bf16[96,384]{1,0:T(8,128)(2,1)S(1)}, u32[]{:S(2)}) copy-start(bf16[96,384]{1,0:T(8,128)(2,1)S(1)} %collective-permute-done.refs_0_) | copy-start | bytes 221188
  42.8 16.1 %collective-permute-start.13 = (bf16[96,384]{1,0:T(8,128)(2,1)S(1)}, bf16[96,384]{1,0:T(8,128)(2,1)S(1)}, u32[]{:S(2)}, u32[]{:S(2)}) collective-permute-start(bf16[96,384]{1,0:T(8,128)(2,1)S(1)} %copy-done.27), channel_id=1, source_target_pairs={{0,29},{1,28},{2,31},{3,30},{4,25},{5,24},{6,27},{7,26},{8,21},{9,... | collective-permute-start | bytes 221192 | tf_op jit(solution)/shard_map/ppermute | solution.py:278
  49.7 19.1 %copy-start.2 = (bf16[96,384]{1,0:T(8,128)(2,1)}, bf16[96,384]{1,0:T(8,128)(2,1)S(1)}, u32[]{:S(2)}) copy-start(bf16[96,384]{1,0:T(8,128)(2,1)S(1)} %collective-permute-done.1.refs_1_) | copy-start | bytes 221188
  49.7 22.9 %collective-permute-start.14 = (bf16[96,384]{1,0:T(8,128)(2,1)S(1)}, bf16[96,384]{1,0:T(8,128)(2,1)S(1)}, u32[]{:S(2)}, u32[]{:S(2)}) collective-permute-start(bf16[96,384]{1,0:T(8,128)(2,1)S(1)} %copy-done.26), channel_id=1, source_target_pairs={{0,30},{1,31},{2,28},{3,29},{4,26},{5,27},{6,24},{7,25},{8,22},{9,... | collective-permute-start | bytes 221192 | tf_op jit(solution)/shard_map/ppermute | solution.py:278
  52.3 16.5 %copy-start.3 = (bf16[96,384]{1,0:T(8,128)(2,1)}, bf16[96,384]{1,0:T(8,128)(2,1)S(1)}, u32[]{:S(2)}) copy-start(bf16[96,384]{1,0:T(8,128)(2,1)S(1)} %collective-permute-done.10.refs_10_) | copy-start | bytes 221188
  52.3 24.6 %collective-permute-start.15 = (bf16[96,384]{1,0:T(8,128)(2,1)S(1)}, bf16[96,384]{1,0:T(8,128)(2,1)S(1)}, u32[]{:S(2)}, u32[]{:S(2)}) collective-permute-start(bf16[96,384]{1,0:T(8,128)(2,1)S(1)} %copy-done.25), channel_id=1, source_target_pairs={{0,31},{1,30},{2,29},{3,28},{4,27},{5,26},{6,25},{7,24},{8,23},{9,... | collective-permute-start | bytes 221192 | tf_op jit(solution)/shard_map/ppermute | solution.py:278
  56.1 12.7 %copy-start.4 = (bf16[96,384]{1,0:T(8,128)(2,1)}, bf16[96,384]{1,0:T(8,128)(2,1)S(1)}, u32[]{:S(2)}) copy-start(bf16[96,384]{1,0:T(8,128)(2,1)S(1)} %collective-permute-done.11.refs_11_) | copy-start | bytes 221188
  56.1 22.0 %collective-permute-start.2 = (bf16[96,384]{1,0:T(8,128)(2,1)S(1)}, bf16[96,384]{1,0:T(8,128)(2,1)S(1)}, u32[]{:S(2)}, u32[]{:S(2)}) collective-permute-start(bf16[96,384]{1,0:T(8,128)(2,1)S(1)} %copy-done.24), channel_id=1, source_target_pairs={{0,18},{1,19},{2,16},{3,17},{4,22},{5,23},{6,20},{7,21},{8,26},{9,... | collective-permute-start | bytes 221192 | tf_op jit(solution)/shard_map/ppermute | solution.py:278
  57.8 11.0 %copy-start.5 = (bf16[96,384]{1,0:T(8,128)(2,1)}, bf16[96,384]{1,0:T(8,128)(2,1)S(1)}, u32[]{:S(2)}) copy-start(bf16[96,384]{1,0:T(8,128)(2,1)S(1)} %collective-permute-done.12.refs_12_) | copy-start | bytes 221188
  57.8 23.6 %collective-permute-start.3 = (bf16[96,384]{1,0:T(8,128)(2,1)S(1)}, bf16[96,384]{1,0:T(8,128)(2,1)S(1)}, u32[]{:S(2)}, u32[]{:S(2)}) collective-permute-start(bf16[96,384]{1,0:T(8,128)(2,1)S(1)} %copy-done.23), channel_id=1, source_target_pairs={{0,19},{1,18},{2,17},{3,16},{4,23},{5,22},{6,21},{7,20},{8,27},{9,... | collective-permute-start | bytes 221192 | tf_op jit(solution)/shard_map/ppermute | solution.py:278
  58.9 10.0 %copy-start.6 = (bf16[96,384]{1,0:T(8,128)(2,1)}, bf16[96,384]{1,0:T(8,128)(2,1)S(1)}, u32[]{:S(2)}) copy-start(bf16[96,384]{1,0:T(8,128)(2,1)S(1)} %collective-permute-done.13.refs_13_) | copy-start | bytes 221188
  58.9 23.4 %collective-permute-start.4 = (bf16[96,384]{1,0:T(8,128)(2,1)S(1)}, bf16[96,384]{1,0:T(8,128)(2,1)S(1)}, u32[]{:S(2)}, u32[]{:S(2)}) collective-permute-start(bf16[96,384]{1,0:T(8,128)(2,1)S(1)} %copy-done.22), channel_id=1, source_target_pairs={{0,20},{1,21},{2,22},{3,23},{4,16},{5,17},{6,18},{7,19},{8,28},{9,... | collective-permute-start | bytes 221192 | tf_op jit(solution)/shard_map/ppermute | solution.py:278
  68.8 3.8 %copy-start.21 = (bf16[96,384]{1,0:T(8,128)(2,1)S(1)}, bf16[96,384]{1,0:T(8,128)(2,1)}, u32[]{:S(2)}) copy-start(bf16[96,384]{1,0:T(8,128)(2,1)} %get-tuple-element.32) | copy-start | bytes 221188
  68.8 8.0 %copy-start.20 = (bf16[96,384]{1,0:T(8,128)(2,1)S(1)}, bf16[96,384]{1,0:T(8,128)(2,1)}, u32[]{:S(2)}) copy-start(bf16[96,384]{1,0:T(8,128)(2,1)} %get-tuple-element.33) | copy-start | bytes 221188
  68.8 9.2 %copy-start.19 = (bf16[96,384]{1,0:T(8,128)(2,1)S(1)}, bf16[96,384]{1,0:T(8,128)(2,1)}, u32[]{:S(2)}) copy-start(bf16[96,384]{1,0:T(8,128)(2,1)} %get-tuple-element.34) | copy-start | bytes 221188
  68.9 12.5 %copy-start.18 = (bf16[96,384]{1,0:T(8,128)(2,1)S(1)}, bf16[96,384]{1,0:T(8,128)(2,1)}, u32[]{:S(2)}) copy-start(bf16[96,384]{1,0:T(8,128)(2,1)} %get-tuple-element.35) | copy-start | bytes 221188
  68.9 13.4 %copy-start.17 = (bf16[96,384]{1,0:T(8,128)(2,1)S(1)}, bf16[96,384]{1,0:T(8,128)(2,1)}, u32[]{:S(2)}) copy-start(bf16[96,384]{1,0:T(8,128)(2,1)} %get-tuple-element.36) | copy-start | bytes 221188
  68.9 23.2 %all-to-all-start.1 = ((bf16[16,144,128]{2,1,0:T(8,128)(2,1)}), bf16[16,144,128]{2,1,0:T(8,128)(2,1)S(1)}, u32[]{:S(2)}, u32[]{:S(2)}) async-start(bf16[16,144,128]{2,1,0:T(8,128)(2,1)} %get-tuple-element.25), calls=%async_computation.1 | async-start | bytes 1179648 | tf_op jit(solution)/shard_map/all_to_all | solution.py:316
  72.6 16.8 %copy-start.7 = (bf16[96,384]{1,0:T(8,128)(2,1)}, bf16[96,384]{1,0:T(8,128)(2,1)S(1)}, u32[]{:S(2)}) copy-start(bf16[96,384]{1,0:T(8,128)(2,1)S(1)} %collective-permute-done.14.refs_14_) | copy-start | bytes 221188
  72.6 16.8 %collective-permute-start.5 = (bf16[96,384]{1,0:T(8,128)(2,1)S(1)}, bf16[96,384]{1,0:T(8,128)(2,1)S(1)}, u32[]{:S(2)}, u32[]{:S(2)}) collective-permute-start(bf16[96,384]{1,0:T(8,128)(2,1)S(1)} %copy-done.21), channel_id=1, source_target_pairs={{0,21},{1,20},{2,23},{3,22},{4,17},{5,16},{6,19},{7,18},{8,29},{9,... | collective-permute-start | bytes 221192 | tf_op jit(solution)/shard_map/ppermute | solution.py:278
  76.8 12.6 %copy-start.8 = (bf16[96,384]{1,0:T(8,128)(2,1)}, bf16[96,384]{1,0:T(8,128)(2,1)S(1)}, u32[]{:S(2)}) copy-start(bf16[96,384]{1,0:T(8,128)(2,1)S(1)} %collective-permute-done.15.refs_15_) | copy-start | bytes 221188
  76.8 12.6 %collective-permute-start.6 = (bf16[96,384]{1,0:T(8,128)(2,1)S(1)}, bf16[96,384]{1,0:T(8,128)(2,1)S(1)}, u32[]{:S(2)}, u32[]{:S(2)}) collective-permute-start(bf16[96,384]{1,0:T(8,128)(2,1)S(1)} %copy-done.20), channel_id=1, source_target_pairs={{0,22},{1,23},{2,20},{3,21},{4,18},{5,19},{6,16},{7,17},{8,30},{9,... | collective-permute-start | bytes 221192 | tf_op jit(solution)/shard_map/ppermute | solution.py:278
  78.1 11.3 %copy-start.9 = (bf16[96,384]{1,0:T(8,128)(2,1)}, bf16[96,384]{1,0:T(8,128)(2,1)S(1)}, u32[]{:S(2)}) copy-start(bf16[96,384]{1,0:T(8,128)(2,1)S(1)} %collective-permute-done.2.refs_2_) | copy-start | bytes 221188
  78.1 11.4 %collective-permute-start.7 = (bf16[96,384]{1,0:T(8,128)(2,1)S(1)}, bf16[96,384]{1,0:T(8,128)(2,1)S(1)}, u32[]{:S(2)}, u32[]{:S(2)}) collective-permute-start(bf16[96,384]{1,0:T(8,128)(2,1)S(1)} %copy-done.19), channel_id=1, source_target_pairs={{0,23},{1,22},{2,21},{3,20},{4,19},{5,18},{6,17},{7,16},{8,31},{9,... | collective-permute-start | bytes 221192 | tf_op jit(solution)/shard_map/ppermute | solution.py:278
  81.4 8.1 %copy-start.10 = (bf16[96,384]{1,0:T(8,128)(2,1)}, bf16[96,384]{1,0:T(8,128)(2,1)S(1)}, u32[]{:S(2)}) copy-start(bf16[96,384]{1,0:T(8,128)(2,1)S(1)} %collective-permute-done.3.refs_3_) | copy-start | bytes 221188
  81.4 10.0 %collective-permute-start.8 = (bf16[96,384]{1,0:T(8,128)(2,1)S(1)}, bf16[96,384]{1,0:T(8,128)(2,1)S(1)}, u32[]{:S(2)}, u32[]{:S(2)}) collective-permute-start(bf16[96,384]{1,0:T(8,128)(2,1)S(1)} %copy-done.18), channel_id=1, source_target_pairs={{0,24},{1,25},{2,26},{3,27},{4,28},{5,29},{6,30},{7,31},{8,16},{9,... | collective-permute-start | bytes 221192 | tf_op jit(solution)/shard_map/ppermute | solution.py:278
  82.2 7.2 %copy-start.11 = (bf16[96,384]{1,0:T(8,128)(2,1)}, bf16[96,384]{1,0:T(8,128)(2,1)S(1)}, u32[]{:S(2)}) copy-start(bf16[96,384]{1,0:T(8,128)(2,1)S(1)} %collective-permute-done.4.refs_4_) | copy-start | bytes 221188
  82.2 9.8 %collective-permute-start.9 = (bf16[96,384]{1,0:T(8,128)(2,1)S(1)}, bf16[96,384]{1,0:T(8,128)(2,1)S(1)}, u32[]{:S(2)}, u32[]{:S(2)}) collective-permute-start(bf16[96,384]{1,0:T(8,128)(2,1)S(1)} %copy-done.17), channel_id=1, source_target_pairs={{0,25},{1,24},{2,27},{3,26},{4,29},{5,28},{6,31},{7,30},{8,17},{9,... | collective-permute-start | bytes 221192 | tf_op jit(solution)/shard_map/ppermute | solution.py:278
  89.5 2.6 %copy-start.12 = (bf16[96,384]{1,0:T(8,128)(2,1)}, bf16[96,384]{1,0:T(8,128)(2,1)S(1)}, u32[]{:S(2)}) copy-start(bf16[96,384]{1,0:T(8,128)(2,1)S(1)} %collective-permute-done.5.refs_5_) | copy-start | bytes 221188
  89.5 2.6 %copy-start.13 = (bf16[96,384]{1,0:T(8,128)(2,1)}, bf16[96,384]{1,0:T(8,128)(2,1)S(1)}, u32[]{:S(2)}) copy-start(bf16[96,384]{1,0:T(8,128)(2,1)S(1)} %collective-permute-done.6.refs_6_) | copy-start | bytes 221188
  89.5 2.5 %copy-start.14 = (bf16[96,384]{1,0:T(8,128)(2,1)}, bf16[96,384]{1,0:T(8,128)(2,1)S(1)}, u32[]{:S(2)}) copy-start(bf16[96,384]{1,0:T(8,128)(2,1)S(1)} %collective-permute-done.7.refs_7_) | copy-start | bytes 221188
  (3 other events, 2.1 us)

commit v7 on v4

--- a/solution.py
+++ b/solution.py
@@ -73,23 +73,36 @@
     )
 
 
-def right_kernel(pair_ref, gain_ref, shift_ref, w_ref, b_ref, out_ref, wt, bt):
-    @pl.when(pl.program_id(0) == 0)
-    def _():
-        wt[...] = w_ref[...].astype(f32).T.astype(bf16)
-        bt[...] = column(b_ref[...])
-
-    k, width = pair_ref.shape[1:]
-    x = pair_ref[...].astype(f32).reshape(STEP * k, width)
-    normed = normalize(x, gain_ref[...], shift_ref[...])
-    out = as_rows(factor(normed, wt[...], bt[...]), k).astype(bf16)
-    for p in range(out_ref.shape[0]):
-        out_ref[p] = out
-
-
-def left_kernel(pair_ref, gain_ref, shift_ref, w_ref, b_ref, *refs):
+def right_kernel(pair_ref, gain_ref, shift_ref, w_ref, b_ref, out_ref, pair, made, arrive, leave):
+    rows, k, width = pair.shape
+    starts = range(0, rows, STEP)
+    loads = [
+        pltpu.make_async_copy(pair_ref.at[pl.ds(r, STEP)], pair.at[pl.ds(r, STEP)], arrive.at[n])
+        for n, r in enumerate(starts)
+    ]
+    for load in loads:
+        load.start()
+    wt = w_ref[...].astype(f32).T.astype(bf16)
+    bt = column(b_ref[...])
+    stores = []
+    for n, r in enumerate(starts):
+        loads[n].wait()
+        x = pair[r : r + STEP].astype(f32).reshape(STEP * k, width)
+        normed = normalize(x, gain_ref[...], shift_ref[...])
+        at = pl.ds(r * BLOCK, STEP * BLOCK)
+        made[:, at, :] = as_rows(factor(normed, wt, bt), k).astype(bf16)
+        for p in range(out_ref.shape[0]):
+            stores.append(
+                pltpu.make_async_copy(made.at[:, at, :], out_ref.at[p, :, at, :], leave.at[p, n])
+            )
+            stores[-1].start()
+    for store in stores:
+        store.wait()
+
+
+def left_kernel(pair_ref, gain_ref, shift_ref, w_ref, b_ref, gw_ref, gb_ref, *refs):
     wf, bf, wt, bt = refs[-4:]
-    normed_ref = refs[-5]
+    gate_ref = refs[-5]
     outs = refs[:-5]
     k, width = pair_ref.shape[1:]
     hidden = w_ref.shape[1] // 2
@@ -111,17 +124,11 @@
 
     x = pair_ref[...].astype(f32).reshape(STEP * k, width)
     normed = normalize(x, gain_ref[...], shift_ref[...])
-    normed_ref[...] = normed.reshape(STEP, k, width)
+    gate = sigmoid(dot(normed, gw_ref[...]) + gb_ref[...])
+    gate_ref[...] = gate.reshape(STEP, k, width).astype(bf16)
     rows = as_rows(factor(normed, wt[...], bt[...]), k).astype(bf16)
     for b, out in enumerate(outs):
         out[...] = rows[b]
-
-
-def gate_kernel(normed_ref, gw_ref, gb_ref, gate_ref):
-    k, width = normed_ref.shape[1:]
-    normed = normed_ref[...].reshape(STEP * k, width)
-    gate = sigmoid(dot(normed, gw_ref[...]) + gb_ref[...])
-    gate_ref[...] = gate.reshape(gate_ref.shape).astype(gate_ref.dtype)
 
 
 def regroup(pieces, target, matrix):
@@ -169,24 +176,26 @@
     multiply(left, right_ref, right, held, store)
 
 
-def final_kernel(x_ref, gate_ref, g_ref, s_ref, w_ref, b_ref, out_ref, gt, st):
-    @pl.when(pl.program_id(0) == 0)
-    def _():
-        gt[...] = column(g_ref[...])
-        st[...] = column(s_ref[...])
-
+def final_kernel(x_ref, gate_ref, g_ref, s_ref, w_ref, b_ref, out_ref, made, leave):
     hosts, _, j = x_ref.shape
+    rows = gate_ref.shape[0]
     width = hosts * BLOCK
-    for r in range(0, STEP, 2):
+    gain, shift = widen(column(g_ref[...]), j), widen(column(s_ref[...]), j)
+    stores = []
+    for r in range(0, rows, 2):
         pair = x_ref[:, r * BLOCK : (r + 2) * BLOCK].astype(f32)
         for n in range(2):
             x = pair[:, n * BLOCK : (n + 1) * BLOCK].reshape(width, j)
             centered = x - jnp.mean(x, axis=0, keepdims=True)
             variance = jnp.mean(centered * centered, axis=0, keepdims=True)
-            normed = centered * lax.rsqrt(variance + epsilon)
-            normed = normed * widen(gt[...], j) + widen(st[...], j)
-            outward = dot(normed.T.astype(bf16), w_ref[...]) + b_ref[...]
-            out_ref[r + n] = (gate_ref[r + n].astype(f32) * outward).astype(bf16)
+            normed = centered * lax.rsqrt(variance + epsilon) * gain + shift
+            outward = dot(normed.astype(bf16).T, w_ref[...]) + b_ref[...]
+            made[r + n] = (gate_ref[r + n].astype(f32) * outward).astype(bf16)
+        at = pl.ds(r, 2)
+        stores.append(pltpu.make_async_copy(made.at[at], out_ref.at[at], leave.at[r // 2]))
+        stores[-1].start()
+    for store in stores:
+        store.wait()
 
 
 def whole(shape):
@@ -217,19 +226,26 @@
     work = rows * k * width
     bfloat = lambda *shape: jax.ShapeDtypeStruct(shape, bf16)
 
+    vmem = pl.BlockSpec(memory_space=pltpu.VMEM)
+    anywhere = pl.BlockSpec(memory_space=pl.ANY)
     right = pl.pallas_call(
         right_kernel,
-        grid=(steps,),
+        grid=(1,),
         in_specs=[
-            row_block,
+            anywhere,
             whole((1, width)),
             whole((1, width)),
             pl.BlockSpec((width, 2 * hidden), lambda s: (0, 1)),
             pl.BlockSpec((1, 2 * hidden), lambda s: (0, 1)),
         ],
-        out_specs=pl.BlockSpec((parts, hosts, STEP * BLOCK, k), lambda s: (0, 0, s, 0)),
+        out_specs=anywhere,
         out_shape=bfloat(parts, hosts, tall, k),
-        scratch_shapes=[pltpu.VMEM((2 * hidden, width), bf16), pltpu.VMEM((2 * hidden, LANES), f32)],
+        scratch_shapes=[
+            pltpu.VMEM((rows, k, width), bf16),
+            pltpu.VMEM((hosts, tall, k), bf16),
+            pltpu.SemaphoreType.DMA((steps,)),
+            pltpu.SemaphoreType.DMA((parts, steps)),
+        ],
         compiler_params=params(60),
         cost_estimate=cost(4 * work * hidden, 6 * work),
         name="right_factor",
@@ -237,12 +253,10 @@
     right = lax.all_to_all(right.reshape(devices, tall, k), everywhere, 0, 0, tiled=True)
 
     def send(values, b):
-        if b == 0:
-            return values
         pairs = [(p * hosts + h, p * hosts + (h ^ b)) for p in range(parts) for h in range(hosts)]
         return lax.ppermute(values, everywhere, pairs)
 
-    *lefts, normed = pl.pallas_call(
+    *lefts, gate = pl.pallas_call(
         left_kernel,
         grid=(steps,),
         in_specs=[
@@ -251,6 +265,8 @@
             whole((1, width)),
             whole((width, 2 * hidden)),
             whole((1, 2 * hidden)),
+            whole((width, width)),
+            whole((1, width)),
         ],
         out_specs=[pl.BlockSpec((STEP * BLOCK, k), lambda s: (s, 0))] * hosts + [row_block],
         out_shape=[bfloat(tall, k)] * hosts + [bfloat(*pair.shape)],
@@ -263,10 +279,17 @@
         compiler_params=params(),
         cost_estimate=cost(4 * work * hidden, 6 * work),
         name="left_factor",
-    )(pair, row(norm_gain), row(norm_shift), factor_weight, row(factor_bias))
-    lefts = [send(values, b) for b, values in enumerate(lefts)]
-
-    vmem = pl.BlockSpec(memory_space=pltpu.VMEM)
+    )(
+        pair,
+        row(norm_gain),
+        row(norm_shift),
+        factor_weight,
+        row(factor_bias),
+        gate_weight,
+        row(gate_bias),
+    )
+    lefts = [lefts[0]] + [send(lefts[b], b) for b in reversed(range(1, hosts))][::-1]
+
     left = pl.pallas_call(
         gather_kernel,
         in_specs=[vmem] * hosts,
@@ -276,17 +299,6 @@
         cost_estimate=cost(2 * work * BLOCK * SIZE, 4 * work),
         name="gather_left",
     )(*lefts)
-
-    gate = pl.pallas_call(
-        gate_kernel,
-        grid=(steps,),
-        in_specs=[row_block, whole((width, width)), whole((1, width))],
-        out_specs=row_block,
-        out_shape=bfloat(*pair.shape),
-        compiler_params=params(),
-        cost_estimate=cost(2 * work * width, 4 * work),
-        name="gate",
-    )(normed, gate_weight, row(gate_bias))
 
     span = GATHER * rows
     product = pl.pallas_call(
@@ -304,18 +316,10 @@
 
     return pl.pallas_call(
         final_kernel,
-        grid=(steps,),
-        in_specs=[
-            pl.BlockSpec((hosts, STEP * BLOCK, devices * rows), lambda s: (0, s, 0)),
-            row_block,
-            whole((1, hidden)),
-            whole((1, hidden)),
-            whole((hidden, width)),
-            whole((1, width)),
-        ],
-        out_specs=row_block,
+        in_specs=[vmem] * 6,
+        out_specs=anywhere,
         out_shape=bfloat(*pair.shape),
-        scratch_shapes=[pltpu.VMEM((hidden, LANES), f32), pltpu.VMEM((hidden, LANES), f32)],
+        scratch_shapes=[pltpu.VMEM(pair.shape, bf16), pltpu.SemaphoreType.DMA((rows // 2,))],
         compiler_params=params(),
         cost_estimate=cost(2 * work * width, 6 * work),
         name="update",

time: 97.4 us -> 94.8 us (0.973)
  blocking collectives: 0 us -> 21.8 us
  waiting for transfers between devices: 46.9 us -> 29.8 us
  starting transfers between devices: 31 us -> 26.5 us
  local copies, waits for them, and re-layouts: 4.47 us -> 2.73 us
  Pallas kernels: 14.4 us -> 13.4 us
    all_to_all x0 -> x1, blocking collectives: none -> 21.8 us  [shards(): product = lax.all_to_all(product, in_part, 0, 0, tiled=True)]
    all_to_all x1 -> x0, waiting for transfers between devices: 16.1 us -> none  [shards(): product = lax.all_to_all(product, in_part, 0, 0, tiled=True)]
    all_to_all x1 -> x0, starting transfers between devices: 4.42 us -> none  [shards(): product = lax.all_to_all(product, in_part, 0, 0, tiled=True)]
    unnamed x28 -> x26, local copies, waits for them, and re-layouts: 4.47 us -> 2.73 us
    pallas_call x3 -> x2, Pallas kernels: 8.7 us -> 7.45 us  [the longest x1 5.36 us: shards(): pl.pallas_call(right_kernel, grid=(1,), in_specs=[anywhere, whole((1, wid...]
    ppermute x15, waiting for transfers between devices: 30.8 us -> 29.8 us  [send(): return lax.ppermute(values, everywhere, pairs)]
  transfers between devices with their start and end apart: 17 -> 16, of which waited for: 9 -> 8; matrix products, arithmetic and copies ran while one was open for 0% -> 0% of each run, Pallas kernels for 4% -> 4%
where the time goes in v7:
time: 94.8 us; the launch traced here: 94.5 us
  waiting for transfers between devices  29.8 us (31%)
  starting transfers between devices  26.5 us (28%)
  blocking collectives  21.8 us (23%)
  Pallas kernels  13.4 us (14%)
  local copies, waits for them, and re-layouts  2.73 us (3%)
    ppermute x15, waiting for transfers between devices, send(): return lax.ppermute(values, everywhere, pairs)  29.8 us
    all_to_all x1, blocking collectives, shards(): product = lax.all_to_all(product, in_part, 0, 0, tiled=True)  21.8 us
    ppermute x15, starting transfers between devices, send(): return lax.ppermute(values, everywhere, pairs)  19.2 us
    all_to_all x1, starting transfers between devices, shards(): lax.all_to_all(right.reshape(devices, tall, k), everywhere, 0, 0, tiled=T...  7.3 us
    pallas_call x1, Pallas kernels, shards(): pl.pallas_call(right_kernel, grid=(1,), in_specs=[anywhere, whole((1, wid...  5.36 us
    pallas_call x1, Pallas kernels, shards(): pl.pallas_call(left_kernel, grid=(steps,), in_specs=[row_block, whole((1,...  3.01 us
    unnamed x26, local copies, waits for them, and re-layouts  2.73 us
    pallas_call x1, Pallas kernels, shards(): pl.pallas_call(product_kernel, grid=(devices // GATHER,), in_specs=[pl.Bl...  2.41 us
  transfers between devices with their start and end apart: 16, of which 8 were waited for; matrix products, arithmetic and copies ran while one was open for 0% of the time, Pallas kernels for 4%

profile of v7, /device:TPU:0, one launch (start us, length us, event | category | flops | bytes accessed | tf_op | source)
XLA Modules:
  0.0 94.5 jit_solution(16474540520136642781)
XLA Ops:
  0.0 5.4 %right_factor.1 = bf16[2,16,96,384]{3,2,1,0:T(8,128)(2,1)} custom-call(bf16[12,384,128]{2,1,0:T(8,128)(2,1)} %pair_ref.3, f32[1,128]{1,0:T(1,128)} %bitcast.12, f32[1,128]{1,0:T(1,128)} %bitcast.14, bf16[128,512]{1,0:T(8,128)(2,1)} %w_ref.4, f32[1,512]{1,0:T(1,128)} %bitcast.10), custom_call_target="tpu_custom_call" | custom-call | flops 301989888 | bytes 3538944 | tf_op jit(solution)/shard_map/right_factor/pallas_call | solution.py:231
  5.4 0.0 copy-start
  5.4 0.0 copy-start.6
  5.4 0.0 copy-start.7
  5.4 0.0 copy-start.8
  5.4 0.0 copy-start.9
  5.4 7.3 %all-to-all-start = ((bf16[32,96,384]{2,1,0:T(8,128)(2,1)}), bf16[32,96,384]{2,1,0:T(8,128)(2,1)S(1)}, u32[]{:S(2)}, u32[]{:S(2)}) async-start(bf16[32,96,384]{2,1,0:T(8,128)(2,1)} %bitcast.20), calls=%async_computation | async-start | bytes 4718592 | tf_op jit(solution)/shard_map/all_to_all | solution.py:253
  12.8 0.0 copy-start.3
  12.8 0.9 copy-done.3
  13.7 0.8 copy-done.5
  14.5 3.0 %left_factor.1 = (bf16[96,384]{1,0:T(8,128)(2,1)S(1)}, bf16[96,384]{1,0:T(8,128)(2,1)S(1)}, bf16[96,384]{1,0:T(8,128)(2,1)S(1)}, bf16[96,384]{1,0:T(8,128)(2,1)S...) custom-call(bf16[12,384,128]{2,1,0:T(8,128)(2,1)S(1)} %copy-done, ...), custom_call_target="tpu_custom_call" | custom-call | flops 301989888 | bytes 3538944 | tf_op jit(solution)/shard_map/left_factor/pallas_call | solution.py:259
  17.5 0.0 copy-start.1
  17.5 1.0 %copy-done.1 = bf16[12,384,128]{2,1,0:T(8,128)(2,1)} copy-done((bf16[12,384,128]{2,1,0:T(8,128)(2,1)}, bf16[12,384,128]{2,1,0:T(8,128)(2,1)S(1)}, u32[]{:S(2)}) %copy-start.1) | copy-done | bytes 1179672
  18.5 0.2 collective-permute-start
  18.7 1.7 %collective-permute-start.1 = (bf16[96,384]{1,0:T(8,128)(2,1)S(1)}, bf16[96,384]{1,0:T(8,128)(2,1)S(1)}, u32[]{:S(2)}, u32[]{:S(2)}) collective-permute-start(bf16[96,384]{1,0:T(8,128)(2,1)S(1)} %get-tuple-element.24), channel_id=1, source_target_pairs={{0,2},{1,3},{2,0},{3,1},{4,6},{5,7},{6,4},{7,5},{8,10},{9,11},{10,... | collective-permute-start | bytes 221192 | tf_op jit(solution)/shard_map/ppermute | solution.py:257
  20.4 1.7 %collective-permute-start.3 = (bf16[96,384]{1,0:T(8,128)(2,1)S(1)}, bf16[96,384]{1,0:T(8,128)(2,1)S(1)}, u32[]{:S(2)}, u32[]{:S(2)}) collective-permute-start(bf16[96,384]{1,0:T(8,128)(2,1)S(1)} %get-tuple-element.26), channel_id=1, source_target_pairs={{0,4},{1,5},{2,6},{3,7},{4,0},{5,1},{6,2},{7,3},{8,12},{9,13},{10,... | collective-permute-start | bytes 221192 | tf_op jit(solution)/shard_map/ppermute | solution.py:257
  22.1 0.1 collective-permute-start.4
  22.2 0.0 collective-permute-done.refs_1_
  22.2 2.6 %collective-permute-start.5 = (bf16[96,384]{1,0:T(8,128)(2,1)S(1)}, bf16[96,384]{1,0:T(8,128)(2,1)S(1)}, u32[]{:S(2)}, u32[]{:S(2)}) collective-permute-start(bf16[96,384]{1,0:T(8,128)(2,1)S(1)} %get-tuple-element.28), channel_id=1, source_target_pairs={{0,6},{1,7},{2,4},{3,5},{4,2},{5,3},{6,0},{7,1},{8,14},{9,15},{10,... | collective-permute-start | bytes 221192 | tf_op jit(solution)/shard_map/ppermute | solution.py:257
  24.8 7.5 %collective-permute-done.1.refs_2_ = bf16[96,384]{1,0:T(8,128)(2,1)S(1)} collective-permute-done((bf16[96,384]{1,0:T(8,128)(2,1)S(1)}, bf16[96,384]{1,0:T(8,128)(2,1)S(1)}, u32[]{:S(2)}, u32[]{:S(2)}) %collective-permute-start.1) | collective-permute-done | bytes 73760 | tf_op jit(solution)/shard_map/ppermute | solution.py:257
  32.3 0.6 collective-permute-start.6
  32.9 0.2 collective-permute-done.2.refs_3_
  33.1 0.3 collective-permute-start.7
  33.4 2.3 %collective-permute-start.8 = (bf16[96,384]{1,0:T(8,128)(2,1)S(1)}, bf16[96,384]{1,0:T(8,128)(2,1)S(1)}, u32[]{:S(2)}, u32[]{:S(2)}) collective-permute-start(bf16[96,384]{1,0:T(8,128)(2,1)S(1)} %get-tuple-element.31), channel_id=1, source_target_pairs={{0,9},{1,8},{2,11},{3,10},{4,13},{5,12},{6,15},{7,14},{8,1},{9,0},... | collective-permute-start | bytes 221192 | tf_op jit(solution)/shard_map/ppermute | solution.py:257
  35.7 0.0 collective-permute-done.4.refs_5_
  35.7 3.3 %collective-permute-start.9 = (bf16[96,384]{1,0:T(8,128)(2,1)S(1)}, bf16[96,384]{1,0:T(8,128)(2,1)S(1)}, u32[]{:S(2)}, u32[]{:S(2)}) collective-permute-start(bf16[96,384]{1,0:T(8,128)(2,1)S(1)} %get-tuple-element.32), channel_id=1, source_target_pairs={{0,10},{1,11},{2,8},{3,9},{4,14},{5,15},{6,12},{7,13},{8,2},{9,3},... | collective-permute-start | bytes 221192 | tf_op jit(solution)/shard_map/ppermute | solution.py:257
  38.9 3.9 %collective-permute-done.5.refs_6_ = bf16[96,384]{1,0:T(8,128)(2,1)S(1)} collective-permute-done((bf16[96,384]{1,0:T(8,128)(2,1)S(1)}, bf16[96,384]{1,0:T(8,128)(2,1)S(1)}, u32[]{:S(2)}, u32[]{:S(2)}) %collective-permute-start.5) | collective-permute-done | bytes 73760 | tf_op jit(solution)/shard_map/ppermute | solution.py:257
  42.8 0.0 collective-permute-start.10
  42.8 0.8 collective-permute-done.6.refs_7_
  43.6 10.4 %collective-permute-done.7.refs_8_ = bf16[96,384]{1,0:T(8,128)(2,1)S(1)} collective-permute-done((bf16[96,384]{1,0:T(8,128)(2,1)S(1)}, bf16[96,384]{1,0:T(8,128)(2,1)S(1)}, u32[]{:S(2)}, u32[]{:S(2)}) %collective-permute-start.7) | collective-permute-done | bytes 73760 | tf_op jit(solution)/shard_map/ppermute | solution.py:257
  54.0 2.0 %collective-permute-start.12 = (bf16[96,384]{1,0:T(8,128)(2,1)S(1)}, bf16[96,384]{1,0:T(8,128)(2,1)S(1)}, u32[]{:S(2)}, u32[]{:S(2)}) collective-permute-start(bf16[96,384]{1,0:T(8,128)(2,1)S(1)} %get-tuple-element.35), channel_id=1, source_target_pairs={{0,13},{1,12},{2,15},{3,14},{4,9},{5,8},{6,11},{7,10},{8,5},{9,4},... | collective-permute-start | bytes 221192 | tf_op jit(solution)/shard_map/ppermute | solution.py:257
  56.0 2.8 %collective-permute-start.13 = (bf16[96,384]{1,0:T(8,128)(2,1)S(1)}, bf16[96,384]{1,0:T(8,128)(2,1)S(1)}, u32[]{:S(2)}, u32[]{:S(2)}) collective-permute-start(bf16[96,384]{1,0:T(8,128)(2,1)S(1)} %get-tuple-element.36), channel_id=1, source_target_pairs={{0,14},{1,15},{2,12},{3,13},{4,10},{5,11},{6,8},{7,9},{8,6},{9,7},... | collective-permute-start | bytes 221192 | tf_op jit(solution)/shard_map/ppermute | solution.py:257
  58.8 1.7 %collective-permute-start.14 = (bf16[96,384]{1,0:T(8,128)(2,1)S(1)}, bf16[96,384]{1,0:T(8,128)(2,1)S(1)}, u32[]{:S(2)}, u32[]{:S(2)}) collective-permute-start(bf16[96,384]{1,0:T(8,128)(2,1)S(1)} %get-tuple-element.37), channel_id=1, source_target_pairs={{0,15},{1,14},{2,13},{3,12},{4,11},{5,10},{6,9},{7,8},{8,7},{9,6},... | collective-permute-start | bytes 221192 | tf_op jit(solution)/shard_map/ppermute | solution.py:257
  60.5 0.0 collective-permute-done.10.refs_11_
  60.5 0.0 collective-permute-done.11.refs_12_
  60.5 1.4 %collective-permute-done.12.refs_13_ = bf16[96,384]{1,0:T(8,128)(2,1)S(1)} collective-permute-done((bf16[96,384]{1,0:T(8,128)(2,1)S(1)}, bf16[96,384]{1,0:T(8,128)(2,1)S(1)}, u32[]{:S(2)}, u32[]{:S(2)}) %collective-permute-start.12) | collective-permute-done | bytes 73760 | tf_op jit(solution)/shard_map/ppermute | solution.py:257
  61.9 3.0 %collective-permute-done.13.refs_14_ = bf16[96,384]{1,0:T(8,128)(2,1)S(1)} collective-permute-done((bf16[96,384]{1,0:T(8,128)(2,1)S(1)}, bf16[96,384]{1,0:T(8,128)(2,1)S(1)}, u32[]{:S(2)}, u32[]{:S(2)}) %collective-permute-start.13) | collective-permute-done | bytes 73760 | tf_op jit(solution)/shard_map/ppermute | solution.py:257
  64.8 2.7 %collective-permute-done.14.refs_15_ = bf16[96,384]{1,0:T(8,128)(2,1)S(1)} collective-permute-done((bf16[96,384]{1,0:T(8,128)(2,1)S(1)}, bf16[96,384]{1,0:T(8,128)(2,1)S(1)}, u32[]{:S(2)}, u32[]{:S(2)}) %collective-permute-start.14) | collective-permute-done | bytes 73760 | tf_op jit(solution)/shard_map/ppermute | solution.py:257
  67.5 0.6 gather_left.1.left
  68.1 0.0 all-to-all-done
  68.1 2.4 %products.1 = bf16[16,96,384]{2,1,0:T(8,128)(2,1)S(1)} custom-call(bf16[3072,384]{1,0:T(8,128)(2,1)S(1)} %bitcast.9, bf16[8,192,384]{2,1,0:T(8,128)(2,1)S(1)} %gather_left.1.left), custom_call_target="tpu_custom_call" | custom-call | flops 226492416 | bytes 3538944 | tf_op jit(solution)/shard_map/products/pallas_call | solution.py:304
  70.5 0.0 copy-start.2
  70.6 0.0 copy-start.4
  70.6 0.0 copy-start.10
  70.6 0.0 copy-start.11
  70.6 0.0 copy-start.12
  70.6 21.8 %all_to_all.10.x_ref = bf16[16,96,384]{2,1,0:T(8,128)(2,1)S(1)} all-to-all(bf16[16,96,384]{2,1,0:T(8,128)(2,1)S(1)} %products.1), channel_id=1, replica_groups=mesh['groups'=1,'part'=2,'chan'=8,'quarter'=2] {'chan','quarter'}, dimensions={0} | all-to-all | bytes 2359296 | tf_op jit(solution)/shard_map/all_to_all | solution.py:315
  92.4 2.1 %update.1 = bf16[12,384,128]{2,1,0:T(8,128)(2,1)} custom-call(bf16[16,96,384]{2,1,0:T(8,128)(2,1)S(1)} %all_to_all.10.x_ref, bf16[12,384,128]{2,1,0:T(8,128)(2,1)S(1)} %copy-done.2, f32[1,128]{1,0:T(1,128)S(1)} %bitcast.17, f32[1,128]{1,0:T(1,128)S(1)} %bitcast.18, bf16[128,128]{1,0:T(8,128)(2,1)S(1)} %copy-done.4, f32[1,128]{1,0:T(1,128)S(1)} %bitcast.19), custom_call_target="tpu_custom_call" | custom-call | flops 150994944 | bytes 3538944 | tf_op jit(solution)/shard_map/update/pallas_call | solution.py:317
  (16 shorter events, 0.0 us)
Async XLA Ops:
  5.4 7.4 %copy-start = (bf16[12,384,128]{2,1,0:T(8,128)(2,1)S(1)}, bf16[12,384,128]{2,1,0:T(8,128)(2,1)}, u32[]{:S(2)}) copy-start(bf16[12,384,128]{2,1,0:T(8,128)(2,1)} %pair_ref.3) | copy-start | bytes 3538948
  5.4 7.4 %copy-start.6 = (f32[512]{0:T(512)S(1)}, f32[512]{0:T(512)}, u32[]{:S(2)}) copy-start(f32[512]{0:T(512)} %param.15) | copy-start | bytes 6148
  5.4 7.4 %copy-start.7 = (f32[128]{0:T(128)S(1)}, f32[128]{0:T(128)}, u32[]{:S(2)}) copy-start(f32[128]{0:T(128)} %param.12) | copy-start | bytes 1540
  5.4 7.4 %copy-start.8 = (f32[128]{0:T(128)S(1)}, f32[128]{0:T(128)}, u32[]{:S(2)}) copy-start(f32[128]{0:T(128)} %param.13) | copy-start | bytes 1540
  5.4 7.4 %copy-start.9 = (f32[128]{0:T(128)S(1)}, f32[128]{0:T(128)}, u32[]{:S(2)}) copy-start(f32[128]{0:T(128)} %param.17) | copy-start | bytes 1540
  5.4 62.7 %all-to-all-start = ((bf16[32,96,384]{2,1,0:T(8,128)(2,1)}), bf16[32,96,384]{2,1,0:T(8,128)(2,1)S(1)}, u32[]{:S(2)}, u32[]{:S(2)}) async-start(bf16[32,96,384]{2,1,0:T(8,128)(2,1)} %bitcast.20), calls=%async_computation | async-start | bytes 4718592 | tf_op jit(solution)/shard_map/all_to_all | solution.py:253
  12.8 0.9 copy-start.3
  13.7 0.8 copy-start.5
  17.5 1.0 %copy-start.1 = (bf16[12,384,128]{2,1,0:T(8,128)(2,1)}, bf16[12,384,128]{2,1,0:T(8,128)(2,1)S(1)}, u32[]{:S(2)}) copy-start(bf16[12,384,128]{2,1,0:T(8,128)(2,1)S(1)} %get-tuple-element.38.gate_ref) | copy-start | bytes 3538948
  18.5 3.7 %collective-permute-start = (bf16[96,384]{1,0:T(8,128)(2,1)S(1)}, bf16[96,384]{1,0:T(8,128)(2,1)S(1)}, u32[]{:S(2)}, u32[]{:S(2)}) collective-permute-start(bf16[96,384]{1,0:T(8,128)(2,1)S(1)} %get-tuple-element.23), channel_id=1, source_target_pairs={{0,1},{1,0},{2,3},{3,2},{4,5},{5,4},{6,7},{7,6},{8,9},{9,8},{10,11... | collective-permute-start | bytes 221192 | tf_op jit(solution)/shard_map/ppermute | solution.py:257
  18.7 13.6 %collective-permute-start.1 = (bf16[96,384]{1,0:T(8,128)(2,1)S(1)}, bf16[96,384]{1,0:T(8,128)(2,1)S(1)}, u32[]{:S(2)}, u32[]{:S(2)}) collective-permute-start(bf16[96,384]{1,0:T(8,128)(2,1)S(1)} %get-tuple-element.24), channel_id=1, source_target_pairs={{0,2},{1,3},{2,0},{3,1},{4,6},{5,7},{6,4},{7,5},{8,10},{9,11},{10,... | collective-permute-start | bytes 221192 | tf_op jit(solution)/shard_map/ppermute | solution.py:257
  20.4 12.7 %collective-permute-start.2 = (bf16[96,384]{1,0:T(8,128)(2,1)S(1)}, bf16[96,384]{1,0:T(8,128)(2,1)S(1)}, u32[]{:S(2)}, u32[]{:S(2)}) collective-permute-start(bf16[96,384]{1,0:T(8,128)(2,1)S(1)} %get-tuple-element.25), channel_id=1, source_target_pairs={{0,3},{1,2},{2,1},{3,0},{4,7},{5,6},{6,5},{7,4},{8,11},{9,10},{10,... | collective-permute-start | bytes 221192 | tf_op jit(solution)/shard_map/ppermute | solution.py:257
  20.4 13.0 %collective-permute-start.3 = (bf16[96,384]{1,0:T(8,128)(2,1)S(1)}, bf16[96,384]{1,0:T(8,128)(2,1)S(1)}, u32[]{:S(2)}, u32[]{:S(2)}) collective-permute-start(bf16[96,384]{1,0:T(8,128)(2,1)S(1)} %get-tuple-element.26), channel_id=1, source_target_pairs={{0,4},{1,5},{2,6},{3,7},{4,0},{5,1},{6,2},{7,3},{8,12},{9,13},{10,... | collective-permute-start | bytes 221192 | tf_op jit(solution)/shard_map/ppermute | solution.py:257
  22.1 13.5 %collective-permute-start.4 = (bf16[96,384]{1,0:T(8,128)(2,1)S(1)}, bf16[96,384]{1,0:T(8,128)(2,1)S(1)}, u32[]{:S(2)}, u32[]{:S(2)}) collective-permute-start(bf16[96,384]{1,0:T(8,128)(2,1)S(1)} %get-tuple-element.27), channel_id=1, source_target_pairs={{0,5},{1,4},{2,7},{3,6},{4,1},{5,0},{6,3},{7,2},{8,13},{9,12},{10,... | collective-permute-start | bytes 221192 | tf_op jit(solution)/shard_map/ppermute | solution.py:257
  22.2 20.5 %collective-permute-start.5 = (bf16[96,384]{1,0:T(8,128)(2,1)S(1)}, bf16[96,384]{1,0:T(8,128)(2,1)S(1)}, u32[]{:S(2)}, u32[]{:S(2)}) collective-permute-start(bf16[96,384]{1,0:T(8,128)(2,1)S(1)} %get-tuple-element.28), channel_id=1, source_target_pairs={{0,6},{1,7},{2,4},{3,5},{4,2},{5,3},{6,0},{7,1},{8,14},{9,15},{10,... | collective-permute-start | bytes 221192 | tf_op jit(solution)/shard_map/ppermute | solution.py:257
  32.3 11.3 %collective-permute-start.6 = (bf16[96,384]{1,0:T(8,128)(2,1)S(1)}, bf16[96,384]{1,0:T(8,128)(2,1)S(1)}, u32[]{:S(2)}, u32[]{:S(2)}) collective-permute-start(bf16[96,384]{1,0:T(8,128)(2,1)S(1)} %get-tuple-element.29), channel_id=1, source_target_pairs={{0,7},{1,6},{2,5},{3,4},{4,3},{5,2},{6,1},{7,0},{8,15},{9,14},{10,... | collective-permute-start | bytes 221192 | tf_op jit(solution)/shard_map/ppermute | solution.py:257
  33.1 20.8 %collective-permute-start.7 = (bf16[96,384]{1,0:T(8,128)(2,1)S(1)}, bf16[96,384]{1,0:T(8,128)(2,1)S(1)}, u32[]{:S(2)}, u32[]{:S(2)}) collective-permute-start(bf16[96,384]{1,0:T(8,128)(2,1)S(1)} %get-tuple-element.30), channel_id=1, source_target_pairs={{0,8},{1,9},{2,10},{3,11},{4,12},{5,13},{6,14},{7,15},{8,0},{9,1},... | collective-permute-start | bytes 221192 | tf_op jit(solution)/shard_map/ppermute | solution.py:257
  33.4 22.6 %collective-permute-start.8 = (bf16[96,384]{1,0:T(8,128)(2,1)S(1)}, bf16[96,384]{1,0:T(8,128)(2,1)S(1)}, u32[]{:S(2)}, u32[]{:S(2)}) collective-permute-start(bf16[96,384]{1,0:T(8,128)(2,1)S(1)} %get-tuple-element.31), channel_id=1, source_target_pairs={{0,9},{1,8},{2,11},{3,10},{4,13},{5,12},{6,15},{7,14},{8,1},{9,0},... | collective-permute-start | bytes 221192 | tf_op jit(solution)/shard_map/ppermute | solution.py:257
  35.7 23.1 %collective-permute-start.9 = (bf16[96,384]{1,0:T(8,128)(2,1)S(1)}, bf16[96,384]{1,0:T(8,128)(2,1)S(1)}, u32[]{:S(2)}, u32[]{:S(2)}) collective-permute-start(bf16[96,384]{1,0:T(8,128)(2,1)S(1)} %get-tuple-element.32), channel_id=1, source_target_pairs={{0,10},{1,11},{2,8},{3,9},{4,14},{5,15},{6,12},{7,13},{8,2},{9,3},... | collective-permute-start | bytes 221192 | tf_op jit(solution)/shard_map/ppermute | solution.py:257
  42.8 17.7 %collective-permute-start.10 = (bf16[96,384]{1,0:T(8,128)(2,1)S(1)}, bf16[96,384]{1,0:T(8,128)(2,1)S(1)}, u32[]{:S(2)}, u32[]{:S(2)}) collective-permute-start(bf16[96,384]{1,0:T(8,128)(2,1)S(1)} %get-tuple-element.33), channel_id=1, source_target_pairs={{0,11},{1,10},{2,9},{3,8},{4,15},{5,14},{6,13},{7,12},{8,3},{9,2},... | collective-permute-start | bytes 221192 | tf_op jit(solution)/shard_map/ppermute | solution.py:257
  43.6 16.9 %collective-permute-start.11 = (bf16[96,384]{1,0:T(8,128)(2,1)S(1)}, bf16[96,384]{1,0:T(8,128)(2,1)S(1)}, u32[]{:S(2)}, u32[]{:S(2)}) collective-permute-start(bf16[96,384]{1,0:T(8,128)(2,1)S(1)} %get-tuple-element.34), channel_id=1, source_target_pairs={{0,12},{1,13},{2,14},{3,15},{4,8},{5,9},{6,10},{7,11},{8,4},{9,5},... | collective-permute-start | bytes 221192 | tf_op jit(solution)/shard_map/ppermute | solution.py:257
  54.0 7.9 %collective-permute-start.12 = (bf16[96,384]{1,0:T(8,128)(2,1)S(1)}, bf16[96,384]{1,0:T(8,128)(2,1)S(1)}, u32[]{:S(2)}, u32[]{:S(2)}) collective-permute-start(bf16[96,384]{1,0:T(8,128)(2,1)S(1)} %get-tuple-element.35), channel_id=1, source_target_pairs={{0,13},{1,12},{2,15},{3,14},{4,9},{5,8},{6,11},{7,10},{8,5},{9,4},... | collective-permute-start | bytes 221192 | tf_op jit(solution)/shard_map/ppermute | solution.py:257
  56.0 8.9 %collective-permute-start.13 = (bf16[96,384]{1,0:T(8,128)(2,1)S(1)}, bf16[96,384]{1,0:T(8,128)(2,1)S(1)}, u32[]{:S(2)}, u32[]{:S(2)}) collective-permute-start(bf16[96,384]{1,0:T(8,128)(2,1)S(1)} %get-tuple-element.36), channel_id=1, source_target_pairs={{0,14},{1,15},{2,12},{3,13},{4,10},{5,11},{6,8},{7,9},{8,6},{9,7},... | collective-permute-start | bytes 221192 | tf_op jit(solution)/shard_map/ppermute | solution.py:257
  58.8 8.8 %collective-permute-start.14 = (bf16[96,384]{1,0:T(8,128)(2,1)S(1)}, bf16[96,384]{1,0:T(8,128)(2,1)S(1)}, u32[]{:S(2)}, u32[]{:S(2)}) collective-permute-start(bf16[96,384]{1,0:T(8,128)(2,1)S(1)} %get-tuple-element.37), channel_id=1, source_target_pairs={{0,15},{1,14},{2,13},{3,12},{4,11},{5,10},{6,9},{7,8},{8,7},{9,6},... | collective-permute-start | bytes 221192 | tf_op jit(solution)/shard_map/ppermute | solution.py:257
  70.5 21.8 %copy-start.2 = (bf16[12,384,128]{2,1,0:T(8,128)(2,1)S(1)}, bf16[12,384,128]{2,1,0:T(8,128)(2,1)}, u32[]{:S(2)}) copy-start(bf16[12,384,128]{2,1,0:T(8,128)(2,1)} %copy-done.1) | copy-start | bytes 3538948
  70.6 21.8 %copy-start.4 = (bf16[128,128]{1,0:T(8,128)(2,1)S(1)}, bf16[128,128]{1,0:T(8,128)(2,1)}, u32[]{:S(2)}) copy-start(bf16[128,128]{1,0:T(8,128)(2,1)} %w_ref.5) | copy-start | bytes 98308
  70.6 21.8 %copy-start.10 = (f32[128]{0:T(128)S(1)}, f32[128]{0:T(128)}, u32[]{:S(2)}) copy-start(f32[128]{0:T(128)} %param.18) | copy-start | bytes 1540
  70.6 21.8 %copy-start.11 = (f32[128]{0:T(128)S(1)}, f32[128]{0:T(128)}, u32[]{:S(2)}) copy-start(f32[128]{0:T(128)} %param.19) | copy-start | bytes 1540
  70.6 21.8 %copy-start.12 = (f32[128]{0:T(128)S(1)}, f32[128]{0:T(128)}, u32[]{:S(2)}) copy-start(f32[128]{0:T(128)} %param.21) | copy-start | bytes 1540

commit v8 on v7

--- a/solution.py
+++ b/solution.py
@@ -12,6 +12,7 @@
 CHANNELS = 128
 BLOCK = 8
 STEP = 4
+PAIRED = 2
 SIZE = 32
 LANES = 128
 GATHER = 32
@@ -66,38 +67,64 @@
     return sigmoid(gate) * value
 
 
-def as_rows(values, k):
+def as_rows(values, k, step=STEP):
     hosts = values.shape[0] // BLOCK
     return jnp.concatenate(
-        [values[:, r * k : (r + 1) * k].reshape(hosts, BLOCK, k) for r in range(STEP)], axis=1
+        [values[:, r * k : (r + 1) * k].reshape(hosts, BLOCK, k) for r in range(step)], axis=1
     )
 
 
-def right_kernel(pair_ref, gain_ref, shift_ref, w_ref, b_ref, out_ref, pair, made, arrive, leave):
+def right_kernel(
+    pair_ref, gain_ref, shift_ref, w_ref, b_ref, out_ref, pair, gain, shift, w, bias, wt, bt, made,
+    arrive, leave, sems,
+):
     rows, k, width = pair.shape
-    starts = range(0, rows, STEP)
+    parts, hosts = out_ref.shape[:2]
+    half = w.shape[1]
     loads = [
-        pltpu.make_async_copy(pair_ref.at[pl.ds(r, STEP)], pair.at[pl.ds(r, STEP)], arrive.at[n])
-        for n, r in enumerate(starts)
+        pltpu.make_async_copy(ref, to, sems.at[n])
+        for n, (ref, to) in enumerate(
+            [
+                (w_ref.at[:, pl.ds(half, half)], w),
+                (b_ref.at[:, pl.ds(half, half)], bias),
+                (gain_ref, gain),
+                (shift_ref, shift),
+            ]
+        )
     ]
-    for load in loads:
-        load.start()
-    wt = w_ref[...].astype(f32).T.astype(bf16)
-    bt = column(b_ref[...])
-    stores = []
-    for n, r in enumerate(starts):
-        loads[n].wait()
-        x = pair[r : r + STEP].astype(f32).reshape(STEP * k, width)
-        normed = normalize(x, gain_ref[...], shift_ref[...])
-        at = pl.ds(r * BLOCK, STEP * BLOCK)
-        made[:, at, :] = as_rows(factor(normed, wt, bt), k).astype(bf16)
-        for p in range(out_ref.shape[0]):
-            stores.append(
-                pltpu.make_async_copy(made.at[:, at, :], out_ref.at[p, :, at, :], leave.at[p, n])
-            )
-            stores[-1].start()
-    for store in stores:
-        store.wait()
+
+    def load(n):
+        at = pl.ds(n * PAIRED, PAIRED)
+        return pltpu.make_async_copy(pair_ref.at[at], pair.at[at], arrive.at[n])
+
+    def store(p, n):
+        at = pl.ds(pl.multiple_of(n * PAIRED * BLOCK, 16), PAIRED * BLOCK)
+        return pltpu.make_async_copy(made.at[:, at, :], out_ref.at[p, :, at, :], leave.at[p, n])
+
+    load(0).start()
+    for copy in loads:
+        copy.start()
+    for n in range(1, rows // PAIRED):
+        load(n).start()
+    for copy in loads:
+        copy.wait()
+    wt[...] = w[...].astype(f32).T.astype(bf16)
+    bt[...] = column(bias[...])
+
+    @pl.loop(0, rows // PAIRED)
+    def _(n):
+        load(n).wait()
+        x = pair[pl.ds(n * PAIRED, PAIRED)].astype(f32).reshape(PAIRED * k, width)
+        normed = normalize(x, gain[...], shift[...])
+        values = as_rows(factor(normed, wt[...], bt[...]), k, PAIRED).astype(bf16)
+        made[:, pl.ds(pl.multiple_of(n * PAIRED * BLOCK, 16), PAIRED * BLOCK), :] = values
+        for p in range(parts):
+            store(p, n).start()
+
+    @pl.loop(0, rows // PAIRED)
+    def _(n):
+        for p in range(parts):
+            store(p, n).wait()
 
 
 def left_kernel(pair_ref, gain_ref, shift_ref, w_ref, b_ref, gw_ref, gb_ref, *refs):
@@ -176,26 +203,35 @@
     multiply(left, right_ref, right, held, store)
 
 
-def final_kernel(x_ref, gate_ref, g_ref, s_ref, w_ref, b_ref, out_ref, made, leave):
+def final_kernel(x_ref, gate_ref, g_ref, s_ref, w_ref, b_ref, out_ref, gain, shift, made, leave):
     hosts, _, j = x_ref.shape
     rows = gate_ref.shape[0]
     width = hosts * BLOCK
-    gain, shift = widen(column(g_ref[...]), j), widen(column(s_ref[...]), j)
-    stores = []
-    for r in range(0, rows, 2):
-        pair = x_ref[:, r * BLOCK : (r + 2) * BLOCK].astype(f32)
-        for n in range(2):
-            x = pair[:, n * BLOCK : (n + 1) * BLOCK].reshape(width, j)
+    gain[...] = column(g_ref[...])
+    shift[...] = column(s_ref[...])
+
+    def store(n):
+        at = pl.ds(n * PAIRED, PAIRED)
+        return pltpu.make_async_copy(made.at[at], out_ref.at[at], leave.at[n])
+
+    @pl.loop(0, rows // PAIRED)
+    def _(n):
+        at = pl.ds(pl.multiple_of(n * PAIRED * BLOCK, 16), PAIRED * BLOCK)
+        pair = x_ref[:, at].astype(f32)
+        for m in range(PAIRED):
+            x = pair[:, m * BLOCK : (m + 1) * BLOCK].reshape(width, j)
             centered = x - jnp.mean(x, axis=0, keepdims=True)
             variance = jnp.mean(centered * centered, axis=0, keepdims=True)
-            normed = centered * lax.rsqrt(variance + epsilon) * gain + shift
+            normed = centered * lax.rsqrt(variance + epsilon)
+            normed = normed * widen(gain[...], j) + widen(shift[...], j)
             outward = dot(normed.astype(bf16).T, w_ref[...]) + b_ref[...]
-            made[r + n] = (gate_ref[r + n].astype(f32) * outward).astype(bf16)
-        at = pl.ds(r, 2)
-        stores.append(pltpu.make_async_copy(made.at[at], out_ref.at[at], leave.at[r // 2]))
-        stores[-1].start()
-    for store in stores:
-        store.wait()
+            row = n * PAIRED + m
+            made[row] = (gate_ref[row].astype(f32) * outward).astype(bf16)
+        store(n).start()
+
+    @pl.loop(0, rows // PAIRED)
+    def _(n):
+        store(n).wait()
 
 
 def whole(shape):
@@ -228,23 +264,24 @@
 
     vmem = pl.BlockSpec(memory_space=pltpu.VMEM)
     anywhere = pl.BlockSpec(memory_space=pl.ANY)
+    turns = rows // PAIRED
     right = pl.pallas_call(
         right_kernel,
-        grid=(1,),
-        in_specs=[
-            anywhere,
-            whole((1, width)),
-            whole((1, width)),
-            pl.BlockSpec((width, 2 * hidden), lambda s: (0, 1)),
-            pl.BlockSpec((1, 2 * hidden), lambda s: (0, 1)),
-        ],
+        in_specs=[anywhere] * 5,
         out_specs=anywhere,
         out_shape=bfloat(parts, hosts, tall, k),
         scratch_shapes=[
             pltpu.VMEM((rows, k, width), bf16),
+            pltpu.VMEM((1, width), f32),
+            pltpu.VMEM((1, width), f32),
+            pltpu.VMEM((width, 2 * hidden), bf16),
+            pltpu.VMEM((1, 2 * hidden), f32),
+            pltpu.VMEM((2 * hidden, width), bf16),
+            pltpu.VMEM((2 * hidden, LANES), f32),
             pltpu.VMEM((hosts, tall, k), bf16),
-            pltpu.SemaphoreType.DMA((steps,)),
-            pltpu.SemaphoreType.DMA((parts, steps)),
+            pltpu.SemaphoreType.DMA((turns,)),
+            pltpu.SemaphoreType.DMA((parts, turns)),
+            pltpu.SemaphoreType.DMA((4,)),
         ],
         compiler_params=params(60),
         cost_estimate=cost(4 * work * hidden, 6 * work),
@@ -319,7 +356,12 @@
         in_specs=[vmem] * 6,
         out_specs=anywhere,
         out_shape=bfloat(*pair.shape),
-        scratch_shapes=[pltpu.VMEM(pair.shape, bf16), pltpu.SemaphoreType.DMA((rows // 2,))],
+        scratch_shapes=[
+            pltpu.VMEM((hidden, LANES), f32),
+            pltpu.VMEM((hidden, LANES), f32),
+            pltpu.VMEM(pair.shape, bf16),
+            pltpu.SemaphoreType.DMA((turns,)),
+        ],
         compiler_params=params(),
         cost_estimate=cost(2 * work * width, 6 * work),
         name="update",

time: 94.8 us -> 95.7 us (level)
  Pallas kernels: 13.4 us -> 14.4 us
where the time goes in v8:
time: 95.7 us; the launch traced here: 95.4 us
  waiting for transfers between devices  29.8 us (31%)
  starting transfers between devices  26.5 us (28%)
  blocking collectives  21.8 us (23%)
  Pallas kernels  14.4 us (15%)
  local copies, waits for them, and re-layouts  2.73 us (3%)
    ppermute x15, waiting for transfers between devices, send(): return lax.ppermute(values, everywhere, pairs)  29.8 us
    all_to_all x1, blocking collectives, shards(): product = lax.all_to_all(product, in_part, 0, 0, tiled=True)  21.8 us
    ppermute x15, starting transfers between devices, send(): return lax.ppermute(values, everywhere, pairs)  19.2 us
    all_to_all x1, starting transfers between devices, shards(): lax.all_to_all(right.reshape(devices, tall, k), everywhere, 0, 0, tiled=T...  7.3 us
    pallas_call x1, Pallas kernels, shards(): pl.pallas_call(right_kernel, in_specs=[anywhere] * 5, out_specs=anywhere,...  5.43 us
    pallas_call x1, Pallas kernels, shards(): pl.pallas_call(left_kernel, grid=(steps,), in_specs=[row_block, whole((1,...  3.01 us
    pallas_call x1, Pallas kernels, shards(): pl.pallas_call(final_kernel, in_specs=[vmem] * 6, out_specs=anywhere, out...  2.97 us
    unnamed x26, local copies, waits for them, and re-layouts  2.73 us
  transfers between devices with their start and end apart: 16, of which 8 were waited for; matrix products, arithmetic and copies ran while one was open for 0% of the time, Pallas kernels for 4%

profile of v8, /device:TPU:0, one launch (start us, length us, event | category | flops | bytes accessed | tf_op | source)
XLA Modules:
  0.0 95.4 jit_solution(17334279737055546190)
XLA Ops:
  0.0 5.4 %right_factor.1 = bf16[2,16,96,384]{3,2,1,0:T(8,128)(2,1)} custom-call(bf16[12,384,128]{2,1,0:T(8,128)(2,1)} %pair_ref.3, f32[1,128]{1,0:T(1,128)} %bitcast.12, f32[1,128]{1,0:T(1,128)} %bitcast.14, bf16[128,512]{1,0:T(8,128)(2,1)} %w_ref.4, f32[1,512]{1,0:T(1,128)} %bitcast.10), custom_call_target="tpu_custom_call" | custom-call | flops 301989888 | bytes 3538944 | tf_op jit(solution)/shard_map/right_factor/pallas_call | solution.py:268
  5.4 0.0 copy-start
  5.4 0.0 copy-start.6
  5.5 0.0 copy-start.7
  5.5 0.0 copy-start.8
  5.5 0.0 copy-start.9
  5.5 7.3 %all-to-all-start = ((bf16[32,96,384]{2,1,0:T(8,128)(2,1)}), bf16[32,96,384]{2,1,0:T(8,128)(2,1)S(1)}, u32[]{:S(2)}, u32[]{:S(2)}) async-start(bf16[32,96,384]{2,1,0:T(8,128)(2,1)} %bitcast.20), calls=%async_computation | async-start | bytes 4718592 | tf_op jit(solution)/shard_map/all_to_all | solution.py:290
  12.9 0.0 copy-start.3
  12.9 0.9 copy-done.3
  13.8 0.8 copy-done.5
  14.5 3.0 %left_factor.1 = (bf16[96,384]{1,0:T(8,128)(2,1)S(1)}, bf16[96,384]{1,0:T(8,128)(2,1)S(1)}, bf16[96,384]{1,0:T(8,128)(2,1)S(1)}, bf16[96,384]{1,0:T(8,128)(2,1)S...) custom-call(bf16[12,384,128]{2,1,0:T(8,128)(2,1)S(1)} %copy-done, ...), custom_call_target="tpu_custom_call" | custom-call | flops 301989888 | bytes 3538944 | tf_op jit(solution)/shard_map/left_factor/pallas_call | solution.py:296
  17.5 0.0 copy-start.1
  17.5 1.0 %copy-done.1 = bf16[12,384,128]{2,1,0:T(8,128)(2,1)} copy-done((bf16[12,384,128]{2,1,0:T(8,128)(2,1)}, bf16[12,384,128]{2,1,0:T(8,128)(2,1)S(1)}, u32[]{:S(2)}) %copy-start.1) | copy-done | bytes 1179672
  18.6 0.2 collective-permute-start
  18.8 1.7 %collective-permute-start.1 = (bf16[96,384]{1,0:T(8,128)(2,1)S(1)}, bf16[96,384]{1,0:T(8,128)(2,1)S(1)}, u32[]{:S(2)}, u32[]{:S(2)}) collective-permute-start(bf16[96,384]{1,0:T(8,128)(2,1)S(1)} %get-tuple-element.24), channel_id=1, source_target_pairs={{0,2},{1,3},{2,0},{3,1},{4,6},{5,7},{6,4},{7,5},{8,10},{9,11},{10,... | collective-permute-start | bytes 221192 | tf_op jit(solution)/shard_map/ppermute | solution.py:294
  20.5 0.0 collective-permute-start.2
  20.5 1.7 %collective-permute-start.3 = (bf16[96,384]{1,0:T(8,128)(2,1)S(1)}, bf16[96,384]{1,0:T(8,128)(2,1)S(1)}, u32[]{:S(2)}, u32[]{:S(2)}) collective-permute-start(bf16[96,384]{1,0:T(8,128)(2,1)S(1)} %get-tuple-element.26), channel_id=1, source_target_pairs={{0,4},{1,5},{2,6},{3,7},{4,0},{5,1},{6,2},{7,3},{8,12},{9,13},{10,... | collective-permute-start | bytes 221192 | tf_op jit(solution)/shard_map/ppermute | solution.py:294
  22.2 0.1 collective-permute-start.4
  22.3 0.0 collective-permute-done.refs_1_
  22.3 2.6 %collective-permute-start.5 = (bf16[96,384]{1,0:T(8,128)(2,1)S(1)}, bf16[96,384]{1,0:T(8,128)(2,1)S(1)}, u32[]{:S(2)}, u32[]{:S(2)}) collective-permute-start(bf16[96,384]{1,0:T(8,128)(2,1)S(1)} %get-tuple-element.28), channel_id=1, source_target_pairs={{0,6},{1,7},{2,4},{3,5},{4,2},{5,3},{6,0},{7,1},{8,14},{9,15},{10,... | collective-permute-start | bytes 221192 | tf_op jit(solution)/shard_map/ppermute | solution.py:294
  24.9 7.5 %collective-permute-done.1.refs_2_ = bf16[96,384]{1,0:T(8,128)(2,1)S(1)} collective-permute-done((bf16[96,384]{1,0:T(8,128)(2,1)S(1)}, bf16[96,384]{1,0:T(8,128)(2,1)S(1)}, u32[]{:S(2)}, u32[]{:S(2)}) %collective-permute-start.1) | collective-permute-done | bytes 73760 | tf_op jit(solution)/shard_map/ppermute | solution.py:294
  32.4 0.6 collective-permute-start.6
  33.0 0.2 collective-permute-done.2.refs_3_
  33.2 0.3 collective-permute-start.7
  33.5 0.0 collective-permute-done.3.refs_4_
  33.5 2.3 %collective-permute-start.8 = (bf16[96,384]{1,0:T(8,128)(2,1)S(1)}, bf16[96,384]{1,0:T(8,128)(2,1)S(1)}, u32[]{:S(2)}, u32[]{:S(2)}) collective-permute-start(bf16[96,384]{1,0:T(8,128)(2,1)S(1)} %get-tuple-element.31), channel_id=1, source_target_pairs={{0,9},{1,8},{2,11},{3,10},{4,13},{5,12},{6,15},{7,14},{8,1},{9,0},... | collective-permute-start | bytes 221192 | tf_op jit(solution)/shard_map/ppermute | solution.py:294
  35.7 0.0 collective-permute-done.4.refs_5_
  35.7 3.2 %collective-permute-start.9 = (bf16[96,384]{1,0:T(8,128)(2,1)S(1)}, bf16[96,384]{1,0:T(8,128)(2,1)S(1)}, u32[]{:S(2)}, u32[]{:S(2)}) collective-permute-start(bf16[96,384]{1,0:T(8,128)(2,1)S(1)} %get-tuple-element.32), channel_id=1, source_target_pairs={{0,10},{1,11},{2,8},{3,9},{4,14},{5,15},{6,12},{7,13},{8,2},{9,3},... | collective-permute-start | bytes 221192 | tf_op jit(solution)/shard_map/ppermute | solution.py:294
  39.0 3.9 %collective-permute-done.5.refs_6_ = bf16[96,384]{1,0:T(8,128)(2,1)S(1)} collective-permute-done((bf16[96,384]{1,0:T(8,128)(2,1)S(1)}, bf16[96,384]{1,0:T(8,128)(2,1)S(1)}, u32[]{:S(2)}, u32[]{:S(2)}) %collective-permute-start.5) | collective-permute-done | bytes 73760 | tf_op jit(solution)/shard_map/ppermute | solution.py:294
  42.8 0.8 collective-permute-done.6.refs_7_
  43.6 0.0 collective-permute-start.11
  43.6 10.4 %collective-permute-done.7.refs_8_ = bf16[96,384]{1,0:T(8,128)(2,1)S(1)} collective-permute-done((bf16[96,384]{1,0:T(8,128)(2,1)S(1)}, bf16[96,384]{1,0:T(8,128)(2,1)S(1)}, u32[]{:S(2)}, u32[]{:S(2)}) %collective-permute-start.7) | collective-permute-done | bytes 73760 | tf_op jit(solution)/shard_map/ppermute | solution.py:294
  54.0 2.0 %collective-permute-start.12 = (bf16[96,384]{1,0:T(8,128)(2,1)S(1)}, bf16[96,384]{1,0:T(8,128)(2,1)S(1)}, u32[]{:S(2)}, u32[]{:S(2)}) collective-permute-start(bf16[96,384]{1,0:T(8,128)(2,1)S(1)} %get-tuple-element.35), channel_id=1, source_target_pairs={{0,13},{1,12},{2,15},{3,14},{4,9},{5,8},{6,11},{7,10},{8,5},{9,4},... | collective-permute-start | bytes 221192 | tf_op jit(solution)/shard_map/ppermute | solution.py:294
  56.0 2.8 %collective-permute-start.13 = (bf16[96,384]{1,0:T(8,128)(2,1)S(1)}, bf16[96,384]{1,0:T(8,128)(2,1)S(1)}, u32[]{:S(2)}, u32[]{:S(2)}) collective-permute-start(bf16[96,384]{1,0:T(8,128)(2,1)S(1)} %get-tuple-element.36), channel_id=1, source_target_pairs={{0,14},{1,15},{2,12},{3,13},{4,10},{5,11},{6,8},{7,9},{8,6},{9,7},... | collective-permute-start | bytes 221192 | tf_op jit(solution)/shard_map/ppermute | solution.py:294
  58.8 0.0 collective-permute-done.9.refs_10_
  58.8 1.7 %collective-permute-start.14 = (bf16[96,384]{1,0:T(8,128)(2,1)S(1)}, bf16[96,384]{1,0:T(8,128)(2,1)S(1)}, u32[]{:S(2)}, u32[]{:S(2)}) collective-permute-start(bf16[96,384]{1,0:T(8,128)(2,1)S(1)} %get-tuple-element.37), channel_id=1, source_target_pairs={{0,15},{1,14},{2,13},{3,12},{4,11},{5,10},{6,9},{7,8},{8,7},{9,6},... | collective-permute-start | bytes 221192 | tf_op jit(solution)/shard_map/ppermute | solution.py:294
  60.5 1.4 %collective-permute-done.12.refs_13_ = bf16[96,384]{1,0:T(8,128)(2,1)S(1)} collective-permute-done((bf16[96,384]{1,0:T(8,128)(2,1)S(1)}, bf16[96,384]{1,0:T(8,128)(2,1)S(1)}, u32[]{:S(2)}, u32[]{:S(2)}) %collective-permute-start.12) | collective-permute-done | bytes 73760 | tf_op jit(solution)/shard_map/ppermute | solution.py:294
  61.9 3.0 %collective-permute-done.13.refs_14_ = bf16[96,384]{1,0:T(8,128)(2,1)S(1)} collective-permute-done((bf16[96,384]{1,0:T(8,128)(2,1)S(1)}, bf16[96,384]{1,0:T(8,128)(2,1)S(1)}, u32[]{:S(2)}, u32[]{:S(2)}) %collective-permute-start.13) | collective-permute-done | bytes 73760 | tf_op jit(solution)/shard_map/ppermute | solution.py:294
  64.9 2.7 %collective-permute-done.14.refs_15_ = bf16[96,384]{1,0:T(8,128)(2,1)S(1)} collective-permute-done((bf16[96,384]{1,0:T(8,128)(2,1)S(1)}, bf16[96,384]{1,0:T(8,128)(2,1)S(1)}, u32[]{:S(2)}, u32[]{:S(2)}) %collective-permute-start.14) | collective-permute-done | bytes 73760 | tf_op jit(solution)/shard_map/ppermute | solution.py:294
  67.6 0.6 gather_left.1.left
  68.2 2.4 %products.1 = bf16[16,96,384]{2,1,0:T(8,128)(2,1)S(1)} custom-call(bf16[3072,384]{1,0:T(8,128)(2,1)S(1)} %bitcast.9, bf16[8,192,384]{2,1,0:T(8,128)(2,1)S(1)} %gather_left.1.left), custom_call_target="tpu_custom_call" | custom-call | flops 226492416 | bytes 3538944 | tf_op jit(solution)/shard_map/products/pallas_call | solution.py:341
  70.6 0.0 copy-start.2
  70.6 0.0 copy-start.4
  70.6 0.0 copy-start.10
  70.6 0.0 copy-start.11
  70.6 0.0 copy-start.12
  70.7 21.8 %all_to_all.10.x_ref = bf16[16,96,384]{2,1,0:T(8,128)(2,1)S(1)} all-to-all(bf16[16,96,384]{2,1,0:T(8,128)(2,1)S(1)} %products.1), channel_id=1, replica_groups=mesh['groups'=1,'part'=2,'chan'=8,'quarter'=2] {'chan','quarter'}, dimensions={0} | all-to-all | bytes 2359296 | tf_op jit(solution)/shard_map/all_to_all | solution.py:352
  92.5 3.0 %update.1 = bf16[12,384,128]{2,1,0:T(8,128)(2,1)} custom-call(bf16[16,96,384]{2,1,0:T(8,128)(2,1)S(1)} %all_to_all.10.x_ref, bf16[12,384,128]{2,1,0:T(8,128)(2,1)S(1)} %copy-done.2, f32[1,128]{1,0:T(1,128)S(1)} %bitcast.17, f32[1,128]{1,0:T(1,128)S(1)} %bitcast.18, bf16[128,128]{1,0:T(8,128)(2,1)S(1)} %copy-done.4, f32[1,128]{1,0:T(1,128)S(1)} %bitcast.19), custom_call_target="tpu_custom_call" | custom-call | flops 150994944 | bytes 3538944 | tf_op jit(solution)/shard_map/update/pallas_call | solution.py:354
  (16 shorter events, 0.0 us)
Async XLA Ops:
  5.4 7.4 %copy-start = (bf16[12,384,128]{2,1,0:T(8,128)(2,1)S(1)}, bf16[12,384,128]{2,1,0:T(8,128)(2,1)}, u32[]{:S(2)}) copy-start(bf16[12,384,128]{2,1,0:T(8,128)(2,1)} %pair_ref.3) | copy-start | bytes 3538948
  5.4 7.4 %copy-start.6 = (f32[512]{0:T(512)S(1)}, f32[512]{0:T(512)}, u32[]{:S(2)}) copy-start(f32[512]{0:T(512)} %param.15) | copy-start | bytes 6148
  5.5 7.4 %copy-start.7 = (f32[128]{0:T(128)S(1)}, f32[128]{0:T(128)}, u32[]{:S(2)}) copy-start(f32[128]{0:T(128)} %param.12) | copy-start | bytes 1540
  5.5 7.4 %copy-start.8 = (f32[128]{0:T(128)S(1)}, f32[128]{0:T(128)}, u32[]{:S(2)}) copy-start(f32[128]{0:T(128)} %param.13) | copy-start | bytes 1540
  5.5 7.4 %copy-start.9 = (f32[128]{0:T(128)S(1)}, f32[128]{0:T(128)}, u32[]{:S(2)}) copy-start(f32[128]{0:T(128)} %param.17) | copy-start | bytes 1540
  5.5 62.7 %all-to-all-start = ((bf16[32,96,384]{2,1,0:T(8,128)(2,1)}), bf16[32,96,384]{2,1,0:T(8,128)(2,1)S(1)}, u32[]{:S(2)}, u32[]{:S(2)}) async-start(bf16[32,96,384]{2,1,0:T(8,128)(2,1)} %bitcast.20), calls=%async_computation | async-start | bytes 4718592 | tf_op jit(solution)/shard_map/all_to_all | solution.py:290
  12.9 0.9 copy-start.3
  13.8 0.8 copy-start.5
  17.5 1.0 %copy-start.1 = (bf16[12,384,128]{2,1,0:T(8,128)(2,1)}, bf16[12,384,128]{2,1,0:T(8,128)(2,1)S(1)}, u32[]{:S(2)}) copy-start(bf16[12,384,128]{2,1,0:T(8,128)(2,1)S(1)} %get-tuple-element.38.gate_ref) | copy-start | bytes 3538948
  18.6 3.7 %collective-permute-start = (bf16[96,384]{1,0:T(8,128)(2,1)S(1)}, bf16[96,384]{1,0:T(8,128)(2,1)S(1)}, u32[]{:S(2)}, u32[]{:S(2)}) collective-permute-start(bf16[96,384]{1,0:T(8,128)(2,1)S(1)} %get-tuple-element.23), channel_id=1, source_target_pairs={{0,1},{1,0},{2,3},{3,2},{4,5},{5,4},{6,7},{7,6},{8,9},{9,8},{10,11... | collective-permute-start | bytes 221192 | tf_op jit(solution)/shard_map/ppermute | solution.py:294
  18.8 13.6 %collective-permute-start.1 = (bf16[96,384]{1,0:T(8,128)(2,1)S(1)}, bf16[96,384]{1,0:T(8,128)(2,1)S(1)}, u32[]{:S(2)}, u32[]{:S(2)}) collective-permute-start(bf16[96,384]{1,0:T(8,128)(2,1)S(1)} %get-tuple-element.24), channel_id=1, source_target_pairs={{0,2},{1,3},{2,0},{3,1},{4,6},{5,7},{6,4},{7,5},{8,10},{9,11},{10,... | collective-permute-start | bytes 221192 | tf_op jit(solution)/shard_map/ppermute | solution.py:294
  20.5 12.7 %collective-permute-start.2 = (bf16[96,384]{1,0:T(8,128)(2,1)S(1)}, bf16[96,384]{1,0:T(8,128)(2,1)S(1)}, u32[]{:S(2)}, u32[]{:S(2)}) collective-permute-start(bf16[96,384]{1,0:T(8,128)(2,1)S(1)} %get-tuple-element.25), channel_id=1, source_target_pairs={{0,3},{1,2},{2,1},{3,0},{4,7},{5,6},{6,5},{7,4},{8,11},{9,10},{10,... | collective-permute-start | bytes 221192 | tf_op jit(solution)/shard_map/ppermute | solution.py:294
  20.5 13.0 %collective-permute-start.3 = (bf16[96,384]{1,0:T(8,128)(2,1)S(1)}, bf16[96,384]{1,0:T(8,128)(2,1)S(1)}, u32[]{:S(2)}, u32[]{:S(2)}) collective-permute-start(bf16[96,384]{1,0:T(8,128)(2,1)S(1)} %get-tuple-element.26), channel_id=1, source_target_pairs={{0,4},{1,5},{2,6},{3,7},{4,0},{5,1},{6,2},{7,3},{8,12},{9,13},{10,... | collective-permute-start | bytes 221192 | tf_op jit(solution)/shard_map/ppermute | solution.py:294
  22.2 13.5 %collective-permute-start.4 = (bf16[96,384]{1,0:T(8,128)(2,1)S(1)}, bf16[96,384]{1,0:T(8,128)(2,1)S(1)}, u32[]{:S(2)}, u32[]{:S(2)}) collective-permute-start(bf16[96,384]{1,0:T(8,128)(2,1)S(1)} %get-tuple-element.27), channel_id=1, source_target_pairs={{0,5},{1,4},{2,7},{3,6},{4,1},{5,0},{6,3},{7,2},{8,13},{9,12},{10,... | collective-permute-start | bytes 221192 | tf_op jit(solution)/shard_map/ppermute | solution.py:294
  22.3 20.5 %collective-permute-start.5 = (bf16[96,384]{1,0:T(8,128)(2,1)S(1)}, bf16[96,384]{1,0:T(8,128)(2,1)S(1)}, u32[]{:S(2)}, u32[]{:S(2)}) collective-permute-start(bf16[96,384]{1,0:T(8,128)(2,1)S(1)} %get-tuple-element.28), channel_id=1, source_target_pairs={{0,6},{1,7},{2,4},{3,5},{4,2},{5,3},{6,0},{7,1},{8,14},{9,15},{10,... | collective-permute-start | bytes 221192 | tf_op jit(solution)/shard_map/ppermute | solution.py:294
  32.4 11.3 %collective-permute-start.6 = (bf16[96,384]{1,0:T(8,128)(2,1)S(1)}, bf16[96,384]{1,0:T(8,128)(2,1)S(1)}, u32[]{:S(2)}, u32[]{:S(2)}) collective-permute-start(bf16[96,384]{1,0:T(8,128)(2,1)S(1)} %get-tuple-element.29), channel_id=1, source_target_pairs={{0,7},{1,6},{2,5},{3,4},{4,3},{5,2},{6,1},{7,0},{8,15},{9,14},{10,... | collective-permute-start | bytes 221192 | tf_op jit(solution)/shard_map/ppermute | solution.py:294
  33.2 20.8 %collective-permute-start.7 = (bf16[96,384]{1,0:T(8,128)(2,1)S(1)}, bf16[96,384]{1,0:T(8,128)(2,1)S(1)}, u32[]{:S(2)}, u32[]{:S(2)}) collective-permute-start(bf16[96,384]{1,0:T(8,128)(2,1)S(1)} %get-tuple-element.30), channel_id=1, source_target_pairs={{0,8},{1,9},{2,10},{3,11},{4,12},{5,13},{6,14},{7,15},{8,0},{9,1},... | collective-permute-start | bytes 221192 | tf_op jit(solution)/shard_map/ppermute | solution.py:294
  33.5 22.6 %collective-permute-start.8 = (bf16[96,384]{1,0:T(8,128)(2,1)S(1)}, bf16[96,384]{1,0:T(8,128)(2,1)S(1)}, u32[]{:S(2)}, u32[]{:S(2)}) collective-permute-start(bf16[96,384]{1,0:T(8,128)(2,1)S(1)} %get-tuple-element.31), channel_id=1, source_target_pairs={{0,9},{1,8},{2,11},{3,10},{4,13},{5,12},{6,15},{7,14},{8,1},{9,0},... | collective-permute-start | bytes 221192 | tf_op jit(solution)/shard_map/ppermute | solution.py:294
  35.7 23.1 %collective-permute-start.9 = (bf16[96,384]{1,0:T(8,128)(2,1)S(1)}, bf16[96,384]{1,0:T(8,128)(2,1)S(1)}, u32[]{:S(2)}, u32[]{:S(2)}) collective-permute-start(bf16[96,384]{1,0:T(8,128)(2,1)S(1)} %get-tuple-element.32), channel_id=1, source_target_pairs={{0,10},{1,11},{2,8},{3,9},{4,14},{5,15},{6,12},{7,13},{8,2},{9,3},... | collective-permute-start | bytes 221192 | tf_op jit(solution)/shard_map/ppermute | solution.py:294
  42.8 17.7 %collective-permute-start.10 = (bf16[96,384]{1,0:T(8,128)(2,1)S(1)}, bf16[96,384]{1,0:T(8,128)(2,1)S(1)}, u32[]{:S(2)}, u32[]{:S(2)}) collective-permute-start(bf16[96,384]{1,0:T(8,128)(2,1)S(1)} %get-tuple-element.33), channel_id=1, source_target_pairs={{0,11},{1,10},{2,9},{3,8},{4,15},{5,14},{6,13},{7,12},{8,3},{9,2},... | collective-permute-start | bytes 221192 | tf_op jit(solution)/shard_map/ppermute | solution.py:294
  43.6 16.9 %collective-permute-start.11 = (bf16[96,384]{1,0:T(8,128)(2,1)S(1)}, bf16[96,384]{1,0:T(8,128)(2,1)S(1)}, u32[]{:S(2)}, u32[]{:S(2)}) collective-permute-start(bf16[96,384]{1,0:T(8,128)(2,1)S(1)} %get-tuple-element.34), channel_id=1, source_target_pairs={{0,12},{1,13},{2,14},{3,15},{4,8},{5,9},{6,10},{7,11},{8,4},{9,5},... | collective-permute-start | bytes 221192 | tf_op jit(solution)/shard_map/ppermute | solution.py:294
  54.0 7.9 %collective-permute-start.12 = (bf16[96,384]{1,0:T(8,128)(2,1)S(1)}, bf16[96,384]{1,0:T(8,128)(2,1)S(1)}, u32[]{:S(2)}, u32[]{:S(2)}) collective-permute-start(bf16[96,384]{1,0:T(8,128)(2,1)S(1)} %get-tuple-element.35), channel_id=1, source_target_pairs={{0,13},{1,12},{2,15},{3,14},{4,9},{5,8},{6,11},{7,10},{8,5},{9,4},... | collective-permute-start | bytes 221192 | tf_op jit(solution)/shard_map/ppermute | solution.py:294
  56.0 8.9 %collective-permute-start.13 = (bf16[96,384]{1,0:T(8,128)(2,1)S(1)}, bf16[96,384]{1,0:T(8,128)(2,1)S(1)}, u32[]{:S(2)}, u32[]{:S(2)}) collective-permute-start(bf16[96,384]{1,0:T(8,128)(2,1)S(1)} %get-tuple-element.36), channel_id=1, source_target_pairs={{0,14},{1,15},{2,12},{3,13},{4,10},{5,11},{6,8},{7,9},{8,6},{9,7},... | collective-permute-start | bytes 221192 | tf_op jit(solution)/shard_map/ppermute | solution.py:294
  58.8 8.8 %collective-permute-start.14 = (bf16[96,384]{1,0:T(8,128)(2,1)S(1)}, bf16[96,384]{1,0:T(8,128)(2,1)S(1)}, u32[]{:S(2)}, u32[]{:S(2)}) collective-permute-start(bf16[96,384]{1,0:T(8,128)(2,1)S(1)} %get-tuple-element.37), channel_id=1, source_target_pairs={{0,15},{1,14},{2,13},{3,12},{4,11},{5,10},{6,9},{7,8},{8,7},{9,6},... | collective-permute-start | bytes 221192 | tf_op jit(solution)/shard_map/ppermute | solution.py:294
  70.6 21.8 %copy-start.2 = (bf16[12,384,128]{2,1,0:T(8,128)(2,1)S(1)}, bf16[12,384,128]{2,1,0:T(8,128)(2,1)}, u32[]{:S(2)}) copy-start(bf16[12,384,128]{2,1,0:T(8,128)(2,1)} %copy-done.1) | copy-start | bytes 3538948
  70.6 21.8 %copy-start.4 = (bf16[128,128]{1,0:T(8,128)(2,1)S(1)}, bf16[128,128]{1,0:T(8,128)(2,1)}, u32[]{:S(2)}) copy-start(bf16[128,128]{1,0:T(8,128)(2,1)} %w_ref.5) | copy-start | bytes 98308
  70.6 21.8 %copy-start.10 = (f32[128]{0:T(128)S(1)}, f32[128]{0:T(128)}, u32[]{:S(2)}) copy-start(f32[128]{0:T(128)} %param.18) | copy-start | bytes 1540
  70.6 21.8 %copy-start.11 = (f32[128]{0:T(128)S(1)}, f32[128]{0:T(128)}, u32[]{:S(2)}) copy-start(f32[128]{0:T(128)} %param.19) | copy-start | bytes 1540
  70.6 21.8 %copy-start.12 = (f32[128]{0:T(128)S(1)}, f32[128]{0:T(128)}, u32[]{:S(2)}) copy-start(f32[128]{0:T(128)} %param.21) | copy-start | bytes 1540

commit v9 on v7

--- a/solution.py
+++ b/solution.py
@@ -60,10 +60,8 @@
 
 def factor(normed, wt, bias):
     width = wt.shape[0] // 2
-    lanes = normed.shape[0]
-    gate = dot_nt(wt[:width], normed) + widen(bias[:width], lanes)
-    value = dot_nt(wt[width:], normed) + widen(bias[width:], lanes)
-    return sigmoid(gate) * value
+    both = dot_nt(wt, normed) + widen(bias, normed.shape[0])
+    return sigmoid(both[:width]) * both[width:]
 
 
 def as_rows(values, k):
@@ -73,31 +71,18 @@
     )
 
 
-def right_kernel(pair_ref, gain_ref, shift_ref, w_ref, b_ref, out_ref, pair, made, arrive, leave):
-    rows, k, width = pair.shape
-    starts = range(0, rows, STEP)
-    loads = [
-        pltpu.make_async_copy(pair_ref.at[pl.ds(r, STEP)], pair.at[pl.ds(r, STEP)], arrive.at[n])
-        for n, r in enumerate(starts)
-    ]
-    for load in loads:
-        load.start()
-    wt = w_ref[...].astype(f32).T.astype(bf16)
-    bt = column(b_ref[...])
-    stores = []
-    for n, r in enumerate(starts):
-        loads[n].wait()
-        x = pair[r : r + STEP].astype(f32).reshape(STEP * k, width)
-        normed = normalize(x, gain_ref[...], shift_ref[...])
-        at = pl.ds(r * BLOCK, STEP * BLOCK)
-        made[:, at, :] = as_rows(factor(normed, wt, bt), k).astype(bf16)
-        for p in range(out_ref.shape[0]):
-            stores.append(
-                pltpu.make_async_copy(made.at[:, at, :], out_ref.at[p, :, at, :], leave.at[p, n])
-            )
-            stores[-1].start()
-    for store in stores:
-        store.wait()
+def right_kernel(pair_ref, gain_ref, shift_ref, w_ref, b_ref, out_ref, wt, bt):
+    @pl.when(pl.program_id(0) == 0)
+    def _():
+        wt[...] = w_ref[...].astype(f32).T.astype(bf16)
+        bt[...] = column(b_ref[...])
+
+    k, width = pair_ref.shape[1:]
+    x = pair_ref[...].astype(f32).reshape(STEP * k, width)
+    normed = normalize(x, gain_ref[...], shift_ref[...])
+    out = as_rows(factor(normed, wt[...], bt[...]), k).astype(bf16)
+    for p in range(out_ref.shape[0]):
+        out_ref[p] = out
 
 
 def left_kernel(pair_ref, gain_ref, shift_ref, w_ref, b_ref, gw_ref, gb_ref, *refs):
@@ -230,22 +215,17 @@
     anywhere = pl.BlockSpec(memory_space=pl.ANY)
     right = pl.pallas_call(
         right_kernel,
-        grid=(1,),
+        grid=(steps,),
         in_specs=[
-            anywhere,
+            row_block,
             whole((1, width)),
             whole((1, width)),
             pl.BlockSpec((width, 2 * hidden), lambda s: (0, 1)),
             pl.BlockSpec((1, 2 * hidden), lambda s: (0, 1)),
         ],
-        out_specs=anywhere,
+        out_specs=pl.BlockSpec((parts, hosts, STEP * BLOCK, k), lambda s: (0, 0, s, 0)),
         out_shape=bfloat(parts, hosts, tall, k),
-        scratch_shapes=[
-            pltpu.VMEM((rows, k, width), bf16),
-            pltpu.VMEM((hosts, tall, k), bf16),
-            pltpu.SemaphoreType.DMA((steps,)),
-            pltpu.SemaphoreType.DMA((parts, steps)),
-        ],
+        scratch_shapes=[pltpu.VMEM((2 * hidden, width), bf16), pltpu.VMEM((2 * hidden, LANES), f32)],
         compiler_params=params(60),
         cost_estimate=cost(4 * work * hidden, 6 * work),
         name="right_factor",

time: 94.8 us -> 94.5 us (level)
  transfers between devices with their start and end apart: 16 -> 16, of which waited for: 8 -> 8; matrix products, arithmetic and copies ran while one was open for 0% -> 0% of each run, Pallas kernels for 4% -> 3%
where the time goes in v9:
time: 94.5 us; the launch traced here: 94.1 us
  waiting for transfers between devices  30.1 us (32%)
  starting transfers between devices  26.6 us (28%)
  blocking collectives  21.8 us (23%)
  Pallas kernels  12.8 us (14%)
  local copies, waits for them, and re-layouts  2.72 us (3%)
    ppermute x15, waiting for transfers between devices, send(): return lax.ppermute(values, everywhere, pairs)  30.1 us
    all_to_all x1, blocking collectives, shards(): product = lax.all_to_all(product, in_part, 0, 0, tiled=True)  21.8 us
    ppermute x15, starting transfers between devices, send(): return lax.ppermute(values, everywhere, pairs)  19.2 us
    all_to_all x1, starting transfers between devices, shards(): lax.all_to_all(right.reshape(devices, tall, k), everywhere, 0, 0, tiled=T...  7.3 us
    pallas_call x1, Pallas kernels, shards(): pl.pallas_call(right_kernel, grid=(steps,), in_specs=[row_block, whole((1...  5 us
    pallas_call x1, Pallas kernels, shards(): pl.pallas_call(left_kernel, grid=(steps,), in_specs=[row_block, whole((1,...  2.73 us
    unnamed x26, local copies, waits for them, and re-layouts  2.72 us
    pallas_call x1, Pallas kernels, shards(): pl.pallas_call(product_kernel, grid=(devices // GATHER,), in_specs=[pl.Bl...  2.41 us
  transfers between devices with their start and end apart: 16, of which 8 were waited for; matrix products, arithmetic and copies ran while one was open for 0% of the time, Pallas kernels for 3%

profile of v9, /device:TPU:0, one launch (start us, length us, event | category | flops | bytes accessed | tf_op | source)
XLA Modules:
  0.0 94.1 jit_solution(17690226938332273059)
XLA Ops:
  0.0 5.0 %right_factor.1 = bf16[2,16,96,384]{3,2,1,0:T(8,128)(2,1)} custom-call(bf16[12,384,128]{2,1,0:T(8,128)(2,1)} %pair_ref.3, f32[1,128]{1,0:T(1,128)} %bitcast.12, f32[1,128]{1,0:T(1,128)} %bitcast.14, bf16[128,512]{1,0:T(8,128)(2,1)} %w_ref.4, f32[1,512]{1,0:T(1,128)} %bitcast.10), custom_call_target="tpu_custom_call" | custom-call | flops 301989888 | bytes 3538944 | tf_op jit(solution)/shard_map/right_factor/pallas_call | solution.py:216
  5.0 0.0 copy-start.8
  5.0 0.0 copy-start.9
  5.0 7.3 %all-to-all-start = ((bf16[32,96,384]{2,1,0:T(8,128)(2,1)}), bf16[32,96,384]{2,1,0:T(8,128)(2,1)S(1)}, u32[]{:S(2)}, u32[]{:S(2)}) async-start(bf16[32,96,384]{2,1,0:T(8,128)(2,1)} %bitcast.20), calls=%async_computation | async-start | bytes 4718592 | tf_op jit(solution)/shard_map/all_to_all | solution.py:233
  12.4 0.0 copy-start.3
  12.4 0.9 copy-done.3
  13.3 0.8 copy-done.5
  14.1 2.7 %left_factor.1 = (bf16[96,384]{1,0:T(8,128)(2,1)S(1)}, bf16[96,384]{1,0:T(8,128)(2,1)S(1)}, bf16[96,384]{1,0:T(8,128)(2,1)S(1)}, bf16[96,384]{1,0:T(8,128)(2,1)S...) custom-call(bf16[12,384,128]{2,1,0:T(8,128)(2,1)S(1)} %copy-done, ...), custom_call_target="tpu_custom_call" | custom-call | flops 301989888 | bytes 3538944 | tf_op jit(solution)/shard_map/left_factor/pallas_call | solution.py:239
  16.8 0.0 copy-start.1
  16.8 1.0 %copy-done.1 = bf16[12,384,128]{2,1,0:T(8,128)(2,1)} copy-done((bf16[12,384,128]{2,1,0:T(8,128)(2,1)}, bf16[12,384,128]{2,1,0:T(8,128)(2,1)S(1)}, u32[]{:S(2)}) %copy-start.1) | copy-done | bytes 1179672
  17.8 0.3 collective-permute-start
  18.1 1.7 %collective-permute-start.1 = (bf16[96,384]{1,0:T(8,128)(2,1)S(1)}, bf16[96,384]{1,0:T(8,128)(2,1)S(1)}, u32[]{:S(2)}, u32[]{:S(2)}) collective-permute-start(bf16[96,384]{1,0:T(8,128)(2,1)S(1)} %get-tuple-element.24), channel_id=1, source_target_pairs={{0,2},{1,3},{2,0},{3,1},{4,6},{5,7},{6,4},{7,5},{8,10},{9,11},{10,... | collective-permute-start | bytes 221192 | tf_op jit(solution)/shard_map/ppermute | solution.py:237
  19.8 0.0 collective-permute-start.2
  19.8 1.7 %collective-permute-start.3 = (bf16[96,384]{1,0:T(8,128)(2,1)S(1)}, bf16[96,384]{1,0:T(8,128)(2,1)S(1)}, u32[]{:S(2)}, u32[]{:S(2)}) collective-permute-start(bf16[96,384]{1,0:T(8,128)(2,1)S(1)} %get-tuple-element.26), channel_id=1, source_target_pairs={{0,4},{1,5},{2,6},{3,7},{4,0},{5,1},{6,2},{7,3},{8,12},{9,13},{10,... | collective-permute-start | bytes 221192 | tf_op jit(solution)/shard_map/ppermute | solution.py:237
  21.5 0.1 collective-permute-start.4
  21.6 0.0 collective-permute-done.refs_1_
  21.6 2.6 %collective-permute-start.5 = (bf16[96,384]{1,0:T(8,128)(2,1)S(1)}, bf16[96,384]{1,0:T(8,128)(2,1)S(1)}, u32[]{:S(2)}, u32[]{:S(2)}) collective-permute-start(bf16[96,384]{1,0:T(8,128)(2,1)S(1)} %get-tuple-element.28), channel_id=1, source_target_pairs={{0,6},{1,7},{2,4},{3,5},{4,2},{5,3},{6,0},{7,1},{8,14},{9,15},{10,... | collective-permute-start | bytes 221192 | tf_op jit(solution)/shard_map/ppermute | solution.py:237
  24.1 7.8 %collective-permute-done.1.refs_2_ = bf16[96,384]{1,0:T(8,128)(2,1)S(1)} collective-permute-done((bf16[96,384]{1,0:T(8,128)(2,1)S(1)}, bf16[96,384]{1,0:T(8,128)(2,1)S(1)}, u32[]{:S(2)}, u32[]{:S(2)}) %collective-permute-start.1) | collective-permute-done | bytes 73760 | tf_op jit(solution)/shard_map/ppermute | solution.py:237
  31.9 0.6 collective-permute-start.6
  32.5 0.2 collective-permute-done.2.refs_3_
  32.7 0.3 collective-permute-start.7
  33.0 0.0 collective-permute-done.3.refs_4_
  33.0 2.3 %collective-permute-start.8 = (bf16[96,384]{1,0:T(8,128)(2,1)S(1)}, bf16[96,384]{1,0:T(8,128)(2,1)S(1)}, u32[]{:S(2)}, u32[]{:S(2)}) collective-permute-start(bf16[96,384]{1,0:T(8,128)(2,1)S(1)} %get-tuple-element.31), channel_id=1, source_target_pairs={{0,9},{1,8},{2,11},{3,10},{4,13},{5,12},{6,15},{7,14},{8,1},{9,0},... | collective-permute-start | bytes 221192 | tf_op jit(solution)/shard_map/ppermute | solution.py:237
  35.3 0.0 collective-permute-done.4.refs_5_
  35.3 3.3 %collective-permute-start.9 = (bf16[96,384]{1,0:T(8,128)(2,1)S(1)}, bf16[96,384]{1,0:T(8,128)(2,1)S(1)}, u32[]{:S(2)}, u32[]{:S(2)}) collective-permute-start(bf16[96,384]{1,0:T(8,128)(2,1)S(1)} %get-tuple-element.32), channel_id=1, source_target_pairs={{0,10},{1,11},{2,8},{3,9},{4,14},{5,15},{6,12},{7,13},{8,2},{9,3},... | collective-permute-start | bytes 221192 | tf_op jit(solution)/shard_map/ppermute | solution.py:237
  38.5 3.8 %collective-permute-done.5.refs_6_ = bf16[96,384]{1,0:T(8,128)(2,1)S(1)} collective-permute-done((bf16[96,384]{1,0:T(8,128)(2,1)S(1)}, bf16[96,384]{1,0:T(8,128)(2,1)S(1)}, u32[]{:S(2)}, u32[]{:S(2)}) %collective-permute-start.5) | collective-permute-done | bytes 73760 | tf_op jit(solution)/shard_map/ppermute | solution.py:237
  42.4 0.0 collective-permute-start.10
  42.4 0.8 collective-permute-done.6.refs_7_
  43.2 0.0 collective-permute-start.11
  43.2 10.3 %collective-permute-done.7.refs_8_ = bf16[96,384]{1,0:T(8,128)(2,1)S(1)} collective-permute-done((bf16[96,384]{1,0:T(8,128)(2,1)S(1)}, bf16[96,384]{1,0:T(8,128)(2,1)S(1)}, u32[]{:S(2)}, u32[]{:S(2)}) %collective-permute-start.7) | collective-permute-done | bytes 73760 | tf_op jit(solution)/shard_map/ppermute | solution.py:237
  53.5 2.0 %collective-permute-start.12 = (bf16[96,384]{1,0:T(8,128)(2,1)S(1)}, bf16[96,384]{1,0:T(8,128)(2,1)S(1)}, u32[]{:S(2)}, u32[]{:S(2)}) collective-permute-start(bf16[96,384]{1,0:T(8,128)(2,1)S(1)} %get-tuple-element.35), channel_id=1, source_target_pairs={{0,13},{1,12},{2,15},{3,14},{4,9},{5,8},{6,11},{7,10},{8,5},{9,4},... | collective-permute-start | bytes 221192 | tf_op jit(solution)/shard_map/ppermute | solution.py:237
  55.6 0.0 collective-permute-done.8.refs_9_
  55.6 2.8 %collective-permute-start.13 = (bf16[96,384]{1,0:T(8,128)(2,1)S(1)}, bf16[96,384]{1,0:T(8,128)(2,1)S(1)}, u32[]{:S(2)}, u32[]{:S(2)}) collective-permute-start(bf16[96,384]{1,0:T(8,128)(2,1)S(1)} %get-tuple-element.36), channel_id=1, source_target_pairs={{0,14},{1,15},{2,12},{3,13},{4,10},{5,11},{6,8},{7,9},{8,6},{9,7},... | collective-permute-start | bytes 221192 | tf_op jit(solution)/shard_map/ppermute | solution.py:237
  58.4 1.7 %collective-permute-start.14 = (bf16[96,384]{1,0:T(8,128)(2,1)S(1)}, bf16[96,384]{1,0:T(8,128)(2,1)S(1)}, u32[]{:S(2)}, u32[]{:S(2)}) collective-permute-start(bf16[96,384]{1,0:T(8,128)(2,1)S(1)} %get-tuple-element.37), channel_id=1, source_target_pairs={{0,15},{1,14},{2,13},{3,12},{4,11},{5,10},{6,9},{7,8},{8,7},{9,6},... | collective-permute-start | bytes 221192 | tf_op jit(solution)/shard_map/ppermute | solution.py:237
  60.1 0.0 collective-permute-done.11.refs_12_
  60.1 1.4 %collective-permute-done.12.refs_13_ = bf16[96,384]{1,0:T(8,128)(2,1)S(1)} collective-permute-done((bf16[96,384]{1,0:T(8,128)(2,1)S(1)}, bf16[96,384]{1,0:T(8,128)(2,1)S(1)}, u32[]{:S(2)}, u32[]{:S(2)}) %collective-permute-start.12) | collective-permute-done | bytes 73760 | tf_op jit(solution)/shard_map/ppermute | solution.py:237
  61.4 3.0 %collective-permute-done.13.refs_14_ = bf16[96,384]{1,0:T(8,128)(2,1)S(1)} collective-permute-done((bf16[96,384]{1,0:T(8,128)(2,1)S(1)}, bf16[96,384]{1,0:T(8,128)(2,1)S(1)}, u32[]{:S(2)}, u32[]{:S(2)}) %collective-permute-start.13) | collective-permute-done | bytes 73760 | tf_op jit(solution)/shard_map/ppermute | solution.py:237
  64.4 2.7 %collective-permute-done.14.refs_15_ = bf16[96,384]{1,0:T(8,128)(2,1)S(1)} collective-permute-done((bf16[96,384]{1,0:T(8,128)(2,1)S(1)}, bf16[96,384]{1,0:T(8,128)(2,1)S(1)}, u32[]{:S(2)}, u32[]{:S(2)}) %collective-permute-start.14) | collective-permute-done | bytes 73760 | tf_op jit(solution)/shard_map/ppermute | solution.py:237
  67.2 0.6 gather_left.1.left
  67.7 0.0 all-to-all-done
  67.7 2.4 %products.1 = bf16[16,96,384]{2,1,0:T(8,128)(2,1)S(1)} custom-call(bf16[3072,384]{1,0:T(8,128)(2,1)S(1)} %bitcast.9, bf16[8,192,384]{2,1,0:T(8,128)(2,1)S(1)} %gather_left.1.left), custom_call_target="tpu_custom_call" | custom-call | flops 226492416 | bytes 3538944 | tf_op jit(solution)/shard_map/products/pallas_call | solution.py:284
  70.1 0.0 copy-start.2
  70.2 0.0 copy-start.4
  70.2 0.0 copy-start.10
  70.2 0.0 copy-start.11
  70.2 0.0 copy-start.12
  70.2 21.8 %all_to_all.10.x_ref = bf16[16,96,384]{2,1,0:T(8,128)(2,1)S(1)} all-to-all(bf16[16,96,384]{2,1,0:T(8,128)(2,1)S(1)} %products.1), channel_id=1, replica_groups=mesh['groups'=1,'part'=2,'chan'=8,'quarter'=2] {'chan','quarter'}, dimensions={0} | all-to-all | bytes 2359296 | tf_op jit(solution)/shard_map/all_to_all | solution.py:295
  92.0 2.1 %update.1 = bf16[12,384,128]{2,1,0:T(8,128)(2,1)} custom-call(bf16[16,96,384]{2,1,0:T(8,128)(2,1)S(1)} %all_to_all.10.x_ref, bf16[12,384,128]{2,1,0:T(8,128)(2,1)S(1)} %copy-done.2, f32[1,128]{1,0:T(1,128)S(1)} %bitcast.17, f32[1,128]{1,0:T(1,128)S(1)} %bitcast.18, bf16[128,128]{1,0:T(8,128)(2,1)S(1)} %copy-done.4, f32[1,128]{1,0:T(1,128)S(1)} %bitcast.19), custom_call_target="tpu_custom_call" | custom-call | flops 150994944 | bytes 3538944 | tf_op jit(solution)/shard_map/update/pallas_call | solution.py:297
  (16 shorter events, 0.0 us)
Async XLA Ops:
  5.0 7.4 %copy-start = (bf16[12,384,128]{2,1,0:T(8,128)(2,1)S(1)}, bf16[12,384,128]{2,1,0:T(8,128)(2,1)}, u32[]{:S(2)}) copy-start(bf16[12,384,128]{2,1,0:T(8,128)(2,1)} %pair_ref.3) | copy-start | bytes 3538948
  5.0 7.4 %copy-start.6 = (f32[512]{0:T(512)S(1)}, f32[512]{0:T(512)}, u32[]{:S(2)}) copy-start(f32[512]{0:T(512)} %param.15) | copy-start | bytes 6148
  5.0 7.4 %copy-start.7 = (f32[128]{0:T(128)S(1)}, f32[128]{0:T(128)}, u32[]{:S(2)}) copy-start(f32[128]{0:T(128)} %param.12) | copy-start | bytes 1540
  5.0 7.4 %copy-start.8 = (f32[128]{0:T(128)S(1)}, f32[128]{0:T(128)}, u32[]{:S(2)}) copy-start(f32[128]{0:T(128)} %param.13) | copy-start | bytes 1540
  5.0 7.4 %copy-start.9 = (f32[128]{0:T(128)S(1)}, f32[128]{0:T(128)}, u32[]{:S(2)}) copy-start(f32[128]{0:T(128)} %param.17) | copy-start | bytes 1540
  5.0 62.7 %all-to-all-start = ((bf16[32,96,384]{2,1,0:T(8,128)(2,1)}), bf16[32,96,384]{2,1,0:T(8,128)(2,1)S(1)}, u32[]{:S(2)}, u32[]{:S(2)}) async-start(bf16[32,96,384]{2,1,0:T(8,128)(2,1)} %bitcast.20), calls=%async_computation | async-start | bytes 4718592 | tf_op jit(solution)/shard_map/all_to_all | solution.py:233
  12.4 0.9 copy-start.3
  13.3 0.8 copy-start.5
  16.8 1.0 %copy-start.1 = (bf16[12,384,128]{2,1,0:T(8,128)(2,1)}, bf16[12,384,128]{2,1,0:T(8,128)(2,1)S(1)}, u32[]{:S(2)}) copy-start(bf16[12,384,128]{2,1,0:T(8,128)(2,1)S(1)} %get-tuple-element.38.gate_ref) | copy-start | bytes 3538948
  17.8 3.8 %collective-permute-start = (bf16[96,384]{1,0:T(8,128)(2,1)S(1)}, bf16[96,384]{1,0:T(8,128)(2,1)S(1)}, u32[]{:S(2)}, u32[]{:S(2)}) collective-permute-start(bf16[96,384]{1,0:T(8,128)(2,1)S(1)} %get-tuple-element.23), channel_id=1, source_target_pairs={{0,1},{1,0},{2,3},{3,2},{4,5},{5,4},{6,7},{7,6},{8,9},{9,8},{10,11... | collective-permute-start | bytes 221192 | tf_op jit(solution)/shard_map/ppermute | solution.py:237
  18.1 13.8 %collective-permute-start.1 = (bf16[96,384]{1,0:T(8,128)(2,1)S(1)}, bf16[96,384]{1,0:T(8,128)(2,1)S(1)}, u32[]{:S(2)}, u32[]{:S(2)}) collective-permute-start(bf16[96,384]{1,0:T(8,128)(2,1)S(1)} %get-tuple-element.24), channel_id=1, source_target_pairs={{0,2},{1,3},{2,0},{3,1},{4,6},{5,7},{6,4},{7,5},{8,10},{9,11},{10,... | collective-permute-start | bytes 221192 | tf_op jit(solution)/shard_map/ppermute | solution.py:237
  19.8 13.0 %collective-permute-start.2 = (bf16[96,384]{1,0:T(8,128)(2,1)S(1)}, bf16[96,384]{1,0:T(8,128)(2,1)S(1)}, u32[]{:S(2)}, u32[]{:S(2)}) collective-permute-start(bf16[96,384]{1,0:T(8,128)(2,1)S(1)} %get-tuple-element.25), channel_id=1, source_target_pairs={{0,3},{1,2},{2,1},{3,0},{4,7},{5,6},{6,5},{7,4},{8,11},{9,10},{10,... | collective-permute-start | bytes 221192 | tf_op jit(solution)/shard_map/ppermute | solution.py:237
  19.8 13.2 %collective-permute-start.3 = (bf16[96,384]{1,0:T(8,128)(2,1)S(1)}, bf16[96,384]{1,0:T(8,128)(2,1)S(1)}, u32[]{:S(2)}, u32[]{:S(2)}) collective-permute-start(bf16[96,384]{1,0:T(8,128)(2,1)S(1)} %get-tuple-element.26), channel_id=1, source_target_pairs={{0,4},{1,5},{2,6},{3,7},{4,0},{5,1},{6,2},{7,3},{8,12},{9,13},{10,... | collective-permute-start | bytes 221192 | tf_op jit(solution)/shard_map/ppermute | solution.py:237
  21.5 13.8 %collective-permute-start.4 = (bf16[96,384]{1,0:T(8,128)(2,1)S(1)}, bf16[96,384]{1,0:T(8,128)(2,1)S(1)}, u32[]{:S(2)}, u32[]{:S(2)}) collective-permute-start(bf16[96,384]{1,0:T(8,128)(2,1)S(1)} %get-tuple-element.27), channel_id=1, source_target_pairs={{0,5},{1,4},{2,7},{3,6},{4,1},{5,0},{6,3},{7,2},{8,13},{9,12},{10,... | collective-permute-start | bytes 221192 | tf_op jit(solution)/shard_map/ppermute | solution.py:237
  21.6 20.8 %collective-permute-start.5 = (bf16[96,384]{1,0:T(8,128)(2,1)S(1)}, bf16[96,384]{1,0:T(8,128)(2,1)S(1)}, u32[]{:S(2)}, u32[]{:S(2)}) collective-permute-start(bf16[96,384]{1,0:T(8,128)(2,1)S(1)} %get-tuple-element.28), channel_id=1, source_target_pairs={{0,6},{1,7},{2,4},{3,5},{4,2},{5,3},{6,0},{7,1},{8,14},{9,15},{10,... | collective-permute-start | bytes 221192 | tf_op jit(solution)/shard_map/ppermute | solution.py:237
  31.9 11.3 %collective-permute-start.6 = (bf16[96,384]{1,0:T(8,128)(2,1)S(1)}, bf16[96,384]{1,0:T(8,128)(2,1)S(1)}, u32[]{:S(2)}, u32[]{:S(2)}) collective-permute-start(bf16[96,384]{1,0:T(8,128)(2,1)S(1)} %get-tuple-element.29), channel_id=1, source_target_pairs={{0,7},{1,6},{2,5},{3,4},{4,3},{5,2},{6,1},{7,0},{8,15},{9,14},{10,... | collective-permute-start | bytes 221192 | tf_op jit(solution)/shard_map/ppermute | solution.py:237
  32.7 20.8 %collective-permute-start.7 = (bf16[96,384]{1,0:T(8,128)(2,1)S(1)}, bf16[96,384]{1,0:T(8,128)(2,1)S(1)}, u32[]{:S(2)}, u32[]{:S(2)}) collective-permute-start(bf16[96,384]{1,0:T(8,128)(2,1)S(1)} %get-tuple-element.30), channel_id=1, source_target_pairs={{0,8},{1,9},{2,10},{3,11},{4,12},{5,13},{6,14},{7,15},{8,0},{9,1},... | collective-permute-start | bytes 221192 | tf_op jit(solution)/shard_map/ppermute | solution.py:237
  33.0 22.6 %collective-permute-start.8 = (bf16[96,384]{1,0:T(8,128)(2,1)S(1)}, bf16[96,384]{1,0:T(8,128)(2,1)S(1)}, u32[]{:S(2)}, u32[]{:S(2)}) collective-permute-start(bf16[96,384]{1,0:T(8,128)(2,1)S(1)} %get-tuple-element.31), channel_id=1, source_target_pairs={{0,9},{1,8},{2,11},{3,10},{4,13},{5,12},{6,15},{7,14},{8,1},{9,0},... | collective-permute-start | bytes 221192 | tf_op jit(solution)/shard_map/ppermute | solution.py:237
  35.3 23.1 %collective-permute-start.9 = (bf16[96,384]{1,0:T(8,128)(2,1)S(1)}, bf16[96,384]{1,0:T(8,128)(2,1)S(1)}, u32[]{:S(2)}, u32[]{:S(2)}) collective-permute-start(bf16[96,384]{1,0:T(8,128)(2,1)S(1)} %get-tuple-element.32), channel_id=1, source_target_pairs={{0,10},{1,11},{2,8},{3,9},{4,14},{5,15},{6,12},{7,13},{8,2},{9,3},... | collective-permute-start | bytes 221192 | tf_op jit(solution)/shard_map/ppermute | solution.py:237
  42.4 17.7 %collective-permute-start.10 = (bf16[96,384]{1,0:T(8,128)(2,1)S(1)}, bf16[96,384]{1,0:T(8,128)(2,1)S(1)}, u32[]{:S(2)}, u32[]{:S(2)}) collective-permute-start(bf16[96,384]{1,0:T(8,128)(2,1)S(1)} %get-tuple-element.33), channel_id=1, source_target_pairs={{0,11},{1,10},{2,9},{3,8},{4,15},{5,14},{6,13},{7,12},{8,3},{9,2},... | collective-permute-start | bytes 221192 | tf_op jit(solution)/shard_map/ppermute | solution.py:237
  43.2 16.9 %collective-permute-start.11 = (bf16[96,384]{1,0:T(8,128)(2,1)S(1)}, bf16[96,384]{1,0:T(8,128)(2,1)S(1)}, u32[]{:S(2)}, u32[]{:S(2)}) collective-permute-start(bf16[96,384]{1,0:T(8,128)(2,1)S(1)} %get-tuple-element.34), channel_id=1, source_target_pairs={{0,12},{1,13},{2,14},{3,15},{4,8},{5,9},{6,10},{7,11},{8,4},{9,5},... | collective-permute-start | bytes 221192 | tf_op jit(solution)/shard_map/ppermute | solution.py:237
  53.5 7.9 %collective-permute-start.12 = (bf16[96,384]{1,0:T(8,128)(2,1)S(1)}, bf16[96,384]{1,0:T(8,128)(2,1)S(1)}, u32[]{:S(2)}, u32[]{:S(2)}) collective-permute-start(bf16[96,384]{1,0:T(8,128)(2,1)S(1)} %get-tuple-element.35), channel_id=1, source_target_pairs={{0,13},{1,12},{2,15},{3,14},{4,9},{5,8},{6,11},{7,10},{8,5},{9,4},... | collective-permute-start | bytes 221192 | tf_op jit(solution)/shard_map/ppermute | solution.py:237
  55.6 8.9 %collective-permute-start.13 = (bf16[96,384]{1,0:T(8,128)(2,1)S(1)}, bf16[96,384]{1,0:T(8,128)(2,1)S(1)}, u32[]{:S(2)}, u32[]{:S(2)}) collective-permute-start(bf16[96,384]{1,0:T(8,128)(2,1)S(1)} %get-tuple-element.36), channel_id=1, source_target_pairs={{0,14},{1,15},{2,12},{3,13},{4,10},{5,11},{6,8},{7,9},{8,6},{9,7},... | collective-permute-start | bytes 221192 | tf_op jit(solution)/shard_map/ppermute | solution.py:237
  58.4 8.8 %collective-permute-start.14 = (bf16[96,384]{1,0:T(8,128)(2,1)S(1)}, bf16[96,384]{1,0:T(8,128)(2,1)S(1)}, u32[]{:S(2)}, u32[]{:S(2)}) collective-permute-start(bf16[96,384]{1,0:T(8,128)(2,1)S(1)} %get-tuple-element.37), channel_id=1, source_target_pairs={{0,15},{1,14},{2,13},{3,12},{4,11},{5,10},{6,9},{7,8},{8,7},{9,6},... | collective-permute-start | bytes 221192 | tf_op jit(solution)/shard_map/ppermute | solution.py:237
  70.1 21.9 %copy-start.2 = (bf16[12,384,128]{2,1,0:T(8,128)(2,1)S(1)}, bf16[12,384,128]{2,1,0:T(8,128)(2,1)}, u32[]{:S(2)}) copy-start(bf16[12,384,128]{2,1,0:T(8,128)(2,1)} %copy-done.1) | copy-start | bytes 3538948
  70.2 21.8 %copy-start.4 = (bf16[128,128]{1,0:T(8,128)(2,1)S(1)}, bf16[128,128]{1,0:T(8,128)(2,1)}, u32[]{:S(2)}) copy-start(bf16[128,128]{1,0:T(8,128)(2,1)} %w_ref.5) | copy-start | bytes 98308
  70.2 21.8 %copy-start.10 = (f32[128]{0:T(128)S(1)}, f32[128]{0:T(128)}, u32[]{:S(2)}) copy-start(f32[128]{0:T(128)} %param.18) | copy-start | bytes 1540
  70.2 21.8 %copy-start.11 = (f32[128]{0:T(128)S(1)}, f32[128]{0:T(128)}, u32[]{:S(2)}) copy-start(f32[128]{0:T(128)} %param.19) | copy-start | bytes 1540
  70.2 21.8 %copy-start.12 = (f32[128]{0:T(128)S(1)}, f32[128]{0:T(128)}, u32[]{:S(2)}) copy-start(f32[128]{0:T(128)} %param.21) | copy-start | bytes 1540

commit v10 on v3

v10 whole, which is shorter than its diff:
```python
import functools

import jax
import jax.numpy as jnp
from jax import lax
from jax.experimental import pallas as pl
from jax.experimental.pallas import tpu as pltpu
from jax.sharding import Mesh
from jax.sharding import PartitionSpec as P

epsilon = 1e-05
CHANNELS = 128
BLOCK = 8
STEP = 4
SIZE = 32
LANES = 128
PAIRED = 2
EARLY = 8
GATHER = 32
MIB = 1024 * 1024

f32, bf16 = jnp.float32, jnp.bfloat16


def sigmoid(x):
    return 0.5 * jnp.tanh(0.5 * x) + 0.5


def dot(a, b):
    return jnp.dot(a, b, preferred_element_type=f32)


def dot_nt(a, b):
    return lax.dot_general(a, b, (((1,), (1,)), ((), ())), preferred_element_type=f32)


def column(row):
    blocks = [
        jnp.broadcast_to(row[:, k : k + LANES], (LANES, LANES)).T
        for k in range(0, row.shape[1], LANES)
    ]
    return jnp.concatenate(blocks, axis=0)


def widen(col, width):
    return jnp.concatenate([col] * (width // LANES), axis=1)


def shuffle(groups, size):
    n = groups * size
    out = lax.broadcasted_iota(jnp.int32, (n, n), 0)
    row = lax.broadcasted_iota(jnp.int32, (n, n), 1)
    want = (out % size) * groups + out // size
    return jnp.where(want == row, 1.0, 0.0).astype(bf16)


def normalize(x, gain, shift):
    centered = x - jnp.mean(x, axis=1, keepdims=True)
    variance = jnp.mean(centered * centered, axis=1, keepdims=True)
    return (centered * lax.rsqrt(variance + epsilon) * gain + shift).astype(bf16)


def factor(normed, wt, bias):
    width = wt.shape[0] // 2
    both = dot_nt(wt, normed) + widen(bias, normed.shape[0])
    return sigmoid(both[:width]) * both[width:]


def as_rows(values, k):
    hosts = values.shape[0] // BLOCK
    return jnp.concatenate(
        [values[:, r * k : (r + 1) * k].reshape(hosts, BLOCK, k) for r in range(STEP)], axis=1
    )


def early_kernel(pair_ref, gain_ref, shift_ref, w_ref, b_ref, out_ref, wt, bt):
    @pl.when(pl.program_id(0) == 0)
    def _():
        wt[...] = w_ref[...].astype(f32).T.astype(bf16)
        bt[...] = column(b_ref[...])

    k, width = pair_ref.shape[1:]
    x = pair_ref[...].astype(f32).reshape(STEP * k, width)
    normed = normalize(x, gain_ref[...], shift_ref[...])
    out = as_rows(factor(normed, wt[...], bt[...]), k).astype(bf16)
    for p in range(out_ref.shape[0]):
        out_ref[p] = out


def left_kernel(own_ref, other_ref, gain_ref, shift_ref, w_ref, b_ref, *refs):
    wf, bf, wt, bt = refs[-4:]
    outs = refs[:-4]
    k, width = own_ref.shape[1:]
    hidden = w_ref.shape[1] // 2
    near = len(outs) * BLOCK
    step = pl.program_id(0)

    @pl.when(step == 0)
    def _():
        wf[...] = w_ref[...].astype(f32).T
        bf[...] = column(b_ref[...])
        host = lax.axis_index(("chan", "quarter"))
        for half in range(2):
            for m in range(0, len(outs), 2):
                source = [
                    pl.ds(
                        pl.multiple_of(half * hidden + (host ^ (2 * (m + n))) * BLOCK, BLOCK), BLOCK
                    )
                    for n in range(2)
                ]
                target = slice(half * near + m * BLOCK, half * near + (m + 2) * BLOCK)
                wt[target] = jnp.concatenate([wf[s] for s in source], axis=0).astype(bf16)
                bt[target] = jnp.concatenate([bf[s] for s in source], axis=0)

    pair = jnp.where(step < pl.num_programs(0) // 2, own_ref[...], other_ref[...])
    normed = normalize(pair.astype(f32).reshape(STEP * k, width), gain_ref[...], shift_ref[...])
    rows = as_rows(factor(normed, wt[...], bt[...]), k).astype(bf16)
    for m, out in enumerate(outs):
        out[...] = rows[m]


def late_kernel(pair_ref, gain_ref, shift_ref, w_ref, b_ref, *refs):
    out_ref = refs[-1]
    k, width = pair_ref.shape[1:]
    x = pair_ref[...].astype(f32).reshape(STEP * k, width)
    normed = normalize(x, gain_ref[...], shift_ref[...])
    wt = w_ref[...].astype(f32).T.astype(bf16)
    out = as_rows(factor(normed, wt, column(b_ref[...])), k).astype(bf16)
    for p in range(out_ref.shape[0]):
        out_ref[p] = out


def gate_kernel(pair_ref, gain_ref, shift_ref, gw_ref, gb_ref, gate_ref):
    k, width = pair_ref.shape[1:]
    x = pair_ref[...].astype(f32).reshape(STEP * k, width)
    normed = normalize(x, gain_ref[...], shift_ref[...])
    gate = sigmoid(dot(normed, gw_ref[...]) + gb_ref[...])
    gate_ref[...] = gate.reshape(gate_ref.shape).astype(gate_ref.dtype)


def regroup(pieces, target, matrix):
    many = SIZE // STEP
    for s in range(len(pieces) // many):
        rows = jnp.concatenate([piece() for piece in pieces[s * many : (s + 1) * many]], axis=0)
        moved = dot(matrix, rows).astype(bf16)
        for c in range(BLOCK):
            target[c, s * SIZE : (s + 1) * SIZE, :] = moved[c * SIZE : (c + 1) * SIZE]


def slices(refs):
    tall = STEP * BLOCK
    return [
        functools.partial(lambda ref, at: ref[at : at + tall, :], ref, at)
        for ref in refs
        for at in range(0, ref.shape[0], tall)
    ]


def multiply(left, right_ref, right, held, store):
    regroup(slices([right_ref]), right, shuffle(BLOCK, SIZE))
    back = shuffle(SIZE, BLOCK)
    for c in range(BLOCK):
        held[c] = dot_nt(left[c], right[c]).astype(bf16)
    for s in range(left.shape[1] // SIZE):
        parts = jnp.concatenate([held[c, s * SIZE : (s + 1) * SIZE, :] for c in range(BLOCK)], axis=0)
        moved = dot(back, parts).astype(bf16)
        for i in range(0, SIZE, STEP):
            store(s * SIZE + i, moved[i * BLOCK : (i + STEP) * BLOCK])


def first_kernel(hosts, right_ref, *refs):
    chips = hosts // 2
    lefts, outs = refs[:chips], refs[chips + 1 : chips + 1 + hosts]
    left_ref, arrived, left, right, held, sems, sem = refs[chips + 1 + hosts :]
    loads = [
        pltpu.make_async_copy(ref, arrived.at[m], sems.at[m]) for m, ref in enumerate(lefts)
    ]
    keep = pltpu.make_async_copy(left, left_ref, sem)
    step = pl.program_id(0)

    @pl.when(step == 0)
    def _():
        for load in loads:
            load.start()
        for load in loads:
            load.wait()
        regroup(slices([arrived.at[m] for m in range(chips)]), left, shuffle(BLOCK, SIZE))
        keep.start()

    rows = left.shape[1] // hosts

    def store(i, values):
        to, at = divmod(i, rows)
        outs[to][at * BLOCK : (at + STEP) * BLOCK, :] = values

    multiply(left, right_ref, right, held, store)

    @pl.when(step == 0)
    def _():
        keep.wait()


def second_kernel(right_ref, left_ref, *refs):
    out_ref, left, right, held, sem = refs[-5:]
    load = pltpu.make_async_copy(left_ref, left, sem)

    @pl.when(pl.program_id(0) == 0)
    def _():
        load.start()
        load.wait()

    rows = left.shape[1] // out_ref.shape[0]
    host = lax.axis_index(("chan", "quarter"))

    def store(i, values):
        to, at = divmod(i, rows)
        out_ref[host ^ to, at * BLOCK : (at + STEP) * BLOCK, :] = values

    multiply(left, right_ref, right, held, store)


def collect_kernel(*refs):
    out_ref, sems = refs[-2:]
    host = lax.axis_index(("chan", "quarter"))
    copies = [
        pltpu.make_async_copy(ref, out_ref.at[host ^ b], sems.at[b])
        for b, ref in enumerate(refs[:-2])
    ]
    for copy in copies:
        copy.start()
    for copy in copies:
        copy.wait()


def final_kernel(
    first_ref, second_ref, gate_ref, g_ref, s_ref, w_ref, b_ref, out_ref, gate, weight, made,
    arrive, leave, sem,
):
    hosts, _, lanes = first_ref.shape
    count, j, width = gate.shape
    gathers = lanes // (GATHER * EARLY)
    early = GATHER * EARLY
    span = j // gathers
    late = span - early

    def load(n):
        at = pl.ds(n * PAIRED, PAIRED)
        return pltpu.make_async_copy(gate_ref.at[at], gate.at[at], arrive.at[n])

    def store(n):
        at = pl.ds(n * PAIRED, PAIRED)
        return pltpu.make_async_copy(made.at[at], out_ref.at[at], leave.at[n])

    turns = count // PAIRED
    fetch = pltpu.make_async_copy(w_ref, weight, sem)
    fetch.start()
    for n in range(turns):
        load(n).start()
    gain, shift = widen(column(g_ref[...]), span), widen(column(s_ref[...]), span)
    each = span // GATHER
    out = lax.broadcasted_iota(jnp.int32, (span, span), 0)
    lane = lax.broadcasted_iota(jnp.int32, (span, span), 1)
    device, at = out // each, out % each
    want = jnp.where(at < EARLY, device * EARLY + at, early + device * (each - EARLY) + at - EARLY)
    order = jnp.where(want == lane, 1.0, 0.0).astype(bf16)
    fetch.wait()
    for n in range(turns):
        load(n).wait()
        rows = slice(n * PAIRED * BLOCK, (n + 1) * PAIRED * BLOCK)
        for g in range(gathers):
            x = jnp.concatenate(
                [
                    first_ref[:, rows, g * early : (g + 1) * early].astype(f32),
                    second_ref[:, rows, g * late : (g + 1) * late].astype(f32),
                ],
                axis=2,
            )
            for m in range(PAIRED):
                one = x[:, m * BLOCK : (m + 1) * BLOCK].reshape(hosts * BLOCK, span)
                centered = one - jnp.mean(one, axis=0, keepdims=True)
                variance = jnp.mean(centered * centered, axis=0, keepdims=True)
                normed = centered * lax.rsqrt(variance + epsilon) * gain + shift
                turned = dot_nt(order, normed.astype(bf16)).astype(bf16)
                outward = dot(turned, weight[...]) + b_ref[...]
                at = slice(g * span, (g + 1) * span)
                row = n * PAIRED + m
                made[row, at, :] = (gate[row, at, :].astype(f32) * outward).astype(bf16)
        store(n).start()
    for n in range(turns):
        store(n).wait()


def whole(shape):
    return pl.BlockSpec(shape, lambda s: (0,) * len(shape))


def cost(flops, size):
    return pl.CostEstimate(flops=flops, bytes_accessed=size, transcendentals=0)


def params(mib=32):
    return pltpu.CompilerParams(vmem_limit_bytes=mib * MIB)


def in_hbm(x):
    return pltpu.with_memory_space_constraint(x, pltpu.HBM)


def shards(parts, pair, norm_gain, norm_shift, factor_weight, factor_bias, gate_weight, gate_bias,
           center_gain, center_shift, out_weight, out_bias):
    rows, k, width = pair.shape
    hidden = out_weight.shape[0]
    hosts = hidden // BLOCK
    steps = rows // STEP
    late = rows - EARLY
    tall = rows * BLOCK
    mine = hosts * rows
    devices = parts * hosts
    gathers = devices // GATHER
    in_part = ("chan", "quarter")
    everywhere = ("part",) + in_part
    row = lambda v: v.reshape(1, -1)
    row_block = pl.BlockSpec((STEP, k, width), lambda s: (s, 0, 0))
    work = rows * k * width
    bfloat = lambda *shape: jax.ShapeDtypeStruct(shape, bf16)

    early_right = pl.pallas_call(
        early_kernel,
        grid=(EARLY // STEP,),
        in_specs=[
            row_block,
            whole((1, width)),
            whole((1, width)),
            pl.BlockSpec((width, 2 * hidden), lambda s: (0, 1)),
            pl.BlockSpec((1, 2 * hidden), lambda s: (0, 1)),
        ],
        out_specs=pl.BlockSpec((parts, hosts, STEP * BLOCK, k), lambda s: (0, 0, s, 0)),
        out_shape=bfloat(parts, hosts, EARLY * BLOCK, k),
        scratch_shapes=[pltpu.VMEM((2 * hidden, width), bf16), pltpu.VMEM((2 * hidden, LANES), f32)],
        compiler_params=params(60),
        cost_estimate=cost(4 * work * hidden, 6 * work),
        name="early_right",
    )(pair, row(norm_gain), row(norm_shift), factor_weight, row(factor_bias))
    early_right = lax.all_to_all(
        early_right.reshape(devices, EARLY * BLOCK, k), everywhere, 0, 0, tiled=True
    )

    other = lax.ppermute(pair, "quarter", [(0, 1), (1, 0)])
    chips = hosts // 2
    *lefts, = pl.pallas_call(
        left_kernel,
        grid=(2 * steps,),
        in_specs=[
            pl.BlockSpec((STEP, k, width), lambda s: (jnp.minimum(s, steps - 1), 0, 0)),
            pl.BlockSpec((STEP, k, width), lambda s: (jnp.maximum(s - steps, 0), 0, 0)),
            whole((1, width)),
            whole((1, width)),
            whole((width, 2 * hidden)),
            whole((1, 2 * hidden)),
        ],
        out_specs=[pl.BlockSpec((STEP * BLOCK, k), lambda s: (s, 0))] * chips,
        out_shape=[bfloat(2 * tall, k)] * chips,
        scratch_shapes=[
            pltpu.VMEM((2 * hidden, width), f32),
            pltpu.VMEM((2 * hidden, LANES), f32),
            pltpu.VMEM((hidden, width), bf16),
            pltpu.VMEM((hidden, LANES), f32),
        ],
        compiler_params=params(),
        cost_estimate=cost(4 * work * hidden, 6 * work),
        name="left_factor",
    )(pair, other, row(norm_gain), row(norm_shift), factor_weight, row(factor_bias))

    def send(values, b):
        pairs = [(p * hosts + h, p * hosts + (h ^ b)) for p in range(parts) for h in range(hosts)]
        return lax.ppermute(values, everywhere, pairs)

    lefts = [lefts[0]] + [send(lefts[m], 2 * m) for m in range(1, chips)]

    lefts = [in_hbm(x) for x in lefts]
    soon = lefts[1 : chips // 2]
    late_right = pl.pallas_call(
        late_kernel,
        grid=(late // STEP,),
        in_specs=[
            pl.BlockSpec((STEP, k, width), lambda s: (s + EARLY // STEP, 0, 0)),
            whole((1, width)),
            whole((1, width)),
            pl.BlockSpec((width, 2 * hidden), lambda s: (0, 1)),
            pl.BlockSpec((1, 2 * hidden), lambda s: (0, 1)),
        ]
        + [pl.BlockSpec(memory_space=pl.ANY)] * len(soon),
        out_specs=pl.BlockSpec((parts, hosts, STEP * BLOCK, k), lambda s: (0, 0, s, 0)),
        out_shape=pltpu.HBM((parts, hosts, late * BLOCK, k), bf16),
        compiler_params=params(),
        cost_estimate=cost(2 * work * hidden, 2 * work),
        name="late_right",
    )(pair, row(norm_gain), row(norm_shift), factor_weight, row(factor_bias), *soon)
    late_right = lax.all_to_all(
        late_right.reshape(devices, late * BLOCK, k), everywhere, 0, 0, tiled=True
    )

    gate = pl.pallas_call(
        gate_kernel,
        grid=(steps,),
        in_specs=[
            row_block,
            whole((1, width)),
            whole((1, width)),
            whole((width, width)),
            whole((1, width)),
        ],
        out_specs=row_block,
        out_shape=pltpu.HBM(pair.shape, bf16),
        compiler_params=params(),
        cost_estimate=cost(1 << 37, 4 * work),
        name="gate",
    )(pair, row(norm_gain), row(norm_shift), gate_weight, row(gate_bias))

    first = GATHER * EARLY
    second = GATHER * late
    spent = cost(2 * BLOCK * mine * mine * k, 6 * BLOCK * mine * k)
    vmem = pl.BlockSpec(memory_space=pltpu.VMEM)
    anywhere = pl.BlockSpec(memory_space=pl.ANY)
    grouped = (BLOCK, mine, k)
    *firsts, left = pl.pallas_call(
        functools.partial(first_kernel, hosts),
        grid=(gathers,),
        in_specs=[pl.BlockSpec((first * BLOCK, k), lambda s: (s, 0))] + [anywhere] * (chips + 1),
        out_specs=[pl.BlockSpec((tall, first), lambda s: (0, s))] * hosts + [anywhere],
        out_shape=[bfloat(tall, gathers * first)] * hosts + [pltpu.HBM(grouped, bf16)],
        scratch_shapes=[
            pltpu.VMEM((chips, 2 * tall, k), bf16),
            pltpu.VMEM(grouped, bf16),
            pltpu.VMEM((BLOCK, first, k), bf16),
            pltpu.VMEM((BLOCK, mine, first), bf16),
            pltpu.SemaphoreType.DMA((chips,)),
            pltpu.SemaphoreType.DMA,
        ],
        compiler_params=params(40),
        cost_estimate=spent,
        name="first_products",
    )(early_right.reshape(devices * EARLY * BLOCK, k), *lefts, in_hbm(gate))
    firsts = [firsts[0]] + [send(firsts[b], b) for b in range(1, hosts)]
    firsts = [in_hbm(x) for x in firsts]

    forced = firsts[hosts // 2 :]
    seconds = pl.pallas_call(
        second_kernel,
        grid=(gathers,),
        in_specs=[pl.BlockSpec((second * BLOCK, k), lambda s: (s, 0))]
        + [anywhere] * (1 + len(forced)),
        out_specs=pl.BlockSpec((hosts, tall, second), lambda s: (0, 0, s)),
        out_shape=pltpu.HBM((hosts, tall, gathers * second), bf16),
        scratch_shapes=[
            pltpu.VMEM(grouped, bf16),
            pltpu.VMEM((BLOCK, second, k), bf16),
            pltpu.VMEM((BLOCK, mine, second), bf16),
            pltpu.SemaphoreType.DMA,
        ],
        compiler_params=params(),
        cost_estimate=spent,
        name="second_products",
    )(late_right.reshape(devices * late * BLOCK, k), in_hbm(left), *forced)
    seconds = lax.all_to_all(seconds, in_part, 0, 0, tiled=True)

    firsts = pl.pallas_call(
        collect_kernel,
        in_specs=[anywhere] * hosts,
        out_specs=vmem,
        out_shape=bfloat(hosts, tall, gathers * first),
        scratch_shapes=[pltpu.SemaphoreType.DMA((hosts,))],
        compiler_params=params(),
        cost_estimate=cost(0, 4 * work),
        name="collect",
    )(*firsts)

    turns = rows // PAIRED
    return pl.pallas_call(
        final_kernel,
        in_specs=[vmem] * 2 + [anywhere] + [vmem] * 2 + [anywhere, vmem],
        out_specs=anywhere,
        out_shape=bfloat(*pair.shape),
        scratch_shapes=[
            pltpu.VMEM(pair.shape, bf16),
            pltpu.VMEM(out_weight.shape, bf16),
            pltpu.VMEM(pair.shape, bf16),
            pltpu.SemaphoreType.DMA((turns,)),
            pltpu.SemaphoreType.DMA((turns,)),
            pltpu.SemaphoreType.DMA,
        ],
        compiler_params=params(40),
        cost_estimate=cost(2 * work * width, 6 * work),
        name="update",
    )(
        firsts,
        seconds,
        in_hbm(gate),
        row(center_gain),
        row(center_shift),
        in_hbm(out_weight),
        row(out_bias),
    )


def solution(mesh):
    groups, chan, quarter = (mesh.shape[a] for a in ("groups", "chan", "quarter"))
    near = CHANNELS // BLOCK // quarter
    parts = chan // near
    split = Mesh(
        mesh.devices.reshape(groups, parts, near, quarter), ("groups", "part", "chan", "quarter")
    )
    rows = P(("groups", "part", "chan", "quarter"), None, None)
    return jax.shard_map(
        functools.partial(shards, parts),
        mesh=split,
        in_specs=(rows,) + (P(),) * 10,
        out_specs=rows,
        check_vma=False,
    )
```

time: 120 us -> 109 us (0.908)
  local copies, waits for them, and re-layouts: 17.3 us -> 4.56 us
  starting transfers between devices: 55 us -> 50.1 us
  Pallas kernels: 23.5 us -> 27.5 us
  waiting for transfers between devices: 22.9 us -> 25.9 us
    unnamed x136 -> x60, local copies, waits for them, and re-layouts: 17.3 us -> 4.56 us
    all_to_all x1, waiting for transfers between devices: 0.01 us -> 9.46 us  [shards(): lax.all_to_all(early_right.reshape(devices, EARLY * BLOCK, k), everywhere...]
    ppermute x30 -> x22, waiting for transfers between devices: 22.9 us -> 13.8 us  [send(): return lax.ppermute(values, everywhere, pairs)]
    ppermute x30 -> x22, starting transfers between devices: 41 us -> 35 us  [send(): return lax.ppermute(values, everywhere, pairs)]
    ppermute x0 -> x1, waiting for transfers between devices: none -> 2.6 us  [shards(): other = lax.ppermute(pair, 'quarter', [(0, 1), (1, 0)])]
    pallas_call x4, Pallas kernels: 12.8 us -> 15.3 us  [the longest x1 5.81 us: shards(): pl.pallas_call(final_kernel, in_specs=[vmem] * 2 + [anywhere] + [vmem] *...]
    pallas_call x1, Pallas kernels: 1.95 us -> 3.2 us  [shards(): pl.pallas_call(second_kernel, grid=(gathers,), in_specs=[pl.BlockSpec((se...]
  transfers between devices with their start and end apart: 33 -> 26, of which waited for: 15 -> 10; matrix products, arithmetic and copies ran while one was open for 0% -> 0% of each run, Pallas kernels for 11% -> 14%
where the time goes in v10:
time: 109 us; the launch traced here: 108 us
  starting transfers between devices  50.1 us (46%)
  Pallas kernels  27.5 us (25%)
  waiting for transfers between devices  25.9 us (24%)
  local copies, waits for them, and re-layouts  4.56 us (4%)
    ppermute x22, starting transfers between devices, send(): return lax.ppermute(values, everywhere, pairs)  35 us
    ppermute x22, waiting for transfers between devices, send(): return lax.ppermute(values, everywhere, pairs)  13.8 us
    all_to_all x1, waiting for transfers between devices, shards(): lax.all_to_all(early_right.reshape(devices, EARLY * BLOCK, k), everywhere...  9.46 us
    all_to_all x1, starting transfers between devices, shards(): lax.all_to_all(early_right.reshape(devices, EARLY * BLOCK, k), everywhere...  7.31 us
    pallas_call x1, Pallas kernels, shards(): pl.pallas_call(final_kernel, in_specs=[vmem] * 2 + [anywhere] + [vmem] *...  5.81 us
    pallas_call x1, Pallas kernels, shards(): pl.pallas_call(left_kernel, grid=(2 * steps,), in_specs=[pl.BlockSpec((ST...  5.32 us
    unnamed x60, local copies, waits for them, and re-layouts  4.56 us
    all_to_all x1, starting transfers between devices, shards(): seconds = lax.all_to_all(seconds, in_part, 0, 0, tiled=True)  3.88 us
  transfers between devices with their start and end apart: 26, of which 10 were waited for; matrix products, arithmetic and copies ran while one was open for 0% of the time, Pallas kernels for 14%

profile of v10, /device:TPU:0, one launch (start us, length us, event | category | flops | bytes accessed | tf_op | source)
XLA Modules:
  0.0 108.5 jit_solution(16293616604481119480)
XLA Ops:
  0.0 3.7 %early_right.1 = bf16[2,16,64,384]{3,2,1,0:T(8,128)(2,1)} custom-call(bf16[12,384,128]{2,1,0:T(8,128)(2,1)} %pair_ref.5, f32[1,128]{1,0:T(1,128)} %bitcast.16, f32[1,128]{1,0:T(1,128)} %bitcast.20, bf16[128,512]{1,0:T(8,128)(2,1)} %w_ref.6, f32[1,512]{1,0:T(1,128)} %bitcast.13), custom_call_target="tpu_custom_call" | custom-call | flops 301989888 | bytes 3538944 | tf_op jit(solution)/shard_map/early_right/pallas_call | solution.py:327
  3.8 7.3 %all-to-all-start = ((bf16[32,64,384]{2,1,0:T(8,128)(2,1)}), bf16[32,64,384]{2,1,0:T(8,128)(2,1)S(1)}, u32[]{:S(2)}, u32[]{:S(2)}) async-start(bf16[32,64,384]{2,1,0:T(8,128)(2,1)} %bitcast.28), calls=%async_computation | async-start | bytes 3145728 | tf_op jit(solution)/shard_map/all_to_all | solution.py:344
  11.1 0.3 collective-permute-start
  11.4 2.6 %collective-permute-done.other_ref = bf16[12,384,128]{2,1,0:T(8,128)(2,1)S(1)} collective-permute-done((bf16[12,384,128]{2,1,0:T(8,128)(2,1)S(1)}, bf16[12,384,128]{2,1,0:T(8,128)(2,1)S(1)}, u32[]{:S(2)}, u32[]{:S(2)}) %collective-permute-start) | collective-permute-done | bytes 1179680 | tf_op jit(solution)/shard_map/ppermute | solution.py:348
  14.0 5.3 %left_factor.1 = (bf16[192,384]{1,0:T(8,128)(2,1)S(1)}, bf16[192,384]{1,0:T(8,128)(2,1)S(1)}, bf16[192,384]{1,0:T(8,128)(2,1)S(1)}, bf16[192,384]{1,0:T(8,128)(2...) custom-call(bf16[12,384,128]{2,1,0:T(8,128)(2,1)S(1)} %copy-done, ...), custom_call_target="tpu_custom_call" | custom-call | flops 301989888 | bytes 3538944 | tf_op jit(solution)/shard_map/left_factor/pallas_call | solution.py:350
  19.3 0.6 copy-done.2
  20.0 1.8 %collective-permute-start.1 = (bf16[192,384]{1,0:T(8,128)(2,1)S(1)}, bf16[192,384]{1,0:T(8,128)(2,1)S(1)}, u32[]{:S(2)}, u32[]{:S(2)}) collective-permute-start(bf16[192,384]{1,0:T(8,128)(2,1)S(1)} %get-tuple-element.31), channel_id=1, source_target_pairs={{0,2},{1,3},{2,0},{3,1},{4,6},{5,7},{6,4},{7,5},{8,10},{9,11},{10,... | collective-permute-start | bytes 442376 | tf_op jit(solution)/shard_map/ppermute | solution.py:376
  21.8 1.5 %collective-permute-start.2 = (bf16[192,384]{1,0:T(8,128)(2,1)S(1)}, bf16[192,384]{1,0:T(8,128)(2,1)S(1)}, u32[]{:S(2)}, u32[]{:S(2)}) collective-permute-start(bf16[192,384]{1,0:T(8,128)(2,1)S(1)} %get-tuple-element.32), channel_id=1, source_target_pairs={{0,4},{1,5},{2,6},{3,7},{4,0},{5,1},{6,2},{7,3},{8,12},{9,13},{10,... | collective-permute-start | bytes 442376 | tf_op jit(solution)/shard_map/ppermute | solution.py:376
  23.2 0.3 collective-permute-start.3
  23.5 1.8 %collective-permute-start.4 = (bf16[192,384]{1,0:T(8,128)(2,1)}, bf16[192,384]{1,0:T(8,128)(2,1)}, u32[]{:S(2)}, u32[]{:S(2)}) collective-permute-start(bf16[192,384]{1,0:T(8,128)(2,1)} %get-tuple-element.34), channel_id=1, source_target_pairs={{0,8},{1,9},{2,10},{3,11},{4,12},{5,13},{6,14},{7,15},{8,0},{9,1},... | collective-permute-start | bytes 442376 | tf_op jit(solution)/shard_map/ppermute | solution.py:376
  25.2 1.5 %collective-permute-start.5 = (bf16[192,384]{1,0:T(8,128)(2,1)}, bf16[192,384]{1,0:T(8,128)(2,1)}, u32[]{:S(2)}, u32[]{:S(2)}) collective-permute-start(bf16[192,384]{1,0:T(8,128)(2,1)} %get-tuple-element.35), channel_id=1, source_target_pairs={{0,10},{1,11},{2,8},{3,9},{4,14},{5,15},{6,12},{7,13},{8,2},{9,3},... | collective-permute-start | bytes 442376 | tf_op jit(solution)/shard_map/ppermute | solution.py:376
  26.7 1.6 %collective-permute-done.1.refs_1_.refs_0_ = bf16[192,384]{1,0:T(8,128)(2,1)S(1)} collective-permute-done((bf16[192,384]{1,0:T(8,128)(2,1)S(1)}, bf16[192,384]{1,0:T(8,128)(2,1)S(1)}, u32[]{:S(2)}, u32[]{:S(2)}) %collective-permute-start.1) | collective-permute-done | bytes 147488 | tf_op jit(solution)/shard_map/ppermute | solution.py:376
  28.3 3.8 %collective-permute-start.6 = (bf16[192,384]{1,0:T(8,128)(2,1)}, bf16[192,384]{1,0:T(8,128)(2,1)}, u32[]{:S(2)}, u32[]{:S(2)}) collective-permute-start(bf16[192,384]{1,0:T(8,128)(2,1)} %get-tuple-element.36), channel_id=1, source_target_pairs={{0,12},{1,13},{2,14},{3,15},{4,8},{5,9},{6,10},{7,11},{8,4},{9,5},... | collective-permute-start | bytes 442376 | tf_op jit(solution)/shard_map/ppermute | solution.py:376
  32.1 4.4 %collective-permute-done.2.refs_2_.refs_1_ = bf16[192,384]{1,0:T(8,128)(2,1)S(1)} collective-permute-done((bf16[192,384]{1,0:T(8,128)(2,1)S(1)}, bf16[192,384]{1,0:T(8,128)(2,1)S(1)}, u32[]{:S(2)}, u32[]{:S(2)}) %collective-permute-start.2) | collective-permute-done | bytes 147488 | tf_op jit(solution)/shard_map/ppermute | solution.py:376
  36.6 0.6 copy-done.13
  37.2 0.7 copy-done.14
  37.8 1.8 %late_right.1 = bf16[2,16,32,384]{3,2,1,0:T(8,128)(2,1)} custom-call(bf16[12,384,128]{2,1,0:T(8,128)(2,1)S(1)} %copy-done, f32[1,128]{1,0:T(1,128)S(1)} %bitcast.18, f32[1,128]{1,0:T(1,128)S(1)} %bitcast.22, bf16[128,512]{1,0:T(8,128)(2,1)S(1)} %copy-done.1, f32[1,512]{1,0:T(1,128)S(1)} %bitcast.15, bf16[192,384]{1,0:T(8,128)(2,1)} %copy-done.12, ...), custom_call_target="tpu_custom_call" | custom-call | flops 150994944 | bytes 1179648 | tf_op jit(solution)/shard_map/late_right/pallas_call | solution.py:382
  39.7 9.5 %all-to-all-done = bf16[32,64,384]{2,1,0:T(8,128)(2,1)S(1)} async-done(((bf16[32,64,384]{2,1,0:T(8,128)(2,1)}), bf16[32,64,384]{2,1,0:T(8,128)(2,1)S(1)}, u32[]{:S(2)}, u32[]{:S(2)}) %all-to-all-start) | async-done | bytes 1572896 | tf_op jit(solution)/shard_map/all_to_all | solution.py:344
  49.1 3.6 %all-to-all-start.1 = ((bf16[32,32,384]{2,1,0:T(8,128)(2,1)}), bf16[32,32,384]{2,1,0:T(8,128)(2,1)S(1)}, u32[]{:S(2)}, u32[]{:S(2)}) async-start(bf16[32,32,384]{2,1,0:T(8,128)(2,1)} %bitcast.29), calls=%async_computation.1 | async-start | bytes 1572864 | tf_op jit(solution)/shard_map/all_to_all | solution.py:399
  52.8 0.7 copy-done.10
  53.6 2.9 %gate.1.refs_8_.gate_ref = bf16[12,384,128]{2,1,0:T(8,128)(2,1)} custom-call(bf16[12,384,128]{2,1,0:T(8,128)(2,1)S(1)} %copy-done, f32[1,128]{1,0:T(1,128)S(1)} %bitcast.19, f32[1,128]{1,0:T(1,128)S(1)} %bitcast.23, bf16[128,128]{1,0:T(8,128)(2,1)S(1)} %copy-done.10, f32[1,128]{1,0:T(1,128)S(1)} %bitcast.27), custom_call_target="tpu_custom_call" | custom-call | flops 137438953472 | bytes 2359296 | tf_op jit(solution)/shard_map/gate/pallas_call | solution.py:403
  56.5 3.4 %first_products.1 = (bf16[96,256]{1,0:T(8,128)(2,1)S(1)}, bf16[96,256]{1,0:T(8,128)(2,1)S(1)}, bf16[96,256]{1,0:T(8,128)(2,1)S(1)}, bf16[96,256]{1,0:T(8,128)(2,...) custom-call(bf16[2048,384]{1,0:T(8,128)(2,1)S(1)} %bitcast.11, ...), custom_call_target="tpu_custom_call" | custom-call | flops 226492416 | bytes 3538944 | tf_op jit(solution)/shard_map/first_products/pallas_call | solution.py:426
  59.9 0.6 copy-done.3
  60.5 1.8 %collective-permute-start.15 = (bf16[96,256]{1,0:T(8,128)(2,1)S(1)}, bf16[96,256]{1,0:T(8,128)(2,1)S(1)}, u32[]{:S(2)}, u32[]{:S(2)}) collective-permute-start(bf16[96,256]{1,0:T(8,128)(2,1)S(1)} %get-tuple-element.46), channel_id=1, source_target_pairs={{0,8},{1,9},{2,10},{3,11},{4,12},{5,13},{6,14},{7,15},{8,0},{9,1},... | collective-permute-start | bytes 147464 | tf_op jit(solution)/shard_map/ppermute | solution.py:376
  62.3 2.4 %collective-permute-start.17 = (bf16[96,256]{1,0:T(8,128)(2,1)S(1)}, bf16[96,256]{1,0:T(8,128)(2,1)S(1)}, u32[]{:S(2)}, u32[]{:S(2)}) collective-permute-start(bf16[96,256]{1,0:T(8,128)(2,1)S(1)} %get-tuple-element.48), channel_id=1, source_target_pairs={{0,10},{1,11},{2,8},{3,9},{4,14},{5,15},{6,12},{7,13},{8,2},{9,3},... | collective-permute-start | bytes 147464 | tf_op jit(solution)/shard_map/ppermute | solution.py:376
  64.7 0.3 collective-permute-start.18
  65.0 2.6 %collective-permute-start.19 = (bf16[96,256]{1,0:T(8,128)(2,1)S(1)}, bf16[96,256]{1,0:T(8,128)(2,1)S(1)}, u32[]{:S(2)}, u32[]{:S(2)}) collective-permute-start(bf16[96,256]{1,0:T(8,128)(2,1)S(1)} %get-tuple-element.50), channel_id=1, source_target_pairs={{0,12},{1,13},{2,14},{3,15},{4,8},{5,9},{6,10},{7,11},{8,4},{9,5},... | collective-permute-start | bytes 147464 | tf_op jit(solution)/shard_map/ppermute | solution.py:376
  67.6 2.5 %collective-permute-start.20 = (bf16[96,256]{1,0:T(8,128)(2,1)S(1)}, bf16[96,256]{1,0:T(8,128)(2,1)S(1)}, u32[]{:S(2)}, u32[]{:S(2)}) collective-permute-start(bf16[96,256]{1,0:T(8,128)(2,1)S(1)} %get-tuple-element.51), channel_id=1, source_target_pairs={{0,13},{1,12},{2,15},{3,14},{4,9},{5,8},{6,11},{7,10},{8,5},{9,4},... | collective-permute-start | bytes 147464 | tf_op jit(solution)/shard_map/ppermute | solution.py:376
  70.0 2.2 %collective-permute-start.21 = (bf16[96,256]{1,0:T(8,128)(2,1)S(1)}, bf16[96,256]{1,0:T(8,128)(2,1)S(1)}, u32[]{:S(2)}, u32[]{:S(2)}) collective-permute-start(bf16[96,256]{1,0:T(8,128)(2,1)S(1)} %get-tuple-element.52), channel_id=1, source_target_pairs={{0,14},{1,15},{2,12},{3,13},{4,10},{5,11},{6,8},{7,9},{8,6},{9,7},... | collective-permute-start | bytes 147464 | tf_op jit(solution)/shard_map/ppermute | solution.py:376
  72.3 2.3 %collective-permute-start.22 = (bf16[96,256]{1,0:T(8,128)(2,1)S(1)}, bf16[96,256]{1,0:T(8,128)(2,1)S(1)}, u32[]{:S(2)}, u32[]{:S(2)}) collective-permute-start(bf16[96,256]{1,0:T(8,128)(2,1)S(1)} %get-tuple-element.53), channel_id=1, source_target_pairs={{0,15},{1,14},{2,13},{3,12},{4,11},{5,10},{6,9},{7,8},{8,7},{9,6},... | collective-permute-start | bytes 147464 | tf_op jit(solution)/shard_map/ppermute | solution.py:376
  74.6 0.4 collective-permute-done.19.refs_12_.refs_4_
  75.0 0.4 collective-permute-done.20.refs_13_.refs_5_
  75.4 2.8 %collective-permute-done.21.refs_14_.refs_6_ = bf16[96,256]{1,0:T(8,128)(2,1)S(1)} collective-permute-done((bf16[96,256]{1,0:T(8,128)(2,1)S(1)}, bf16[96,256]{1,0:T(8,128)(2,1)S(1)}, u32[]{:S(2)}, u32[]{:S(2)}) %collective-permute-start.21) | collective-permute-done | bytes 49184 | tf_op jit(solution)/shard_map/ppermute | solution.py:376
  78.2 0.6 collective-permute-done.22.refs_15_.refs_7_
  78.9 0.6 copy-done.22
  79.4 3.2 %second_products.1 = bf16[16,96,128]{2,1,0:T(8,128)(2,1)} custom-call(bf16[1024,384]{1,0:T(8,128)(2,1)S(1)} %bitcast.12, bf16[8,192,384]{2,1,0:T(8,128)(2,1)} %get-tuple-element.54.left_ref, bf16[96,256]{1,0:T(8,128)(2,1)} %copy-done.15, bf16[96,256]{1,0:T(8,128)(2,1)} %copy-done.16, bf16[96,256]{1,0:T(8,128)(2,1)} %copy-done.17, ...), custom_call_target="tpu_custom_call" | custom-call | flops 226492416 | bytes 3538944 | tf_op jit(solution)/shard_map/second_products/pallas_call | solution.py:448
  82.7 3.9 %all-to-all-start.2 = ((bf16[16,96,128]{2,1,0:T(8,128)(2,1)}), bf16[16,96,128]{2,1,0:T(8,128)(2,1)S(1)}, u32[]{:S(2)}, u32[]{:S(2)}) async-start(bf16[16,96,128]{2,1,0:T(8,128)(2,1)} %second_products.1), calls=%async_computation.2 | async-start | bytes 786432 | tf_op jit(solution)/shard_map/all_to_all | solution.py:465
  86.6 1.4 %collective-permute-start.10 = (bf16[96,256]{1,0:T(8,128)(2,1)S(1)}, bf16[96,256]{1,0:T(8,128)(2,1)S(1)}, u32[]{:S(2)}, u32[]{:S(2)}) collective-permute-start(bf16[96,256]{1,0:T(8,128)(2,1)S(1)} %get-tuple-element.41), channel_id=1, source_target_pairs={{0,3},{1,2},{2,1},{3,0},{4,7},{5,6},{6,5},{7,4},{8,11},{9,10},{10,... | collective-permute-start | bytes 147464 | tf_op jit(solution)/shard_map/ppermute | solution.py:376
  88.0 1.5 %collective-permute-start.11 = (bf16[96,256]{1,0:T(8,128)(2,1)S(1)}, bf16[96,256]{1,0:T(8,128)(2,1)S(1)}, u32[]{:S(2)}, u32[]{:S(2)}) collective-permute-start(bf16[96,256]{1,0:T(8,128)(2,1)S(1)} %get-tuple-element.42), channel_id=1, source_target_pairs={{0,4},{1,5},{2,6},{3,7},{4,0},{5,1},{6,2},{7,3},{8,12},{9,13},{10,... | collective-permute-start | bytes 147464 | tf_op jit(solution)/shard_map/ppermute | solution.py:376
  89.7 1.5 %collective-permute-start.13 = (bf16[96,256]{1,0:T(8,128)(2,1)S(1)}, bf16[96,256]{1,0:T(8,128)(2,1)S(1)}, u32[]{:S(2)}, u32[]{:S(2)}) collective-permute-start(bf16[96,256]{1,0:T(8,128)(2,1)S(1)} %get-tuple-element.44), channel_id=1, source_target_pairs={{0,6},{1,7},{2,4},{3,5},{4,2},{5,3},{6,0},{7,1},{8,14},{9,15},{10,... | collective-permute-start | bytes 147464 | tf_op jit(solution)/shard_map/ppermute | solution.py:376
  91.2 1.2 %collective-permute-start.14 = (bf16[96,256]{1,0:T(8,128)(2,1)S(1)}, bf16[96,256]{1,0:T(8,128)(2,1)S(1)}, u32[]{:S(2)}, u32[]{:S(2)}) collective-permute-start(bf16[96,256]{1,0:T(8,128)(2,1)S(1)} %get-tuple-element.45), channel_id=1, source_target_pairs={{0,7},{1,6},{2,5},{3,4},{4,3},{5,2},{6,1},{7,0},{8,15},{9,14},{10,... | collective-permute-start | bytes 147464 | tf_op jit(solution)/shard_map/ppermute | solution.py:376
  92.4 1.5 %collective-permute-done.10.refs_3_ = bf16[96,256]{1,0:T(8,128)(2,1)S(1)} collective-permute-done((bf16[96,256]{1,0:T(8,128)(2,1)S(1)}, bf16[96,256]{1,0:T(8,128)(2,1)S(1)}, u32[]{:S(2)}, u32[]{:S(2)}) %collective-permute-start.10) | collective-permute-done | bytes 49184 | tf_op jit(solution)/shard_map/ppermute | solution.py:376
  93.9 1.3 %collective-permute-start.8 = (bf16[96,256]{1,0:T(8,128)(2,1)S(1)}, bf16[96,256]{1,0:T(8,128)(2,1)S(1)}, u32[]{:S(2)}, u32[]{:S(2)}) collective-permute-start(bf16[96,256]{1,0:T(8,128)(2,1)S(1)} %get-tuple-element.39), channel_id=1, source_target_pairs={{0,1},{1,0},{2,3},{3,2},{4,5},{5,4},{6,7},{7,6},{8,9},{9,8},{10,11... | collective-permute-start | bytes 147464 | tf_op jit(solution)/shard_map/ppermute | solution.py:376
  95.3 3.2 %collective-permute-start.9 = (bf16[96,256]{1,0:T(8,128)(2,1)S(1)}, bf16[96,256]{1,0:T(8,128)(2,1)S(1)}, u32[]{:S(2)}, u32[]{:S(2)}) collective-permute-start(bf16[96,256]{1,0:T(8,128)(2,1)S(1)} %get-tuple-element.40), channel_id=1, source_target_pairs={{0,2},{1,3},{2,0},{3,1},{4,6},{5,7},{6,4},{7,5},{8,10},{9,11},{10,... | collective-permute-start | bytes 147464 | tf_op jit(solution)/shard_map/ppermute | solution.py:376
  98.6 2.0 %collective-permute-done.9.refs_2_ = bf16[96,256]{1,0:T(8,128)(2,1)S(1)} collective-permute-done((bf16[96,256]{1,0:T(8,128)(2,1)S(1)}, bf16[96,256]{1,0:T(8,128)(2,1)S(1)}, u32[]{:S(2)}, u32[]{:S(2)}) %collective-permute-start.9) | collective-permute-done | bytes 49184 | tf_op jit(solution)/shard_map/ppermute | solution.py:376
  100.6 0.6 copy-done.29
  101.2 1.3 %collect.1.first_ref = bf16[16,96,256]{2,1,0:T(8,128)(2,1)S(1)} custom-call(bf16[96,256]{1,0:T(8,128)(2,1)} %copy-done.3, bf16[96,256]{1,0:T(8,128)(2,1)} %copy-done.28, bf16[96,256]{1,0:T(8,128)(2,1)} %copy-done.29, bf16[96,256]{1,0:T(8,128)(2,1)} %copy-done.23, bf16[96,256]{1,0:T(8,128)(2,1)} %copy-done.24, bf16[96,256]{1,0:T(8,128)(2,1)} %copy-done.25, ...), custom_call_target="tpu_custom_call" | custom-call | bytes 2359296 | tf_op jit(solution)/shard_map/collect/pallas_call | solution.py:467
  102.5 5.8 %update.1 = bf16[12,384,128]{2,1,0:T(8,128)(2,1)} custom-call(bf16[16,96,256]{2,1,0:T(8,128)(2,1)S(1)} %collect.1.first_ref, bf16[16,96,128]{2,1,0:T(8,128)(2,1)S(1)} %all-to-all-done.2.second_ref, bf16[12,384,128]{2,1,0:T(8,128)(2,1)} %gate.1.refs_8_.gate_ref, f32[1,128]{1,0:T(1,128)S(1)} %bitcast.24, f32[1,128]{1,0:T(1,128)S(1)} %bitcast.25, ...), custom_call_target="tpu_custom_call" | custom-call | flops 150994944 | bytes 3538944 | tf_op jit(solution)/shard_map/update/pallas_call | solution.py:479
  (72 shorter events, 0.4 us)
Async XLA Ops:
  3.7 7.4 %copy-start = (bf16[12,384,128]{2,1,0:T(8,128)(2,1)S(1)}, bf16[12,384,128]{2,1,0:T(8,128)(2,1)}, u32[]{:S(2)}) copy-start(bf16[12,384,128]{2,1,0:T(8,128)(2,1)} %pair_ref.5) | copy-start | bytes 3538948
  3.7 10.3 %copy-start.1 = (bf16[128,512]{1,0:T(8,128)(2,1)S(1)}, bf16[128,512]{1,0:T(8,128)(2,1)}, u32[]{:S(2)}) copy-start(bf16[128,512]{1,0:T(8,128)(2,1)} %w_ref.6) | copy-start | bytes 393220
  3.7 10.3 %copy-start.4 = (f32[512]{0:T(512)S(1)}, f32[512]{0:T(512)}, u32[]{:S(2)}) copy-start(f32[512]{0:T(512)} %param.15) | copy-start | bytes 6148
  3.7 10.3 %copy-start.5 = (f32[128]{0:T(128)S(1)}, f32[128]{0:T(128)}, u32[]{:S(2)}) copy-start(f32[128]{0:T(128)} %param.12) | copy-start | bytes 1540
  3.7 10.3 %copy-start.6 = (f32[128]{0:T(128)S(1)}, f32[128]{0:T(128)}, u32[]{:S(2)}) copy-start(f32[128]{0:T(128)} %param.13) | copy-start | bytes 1540
  3.8 45.4 %all-to-all-start = ((bf16[32,64,384]{2,1,0:T(8,128)(2,1)}), bf16[32,64,384]{2,1,0:T(8,128)(2,1)S(1)}, u32[]{:S(2)}, u32[]{:S(2)}) async-start(bf16[32,64,384]{2,1,0:T(8,128)(2,1)} %bitcast.28), calls=%async_computation | async-start | bytes 3145728 | tf_op jit(solution)/shard_map/all_to_all | solution.py:344
  11.1 2.9 %collective-permute-start = (bf16[12,384,128]{2,1,0:T(8,128)(2,1)S(1)}, bf16[12,384,128]{2,1,0:T(8,128)(2,1)S(1)}, u32[]{:S(2)}, u32[]{:S(2)}) collective-permute-start(bf16[12,384,128]{2,1,0:T(8,128)(2,1)S(1)} %copy-done), channel_id=1, source_target_pairs={{0,1},{1,0},{2,3},{3,2},{4,5},{5,4},{6,7},{7,6},{8,9},{9,8},{10,11... | collective-permute-start | bytes 3538952 | tf_op jit(solution)/shard_map/ppermute | solution.py:348
  20.0 8.3 %collective-permute-start.1 = (bf16[192,384]{1,0:T(8,128)(2,1)S(1)}, bf16[192,384]{1,0:T(8,128)(2,1)S(1)}, u32[]{:S(2)}, u32[]{:S(2)}) collective-permute-start(bf16[192,384]{1,0:T(8,128)(2,1)S(1)} %get-tuple-element.31), channel_id=1, source_target_pairs={{0,2},{1,3},{2,0},{3,1},{4,6},{5,7},{6,4},{7,5},{8,10},{9,11},{10,... | collective-permute-start | bytes 442376 | tf_op jit(solution)/shard_map/ppermute | solution.py:376
  21.8 14.8 %collective-permute-start.2 = (bf16[192,384]{1,0:T(8,128)(2,1)S(1)}, bf16[192,384]{1,0:T(8,128)(2,1)S(1)}, u32[]{:S(2)}, u32[]{:S(2)}) collective-permute-start(bf16[192,384]{1,0:T(8,128)(2,1)S(1)} %get-tuple-element.32), channel_id=1, source_target_pairs={{0,4},{1,5},{2,6},{3,7},{4,0},{5,1},{6,2},{7,3},{8,12},{9,13},{10,... | collective-permute-start | bytes 442376 | tf_op jit(solution)/shard_map/ppermute | solution.py:376
  23.2 13.3 %collective-permute-start.3 = (bf16[192,384]{1,0:T(8,128)(2,1)S(1)}, bf16[192,384]{1,0:T(8,128)(2,1)S(1)}, u32[]{:S(2)}, u32[]{:S(2)}) collective-permute-start(bf16[192,384]{1,0:T(8,128)(2,1)S(1)} %get-tuple-element.33), channel_id=1, source_target_pairs={{0,6},{1,7},{2,4},{3,5},{4,2},{5,3},{6,0},{7,1},{8,14},{9,15},{10,... | collective-permute-start | bytes 442376 | tf_op jit(solution)/shard_map/ppermute | solution.py:376
  23.5 33.0 %collective-permute-start.4 = (bf16[192,384]{1,0:T(8,128)(2,1)}, bf16[192,384]{1,0:T(8,128)(2,1)}, u32[]{:S(2)}, u32[]{:S(2)}) collective-permute-start(bf16[192,384]{1,0:T(8,128)(2,1)} %get-tuple-element.34), channel_id=1, source_target_pairs={{0,8},{1,9},{2,10},{3,11},{4,12},{5,13},{6,14},{7,15},{8,0},{9,1},... | collective-permute-start | bytes 442376 | tf_op jit(solution)/shard_map/ppermute | solution.py:376
  25.2 31.2 %collective-permute-start.5 = (bf16[192,384]{1,0:T(8,128)(2,1)}, bf16[192,384]{1,0:T(8,128)(2,1)}, u32[]{:S(2)}, u32[]{:S(2)}) collective-permute-start(bf16[192,384]{1,0:T(8,128)(2,1)} %get-tuple-element.35), channel_id=1, source_target_pairs={{0,10},{1,11},{2,8},{3,9},{4,14},{5,15},{6,12},{7,13},{8,2},{9,3},... | collective-permute-start | bytes 442376 | tf_op jit(solution)/shard_map/ppermute | solution.py:376
  28.3 8.3 %copy-start.12 = (bf16[192,384]{1,0:T(8,128)(2,1)}, bf16[192,384]{1,0:T(8,128)(2,1)S(1)}, u32[]{:S(2)}) copy-start(bf16[192,384]{1,0:T(8,128)(2,1)S(1)} %collective-permute-done.1.refs_1_.refs_0_) | copy-start | bytes 442372
  28.3 28.2 %collective-permute-start.6 = (bf16[192,384]{1,0:T(8,128)(2,1)}, bf16[192,384]{1,0:T(8,128)(2,1)}, u32[]{:S(2)}, u32[]{:S(2)}) collective-permute-start(bf16[192,384]{1,0:T(8,128)(2,1)} %get-tuple-element.36), channel_id=1, source_target_pairs={{0,12},{1,13},{2,14},{3,15},{4,8},{5,9},{6,10},{7,11},{8,4},{9,5},... | collective-permute-start | bytes 442376 | tf_op jit(solution)/shard_map/ppermute | solution.py:376
  36.5 19.9 %collective-permute-start.7 = (bf16[192,384]{1,0:T(8,128)(2,1)}, bf16[192,384]{1,0:T(8,128)(2,1)}, u32[]{:S(2)}, u32[]{:S(2)}) collective-permute-start(bf16[192,384]{1,0:T(8,128)(2,1)} %get-tuple-element.37), channel_id=1, source_target_pairs={{0,14},{1,15},{2,12},{3,13},{4,10},{5,11},{6,8},{7,9},{8,6},{9,7},... | collective-permute-start | bytes 442376 | tf_op jit(solution)/shard_map/ppermute | solution.py:376
  39.7 13.1 %copy-start.11 = (f32[128]{0:T(128)S(1)}, f32[128]{0:T(128)}, u32[]{:S(2)}) copy-start(f32[128]{0:T(128)} %param.17) | copy-start | bytes 1540
  49.1 25.4 %all-to-all-start.1 = ((bf16[32,32,384]{2,1,0:T(8,128)(2,1)}), bf16[32,32,384]{2,1,0:T(8,128)(2,1)S(1)}, u32[]{:S(2)}, u32[]{:S(2)}) async-start(bf16[32,32,384]{2,1,0:T(8,128)(2,1)} %bitcast.29), calls=%async_computation.1 | async-start | bytes 1572864 | tf_op jit(solution)/shard_map/all_to_all | solution.py:399
  60.5 7.1 %collective-permute-start.15 = (bf16[96,256]{1,0:T(8,128)(2,1)S(1)}, bf16[96,256]{1,0:T(8,128)(2,1)S(1)}, u32[]{:S(2)}, u32[]{:S(2)}) collective-permute-start(bf16[96,256]{1,0:T(8,128)(2,1)S(1)} %get-tuple-element.46), channel_id=1, source_target_pairs={{0,8},{1,9},{2,10},{3,11},{4,12},{5,13},{6,14},{7,15},{8,0},{9,1},... | collective-permute-start | bytes 147464 | tf_op jit(solution)/shard_map/ppermute | solution.py:376
  62.3 7.8 %collective-permute-start.16 = (bf16[96,256]{1,0:T(8,128)(2,1)S(1)}, bf16[96,256]{1,0:T(8,128)(2,1)S(1)}, u32[]{:S(2)}, u32[]{:S(2)}) collective-permute-start(bf16[96,256]{1,0:T(8,128)(2,1)S(1)} %get-tuple-element.47), channel_id=1, source_target_pairs={{0,9},{1,8},{2,11},{3,10},{4,13},{5,12},{6,15},{7,14},{8,1},{9,0},... | collective-permute-start | bytes 147464 | tf_op jit(solution)/shard_map/ppermute | solution.py:376
  62.3 10.0 %collective-permute-start.17 = (bf16[96,256]{1,0:T(8,128)(2,1)S(1)}, bf16[96,256]{1,0:T(8,128)(2,1)S(1)}, u32[]{:S(2)}, u32[]{:S(2)}) collective-permute-start(bf16[96,256]{1,0:T(8,128)(2,1)S(1)} %get-tuple-element.48), channel_id=1, source_target_pairs={{0,10},{1,11},{2,8},{3,9},{4,14},{5,15},{6,12},{7,13},{8,2},{9,3},... | collective-permute-start | bytes 147464 | tf_op jit(solution)/shard_map/ppermute | solution.py:376
  64.7 9.9 %collective-permute-start.18 = (bf16[96,256]{1,0:T(8,128)(2,1)S(1)}, bf16[96,256]{1,0:T(8,128)(2,1)S(1)}, u32[]{:S(2)}, u32[]{:S(2)}) collective-permute-start(bf16[96,256]{1,0:T(8,128)(2,1)S(1)} %get-tuple-element.49), channel_id=1, source_target_pairs={{0,11},{1,10},{2,9},{3,8},{4,15},{5,14},{6,13},{7,12},{8,3},{9,2},... | collective-permute-start | bytes 147464 | tf_op jit(solution)/shard_map/ppermute | solution.py:376
  65.0 10.0 %collective-permute-start.19 = (bf16[96,256]{1,0:T(8,128)(2,1)S(1)}, bf16[96,256]{1,0:T(8,128)(2,1)S(1)}, u32[]{:S(2)}, u32[]{:S(2)}) collective-permute-start(bf16[96,256]{1,0:T(8,128)(2,1)S(1)} %get-tuple-element.50), channel_id=1, source_target_pairs={{0,12},{1,13},{2,14},{3,15},{4,8},{5,9},{6,10},{7,11},{8,4},{9,5},... | collective-permute-start | bytes 147464 | tf_op jit(solution)/shard_map/ppermute | solution.py:376
  67.6 11.3 %copy-start.15 = (bf16[96,256]{1,0:T(8,128)(2,1)}, bf16[96,256]{1,0:T(8,128)(2,1)S(1)}, u32[]{:S(2)}) copy-start(bf16[96,256]{1,0:T(8,128)(2,1)S(1)} %collective-permute-done.15.refs_8_.refs_0_) | copy-start | bytes 147460
  67.6 7.8 %collective-permute-start.20 = (bf16[96,256]{1,0:T(8,128)(2,1)S(1)}, bf16[96,256]{1,0:T(8,128)(2,1)S(1)}, u32[]{:S(2)}, u32[]{:S(2)}) collective-permute-start(bf16[96,256]{1,0:T(8,128)(2,1)S(1)} %get-tuple-element.51), channel_id=1, source_target_pairs={{0,13},{1,12},{2,15},{3,14},{4,9},{5,8},{6,11},{7,10},{8,5},{9,4},... | collective-permute-start | bytes 147464 | tf_op jit(solution)/shard_map/ppermute | solution.py:376
  70.0 8.8 %copy-start.16 = (bf16[96,256]{1,0:T(8,128)(2,1)}, bf16[96,256]{1,0:T(8,128)(2,1)S(1)}, u32[]{:S(2)}) copy-start(bf16[96,256]{1,0:T(8,128)(2,1)S(1)} %collective-permute-done.16.refs_9_.refs_1_) | copy-start | bytes 147460
  70.0 8.2 %collective-permute-start.21 = (bf16[96,256]{1,0:T(8,128)(2,1)S(1)}, bf16[96,256]{1,0:T(8,128)(2,1)S(1)}, u32[]{:S(2)}, u32[]{:S(2)}) collective-permute-start(bf16[96,256]{1,0:T(8,128)(2,1)S(1)} %get-tuple-element.52), channel_id=1, source_target_pairs={{0,14},{1,15},{2,12},{3,13},{4,10},{5,11},{6,8},{7,9},{8,6},{9,7},... | collective-permute-start | bytes 147464 | tf_op jit(solution)/shard_map/ppermute | solution.py:376
  72.3 6.6 %copy-start.17 = (bf16[96,256]{1,0:T(8,128)(2,1)}, bf16[96,256]{1,0:T(8,128)(2,1)S(1)}, u32[]{:S(2)}) copy-start(bf16[96,256]{1,0:T(8,128)(2,1)S(1)} %collective-permute-done.17.refs_10_.refs_2_) | copy-start | bytes 147460
  72.3 6.5 %collective-permute-start.22 = (bf16[96,256]{1,0:T(8,128)(2,1)S(1)}, bf16[96,256]{1,0:T(8,128)(2,1)S(1)}, u32[]{:S(2)}, u32[]{:S(2)}) collective-permute-start(bf16[96,256]{1,0:T(8,128)(2,1)S(1)} %get-tuple-element.53), channel_id=1, source_target_pairs={{0,15},{1,14},{2,13},{3,12},{4,11},{5,10},{6,9},{7,8},{8,7},{9,6},... | collective-permute-start | bytes 147464 | tf_op jit(solution)/shard_map/ppermute | solution.py:376
  74.6 4.3 %copy-start.18 = (bf16[96,256]{1,0:T(8,128)(2,1)}, bf16[96,256]{1,0:T(8,128)(2,1)S(1)}, u32[]{:S(2)}) copy-start(bf16[96,256]{1,0:T(8,128)(2,1)S(1)} %collective-permute-done.18.refs_11_.refs_3_) | copy-start | bytes 147460
  75.0 3.9 %copy-start.19 = (bf16[96,256]{1,0:T(8,128)(2,1)}, bf16[96,256]{1,0:T(8,128)(2,1)S(1)}, u32[]{:S(2)}) copy-start(bf16[96,256]{1,0:T(8,128)(2,1)S(1)} %collective-permute-done.19.refs_12_.refs_4_) | copy-start | bytes 147460
  75.4 3.5 %copy-start.20 = (bf16[96,256]{1,0:T(8,128)(2,1)}, bf16[96,256]{1,0:T(8,128)(2,1)S(1)}, u32[]{:S(2)}) copy-start(bf16[96,256]{1,0:T(8,128)(2,1)S(1)} %collective-permute-done.20.refs_13_.refs_5_) | copy-start | bytes 147460
  82.7 19.8 %copy-start.7 = (f32[128]{0:T(128)S(1)}, f32[128]{0:T(128)}, u32[]{:S(2)}) copy-start(f32[128]{0:T(128)} %param.18) | copy-start | bytes 1540
  82.7 19.8 %copy-start.8 = (f32[128]{0:T(128)S(1)}, f32[128]{0:T(128)}, u32[]{:S(2)}) copy-start(f32[128]{0:T(128)} %param.19) | copy-start | bytes 1540
  82.7 19.8 %copy-start.9 = (f32[128]{0:T(128)S(1)}, f32[128]{0:T(128)}, u32[]{:S(2)}) copy-start(f32[128]{0:T(128)} %param.21) | copy-start | bytes 1540
  82.7 19.8 %all-to-all-start.2 = ((bf16[16,96,128]{2,1,0:T(8,128)(2,1)}), bf16[16,96,128]{2,1,0:T(8,128)(2,1)S(1)}, u32[]{:S(2)}, u32[]{:S(2)}) async-start(bf16[16,96,128]{2,1,0:T(8,128)(2,1)} %second_products.1), calls=%async_computation.2 | async-start | bytes 786432 | tf_op jit(solution)/shard_map/all_to_all | solution.py:465
  86.6 7.4 %collective-permute-start.10 = (bf16[96,256]{1,0:T(8,128)(2,1)S(1)}, bf16[96,256]{1,0:T(8,128)(2,1)S(1)}, u32[]{:S(2)}, u32[]{:S(2)}) collective-permute-start(bf16[96,256]{1,0:T(8,128)(2,1)S(1)} %get-tuple-element.41), channel_id=1, source_target_pairs={{0,3},{1,2},{2,1},{3,0},{4,7},{5,6},{6,5},{7,4},{8,11},{9,10},{10,... | collective-permute-start | bytes 147464 | tf_op jit(solution)/shard_map/ppermute | solution.py:376
  88.0 7.2 %collective-permute-start.11 = (bf16[96,256]{1,0:T(8,128)(2,1)S(1)}, bf16[96,256]{1,0:T(8,128)(2,1)S(1)}, u32[]{:S(2)}, u32[]{:S(2)}) collective-permute-start(bf16[96,256]{1,0:T(8,128)(2,1)S(1)} %get-tuple-element.42), channel_id=1, source_target_pairs={{0,4},{1,5},{2,6},{3,7},{4,0},{5,1},{6,2},{7,3},{8,12},{9,13},{10,... | collective-permute-start | bytes 147464 | tf_op jit(solution)/shard_map/ppermute | solution.py:376
  89.5 9.0 %collective-permute-start.12 = (bf16[96,256]{1,0:T(8,128)(2,1)S(1)}, bf16[96,256]{1,0:T(8,128)(2,1)S(1)}, u32[]{:S(2)}, u32[]{:S(2)}) collective-permute-start(bf16[96,256]{1,0:T(8,128)(2,1)S(1)} %get-tuple-element.43), channel_id=1, source_target_pairs={{0,5},{1,4},{2,7},{3,6},{4,1},{5,0},{6,3},{7,2},{8,13},{9,12},{10,... | collective-permute-start | bytes 147464 | tf_op jit(solution)/shard_map/ppermute | solution.py:376
  89.7 8.8 %collective-permute-start.13 = (bf16[96,256]{1,0:T(8,128)(2,1)S(1)}, bf16[96,256]{1,0:T(8,128)(2,1)S(1)}, u32[]{:S(2)}, u32[]{:S(2)}) collective-permute-start(bf16[96,256]{1,0:T(8,128)(2,1)S(1)} %get-tuple-element.44), channel_id=1, source_target_pairs={{0,6},{1,7},{2,4},{3,5},{4,2},{5,3},{6,0},{7,1},{8,14},{9,15},{10,... | collective-permute-start | bytes 147464 | tf_op jit(solution)/shard_map/ppermute | solution.py:376
  91.2 7.3 %collective-permute-start.14 = (bf16[96,256]{1,0:T(8,128)(2,1)S(1)}, bf16[96,256]{1,0:T(8,128)(2,1)S(1)}, u32[]{:S(2)}, u32[]{:S(2)}) collective-permute-start(bf16[96,256]{1,0:T(8,128)(2,1)S(1)} %get-tuple-element.45), channel_id=1, source_target_pairs={{0,7},{1,6},{2,5},{3,4},{4,3},{5,2},{6,1},{7,0},{8,15},{9,14},{10,... | collective-permute-start | bytes 147464 | tf_op jit(solution)/shard_map/ppermute | solution.py:376
  93.9 6.7 %copy-start.23 = (bf16[96,256]{1,0:T(8,128)(2,1)}, bf16[96,256]{1,0:T(8,128)(2,1)S(1)}, u32[]{:S(2)}) copy-start(bf16[96,256]{1,0:T(8,128)(2,1)S(1)} %collective-permute-done.10.refs_3_) | copy-start | bytes 147460
  93.9 4.6 %collective-permute-start.8 = (bf16[96,256]{1,0:T(8,128)(2,1)S(1)}, bf16[96,256]{1,0:T(8,128)(2,1)S(1)}, u32[]{:S(2)}, u32[]{:S(2)}) collective-permute-start(bf16[96,256]{1,0:T(8,128)(2,1)S(1)} %get-tuple-element.39), channel_id=1, source_target_pairs={{0,1},{1,0},{2,3},{3,2},{4,5},{5,4},{6,7},{7,6},{8,9},{9,8},{10,11... | collective-permute-start | bytes 147464 | tf_op jit(solution)/shard_map/ppermute | solution.py:376
  95.3 5.3 %copy-start.24 = (bf16[96,256]{1,0:T(8,128)(2,1)}, bf16[96,256]{1,0:T(8,128)(2,1)S(1)}, u32[]{:S(2)}) copy-start(bf16[96,256]{1,0:T(8,128)(2,1)S(1)} %collective-permute-done.11.refs_4_) | copy-start | bytes 147460
  95.3 5.3 %collective-permute-start.9 = (bf16[96,256]{1,0:T(8,128)(2,1)S(1)}, bf16[96,256]{1,0:T(8,128)(2,1)S(1)}, u32[]{:S(2)}, u32[]{:S(2)}) collective-permute-start(bf16[96,256]{1,0:T(8,128)(2,1)S(1)} %get-tuple-element.40), channel_id=1, source_target_pairs={{0,2},{1,3},{2,0},{3,1},{4,6},{5,7},{6,4},{7,5},{8,10},{9,11},{10,... | collective-permute-start | bytes 147464 | tf_op jit(solution)/shard_map/ppermute | solution.py:376
  98.5 2.1 %copy-start.25 = (bf16[96,256]{1,0:T(8,128)(2,1)}, bf16[96,256]{1,0:T(8,128)(2,1)S(1)}, u32[]{:S(2)}) copy-start(bf16[96,256]{1,0:T(8,128)(2,1)S(1)} %collective-permute-done.12.refs_5_) | copy-start | bytes 147460
  98.5 2.1 %copy-start.26 = (bf16[96,256]{1,0:T(8,128)(2,1)}, bf16[96,256]{1,0:T(8,128)(2,1)S(1)}, u32[]{:S(2)}) copy-start(bf16[96,256]{1,0:T(8,128)(2,1)S(1)} %collective-permute-done.13.refs_6_) | copy-start | bytes 147460
  98.5 2.1 %copy-start.27 = (bf16[96,256]{1,0:T(8,128)(2,1)}, bf16[96,256]{1,0:T(8,128)(2,1)S(1)}, u32[]{:S(2)}) copy-start(bf16[96,256]{1,0:T(8,128)(2,1)S(1)} %collective-permute-done.14.refs_7_) | copy-start | bytes 147460
  98.6 2.1 %copy-start.28 = (bf16[96,256]{1,0:T(8,128)(2,1)}, bf16[96,256]{1,0:T(8,128)(2,1)S(1)}, u32[]{:S(2)}) copy-start(bf16[96,256]{1,0:T(8,128)(2,1)S(1)} %collective-permute-done.8.refs_1_) | copy-start | bytes 147460
  (8 other events, 5.2 us)

commit v11 on v7

--- a/solution.py
+++ b/solution.py
@@ -12,6 +12,7 @@
 CHANNELS = 128
 BLOCK = 8
 STEP = 4
+PAIRED = 2
 SIZE = 32
 LANES = 128
 GATHER = 32
@@ -60,37 +61,57 @@
 
 def factor(normed, wt, bias):
     width = wt.shape[0] // 2
-    lanes = normed.shape[0]
-    gate = dot_nt(wt[:width], normed) + widen(bias[:width], lanes)
-    value = dot_nt(wt[width:], normed) + widen(bias[width:], lanes)
-    return sigmoid(gate) * value
-
-
-def as_rows(values, k):
+    both = dot_nt(wt, normed) + widen(bias, normed.shape[0])
+    return sigmoid(both[:width]) * both[width:]
+
+
+def as_rows(values, k, step=STEP):
     hosts = values.shape[0] // BLOCK
     return jnp.concatenate(
-        [values[:, r * k : (r + 1) * k].reshape(hosts, BLOCK, k) for r in range(STEP)], axis=1
+        [values[:, r * k : (r + 1) * k].reshape(hosts, BLOCK, k) for r in range(step)], axis=1
     )
 
 
-def right_kernel(pair_ref, gain_ref, shift_ref, w_ref, b_ref, out_ref, pair, made, arrive, leave):
+def turns_of(rows):
+    cuts = [0, PAIRED, *range(PAIRED + STEP, rows - PAIRED + 1, STEP), rows]
+    return list(zip(cuts[:-1], (n - m for m, n in zip(cuts[:-1], cuts[1:]))))
+
+
+def right_kernel(
+    pair_ref, gain_ref, shift_ref, w_ref, b_ref, out_ref, pair, gain, shift, w, bias, made,
+    arrive, leave, sems,
+):
     rows, k, width = pair.shape
-    starts = range(0, rows, STEP)
+    half = w.shape[1]
+    turns = turns_of(rows)
     loads = [
-        pltpu.make_async_copy(pair_ref.at[pl.ds(r, STEP)], pair.at[pl.ds(r, STEP)], arrive.at[n])
-        for n, r in enumerate(starts)
+        pltpu.make_async_copy(pair_ref.at[pl.ds(r, size)], pair.at[pl.ds(r, size)], arrive.at[n])
+        for n, (r, size) in enumerate(turns)
     ]
-    for load in loads:
-        load.start()
-    wt = w_ref[...].astype(f32).T.astype(bf16)
-    bt = column(b_ref[...])
+    small = [
+        pltpu.make_async_copy(ref, to, sems.at[n])
+        for n, (ref, to) in enumerate(
+            [
+                (w_ref.at[:, pl.ds(half, half)], w),
+                (b_ref.at[:, pl.ds(half, half)], bias),
+                (gain_ref, gain),
+                (shift_ref, shift),
+            ]
+        )
+    ]
+    for copy in loads[:1] + small + loads[1:]:
+        copy.start()
+    for copy in small:
+        copy.wait()
+    wt = w[...].astype(f32).T.astype(bf16)
+    bt = column(bias[...])
     stores = []
-    for n, r in enumerate(starts):
+    for n, (r, size) in enumerate(turns):
         loads[n].wait()
-        x = pair[r : r + STEP].astype(f32).reshape(STEP * k, width)
-        normed = normalize(x, gain_ref[...], shift_ref[...])
-        at = pl.ds(r * BLOCK, STEP * BLOCK)
-        made[:, at, :] = as_rows(factor(normed, wt, bt), k).astype(bf16)
+        x = pair[r : r + size].astype(f32).reshape(size * k, width)
+        normed = normalize(x, gain[...], shift[...])
+        at = pl.ds(r * BLOCK, size * BLOCK)
+        made[:, at, :] = as_rows(factor(normed, wt, bt), k, size).astype(bf16)
         for p in range(out_ref.shape[0]):
             stores.append(
                 pltpu.make_async_copy(made.at[:, at, :], out_ref.at[p, :, at, :], leave.at[p, n])
@@ -228,23 +249,22 @@
 
     vmem = pl.BlockSpec(memory_space=pltpu.VMEM)
     anywhere = pl.BlockSpec(memory_space=pl.ANY)
+    turns = len(turns_of(rows))
     right = pl.pallas_call(
         right_kernel,
-        grid=(1,),
-        in_specs=[
-            anywhere,
-            whole((1, width)),
-            whole((1, width)),
-            pl.BlockSpec((width, 2 * hidden), lambda s: (0, 1)),
-            pl.BlockSpec((1, 2 * hidden), lambda s: (0, 1)),
-        ],
+        in_specs=[anywhere] * 5,
         out_specs=anywhere,
         out_shape=bfloat(parts, hosts, tall, k),
         scratch_shapes=[
             pltpu.VMEM((rows, k, width), bf16),
+            pltpu.VMEM((1, width), f32),
+            pltpu.VMEM((1, width), f32),
+            pltpu.VMEM((width, 2 * hidden), bf16),
+            pltpu.VMEM((1, 2 * hidden), f32),
             pltpu.VMEM((hosts, tall, k), bf16),
-            pltpu.SemaphoreType.DMA((steps,)),
-            pltpu.SemaphoreType.DMA((parts, steps)),
+            pltpu.SemaphoreType.DMA((turns,)),
+            pltpu.SemaphoreType.DMA((parts, turns)),
+            pltpu.SemaphoreType.DMA((4,)),
         ],
         compiler_params=params(60),
         cost_estimate=cost(4 * work * hidden, 6 * work),
@@ -301,11 +321,18 @@
     )(*lefts)
 
     span = GATHER * rows
+    gathers = devices // GATHER
+    if gathers == 1:
+        blocks = dict(in_specs=[vmem] * 2, out_specs=vmem)
+    else:
+        blocks = dict(
+            grid=(gathers,),
+            in_specs=[pl.BlockSpec((span * BLOCK, k), lambda s: (s, 0)), whole((BLOCK, mine, k))],
+            out_specs=pl.BlockSpec((hosts, tall, span), lambda s: (0, 0, s)),
+        )
     product = pl.pallas_call(
         product_kernel,
-        grid=(devices // GATHER,),
-        in_specs=[pl.BlockSpec((span * BLOCK, k), lambda s: (s, 0)), whole((BLOCK, mine, k))],
-        out_specs=pl.BlockSpec((hosts, tall, span), lambda s: (0, 0, s)),
+        **blocks,
         out_shape=bfloat(hosts, tall, devices * rows),
         scratch_shapes=[pltpu.VMEM((BLOCK, span, k), bf16), pltpu.VMEM((BLOCK, mine, span), bf16)],
         compiler_params=params(40),

time: 94.8 us -> 94.4 us (level)
  transfers between devices with their start and end apart: 16 -> 16, of which waited for: 8 -> 8; matrix products, arithmetic and copies ran while one was open for 0% -> 0% of each run, Pallas kernels for 4% -> 3%
where the time goes in v11:
time: 94.4 us; the launch traced here: 94.1 us
  waiting for transfers between devices  30.1 us (32%)
  starting transfers between devices  26.6 us (28%)
  blocking collectives  21.8 us (23%)
  Pallas kernels  12.7 us (13%)
  local copies, waits for them, and re-layouts  2.73 us (3%)
    ppermute x15, waiting for transfers between devices, send(): return lax.ppermute(values, everywhere, pairs)  30.1 us
    all_to_all x1, blocking collectives, shards(): product = lax.all_to_all(product, in_part, 0, 0, tiled=True)  21.8 us
    ppermute x15, starting transfers between devices, send(): return lax.ppermute(values, everywhere, pairs)  19.2 us
    all_to_all x1, starting transfers between devices, shards(): lax.all_to_all(right.reshape(devices, tall, k), everywhere, 0, 0, tiled=T...  7.3 us
    pallas_call x1, Pallas kernels, shards(): pl.pallas_call(right_kernel, in_specs=[anywhere] * 5, out_specs=anywhere,...  4.91 us
    pallas_call x1, Pallas kernels, shards(): pl.pallas_call(left_kernel, grid=(steps,), in_specs=[row_block, whole((1,...  2.73 us
    unnamed x26, local copies, waits for them, and re-layouts  2.73 us
    pallas_call x1, Pallas kernels, shards(): pl.pallas_call(product_kernel, **blocks, out_shape=bfloat(hosts, tall, de...  2.41 us
  transfers between devices with their start and end apart: 16, of which 8 were waited for; matrix products, arithmetic and copies ran while one was open for 0% of the time, Pallas kernels for 3%

profile of v11, /device:TPU:0, one launch (start us, length us, event | category | flops | bytes accessed | tf_op | source)
XLA Modules:
  0.0 94.1 jit_solution(1643249876333533249)
XLA Ops:
  0.0 4.9 %right_factor.1 = bf16[2,16,96,384]{3,2,1,0:T(8,128)(2,1)} custom-call(bf16[12,384,128]{2,1,0:T(8,128)(2,1)} %pair_ref.3, f32[1,128]{1,0:T(1,128)} %bitcast.12, f32[1,128]{1,0:T(1,128)} %bitcast.14, bf16[128,512]{1,0:T(8,128)(2,1)} %w_ref.4, f32[1,512]{1,0:T(1,128)} %bitcast.10), custom_call_target="tpu_custom_call" | custom-call | flops 301989888 | bytes 3538944 | tf_op jit(solution)/shard_map/right_factor/pallas_call | solution.py:253
  4.9 0.0 copy-start
  4.9 0.0 copy-start.6
  4.9 0.0 copy-start.7
  5.0 0.0 copy-start.8
  5.0 0.0 copy-start.9
  5.0 7.3 %all-to-all-start = ((bf16[32,96,384]{2,1,0:T(8,128)(2,1)}), bf16[32,96,384]{2,1,0:T(8,128)(2,1)S(1)}, u32[]{:S(2)}, u32[]{:S(2)}) async-start(bf16[32,96,384]{2,1,0:T(8,128)(2,1)} %bitcast.20), calls=%async_computation | async-start | bytes 4718592 | tf_op jit(solution)/shard_map/all_to_all | solution.py:273
  12.3 0.0 copy-start.3
  12.4 0.9 copy-done.3
  13.3 0.8 copy-done.5
  14.0 2.7 %left_factor.1 = (bf16[96,384]{1,0:T(8,128)(2,1)S(1)}, bf16[96,384]{1,0:T(8,128)(2,1)S(1)}, bf16[96,384]{1,0:T(8,128)(2,1)S(1)}, bf16[96,384]{1,0:T(8,128)(2,1)S...) custom-call(bf16[12,384,128]{2,1,0:T(8,128)(2,1)S(1)} %copy-done, ...), custom_call_target="tpu_custom_call" | custom-call | flops 301989888 | bytes 3538944 | tf_op jit(solution)/shard_map/left_factor/pallas_call | solution.py:279
  16.7 0.0 copy-start.1
  16.8 1.0 %copy-done.1 = bf16[12,384,128]{2,1,0:T(8,128)(2,1)} copy-done((bf16[12,384,128]{2,1,0:T(8,128)(2,1)}, bf16[12,384,128]{2,1,0:T(8,128)(2,1)S(1)}, u32[]{:S(2)}) %copy-start.1) | copy-done | bytes 1179672
  17.8 0.2 collective-permute-start
  18.0 1.7 %collective-permute-start.1 = (bf16[96,384]{1,0:T(8,128)(2,1)S(1)}, bf16[96,384]{1,0:T(8,128)(2,1)S(1)}, u32[]{:S(2)}, u32[]{:S(2)}) collective-permute-start(bf16[96,384]{1,0:T(8,128)(2,1)S(1)} %get-tuple-element.24), channel_id=1, source_target_pairs={{0,2},{1,3},{2,0},{3,1},{4,6},{5,7},{6,4},{7,5},{8,10},{9,11},{10,... | collective-permute-start | bytes 221192 | tf_op jit(solution)/shard_map/ppermute | solution.py:277
  19.7 1.7 %collective-permute-start.3 = (bf16[96,384]{1,0:T(8,128)(2,1)S(1)}, bf16[96,384]{1,0:T(8,128)(2,1)S(1)}, u32[]{:S(2)}, u32[]{:S(2)}) collective-permute-start(bf16[96,384]{1,0:T(8,128)(2,1)S(1)} %get-tuple-element.26), channel_id=1, source_target_pairs={{0,4},{1,5},{2,6},{3,7},{4,0},{5,1},{6,2},{7,3},{8,12},{9,13},{10,... | collective-permute-start | bytes 221192 | tf_op jit(solution)/shard_map/ppermute | solution.py:277
  21.4 0.1 collective-permute-start.4
  21.5 0.0 collective-permute-done.refs_1_
  21.5 2.6 %collective-permute-start.5 = (bf16[96,384]{1,0:T(8,128)(2,1)S(1)}, bf16[96,384]{1,0:T(8,128)(2,1)S(1)}, u32[]{:S(2)}, u32[]{:S(2)}) collective-permute-start(bf16[96,384]{1,0:T(8,128)(2,1)S(1)} %get-tuple-element.28), channel_id=1, source_target_pairs={{0,6},{1,7},{2,4},{3,5},{4,2},{5,3},{6,0},{7,1},{8,14},{9,15},{10,... | collective-permute-start | bytes 221192 | tf_op jit(solution)/shard_map/ppermute | solution.py:277
  24.1 7.8 %collective-permute-done.1.refs_2_ = bf16[96,384]{1,0:T(8,128)(2,1)S(1)} collective-permute-done((bf16[96,384]{1,0:T(8,128)(2,1)S(1)}, bf16[96,384]{1,0:T(8,128)(2,1)S(1)}, u32[]{:S(2)}, u32[]{:S(2)}) %collective-permute-start.1) | collective-permute-done | bytes 73760 | tf_op jit(solution)/shard_map/ppermute | solution.py:277
  31.8 0.6 collective-permute-start.6
  32.4 0.2 collective-permute-done.2.refs_3_
  32.7 0.3 collective-permute-start.7
  32.9 0.0 collective-permute-done.3.refs_4_
  32.9 2.3 %collective-permute-start.8 = (bf16[96,384]{1,0:T(8,128)(2,1)S(1)}, bf16[96,384]{1,0:T(8,128)(2,1)S(1)}, u32[]{:S(2)}, u32[]{:S(2)}) collective-permute-start(bf16[96,384]{1,0:T(8,128)(2,1)S(1)} %get-tuple-element.31), channel_id=1, source_target_pairs={{0,9},{1,8},{2,11},{3,10},{4,13},{5,12},{6,15},{7,14},{8,1},{9,0},... | collective-permute-start | bytes 221192 | tf_op jit(solution)/shard_map/ppermute | solution.py:277
  35.2 0.0 collective-permute-done.4.refs_5_
  35.2 3.3 %collective-permute-start.9 = (bf16[96,384]{1,0:T(8,128)(2,1)S(1)}, bf16[96,384]{1,0:T(8,128)(2,1)S(1)}, u32[]{:S(2)}, u32[]{:S(2)}) collective-permute-start(bf16[96,384]{1,0:T(8,128)(2,1)S(1)} %get-tuple-element.32), channel_id=1, source_target_pairs={{0,10},{1,11},{2,8},{3,9},{4,14},{5,15},{6,12},{7,13},{8,2},{9,3},... | collective-permute-start | bytes 221192 | tf_op jit(solution)/shard_map/ppermute | solution.py:277
  38.5 3.8 %collective-permute-done.5.refs_6_ = bf16[96,384]{1,0:T(8,128)(2,1)S(1)} collective-permute-done((bf16[96,384]{1,0:T(8,128)(2,1)S(1)}, bf16[96,384]{1,0:T(8,128)(2,1)S(1)}, u32[]{:S(2)}, u32[]{:S(2)}) %collective-permute-start.5) | collective-permute-done | bytes 73760 | tf_op jit(solution)/shard_map/ppermute | solution.py:277
  42.3 0.8 collective-permute-done.6.refs_7_
  43.1 0.0 collective-permute-start.11
  43.1 10.3 %collective-permute-done.7.refs_8_ = bf16[96,384]{1,0:T(8,128)(2,1)S(1)} collective-permute-done((bf16[96,384]{1,0:T(8,128)(2,1)S(1)}, bf16[96,384]{1,0:T(8,128)(2,1)S(1)}, u32[]{:S(2)}, u32[]{:S(2)}) %collective-permute-start.7) | collective-permute-done | bytes 73760 | tf_op jit(solution)/shard_map/ppermute | solution.py:277
  53.5 2.0 %collective-permute-start.12 = (bf16[96,384]{1,0:T(8,128)(2,1)S(1)}, bf16[96,384]{1,0:T(8,128)(2,1)S(1)}, u32[]{:S(2)}, u32[]{:S(2)}) collective-permute-start(bf16[96,384]{1,0:T(8,128)(2,1)S(1)} %get-tuple-element.35), channel_id=1, source_target_pairs={{0,13},{1,12},{2,15},{3,14},{4,9},{5,8},{6,11},{7,10},{8,5},{9,4},... | collective-permute-start | bytes 221192 | tf_op jit(solution)/shard_map/ppermute | solution.py:277
  55.5 2.8 %collective-permute-start.13 = (bf16[96,384]{1,0:T(8,128)(2,1)S(1)}, bf16[96,384]{1,0:T(8,128)(2,1)S(1)}, u32[]{:S(2)}, u32[]{:S(2)}) collective-permute-start(bf16[96,384]{1,0:T(8,128)(2,1)S(1)} %get-tuple-element.36), channel_id=1, source_target_pairs={{0,14},{1,15},{2,12},{3,13},{4,10},{5,11},{6,8},{7,9},{8,6},{9,7},... | collective-permute-start | bytes 221192 | tf_op jit(solution)/shard_map/ppermute | solution.py:277
  58.3 0.0 collective-permute-done.9.refs_10_
  58.3 1.7 %collective-permute-start.14 = (bf16[96,384]{1,0:T(8,128)(2,1)S(1)}, bf16[96,384]{1,0:T(8,128)(2,1)S(1)}, u32[]{:S(2)}, u32[]{:S(2)}) collective-permute-start(bf16[96,384]{1,0:T(8,128)(2,1)S(1)} %get-tuple-element.37), channel_id=1, source_target_pairs={{0,15},{1,14},{2,13},{3,12},{4,11},{5,10},{6,9},{7,8},{8,7},{9,6},... | collective-permute-start | bytes 221192 | tf_op jit(solution)/shard_map/ppermute | solution.py:277
  60.0 1.4 %collective-permute-done.12.refs_13_ = bf16[96,384]{1,0:T(8,128)(2,1)S(1)} collective-permute-done((bf16[96,384]{1,0:T(8,128)(2,1)S(1)}, bf16[96,384]{1,0:T(8,128)(2,1)S(1)}, u32[]{:S(2)}, u32[]{:S(2)}) %collective-permute-start.12) | collective-permute-done | bytes 73760 | tf_op jit(solution)/shard_map/ppermute | solution.py:277
  61.4 3.0 %collective-permute-done.13.refs_14_ = bf16[96,384]{1,0:T(8,128)(2,1)S(1)} collective-permute-done((bf16[96,384]{1,0:T(8,128)(2,1)S(1)}, bf16[96,384]{1,0:T(8,128)(2,1)S(1)}, u32[]{:S(2)}, u32[]{:S(2)}) %collective-permute-start.13) | collective-permute-done | bytes 73760 | tf_op jit(solution)/shard_map/ppermute | solution.py:277
  64.4 2.7 %collective-permute-done.14.refs_15_ = bf16[96,384]{1,0:T(8,128)(2,1)S(1)} collective-permute-done((bf16[96,384]{1,0:T(8,128)(2,1)S(1)}, bf16[96,384]{1,0:T(8,128)(2,1)S(1)}, u32[]{:S(2)}, u32[]{:S(2)}) %collective-permute-start.14) | collective-permute-done | bytes 73760 | tf_op jit(solution)/shard_map/ppermute | solution.py:277
  67.1 0.6 gather_left.1.left
  67.7 0.0 all-to-all-done
  67.7 2.4 %products.1 = bf16[16,96,384]{2,1,0:T(8,128)(2,1)S(1)} custom-call(bf16[3072,384]{1,0:T(8,128)(2,1)S(1)} %bitcast.9, bf16[8,192,384]{2,1,0:T(8,128)(2,1)S(1)} %gather_left.1.left), custom_call_target="tpu_custom_call" | custom-call | flops 226492416 | bytes 3538944 | tf_op jit(solution)/shard_map/products/pallas_call | solution.py:333
  70.1 0.0 copy-start.2
  70.1 0.0 copy-start.4
  70.1 0.0 copy-start.10
  70.1 0.0 copy-start.11
  70.1 0.0 copy-start.12
  70.1 21.8 %all_to_all.10.x_ref = bf16[16,96,384]{2,1,0:T(8,128)(2,1)S(1)} all-to-all(bf16[16,96,384]{2,1,0:T(8,128)(2,1)S(1)} %products.1), channel_id=1, replica_groups=mesh['groups'=1,'part'=2,'chan'=8,'quarter'=2] {'chan','quarter'}, dimensions={0} | all-to-all | bytes 2359296 | tf_op jit(solution)/shard_map/all_to_all | solution.py:342
  92.0 2.1 %update.1 = bf16[12,384,128]{2,1,0:T(8,128)(2,1)} custom-call(bf16[16,96,384]{2,1,0:T(8,128)(2,1)S(1)} %all_to_all.10.x_ref, bf16[12,384,128]{2,1,0:T(8,128)(2,1)S(1)} %copy-done.2, f32[1,128]{1,0:T(1,128)S(1)} %bitcast.17, f32[1,128]{1,0:T(1,128)S(1)} %bitcast.18, bf16[128,128]{1,0:T(8,128)(2,1)S(1)} %copy-done.4, f32[1,128]{1,0:T(1,128)S(1)} %bitcast.19), custom_call_target="tpu_custom_call" | custom-call | flops 150994944 | bytes 3538944 | tf_op jit(solution)/shard_map/update/pallas_call | solution.py:344
  (16 shorter events, 0.0 us)
Async XLA Ops:
  4.9 7.4 %copy-start = (bf16[12,384,128]{2,1,0:T(8,128)(2,1)S(1)}, bf16[12,384,128]{2,1,0:T(8,128)(2,1)}, u32[]{:S(2)}) copy-start(bf16[12,384,128]{2,1,0:T(8,128)(2,1)} %pair_ref.3) | copy-start | bytes 3538948
  4.9 7.4 %copy-start.6 = (f32[512]{0:T(512)S(1)}, f32[512]{0:T(512)}, u32[]{:S(2)}) copy-start(f32[512]{0:T(512)} %param.15) | copy-start | bytes 6148
  4.9 7.4 %copy-start.7 = (f32[128]{0:T(128)S(1)}, f32[128]{0:T(128)}, u32[]{:S(2)}) copy-start(f32[128]{0:T(128)} %param.12) | copy-start | bytes 1540
  5.0 7.4 %copy-start.8 = (f32[128]{0:T(128)S(1)}, f32[128]{0:T(128)}, u32[]{:S(2)}) copy-start(f32[128]{0:T(128)} %param.13) | copy-start | bytes 1540
  5.0 7.4 %copy-start.9 = (f32[128]{0:T(128)S(1)}, f32[128]{0:T(128)}, u32[]{:S(2)}) copy-start(f32[128]{0:T(128)} %param.17) | copy-start | bytes 1540
  5.0 62.7 %all-to-all-start = ((bf16[32,96,384]{2,1,0:T(8,128)(2,1)}), bf16[32,96,384]{2,1,0:T(8,128)(2,1)S(1)}, u32[]{:S(2)}, u32[]{:S(2)}) async-start(bf16[32,96,384]{2,1,0:T(8,128)(2,1)} %bitcast.20), calls=%async_computation | async-start | bytes 4718592 | tf_op jit(solution)/shard_map/all_to_all | solution.py:273
  12.3 0.9 copy-start.3
  13.2 0.8 copy-start.5
  16.7 1.0 %copy-start.1 = (bf16[12,384,128]{2,1,0:T(8,128)(2,1)}, bf16[12,384,128]{2,1,0:T(8,128)(2,1)S(1)}, u32[]{:S(2)}) copy-start(bf16[12,384,128]{2,1,0:T(8,128)(2,1)S(1)} %get-tuple-element.38.gate_ref) | copy-start | bytes 3538948
  17.8 3.7 %collective-permute-start = (bf16[96,384]{1,0:T(8,128)(2,1)S(1)}, bf16[96,384]{1,0:T(8,128)(2,1)S(1)}, u32[]{:S(2)}, u32[]{:S(2)}) collective-permute-start(bf16[96,384]{1,0:T(8,128)(2,1)S(1)} %get-tuple-element.23), channel_id=1, source_target_pairs={{0,1},{1,0},{2,3},{3,2},{4,5},{5,4},{6,7},{7,6},{8,9},{9,8},{10,11... | collective-permute-start | bytes 221192 | tf_op jit(solution)/shard_map/ppermute | solution.py:277
  18.0 13.8 %collective-permute-start.1 = (bf16[96,384]{1,0:T(8,128)(2,1)S(1)}, bf16[96,384]{1,0:T(8,128)(2,1)S(1)}, u32[]{:S(2)}, u32[]{:S(2)}) collective-permute-start(bf16[96,384]{1,0:T(8,128)(2,1)S(1)} %get-tuple-element.24), channel_id=1, source_target_pairs={{0,2},{1,3},{2,0},{3,1},{4,6},{5,7},{6,4},{7,5},{8,10},{9,11},{10,... | collective-permute-start | bytes 221192 | tf_op jit(solution)/shard_map/ppermute | solution.py:277
  19.7 13.0 %collective-permute-start.2 = (bf16[96,384]{1,0:T(8,128)(2,1)S(1)}, bf16[96,384]{1,0:T(8,128)(2,1)S(1)}, u32[]{:S(2)}, u32[]{:S(2)}) collective-permute-start(bf16[96,384]{1,0:T(8,128)(2,1)S(1)} %get-tuple-element.25), channel_id=1, source_target_pairs={{0,3},{1,2},{2,1},{3,0},{4,7},{5,6},{6,5},{7,4},{8,11},{9,10},{10,... | collective-permute-start | bytes 221192 | tf_op jit(solution)/shard_map/ppermute | solution.py:277
  19.7 13.2 %collective-permute-start.3 = (bf16[96,384]{1,0:T(8,128)(2,1)S(1)}, bf16[96,384]{1,0:T(8,128)(2,1)S(1)}, u32[]{:S(2)}, u32[]{:S(2)}) collective-permute-start(bf16[96,384]{1,0:T(8,128)(2,1)S(1)} %get-tuple-element.26), channel_id=1, source_target_pairs={{0,4},{1,5},{2,6},{3,7},{4,0},{5,1},{6,2},{7,3},{8,12},{9,13},{10,... | collective-permute-start | bytes 221192 | tf_op jit(solution)/shard_map/ppermute | solution.py:277
  21.4 13.8 %collective-permute-start.4 = (bf16[96,384]{1,0:T(8,128)(2,1)S(1)}, bf16[96,384]{1,0:T(8,128)(2,1)S(1)}, u32[]{:S(2)}, u32[]{:S(2)}) collective-permute-start(bf16[96,384]{1,0:T(8,128)(2,1)S(1)} %get-tuple-element.27), channel_id=1, source_target_pairs={{0,5},{1,4},{2,7},{3,6},{4,1},{5,0},{6,3},{7,2},{8,13},{9,12},{10,... | collective-permute-start | bytes 221192 | tf_op jit(solution)/shard_map/ppermute | solution.py:277
  21.5 20.8 %collective-permute-start.5 = (bf16[96,384]{1,0:T(8,128)(2,1)S(1)}, bf16[96,384]{1,0:T(8,128)(2,1)S(1)}, u32[]{:S(2)}, u32[]{:S(2)}) collective-permute-start(bf16[96,384]{1,0:T(8,128)(2,1)S(1)} %get-tuple-element.28), channel_id=1, source_target_pairs={{0,6},{1,7},{2,4},{3,5},{4,2},{5,3},{6,0},{7,1},{8,14},{9,15},{10,... | collective-permute-start | bytes 221192 | tf_op jit(solution)/shard_map/ppermute | solution.py:277
  31.8 11.3 %collective-permute-start.6 = (bf16[96,384]{1,0:T(8,128)(2,1)S(1)}, bf16[96,384]{1,0:T(8,128)(2,1)S(1)}, u32[]{:S(2)}, u32[]{:S(2)}) collective-permute-start(bf16[96,384]{1,0:T(8,128)(2,1)S(1)} %get-tuple-element.29), channel_id=1, source_target_pairs={{0,7},{1,6},{2,5},{3,4},{4,3},{5,2},{6,1},{7,0},{8,15},{9,14},{10,... | collective-permute-start | bytes 221192 | tf_op jit(solution)/shard_map/ppermute | solution.py:277
  32.7 20.8 %collective-permute-start.7 = (bf16[96,384]{1,0:T(8,128)(2,1)S(1)}, bf16[96,384]{1,0:T(8,128)(2,1)S(1)}, u32[]{:S(2)}, u32[]{:S(2)}) collective-permute-start(bf16[96,384]{1,0:T(8,128)(2,1)S(1)} %get-tuple-element.30), channel_id=1, source_target_pairs={{0,8},{1,9},{2,10},{3,11},{4,12},{5,13},{6,14},{7,15},{8,0},{9,1},... | collective-permute-start | bytes 221192 | tf_op jit(solution)/shard_map/ppermute | solution.py:277
  32.9 22.6 %collective-permute-start.8 = (bf16[96,384]{1,0:T(8,128)(2,1)S(1)}, bf16[96,384]{1,0:T(8,128)(2,1)S(1)}, u32[]{:S(2)}, u32[]{:S(2)}) collective-permute-start(bf16[96,384]{1,0:T(8,128)(2,1)S(1)} %get-tuple-element.31), channel_id=1, source_target_pairs={{0,9},{1,8},{2,11},{3,10},{4,13},{5,12},{6,15},{7,14},{8,1},{9,0},... | collective-permute-start | bytes 221192 | tf_op jit(solution)/shard_map/ppermute | solution.py:277
  35.2 23.1 %collective-permute-start.9 = (bf16[96,384]{1,0:T(8,128)(2,1)S(1)}, bf16[96,384]{1,0:T(8,128)(2,1)S(1)}, u32[]{:S(2)}, u32[]{:S(2)}) collective-permute-start(bf16[96,384]{1,0:T(8,128)(2,1)S(1)} %get-tuple-element.32), channel_id=1, source_target_pairs={{0,10},{1,11},{2,8},{3,9},{4,14},{5,15},{6,12},{7,13},{8,2},{9,3},... | collective-permute-start | bytes 221192 | tf_op jit(solution)/shard_map/ppermute | solution.py:277
  42.3 17.7 %collective-permute-start.10 = (bf16[96,384]{1,0:T(8,128)(2,1)S(1)}, bf16[96,384]{1,0:T(8,128)(2,1)S(1)}, u32[]{:S(2)}, u32[]{:S(2)}) collective-permute-start(bf16[96,384]{1,0:T(8,128)(2,1)S(1)} %get-tuple-element.33), channel_id=1, source_target_pairs={{0,11},{1,10},{2,9},{3,8},{4,15},{5,14},{6,13},{7,12},{8,3},{9,2},... | collective-permute-start | bytes 221192 | tf_op jit(solution)/shard_map/ppermute | solution.py:277
  43.1 16.9 %collective-permute-start.11 = (bf16[96,384]{1,0:T(8,128)(2,1)S(1)}, bf16[96,384]{1,0:T(8,128)(2,1)S(1)}, u32[]{:S(2)}, u32[]{:S(2)}) collective-permute-start(bf16[96,384]{1,0:T(8,128)(2,1)S(1)} %get-tuple-element.34), channel_id=1, source_target_pairs={{0,12},{1,13},{2,14},{3,15},{4,8},{5,9},{6,10},{7,11},{8,4},{9,5},... | collective-permute-start | bytes 221192 | tf_op jit(solution)/shard_map/ppermute | solution.py:277
  53.5 7.9 %collective-permute-start.12 = (bf16[96,384]{1,0:T(8,128)(2,1)S(1)}, bf16[96,384]{1,0:T(8,128)(2,1)S(1)}, u32[]{:S(2)}, u32[]{:S(2)}) collective-permute-start(bf16[96,384]{1,0:T(8,128)(2,1)S(1)} %get-tuple-element.35), channel_id=1, source_target_pairs={{0,13},{1,12},{2,15},{3,14},{4,9},{5,8},{6,11},{7,10},{8,5},{9,4},... | collective-permute-start | bytes 221192 | tf_op jit(solution)/shard_map/ppermute | solution.py:277
  55.5 8.9 %collective-permute-start.13 = (bf16[96,384]{1,0:T(8,128)(2,1)S(1)}, bf16[96,384]{1,0:T(8,128)(2,1)S(1)}, u32[]{:S(2)}, u32[]{:S(2)}) collective-permute-start(bf16[96,384]{1,0:T(8,128)(2,1)S(1)} %get-tuple-element.36), channel_id=1, source_target_pairs={{0,14},{1,15},{2,12},{3,13},{4,10},{5,11},{6,8},{7,9},{8,6},{9,7},... | collective-permute-start | bytes 221192 | tf_op jit(solution)/shard_map/ppermute | solution.py:277
  58.3 8.8 %collective-permute-start.14 = (bf16[96,384]{1,0:T(8,128)(2,1)S(1)}, bf16[96,384]{1,0:T(8,128)(2,1)S(1)}, u32[]{:S(2)}, u32[]{:S(2)}) collective-permute-start(bf16[96,384]{1,0:T(8,128)(2,1)S(1)} %get-tuple-element.37), channel_id=1, source_target_pairs={{0,15},{1,14},{2,13},{3,12},{4,11},{5,10},{6,9},{7,8},{8,7},{9,6},... | collective-permute-start | bytes 221192 | tf_op jit(solution)/shard_map/ppermute | solution.py:277
  70.1 21.9 %copy-start.2 = (bf16[12,384,128]{2,1,0:T(8,128)(2,1)S(1)}, bf16[12,384,128]{2,1,0:T(8,128)(2,1)}, u32[]{:S(2)}) copy-start(bf16[12,384,128]{2,1,0:T(8,128)(2,1)} %copy-done.1) | copy-start | bytes 3538948
  70.1 21.8 %copy-start.4 = (bf16[128,128]{1,0:T(8,128)(2,1)S(1)}, bf16[128,128]{1,0:T(8,128)(2,1)}, u32[]{:S(2)}) copy-start(bf16[128,128]{1,0:T(8,128)(2,1)} %w_ref.5) | copy-start | bytes 98308
  70.1 21.8 %copy-start.10 = (f32[128]{0:T(128)S(1)}, f32[128]{0:T(128)}, u32[]{:S(2)}) copy-start(f32[128]{0:T(128)} %param.18) | copy-start | bytes 1540
  70.1 21.8 %copy-start.11 = (f32[128]{0:T(128)S(1)}, f32[128]{0:T(128)}, u32[]{:S(2)}) copy-start(f32[128]{0:T(128)} %param.19) | copy-start | bytes 1540
  70.1 21.8 %copy-start.12 = (f32[128]{0:T(128)S(1)}, f32[128]{0:T(128)}, u32[]{:S(2)}) copy-start(f32[128]{0:T(128)} %param.21) | copy-start | bytes 1540

commit v12 on v11

--- a/solution.py
+++ b/solution.py
@@ -186,31 +186,51 @@
     regroup(slices(refs[:-1]), refs[-1], shuffle(BLOCK, SIZE))
 
 
-def product_kernel(right_ref, left, out_ref, right, held):
-    rows = left.shape[1] // out_ref.shape[0]
-    host = lax.axis_index(("chan", "quarter"))
+def sending_order(hosts):
+    far, near = list(range(hosts // 2, hosts)), list(range(1, hosts // 2))
+    order = [0]
+    while far:
+        order += far[:2] + near[:1]
+        far, near = far[2:], near[1:]
+    return order + near
+
+
+def product_kernel(right_ref, left, *refs):
+    outs = refs[:-2]
+    right, held = refs[-2:]
+    rows = left.shape[1] // len(outs)
 
     def store(i, values):
         to, at = divmod(i, rows)
-        out_ref[host ^ to, at * BLOCK : (at + STEP) * BLOCK, :] = values
+        outs[to][at * BLOCK : (at + STEP) * BLOCK, :] = values
 
     multiply(left, right_ref, right, held, store)
 
 
-def final_kernel(x_ref, gate_ref, g_ref, s_ref, w_ref, b_ref, out_ref, made, leave):
-    hosts, _, j = x_ref.shape
-    rows = gate_ref.shape[0]
-    width = hosts * BLOCK
-    gain, shift = widen(column(g_ref[...]), j), widen(column(s_ref[...]), j)
+def final_kernel(hosts, *refs):
+    products = refs[:hosts]
+    gate_ref, g_ref, s_ref, w_ref, b_ref, out_ref, made, plain, mixed, leave = refs[hosts:]
+    j = products[0].shape[1]
+    rows, _, width = gate_ref.shape
+    plain[0] = column(g_ref[...])
+    plain[1] = column(s_ref[...])
+    plain[2] = w_ref[...].astype(f32)
+    host = lax.axis_index(("chan", "quarter"))
+    for m, b in enumerate(sending_order(hosts)):
+        source = pl.ds(pl.multiple_of((host ^ b) * BLOCK, BLOCK), BLOCK)
+        for n in range(3):
+            mixed[n, m * BLOCK : (m + 1) * BLOCK] = plain[n, source]
+    gain, shift = widen(mixed[0], j), widen(mixed[1], j)
+    weight = mixed[2].astype(bf16)
     stores = []
     for r in range(0, rows, 2):
-        pair = x_ref[:, r * BLOCK : (r + 2) * BLOCK].astype(f32)
+        pair = [ref[r * BLOCK : (r + 2) * BLOCK, :].astype(f32) for ref in products]
         for n in range(2):
-            x = pair[:, n * BLOCK : (n + 1) * BLOCK].reshape(width, j)
+            x = jnp.concatenate([one[n * BLOCK : (n + 1) * BLOCK] for one in pair], axis=0)
             centered = x - jnp.mean(x, axis=0, keepdims=True)
             variance = jnp.mean(centered * centered, axis=0, keepdims=True)
             normed = centered * lax.rsqrt(variance + epsilon) * gain + shift
-            outward = dot(normed.astype(bf16).T, w_ref[...]) + b_ref[...]
+            outward = dot(normed.astype(bf16).T, weight) + b_ref[...]
             made[r + n] = (gate_ref[r + n].astype(f32) * outward).astype(bf16)
         at = pl.ds(r, 2)
         stores.append(pltpu.make_async_copy(made.at[at], out_ref.at[at], leave.at[r // 2]))
@@ -323,34 +343,39 @@
     span = GATHER * rows
     gathers = devices // GATHER
     if gathers == 1:
-        blocks = dict(in_specs=[vmem] * 2, out_specs=vmem)
+        blocks = dict(in_specs=[vmem] * 2, out_specs=[vmem] * hosts)
     else:
         blocks = dict(
             grid=(gathers,),
             in_specs=[pl.BlockSpec((span * BLOCK, k), lambda s: (s, 0)), whole((BLOCK, mine, k))],
-            out_specs=pl.BlockSpec((hosts, tall, span), lambda s: (0, 0, s)),
+            out_specs=[pl.BlockSpec((tall, span), lambda s: (0, s))] * hosts,
         )
-    product = pl.pallas_call(
+    products = pl.pallas_call(
         product_kernel,
         **blocks,
-        out_shape=bfloat(hosts, tall, devices * rows),
+        out_shape=[bfloat(tall, devices * rows)] * hosts,
         scratch_shapes=[pltpu.VMEM((BLOCK, span, k), bf16), pltpu.VMEM((BLOCK, mine, span), bf16)],
         compiler_params=params(40),
         cost_estimate=cost(2 * BLOCK * mine * mine * k, 6 * BLOCK * mine * k),
         name="products",
     )(right.reshape(devices * tall, k), left)
-    product = lax.all_to_all(product, in_part, 0, 0, tiled=True)
+    products = [send(products[b], b) if b else products[b] for b in sending_order(hosts)]
 
     return pl.pallas_call(
-        final_kernel,
-        in_specs=[vmem] * 6,
+        functools.partial(final_kernel, hosts),
+        in_specs=[vmem] * (hosts + 5),
         out_specs=anywhere,
         out_shape=bfloat(*pair.shape),
-        scratch_shapes=[pltpu.VMEM(pair.shape, bf16), pltpu.SemaphoreType.DMA((rows // 2,))],
+        scratch_shapes=[
+            pltpu.VMEM(pair.shape, bf16),
+            pltpu.VMEM((3, hidden, LANES), f32),
+            pltpu.VMEM((3, hidden, LANES), f32),
+            pltpu.SemaphoreType.DMA((rows // 2,)),
+        ],
         compiler_params=params(),
         cost_estimate=cost(2 * work * width, 6 * work),
         name="update",
-    )(product, gate, row(center_gain), row(center_shift), out_weight, row(out_bias))
+    )(*products, gate, row(center_gain), row(center_shift), out_weight, row(out_bias))
 
 
 def solution(mesh):

time: 94.4 us -> 97.5 us (1.033)
  blocking collectives: 21.8 us -> 0 us
  starting transfers between devices: 26.6 us -> 43.9 us
  waiting for transfers between devices: 30.1 us -> 37.6 us
    all_to_all x1 -> x0, blocking collectives: 21.8 us -> none  [shards(): product = lax.all_to_all(product, in_part, 0, 0, tiled=True)]
    ppermute x15 -> x30, starting transfers between devices: 19.2 us -> 36.6 us  [send(): return lax.ppermute(values, everywhere, pairs)]
    ppermute x15 -> x30, waiting for transfers between devices: 30.1 us -> 37.6 us  [send(): return lax.ppermute(values, everywhere, pairs)]
  transfers between devices with their start and end apart: 16 -> 31, of which waited for: 8 -> 13; matrix products, arithmetic and copies ran while one was open for 0% -> 0% of each run, Pallas kernels for 3% -> 3%
where the time goes in v12:
time: 97.5 us; the launch traced here: 97.3 us
  starting transfers between devices  43.9 us (45%)
  waiting for transfers between devices  37.6 us (39%)
  Pallas kernels  12.8 us (13%)
  local copies, waits for them, and re-layouts  2.73 us (3%)
    ppermute x30, waiting for transfers between devices, send(): return lax.ppermute(values, everywhere, pairs)  37.6 us
    ppermute x30, starting transfers between devices, send(): return lax.ppermute(values, everywhere, pairs)  36.6 us
    all_to_all x1, starting transfers between devices, shards(): lax.all_to_all(right.reshape(devices, tall, k), everywhere, 0, 0, tiled=T...  7.3 us
    pallas_call x1, Pallas kernels, shards(): pl.pallas_call(right_kernel, in_specs=[anywhere] * 5, out_specs=anywhere,...  4.87 us
    pallas_call x1, Pallas kernels, shards(): pl.pallas_call(left_kernel, grid=(steps,), in_specs=[row_block, whole((1,...  2.73 us
    unnamed x26, local copies, waits for them, and re-layouts  2.73 us
    pallas_call x1, Pallas kernels, shards(): pl.pallas_call(product_kernel, **blocks, out_shape=[bfloat(tall, devices...  2.41 us
    pallas_call x1, Pallas kernels, shards(): pl.pallas_call(functools.partial(final_kernel, hosts), in_specs=[vmem] *...  2.22 us
  transfers between devices with their start and end apart: 31, of which 13 were waited for; matrix products, arithmetic and copies ran while one was open for 0% of the time, Pallas kernels for 3%

profile of v12, /device:TPU:0, one launch (start us, length us, event | category | flops | bytes accessed | tf_op | source)
XLA Modules:
  0.0 97.3 jit_solution(18350026888517365473)
XLA Ops:
  0.0 4.9 %right_factor.1 = bf16[2,16,96,384]{3,2,1,0:T(8,128)(2,1)} custom-call(bf16[12,384,128]{2,1,0:T(8,128)(2,1)} %pair_ref.3, f32[1,128]{1,0:T(1,128)} %bitcast.12, f32[1,128]{1,0:T(1,128)} %bitcast.14, bf16[128,512]{1,0:T(8,128)(2,1)} %w_ref.3, f32[1,512]{1,0:T(1,128)} %bitcast.10), custom_call_target="tpu_custom_call" | custom-call | flops 301989888 | bytes 3538944 | tf_op jit(solution)/shard_map/right_factor/pallas_call | solution.py:273
  4.9 7.3 %all-to-all-start = ((bf16[32,96,384]{2,1,0:T(8,128)(2,1)}), bf16[32,96,384]{2,1,0:T(8,128)(2,1)S(1)}, u32[]{:S(2)}, u32[]{:S(2)}) async-start(bf16[32,96,384]{2,1,0:T(8,128)(2,1)} %bitcast.20), calls=%async_computation | async-start | bytes 4718592 | tf_op jit(solution)/shard_map/all_to_all | solution.py:293
  12.3 0.9 copy-done.3
  13.2 0.8 copy-done.5
  14.0 2.7 %left_factor.1 = (bf16[96,384]{1,0:T(8,128)(2,1)S(1)}, bf16[96,384]{1,0:T(8,128)(2,1)S(1)}, bf16[96,384]{1,0:T(8,128)(2,1)S(1)}, bf16[96,384]{1,0:T(8,128)(2,1)S...) custom-call(bf16[12,384,128]{2,1,0:T(8,128)(2,1)S(1)} %copy-done, ...), custom_call_target="tpu_custom_call" | custom-call | flops 301989888 | bytes 3538944 | tf_op jit(solution)/shard_map/left_factor/pallas_call | solution.py:299
  16.7 1.0 %copy-done.1 = bf16[12,384,128]{2,1,0:T(8,128)(2,1)} copy-done((bf16[12,384,128]{2,1,0:T(8,128)(2,1)}, bf16[12,384,128]{2,1,0:T(8,128)(2,1)S(1)}, u32[]{:S(2)}) %copy-start.1) | copy-done | bytes 1179672
  17.7 0.2 collective-permute-start
  18.0 1.7 %collective-permute-start.1 = (bf16[96,384]{1,0:T(8,128)(2,1)S(1)}, bf16[96,384]{1,0:T(8,128)(2,1)S(1)}, u32[]{:S(2)}, u32[]{:S(2)}) collective-permute-start(bf16[96,384]{1,0:T(8,128)(2,1)S(1)} %get-tuple-element.40), channel_id=1, source_target_pairs={{0,2},{1,3},{2,0},{3,1},{4,6},{5,7},{6,4},{7,5},{8,10},{9,11},{10,... | collective-permute-start | bytes 221192 | tf_op jit(solution)/shard_map/ppermute | solution.py:297
  19.7 1.7 %collective-permute-start.3 = (bf16[96,384]{1,0:T(8,128)(2,1)S(1)}, bf16[96,384]{1,0:T(8,128)(2,1)S(1)}, u32[]{:S(2)}, u32[]{:S(2)}) collective-permute-start(bf16[96,384]{1,0:T(8,128)(2,1)S(1)} %get-tuple-element.42), channel_id=1, source_target_pairs={{0,4},{1,5},{2,6},{3,7},{4,0},{5,1},{6,2},{7,3},{8,12},{9,13},{10,... | collective-permute-start | bytes 221192 | tf_op jit(solution)/shard_map/ppermute | solution.py:297
  21.3 0.1 collective-permute-start.4
  21.5 2.6 %collective-permute-start.5 = (bf16[96,384]{1,0:T(8,128)(2,1)S(1)}, bf16[96,384]{1,0:T(8,128)(2,1)S(1)}, u32[]{:S(2)}, u32[]{:S(2)}) collective-permute-start(bf16[96,384]{1,0:T(8,128)(2,1)S(1)} %get-tuple-element.44), channel_id=1, source_target_pairs={{0,6},{1,7},{2,4},{3,5},{4,2},{5,3},{6,0},{7,1},{8,14},{9,15},{10,... | collective-permute-start | bytes 221192 | tf_op jit(solution)/shard_map/ppermute | solution.py:297
  24.0 7.8 %collective-permute-done.1.refs_2_ = bf16[96,384]{1,0:T(8,128)(2,1)S(1)} collective-permute-done((bf16[96,384]{1,0:T(8,128)(2,1)S(1)}, bf16[96,384]{1,0:T(8,128)(2,1)S(1)}, u32[]{:S(2)}, u32[]{:S(2)}) %collective-permute-start.1) | collective-permute-done | bytes 73760 | tf_op jit(solution)/shard_map/ppermute | solution.py:297
  31.8 0.6 collective-permute-start.6
  32.4 0.2 collective-permute-done.2.refs_3_
  32.6 0.3 collective-permute-start.7
  32.9 2.3 %collective-permute-start.8 = (bf16[96,384]{1,0:T(8,128)(2,1)S(1)}, bf16[96,384]{1,0:T(8,128)(2,1)S(1)}, u32[]{:S(2)}, u32[]{:S(2)}) collective-permute-start(bf16[96,384]{1,0:T(8,128)(2,1)S(1)} %get-tuple-element.47), channel_id=1, source_target_pairs={{0,9},{1,8},{2,11},{3,10},{4,13},{5,12},{6,15},{7,14},{8,1},{9,0},... | collective-permute-start | bytes 221192 | tf_op jit(solution)/shard_map/ppermute | solution.py:297
  35.2 3.3 %collective-permute-start.9 = (bf16[96,384]{1,0:T(8,128)(2,1)S(1)}, bf16[96,384]{1,0:T(8,128)(2,1)S(1)}, u32[]{:S(2)}, u32[]{:S(2)}) collective-permute-start(bf16[96,384]{1,0:T(8,128)(2,1)S(1)} %get-tuple-element.48), channel_id=1, source_target_pairs={{0,10},{1,11},{2,8},{3,9},{4,14},{5,15},{6,12},{7,13},{8,2},{9,3},... | collective-permute-start | bytes 221192 | tf_op jit(solution)/shard_map/ppermute | solution.py:297
  38.4 3.8 %collective-permute-done.5.refs_6_ = bf16[96,384]{1,0:T(8,128)(2,1)S(1)} collective-permute-done((bf16[96,384]{1,0:T(8,128)(2,1)S(1)}, bf16[96,384]{1,0:T(8,128)(2,1)S(1)}, u32[]{:S(2)}, u32[]{:S(2)}) %collective-permute-start.5) | collective-permute-done | bytes 73760 | tf_op jit(solution)/shard_map/ppermute | solution.py:297
  42.3 0.8 collective-permute-done.6.refs_7_
  43.1 10.3 %collective-permute-done.7.refs_8_ = bf16[96,384]{1,0:T(8,128)(2,1)S(1)} collective-permute-done((bf16[96,384]{1,0:T(8,128)(2,1)S(1)}, bf16[96,384]{1,0:T(8,128)(2,1)S(1)}, u32[]{:S(2)}, u32[]{:S(2)}) %collective-permute-start.7) | collective-permute-done | bytes 73760 | tf_op jit(solution)/shard_map/ppermute | solution.py:297
  53.4 2.0 %collective-permute-start.12 = (bf16[96,384]{1,0:T(8,128)(2,1)S(1)}, bf16[96,384]{1,0:T(8,128)(2,1)S(1)}, u32[]{:S(2)}, u32[]{:S(2)}) collective-permute-start(bf16[96,384]{1,0:T(8,128)(2,1)S(1)} %get-tuple-element.51), channel_id=1, source_target_pairs={{0,13},{1,12},{2,15},{3,14},{4,9},{5,8},{6,11},{7,10},{8,5},{9,4},... | collective-permute-start | bytes 221192 | tf_op jit(solution)/shard_map/ppermute | solution.py:297
  55.5 2.8 %collective-permute-start.13 = (bf16[96,384]{1,0:T(8,128)(2,1)S(1)}, bf16[96,384]{1,0:T(8,128)(2,1)S(1)}, u32[]{:S(2)}, u32[]{:S(2)}) collective-permute-start(bf16[96,384]{1,0:T(8,128)(2,1)S(1)} %get-tuple-element.52), channel_id=1, source_target_pairs={{0,14},{1,15},{2,12},{3,13},{4,10},{5,11},{6,8},{7,9},{8,6},{9,7},... | collective-permute-start | bytes 221192 | tf_op jit(solution)/shard_map/ppermute | solution.py:297
  58.3 1.7 %collective-permute-start.14 = (bf16[96,384]{1,0:T(8,128)(2,1)S(1)}, bf16[96,384]{1,0:T(8,128)(2,1)S(1)}, u32[]{:S(2)}, u32[]{:S(2)}) collective-permute-start(bf16[96,384]{1,0:T(8,128)(2,1)S(1)} %get-tuple-element.53), channel_id=1, source_target_pairs={{0,15},{1,14},{2,13},{3,12},{4,11},{5,10},{6,9},{7,8},{8,7},{9,6},... | collective-permute-start | bytes 221192 | tf_op jit(solution)/shard_map/ppermute | solution.py:297
  60.0 1.4 %collective-permute-done.12.refs_13_ = bf16[96,384]{1,0:T(8,128)(2,1)S(1)} collective-permute-done((bf16[96,384]{1,0:T(8,128)(2,1)S(1)}, bf16[96,384]{1,0:T(8,128)(2,1)S(1)}, u32[]{:S(2)}, u32[]{:S(2)}) %collective-permute-start.12) | collective-permute-done | bytes 73760 | tf_op jit(solution)/shard_map/ppermute | solution.py:297
  61.3 3.0 %collective-permute-done.13.refs_14_ = bf16[96,384]{1,0:T(8,128)(2,1)S(1)} collective-permute-done((bf16[96,384]{1,0:T(8,128)(2,1)S(1)}, bf16[96,384]{1,0:T(8,128)(2,1)S(1)}, u32[]{:S(2)}, u32[]{:S(2)}) %collective-permute-start.13) | collective-permute-done | bytes 73760 | tf_op jit(solution)/shard_map/ppermute | solution.py:297
  64.3 2.7 %collective-permute-done.14.refs_15_ = bf16[96,384]{1,0:T(8,128)(2,1)S(1)} collective-permute-done((bf16[96,384]{1,0:T(8,128)(2,1)S(1)}, bf16[96,384]{1,0:T(8,128)(2,1)S(1)}, u32[]{:S(2)}, u32[]{:S(2)}) %collective-permute-start.14) | collective-permute-done | bytes 73760 | tf_op jit(solution)/shard_map/ppermute | solution.py:297
  67.0 0.6 gather_left.1.left
  67.7 2.4 %products.1 = (bf16[96,384]{1,0:T(8,128)(2,1)S(1)}, bf16[96,384]{1,0:T(8,128)(2,1)S(1)}, bf16[96,384]{1,0:T(8,128)(2,1)S(1)}, bf16[96,384]{1,0:T(8,128)(2,1)S(1)...) custom-call(bf16[3072,384]{1,0:T(8,128)(2,1)S(1)} %bitcast.9, ...), custom_call_target="tpu_custom_call" | custom-call | flops 226492416 | bytes 3538944 | tf_op jit(solution)/shard_map/products/pallas_call | solution.py:353
  70.1 2.4 %collective-permute-start.15 = (bf16[96,384]{1,0:T(8,128)(2,1)S(1)}, bf16[96,384]{1,0:T(8,128)(2,1)S(1)}, u32[]{:S(2)}, u32[]{:S(2)}) collective-permute-start(bf16[96,384]{1,0:T(8,128)(2,1)S(1)} %get-tuple-element.55), channel_id=1, source_target_pairs={{0,8},{1,9},{2,10},{3,11},{4,12},{5,13},{6,14},{7,15},{8,0},{9,1},... | collective-permute-start | bytes 221192 | tf_op jit(solution)/shard_map/ppermute | solution.py:297
  72.5 0.2 collective-permute-start.17
  72.7 2.5 %collective-permute-start.18 = (bf16[96,384]{1,0:T(8,128)(2,1)S(1)}, bf16[96,384]{1,0:T(8,128)(2,1)S(1)}, u32[]{:S(2)}, u32[]{:S(2)}) collective-permute-start(bf16[96,384]{1,0:T(8,128)(2,1)S(1)} %get-tuple-element.58), channel_id=1, source_target_pairs={{0,10},{1,11},{2,8},{3,9},{4,14},{5,15},{6,12},{7,13},{8,2},{9,3},... | collective-permute-start | bytes 221192 | tf_op jit(solution)/shard_map/ppermute | solution.py:297
  75.2 0.1 collective-permute-start.19
  75.3 1.1 %collective-permute-start.20 = (bf16[96,384]{1,0:T(8,128)(2,1)S(1)}, bf16[96,384]{1,0:T(8,128)(2,1)S(1)}, u32[]{:S(2)}, u32[]{:S(2)}) collective-permute-start(bf16[96,384]{1,0:T(8,128)(2,1)S(1)} %get-tuple-element.60), channel_id=1, source_target_pairs={{0,2},{1,3},{2,0},{3,1},{4,6},{5,7},{6,4},{7,5},{8,10},{9,11},{10,... | collective-permute-start | bytes 221192 | tf_op jit(solution)/shard_map/ppermute | solution.py:297
  76.3 0.5 collective-permute-done.16.refs_2_
  76.9 1.1 %collective-permute-start.21 = (bf16[96,384]{1,0:T(8,128)(2,1)S(1)}, bf16[96,384]{1,0:T(8,128)(2,1)S(1)}, u32[]{:S(2)}, u32[]{:S(2)}) collective-permute-start(bf16[96,384]{1,0:T(8,128)(2,1)S(1)} %get-tuple-element.61), channel_id=1, source_target_pairs={{0,12},{1,13},{2,14},{3,15},{4,8},{5,9},{6,10},{7,11},{8,4},{9,5},... | collective-permute-start | bytes 221192 | tf_op jit(solution)/shard_map/ppermute | solution.py:297
  77.9 1.4 %collective-permute-start.22 = (bf16[96,384]{1,0:T(8,128)(2,1)S(1)}, bf16[96,384]{1,0:T(8,128)(2,1)S(1)}, u32[]{:S(2)}, u32[]{:S(2)}) collective-permute-start(bf16[96,384]{1,0:T(8,128)(2,1)S(1)} %get-tuple-element.62), channel_id=1, source_target_pairs={{0,13},{1,12},{2,15},{3,14},{4,9},{5,8},{6,11},{7,10},{8,5},{9,4},... | collective-permute-start | bytes 221192 | tf_op jit(solution)/shard_map/ppermute | solution.py:297
  79.3 1.3 %collective-permute-start.23 = (bf16[96,384]{1,0:T(8,128)(2,1)S(1)}, bf16[96,384]{1,0:T(8,128)(2,1)S(1)}, u32[]{:S(2)}, u32[]{:S(2)}) collective-permute-start(bf16[96,384]{1,0:T(8,128)(2,1)S(1)} %get-tuple-element.63), channel_id=1, source_target_pairs={{0,3},{1,2},{2,1},{3,0},{4,7},{5,6},{6,5},{7,4},{8,11},{9,10},{10,... | collective-permute-start | bytes 221192 | tf_op jit(solution)/shard_map/ppermute | solution.py:297
  80.6 0.2 collective-permute-done.19.refs_5_
  80.8 1.3 %collective-permute-start.24 = (bf16[96,384]{1,0:T(8,128)(2,1)S(1)}, bf16[96,384]{1,0:T(8,128)(2,1)S(1)}, u32[]{:S(2)}, u32[]{:S(2)}) collective-permute-start(bf16[96,384]{1,0:T(8,128)(2,1)S(1)} %get-tuple-element.64), channel_id=1, source_target_pairs={{0,14},{1,15},{2,12},{3,13},{4,10},{5,11},{6,8},{7,9},{8,6},{9,7},... | collective-permute-start | bytes 221192 | tf_op jit(solution)/shard_map/ppermute | solution.py:297
  82.1 0.2 collective-permute-done.20.refs_6_
  82.3 1.7 %collective-permute-start.25 = (bf16[96,384]{1,0:T(8,128)(2,1)S(1)}, bf16[96,384]{1,0:T(8,128)(2,1)S(1)}, u32[]{:S(2)}, u32[]{:S(2)}) collective-permute-start(bf16[96,384]{1,0:T(8,128)(2,1)S(1)} %get-tuple-element.65), channel_id=1, source_target_pairs={{0,15},{1,14},{2,13},{3,12},{4,11},{5,10},{6,9},{7,8},{8,7},{9,6},... | collective-permute-start | bytes 221192 | tf_op jit(solution)/shard_map/ppermute | solution.py:297
  84.0 2.0 %collective-permute-start.26 = (bf16[96,384]{1,0:T(8,128)(2,1)S(1)}, bf16[96,384]{1,0:T(8,128)(2,1)S(1)}, u32[]{:S(2)}, u32[]{:S(2)}) collective-permute-start(bf16[96,384]{1,0:T(8,128)(2,1)S(1)} %get-tuple-element.66), channel_id=1, source_target_pairs={{0,4},{1,5},{2,6},{3,7},{4,0},{5,1},{6,2},{7,3},{8,12},{9,13},{10,... | collective-permute-start | bytes 221192 | tf_op jit(solution)/shard_map/ppermute | solution.py:297
  86.0 0.1 collective-permute-start.27
  86.1 2.1 %collective-permute-start.28 = (bf16[96,384]{1,0:T(8,128)(2,1)S(1)}, bf16[96,384]{1,0:T(8,128)(2,1)S(1)}, u32[]{:S(2)}, u32[]{:S(2)}) collective-permute-start(bf16[96,384]{1,0:T(8,128)(2,1)S(1)} %get-tuple-element.68), channel_id=1, source_target_pairs={{0,6},{1,7},{2,4},{3,5},{4,2},{5,3},{6,0},{7,1},{8,14},{9,15},{10,... | collective-permute-start | bytes 221192 | tf_op jit(solution)/shard_map/ppermute | solution.py:297
  88.2 0.2 collective-permute-start.29
  88.4 4.6 %collective-permute-done.26.refs_12_ = bf16[96,384]{1,0:T(8,128)(2,1)S(1)} collective-permute-done((bf16[96,384]{1,0:T(8,128)(2,1)S(1)}, bf16[96,384]{1,0:T(8,128)(2,1)S(1)}, u32[]{:S(2)}, u32[]{:S(2)}) %collective-permute-start.26) | collective-permute-done | bytes 73760 | tf_op jit(solution)/shard_map/ppermute | solution.py:297
  93.0 2.0 %collective-permute-done.27.refs_13_ = bf16[96,384]{1,0:T(8,128)(2,1)S(1)} collective-permute-done((bf16[96,384]{1,0:T(8,128)(2,1)S(1)}, bf16[96,384]{1,0:T(8,128)(2,1)S(1)}, u32[]{:S(2)}, u32[]{:S(2)}) %collective-permute-start.27) | collective-permute-done | bytes 73760 | tf_op jit(solution)/shard_map/ppermute | solution.py:297
  95.0 2.2 %update.1 = bf16[12,384,128]{2,1,0:T(8,128)(2,1)} custom-call(bf16[96,384]{1,0:T(8,128)(2,1)S(1)} %get-tuple-element.54.refs_0_, bf16[96,384]{1,0:T(8,128)(2,1)S(1)} %collective-permute-done.15.refs_1_, bf16[96,384]{1,0:T(8,128)(2,1)S(1)} %collective-permute-done.16.refs_2_, bf16[96,384]{1,0:T(8,128)(2,1)S(1)} %collective-permute-done.17.refs_3_, ...), custom_call_target="tpu_custom_call" | custom-call | flops 150994944 | bytes 3538944 | tf_op jit(solution)/shard_map/update/pallas_call | solution.py:364
  (45 shorter events, 0.1 us)
Async XLA Ops:
  4.9 7.4 %copy-start = (bf16[12,384,128]{2,1,0:T(8,128)(2,1)S(1)}, bf16[12,384,128]{2,1,0:T(8,128)(2,1)}, u32[]{:S(2)}) copy-start(bf16[12,384,128]{2,1,0:T(8,128)(2,1)} %pair_ref.3) | copy-start | bytes 3538948
  4.9 7.4 %copy-start.6 = (f32[512]{0:T(512)S(1)}, f32[512]{0:T(512)}, u32[]{:S(2)}) copy-start(f32[512]{0:T(512)} %param.15) | copy-start | bytes 6148
  4.9 7.4 %copy-start.7 = (f32[128]{0:T(128)S(1)}, f32[128]{0:T(128)}, u32[]{:S(2)}) copy-start(f32[128]{0:T(128)} %param.12) | copy-start | bytes 1540
  4.9 7.4 %copy-start.8 = (f32[128]{0:T(128)S(1)}, f32[128]{0:T(128)}, u32[]{:S(2)}) copy-start(f32[128]{0:T(128)} %param.13) | copy-start | bytes 1540
  4.9 7.4 %copy-start.9 = (f32[128]{0:T(128)S(1)}, f32[128]{0:T(128)}, u32[]{:S(2)}) copy-start(f32[128]{0:T(128)} %param.17) | copy-start | bytes 1540
  4.9 62.7 %all-to-all-start = ((bf16[32,96,384]{2,1,0:T(8,128)(2,1)}), bf16[32,96,384]{2,1,0:T(8,128)(2,1)S(1)}, u32[]{:S(2)}, u32[]{:S(2)}) async-start(bf16[32,96,384]{2,1,0:T(8,128)(2,1)} %bitcast.20), calls=%async_computation | async-start | bytes 4718592 | tf_op jit(solution)/shard_map/all_to_all | solution.py:293
  12.3 0.9 copy-start.3
  13.2 0.8 copy-start.5
  16.7 1.0 %copy-start.1 = (bf16[12,384,128]{2,1,0:T(8,128)(2,1)}, bf16[12,384,128]{2,1,0:T(8,128)(2,1)S(1)}, u32[]{:S(2)}) copy-start(bf16[12,384,128]{2,1,0:T(8,128)(2,1)S(1)} %get-tuple-element.70.refs_16_) | copy-start | bytes 3538948
  17.7 3.7 %collective-permute-start = (bf16[96,384]{1,0:T(8,128)(2,1)S(1)}, bf16[96,384]{1,0:T(8,128)(2,1)S(1)}, u32[]{:S(2)}, u32[]{:S(2)}) collective-permute-start(bf16[96,384]{1,0:T(8,128)(2,1)S(1)} %get-tuple-element.39), channel_id=1, source_target_pairs={{0,1},{1,0},{2,3},{3,2},{4,5},{5,4},{6,7},{7,6},{8,9},{9,8},{10,11... | collective-permute-start | bytes 221192 | tf_op jit(solution)/shard_map/ppermute | solution.py:297
  18.0 13.8 %collective-permute-start.1 = (bf16[96,384]{1,0:T(8,128)(2,1)S(1)}, bf16[96,384]{1,0:T(8,128)(2,1)S(1)}, u32[]{:S(2)}, u32[]{:S(2)}) collective-permute-start(bf16[96,384]{1,0:T(8,128)(2,1)S(1)} %get-tuple-element.40), channel_id=1, source_target_pairs={{0,2},{1,3},{2,0},{3,1},{4,6},{5,7},{6,4},{7,5},{8,10},{9,11},{10,... | collective-permute-start | bytes 221192 | tf_op jit(solution)/shard_map/ppermute | solution.py:297
  19.7 13.0 %collective-permute-start.2 = (bf16[96,384]{1,0:T(8,128)(2,1)S(1)}, bf16[96,384]{1,0:T(8,128)(2,1)S(1)}, u32[]{:S(2)}, u32[]{:S(2)}) collective-permute-start(bf16[96,384]{1,0:T(8,128)(2,1)S(1)} %get-tuple-element.41), channel_id=1, source_target_pairs={{0,3},{1,2},{2,1},{3,0},{4,7},{5,6},{6,5},{7,4},{8,11},{9,10},{10,... | collective-permute-start | bytes 221192 | tf_op jit(solution)/shard_map/ppermute | solution.py:297
  19.7 13.2 %collective-permute-start.3 = (bf16[96,384]{1,0:T(8,128)(2,1)S(1)}, bf16[96,384]{1,0:T(8,128)(2,1)S(1)}, u32[]{:S(2)}, u32[]{:S(2)}) collective-permute-start(bf16[96,384]{1,0:T(8,128)(2,1)S(1)} %get-tuple-element.42), channel_id=1, source_target_pairs={{0,4},{1,5},{2,6},{3,7},{4,0},{5,1},{6,2},{7,3},{8,12},{9,13},{10,... | collective-permute-start | bytes 221192 | tf_op jit(solution)/shard_map/ppermute | solution.py:297
  21.3 13.8 %collective-permute-start.4 = (bf16[96,384]{1,0:T(8,128)(2,1)S(1)}, bf16[96,384]{1,0:T(8,128)(2,1)S(1)}, u32[]{:S(2)}, u32[]{:S(2)}) collective-permute-start(bf16[96,384]{1,0:T(8,128)(2,1)S(1)} %get-tuple-element.43), channel_id=1, source_target_pairs={{0,5},{1,4},{2,7},{3,6},{4,1},{5,0},{6,3},{7,2},{8,13},{9,12},{10,... | collective-permute-start | bytes 221192 | tf_op jit(solution)/shard_map/ppermute | solution.py:297
  21.5 20.8 %collective-permute-start.5 = (bf16[96,384]{1,0:T(8,128)(2,1)S(1)}, bf16[96,384]{1,0:T(8,128)(2,1)S(1)}, u32[]{:S(2)}, u32[]{:S(2)}) collective-permute-start(bf16[96,384]{1,0:T(8,128)(2,1)S(1)} %get-tuple-element.44), channel_id=1, source_target_pairs={{0,6},{1,7},{2,4},{3,5},{4,2},{5,3},{6,0},{7,1},{8,14},{9,15},{10,... | collective-permute-start | bytes 221192 | tf_op jit(solution)/shard_map/ppermute | solution.py:297
  31.8 11.3 %collective-permute-start.6 = (bf16[96,384]{1,0:T(8,128)(2,1)S(1)}, bf16[96,384]{1,0:T(8,128)(2,1)S(1)}, u32[]{:S(2)}, u32[]{:S(2)}) collective-permute-start(bf16[96,384]{1,0:T(8,128)(2,1)S(1)} %get-tuple-element.45), channel_id=1, source_target_pairs={{0,7},{1,6},{2,5},{3,4},{4,3},{5,2},{6,1},{7,0},{8,15},{9,14},{10,... | collective-permute-start | bytes 221192 | tf_op jit(solution)/shard_map/ppermute | solution.py:297
  32.6 20.8 %collective-permute-start.7 = (bf16[96,384]{1,0:T(8,128)(2,1)S(1)}, bf16[96,384]{1,0:T(8,128)(2,1)S(1)}, u32[]{:S(2)}, u32[]{:S(2)}) collective-permute-start(bf16[96,384]{1,0:T(8,128)(2,1)S(1)} %get-tuple-element.46), channel_id=1, source_target_pairs={{0,8},{1,9},{2,10},{3,11},{4,12},{5,13},{6,14},{7,15},{8,0},{9,1},... | collective-permute-start | bytes 221192 | tf_op jit(solution)/shard_map/ppermute | solution.py:297
  32.9 22.6 %collective-permute-start.8 = (bf16[96,384]{1,0:T(8,128)(2,1)S(1)}, bf16[96,384]{1,0:T(8,128)(2,1)S(1)}, u32[]{:S(2)}, u32[]{:S(2)}) collective-permute-start(bf16[96,384]{1,0:T(8,128)(2,1)S(1)} %get-tuple-element.47), channel_id=1, source_target_pairs={{0,9},{1,8},{2,11},{3,10},{4,13},{5,12},{6,15},{7,14},{8,1},{9,0},... | collective-permute-start | bytes 221192 | tf_op jit(solution)/shard_map/ppermute | solution.py:297
  35.2 23.1 %collective-permute-start.9 = (bf16[96,384]{1,0:T(8,128)(2,1)S(1)}, bf16[96,384]{1,0:T(8,128)(2,1)S(1)}, u32[]{:S(2)}, u32[]{:S(2)}) collective-permute-start(bf16[96,384]{1,0:T(8,128)(2,1)S(1)} %get-tuple-element.48), channel_id=1, source_target_pairs={{0,10},{1,11},{2,8},{3,9},{4,14},{5,15},{6,12},{7,13},{8,2},{9,3},... | collective-permute-start | bytes 221192 | tf_op jit(solution)/shard_map/ppermute | solution.py:297
  42.3 17.7 %collective-permute-start.10 = (bf16[96,384]{1,0:T(8,128)(2,1)S(1)}, bf16[96,384]{1,0:T(8,128)(2,1)S(1)}, u32[]{:S(2)}, u32[]{:S(2)}) collective-permute-start(bf16[96,384]{1,0:T(8,128)(2,1)S(1)} %get-tuple-element.49), channel_id=1, source_target_pairs={{0,11},{1,10},{2,9},{3,8},{4,15},{5,14},{6,13},{7,12},{8,3},{9,2},... | collective-permute-start | bytes 221192 | tf_op jit(solution)/shard_map/ppermute | solution.py:297
  43.1 16.9 %collective-permute-start.11 = (bf16[96,384]{1,0:T(8,128)(2,1)S(1)}, bf16[96,384]{1,0:T(8,128)(2,1)S(1)}, u32[]{:S(2)}, u32[]{:S(2)}) collective-permute-start(bf16[96,384]{1,0:T(8,128)(2,1)S(1)} %get-tuple-element.50), channel_id=1, source_target_pairs={{0,12},{1,13},{2,14},{3,15},{4,8},{5,9},{6,10},{7,11},{8,4},{9,5},... | collective-permute-start | bytes 221192 | tf_op jit(solution)/shard_map/ppermute | solution.py:297
  53.4 7.9 %collective-permute-start.12 = (bf16[96,384]{1,0:T(8,128)(2,1)S(1)}, bf16[96,384]{1,0:T(8,128)(2,1)S(1)}, u32[]{:S(2)}, u32[]{:S(2)}) collective-permute-start(bf16[96,384]{1,0:T(8,128)(2,1)S(1)} %get-tuple-element.51), channel_id=1, source_target_pairs={{0,13},{1,12},{2,15},{3,14},{4,9},{5,8},{6,11},{7,10},{8,5},{9,4},... | collective-permute-start | bytes 221192 | tf_op jit(solution)/shard_map/ppermute | solution.py:297
  55.5 8.9 %collective-permute-start.13 = (bf16[96,384]{1,0:T(8,128)(2,1)S(1)}, bf16[96,384]{1,0:T(8,128)(2,1)S(1)}, u32[]{:S(2)}, u32[]{:S(2)}) collective-permute-start(bf16[96,384]{1,0:T(8,128)(2,1)S(1)} %get-tuple-element.52), channel_id=1, source_target_pairs={{0,14},{1,15},{2,12},{3,13},{4,10},{5,11},{6,8},{7,9},{8,6},{9,7},... | collective-permute-start | bytes 221192 | tf_op jit(solution)/shard_map/ppermute | solution.py:297
  58.3 8.8 %collective-permute-start.14 = (bf16[96,384]{1,0:T(8,128)(2,1)S(1)}, bf16[96,384]{1,0:T(8,128)(2,1)S(1)}, u32[]{:S(2)}, u32[]{:S(2)}) collective-permute-start(bf16[96,384]{1,0:T(8,128)(2,1)S(1)} %get-tuple-element.53), channel_id=1, source_target_pairs={{0,15},{1,14},{2,13},{3,12},{4,11},{5,10},{6,9},{7,8},{8,7},{9,6},... | collective-permute-start | bytes 221192 | tf_op jit(solution)/shard_map/ppermute | solution.py:297
  67.6 27.4 %copy-start.2 = (bf16[12,384,128]{2,1,0:T(8,128)(2,1)S(1)}, bf16[12,384,128]{2,1,0:T(8,128)(2,1)}, u32[]{:S(2)}) copy-start(bf16[12,384,128]{2,1,0:T(8,128)(2,1)} %copy-done.1) | copy-start | bytes 3538948
  67.6 27.4 %copy-start.4 = (bf16[128,128]{1,0:T(8,128)(2,1)S(1)}, bf16[128,128]{1,0:T(8,128)(2,1)}, u32[]{:S(2)}) copy-start(bf16[128,128]{1,0:T(8,128)(2,1)} %refs_19_.1) | copy-start | bytes 98308
  67.6 27.4 %copy-start.10 = (f32[128]{0:T(128)S(1)}, f32[128]{0:T(128)}, u32[]{:S(2)}) copy-start(f32[128]{0:T(128)} %param.18) | copy-start | bytes 1540
  67.7 27.4 %copy-start.11 = (f32[128]{0:T(128)S(1)}, f32[128]{0:T(128)}, u32[]{:S(2)}) copy-start(f32[128]{0:T(128)} %param.19) | copy-start | bytes 1540
  67.7 27.4 %copy-start.12 = (f32[128]{0:T(128)S(1)}, f32[128]{0:T(128)}, u32[]{:S(2)}) copy-start(f32[128]{0:T(128)} %param.21) | copy-start | bytes 1540
  70.1 5.2 %collective-permute-start.15 = (bf16[96,384]{1,0:T(8,128)(2,1)S(1)}, bf16[96,384]{1,0:T(8,128)(2,1)S(1)}, u32[]{:S(2)}, u32[]{:S(2)}) collective-permute-start(bf16[96,384]{1,0:T(8,128)(2,1)S(1)} %get-tuple-element.55), channel_id=1, source_target_pairs={{0,8},{1,9},{2,10},{3,11},{4,12},{5,13},{6,14},{7,15},{8,0},{9,1},... | collective-permute-start | bytes 221192 | tf_op jit(solution)/shard_map/ppermute | solution.py:297
  72.5 4.4 %collective-permute-start.16 = (bf16[96,384]{1,0:T(8,128)(2,1)S(1)}, bf16[96,384]{1,0:T(8,128)(2,1)S(1)}, u32[]{:S(2)}, u32[]{:S(2)}) collective-permute-start(bf16[96,384]{1,0:T(8,128)(2,1)S(1)} %get-tuple-element.56), channel_id=1, source_target_pairs={{0,9},{1,8},{2,11},{3,10},{4,13},{5,12},{6,15},{7,14},{8,1},{9,0},... | collective-permute-start | bytes 221192 | tf_op jit(solution)/shard_map/ppermute | solution.py:297
  72.5 5.4 %collective-permute-start.17 = (bf16[96,384]{1,0:T(8,128)(2,1)S(1)}, bf16[96,384]{1,0:T(8,128)(2,1)S(1)}, u32[]{:S(2)}, u32[]{:S(2)}) collective-permute-start(bf16[96,384]{1,0:T(8,128)(2,1)S(1)} %get-tuple-element.57), channel_id=1, source_target_pairs={{0,1},{1,0},{2,3},{3,2},{4,5},{5,4},{6,7},{7,6},{8,9},{9,8},{10,11... | collective-permute-start | bytes 221192 | tf_op jit(solution)/shard_map/ppermute | solution.py:297
  72.7 6.6 %collective-permute-start.18 = (bf16[96,384]{1,0:T(8,128)(2,1)S(1)}, bf16[96,384]{1,0:T(8,128)(2,1)S(1)}, u32[]{:S(2)}, u32[]{:S(2)}) collective-permute-start(bf16[96,384]{1,0:T(8,128)(2,1)S(1)} %get-tuple-element.58), channel_id=1, source_target_pairs={{0,10},{1,11},{2,8},{3,9},{4,14},{5,15},{6,12},{7,13},{8,2},{9,3},... | collective-permute-start | bytes 221192 | tf_op jit(solution)/shard_map/ppermute | solution.py:297
  75.2 5.6 %collective-permute-start.19 = (bf16[96,384]{1,0:T(8,128)(2,1)S(1)}, bf16[96,384]{1,0:T(8,128)(2,1)S(1)}, u32[]{:S(2)}, u32[]{:S(2)}) collective-permute-start(bf16[96,384]{1,0:T(8,128)(2,1)S(1)} %get-tuple-element.59), channel_id=1, source_target_pairs={{0,11},{1,10},{2,9},{3,8},{4,15},{5,14},{6,13},{7,12},{8,3},{9,2},... | collective-permute-start | bytes 221192 | tf_op jit(solution)/shard_map/ppermute | solution.py:297
  75.3 7.1 %collective-permute-start.20 = (bf16[96,384]{1,0:T(8,128)(2,1)S(1)}, bf16[96,384]{1,0:T(8,128)(2,1)S(1)}, u32[]{:S(2)}, u32[]{:S(2)}) collective-permute-start(bf16[96,384]{1,0:T(8,128)(2,1)S(1)} %get-tuple-element.60), channel_id=1, source_target_pairs={{0,2},{1,3},{2,0},{3,1},{4,6},{5,7},{6,4},{7,5},{8,10},{9,11},{10,... | collective-permute-start | bytes 221192 | tf_op jit(solution)/shard_map/ppermute | solution.py:297
  76.9 7.1 %collective-permute-start.21 = (bf16[96,384]{1,0:T(8,128)(2,1)S(1)}, bf16[96,384]{1,0:T(8,128)(2,1)S(1)}, u32[]{:S(2)}, u32[]{:S(2)}) collective-permute-start(bf16[96,384]{1,0:T(8,128)(2,1)S(1)} %get-tuple-element.61), channel_id=1, source_target_pairs={{0,12},{1,13},{2,14},{3,15},{4,8},{5,9},{6,10},{7,11},{8,4},{9,5},... | collective-permute-start | bytes 221192 | tf_op jit(solution)/shard_map/ppermute | solution.py:297
  77.9 8.1 %collective-permute-start.22 = (bf16[96,384]{1,0:T(8,128)(2,1)S(1)}, bf16[96,384]{1,0:T(8,128)(2,1)S(1)}, u32[]{:S(2)}, u32[]{:S(2)}) collective-permute-start(bf16[96,384]{1,0:T(8,128)(2,1)S(1)} %get-tuple-element.62), channel_id=1, source_target_pairs={{0,13},{1,12},{2,15},{3,14},{4,9},{5,8},{6,11},{7,10},{8,5},{9,4},... | collective-permute-start | bytes 221192 | tf_op jit(solution)/shard_map/ppermute | solution.py:297
  79.3 6.8 %collective-permute-start.23 = (bf16[96,384]{1,0:T(8,128)(2,1)S(1)}, bf16[96,384]{1,0:T(8,128)(2,1)S(1)}, u32[]{:S(2)}, u32[]{:S(2)}) collective-permute-start(bf16[96,384]{1,0:T(8,128)(2,1)S(1)} %get-tuple-element.63), channel_id=1, source_target_pairs={{0,3},{1,2},{2,1},{3,0},{4,7},{5,6},{6,5},{7,4},{8,11},{9,10},{10,... | collective-permute-start | bytes 221192 | tf_op jit(solution)/shard_map/ppermute | solution.py:297
  80.8 7.5 %collective-permute-start.24 = (bf16[96,384]{1,0:T(8,128)(2,1)S(1)}, bf16[96,384]{1,0:T(8,128)(2,1)S(1)}, u32[]{:S(2)}, u32[]{:S(2)}) collective-permute-start(bf16[96,384]{1,0:T(8,128)(2,1)S(1)} %get-tuple-element.64), channel_id=1, source_target_pairs={{0,14},{1,15},{2,12},{3,13},{4,10},{5,11},{6,8},{7,9},{8,6},{9,7},... | collective-permute-start | bytes 221192 | tf_op jit(solution)/shard_map/ppermute | solution.py:297
  82.3 6.1 %collective-permute-start.25 = (bf16[96,384]{1,0:T(8,128)(2,1)S(1)}, bf16[96,384]{1,0:T(8,128)(2,1)S(1)}, u32[]{:S(2)}, u32[]{:S(2)}) collective-permute-start(bf16[96,384]{1,0:T(8,128)(2,1)S(1)} %get-tuple-element.65), channel_id=1, source_target_pairs={{0,15},{1,14},{2,13},{3,12},{4,11},{5,10},{6,9},{7,8},{8,7},{9,6},... | collective-permute-start | bytes 221192 | tf_op jit(solution)/shard_map/ppermute | solution.py:297
  84.0 9.0 %collective-permute-start.26 = (bf16[96,384]{1,0:T(8,128)(2,1)S(1)}, bf16[96,384]{1,0:T(8,128)(2,1)S(1)}, u32[]{:S(2)}, u32[]{:S(2)}) collective-permute-start(bf16[96,384]{1,0:T(8,128)(2,1)S(1)} %get-tuple-element.66), channel_id=1, source_target_pairs={{0,4},{1,5},{2,6},{3,7},{4,0},{5,1},{6,2},{7,3},{8,12},{9,13},{10,... | collective-permute-start | bytes 221192 | tf_op jit(solution)/shard_map/ppermute | solution.py:297
  86.0 9.0 %collective-permute-start.27 = (bf16[96,384]{1,0:T(8,128)(2,1)S(1)}, bf16[96,384]{1,0:T(8,128)(2,1)S(1)}, u32[]{:S(2)}, u32[]{:S(2)}) collective-permute-start(bf16[96,384]{1,0:T(8,128)(2,1)S(1)} %get-tuple-element.67), channel_id=1, source_target_pairs={{0,5},{1,4},{2,7},{3,6},{4,1},{5,0},{6,3},{7,2},{8,13},{9,12},{10,... | collective-permute-start | bytes 221192 | tf_op jit(solution)/shard_map/ppermute | solution.py:297
  86.1 8.9 %collective-permute-start.28 = (bf16[96,384]{1,0:T(8,128)(2,1)S(1)}, bf16[96,384]{1,0:T(8,128)(2,1)S(1)}, u32[]{:S(2)}, u32[]{:S(2)}) collective-permute-start(bf16[96,384]{1,0:T(8,128)(2,1)S(1)} %get-tuple-element.68), channel_id=1, source_target_pairs={{0,6},{1,7},{2,4},{3,5},{4,2},{5,3},{6,0},{7,1},{8,14},{9,15},{10,... | collective-permute-start | bytes 221192 | tf_op jit(solution)/shard_map/ppermute | solution.py:297
  88.2 6.8 %collective-permute-start.29 = (bf16[96,384]{1,0:T(8,128)(2,1)S(1)}, bf16[96,384]{1,0:T(8,128)(2,1)S(1)}, u32[]{:S(2)}, u32[]{:S(2)}) collective-permute-start(bf16[96,384]{1,0:T(8,128)(2,1)S(1)} %get-tuple-element.69), channel_id=1, source_target_pairs={{0,7},{1,6},{2,5},{3,4},{4,3},{5,2},{6,1},{7,0},{8,15},{9,14},{10,... | collective-permute-start | bytes 221192 | tf_op jit(solution)/shard_map/ppermute | solution.py:297

commit v13 on v9

--- a/solution.py
+++ b/solution.py
@@ -64,10 +64,10 @@
     return sigmoid(both[:width]) * both[width:]
 
 
-def as_rows(values, k):
+def as_rows(values, k, step=STEP):
     hosts = values.shape[0] // BLOCK
     return jnp.concatenate(
-        [values[:, r * k : (r + 1) * k].reshape(hosts, BLOCK, k) for r in range(STEP)], axis=1
+        [values[:, r * k : (r + 1) * k].reshape(hosts, BLOCK, k) for r in range(step)], axis=1
     )
 
 
@@ -96,7 +96,7 @@
     def _():
         wf[...] = w_ref[...].astype(f32).T
         bf[...] = column(b_ref[...])
-        host = lax.axis_index(("chan", "quarter"))
+        host = lax.axis_index(("side", "chan", "quarter"))
         for half in range(2):
             for b in range(0, len(outs), 2):
                 source = [
@@ -134,8 +134,7 @@
     ]
 
 
-def multiply(left, right_ref, right, held, store):
-    regroup(slices([right_ref]), right, shuffle(BLOCK, SIZE))
+def multiply(left, right, held, store):
     back = shuffle(SIZE, BLOCK)
     for c in range(BLOCK):
         held[c] = dot_nt(left[c], right[c]).astype(bf16)
@@ -150,27 +149,59 @@
     regroup(slices(refs[:-1]), refs[-1], shuffle(BLOCK, SIZE))
 
 
-def product_kernel(right_ref, left, out_ref, right, held):
-    rows = left.shape[1] // out_ref.shape[0]
+def far_kernel(right_ref, left_ref, *refs):
+    outs, (right, held) = refs[:-2], refs[-2:]
+    count = left_ref.shape[1] // 2
+    rows = count // len(outs)
+    regroup(slices([right_ref]), right, shuffle(BLOCK, SIZE))
+
+    def store(i, values):
+        to, at = divmod(i, rows)
+        outs[to][at * BLOCK : (at + STEP) * BLOCK, :] = values
+
+    multiply(left_ref.at[:, count:], right, held, store)
+
+
+def near_kernel(left_ref, right_ref, out_ref, held):
+    near = out_ref.shape[0]
+    count = left_ref.shape[1] // 2
+    rows = count // near
     host = lax.axis_index(("chan", "quarter"))
 
     def store(i, values):
         to, at = divmod(i, rows)
         out_ref[host ^ to, at * BLOCK : (at + STEP) * BLOCK, :] = values
 
-    multiply(left, right_ref, right, held, store)
-
-
-def final_kernel(x_ref, gate_ref, g_ref, s_ref, w_ref, b_ref, out_ref, made, leave):
-    hosts, _, j = x_ref.shape
-    rows = gate_ref.shape[0]
-    width = hosts * BLOCK
-    gain, shift = widen(column(g_ref[...]), j), widen(column(s_ref[...]), j)
+    multiply(left_ref.at[:, :count], right_ref, held, store)
+
+
+def prepare_kernel(near, g_ref, s_ref, w_ref, columns_ref, weight_ref, plain, mixed):
+    plain[0] = column(g_ref[...])
+    plain[1] = column(s_ref[...])
+    plain[2] = w_ref[...].astype(f32)
+    host = lax.axis_index(("side", "chan", "quarter"))
+    order = [host // near * near + n for n in range(near)]
+    order += [host ^ (near + n) for n in range(near)]
+    for m, one in enumerate(order):
+        source = pl.ds(pl.multiple_of(one * BLOCK, BLOCK), BLOCK)
+        for n in range(3):
+            mixed[n, m * BLOCK : (m + 1) * BLOCK] = plain[n, source]
+    columns_ref[...] = mixed[:2]
+    weight_ref[...] = mixed[2].astype(bf16)
+
+
+def final_kernel(near_ref, *refs):
+    near, _, j = near_ref.shape
+    fars = refs[:near]
+    gate_ref, columns_ref, w_ref, b_ref, out_ref, made, leave = refs[near:]
+    rows, _, width = gate_ref.shape
+    gain, shift = widen(columns_ref[0], j), widen(columns_ref[1], j)
     stores = []
     for r in range(0, rows, 2):
-        pair = x_ref[:, r * BLOCK : (r + 2) * BLOCK].astype(f32)
+        pair = [near_ref[h, r * BLOCK : (r + 2) * BLOCK, :].astype(f32) for h in range(near)]
+        pair += [ref[r * BLOCK : (r + 2) * BLOCK, :].astype(f32) for ref in fars]
         for n in range(2):
-            x = pair[:, n * BLOCK : (n + 1) * BLOCK].reshape(width, j)
+            x = jnp.concatenate([one[n * BLOCK : (n + 1) * BLOCK] for one in pair], axis=0)
             centered = x - jnp.mean(x, axis=0, keepdims=True)
             variance = jnp.mean(centered * centered, axis=0, keepdims=True)
             normed = centered * lax.rsqrt(variance + epsilon) * gain + shift
@@ -204,7 +235,7 @@
     tall = rows * BLOCK
     mine = hosts * rows
     devices = parts * hosts
-    in_part = ("chan", "quarter")
+    in_part = ("side", "chan", "quarter")
     everywhere = ("part",) + in_part
     row = lambda v: v.reshape(1, -1)
     row_block = pl.BlockSpec((STEP, k, width), lambda s: (s, 0, 0))
@@ -280,30 +311,70 @@
         name="gather_left",
     )(*lefts)
 
+    near = hosts // 2
     span = GATHER * rows
-    product = pl.pallas_call(
-        product_kernel,
-        grid=(devices // GATHER,),
-        in_specs=[pl.BlockSpec((span * BLOCK, k), lambda s: (s, 0)), whole((BLOCK, mine, k))],
-        out_specs=pl.BlockSpec((hosts, tall, span), lambda s: (0, 0, s)),
-        out_shape=bfloat(hosts, tall, devices * rows),
-        scratch_shapes=[pltpu.VMEM((BLOCK, span, k), bf16), pltpu.VMEM((BLOCK, mine, span), bf16)],
+    gathers = devices // GATHER
+    if gathers == 1:
+        blocks = dict(in_specs=[vmem] * 2, out_specs=[vmem] * (near + 1))
+        rest = dict(in_specs=[vmem] * 2, out_specs=vmem)
+    else:
+        grouped = pl.BlockSpec((BLOCK, span, k), lambda s: (0, s, 0))
+        blocks = dict(
+            grid=(gathers,),
+            in_specs=[pl.BlockSpec((span * BLOCK, k), lambda s: (s, 0)), whole((BLOCK, mine, k))],
+            out_specs=[pl.BlockSpec((tall, span), lambda s: (0, s))] * near + [grouped],
+        )
+        rest = dict(
+            grid=(gathers,),
+            in_specs=[whole((BLOCK, mine, k)), grouped],
+            out_specs=pl.BlockSpec((near, tall, span), lambda s: (0, 0, s)),
+        )
+    spent = BLOCK * mine * mine * k
+    *fars, right = pl.pallas_call(
+        far_kernel,
+        **blocks,
+        out_shape=[pltpu.HBM((tall, devices * rows), bf16)] * near + [bfloat(BLOCK, devices * rows, k)],
+        scratch_shapes=[pltpu.VMEM((BLOCK, mine // 2, span), bf16)],
         compiler_params=params(40),
-        cost_estimate=cost(2 * BLOCK * mine * mine * k, 6 * BLOCK * mine * k),
-        name="products",
+        cost_estimate=cost(spent, 6 * BLOCK * mine * k),
+        name="far_products",
     )(right.reshape(devices * tall, k), left)
-    product = lax.all_to_all(product, in_part, 0, 0, tiled=True)
+    fars = [send(values, near + b) for b, values in enumerate(fars)]
+    nears = pl.pallas_call(
+        near_kernel,
+        **rest,
+        out_shape=bfloat(near, tall, devices * rows),
+        scratch_shapes=[pltpu.VMEM((BLOCK, mine // 2, span), bf16)],
+        compiler_params=params(),
+        cost_estimate=cost(spent, 6 * BLOCK * mine * k),
+        name="near_products",
+    )(left, right)
+    nears = lax.all_to_all(nears, ("chan", "quarter"), 0, 0, tiled=True)
+
+    columns, weight = pl.pallas_call(
+        functools.partial(prepare_kernel, near),
+        in_specs=[vmem] * 3,
+        out_specs=[vmem] * 2,
+        out_shape=[jax.ShapeDtypeStruct((2, hidden, LANES), f32), bfloat(hidden, width)],
+        scratch_shapes=[pltpu.VMEM((3, hidden, LANES), f32)] * 2,
+        compiler_params=params(),
+        cost_estimate=cost(1 << 37, 4 * hidden * width),
+        name="prepare",
+    )(row(center_gain), row(center_shift), out_weight)
 
     return pl.pallas_call(
         final_kernel,
-        in_specs=[vmem] * 6,
+        in_specs=[vmem] * (near + 5),
         out_specs=anywhere,
         out_shape=bfloat(*pair.shape),
-        scratch_shapes=[pltpu.VMEM(pair.shape, bf16), pltpu.SemaphoreType.DMA((rows // 2,))],
+        scratch_shapes=[
+            pltpu.VMEM(pair.shape, bf16),
+            pltpu.SemaphoreType.DMA((rows // 2,)),
+        ],
         compiler_params=params(),
         cost_estimate=cost(2 * work * width, 6 * work),
         name="update",
-    )(product, gate, row(center_gain), row(center_shift), out_weight, row(out_bias))
+    )(nears, *fars, gate, columns, weight, row(out_bias))
 
 
 def solution(mesh):
@@ -311,9 +382,10 @@
     near = CHANNELS // BLOCK // quarter
     parts = chan // near
     split = Mesh(
-        mesh.devices.reshape(groups, parts, near, quarter), ("groups", "part", "chan", "quarter")
+        mesh.devices.reshape(groups, parts, 2, near // 2, quarter),
+        ("groups", "part", "side", "chan", "quarter"),
     )
-    rows = P(("groups", "part", "chan", "quarter"), None, None)
+    rows = P(("groups", "part", "side", "chan", "quarter"), None, None)
     return jax.shard_map(
         functools.partial(shards, parts),
         mesh=split,

time: 94.5 us -> 106 us (1.12)
  blocking collectives: 21.8 us -> 0 us
  starting transfers between devices: 26.6 us -> 46.8 us
  waiting for transfers between devices: 30.1 us -> 40.7 us
  Pallas kernels: 12.8 us -> 15.3 us
    all_to_all x1 -> x0, blocking collectives: 21.8 us -> none  [shards(): product = lax.all_to_all(product, in_part, 0, 0, tiled=True)]
    ppermute x15 -> x23, starting transfers between devices: 19.2 us -> 35.6 us  [send(): return lax.ppermute(values, everywhere, pairs)]
    ppermute x15 -> x23, waiting for transfers between devices: 30.1 us -> 38.9 us  [send(): return lax.ppermute(values, everywhere, pairs)]
    all_to_all x0 -> x1, starting transfers between devices: none -> 3.92 us  [shards(): nears = lax.all_to_all(nears, ('chan', 'quarter'), 0, 0, tiled=True)]
    pallas_call x2 -> x4, Pallas kernels: 4.49 us -> 7.01 us  [the longest x1 2.7 us: shards(): pl.pallas_call(far_kernel, **blocks, out_shape=[pltpu.HBM((tall, devices...]
    all_to_all x0 -> x1, waiting for transfers between devices: none -> 1.77 us  [shards(): nears = lax.all_to_all(nears, ('chan', 'quarter'), 0, 0, tiled=True)]
    unnamed x26 -> x36, local copies, waits for them, and re-layouts: 2.72 us -> 2.74 us
  transfers between devices with their start and end apart: 16 -> 25, of which waited for: 8 -> 11; matrix products, arithmetic and copies ran while one was open for 0% -> 0% of each run, Pallas kernels for 3% -> 5%
where the time goes in v13:
time: 106 us
  starting transfers between devices  46.8 us (44%)
  waiting for transfers between devices  40.7 us (38%)
  Pallas kernels  15.3 us (14%)
  local copies, waits for them, and re-layouts  2.74 us (3%)
    ppermute x23, waiting for transfers between devices, send(): return lax.ppermute(values, everywhere, pairs)  38.9 us
    ppermute x23, starting transfers between devices, send(): return lax.ppermute(values, everywhere, pairs)  35.6 us
    all_to_all x1, starting transfers between devices, shards(): lax.all_to_all(right.reshape(devices, tall, k), everywhere, 0, 0, tiled=T...  7.3 us
    pallas_call x1, Pallas kernels, shards(): pl.pallas_call(right_kernel, grid=(steps,), in_specs=[row_block, whole((1...  4.99 us
    all_to_all x1, starting transfers between devices, shards(): nears = lax.all_to_all(nears, ('chan', 'quarter'), 0, 0, tiled=True)  3.92 us
    unnamed x36, local copies, waits for them, and re-layouts  2.74 us
    pallas_call x1, Pallas kernels, shards(): pl.pallas_call(left_kernel, grid=(steps,), in_specs=[row_block, whole((1,...  2.73 us
    pallas_call x1, Pallas kernels, shards(): pl.pallas_call(far_kernel, **blocks, out_shape=[pltpu.HBM((tall, devices...  2.7 us
  transfers between devices with their start and end apart: 25, of which 11 were waited for; matrix products, arithmetic and copies ran while one was open for 0% of the time, Pallas kernels for 5%

profile of v13, /device:TPU:0, one launch (start us, length us, event | category | flops | bytes accessed | tf_op | source)
XLA Modules:
  0.0 105.8 jit_solution(16634008505552401932)
XLA Ops:
  0.0 5.0 %right_factor.1 = bf16[2,16,96,384]{3,2,1,0:T(8,128)(2,1)} custom-call(bf16[12,384,128]{2,1,0:T(8,128)(2,1)} %pair_ref.3, f32[1,128]{1,0:T(1,128)} %bitcast.12, f32[1,128]{1,0:T(1,128)} %bitcast.14, bf16[128,512]{1,0:T(8,128)(2,1)} %w_ref.4, f32[1,512]{1,0:T(1,128)} %bitcast.10), custom_call_target="tpu_custom_call" | custom-call | flops 301989888 | bytes 3538944 | tf_op jit(solution)/shard_map/right_factor/pallas_call | solution.py:247
  5.0 0.0 copy-start.7
  5.0 7.3 %all-to-all-start = ((bf16[32,96,384]{2,1,0:T(8,128)(2,1)}), bf16[32,96,384]{2,1,0:T(8,128)(2,1)S(1)}, u32[]{:S(2)}, u32[]{:S(2)}) async-start(bf16[32,96,384]{2,1,0:T(8,128)(2,1)} %bitcast.20), calls=%async_computation | async-start | bytes 4718592 | tf_op jit(solution)/shard_map/all_to_all | solution.py:264
  12.4 0.0 copy-start.3
  12.4 0.9 copy-done.3
  13.3 0.8 copy-done.4
  14.1 2.7 %left_factor.1 = (bf16[96,384]{1,0:T(8,128)(2,1)S(1)}, bf16[96,384]{1,0:T(8,128)(2,1)S(1)}, bf16[96,384]{1,0:T(8,128)(2,1)S(1)}, bf16[96,384]{1,0:T(8,128)(2,1)S...) custom-call(bf16[12,384,128]{2,1,0:T(8,128)(2,1)S(1)} %copy-done, ...), custom_call_target="tpu_custom_call" | custom-call | flops 301989888 | bytes 3538944 | tf_op jit(solution)/shard_map/left_factor/pallas_call | solution.py:270
  16.8 0.0 copy-start.1
  16.8 1.0 copy-done.1
  17.8 0.2 collective-permute-start
  18.1 1.7 %collective-permute-start.1 = (bf16[96,384]{1,0:T(8,128)(2,1)S(1)}, bf16[96,384]{1,0:T(8,128)(2,1)S(1)}, u32[]{:S(2)}, u32[]{:S(2)}) collective-permute-start(bf16[96,384]{1,0:T(8,128)(2,1)S(1)} %get-tuple-element.35), channel_id=1, source_target_pairs={{0,2},{1,3},{2,0},{3,1},{4,6},{5,7},{6,4},{7,5},{8,10},{9,11},{10,... | collective-permute-start | bytes 221192 | tf_op jit(solution)/shard_map/ppermute | solution.py:268
  19.7 1.1 %collective-permute-start.10 = (bf16[96,384]{1,0:T(8,128)(2,1)S(1)}, bf16[96,384]{1,0:T(8,128)(2,1)S(1)}, u32[]{:S(2)}, u32[]{:S(2)}) collective-permute-start(bf16[96,384]{1,0:T(8,128)(2,1)S(1)} %get-tuple-element.44), channel_id=1, source_target_pairs={{0,11},{1,10},{2,9},{3,8},{4,15},{5,14},{6,13},{7,12},{8,3},{9,2},... | collective-permute-start | bytes 221192 | tf_op jit(solution)/shard_map/ppermute | solution.py:268
  20.9 1.5 %collective-permute-start.11 = (bf16[96,384]{1,0:T(8,128)(2,1)S(1)}, bf16[96,384]{1,0:T(8,128)(2,1)S(1)}, u32[]{:S(2)}, u32[]{:S(2)}) collective-permute-start(bf16[96,384]{1,0:T(8,128)(2,1)S(1)} %get-tuple-element.45), channel_id=1, source_target_pairs={{0,12},{1,13},{2,14},{3,15},{4,8},{5,9},{6,10},{7,11},{8,4},{9,5},... | collective-permute-start | bytes 221192 | tf_op jit(solution)/shard_map/ppermute | solution.py:268
  22.3 1.2 %collective-permute-start.12 = (bf16[96,384]{1,0:T(8,128)(2,1)S(1)}, bf16[96,384]{1,0:T(8,128)(2,1)S(1)}, u32[]{:S(2)}, u32[]{:S(2)}) collective-permute-start(bf16[96,384]{1,0:T(8,128)(2,1)S(1)} %get-tuple-element.46), channel_id=1, source_target_pairs={{0,13},{1,12},{2,15},{3,14},{4,9},{5,8},{6,11},{7,10},{8,5},{9,4},... | collective-permute-start | bytes 221192 | tf_op jit(solution)/shard_map/ppermute | solution.py:268
  23.6 2.4 %collective-permute-start.13 = (bf16[96,384]{1,0:T(8,128)(2,1)S(1)}, bf16[96,384]{1,0:T(8,128)(2,1)S(1)}, u32[]{:S(2)}, u32[]{:S(2)}) collective-permute-start(bf16[96,384]{1,0:T(8,128)(2,1)S(1)} %get-tuple-element.47), channel_id=1, source_target_pairs={{0,14},{1,15},{2,12},{3,13},{4,10},{5,11},{6,8},{7,9},{8,6},{9,7},... | collective-permute-start | bytes 221192 | tf_op jit(solution)/shard_map/ppermute | solution.py:268
  25.9 5.3 %collective-permute-done.1.refs_2_ = bf16[96,384]{1,0:T(8,128)(2,1)S(1)} collective-permute-done((bf16[96,384]{1,0:T(8,128)(2,1)S(1)}, bf16[96,384]{1,0:T(8,128)(2,1)S(1)}, u32[]{:S(2)}, u32[]{:S(2)}) %collective-permute-start.1) | collective-permute-done | bytes 73760 | tf_op jit(solution)/shard_map/ppermute | solution.py:268
  31.3 22.2 %collective-permute-done.10.refs_11_ = bf16[96,384]{1,0:T(8,128)(2,1)S(1)} collective-permute-done((bf16[96,384]{1,0:T(8,128)(2,1)S(1)}, bf16[96,384]{1,0:T(8,128)(2,1)S(1)}, u32[]{:S(2)}, u32[]{:S(2)}) %collective-permute-start.10) | collective-permute-done | bytes 73760 | tf_op jit(solution)/shard_map/ppermute | solution.py:268
  53.5 0.2 collective-permute-start.2
  53.7 1.3 %collective-permute-done.11.refs_12_ = bf16[96,384]{1,0:T(8,128)(2,1)S(1)} collective-permute-done((bf16[96,384]{1,0:T(8,128)(2,1)S(1)}, bf16[96,384]{1,0:T(8,128)(2,1)S(1)}, u32[]{:S(2)}, u32[]{:S(2)}) %collective-permute-start.11) | collective-permute-done | bytes 73760 | tf_op jit(solution)/shard_map/ppermute | solution.py:268
  55.1 1.5 %collective-permute-start.3 = (bf16[96,384]{1,0:T(8,128)(2,1)S(1)}, bf16[96,384]{1,0:T(8,128)(2,1)S(1)}, u32[]{:S(2)}, u32[]{:S(2)}) collective-permute-start(bf16[96,384]{1,0:T(8,128)(2,1)S(1)} %get-tuple-element.37), channel_id=1, source_target_pairs={{0,4},{1,5},{2,6},{3,7},{4,0},{5,1},{6,2},{7,3},{8,12},{9,13},{10,... | collective-permute-start | bytes 221192 | tf_op jit(solution)/shard_map/ppermute | solution.py:268
  56.5 0.4 collective-permute-done.12.refs_13_
  56.9 0.0 collective-permute-start.4
  57.0 1.6 %collective-permute-done.13.refs_14_ = bf16[96,384]{1,0:T(8,128)(2,1)S(1)} collective-permute-done((bf16[96,384]{1,0:T(8,128)(2,1)S(1)}, bf16[96,384]{1,0:T(8,128)(2,1)S(1)}, u32[]{:S(2)}, u32[]{:S(2)}) %collective-permute-start.13) | collective-permute-done | bytes 73760 | tf_op jit(solution)/shard_map/ppermute | solution.py:268
  58.6 2.2 %collective-permute-start.5 = (bf16[96,384]{1,0:T(8,128)(2,1)S(1)}, bf16[96,384]{1,0:T(8,128)(2,1)S(1)}, u32[]{:S(2)}, u32[]{:S(2)}) collective-permute-start(bf16[96,384]{1,0:T(8,128)(2,1)S(1)} %get-tuple-element.39), channel_id=1, source_target_pairs={{0,6},{1,7},{2,4},{3,5},{4,2},{5,3},{6,0},{7,1},{8,14},{9,15},{10,... | collective-permute-start | bytes 221192 | tf_op jit(solution)/shard_map/ppermute | solution.py:268
  60.8 0.7 collective-permute-start.6
  61.5 4.6 %collective-permute-start.7 = (bf16[96,384]{1,0:T(8,128)(2,1)S(1)}, bf16[96,384]{1,0:T(8,128)(2,1)S(1)}, u32[]{:S(2)}, u32[]{:S(2)}) collective-permute-start(bf16[96,384]{1,0:T(8,128)(2,1)S(1)} %get-tuple-element.41), channel_id=1, source_target_pairs={{0,8},{1,9},{2,10},{3,11},{4,12},{5,13},{6,14},{7,15},{8,0},{9,1},... | collective-permute-start | bytes 221192 | tf_op jit(solution)/shard_map/ppermute | solution.py:268
  66.1 1.2 %collective-permute-start.8 = (bf16[96,384]{1,0:T(8,128)(2,1)S(1)}, bf16[96,384]{1,0:T(8,128)(2,1)S(1)}, u32[]{:S(2)}, u32[]{:S(2)}) collective-permute-start(bf16[96,384]{1,0:T(8,128)(2,1)S(1)} %get-tuple-element.42), channel_id=1, source_target_pairs={{0,9},{1,8},{2,11},{3,10},{4,13},{5,12},{6,15},{7,14},{8,1},{9,0},... | collective-permute-start | bytes 221192 | tf_op jit(solution)/shard_map/ppermute | solution.py:268
  67.2 5.2 %collective-permute-start.9 = (bf16[96,384]{1,0:T(8,128)(2,1)S(1)}, bf16[96,384]{1,0:T(8,128)(2,1)S(1)}, u32[]{:S(2)}, u32[]{:S(2)}) collective-permute-start(bf16[96,384]{1,0:T(8,128)(2,1)S(1)} %get-tuple-element.43), channel_id=1, source_target_pairs={{0,10},{1,11},{2,8},{3,9},{4,14},{5,15},{6,12},{7,13},{8,2},{9,3},... | collective-permute-start | bytes 221192 | tf_op jit(solution)/shard_map/ppermute | solution.py:268
  72.4 2.4 %collective-permute-done.9.refs_10_ = bf16[96,384]{1,0:T(8,128)(2,1)S(1)} collective-permute-done((bf16[96,384]{1,0:T(8,128)(2,1)S(1)}, bf16[96,384]{1,0:T(8,128)(2,1)S(1)}, u32[]{:S(2)}, u32[]{:S(2)}) %collective-permute-start.9) | collective-permute-done | bytes 73760 | tf_op jit(solution)/shard_map/ppermute | solution.py:268
  74.9 0.6 gather_left.1.left_ref
  75.4 2.7 %far_products.1 = (bf16[96,384]{1,0:T(8,128)(2,1)}, bf16[96,384]{1,0:T(8,128)(2,1)}, bf16[96,384]{1,0:T(8,128)(2,1)}, bf16[96,384]{1,0:T(8,128)(2,1)}, bf16[96,3...) custom-call(bf16[3072,384]{1,0:T(8,128)(2,1)S(1)} %bitcast.9, ...), custom_call_target="tpu_custom_call" | custom-call | flops 113246208 | bytes 3538944 | tf_op jit(solution)/shard_map/far_products/pallas_call | solution.py:333
  78.1 2.0 %collective-permute-start.15 = (bf16[96,384]{1,0:T(8,128)(2,1)}, bf16[96,384]{1,0:T(8,128)(2,1)S(1)}, u32[]{:S(2)}, u32[]{:S(2)}) collective-permute-start(bf16[96,384]{1,0:T(8,128)(2,1)} %get-tuple-element.50), channel_id=1, source_target_pairs={{0,8},{1,9},{2,10},{3,11},{4,12},{5,13},{6,14},{7,15},{8,0},{9,1},... | collective-permute-start | bytes 221192 | tf_op jit(solution)/shard_map/ppermute | solution.py:268
  80.1 1.1 %collective-permute-start.17 = (bf16[96,384]{1,0:T(8,128)(2,1)}, bf16[96,384]{1,0:T(8,128)(2,1)S(1)}, u32[]{:S(2)}, u32[]{:S(2)}) collective-permute-start(bf16[96,384]{1,0:T(8,128)(2,1)} %get-tuple-element.52), channel_id=1, source_target_pairs={{0,10},{1,11},{2,8},{3,9},{4,14},{5,15},{6,12},{7,13},{8,2},{9,3},... | collective-permute-start | bytes 221192 | tf_op jit(solution)/shard_map/ppermute | solution.py:268
  81.3 2.0 %near_products.1 = bf16[8,96,384]{2,1,0:T(8,128)(2,1)} custom-call(bf16[8,192,384]{2,1,0:T(8,128)(2,1)S(1)} %gather_left.1.left_ref, bf16[8,384,384]{2,1,0:T(8,128)(2,1)S(1)} %get-tuple-element.49.right_ref), custom_call_target="tpu_custom_call" | custom-call | flops 113246208 | bytes 3538944 | tf_op jit(solution)/shard_map/near_products/pallas_call | solution.py:343
  83.3 0.0 copy-start.10
  83.4 3.9 %all-to-all-start.1 = ((bf16[8,96,384]{2,1,0:T(8,128)(2,1)}), bf16[8,96,384]{2,1,0:T(8,128)(2,1)S(1)}, u32[]{:S(2)}, u32[]{:S(2)}) async-start(bf16[8,96,384]{2,1,0:T(8,128)(2,1)} %near_products.1), calls=%async_computation.1 | async-start | bytes 1179648 | tf_op jit(solution)/shard_map/all_to_all | solution.py:352
  87.3 2.6 %collective-permute-start.18 = (bf16[96,384]{1,0:T(8,128)(2,1)S(1)}, bf16[96,384]{1,0:T(8,128)(2,1)S(1)}, u32[]{:S(2)}, u32[]{:S(2)}) collective-permute-start(bf16[96,384]{1,0:T(8,128)(2,1)S(1)} %copy-done.17), channel_id=1, source_target_pairs={{0,11},{1,10},{2,9},{3,8},{4,15},{5,14},{6,13},{7,12},{8,3},{9,2},... | collective-permute-start | bytes 221192 | tf_op jit(solution)/shard_map/ppermute | solution.py:268
  89.9 1.6 %collective-permute-start.19 = (bf16[96,384]{1,0:T(8,128)(2,1)S(1)}, bf16[96,384]{1,0:T(8,128)(2,1)S(1)}, u32[]{:S(2)}, u32[]{:S(2)}) collective-permute-start(bf16[96,384]{1,0:T(8,128)(2,1)S(1)} %copy-done.16), channel_id=1, source_target_pairs={{0,12},{1,13},{2,14},{3,15},{4,8},{5,9},{6,10},{7,11},{8,4},{9,5},... | collective-permute-start | bytes 221192 | tf_op jit(solution)/shard_map/ppermute | solution.py:268
  91.5 1.1 collective-permute-start.20
  92.5 1.5 %collective-permute-start.21 = (bf16[96,384]{1,0:T(8,128)(2,1)S(1)}, bf16[96,384]{1,0:T(8,128)(2,1)S(1)}, u32[]{:S(2)}, u32[]{:S(2)}) collective-permute-start(bf16[96,384]{1,0:T(8,128)(2,1)S(1)} %copy-done.14), channel_id=1, source_target_pairs={{0,14},{1,15},{2,12},{3,13},{4,10},{5,11},{6,8},{7,9},{8,6},{9,7},... | collective-permute-start | bytes 221192 | tf_op jit(solution)/shard_map/ppermute | solution.py:268
  94.1 2.0 %collective-permute-start.22 = (bf16[96,384]{1,0:T(8,128)(2,1)S(1)}, bf16[96,384]{1,0:T(8,128)(2,1)S(1)}, u32[]{:S(2)}, u32[]{:S(2)}) collective-permute-start(bf16[96,384]{1,0:T(8,128)(2,1)S(1)} %copy-done.13), channel_id=1, source_target_pairs={{0,15},{1,14},{2,13},{3,12},{4,11},{5,10},{6,9},{7,8},{8,7},{9,6},... | collective-permute-start | bytes 221192 | tf_op jit(solution)/shard_map/ppermute | solution.py:268
  96.1 0.1 prepare.1
  96.3 1.2 %collective-permute-done.19.refs_4_ = bf16[96,384]{1,0:T(8,128)(2,1)S(1)} collective-permute-done((bf16[96,384]{1,0:T(8,128)(2,1)S(1)}, bf16[96,384]{1,0:T(8,128)(2,1)S(1)}, u32[]{:S(2)}, u32[]{:S(2)}) %collective-permute-start.19) | collective-permute-done | bytes 73760 | tf_op jit(solution)/shard_map/ppermute | solution.py:268
  97.4 1.8 %collective-permute-done.20.refs_5_ = bf16[96,384]{1,0:T(8,128)(2,1)S(1)} collective-permute-done((bf16[96,384]{1,0:T(8,128)(2,1)S(1)}, bf16[96,384]{1,0:T(8,128)(2,1)S(1)}, u32[]{:S(2)}, u32[]{:S(2)}) %collective-permute-start.20) | collective-permute-done | bytes 73760 | tf_op jit(solution)/shard_map/ppermute | solution.py:268
  99.2 1.7 %collective-permute-done.21.refs_6_ = bf16[96,384]{1,0:T(8,128)(2,1)S(1)} collective-permute-done((bf16[96,384]{1,0:T(8,128)(2,1)S(1)}, bf16[96,384]{1,0:T(8,128)(2,1)S(1)}, u32[]{:S(2)}, u32[]{:S(2)}) %collective-permute-start.21) | collective-permute-done | bytes 73760 | tf_op jit(solution)/shard_map/ppermute | solution.py:268
  100.9 0.9 collective-permute-done.22.refs_7_
  101.9 1.8 %all-to-all-done.1.near_ref = bf16[8,96,384]{2,1,0:T(8,128)(2,1)S(1)} async-done(((bf16[8,96,384]{2,1,0:T(8,128)(2,1)}), bf16[8,96,384]{2,1,0:T(8,128)(2,1)S(1)}, u32[]{:S(2)}, u32[]{:S(2)}) %all-to-all-start.1) | async-done | bytes 589856 | tf_op jit(solution)/shard_map/all_to_all | solution.py:352
  103.6 2.1 %update.1 = bf16[12,384,128]{2,1,0:T(8,128)(2,1)} custom-call(bf16[8,96,384]{2,1,0:T(8,128)(2,1)S(1)} %all-to-all-done.1.near_ref, bf16[96,384]{1,0:T(8,128)(2,1)S(1)} %collective-permute-done.15.refs_0_, bf16[96,384]{1,0:T(8,128)(2,1)S(1)} %collective-permute-done.16.refs_1_, bf16[96,384]{1,0:T(8,128)(2,1)S(1)} %collective-permute-done.17.refs_2_, ...), custom_call_target="tpu_custom_call" | custom-call | flops 150994944 | bytes 3538944 | tf_op jit(solution)/shard_map/update/pallas_call | solution.py:365
  (45 shorter events, 0.1 us)
Async XLA Ops:
  5.0 7.4 %copy-start = (bf16[12,384,128]{2,1,0:T(8,128)(2,1)S(1)}, bf16[12,384,128]{2,1,0:T(8,128)(2,1)}, u32[]{:S(2)}) copy-start(bf16[12,384,128]{2,1,0:T(8,128)(2,1)} %pair_ref.3) | copy-start | bytes 3538948
  5.0 7.4 %copy-start.5 = (f32[512]{0:T(512)S(1)}, f32[512]{0:T(512)}, u32[]{:S(2)}) copy-start(f32[512]{0:T(512)} %param.15) | copy-start | bytes 6148
  5.0 7.4 %copy-start.6 = (f32[128]{0:T(128)S(1)}, f32[128]{0:T(128)}, u32[]{:S(2)}) copy-start(f32[128]{0:T(128)} %param.12) | copy-start | bytes 1540
  5.0 7.4 %copy-start.7 = (f32[128]{0:T(128)S(1)}, f32[128]{0:T(128)}, u32[]{:S(2)}) copy-start(f32[128]{0:T(128)} %param.13) | copy-start | bytes 1540
  5.0 7.4 %copy-start.8 = (f32[128]{0:T(128)S(1)}, f32[128]{0:T(128)}, u32[]{:S(2)}) copy-start(f32[128]{0:T(128)} %param.17) | copy-start | bytes 1540
  5.0 70.4 %all-to-all-start = ((bf16[32,96,384]{2,1,0:T(8,128)(2,1)}), bf16[32,96,384]{2,1,0:T(8,128)(2,1)S(1)}, u32[]{:S(2)}, u32[]{:S(2)}) async-start(bf16[32,96,384]{2,1,0:T(8,128)(2,1)} %bitcast.20), calls=%async_computation | async-start | bytes 4718592 | tf_op jit(solution)/shard_map/all_to_all | solution.py:264
  12.4 0.9 copy-start.3
  13.3 0.8 copy-start.4
  16.8 1.0 copy-start.1
  17.8 5.8 %collective-permute-start = (bf16[96,384]{1,0:T(8,128)(2,1)S(1)}, bf16[96,384]{1,0:T(8,128)(2,1)S(1)}, u32[]{:S(2)}, u32[]{:S(2)}) collective-permute-start(bf16[96,384]{1,0:T(8,128)(2,1)S(1)} %get-tuple-element.34), channel_id=1, source_target_pairs={{0,1},{1,0},{2,3},{3,2},{4,5},{5,4},{6,7},{7,6},{8,9},{9,8},{10,11... | collective-permute-start | bytes 221192 | tf_op jit(solution)/shard_map/ppermute | solution.py:268
  18.1 13.2 %collective-permute-start.1 = (bf16[96,384]{1,0:T(8,128)(2,1)S(1)}, bf16[96,384]{1,0:T(8,128)(2,1)S(1)}, u32[]{:S(2)}, u32[]{:S(2)}) collective-permute-start(bf16[96,384]{1,0:T(8,128)(2,1)S(1)} %get-tuple-element.35), channel_id=1, source_target_pairs={{0,2},{1,3},{2,0},{3,1},{4,6},{5,7},{6,4},{7,5},{8,10},{9,11},{10,... | collective-permute-start | bytes 221192 | tf_op jit(solution)/shard_map/ppermute | solution.py:268
  19.7 33.8 %collective-permute-start.10 = (bf16[96,384]{1,0:T(8,128)(2,1)S(1)}, bf16[96,384]{1,0:T(8,128)(2,1)S(1)}, u32[]{:S(2)}, u32[]{:S(2)}) collective-permute-start(bf16[96,384]{1,0:T(8,128)(2,1)S(1)} %get-tuple-element.44), channel_id=1, source_target_pairs={{0,11},{1,10},{2,9},{3,8},{4,15},{5,14},{6,13},{7,12},{8,3},{9,2},... | collective-permute-start | bytes 221192 | tf_op jit(solution)/shard_map/ppermute | solution.py:268
  20.9 34.2 %collective-permute-start.11 = (bf16[96,384]{1,0:T(8,128)(2,1)S(1)}, bf16[96,384]{1,0:T(8,128)(2,1)S(1)}, u32[]{:S(2)}, u32[]{:S(2)}) collective-permute-start(bf16[96,384]{1,0:T(8,128)(2,1)S(1)} %get-tuple-element.45), channel_id=1, source_target_pairs={{0,12},{1,13},{2,14},{3,15},{4,8},{5,9},{6,10},{7,11},{8,4},{9,5},... | collective-permute-start | bytes 221192 | tf_op jit(solution)/shard_map/ppermute | solution.py:268
  22.3 34.6 %collective-permute-start.12 = (bf16[96,384]{1,0:T(8,128)(2,1)S(1)}, bf16[96,384]{1,0:T(8,128)(2,1)S(1)}, u32[]{:S(2)}, u32[]{:S(2)}) collective-permute-start(bf16[96,384]{1,0:T(8,128)(2,1)S(1)} %get-tuple-element.46), channel_id=1, source_target_pairs={{0,13},{1,12},{2,15},{3,14},{4,9},{5,8},{6,11},{7,10},{8,5},{9,4},... | collective-permute-start | bytes 221192 | tf_op jit(solution)/shard_map/ppermute | solution.py:268
  23.6 35.0 %collective-permute-start.13 = (bf16[96,384]{1,0:T(8,128)(2,1)S(1)}, bf16[96,384]{1,0:T(8,128)(2,1)S(1)}, u32[]{:S(2)}, u32[]{:S(2)}) collective-permute-start(bf16[96,384]{1,0:T(8,128)(2,1)S(1)} %get-tuple-element.47), channel_id=1, source_target_pairs={{0,14},{1,15},{2,12},{3,13},{4,10},{5,11},{6,8},{7,9},{8,6},{9,7},... | collective-permute-start | bytes 221192 | tf_op jit(solution)/shard_map/ppermute | solution.py:268
  31.3 29.5 %collective-permute-start.14 = (bf16[96,384]{1,0:T(8,128)(2,1)S(1)}, bf16[96,384]{1,0:T(8,128)(2,1)S(1)}, u32[]{:S(2)}, u32[]{:S(2)}) collective-permute-start(bf16[96,384]{1,0:T(8,128)(2,1)S(1)} %get-tuple-element.48), channel_id=1, source_target_pairs={{0,15},{1,14},{2,13},{3,12},{4,11},{5,10},{6,9},{7,8},{8,7},{9,6},... | collective-permute-start | bytes 221192 | tf_op jit(solution)/shard_map/ppermute | solution.py:268
  53.5 8.0 %collective-permute-start.2 = (bf16[96,384]{1,0:T(8,128)(2,1)S(1)}, bf16[96,384]{1,0:T(8,128)(2,1)S(1)}, u32[]{:S(2)}, u32[]{:S(2)}) collective-permute-start(bf16[96,384]{1,0:T(8,128)(2,1)S(1)} %get-tuple-element.36), channel_id=1, source_target_pairs={{0,3},{1,2},{2,1},{3,0},{4,7},{5,6},{6,5},{7,4},{8,11},{9,10},{10,... | collective-permute-start | bytes 221192 | tf_op jit(solution)/shard_map/ppermute | solution.py:268
  55.1 11.0 %collective-permute-start.3 = (bf16[96,384]{1,0:T(8,128)(2,1)S(1)}, bf16[96,384]{1,0:T(8,128)(2,1)S(1)}, u32[]{:S(2)}, u32[]{:S(2)}) collective-permute-start(bf16[96,384]{1,0:T(8,128)(2,1)S(1)} %get-tuple-element.37), channel_id=1, source_target_pairs={{0,4},{1,5},{2,6},{3,7},{4,0},{5,1},{6,2},{7,3},{8,12},{9,13},{10,... | collective-permute-start | bytes 221192 | tf_op jit(solution)/shard_map/ppermute | solution.py:268
  56.9 10.3 %collective-permute-start.4 = (bf16[96,384]{1,0:T(8,128)(2,1)S(1)}, bf16[96,384]{1,0:T(8,128)(2,1)S(1)}, u32[]{:S(2)}, u32[]{:S(2)}) collective-permute-start(bf16[96,384]{1,0:T(8,128)(2,1)S(1)} %get-tuple-element.38), channel_id=1, source_target_pairs={{0,5},{1,4},{2,7},{3,6},{4,1},{5,0},{6,3},{7,2},{8,13},{9,12},{10,... | collective-permute-start | bytes 221192 | tf_op jit(solution)/shard_map/ppermute | solution.py:268
  58.6 13.9 %collective-permute-start.5 = (bf16[96,384]{1,0:T(8,128)(2,1)S(1)}, bf16[96,384]{1,0:T(8,128)(2,1)S(1)}, u32[]{:S(2)}, u32[]{:S(2)}) collective-permute-start(bf16[96,384]{1,0:T(8,128)(2,1)S(1)} %get-tuple-element.39), channel_id=1, source_target_pairs={{0,6},{1,7},{2,4},{3,5},{4,2},{5,3},{6,0},{7,1},{8,14},{9,15},{10,... | collective-permute-start | bytes 221192 | tf_op jit(solution)/shard_map/ppermute | solution.py:268
  60.8 11.6 %collective-permute-start.6 = (bf16[96,384]{1,0:T(8,128)(2,1)S(1)}, bf16[96,384]{1,0:T(8,128)(2,1)S(1)}, u32[]{:S(2)}, u32[]{:S(2)}) collective-permute-start(bf16[96,384]{1,0:T(8,128)(2,1)S(1)} %get-tuple-element.40), channel_id=1, source_target_pairs={{0,7},{1,6},{2,5},{3,4},{4,3},{5,2},{6,1},{7,0},{8,15},{9,14},{10,... | collective-permute-start | bytes 221192 | tf_op jit(solution)/shard_map/ppermute | solution.py:268
  61.5 10.9 %collective-permute-start.7 = (bf16[96,384]{1,0:T(8,128)(2,1)S(1)}, bf16[96,384]{1,0:T(8,128)(2,1)S(1)}, u32[]{:S(2)}, u32[]{:S(2)}) collective-permute-start(bf16[96,384]{1,0:T(8,128)(2,1)S(1)} %get-tuple-element.41), channel_id=1, source_target_pairs={{0,8},{1,9},{2,10},{3,11},{4,12},{5,13},{6,14},{7,15},{8,0},{9,1},... | collective-permute-start | bytes 221192 | tf_op jit(solution)/shard_map/ppermute | solution.py:268
  66.1 6.4 %collective-permute-start.8 = (bf16[96,384]{1,0:T(8,128)(2,1)S(1)}, bf16[96,384]{1,0:T(8,128)(2,1)S(1)}, u32[]{:S(2)}, u32[]{:S(2)}) collective-permute-start(bf16[96,384]{1,0:T(8,128)(2,1)S(1)} %get-tuple-element.42), channel_id=1, source_target_pairs={{0,9},{1,8},{2,11},{3,10},{4,13},{5,12},{6,15},{7,14},{8,1},{9,0},... | collective-permute-start | bytes 221192 | tf_op jit(solution)/shard_map/ppermute | solution.py:268
  67.2 7.6 %collective-permute-start.9 = (bf16[96,384]{1,0:T(8,128)(2,1)S(1)}, bf16[96,384]{1,0:T(8,128)(2,1)S(1)}, u32[]{:S(2)}, u32[]{:S(2)}) collective-permute-start(bf16[96,384]{1,0:T(8,128)(2,1)S(1)} %get-tuple-element.43), channel_id=1, source_target_pairs={{0,10},{1,11},{2,8},{3,9},{4,14},{5,15},{6,12},{7,13},{8,2},{9,3},... | collective-permute-start | bytes 221192 | tf_op jit(solution)/shard_map/ppermute | solution.py:268
  78.1 13.3 %collective-permute-start.15 = (bf16[96,384]{1,0:T(8,128)(2,1)}, bf16[96,384]{1,0:T(8,128)(2,1)S(1)}, u32[]{:S(2)}, u32[]{:S(2)}) collective-permute-start(bf16[96,384]{1,0:T(8,128)(2,1)} %get-tuple-element.50), channel_id=1, source_target_pairs={{0,8},{1,9},{2,10},{3,11},{4,12},{5,13},{6,14},{7,15},{8,0},{9,1},... | collective-permute-start | bytes 221192 | tf_op jit(solution)/shard_map/ppermute | solution.py:268
  80.1 12.4 %collective-permute-start.16 = (bf16[96,384]{1,0:T(8,128)(2,1)}, bf16[96,384]{1,0:T(8,128)(2,1)S(1)}, u32[]{:S(2)}, u32[]{:S(2)}) collective-permute-start(bf16[96,384]{1,0:T(8,128)(2,1)} %get-tuple-element.51), channel_id=1, source_target_pairs={{0,9},{1,8},{2,11},{3,10},{4,13},{5,12},{6,15},{7,14},{8,1},{9,0},... | collective-permute-start | bytes 221192 | tf_op jit(solution)/shard_map/ppermute | solution.py:268
  80.1 13.9 %collective-permute-start.17 = (bf16[96,384]{1,0:T(8,128)(2,1)}, bf16[96,384]{1,0:T(8,128)(2,1)S(1)}, u32[]{:S(2)}, u32[]{:S(2)}) collective-permute-start(bf16[96,384]{1,0:T(8,128)(2,1)} %get-tuple-element.52), channel_id=1, source_target_pairs={{0,10},{1,11},{2,8},{3,9},{4,14},{5,15},{6,12},{7,13},{8,2},{9,3},... | collective-permute-start | bytes 221192 | tf_op jit(solution)/shard_map/ppermute | solution.py:268
  83.3 4.0 %copy-start.17 = (bf16[96,384]{1,0:T(8,128)(2,1)S(1)}, bf16[96,384]{1,0:T(8,128)(2,1)}, u32[]{:S(2)}) copy-start(bf16[96,384]{1,0:T(8,128)(2,1)} %get-tuple-element.53) | copy-start | bytes 221188
  83.3 6.6 %copy-start.16 = (bf16[96,384]{1,0:T(8,128)(2,1)S(1)}, bf16[96,384]{1,0:T(8,128)(2,1)}, u32[]{:S(2)}) copy-start(bf16[96,384]{1,0:T(8,128)(2,1)} %get-tuple-element.54) | copy-start | bytes 221188
  83.3 8.1 %copy-start.15 = (bf16[96,384]{1,0:T(8,128)(2,1)S(1)}, bf16[96,384]{1,0:T(8,128)(2,1)}, u32[]{:S(2)}) copy-start(bf16[96,384]{1,0:T(8,128)(2,1)} %get-tuple-element.55) | copy-start | bytes 221188
  83.3 9.2 %copy-start.14 = (bf16[96,384]{1,0:T(8,128)(2,1)S(1)}, bf16[96,384]{1,0:T(8,128)(2,1)}, u32[]{:S(2)}) copy-start(bf16[96,384]{1,0:T(8,128)(2,1)} %get-tuple-element.56) | copy-start | bytes 221188
  83.3 10.7 %copy-start.13 = (bf16[96,384]{1,0:T(8,128)(2,1)S(1)}, bf16[96,384]{1,0:T(8,128)(2,1)}, u32[]{:S(2)}) copy-start(bf16[96,384]{1,0:T(8,128)(2,1)} %get-tuple-element.57) | copy-start | bytes 221188
  83.3 12.8 %copy-start.10 = (bf16[128,128]{1,0:T(8,128)(2,1)S(1)}, bf16[128,128]{1,0:T(8,128)(2,1)}, u32[]{:S(2)}) copy-start(bf16[128,128]{1,0:T(8,128)(2,1)} %w_ref.5) | copy-start | bytes 98308
  83.3 12.8 %copy-start.11 = (f32[128]{0:T(128)S(1)}, f32[128]{0:T(128)}, u32[]{:S(2)}) copy-start(f32[128]{0:T(128)} %param.18) | copy-start | bytes 1540
  83.4 12.8 %copy-start.12 = (f32[128]{0:T(128)S(1)}, f32[128]{0:T(128)}, u32[]{:S(2)}) copy-start(f32[128]{0:T(128)} %param.19) | copy-start | bytes 1540
  83.4 20.3 %all-to-all-start.1 = ((bf16[8,96,384]{2,1,0:T(8,128)(2,1)}), bf16[8,96,384]{2,1,0:T(8,128)(2,1)S(1)}, u32[]{:S(2)}, u32[]{:S(2)}) async-start(bf16[8,96,384]{2,1,0:T(8,128)(2,1)} %near_products.1), calls=%async_computation.1 | async-start | bytes 1179648 | tf_op jit(solution)/shard_map/all_to_all | solution.py:352
  87.3 9.0 %collective-permute-start.18 = (bf16[96,384]{1,0:T(8,128)(2,1)S(1)}, bf16[96,384]{1,0:T(8,128)(2,1)S(1)}, u32[]{:S(2)}, u32[]{:S(2)}) collective-permute-start(bf16[96,384]{1,0:T(8,128)(2,1)S(1)} %copy-done.17), channel_id=1, source_target_pairs={{0,11},{1,10},{2,9},{3,8},{4,15},{5,14},{6,13},{7,12},{8,3},{9,2},... | collective-permute-start | bytes 221192 | tf_op jit(solution)/shard_map/ppermute | solution.py:268
  89.9 7.6 %collective-permute-start.19 = (bf16[96,384]{1,0:T(8,128)(2,1)S(1)}, bf16[96,384]{1,0:T(8,128)(2,1)S(1)}, u32[]{:S(2)}, u32[]{:S(2)}) collective-permute-start(bf16[96,384]{1,0:T(8,128)(2,1)S(1)} %copy-done.16), channel_id=1, source_target_pairs={{0,12},{1,13},{2,14},{3,15},{4,8},{5,9},{6,10},{7,11},{8,4},{9,5},... | collective-permute-start | bytes 221192 | tf_op jit(solution)/shard_map/ppermute | solution.py:268
  91.5 7.8 %collective-permute-start.20 = (bf16[96,384]{1,0:T(8,128)(2,1)S(1)}, bf16[96,384]{1,0:T(8,128)(2,1)S(1)}, u32[]{:S(2)}, u32[]{:S(2)}) collective-permute-start(bf16[96,384]{1,0:T(8,128)(2,1)S(1)} %copy-done.15), channel_id=1, source_target_pairs={{0,13},{1,12},{2,15},{3,14},{4,9},{5,8},{6,11},{7,10},{8,5},{9,4},... | collective-permute-start | bytes 221192 | tf_op jit(solution)/shard_map/ppermute | solution.py:268
  92.5 8.4 %collective-permute-start.21 = (bf16[96,384]{1,0:T(8,128)(2,1)S(1)}, bf16[96,384]{1,0:T(8,128)(2,1)S(1)}, u32[]{:S(2)}, u32[]{:S(2)}) collective-permute-start(bf16[96,384]{1,0:T(8,128)(2,1)S(1)} %copy-done.14), channel_id=1, source_target_pairs={{0,14},{1,15},{2,12},{3,13},{4,10},{5,11},{6,8},{7,9},{8,6},{9,7},... | collective-permute-start | bytes 221192 | tf_op jit(solution)/shard_map/ppermute | solution.py:268
  94.1 7.8 %collective-permute-start.22 = (bf16[96,384]{1,0:T(8,128)(2,1)S(1)}, bf16[96,384]{1,0:T(8,128)(2,1)S(1)}, u32[]{:S(2)}, u32[]{:S(2)}) collective-permute-start(bf16[96,384]{1,0:T(8,128)(2,1)S(1)} %copy-done.13), channel_id=1, source_target_pairs={{0,15},{1,14},{2,13},{3,12},{4,11},{5,10},{6,9},{7,8},{8,7},{9,6},... | collective-permute-start | bytes 221192 | tf_op jit(solution)/shard_map/ppermute | solution.py:268
  96.1 7.5 %copy-start.2 = (bf16[12,384,128]{2,1,0:T(8,128)(2,1)S(1)}, bf16[12,384,128]{2,1,0:T(8,128)(2,1)}, u32[]{:S(2)}) copy-start(bf16[12,384,128]{2,1,0:T(8,128)(2,1)} %copy-done.1) | copy-start | bytes 3538948
  96.1 7.5 %copy-start.9 = (f32[128]{0:T(128)S(1)}, f32[128]{0:T(128)}, u32[]{:S(2)}) copy-start(f32[128]{0:T(128)} %param.21) | copy-start | bytes 1540

commit v14 on v9

--- a/solution.py
+++ b/solution.py
@@ -134,31 +134,32 @@
     ]
 
 
-def multiply(left, right_ref, right, held, store):
-    regroup(slices([right_ref]), right, shuffle(BLOCK, SIZE))
+def regroup_right_kernel(rows_ref, out_ref):
+    regroup(slices([rows_ref]), out_ref, shuffle(BLOCK, SIZE))
+
+
+def regroup_left_kernel(*refs):
+    regroup(slices(refs[:-1]), refs[-1], shuffle(BLOCK, SIZE))
+
+
+def product_kernel(right, near, *refs):
+    lefts = refs[:-3]
+    out_ref, far, held = refs[-3:]
+    rows = lefts[0].shape[0] // BLOCK
+    host = lax.axis_index(("chan", "quarter"))
+    regroup(slices(lefts), far, shuffle(BLOCK, SIZE))
+    for c in range(BLOCK):
+        left = jnp.concatenate([near[c], far[c]], axis=0)
+        held[c] = dot_nt(left, right[c]).astype(bf16)
     back = shuffle(SIZE, BLOCK)
-    for c in range(BLOCK):
-        held[c] = dot_nt(left[c], right[c]).astype(bf16)
-    for s in range(left.shape[1] // SIZE):
+    for s in range(held.shape[1] // SIZE):
         parts = jnp.concatenate([held[c, s * SIZE : (s + 1) * SIZE, :] for c in range(BLOCK)], axis=0)
         moved = dot(back, parts).astype(bf16)
         for i in range(0, SIZE, STEP):
-            store(s * SIZE + i, moved[i * BLOCK : (i + STEP) * BLOCK])
-
-
-def gather_kernel(*refs):
-    regroup(slices(refs[:-1]), refs[-1], shuffle(BLOCK, SIZE))
-
-
-def product_kernel(right_ref, left, out_ref, right, held):
-    rows = left.shape[1] // out_ref.shape[0]
-    host = lax.axis_index(("chan", "quarter"))
-
-    def store(i, values):
-        to, at = divmod(i, rows)
-        out_ref[host ^ to, at * BLOCK : (at + STEP) * BLOCK, :] = values
-
-    multiply(left, right_ref, right, held, store)
+            to, at = divmod(s * SIZE + i, rows)
+            out_ref[host ^ to, at * BLOCK : (at + STEP) * BLOCK, :] = moved[
+                i * BLOCK : (i + STEP) * BLOCK
+            ]
 
 
 def final_kernel(x_ref, gate_ref, g_ref, s_ref, w_ref, b_ref, out_ref, made, leave):
@@ -270,28 +271,56 @@
     )
     lefts = [lefts[0]] + [send(lefts[b], b) for b in reversed(range(1, hosts))][::-1]
 
-    left = pl.pallas_call(
-        gather_kernel,
-        in_specs=[vmem] * hosts,
+    half = hosts // 2
+    near = pl.pallas_call(
+        regroup_left_kernel,
+        in_specs=[vmem] * half,
         out_specs=vmem,
-        out_shape=bfloat(BLOCK, mine, k),
+        out_shape=bfloat(BLOCK, mine // 2, k),
         compiler_params=params(),
-        cost_estimate=cost(2 * work * BLOCK * SIZE, 4 * work),
-        name="gather_left",
-    )(*lefts)
+        cost_estimate=cost(work * BLOCK * SIZE, 2 * work),
+        name="regroup_left",
+    )(*lefts[:half])
 
     span = GATHER * rows
+    gathers = devices // GATHER
+    grouped = pl.BlockSpec((BLOCK, span, k), lambda s: (0, s, 0))
+    if gathers == 1:
+        limit = params()
+        blocks = dict(in_specs=[vmem], out_specs=vmem)
+        rest = dict(in_specs=[vmem] * (2 + half), out_specs=vmem)
+    else:
+        limit = params(60)
+        blocks = dict(
+            grid=(gathers,),
+            in_specs=[pl.BlockSpec((span * BLOCK, k), lambda s: (s, 0))],
+            out_specs=grouped,
+        )
+        rest = dict(
+            grid=(gathers,),
+            in_specs=[grouped, whole((BLOCK, mine // 2, k))] + [whole((tall, k))] * half,
+            out_specs=pl.BlockSpec((hosts, tall, span), lambda s: (0, 0, s)),
+        )
+    right = pl.pallas_call(
+        regroup_right_kernel,
+        **blocks,
+        out_shape=bfloat(BLOCK, devices * rows, k),
+        compiler_params=limit,
+        cost_estimate=cost(1 << 37, 4 * devices * tall * k),
+        name="regroup_right",
+    )(right.reshape(devices * tall, k))
     product = pl.pallas_call(
         product_kernel,
-        grid=(devices // GATHER,),
-        in_specs=[pl.BlockSpec((span * BLOCK, k), lambda s: (s, 0)), whole((BLOCK, mine, k))],
-        out_specs=pl.BlockSpec((hosts, tall, span), lambda s: (0, 0, s)),
+        **rest,
         out_shape=bfloat(hosts, tall, devices * rows),
-        scratch_shapes=[pltpu.VMEM((BLOCK, span, k), bf16), pltpu.VMEM((BLOCK, mine, span), bf16)],
-        compiler_params=params(40),
+        scratch_shapes=[
+            pltpu.VMEM((BLOCK, mine // 2, k), bf16),
+            pltpu.VMEM((BLOCK, mine, span), bf16),
+        ],
+        compiler_params=limit,
         cost_estimate=cost(2 * BLOCK * mine * mine * k, 6 * BLOCK * mine * k),
         name="products",
-    )(right.reshape(devices * tall, k), left)
+    )(right, near, *lefts[half:])
     product = lax.all_to_all(product, in_part, 0, 0, tiled=True)
 
     return pl.pallas_call(

time: 94.5 us -> 93.3 us (0.987)
  waiting for transfers between devices: 30.1 us -> 29.1 us
    ppermute x15, waiting for transfers between devices: 30.1 us -> 22.2 us  [send(): return lax.ppermute(values, everywhere, pairs)]
    all_to_all x1, waiting for transfers between devices: 0.01 us -> 6.88 us  [shards(): lax.all_to_all(right.reshape(devices, tall, k), everywhere, 0, 0, tiled=T...]
    pallas_call x2 -> x3, Pallas kernels: 2.97 us -> 3.09 us  [the longest x1 1.77 us: shards(): pl.pallas_call(product_kernel, **rest, out_shape=bfloat(hosts, tall, devi...]
  transfers between devices with their start and end apart: 16 -> 16, of which waited for: 8 -> 6; matrix products, arithmetic and copies ran while one was open for 0% -> 0% of each run, Pallas kernels for 3% -> 5%
where the time goes in v14:
time: 93.3 us; the launch traced here: 93 us
  waiting for transfers between devices  29.1 us (31%)
  starting transfers between devices  26.4 us (28%)
  blocking collectives  21.1 us (23%)
  Pallas kernels  13.6 us (15%)
  local copies, waits for them, and re-layouts  2.72 us (3%)
    ppermute x15, waiting for transfers between devices, send(): return lax.ppermute(values, everywhere, pairs)  22.2 us
    all_to_all x1, blocking collectives, shards(): product = lax.all_to_all(product, in_part, 0, 0, tiled=True)  21.1 us
    ppermute x15, starting transfers between devices, send(): return lax.ppermute(values, everywhere, pairs)  19 us
    all_to_all x1, starting transfers between devices, shards(): lax.all_to_all(right.reshape(devices, tall, k), everywhere, 0, 0, tiled=T...  7.3 us
    all_to_all x1, waiting for transfers between devices, shards(): lax.all_to_all(right.reshape(devices, tall, k), everywhere, 0, 0, tiled=T...  6.88 us
    pallas_call x1, Pallas kernels, shards(): pl.pallas_call(right_kernel, grid=(steps,), in_specs=[row_block, whole((1...  5 us
    pallas_call x1, Pallas kernels, shards(): pl.pallas_call(left_kernel, grid=(steps,), in_specs=[row_block, whole((1,...  3.39 us
    unnamed x26, local copies, waits for them, and re-layouts  2.72 us
  transfers between devices with their start and end apart: 16, of which 6 were waited for; matrix products, arithmetic and copies ran while one was open for 0% of the time, Pallas kernels for 5%

profile of v14, /device:TPU:0, one launch (start us, length us, event | category | flops | bytes accessed | tf_op | source)
XLA Modules:
  0.0 93.0 jit_solution(8240519446248077544)
XLA Ops:
  0.0 5.0 %right_factor.1 = bf16[2,16,96,384]{3,2,1,0:T(8,128)(2,1)} custom-call(bf16[12,384,128]{2,1,0:T(8,128)(2,1)} %pair_ref.3, f32[1,128]{1,0:T(1,128)} %bitcast.12, f32[1,128]{1,0:T(1,128)} %bitcast.14, bf16[128,512]{1,0:T(8,128)(2,1)} %w_ref.4, f32[1,512]{1,0:T(1,128)} %bitcast.10), custom_call_target="tpu_custom_call" | custom-call | flops 301989888 | bytes 3538944 | tf_op jit(solution)/shard_map/right_factor/pallas_call | solution.py:217
  5.0 0.0 copy-start.8
  5.0 0.0 copy-start.9
  5.0 7.3 %all-to-all-start = ((bf16[32,96,384]{2,1,0:T(8,128)(2,1)}), bf16[32,96,384]{2,1,0:T(8,128)(2,1)S(1)}, u32[]{:S(2)}, u32[]{:S(2)}) async-start(bf16[32,96,384]{2,1,0:T(8,128)(2,1)} %bitcast.20), calls=%async_computation | async-start | bytes 4718592 | tf_op jit(solution)/shard_map/all_to_all | solution.py:234
  12.4 0.0 copy-start.3
  12.4 0.9 copy-done.3
  13.3 0.8 copy-done.5
  14.1 3.4 %left_factor.1 = (bf16[96,384]{1,0:T(8,128)(2,1)S(1)}, bf16[96,384]{1,0:T(8,128)(2,1)S(1)}, bf16[96,384]{1,0:T(8,128)(2,1)S(1)}, bf16[96,384]{1,0:T(8,128)(2,1)S...) custom-call(bf16[12,384,128]{2,1,0:T(8,128)(2,1)S(1)} %copy-done, ...), custom_call_target="tpu_custom_call" | custom-call | flops 301989888 | bytes 3538944 | tf_op jit(solution)/shard_map/left_factor/pallas_call | solution.py:240
  17.5 1.0 %copy-done.1 = bf16[12,384,128]{2,1,0:T(8,128)(2,1)} copy-done((bf16[12,384,128]{2,1,0:T(8,128)(2,1)}, bf16[12,384,128]{2,1,0:T(8,128)(2,1)S(1)}, u32[]{:S(2)}) %copy-start.1) | copy-done | bytes 1179672
  18.5 0.3 collective-permute-start
  18.7 1.7 %collective-permute-start.1 = (bf16[96,384]{1,0:T(8,128)(2,1)S(1)}, bf16[96,384]{1,0:T(8,128)(2,1)S(1)}, u32[]{:S(2)}, u32[]{:S(2)}) collective-permute-start(bf16[96,384]{1,0:T(8,128)(2,1)S(1)} %get-tuple-element.24), channel_id=1, source_target_pairs={{0,2},{1,3},{2,0},{3,1},{4,6},{5,7},{6,4},{7,5},{8,10},{9,11},{10,... | collective-permute-start | bytes 221192 | tf_op jit(solution)/shard_map/ppermute | solution.py:238
  20.4 0.0 collective-permute-start.2
  20.4 1.7 %collective-permute-start.3 = (bf16[96,384]{1,0:T(8,128)(2,1)S(1)}, bf16[96,384]{1,0:T(8,128)(2,1)S(1)}, u32[]{:S(2)}, u32[]{:S(2)}) collective-permute-start(bf16[96,384]{1,0:T(8,128)(2,1)S(1)} %get-tuple-element.26), channel_id=1, source_target_pairs={{0,4},{1,5},{2,6},{3,7},{4,0},{5,1},{6,2},{7,3},{8,12},{9,13},{10,... | collective-permute-start | bytes 221192 | tf_op jit(solution)/shard_map/ppermute | solution.py:238
  22.1 0.1 collective-permute-start.4
  22.2 0.0 collective-permute-done.refs_1_
  22.2 2.6 %collective-permute-start.5 = (bf16[96,384]{1,0:T(8,128)(2,1)S(1)}, bf16[96,384]{1,0:T(8,128)(2,1)S(1)}, u32[]{:S(2)}, u32[]{:S(2)}) collective-permute-start(bf16[96,384]{1,0:T(8,128)(2,1)S(1)} %get-tuple-element.28), channel_id=1, source_target_pairs={{0,6},{1,7},{2,4},{3,5},{4,2},{5,3},{6,0},{7,1},{8,14},{9,15},{10,... | collective-permute-start | bytes 221192 | tf_op jit(solution)/shard_map/ppermute | solution.py:238
  24.8 7.1 %collective-permute-done.1.refs_2_ = bf16[96,384]{1,0:T(8,128)(2,1)S(1)} collective-permute-done((bf16[96,384]{1,0:T(8,128)(2,1)S(1)}, bf16[96,384]{1,0:T(8,128)(2,1)S(1)}, u32[]{:S(2)}, u32[]{:S(2)}) %collective-permute-start.1) | collective-permute-done | bytes 73760 | tf_op jit(solution)/shard_map/ppermute | solution.py:238
  31.9 0.6 collective-permute-start.6
  32.5 0.2 collective-permute-done.2.refs_3_
  32.7 0.3 collective-permute-start.7
  33.0 0.0 collective-permute-done.3.refs_4_
  33.0 2.3 %collective-permute-start.8 = (bf16[96,384]{1,0:T(8,128)(2,1)S(1)}, bf16[96,384]{1,0:T(8,128)(2,1)S(1)}, u32[]{:S(2)}, u32[]{:S(2)}) collective-permute-start(bf16[96,384]{1,0:T(8,128)(2,1)S(1)} %get-tuple-element.31), channel_id=1, source_target_pairs={{0,9},{1,8},{2,11},{3,10},{4,13},{5,12},{6,15},{7,14},{8,1},{9,0},... | collective-permute-start | bytes 221192 | tf_op jit(solution)/shard_map/ppermute | solution.py:238
  35.3 0.0 collective-permute-done.4.refs_5_
  35.3 3.2 %collective-permute-start.9 = (bf16[96,384]{1,0:T(8,128)(2,1)S(1)}, bf16[96,384]{1,0:T(8,128)(2,1)S(1)}, u32[]{:S(2)}, u32[]{:S(2)}) collective-permute-start(bf16[96,384]{1,0:T(8,128)(2,1)S(1)} %get-tuple-element.32), channel_id=1, source_target_pairs={{0,10},{1,11},{2,8},{3,9},{4,14},{5,15},{6,12},{7,13},{8,2},{9,3},... | collective-permute-start | bytes 221192 | tf_op jit(solution)/shard_map/ppermute | solution.py:238
  38.4 3.9 %collective-permute-done.5.refs_6_ = bf16[96,384]{1,0:T(8,128)(2,1)S(1)} collective-permute-done((bf16[96,384]{1,0:T(8,128)(2,1)S(1)}, bf16[96,384]{1,0:T(8,128)(2,1)S(1)}, u32[]{:S(2)}, u32[]{:S(2)}) %collective-permute-start.5) | collective-permute-done | bytes 73760 | tf_op jit(solution)/shard_map/ppermute | solution.py:238
  42.4 0.0 collective-permute-start.10
  42.4 0.8 collective-permute-done.6.refs_7_
  43.2 0.0 collective-permute-start.11
  43.2 0.4 regroup_left.1.near
  43.6 10.1 %collective-permute-done.7.refs_0_ = bf16[96,384]{1,0:T(8,128)(2,1)S(1)} collective-permute-done((bf16[96,384]{1,0:T(8,128)(2,1)S(1)}, bf16[96,384]{1,0:T(8,128)(2,1)S(1)}, u32[]{:S(2)}, u32[]{:S(2)}) %collective-permute-start.7) | collective-permute-done | bytes 73760 | tf_op jit(solution)/shard_map/ppermute | solution.py:238
  53.6 1.9 %collective-permute-start.12 = (bf16[96,384]{1,0:T(8,128)(2,1)}, bf16[96,384]{1,0:T(8,128)(2,1)S(1)}, u32[]{:S(2)}, u32[]{:S(2)}) collective-permute-start(bf16[96,384]{1,0:T(8,128)(2,1)} %get-tuple-element.35), channel_id=1, source_target_pairs={{0,13},{1,12},{2,15},{3,14},{4,9},{5,8},{6,11},{7,10},{8,5},{9,4},... | collective-permute-start | bytes 221192 | tf_op jit(solution)/shard_map/ppermute | solution.py:238
  55.6 0.0 collective-permute-done.8.refs_1_
  55.6 2.8 %collective-permute-start.13 = (bf16[96,384]{1,0:T(8,128)(2,1)}, bf16[96,384]{1,0:T(8,128)(2,1)S(1)}, u32[]{:S(2)}, u32[]{:S(2)}) collective-permute-start(bf16[96,384]{1,0:T(8,128)(2,1)} %get-tuple-element.36), channel_id=1, source_target_pairs={{0,14},{1,15},{2,12},{3,13},{4,10},{5,11},{6,8},{7,9},{8,6},{9,7},... | collective-permute-start | bytes 221192 | tf_op jit(solution)/shard_map/ppermute | solution.py:238
  58.4 0.0 collective-permute-done.9.refs_2_
  58.4 1.7 %collective-permute-start.14 = (bf16[96,384]{1,0:T(8,128)(2,1)}, bf16[96,384]{1,0:T(8,128)(2,1)S(1)}, u32[]{:S(2)}, u32[]{:S(2)}) collective-permute-start(bf16[96,384]{1,0:T(8,128)(2,1)} %get-tuple-element.37), channel_id=1, source_target_pairs={{0,15},{1,14},{2,13},{3,12},{4,11},{5,10},{6,9},{7,8},{8,7},{9,6},... | collective-permute-start | bytes 221192 | tf_op jit(solution)/shard_map/ppermute | solution.py:238
  60.1 6.9 %all-to-all-done = bf16[32,96,384]{2,1,0:T(8,128)(2,1)S(1)} async-done(((bf16[32,96,384]{2,1,0:T(8,128)(2,1)}), bf16[32,96,384]{2,1,0:T(8,128)(2,1)S(1)}, u32[]{:S(2)}, u32[]{:S(2)}) %all-to-all-start) | async-done | bytes 2359328 | tf_op jit(solution)/shard_map/all_to_all | solution.py:234
  66.9 1.0 %regroup_right.1.right = bf16[8,384,384]{2,1,0:T(8,128)(2,1)S(1)} custom-call(bf16[3072,384]{1,0:T(8,128)(2,1)S(1)} %bitcast.9), custom_call_target="tpu_custom_call" | custom-call | flops 137438953472 | bytes 4718592 | tf_op jit(solution)/shard_map/regroup_right/pallas_call | solution.py:304
  67.9 0.0 collective-permute-done.10.refs_3_
  68.0 0.0 collective-permute-done.13.refs_6_
  68.0 0.0 collective-permute-done.14.refs_7_
  68.0 1.8 %products.1 = bf16[16,96,384]{2,1,0:T(8,128)(2,1)S(1)} custom-call(bf16[8,384,384]{2,1,0:T(8,128)(2,1)S(1)} %regroup_right.1.right, bf16[8,96,384]{2,1,0:T(8,128)(2,1)S(1)} %regroup_left.1.near, bf16[96,384]{1,0:T(8,128)(2,1)S(1)} %collective-permute-done.7.refs_0_, bf16[96,384]{1,0:T(8,128)(2,1)S(1)} %collective-permute-done.8.refs_1_, ...), custom_call_target="tpu_custom_call" | custom-call | flops 226492416 | bytes 3538944 | tf_op jit(solution)/shard_map/products/pallas_call | solution.py:312
  69.7 0.0 copy-start.2
  69.8 0.0 copy-start.4
  69.8 0.0 copy-start.10
  69.8 0.0 copy-start.11
  69.8 0.0 copy-start.12
  69.8 21.1 %all_to_all.10.x_ref = bf16[16,96,384]{2,1,0:T(8,128)(2,1)S(1)} all-to-all(bf16[16,96,384]{2,1,0:T(8,128)(2,1)S(1)} %products.1), channel_id=1, replica_groups=mesh['groups'=1,'part'=2,'chan'=8,'quarter'=2] {'chan','quarter'}, dimensions={0} | all-to-all | bytes 2359296 | tf_op jit(solution)/shard_map/all_to_all | solution.py:324
  90.9 2.1 %update.1 = bf16[12,384,128]{2,1,0:T(8,128)(2,1)} custom-call(bf16[16,96,384]{2,1,0:T(8,128)(2,1)S(1)} %all_to_all.10.x_ref, bf16[12,384,128]{2,1,0:T(8,128)(2,1)S(1)} %copy-done.2, f32[1,128]{1,0:T(1,128)S(1)} %bitcast.17, f32[1,128]{1,0:T(1,128)S(1)} %bitcast.18, bf16[128,128]{1,0:T(8,128)(2,1)S(1)} %copy-done.4, f32[1,128]{1,0:T(1,128)S(1)} %bitcast.19), custom_call_target="tpu_custom_call" | custom-call | flops 150994944 | bytes 3538944 | tf_op jit(solution)/shard_map/update/pallas_call | solution.py:326
  (17 shorter events, 0.0 us)
Async XLA Ops:
  5.0 7.4 %copy-start = (bf16[12,384,128]{2,1,0:T(8,128)(2,1)S(1)}, bf16[12,384,128]{2,1,0:T(8,128)(2,1)}, u32[]{:S(2)}) copy-start(bf16[12,384,128]{2,1,0:T(8,128)(2,1)} %pair_ref.3) | copy-start | bytes 3538948
  5.0 7.4 %copy-start.6 = (f32[512]{0:T(512)S(1)}, f32[512]{0:T(512)}, u32[]{:S(2)}) copy-start(f32[512]{0:T(512)} %param.15) | copy-start | bytes 6148
  5.0 7.4 %copy-start.7 = (f32[128]{0:T(128)S(1)}, f32[128]{0:T(128)}, u32[]{:S(2)}) copy-start(f32[128]{0:T(128)} %param.12) | copy-start | bytes 1540
  5.0 7.4 %copy-start.8 = (f32[128]{0:T(128)S(1)}, f32[128]{0:T(128)}, u32[]{:S(2)}) copy-start(f32[128]{0:T(128)} %param.13) | copy-start | bytes 1540
  5.0 7.4 %copy-start.9 = (f32[128]{0:T(128)S(1)}, f32[128]{0:T(128)}, u32[]{:S(2)}) copy-start(f32[128]{0:T(128)} %param.17) | copy-start | bytes 1540
  5.0 61.9 %all-to-all-start = ((bf16[32,96,384]{2,1,0:T(8,128)(2,1)}), bf16[32,96,384]{2,1,0:T(8,128)(2,1)S(1)}, u32[]{:S(2)}, u32[]{:S(2)}) async-start(bf16[32,96,384]{2,1,0:T(8,128)(2,1)} %bitcast.20), calls=%async_computation | async-start | bytes 4718592 | tf_op jit(solution)/shard_map/all_to_all | solution.py:234
  12.4 0.9 copy-start.3
  13.3 0.8 copy-start.5
  17.5 1.0 %copy-start.1 = (bf16[12,384,128]{2,1,0:T(8,128)(2,1)}, bf16[12,384,128]{2,1,0:T(8,128)(2,1)S(1)}, u32[]{:S(2)}) copy-start(bf16[12,384,128]{2,1,0:T(8,128)(2,1)S(1)} %get-tuple-element.38.gate_ref) | copy-start | bytes 3538948
  18.5 3.7 %collective-permute-start = (bf16[96,384]{1,0:T(8,128)(2,1)S(1)}, bf16[96,384]{1,0:T(8,128)(2,1)S(1)}, u32[]{:S(2)}, u32[]{:S(2)}) collective-permute-start(bf16[96,384]{1,0:T(8,128)(2,1)S(1)} %get-tuple-element.23), channel_id=1, source_target_pairs={{0,1},{1,0},{2,3},{3,2},{4,5},{5,4},{6,7},{7,6},{8,9},{9,8},{10,11... | collective-permute-start | bytes 221192 | tf_op jit(solution)/shard_map/ppermute | solution.py:238
  18.7 13.2 %collective-permute-start.1 = (bf16[96,384]{1,0:T(8,128)(2,1)S(1)}, bf16[96,384]{1,0:T(8,128)(2,1)S(1)}, u32[]{:S(2)}, u32[]{:S(2)}) collective-permute-start(bf16[96,384]{1,0:T(8,128)(2,1)S(1)} %get-tuple-element.24), channel_id=1, source_target_pairs={{0,2},{1,3},{2,0},{3,1},{4,6},{5,7},{6,4},{7,5},{8,10},{9,11},{10,... | collective-permute-start | bytes 221192 | tf_op jit(solution)/shard_map/ppermute | solution.py:238
  20.4 12.3 %collective-permute-start.2 = (bf16[96,384]{1,0:T(8,128)(2,1)S(1)}, bf16[96,384]{1,0:T(8,128)(2,1)S(1)}, u32[]{:S(2)}, u32[]{:S(2)}) collective-permute-start(bf16[96,384]{1,0:T(8,128)(2,1)S(1)} %get-tuple-element.25), channel_id=1, source_target_pairs={{0,3},{1,2},{2,1},{3,0},{4,7},{5,6},{6,5},{7,4},{8,11},{9,10},{10,... | collective-permute-start | bytes 221192 | tf_op jit(solution)/shard_map/ppermute | solution.py:238
  20.4 12.6 %collective-permute-start.3 = (bf16[96,384]{1,0:T(8,128)(2,1)S(1)}, bf16[96,384]{1,0:T(8,128)(2,1)S(1)}, u32[]{:S(2)}, u32[]{:S(2)}) collective-permute-start(bf16[96,384]{1,0:T(8,128)(2,1)S(1)} %get-tuple-element.26), channel_id=1, source_target_pairs={{0,4},{1,5},{2,6},{3,7},{4,0},{5,1},{6,2},{7,3},{8,12},{9,13},{10,... | collective-permute-start | bytes 221192 | tf_op jit(solution)/shard_map/ppermute | solution.py:238
  22.1 13.2 %collective-permute-start.4 = (bf16[96,384]{1,0:T(8,128)(2,1)S(1)}, bf16[96,384]{1,0:T(8,128)(2,1)S(1)}, u32[]{:S(2)}, u32[]{:S(2)}) collective-permute-start(bf16[96,384]{1,0:T(8,128)(2,1)S(1)} %get-tuple-element.27), channel_id=1, source_target_pairs={{0,5},{1,4},{2,7},{3,6},{4,1},{5,0},{6,3},{7,2},{8,13},{9,12},{10,... | collective-permute-start | bytes 221192 | tf_op jit(solution)/shard_map/ppermute | solution.py:238
  22.2 20.2 %collective-permute-start.5 = (bf16[96,384]{1,0:T(8,128)(2,1)S(1)}, bf16[96,384]{1,0:T(8,128)(2,1)S(1)}, u32[]{:S(2)}, u32[]{:S(2)}) collective-permute-start(bf16[96,384]{1,0:T(8,128)(2,1)S(1)} %get-tuple-element.28), channel_id=1, source_target_pairs={{0,6},{1,7},{2,4},{3,5},{4,2},{5,3},{6,0},{7,1},{8,14},{9,15},{10,... | collective-permute-start | bytes 221192 | tf_op jit(solution)/shard_map/ppermute | solution.py:238
  31.9 11.3 %collective-permute-start.6 = (bf16[96,384]{1,0:T(8,128)(2,1)S(1)}, bf16[96,384]{1,0:T(8,128)(2,1)S(1)}, u32[]{:S(2)}, u32[]{:S(2)}) collective-permute-start(bf16[96,384]{1,0:T(8,128)(2,1)S(1)} %get-tuple-element.29), channel_id=1, source_target_pairs={{0,7},{1,6},{2,5},{3,4},{4,3},{5,2},{6,1},{7,0},{8,15},{9,14},{10,... | collective-permute-start | bytes 221192 | tf_op jit(solution)/shard_map/ppermute | solution.py:238
  32.7 20.9 %collective-permute-start.7 = (bf16[96,384]{1,0:T(8,128)(2,1)S(1)}, bf16[96,384]{1,0:T(8,128)(2,1)S(1)}, u32[]{:S(2)}, u32[]{:S(2)}) collective-permute-start(bf16[96,384]{1,0:T(8,128)(2,1)S(1)} %get-tuple-element.30), channel_id=1, source_target_pairs={{0,8},{1,9},{2,10},{3,11},{4,12},{5,13},{6,14},{7,15},{8,0},{9,1},... | collective-permute-start | bytes 221192 | tf_op jit(solution)/shard_map/ppermute | solution.py:238
  33.0 22.6 %collective-permute-start.8 = (bf16[96,384]{1,0:T(8,128)(2,1)S(1)}, bf16[96,384]{1,0:T(8,128)(2,1)S(1)}, u32[]{:S(2)}, u32[]{:S(2)}) collective-permute-start(bf16[96,384]{1,0:T(8,128)(2,1)S(1)} %get-tuple-element.31), channel_id=1, source_target_pairs={{0,9},{1,8},{2,11},{3,10},{4,13},{5,12},{6,15},{7,14},{8,1},{9,0},... | collective-permute-start | bytes 221192 | tf_op jit(solution)/shard_map/ppermute | solution.py:238
  35.3 23.1 %collective-permute-start.9 = (bf16[96,384]{1,0:T(8,128)(2,1)S(1)}, bf16[96,384]{1,0:T(8,128)(2,1)S(1)}, u32[]{:S(2)}, u32[]{:S(2)}) collective-permute-start(bf16[96,384]{1,0:T(8,128)(2,1)S(1)} %get-tuple-element.32), channel_id=1, source_target_pairs={{0,10},{1,11},{2,8},{3,9},{4,14},{5,15},{6,12},{7,13},{8,2},{9,3},... | collective-permute-start | bytes 221192 | tf_op jit(solution)/shard_map/ppermute | solution.py:238
  42.4 25.5 %collective-permute-start.10 = (bf16[96,384]{1,0:T(8,128)(2,1)}, bf16[96,384]{1,0:T(8,128)(2,1)S(1)}, u32[]{:S(2)}, u32[]{:S(2)}) collective-permute-start(bf16[96,384]{1,0:T(8,128)(2,1)} %get-tuple-element.33), channel_id=1, source_target_pairs={{0,11},{1,10},{2,9},{3,8},{4,15},{5,14},{6,13},{7,12},{8,3},{9,2},... | collective-permute-start | bytes 221192 | tf_op jit(solution)/shard_map/ppermute | solution.py:238
  43.2 24.7 %collective-permute-start.11 = (bf16[96,384]{1,0:T(8,128)(2,1)}, bf16[96,384]{1,0:T(8,128)(2,1)S(1)}, u32[]{:S(2)}, u32[]{:S(2)}) collective-permute-start(bf16[96,384]{1,0:T(8,128)(2,1)} %get-tuple-element.34), channel_id=1, source_target_pairs={{0,12},{1,13},{2,14},{3,15},{4,8},{5,9},{6,10},{7,11},{8,4},{9,5},... | collective-permute-start | bytes 221192 | tf_op jit(solution)/shard_map/ppermute | solution.py:238
  53.6 14.3 %collective-permute-start.12 = (bf16[96,384]{1,0:T(8,128)(2,1)}, bf16[96,384]{1,0:T(8,128)(2,1)S(1)}, u32[]{:S(2)}, u32[]{:S(2)}) collective-permute-start(bf16[96,384]{1,0:T(8,128)(2,1)} %get-tuple-element.35), channel_id=1, source_target_pairs={{0,13},{1,12},{2,15},{3,14},{4,9},{5,8},{6,11},{7,10},{8,5},{9,4},... | collective-permute-start | bytes 221192 | tf_op jit(solution)/shard_map/ppermute | solution.py:238
  55.6 12.4 %collective-permute-start.13 = (bf16[96,384]{1,0:T(8,128)(2,1)}, bf16[96,384]{1,0:T(8,128)(2,1)S(1)}, u32[]{:S(2)}, u32[]{:S(2)}) collective-permute-start(bf16[96,384]{1,0:T(8,128)(2,1)} %get-tuple-element.36), channel_id=1, source_target_pairs={{0,14},{1,15},{2,12},{3,13},{4,10},{5,11},{6,8},{7,9},{8,6},{9,7},... | collective-permute-start | bytes 221192 | tf_op jit(solution)/shard_map/ppermute | solution.py:238
  58.4 9.6 %collective-permute-start.14 = (bf16[96,384]{1,0:T(8,128)(2,1)}, bf16[96,384]{1,0:T(8,128)(2,1)S(1)}, u32[]{:S(2)}, u32[]{:S(2)}) collective-permute-start(bf16[96,384]{1,0:T(8,128)(2,1)} %get-tuple-element.37), channel_id=1, source_target_pairs={{0,15},{1,14},{2,13},{3,12},{4,11},{5,10},{6,9},{7,8},{8,7},{9,6},... | collective-permute-start | bytes 221192 | tf_op jit(solution)/shard_map/ppermute | solution.py:238
  69.7 21.1 %copy-start.2 = (bf16[12,384,128]{2,1,0:T(8,128)(2,1)S(1)}, bf16[12,384,128]{2,1,0:T(8,128)(2,1)}, u32[]{:S(2)}) copy-start(bf16[12,384,128]{2,1,0:T(8,128)(2,1)} %copy-done.1) | copy-start | bytes 3538948
  69.8 21.1 %copy-start.4 = (bf16[128,128]{1,0:T(8,128)(2,1)S(1)}, bf16[128,128]{1,0:T(8,128)(2,1)}, u32[]{:S(2)}) copy-start(bf16[128,128]{1,0:T(8,128)(2,1)} %w_ref.5) | copy-start | bytes 98308
  69.8 21.1 %copy-start.10 = (f32[128]{0:T(128)S(1)}, f32[128]{0:T(128)}, u32[]{:S(2)}) copy-start(f32[128]{0:T(128)} %param.18) | copy-start | bytes 1540
  69.8 21.1 %copy-start.11 = (f32[128]{0:T(128)S(1)}, f32[128]{0:T(128)}, u32[]{:S(2)}) copy-start(f32[128]{0:T(128)} %param.19) | copy-start | bytes 1540
  69.8 21.1 %copy-start.12 = (f32[128]{0:T(128)S(1)}, f32[128]{0:T(128)}, u32[]{:S(2)}) copy-start(f32[128]{0:T(128)} %param.21) | copy-start | bytes 1540

commit v15 on v14

--- a/solution.py
+++ b/solution.py
@@ -53,8 +53,13 @@
 
 
 def normalize(x, gain, shift):
-    centered = x - jnp.mean(x, axis=1, keepdims=True)
-    variance = jnp.mean(centered * centered, axis=1, keepdims=True)
+    width = x.shape[1]
+    ones = jnp.ones((width, width), bf16)
+    centered = x.astype(f32) - dot(x, ones) * (1.0 / width)
+    square = centered * centered
+    high = square.astype(bf16)
+    low = (square - high.astype(f32)).astype(bf16)
+    variance = (dot(high, ones) + dot(low, ones)) * (1.0 / width)
     return (centered * lax.rsqrt(variance + epsilon) * gain + shift).astype(bf16)
 
 
@@ -78,7 +83,7 @@
         bt[...] = column(b_ref[...])
 
     k, width = pair_ref.shape[1:]
-    x = pair_ref[...].astype(f32).reshape(STEP * k, width)
+    x = pair_ref[...].reshape(STEP * k, width)
     normed = normalize(x, gain_ref[...], shift_ref[...])
     out = as_rows(factor(normed, wt[...], bt[...]), k).astype(bf16)
     for p in range(out_ref.shape[0]):
@@ -107,7 +112,7 @@
                 wt[target] = jnp.concatenate([wf[s] for s in source], axis=0).astype(bf16)
                 bt[target] = jnp.concatenate([bf[s] for s in source], axis=0)
 
-    x = pair_ref[...].astype(f32).reshape(STEP * k, width)
+    x = pair_ref[...].reshape(STEP * k, width)
     normed = normalize(x, gain_ref[...], shift_ref[...])
     gate = sigmoid(dot(normed, gw_ref[...]) + gb_ref[...])
     gate_ref[...] = gate.reshape(STEP, k, width).astype(bf16)

time: 93.3 us -> 93.8 us (level)
  Pallas kernels: 13.6 us -> 14.6 us
  transfers between devices with their start and end apart: 16 -> 16, of which waited for: 6 -> 6; matrix products, arithmetic and copies ran while one was open for 0% -> 0% of each run, Pallas kernels for 5% -> 6%
where the time goes in v15:
time: 93.8 us; the launch traced here: 93.4 us
  waiting for transfers between devices  28.4 us (30%)
  starting transfers between devices  26.4 us (28%)
  blocking collectives  21.1 us (22%)
  Pallas kernels  14.6 us (16%)
  local copies, waits for them, and re-layouts  2.72 us (3%)
    ppermute x15, waiting for transfers between devices, send(): return lax.ppermute(values, everywhere, pairs)  21.5 us
    all_to_all x1, blocking collectives, shards(): product = lax.all_to_all(product, in_part, 0, 0, tiled=True)  21.1 us
    ppermute x15, starting transfers between devices, send(): return lax.ppermute(values, everywhere, pairs)  19.1 us
    all_to_all x1, starting transfers between devices, shards(): lax.all_to_all(right.reshape(devices, tall, k), everywhere, 0, 0, tiled=T...  7.3 us
    all_to_all x1, waiting for transfers between devices, shards(): lax.all_to_all(right.reshape(devices, tall, k), everywhere, 0, 0, tiled=T...  6.89 us
    pallas_call x1, Pallas kernels, shards(): pl.pallas_call(right_kernel, grid=(steps,), in_specs=[row_block, whole((1...  5.41 us
    pallas_call x1, Pallas kernels, shards(): pl.pallas_call(left_kernel, grid=(steps,), in_specs=[row_block, whole((1,...  4.07 us
    unnamed x26, local copies, waits for them, and re-layouts  2.72 us
  transfers between devices with their start and end apart: 16, of which 6 were waited for; matrix products, arithmetic and copies ran while one was open for 0% of the time, Pallas kernels for 6%

profile of v15, /device:TPU:0, one launch (start us, length us, event | category | flops | bytes accessed | tf_op | source)
XLA Modules:
  0.0 93.4 jit_solution(3008449632412232749)
XLA Ops:
  0.0 5.4 %right_factor.1 = bf16[2,16,96,384]{3,2,1,0:T(8,128)(2,1)} custom-call(bf16[12,384,128]{2,1,0:T(8,128)(2,1)} %pair_ref.3, f32[1,128]{1,0:T(1,128)} %bitcast.12, f32[1,128]{1,0:T(1,128)} %bitcast.14, bf16[128,512]{1,0:T(8,128)(2,1)} %w_ref.4, f32[1,512]{1,0:T(1,128)} %bitcast.10), custom_call_target="tpu_custom_call" | custom-call | flops 301989888 | bytes 3538944 | tf_op jit(solution)/shard_map/right_factor/pallas_call | solution.py:222
  5.4 0.0 copy-start.8
  5.4 0.0 copy-start.9
  5.4 7.3 %all-to-all-start = ((bf16[32,96,384]{2,1,0:T(8,128)(2,1)}), bf16[32,96,384]{2,1,0:T(8,128)(2,1)S(1)}, u32[]{:S(2)}, u32[]{:S(2)}) async-start(bf16[32,96,384]{2,1,0:T(8,128)(2,1)} %bitcast.20), calls=%async_computation | async-start | bytes 4718592 | tf_op jit(solution)/shard_map/all_to_all | solution.py:239
  12.8 0.0 copy-start.3
  12.8 0.9 copy-done.3
  13.7 0.8 copy-done.5
  14.5 4.1 %left_factor.1 = (bf16[96,384]{1,0:T(8,128)(2,1)S(1)}, bf16[96,384]{1,0:T(8,128)(2,1)S(1)}, bf16[96,384]{1,0:T(8,128)(2,1)S(1)}, bf16[96,384]{1,0:T(8,128)(2,1)S...) custom-call(bf16[12,384,128]{2,1,0:T(8,128)(2,1)S(1)} %copy-done, ...), custom_call_target="tpu_custom_call" | custom-call | flops 301989888 | bytes 3538944 | tf_op jit(solution)/shard_map/left_factor/pallas_call | solution.py:245
  18.5 1.0 %copy-done.1 = bf16[12,384,128]{2,1,0:T(8,128)(2,1)} copy-done((bf16[12,384,128]{2,1,0:T(8,128)(2,1)}, bf16[12,384,128]{2,1,0:T(8,128)(2,1)S(1)}, u32[]{:S(2)}) %copy-start.1) | copy-done | bytes 1179672
  19.6 0.3 collective-permute-start
  19.8 1.7 %collective-permute-start.1 = (bf16[96,384]{1,0:T(8,128)(2,1)S(1)}, bf16[96,384]{1,0:T(8,128)(2,1)S(1)}, u32[]{:S(2)}, u32[]{:S(2)}) collective-permute-start(bf16[96,384]{1,0:T(8,128)(2,1)S(1)} %get-tuple-element.24), channel_id=1, source_target_pairs={{0,2},{1,3},{2,0},{3,1},{4,6},{5,7},{6,4},{7,5},{8,10},{9,11},{10,... | collective-permute-start | bytes 221192 | tf_op jit(solution)/shard_map/ppermute | solution.py:243
  21.5 0.0 collective-permute-start.2
  21.5 1.7 %collective-permute-start.3 = (bf16[96,384]{1,0:T(8,128)(2,1)S(1)}, bf16[96,384]{1,0:T(8,128)(2,1)S(1)}, u32[]{:S(2)}, u32[]{:S(2)}) collective-permute-start(bf16[96,384]{1,0:T(8,128)(2,1)S(1)} %get-tuple-element.26), channel_id=1, source_target_pairs={{0,4},{1,5},{2,6},{3,7},{4,0},{5,1},{6,2},{7,3},{8,12},{9,13},{10,... | collective-permute-start | bytes 221192 | tf_op jit(solution)/shard_map/ppermute | solution.py:243
  23.2 0.1 collective-permute-start.4
  23.3 0.0 collective-permute-done.refs_1_
  23.3 2.6 %collective-permute-start.5 = (bf16[96,384]{1,0:T(8,128)(2,1)S(1)}, bf16[96,384]{1,0:T(8,128)(2,1)S(1)}, u32[]{:S(2)}, u32[]{:S(2)}) collective-permute-start(bf16[96,384]{1,0:T(8,128)(2,1)S(1)} %get-tuple-element.28), channel_id=1, source_target_pairs={{0,6},{1,7},{2,4},{3,5},{4,2},{5,3},{6,0},{7,1},{8,14},{9,15},{10,... | collective-permute-start | bytes 221192 | tf_op jit(solution)/shard_map/ppermute | solution.py:243
  25.9 6.4 %collective-permute-done.1.refs_2_ = bf16[96,384]{1,0:T(8,128)(2,1)S(1)} collective-permute-done((bf16[96,384]{1,0:T(8,128)(2,1)S(1)}, bf16[96,384]{1,0:T(8,128)(2,1)S(1)}, u32[]{:S(2)}, u32[]{:S(2)}) %collective-permute-start.1) | collective-permute-done | bytes 73760 | tf_op jit(solution)/shard_map/ppermute | solution.py:243
  32.3 0.6 collective-permute-start.6
  32.9 0.2 collective-permute-done.2.refs_3_
  33.1 0.3 collective-permute-start.7
  33.4 0.0 collective-permute-done.3.refs_4_
  33.4 2.3 %collective-permute-start.8 = (bf16[96,384]{1,0:T(8,128)(2,1)S(1)}, bf16[96,384]{1,0:T(8,128)(2,1)S(1)}, u32[]{:S(2)}, u32[]{:S(2)}) collective-permute-start(bf16[96,384]{1,0:T(8,128)(2,1)S(1)} %get-tuple-element.31), channel_id=1, source_target_pairs={{0,9},{1,8},{2,11},{3,10},{4,13},{5,12},{6,15},{7,14},{8,1},{9,0},... | collective-permute-start | bytes 221192 | tf_op jit(solution)/shard_map/ppermute | solution.py:243
  35.7 0.0 collective-permute-done.4.refs_5_
  35.7 3.2 %collective-permute-start.9 = (bf16[96,384]{1,0:T(8,128)(2,1)S(1)}, bf16[96,384]{1,0:T(8,128)(2,1)S(1)}, u32[]{:S(2)}, u32[]{:S(2)}) collective-permute-start(bf16[96,384]{1,0:T(8,128)(2,1)S(1)} %get-tuple-element.32), channel_id=1, source_target_pairs={{0,10},{1,11},{2,8},{3,9},{4,14},{5,15},{6,12},{7,13},{8,2},{9,3},... | collective-permute-start | bytes 221192 | tf_op jit(solution)/shard_map/ppermute | solution.py:243
  38.9 3.9 %collective-permute-done.5.refs_6_ = bf16[96,384]{1,0:T(8,128)(2,1)S(1)} collective-permute-done((bf16[96,384]{1,0:T(8,128)(2,1)S(1)}, bf16[96,384]{1,0:T(8,128)(2,1)S(1)}, u32[]{:S(2)}, u32[]{:S(2)}) %collective-permute-start.5) | collective-permute-done | bytes 73760 | tf_op jit(solution)/shard_map/ppermute | solution.py:243
  42.8 0.0 collective-permute-start.10
  42.8 0.8 collective-permute-done.6.refs_7_
  43.6 0.0 collective-permute-start.11
  43.6 0.4 regroup_left.1.near
  44.0 10.1 %collective-permute-done.7.refs_0_ = bf16[96,384]{1,0:T(8,128)(2,1)S(1)} collective-permute-done((bf16[96,384]{1,0:T(8,128)(2,1)S(1)}, bf16[96,384]{1,0:T(8,128)(2,1)S(1)}, u32[]{:S(2)}, u32[]{:S(2)}) %collective-permute-start.7) | collective-permute-done | bytes 73760 | tf_op jit(solution)/shard_map/ppermute | solution.py:243
  54.0 1.9 %collective-permute-start.12 = (bf16[96,384]{1,0:T(8,128)(2,1)}, bf16[96,384]{1,0:T(8,128)(2,1)S(1)}, u32[]{:S(2)}, u32[]{:S(2)}) collective-permute-start(bf16[96,384]{1,0:T(8,128)(2,1)} %get-tuple-element.35), channel_id=1, source_target_pairs={{0,13},{1,12},{2,15},{3,14},{4,9},{5,8},{6,11},{7,10},{8,5},{9,4},... | collective-permute-start | bytes 221192 | tf_op jit(solution)/shard_map/ppermute | solution.py:243
  56.0 0.0 collective-permute-done.8.refs_1_
  56.0 2.8 %collective-permute-start.13 = (bf16[96,384]{1,0:T(8,128)(2,1)}, bf16[96,384]{1,0:T(8,128)(2,1)S(1)}, u32[]{:S(2)}, u32[]{:S(2)}) collective-permute-start(bf16[96,384]{1,0:T(8,128)(2,1)} %get-tuple-element.36), channel_id=1, source_target_pairs={{0,14},{1,15},{2,12},{3,13},{4,10},{5,11},{6,8},{7,9},{8,6},{9,7},... | collective-permute-start | bytes 221192 | tf_op jit(solution)/shard_map/ppermute | solution.py:243
  58.8 0.0 collective-permute-done.9.refs_2_
  58.8 1.7 %collective-permute-start.14 = (bf16[96,384]{1,0:T(8,128)(2,1)}, bf16[96,384]{1,0:T(8,128)(2,1)S(1)}, u32[]{:S(2)}, u32[]{:S(2)}) collective-permute-start(bf16[96,384]{1,0:T(8,128)(2,1)} %get-tuple-element.37), channel_id=1, source_target_pairs={{0,15},{1,14},{2,13},{3,12},{4,11},{5,10},{6,9},{7,8},{8,7},{9,6},... | collective-permute-start | bytes 221192 | tf_op jit(solution)/shard_map/ppermute | solution.py:243
  60.5 6.9 %all-to-all-done = bf16[32,96,384]{2,1,0:T(8,128)(2,1)S(1)} async-done(((bf16[32,96,384]{2,1,0:T(8,128)(2,1)}), bf16[32,96,384]{2,1,0:T(8,128)(2,1)S(1)}, u32[]{:S(2)}, u32[]{:S(2)}) %all-to-all-start) | async-done | bytes 2359328 | tf_op jit(solution)/shard_map/all_to_all | solution.py:239
  67.4 1.0 %regroup_right.1.right = bf16[8,384,384]{2,1,0:T(8,128)(2,1)S(1)} custom-call(bf16[3072,384]{1,0:T(8,128)(2,1)S(1)} %bitcast.9), custom_call_target="tpu_custom_call" | custom-call | flops 137438953472 | bytes 4718592 | tf_op jit(solution)/shard_map/regroup_right/pallas_call | solution.py:309
  68.3 0.0 collective-permute-done.10.refs_3_
  68.4 0.0 collective-permute-done.12.refs_5_
  68.4 0.0 collective-permute-done.13.refs_6_
  68.4 1.8 %products.1 = bf16[16,96,384]{2,1,0:T(8,128)(2,1)S(1)} custom-call(bf16[8,384,384]{2,1,0:T(8,128)(2,1)S(1)} %regroup_right.1.right, bf16[8,96,384]{2,1,0:T(8,128)(2,1)S(1)} %regroup_left.1.near, bf16[96,384]{1,0:T(8,128)(2,1)S(1)} %collective-permute-done.7.refs_0_, bf16[96,384]{1,0:T(8,128)(2,1)S(1)} %collective-permute-done.8.refs_1_, ...), custom_call_target="tpu_custom_call" | custom-call | flops 226492416 | bytes 3538944 | tf_op jit(solution)/shard_map/products/pallas_call | solution.py:317
  70.2 0.0 copy-start.2
  70.2 0.0 copy-start.4
  70.2 0.0 copy-start.10
  70.2 0.0 copy-start.11
  70.2 0.0 copy-start.12
  70.2 21.1 %all_to_all.10.x_ref = bf16[16,96,384]{2,1,0:T(8,128)(2,1)S(1)} all-to-all(bf16[16,96,384]{2,1,0:T(8,128)(2,1)S(1)} %products.1), channel_id=1, replica_groups=mesh['groups'=1,'part'=2,'chan'=8,'quarter'=2] {'chan','quarter'}, dimensions={0} | all-to-all | bytes 2359296 | tf_op jit(solution)/shard_map/all_to_all | solution.py:329
  91.3 2.1 %update.1 = bf16[12,384,128]{2,1,0:T(8,128)(2,1)} custom-call(bf16[16,96,384]{2,1,0:T(8,128)(2,1)S(1)} %all_to_all.10.x_ref, bf16[12,384,128]{2,1,0:T(8,128)(2,1)S(1)} %copy-done.2, f32[1,128]{1,0:T(1,128)S(1)} %bitcast.17, f32[1,128]{1,0:T(1,128)S(1)} %bitcast.18, bf16[128,128]{1,0:T(8,128)(2,1)S(1)} %copy-done.4, f32[1,128]{1,0:T(1,128)S(1)} %bitcast.19), custom_call_target="tpu_custom_call" | custom-call | flops 150994944 | bytes 3538944 | tf_op jit(solution)/shard_map/update/pallas_call | solution.py:331
  (17 shorter events, 0.0 us)
Async XLA Ops:
  5.4 7.3 %copy-start = (bf16[12,384,128]{2,1,0:T(8,128)(2,1)S(1)}, bf16[12,384,128]{2,1,0:T(8,128)(2,1)}, u32[]{:S(2)}) copy-start(bf16[12,384,128]{2,1,0:T(8,128)(2,1)} %pair_ref.3) | copy-start | bytes 3538948
  5.4 7.4 %copy-start.6 = (f32[512]{0:T(512)S(1)}, f32[512]{0:T(512)}, u32[]{:S(2)}) copy-start(f32[512]{0:T(512)} %param.15) | copy-start | bytes 6148
  5.4 7.4 %copy-start.7 = (f32[128]{0:T(128)S(1)}, f32[128]{0:T(128)}, u32[]{:S(2)}) copy-start(f32[128]{0:T(128)} %param.12) | copy-start | bytes 1540
  5.4 7.4 %copy-start.8 = (f32[128]{0:T(128)S(1)}, f32[128]{0:T(128)}, u32[]{:S(2)}) copy-start(f32[128]{0:T(128)} %param.13) | copy-start | bytes 1540
  5.4 7.4 %copy-start.9 = (f32[128]{0:T(128)S(1)}, f32[128]{0:T(128)}, u32[]{:S(2)}) copy-start(f32[128]{0:T(128)} %param.17) | copy-start | bytes 1540
  5.4 61.9 %all-to-all-start = ((bf16[32,96,384]{2,1,0:T(8,128)(2,1)}), bf16[32,96,384]{2,1,0:T(8,128)(2,1)S(1)}, u32[]{:S(2)}, u32[]{:S(2)}) async-start(bf16[32,96,384]{2,1,0:T(8,128)(2,1)} %bitcast.20), calls=%async_computation | async-start | bytes 4718592 | tf_op jit(solution)/shard_map/all_to_all | solution.py:239
  12.8 0.9 copy-start.3
  13.7 0.8 copy-start.5
  18.5 1.0 %copy-start.1 = (bf16[12,384,128]{2,1,0:T(8,128)(2,1)}, bf16[12,384,128]{2,1,0:T(8,128)(2,1)S(1)}, u32[]{:S(2)}) copy-start(bf16[12,384,128]{2,1,0:T(8,128)(2,1)S(1)} %get-tuple-element.38.gate_ref) | copy-start | bytes 3538948
  19.6 3.7 %collective-permute-start = (bf16[96,384]{1,0:T(8,128)(2,1)S(1)}, bf16[96,384]{1,0:T(8,128)(2,1)S(1)}, u32[]{:S(2)}, u32[]{:S(2)}) collective-permute-start(bf16[96,384]{1,0:T(8,128)(2,1)S(1)} %get-tuple-element.23), channel_id=1, source_target_pairs={{0,1},{1,0},{2,3},{3,2},{4,5},{5,4},{6,7},{7,6},{8,9},{9,8},{10,11... | collective-permute-start | bytes 221192 | tf_op jit(solution)/shard_map/ppermute | solution.py:243
  19.8 12.5 %collective-permute-start.1 = (bf16[96,384]{1,0:T(8,128)(2,1)S(1)}, bf16[96,384]{1,0:T(8,128)(2,1)S(1)}, u32[]{:S(2)}, u32[]{:S(2)}) collective-permute-start(bf16[96,384]{1,0:T(8,128)(2,1)S(1)} %get-tuple-element.24), channel_id=1, source_target_pairs={{0,2},{1,3},{2,0},{3,1},{4,6},{5,7},{6,4},{7,5},{8,10},{9,11},{10,... | collective-permute-start | bytes 221192 | tf_op jit(solution)/shard_map/ppermute | solution.py:243
  21.5 11.6 %collective-permute-start.2 = (bf16[96,384]{1,0:T(8,128)(2,1)S(1)}, bf16[96,384]{1,0:T(8,128)(2,1)S(1)}, u32[]{:S(2)}, u32[]{:S(2)}) collective-permute-start(bf16[96,384]{1,0:T(8,128)(2,1)S(1)} %get-tuple-element.25), channel_id=1, source_target_pairs={{0,3},{1,2},{2,1},{3,0},{4,7},{5,6},{6,5},{7,4},{8,11},{9,10},{10,... | collective-permute-start | bytes 221192 | tf_op jit(solution)/shard_map/ppermute | solution.py:243
  21.5 11.9 %collective-permute-start.3 = (bf16[96,384]{1,0:T(8,128)(2,1)S(1)}, bf16[96,384]{1,0:T(8,128)(2,1)S(1)}, u32[]{:S(2)}, u32[]{:S(2)}) collective-permute-start(bf16[96,384]{1,0:T(8,128)(2,1)S(1)} %get-tuple-element.26), channel_id=1, source_target_pairs={{0,4},{1,5},{2,6},{3,7},{4,0},{5,1},{6,2},{7,3},{8,12},{9,13},{10,... | collective-permute-start | bytes 221192 | tf_op jit(solution)/shard_map/ppermute | solution.py:243
  23.2 12.5 %collective-permute-start.4 = (bf16[96,384]{1,0:T(8,128)(2,1)S(1)}, bf16[96,384]{1,0:T(8,128)(2,1)S(1)}, u32[]{:S(2)}, u32[]{:S(2)}) collective-permute-start(bf16[96,384]{1,0:T(8,128)(2,1)S(1)} %get-tuple-element.27), channel_id=1, source_target_pairs={{0,5},{1,4},{2,7},{3,6},{4,1},{5,0},{6,3},{7,2},{8,13},{9,12},{10,... | collective-permute-start | bytes 221192 | tf_op jit(solution)/shard_map/ppermute | solution.py:243
  23.3 19.5 %collective-permute-start.5 = (bf16[96,384]{1,0:T(8,128)(2,1)S(1)}, bf16[96,384]{1,0:T(8,128)(2,1)S(1)}, u32[]{:S(2)}, u32[]{:S(2)}) collective-permute-start(bf16[96,384]{1,0:T(8,128)(2,1)S(1)} %get-tuple-element.28), channel_id=1, source_target_pairs={{0,6},{1,7},{2,4},{3,5},{4,2},{5,3},{6,0},{7,1},{8,14},{9,15},{10,... | collective-permute-start | bytes 221192 | tf_op jit(solution)/shard_map/ppermute | solution.py:243
  32.3 11.3 %collective-permute-start.6 = (bf16[96,384]{1,0:T(8,128)(2,1)S(1)}, bf16[96,384]{1,0:T(8,128)(2,1)S(1)}, u32[]{:S(2)}, u32[]{:S(2)}) collective-permute-start(bf16[96,384]{1,0:T(8,128)(2,1)S(1)} %get-tuple-element.29), channel_id=1, source_target_pairs={{0,7},{1,6},{2,5},{3,4},{4,3},{5,2},{6,1},{7,0},{8,15},{9,14},{10,... | collective-permute-start | bytes 221192 | tf_op jit(solution)/shard_map/ppermute | solution.py:243
  33.1 20.9 %collective-permute-start.7 = (bf16[96,384]{1,0:T(8,128)(2,1)S(1)}, bf16[96,384]{1,0:T(8,128)(2,1)S(1)}, u32[]{:S(2)}, u32[]{:S(2)}) collective-permute-start(bf16[96,384]{1,0:T(8,128)(2,1)S(1)} %get-tuple-element.30), channel_id=1, source_target_pairs={{0,8},{1,9},{2,10},{3,11},{4,12},{5,13},{6,14},{7,15},{8,0},{9,1},... | collective-permute-start | bytes 221192 | tf_op jit(solution)/shard_map/ppermute | solution.py:243
  33.4 22.6 %collective-permute-start.8 = (bf16[96,384]{1,0:T(8,128)(2,1)S(1)}, bf16[96,384]{1,0:T(8,128)(2,1)S(1)}, u32[]{:S(2)}, u32[]{:S(2)}) collective-permute-start(bf16[96,384]{1,0:T(8,128)(2,1)S(1)} %get-tuple-element.31), channel_id=1, source_target_pairs={{0,9},{1,8},{2,11},{3,10},{4,13},{5,12},{6,15},{7,14},{8,1},{9,0},... | collective-permute-start | bytes 221192 | tf_op jit(solution)/shard_map/ppermute | solution.py:243
  35.7 23.1 %collective-permute-start.9 = (bf16[96,384]{1,0:T(8,128)(2,1)S(1)}, bf16[96,384]{1,0:T(8,128)(2,1)S(1)}, u32[]{:S(2)}, u32[]{:S(2)}) collective-permute-start(bf16[96,384]{1,0:T(8,128)(2,1)S(1)} %get-tuple-element.32), channel_id=1, source_target_pairs={{0,10},{1,11},{2,8},{3,9},{4,14},{5,15},{6,12},{7,13},{8,2},{9,3},... | collective-permute-start | bytes 221192 | tf_op jit(solution)/shard_map/ppermute | solution.py:243
  42.8 25.5 %collective-permute-start.10 = (bf16[96,384]{1,0:T(8,128)(2,1)}, bf16[96,384]{1,0:T(8,128)(2,1)S(1)}, u32[]{:S(2)}, u32[]{:S(2)}) collective-permute-start(bf16[96,384]{1,0:T(8,128)(2,1)} %get-tuple-element.33), channel_id=1, source_target_pairs={{0,11},{1,10},{2,9},{3,8},{4,15},{5,14},{6,13},{7,12},{8,3},{9,2},... | collective-permute-start | bytes 221192 | tf_op jit(solution)/shard_map/ppermute | solution.py:243
  43.6 24.8 %collective-permute-start.11 = (bf16[96,384]{1,0:T(8,128)(2,1)}, bf16[96,384]{1,0:T(8,128)(2,1)S(1)}, u32[]{:S(2)}, u32[]{:S(2)}) collective-permute-start(bf16[96,384]{1,0:T(8,128)(2,1)} %get-tuple-element.34), channel_id=1, source_target_pairs={{0,12},{1,13},{2,14},{3,15},{4,8},{5,9},{6,10},{7,11},{8,4},{9,5},... | collective-permute-start | bytes 221192 | tf_op jit(solution)/shard_map/ppermute | solution.py:243
  54.0 14.3 %collective-permute-start.12 = (bf16[96,384]{1,0:T(8,128)(2,1)}, bf16[96,384]{1,0:T(8,128)(2,1)S(1)}, u32[]{:S(2)}, u32[]{:S(2)}) collective-permute-start(bf16[96,384]{1,0:T(8,128)(2,1)} %get-tuple-element.35), channel_id=1, source_target_pairs={{0,13},{1,12},{2,15},{3,14},{4,9},{5,8},{6,11},{7,10},{8,5},{9,4},... | collective-permute-start | bytes 221192 | tf_op jit(solution)/shard_map/ppermute | solution.py:243
  56.0 12.4 %collective-permute-start.13 = (bf16[96,384]{1,0:T(8,128)(2,1)}, bf16[96,384]{1,0:T(8,128)(2,1)S(1)}, u32[]{:S(2)}, u32[]{:S(2)}) collective-permute-start(bf16[96,384]{1,0:T(8,128)(2,1)} %get-tuple-element.36), channel_id=1, source_target_pairs={{0,14},{1,15},{2,12},{3,13},{4,10},{5,11},{6,8},{7,9},{8,6},{9,7},... | collective-permute-start | bytes 221192 | tf_op jit(solution)/shard_map/ppermute | solution.py:243
  58.8 9.6 %collective-permute-start.14 = (bf16[96,384]{1,0:T(8,128)(2,1)}, bf16[96,384]{1,0:T(8,128)(2,1)S(1)}, u32[]{:S(2)}, u32[]{:S(2)}) collective-permute-start(bf16[96,384]{1,0:T(8,128)(2,1)} %get-tuple-element.37), channel_id=1, source_target_pairs={{0,15},{1,14},{2,13},{3,12},{4,11},{5,10},{6,9},{7,8},{8,7},{9,6},... | collective-permute-start | bytes 221192 | tf_op jit(solution)/shard_map/ppermute | solution.py:243
  70.2 21.1 %copy-start.2 = (bf16[12,384,128]{2,1,0:T(8,128)(2,1)S(1)}, bf16[12,384,128]{2,1,0:T(8,128)(2,1)}, u32[]{:S(2)}) copy-start(bf16[12,384,128]{2,1,0:T(8,128)(2,1)} %copy-done.1) | copy-start | bytes 3538948
  70.2 21.1 %copy-start.4 = (bf16[128,128]{1,0:T(8,128)(2,1)S(1)}, bf16[128,128]{1,0:T(8,128)(2,1)}, u32[]{:S(2)}) copy-start(bf16[128,128]{1,0:T(8,128)(2,1)} %w_ref.5) | copy-start | bytes 98308
  70.2 21.1 %copy-start.10 = (f32[128]{0:T(128)S(1)}, f32[128]{0:T(128)}, u32[]{:S(2)}) copy-start(f32[128]{0:T(128)} %param.18) | copy-start | bytes 1540
  70.2 21.1 %copy-start.11 = (f32[128]{0:T(128)S(1)}, f32[128]{0:T(128)}, u32[]{:S(2)}) copy-start(f32[128]{0:T(128)} %param.19) | copy-start | bytes 1540
  70.2 21.1 %copy-start.12 = (f32[128]{0:T(128)S(1)}, f32[128]{0:T(128)}, u32[]{:S(2)}) copy-start(f32[128]{0:T(128)} %param.21) | copy-start | bytes 1540

commit v16 on v14

--- a/solution.py
+++ b/solution.py
@@ -71,16 +71,14 @@
     )
 
 
-def right_kernel(pair_ref, gain_ref, shift_ref, w_ref, b_ref, out_ref, wt, bt):
-    @pl.when(pl.program_id(0) == 0)
-    def _():
-        wt[...] = w_ref[...].astype(f32).T.astype(bf16)
-        bt[...] = column(b_ref[...])
-
+def right_kernel(pair_ref, gain_ref, shift_ref, w_ref, b_ref, out_ref):
     k, width = pair_ref.shape[1:]
+    half = w_ref.shape[1] // 2
     x = pair_ref[...].astype(f32).reshape(STEP * k, width)
     normed = normalize(x, gain_ref[...], shift_ref[...])
-    out = as_rows(factor(normed, wt[...], bt[...]), k).astype(bf16)
+    both = dot(normed, w_ref[...]) + b_ref[...]
+    values = sigmoid(both[:, :half]) * both[:, half:]
+    out = as_rows(values.T, k).astype(bf16)
     for p in range(out_ref.shape[0]):
         out_ref[p] = out
 
@@ -226,7 +224,6 @@
         ],
         out_specs=pl.BlockSpec((parts, hosts, STEP * BLOCK, k), lambda s: (0, 0, s, 0)),
         out_shape=bfloat(parts, hosts, tall, k),
-        scratch_shapes=[pltpu.VMEM((2 * hidden, width), bf16), pltpu.VMEM((2 * hidden, LANES), f32)],
         compiler_params=params(60),
         cost_estimate=cost(4 * work * hidden, 6 * work),
         name="right_factor",

time: 93.3 us -> 93.3 us (level)
  no operation moved by 1% of the time
where the time goes in v16:
time: 93.3 us; the launch traced here: 92.9 us
  waiting for transfers between devices  29.1 us (31%)
  starting transfers between devices  26.4 us (28%)
  blocking collectives  21.1 us (23%)
  Pallas kernels  13.5 us (14%)
  local copies, waits for them, and re-layouts  2.72 us (3%)
    ppermute x15, waiting for transfers between devices, send(): return lax.ppermute(values, everywhere, pairs)  22.2 us
    all_to_all x1, blocking collectives, shards(): product = lax.all_to_all(product, in_part, 0, 0, tiled=True)  21.1 us
    ppermute x15, starting transfers between devices, send(): return lax.ppermute(values, everywhere, pairs)  19 us
    all_to_all x1, starting transfers between devices, shards(): lax.all_to_all(right.reshape(devices, tall, k), everywhere, 0, 0, tiled=T...  7.31 us
    all_to_all x1, waiting for transfers between devices, shards(): lax.all_to_all(right.reshape(devices, tall, k), everywhere, 0, 0, tiled=T...  6.88 us
    pallas_call x1, Pallas kernels, shards(): pl.pallas_call(right_kernel, grid=(steps,), in_specs=[row_block, whole((1...  4.91 us
    pallas_call x1, Pallas kernels, shards(): pl.pallas_call(left_kernel, grid=(steps,), in_specs=[row_block, whole((1,...  3.39 us
    unnamed x26, local copies, waits for them, and re-layouts  2.72 us
  transfers between devices with their start and end apart: 16, of which 6 were waited for; matrix products, arithmetic and copies ran while one was open for 0% of the time, Pallas kernels for 5%

profile of v16, /device:TPU:0, one launch (start us, length us, event | category | flops | bytes accessed | tf_op | source)
XLA Modules:
  0.0 92.9 jit_solution(3574444959166619825)
XLA Ops:
  0.0 4.9 %right_factor.1 = bf16[2,16,96,384]{3,2,1,0:T(8,128)(2,1)} custom-call(bf16[12,384,128]{2,1,0:T(8,128)(2,1)} %pair_ref.3, f32[1,128]{1,0:T(1,128)} %bitcast.12, f32[1,128]{1,0:T(1,128)} %bitcast.14, bf16[128,512]{1,0:T(8,128)(2,1)} %w_ref.4, f32[1,512]{1,0:T(1,128)} %bitcast.10), custom_call_target="tpu_custom_call" | custom-call | flops 301989888 | bytes 3538944 | tf_op jit(solution)/shard_map/right_factor/pallas_call | solution.py:215
  4.9 0.0 copy-start.8
  4.9 0.0 copy-start.9
  4.9 7.3 %all-to-all-start = ((bf16[32,96,384]{2,1,0:T(8,128)(2,1)}), bf16[32,96,384]{2,1,0:T(8,128)(2,1)S(1)}, u32[]{:S(2)}, u32[]{:S(2)}) async-start(bf16[32,96,384]{2,1,0:T(8,128)(2,1)} %bitcast.20), calls=%async_computation | async-start | bytes 4718592 | tf_op jit(solution)/shard_map/all_to_all | solution.py:231
  12.3 0.0 copy-start.3
  12.3 0.9 copy-done.3
  13.2 0.8 copy-done.5
  14.0 3.4 %left_factor.1 = (bf16[96,384]{1,0:T(8,128)(2,1)S(1)}, bf16[96,384]{1,0:T(8,128)(2,1)S(1)}, bf16[96,384]{1,0:T(8,128)(2,1)S(1)}, bf16[96,384]{1,0:T(8,128)(2,1)S...) custom-call(bf16[12,384,128]{2,1,0:T(8,128)(2,1)S(1)} %copy-done, ...), custom_call_target="tpu_custom_call" | custom-call | flops 301989888 | bytes 3538944 | tf_op jit(solution)/shard_map/left_factor/pallas_call | solution.py:237
  17.4 1.0 %copy-done.1 = bf16[12,384,128]{2,1,0:T(8,128)(2,1)} copy-done((bf16[12,384,128]{2,1,0:T(8,128)(2,1)}, bf16[12,384,128]{2,1,0:T(8,128)(2,1)S(1)}, u32[]{:S(2)}) %copy-start.1) | copy-done | bytes 1179672
  18.4 0.3 collective-permute-start
  18.6 1.7 %collective-permute-start.1 = (bf16[96,384]{1,0:T(8,128)(2,1)S(1)}, bf16[96,384]{1,0:T(8,128)(2,1)S(1)}, u32[]{:S(2)}, u32[]{:S(2)}) collective-permute-start(bf16[96,384]{1,0:T(8,128)(2,1)S(1)} %get-tuple-element.24), channel_id=1, source_target_pairs={{0,2},{1,3},{2,0},{3,1},{4,6},{5,7},{6,4},{7,5},{8,10},{9,11},{10,... | collective-permute-start | bytes 221192 | tf_op jit(solution)/shard_map/ppermute | solution.py:235
  20.3 0.0 collective-permute-start.2
  20.3 1.7 %collective-permute-start.3 = (bf16[96,384]{1,0:T(8,128)(2,1)S(1)}, bf16[96,384]{1,0:T(8,128)(2,1)S(1)}, u32[]{:S(2)}, u32[]{:S(2)}) collective-permute-start(bf16[96,384]{1,0:T(8,128)(2,1)S(1)} %get-tuple-element.26), channel_id=1, source_target_pairs={{0,4},{1,5},{2,6},{3,7},{4,0},{5,1},{6,2},{7,3},{8,12},{9,13},{10,... | collective-permute-start | bytes 221192 | tf_op jit(solution)/shard_map/ppermute | solution.py:235
  22.0 0.1 collective-permute-start.4
  22.1 0.0 collective-permute-done.refs_1_
  22.1 2.6 %collective-permute-start.5 = (bf16[96,384]{1,0:T(8,128)(2,1)S(1)}, bf16[96,384]{1,0:T(8,128)(2,1)S(1)}, u32[]{:S(2)}, u32[]{:S(2)}) collective-permute-start(bf16[96,384]{1,0:T(8,128)(2,1)S(1)} %get-tuple-element.28), channel_id=1, source_target_pairs={{0,6},{1,7},{2,4},{3,5},{4,2},{5,3},{6,0},{7,1},{8,14},{9,15},{10,... | collective-permute-start | bytes 221192 | tf_op jit(solution)/shard_map/ppermute | solution.py:235
  24.7 7.1 %collective-permute-done.1.refs_2_ = bf16[96,384]{1,0:T(8,128)(2,1)S(1)} collective-permute-done((bf16[96,384]{1,0:T(8,128)(2,1)S(1)}, bf16[96,384]{1,0:T(8,128)(2,1)S(1)}, u32[]{:S(2)}, u32[]{:S(2)}) %collective-permute-start.1) | collective-permute-done | bytes 73760 | tf_op jit(solution)/shard_map/ppermute | solution.py:235
  31.8 0.6 collective-permute-start.6
  32.4 0.2 collective-permute-done.2.refs_3_
  32.6 0.3 collective-permute-start.7
  32.9 0.0 collective-permute-done.3.refs_4_
  32.9 2.3 %collective-permute-start.8 = (bf16[96,384]{1,0:T(8,128)(2,1)S(1)}, bf16[96,384]{1,0:T(8,128)(2,1)S(1)}, u32[]{:S(2)}, u32[]{:S(2)}) collective-permute-start(bf16[96,384]{1,0:T(8,128)(2,1)S(1)} %get-tuple-element.31), channel_id=1, source_target_pairs={{0,9},{1,8},{2,11},{3,10},{4,13},{5,12},{6,15},{7,14},{8,1},{9,0},... | collective-permute-start | bytes 221192 | tf_op jit(solution)/shard_map/ppermute | solution.py:235
  35.2 0.0 collective-permute-done.4.refs_5_
  35.2 3.2 %collective-permute-start.9 = (bf16[96,384]{1,0:T(8,128)(2,1)S(1)}, bf16[96,384]{1,0:T(8,128)(2,1)S(1)}, u32[]{:S(2)}, u32[]{:S(2)}) collective-permute-start(bf16[96,384]{1,0:T(8,128)(2,1)S(1)} %get-tuple-element.32), channel_id=1, source_target_pairs={{0,10},{1,11},{2,8},{3,9},{4,14},{5,15},{6,12},{7,13},{8,2},{9,3},... | collective-permute-start | bytes 221192 | tf_op jit(solution)/shard_map/ppermute | solution.py:235
  38.4 3.9 %collective-permute-done.5.refs_6_ = bf16[96,384]{1,0:T(8,128)(2,1)S(1)} collective-permute-done((bf16[96,384]{1,0:T(8,128)(2,1)S(1)}, bf16[96,384]{1,0:T(8,128)(2,1)S(1)}, u32[]{:S(2)}, u32[]{:S(2)}) %collective-permute-start.5) | collective-permute-done | bytes 73760 | tf_op jit(solution)/shard_map/ppermute | solution.py:235
  42.3 0.0 collective-permute-start.10
  42.3 0.8 collective-permute-done.6.refs_7_
  43.1 0.0 collective-permute-start.11
  43.1 0.4 regroup_left.1.near
  43.5 10.1 %collective-permute-done.7.refs_0_ = bf16[96,384]{1,0:T(8,128)(2,1)S(1)} collective-permute-done((bf16[96,384]{1,0:T(8,128)(2,1)S(1)}, bf16[96,384]{1,0:T(8,128)(2,1)S(1)}, u32[]{:S(2)}, u32[]{:S(2)}) %collective-permute-start.7) | collective-permute-done | bytes 73760 | tf_op jit(solution)/shard_map/ppermute | solution.py:235
  53.5 1.9 %collective-permute-start.12 = (bf16[96,384]{1,0:T(8,128)(2,1)}, bf16[96,384]{1,0:T(8,128)(2,1)S(1)}, u32[]{:S(2)}, u32[]{:S(2)}) collective-permute-start(bf16[96,384]{1,0:T(8,128)(2,1)} %get-tuple-element.35), channel_id=1, source_target_pairs={{0,13},{1,12},{2,15},{3,14},{4,9},{5,8},{6,11},{7,10},{8,5},{9,4},... | collective-permute-start | bytes 221192 | tf_op jit(solution)/shard_map/ppermute | solution.py:235
  55.5 0.0 collective-permute-done.8.refs_1_
  55.5 2.8 %collective-permute-start.13 = (bf16[96,384]{1,0:T(8,128)(2,1)}, bf16[96,384]{1,0:T(8,128)(2,1)S(1)}, u32[]{:S(2)}, u32[]{:S(2)}) collective-permute-start(bf16[96,384]{1,0:T(8,128)(2,1)} %get-tuple-element.36), channel_id=1, source_target_pairs={{0,14},{1,15},{2,12},{3,13},{4,10},{5,11},{6,8},{7,9},{8,6},{9,7},... | collective-permute-start | bytes 221192 | tf_op jit(solution)/shard_map/ppermute | solution.py:235
  58.3 0.0 collective-permute-done.9.refs_2_
  58.3 1.7 %collective-permute-start.14 = (bf16[96,384]{1,0:T(8,128)(2,1)}, bf16[96,384]{1,0:T(8,128)(2,1)S(1)}, u32[]{:S(2)}, u32[]{:S(2)}) collective-permute-start(bf16[96,384]{1,0:T(8,128)(2,1)} %get-tuple-element.37), channel_id=1, source_target_pairs={{0,15},{1,14},{2,13},{3,12},{4,11},{5,10},{6,9},{7,8},{8,7},{9,6},... | collective-permute-start | bytes 221192 | tf_op jit(solution)/shard_map/ppermute | solution.py:235
  60.0 6.9 %all-to-all-done = bf16[32,96,384]{2,1,0:T(8,128)(2,1)S(1)} async-done(((bf16[32,96,384]{2,1,0:T(8,128)(2,1)}), bf16[32,96,384]{2,1,0:T(8,128)(2,1)S(1)}, u32[]{:S(2)}, u32[]{:S(2)}) %all-to-all-start) | async-done | bytes 2359328 | tf_op jit(solution)/shard_map/all_to_all | solution.py:231
  66.9 1.0 %regroup_right.1.right = bf16[8,384,384]{2,1,0:T(8,128)(2,1)S(1)} custom-call(bf16[3072,384]{1,0:T(8,128)(2,1)S(1)} %bitcast.9), custom_call_target="tpu_custom_call" | custom-call | flops 137438953472 | bytes 4718592 | tf_op jit(solution)/shard_map/regroup_right/pallas_call | solution.py:301
  67.8 0.0 collective-permute-done.10.refs_3_
  67.8 0.0 collective-permute-done.11.refs_4_
  67.9 0.0 collective-permute-done.12.refs_5_
  67.9 1.8 %products.1 = bf16[16,96,384]{2,1,0:T(8,128)(2,1)S(1)} custom-call(bf16[8,384,384]{2,1,0:T(8,128)(2,1)S(1)} %regroup_right.1.right, bf16[8,96,384]{2,1,0:T(8,128)(2,1)S(1)} %regroup_left.1.near, bf16[96,384]{1,0:T(8,128)(2,1)S(1)} %collective-permute-done.7.refs_0_, bf16[96,384]{1,0:T(8,128)(2,1)S(1)} %collective-permute-done.8.refs_1_, ...), custom_call_target="tpu_custom_call" | custom-call | flops 226492416 | bytes 3538944 | tf_op jit(solution)/shard_map/products/pallas_call | solution.py:309
  69.7 0.0 copy-start.2
  69.7 0.0 copy-start.4
  69.7 0.0 copy-start.10
  69.7 0.0 copy-start.11
  69.7 0.0 copy-start.12
  69.7 21.1 %all_to_all.10.x_ref = bf16[16,96,384]{2,1,0:T(8,128)(2,1)S(1)} all-to-all(bf16[16,96,384]{2,1,0:T(8,128)(2,1)S(1)} %products.1), channel_id=1, replica_groups=mesh['groups'=1,'part'=2,'chan'=8,'quarter'=2] {'chan','quarter'}, dimensions={0} | all-to-all | bytes 2359296 | tf_op jit(solution)/shard_map/all_to_all | solution.py:321
  90.8 2.1 %update.1 = bf16[12,384,128]{2,1,0:T(8,128)(2,1)} custom-call(bf16[16,96,384]{2,1,0:T(8,128)(2,1)S(1)} %all_to_all.10.x_ref, bf16[12,384,128]{2,1,0:T(8,128)(2,1)S(1)} %copy-done.2, f32[1,128]{1,0:T(1,128)S(1)} %bitcast.17, f32[1,128]{1,0:T(1,128)S(1)} %bitcast.18, bf16[128,128]{1,0:T(8,128)(2,1)S(1)} %copy-done.4, f32[1,128]{1,0:T(1,128)S(1)} %bitcast.19), custom_call_target="tpu_custom_call" | custom-call | flops 150994944 | bytes 3538944 | tf_op jit(solution)/shard_map/update/pallas_call | solution.py:323
  (17 shorter events, 0.0 us)
Async XLA Ops:
  4.9 7.4 %copy-start = (bf16[12,384,128]{2,1,0:T(8,128)(2,1)S(1)}, bf16[12,384,128]{2,1,0:T(8,128)(2,1)}, u32[]{:S(2)}) copy-start(bf16[12,384,128]{2,1,0:T(8,128)(2,1)} %pair_ref.3) | copy-start | bytes 3538948
  4.9 7.4 %copy-start.6 = (f32[512]{0:T(512)S(1)}, f32[512]{0:T(512)}, u32[]{:S(2)}) copy-start(f32[512]{0:T(512)} %param.15) | copy-start | bytes 6148
  4.9 7.4 %copy-start.7 = (f32[128]{0:T(128)S(1)}, f32[128]{0:T(128)}, u32[]{:S(2)}) copy-start(f32[128]{0:T(128)} %param.12) | copy-start | bytes 1540
  4.9 7.4 %copy-start.8 = (f32[128]{0:T(128)S(1)}, f32[128]{0:T(128)}, u32[]{:S(2)}) copy-start(f32[128]{0:T(128)} %param.13) | copy-start | bytes 1540
  4.9 7.4 %copy-start.9 = (f32[128]{0:T(128)S(1)}, f32[128]{0:T(128)}, u32[]{:S(2)}) copy-start(f32[128]{0:T(128)} %param.17) | copy-start | bytes 1540
  4.9 61.9 %all-to-all-start = ((bf16[32,96,384]{2,1,0:T(8,128)(2,1)}), bf16[32,96,384]{2,1,0:T(8,128)(2,1)S(1)}, u32[]{:S(2)}, u32[]{:S(2)}) async-start(bf16[32,96,384]{2,1,0:T(8,128)(2,1)} %bitcast.20), calls=%async_computation | async-start | bytes 4718592 | tf_op jit(solution)/shard_map/all_to_all | solution.py:231
  12.3 0.9 copy-start.3
  13.2 0.8 copy-start.5
  17.4 1.0 %copy-start.1 = (bf16[12,384,128]{2,1,0:T(8,128)(2,1)}, bf16[12,384,128]{2,1,0:T(8,128)(2,1)S(1)}, u32[]{:S(2)}) copy-start(bf16[12,384,128]{2,1,0:T(8,128)(2,1)S(1)} %get-tuple-element.38.gate_ref) | copy-start | bytes 3538948
  18.4 3.7 %collective-permute-start = (bf16[96,384]{1,0:T(8,128)(2,1)S(1)}, bf16[96,384]{1,0:T(8,128)(2,1)S(1)}, u32[]{:S(2)}, u32[]{:S(2)}) collective-permute-start(bf16[96,384]{1,0:T(8,128)(2,1)S(1)} %get-tuple-element.23), channel_id=1, source_target_pairs={{0,1},{1,0},{2,3},{3,2},{4,5},{5,4},{6,7},{7,6},{8,9},{9,8},{10,11... | collective-permute-start | bytes 221192 | tf_op jit(solution)/shard_map/ppermute | solution.py:235
  18.6 13.2 %collective-permute-start.1 = (bf16[96,384]{1,0:T(8,128)(2,1)S(1)}, bf16[96,384]{1,0:T(8,128)(2,1)S(1)}, u32[]{:S(2)}, u32[]{:S(2)}) collective-permute-start(bf16[96,384]{1,0:T(8,128)(2,1)S(1)} %get-tuple-element.24), channel_id=1, source_target_pairs={{0,2},{1,3},{2,0},{3,1},{4,6},{5,7},{6,4},{7,5},{8,10},{9,11},{10,... | collective-permute-start | bytes 221192 | tf_op jit(solution)/shard_map/ppermute | solution.py:235
  20.3 12.3 %collective-permute-start.2 = (bf16[96,384]{1,0:T(8,128)(2,1)S(1)}, bf16[96,384]{1,0:T(8,128)(2,1)S(1)}, u32[]{:S(2)}, u32[]{:S(2)}) collective-permute-start(bf16[96,384]{1,0:T(8,128)(2,1)S(1)} %get-tuple-element.25), channel_id=1, source_target_pairs={{0,3},{1,2},{2,1},{3,0},{4,7},{5,6},{6,5},{7,4},{8,11},{9,10},{10,... | collective-permute-start | bytes 221192 | tf_op jit(solution)/shard_map/ppermute | solution.py:235
  20.3 12.6 %collective-permute-start.3 = (bf16[96,384]{1,0:T(8,128)(2,1)S(1)}, bf16[96,384]{1,0:T(8,128)(2,1)S(1)}, u32[]{:S(2)}, u32[]{:S(2)}) collective-permute-start(bf16[96,384]{1,0:T(8,128)(2,1)S(1)} %get-tuple-element.26), channel_id=1, source_target_pairs={{0,4},{1,5},{2,6},{3,7},{4,0},{5,1},{6,2},{7,3},{8,12},{9,13},{10,... | collective-permute-start | bytes 221192 | tf_op jit(solution)/shard_map/ppermute | solution.py:235
  22.0 13.2 %collective-permute-start.4 = (bf16[96,384]{1,0:T(8,128)(2,1)S(1)}, bf16[96,384]{1,0:T(8,128)(2,1)S(1)}, u32[]{:S(2)}, u32[]{:S(2)}) collective-permute-start(bf16[96,384]{1,0:T(8,128)(2,1)S(1)} %get-tuple-element.27), channel_id=1, source_target_pairs={{0,5},{1,4},{2,7},{3,6},{4,1},{5,0},{6,3},{7,2},{8,13},{9,12},{10,... | collective-permute-start | bytes 221192 | tf_op jit(solution)/shard_map/ppermute | solution.py:235
  22.1 20.2 %collective-permute-start.5 = (bf16[96,384]{1,0:T(8,128)(2,1)S(1)}, bf16[96,384]{1,0:T(8,128)(2,1)S(1)}, u32[]{:S(2)}, u32[]{:S(2)}) collective-permute-start(bf16[96,384]{1,0:T(8,128)(2,1)S(1)} %get-tuple-element.28), channel_id=1, source_target_pairs={{0,6},{1,7},{2,4},{3,5},{4,2},{5,3},{6,0},{7,1},{8,14},{9,15},{10,... | collective-permute-start | bytes 221192 | tf_op jit(solution)/shard_map/ppermute | solution.py:235
  31.8 11.3 %collective-permute-start.6 = (bf16[96,384]{1,0:T(8,128)(2,1)S(1)}, bf16[96,384]{1,0:T(8,128)(2,1)S(1)}, u32[]{:S(2)}, u32[]{:S(2)}) collective-permute-start(bf16[96,384]{1,0:T(8,128)(2,1)S(1)} %get-tuple-element.29), channel_id=1, source_target_pairs={{0,7},{1,6},{2,5},{3,4},{4,3},{5,2},{6,1},{7,0},{8,15},{9,14},{10,... | collective-permute-start | bytes 221192 | tf_op jit(solution)/shard_map/ppermute | solution.py:235
  32.6 20.9 %collective-permute-start.7 = (bf16[96,384]{1,0:T(8,128)(2,1)S(1)}, bf16[96,384]{1,0:T(8,128)(2,1)S(1)}, u32[]{:S(2)}, u32[]{:S(2)}) collective-permute-start(bf16[96,384]{1,0:T(8,128)(2,1)S(1)} %get-tuple-element.30), channel_id=1, source_target_pairs={{0,8},{1,9},{2,10},{3,11},{4,12},{5,13},{6,14},{7,15},{8,0},{9,1},... | collective-permute-start | bytes 221192 | tf_op jit(solution)/shard_map/ppermute | solution.py:235
  32.9 22.6 %collective-permute-start.8 = (bf16[96,384]{1,0:T(8,128)(2,1)S(1)}, bf16[96,384]{1,0:T(8,128)(2,1)S(1)}, u32[]{:S(2)}, u32[]{:S(2)}) collective-permute-start(bf16[96,384]{1,0:T(8,128)(2,1)S(1)} %get-tuple-element.31), channel_id=1, source_target_pairs={{0,9},{1,8},{2,11},{3,10},{4,13},{5,12},{6,15},{7,14},{8,1},{9,0},... | collective-permute-start | bytes 221192 | tf_op jit(solution)/shard_map/ppermute | solution.py:235
  35.2 23.1 %collective-permute-start.9 = (bf16[96,384]{1,0:T(8,128)(2,1)S(1)}, bf16[96,384]{1,0:T(8,128)(2,1)S(1)}, u32[]{:S(2)}, u32[]{:S(2)}) collective-permute-start(bf16[96,384]{1,0:T(8,128)(2,1)S(1)} %get-tuple-element.32), channel_id=1, source_target_pairs={{0,10},{1,11},{2,8},{3,9},{4,14},{5,15},{6,12},{7,13},{8,2},{9,3},... | collective-permute-start | bytes 221192 | tf_op jit(solution)/shard_map/ppermute | solution.py:235
  42.3 25.5 %collective-permute-start.10 = (bf16[96,384]{1,0:T(8,128)(2,1)}, bf16[96,384]{1,0:T(8,128)(2,1)S(1)}, u32[]{:S(2)}, u32[]{:S(2)}) collective-permute-start(bf16[96,384]{1,0:T(8,128)(2,1)} %get-tuple-element.33), channel_id=1, source_target_pairs={{0,11},{1,10},{2,9},{3,8},{4,15},{5,14},{6,13},{7,12},{8,3},{9,2},... | collective-permute-start | bytes 221192 | tf_op jit(solution)/shard_map/ppermute | solution.py:235
  43.1 24.7 %collective-permute-start.11 = (bf16[96,384]{1,0:T(8,128)(2,1)}, bf16[96,384]{1,0:T(8,128)(2,1)S(1)}, u32[]{:S(2)}, u32[]{:S(2)}) collective-permute-start(bf16[96,384]{1,0:T(8,128)(2,1)} %get-tuple-element.34), channel_id=1, source_target_pairs={{0,12},{1,13},{2,14},{3,15},{4,8},{5,9},{6,10},{7,11},{8,4},{9,5},... | collective-permute-start | bytes 221192 | tf_op jit(solution)/shard_map/ppermute | solution.py:235
  53.5 14.3 %collective-permute-start.12 = (bf16[96,384]{1,0:T(8,128)(2,1)}, bf16[96,384]{1,0:T(8,128)(2,1)S(1)}, u32[]{:S(2)}, u32[]{:S(2)}) collective-permute-start(bf16[96,384]{1,0:T(8,128)(2,1)} %get-tuple-element.35), channel_id=1, source_target_pairs={{0,13},{1,12},{2,15},{3,14},{4,9},{5,8},{6,11},{7,10},{8,5},{9,4},... | collective-permute-start | bytes 221192 | tf_op jit(solution)/shard_map/ppermute | solution.py:235
  55.5 12.4 %collective-permute-start.13 = (bf16[96,384]{1,0:T(8,128)(2,1)}, bf16[96,384]{1,0:T(8,128)(2,1)S(1)}, u32[]{:S(2)}, u32[]{:S(2)}) collective-permute-start(bf16[96,384]{1,0:T(8,128)(2,1)} %get-tuple-element.36), channel_id=1, source_target_pairs={{0,14},{1,15},{2,12},{3,13},{4,10},{5,11},{6,8},{7,9},{8,6},{9,7},... | collective-permute-start | bytes 221192 | tf_op jit(solution)/shard_map/ppermute | solution.py:235
  58.3 9.6 %collective-permute-start.14 = (bf16[96,384]{1,0:T(8,128)(2,1)}, bf16[96,384]{1,0:T(8,128)(2,1)S(1)}, u32[]{:S(2)}, u32[]{:S(2)}) collective-permute-start(bf16[96,384]{1,0:T(8,128)(2,1)} %get-tuple-element.37), channel_id=1, source_target_pairs={{0,15},{1,14},{2,13},{3,12},{4,11},{5,10},{6,9},{7,8},{8,7},{9,6},... | collective-permute-start | bytes 221192 | tf_op jit(solution)/shard_map/ppermute | solution.py:235
  69.7 21.1 %copy-start.2 = (bf16[12,384,128]{2,1,0:T(8,128)(2,1)S(1)}, bf16[12,384,128]{2,1,0:T(8,128)(2,1)}, u32[]{:S(2)}) copy-start(bf16[12,384,128]{2,1,0:T(8,128)(2,1)} %copy-done.1) | copy-start | bytes 3538948
  69.7 21.1 %copy-start.4 = (bf16[128,128]{1,0:T(8,128)(2,1)S(1)}, bf16[128,128]{1,0:T(8,128)(2,1)}, u32[]{:S(2)}) copy-start(bf16[128,128]{1,0:T(8,128)(2,1)} %w_ref.5) | copy-start | bytes 98308
  69.7 21.1 %copy-start.10 = (f32[128]{0:T(128)S(1)}, f32[128]{0:T(128)}, u32[]{:S(2)}) copy-start(f32[128]{0:T(128)} %param.18) | copy-start | bytes 1540
  69.7 21.1 %copy-start.11 = (f32[128]{0:T(128)S(1)}, f32[128]{0:T(128)}, u32[]{:S(2)}) copy-start(f32[128]{0:T(128)} %param.19) | copy-start | bytes 1540
  69.7 21.1 %copy-start.12 = (f32[128]{0:T(128)S(1)}, f32[128]{0:T(128)}, u32[]{:S(2)}) copy-start(f32[128]{0:T(128)} %param.21) | copy-start | bytes 1540

commit v17 on v16

--- a/solution.py
+++ b/solution.py
@@ -132,32 +132,57 @@
     ]
 
 
-def regroup_right_kernel(rows_ref, out_ref):
-    regroup(slices([rows_ref]), out_ref, shuffle(BLOCK, SIZE))
-
-
 def regroup_left_kernel(*refs):
     regroup(slices(refs[:-1]), refs[-1], shuffle(BLOCK, SIZE))
 
 
-def product_kernel(right, near, *refs):
-    lefts = refs[:-3]
-    out_ref, far, held = refs[-3:]
-    rows = lefts[0].shape[0] // BLOCK
-    host = lax.axis_index(("chan", "quarter"))
-    regroup(slices(lefts), far, shuffle(BLOCK, SIZE))
+def multiply(left, right, held, store):
     for c in range(BLOCK):
-        left = jnp.concatenate([near[c], far[c]], axis=0)
-        held[c] = dot_nt(left, right[c]).astype(bf16)
+        held[c] = dot_nt(left[c], right[c]).astype(bf16)
     back = shuffle(SIZE, BLOCK)
     for s in range(held.shape[1] // SIZE):
         parts = jnp.concatenate([held[c, s * SIZE : (s + 1) * SIZE, :] for c in range(BLOCK)], axis=0)
         moved = dot(back, parts).astype(bf16)
         for i in range(0, SIZE, STEP):
-            to, at = divmod(s * SIZE + i, rows)
-            out_ref[host ^ to, at * BLOCK : (at + STEP) * BLOCK, :] = moved[
-                i * BLOCK : (i + STEP) * BLOCK
-            ]
+            store(s * SIZE + i, moved[i * BLOCK : (i + STEP) * BLOCK])
+
+
+def near_kernel(rows_ref, left, out_ref, right, held):
+    regroup(slices([rows_ref]), right, shuffle(BLOCK, SIZE))
+    rows = left.shape[1] // out_ref.shape[0]
+
+    def store(i, values):
+        to, at = divmod(i, rows)
+        out_ref[to, at * BLOCK : (at + STEP) * BLOCK, :] = values
+
+    multiply(left, right, held, store)
+
+
+def far_again_kernel(rows_ref, near_ref, *refs):
+    regroup(slices([rows_ref]), refs[-1], shuffle(BLOCK, SIZE))
+    far_kernel(refs[-1], near_ref, *refs[:-1])
+
+
+def far_kernel(right, near_ref, *refs):
+    lefts = refs[:-4]
+    out_ref, left, held, sems = refs[-4:]
+    half = len(lefts)
+    rows = lefts[0].shape[0] // BLOCK
+    host = lax.axis_index(("chan", "quarter"))
+    copies = [
+        pltpu.make_async_copy(near_ref.at[b], out_ref.at[host ^ b], sems.at[b]) for b in range(half)
+    ]
+    for copy in copies:
+        copy.start()
+    regroup(slices(lefts), left, shuffle(BLOCK, SIZE))
+
+    def store(i, values):
+        to, at = divmod(i, rows)
+        out_ref[host ^ (half + to), at * BLOCK : (at + STEP) * BLOCK, :] = values
+
+    multiply(left, right, held, store)
+    for copy in copies:
+        copy.wait()
 
 
 def final_kernel(x_ref, gate_ref, g_ref, s_ref, w_ref, b_ref, out_ref, made, leave):
@@ -281,43 +306,53 @@
 
     span = GATHER * rows
     gathers = devices // GATHER
-    grouped = pl.BlockSpec((BLOCK, span, k), lambda s: (0, s, 0))
+    right = right.reshape(devices * tall, k)
+    part = bfloat(half, tall, devices * rows)
+    spent = BLOCK * mine * mine * k
+    held = pltpu.VMEM((BLOCK, mine // 2, span), bf16)
+    scratch = [pltpu.VMEM((BLOCK, mine // 2, k), bf16), held, pltpu.SemaphoreType.DMA((half,))]
     if gathers == 1:
         limit = params()
-        blocks = dict(in_specs=[vmem], out_specs=vmem)
-        rest = dict(in_specs=[vmem] * (2 + half), out_specs=vmem)
+        early = dict(
+            in_specs=[vmem] * 2,
+            out_specs=[vmem] * 2,
+            out_shape=[part, bfloat(BLOCK, devices * rows, k)],
+            scratch_shapes=[held],
+        )
+        rest = dict(in_specs=[vmem] * (2 + half), out_specs=vmem, scratch_shapes=scratch)
     else:
         limit = params(60)
-        blocks = dict(
+        regrouped = [pltpu.VMEM((BLOCK, span, k), bf16)]
+        block = pl.BlockSpec((span * BLOCK, k), lambda s: (s, 0))
+        part_block = pl.BlockSpec((half, tall, span), lambda s: (0, 0, s))
+        early = dict(
             grid=(gathers,),
-            in_specs=[pl.BlockSpec((span * BLOCK, k), lambda s: (s, 0))],
-            out_specs=grouped,
+            in_specs=[block, whole((BLOCK, mine // 2, k))],
+            out_specs=[part_block],
+            out_shape=[part],
+            scratch_shapes=regrouped + [held],
         )
         rest = dict(
             grid=(gathers,),
-            in_specs=[grouped, whole((BLOCK, mine // 2, k))] + [whole((tall, k))] * half,
+            in_specs=[block, part_block] + [whole((tall, k))] * half,
             out_specs=pl.BlockSpec((hosts, tall, span), lambda s: (0, 0, s)),
+            scratch_shapes=scratch + regrouped,
         )
-    right = pl.pallas_call(
-        regroup_right_kernel,
-        **blocks,
-        out_shape=bfloat(BLOCK, devices * rows, k),
+    near, *regrouped = pl.pallas_call(
+        near_kernel,
+        **early,
         compiler_params=limit,
-        cost_estimate=cost(1 << 37, 4 * devices * tall * k),
-        name="regroup_right",
-    )(right.reshape(devices * tall, k))
+        cost_estimate=cost(1 << 37, 6 * BLOCK * mine * k),
+        name="near_products",
+    )(right, near)
     product = pl.pallas_call(
-        product_kernel,
+        far_kernel if regrouped else far_again_kernel,
         **rest,
         out_shape=bfloat(hosts, tall, devices * rows),
-        scratch_shapes=[
-            pltpu.VMEM((BLOCK, mine // 2, k), bf16),
-            pltpu.VMEM((BLOCK, mine, span), bf16),
-        ],
         compiler_params=limit,
-        cost_estimate=cost(2 * BLOCK * mine * mine * k, 6 * BLOCK * mine * k),
-        name="products",
-    )(right, near, *lefts[half:])
+        cost_estimate=cost(spent, 6 * BLOCK * mine * k),
+        name="far_products",
+    )(*regrouped or [right], near, *lefts[half:])
     product = lax.all_to_all(product, in_part, 0, 0, tiled=True)
 
     return pl.pallas_call(

time: 93.3 us -> 94.8 us (1.016)
  Pallas kernels: 13.5 us -> 15 us
    pallas_call x2, Pallas kernels: 2.74 us -> 4.32 us  [the longest x1 2.32 us: shards(): pl.pallas_call(far_kernel if regrouped else far_again_kernel, **rest, out...]
  transfers between devices with their start and end apart: 16 -> 16, of which waited for: 6 -> 6; matrix products, arithmetic and copies ran while one was open for 0% -> 0% of each run, Pallas kernels for 5% -> 6%
where the time goes in v17:
time: 94.8 us; the launch traced here: 94.4 us
  waiting for transfers between devices  29.1 us (31%)
  starting transfers between devices  26.4 us (28%)
  blocking collectives  21.1 us (22%)
  Pallas kernels  15 us (16%)
  local copies, waits for them, and re-layouts  2.73 us (3%)
    ppermute x15, waiting for transfers between devices, send(): return lax.ppermute(values, everywhere, pairs)  22.2 us
    all_to_all x1, blocking collectives, shards(): product = lax.all_to_all(product, in_part, 0, 0, tiled=True)  21.1 us
    ppermute x15, starting transfers between devices, send(): return lax.ppermute(values, everywhere, pairs)  19.1 us
    all_to_all x1, starting transfers between devices, shards(): lax.all_to_all(right.reshape(devices, tall, k), everywhere, 0, 0, tiled=T...  7.31 us
    all_to_all x1, waiting for transfers between devices, shards(): lax.all_to_all(right.reshape(devices, tall, k), everywhere, 0, 0, tiled=T...  6.89 us
    pallas_call x1, Pallas kernels, shards(): pl.pallas_call(right_kernel, grid=(steps,), in_specs=[row_block, whole((1...  4.86 us
    pallas_call x1, Pallas kernels, shards(): pl.pallas_call(left_kernel, grid=(steps,), in_specs=[row_block, whole((1,...  3.39 us
    unnamed x26, local copies, waits for them, and re-layouts  2.73 us
  transfers between devices with their start and end apart: 16, of which 6 were waited for; matrix products, arithmetic and copies ran while one was open for 0% of the time, Pallas kernels for 6%

profile of v17, /device:TPU:0, one launch (start us, length us, event | category | flops | bytes accessed | tf_op | source)
XLA Modules:
  0.0 94.4 jit_solution(2082965207362458143)
XLA Ops:
  0.0 4.9 %right_factor.1 = bf16[2,16,96,384]{3,2,1,0:T(8,128)(2,1)} custom-call(bf16[12,384,128]{2,1,0:T(8,128)(2,1)} %pair_ref.3, f32[1,128]{1,0:T(1,128)} %bitcast.12, f32[1,128]{1,0:T(1,128)} %bitcast.14, bf16[128,512]{1,0:T(8,128)(2,1)} %w_ref.4, f32[1,512]{1,0:T(1,128)} %bitcast.10), custom_call_target="tpu_custom_call" | custom-call | flops 301989888 | bytes 3538944 | tf_op jit(solution)/shard_map/right_factor/pallas_call | solution.py:240
  4.9 0.0 copy-start.8
  4.9 0.0 copy-start.9
  4.9 7.3 %all-to-all-start = ((bf16[32,96,384]{2,1,0:T(8,128)(2,1)}), bf16[32,96,384]{2,1,0:T(8,128)(2,1)S(1)}, u32[]{:S(2)}, u32[]{:S(2)}) async-start(bf16[32,96,384]{2,1,0:T(8,128)(2,1)} %bitcast.20), calls=%async_computation | async-start | bytes 4718592 | tf_op jit(solution)/shard_map/all_to_all | solution.py:256
  12.3 0.0 copy-start.3
  12.3 0.9 copy-done.3
  13.2 0.8 copy-done.5
  13.9 3.4 %left_factor.1 = (bf16[96,384]{1,0:T(8,128)(2,1)S(1)}, bf16[96,384]{1,0:T(8,128)(2,1)S(1)}, bf16[96,384]{1,0:T(8,128)(2,1)S(1)}, bf16[96,384]{1,0:T(8,128)(2,1)S...) custom-call(bf16[12,384,128]{2,1,0:T(8,128)(2,1)S(1)} %copy-done, ...), custom_call_target="tpu_custom_call" | custom-call | flops 301989888 | bytes 3538944 | tf_op jit(solution)/shard_map/left_factor/pallas_call | solution.py:262
  17.3 1.0 %copy-done.1 = bf16[12,384,128]{2,1,0:T(8,128)(2,1)} copy-done((bf16[12,384,128]{2,1,0:T(8,128)(2,1)}, bf16[12,384,128]{2,1,0:T(8,128)(2,1)S(1)}, u32[]{:S(2)}) %copy-start.1) | copy-done | bytes 1179672
  18.3 0.3 collective-permute-start
  18.6 1.7 %collective-permute-start.1 = (bf16[96,384]{1,0:T(8,128)(2,1)S(1)}, bf16[96,384]{1,0:T(8,128)(2,1)S(1)}, u32[]{:S(2)}, u32[]{:S(2)}) collective-permute-start(bf16[96,384]{1,0:T(8,128)(2,1)S(1)} %get-tuple-element.26), channel_id=1, source_target_pairs={{0,2},{1,3},{2,0},{3,1},{4,6},{5,7},{6,4},{7,5},{8,10},{9,11},{10,... | collective-permute-start | bytes 221192 | tf_op jit(solution)/shard_map/ppermute | solution.py:260
  20.3 0.0 collective-permute-start.2
  20.3 1.7 %collective-permute-start.3 = (bf16[96,384]{1,0:T(8,128)(2,1)S(1)}, bf16[96,384]{1,0:T(8,128)(2,1)S(1)}, u32[]{:S(2)}, u32[]{:S(2)}) collective-permute-start(bf16[96,384]{1,0:T(8,128)(2,1)S(1)} %get-tuple-element.28), channel_id=1, source_target_pairs={{0,4},{1,5},{2,6},{3,7},{4,0},{5,1},{6,2},{7,3},{8,12},{9,13},{10,... | collective-permute-start | bytes 221192 | tf_op jit(solution)/shard_map/ppermute | solution.py:260
  22.0 0.1 collective-permute-start.4
  22.1 0.0 collective-permute-done.refs_1_
  22.1 2.6 %collective-permute-start.5 = (bf16[96,384]{1,0:T(8,128)(2,1)S(1)}, bf16[96,384]{1,0:T(8,128)(2,1)S(1)}, u32[]{:S(2)}, u32[]{:S(2)}) collective-permute-start(bf16[96,384]{1,0:T(8,128)(2,1)S(1)} %get-tuple-element.30), channel_id=1, source_target_pairs={{0,6},{1,7},{2,4},{3,5},{4,2},{5,3},{6,0},{7,1},{8,14},{9,15},{10,... | collective-permute-start | bytes 221192 | tf_op jit(solution)/shard_map/ppermute | solution.py:260
  24.7 7.1 %collective-permute-done.1.refs_2_ = bf16[96,384]{1,0:T(8,128)(2,1)S(1)} collective-permute-done((bf16[96,384]{1,0:T(8,128)(2,1)S(1)}, bf16[96,384]{1,0:T(8,128)(2,1)S(1)}, u32[]{:S(2)}, u32[]{:S(2)}) %collective-permute-start.1) | collective-permute-done | bytes 73760 | tf_op jit(solution)/shard_map/ppermute | solution.py:260
  31.8 0.6 collective-permute-start.6
  32.4 0.2 collective-permute-done.2.refs_3_
  32.6 0.3 collective-permute-start.7
  32.9 0.0 collective-permute-done.3.refs_4_
  32.9 2.3 %collective-permute-start.8 = (bf16[96,384]{1,0:T(8,128)(2,1)S(1)}, bf16[96,384]{1,0:T(8,128)(2,1)S(1)}, u32[]{:S(2)}, u32[]{:S(2)}) collective-permute-start(bf16[96,384]{1,0:T(8,128)(2,1)S(1)} %get-tuple-element.35), channel_id=1, source_target_pairs={{0,9},{1,8},{2,11},{3,10},{4,13},{5,12},{6,15},{7,14},{8,1},{9,0},... | collective-permute-start | bytes 221192 | tf_op jit(solution)/shard_map/ppermute | solution.py:260
  35.1 0.0 collective-permute-done.4.refs_5_
  35.1 3.2 %collective-permute-start.9 = (bf16[96,384]{1,0:T(8,128)(2,1)S(1)}, bf16[96,384]{1,0:T(8,128)(2,1)S(1)}, u32[]{:S(2)}, u32[]{:S(2)}) collective-permute-start(bf16[96,384]{1,0:T(8,128)(2,1)S(1)} %get-tuple-element.36), channel_id=1, source_target_pairs={{0,10},{1,11},{2,8},{3,9},{4,14},{5,15},{6,12},{7,13},{8,2},{9,3},... | collective-permute-start | bytes 221192 | tf_op jit(solution)/shard_map/ppermute | solution.py:260
  38.3 3.9 %collective-permute-done.5.refs_6_ = bf16[96,384]{1,0:T(8,128)(2,1)S(1)} collective-permute-done((bf16[96,384]{1,0:T(8,128)(2,1)S(1)}, bf16[96,384]{1,0:T(8,128)(2,1)S(1)}, u32[]{:S(2)}, u32[]{:S(2)}) %collective-permute-start.5) | collective-permute-done | bytes 73760 | tf_op jit(solution)/shard_map/ppermute | solution.py:260
  42.2 0.0 collective-permute-start.10
  42.3 0.8 collective-permute-done.6.refs_7_
  43.1 0.0 collective-permute-start.11
  43.1 0.4 regroup_left.1.left
  43.4 10.1 %collective-permute-done.7.refs_0_ = bf16[96,384]{1,0:T(8,128)(2,1)S(1)} collective-permute-done((bf16[96,384]{1,0:T(8,128)(2,1)S(1)}, bf16[96,384]{1,0:T(8,128)(2,1)S(1)}, u32[]{:S(2)}, u32[]{:S(2)}) %collective-permute-start.7) | collective-permute-done | bytes 73760 | tf_op jit(solution)/shard_map/ppermute | solution.py:260
  53.5 1.9 %collective-permute-start.12 = (bf16[96,384]{1,0:T(8,128)(2,1)}, bf16[96,384]{1,0:T(8,128)(2,1)S(1)}, u32[]{:S(2)}, u32[]{:S(2)}) collective-permute-start(bf16[96,384]{1,0:T(8,128)(2,1)} %get-tuple-element.39), channel_id=1, source_target_pairs={{0,13},{1,12},{2,15},{3,14},{4,9},{5,8},{6,11},{7,10},{8,5},{9,4},... | collective-permute-start | bytes 221192 | tf_op jit(solution)/shard_map/ppermute | solution.py:260
  55.4 0.0 collective-permute-done.8.refs_1_
  55.4 2.8 %collective-permute-start.13 = (bf16[96,384]{1,0:T(8,128)(2,1)}, bf16[96,384]{1,0:T(8,128)(2,1)S(1)}, u32[]{:S(2)}, u32[]{:S(2)}) collective-permute-start(bf16[96,384]{1,0:T(8,128)(2,1)} %get-tuple-element.40), channel_id=1, source_target_pairs={{0,14},{1,15},{2,12},{3,13},{4,10},{5,11},{6,8},{7,9},{8,6},{9,7},... | collective-permute-start | bytes 221192 | tf_op jit(solution)/shard_map/ppermute | solution.py:260
  58.2 1.7 %collective-permute-start.14 = (bf16[96,384]{1,0:T(8,128)(2,1)}, bf16[96,384]{1,0:T(8,128)(2,1)S(1)}, u32[]{:S(2)}, u32[]{:S(2)}) collective-permute-start(bf16[96,384]{1,0:T(8,128)(2,1)} %get-tuple-element.41), channel_id=1, source_target_pairs={{0,15},{1,14},{2,13},{3,12},{4,11},{5,10},{6,9},{7,8},{8,7},{9,6},... | collective-permute-start | bytes 221192 | tf_op jit(solution)/shard_map/ppermute | solution.py:260
  59.9 6.9 %all-to-all-done = bf16[32,96,384]{2,1,0:T(8,128)(2,1)S(1)} async-done(((bf16[32,96,384]{2,1,0:T(8,128)(2,1)}), bf16[32,96,384]{2,1,0:T(8,128)(2,1)S(1)}, u32[]{:S(2)}, u32[]{:S(2)}) %all-to-all-start) | async-done | bytes 2359328 | tf_op jit(solution)/shard_map/all_to_all | solution.py:256
  66.8 2.0 %near_products.1 = (bf16[8,96,384]{2,1,0:T(8,128)(2,1)S(1)}, bf16[8,384,384]{2,1,0:T(8,128)(2,1)S(1)}) custom-call(bf16[3072,384]{1,0:T(8,128)(2,1)S(1)} %bitcast.9, bf16[8,96,384]{2,1,0:T(8,128)(2,1)S(1)} %regroup_left.1.left), custom_call_target="tpu_custom_call" | custom-call | flops 137438953472 | bytes 3538944 | tf_op jit(solution)/shard_map/near_products/pallas_call | solution.py:341
  68.8 0.0 collective-permute-done.10.refs_3_
  68.8 0.0 collective-permute-done.11.refs_4_
  68.9 0.0 collective-permute-done.13.refs_6_
  68.9 0.0 collective-permute-done.14.refs_7_
  68.9 2.3 %far_products.1 = bf16[16,96,384]{2,1,0:T(8,128)(2,1)S(1)} custom-call(bf16[8,384,384]{2,1,0:T(8,128)(2,1)S(1)} %get-tuple-element.32.right, bf16[8,96,384]{2,1,0:T(8,128)(2,1)S(1)} %get-tuple-element.33.near_ref, bf16[96,384]{1,0:T(8,128)(2,1)S(1)} %collective-permute-done.7.refs_0_, bf16[96,384]{1,0:T(8,128)(2,1)S(1)} %collective-permute-done.8.refs_1_, ...), custom_call_target="tpu_custom_call" | custom-call | flops 113246208 | bytes 3538944 | tf_op jit(solution)/shard_map/far_products/pallas_call | solution.py:348
  71.2 0.0 copy-start.2
  71.2 0.0 copy-start.4
  71.2 0.0 copy-start.10
  71.2 0.0 copy-start.11
  71.2 0.0 copy-start.12
  71.3 21.1 %all_to_all.10.x_ref = bf16[16,96,384]{2,1,0:T(8,128)(2,1)S(1)} all-to-all(bf16[16,96,384]{2,1,0:T(8,128)(2,1)S(1)} %far_products.1), channel_id=1, replica_groups=mesh['groups'=1,'part'=2,'chan'=8,'quarter'=2] {'chan','quarter'}, dimensions={0} | all-to-all | bytes 2359296 | tf_op jit(solution)/shard_map/all_to_all | solution.py:356
  92.4 2.1 %update.1 = bf16[12,384,128]{2,1,0:T(8,128)(2,1)} custom-call(bf16[16,96,384]{2,1,0:T(8,128)(2,1)S(1)} %all_to_all.10.x_ref, bf16[12,384,128]{2,1,0:T(8,128)(2,1)S(1)} %copy-done.2, f32[1,128]{1,0:T(1,128)S(1)} %bitcast.17, f32[1,128]{1,0:T(1,128)S(1)} %bitcast.18, bf16[128,128]{1,0:T(8,128)(2,1)S(1)} %copy-done.4, f32[1,128]{1,0:T(1,128)S(1)} %bitcast.19), custom_call_target="tpu_custom_call" | custom-call | flops 150994944 | bytes 3538944 | tf_op jit(solution)/shard_map/update/pallas_call | solution.py:358
  (17 shorter events, 0.0 us)
Async XLA Ops:
  4.9 7.4 %copy-start = (bf16[12,384,128]{2,1,0:T(8,128)(2,1)S(1)}, bf16[12,384,128]{2,1,0:T(8,128)(2,1)}, u32[]{:S(2)}) copy-start(bf16[12,384,128]{2,1,0:T(8,128)(2,1)} %pair_ref.3) | copy-start | bytes 3538948
  4.9 7.4 %copy-start.6 = (f32[512]{0:T(512)S(1)}, f32[512]{0:T(512)}, u32[]{:S(2)}) copy-start(f32[512]{0:T(512)} %param.15) | copy-start | bytes 6148
  4.9 7.4 %copy-start.7 = (f32[128]{0:T(128)S(1)}, f32[128]{0:T(128)}, u32[]{:S(2)}) copy-start(f32[128]{0:T(128)} %param.12) | copy-start | bytes 1540
  4.9 7.4 %copy-start.8 = (f32[128]{0:T(128)S(1)}, f32[128]{0:T(128)}, u32[]{:S(2)}) copy-start(f32[128]{0:T(128)} %param.13) | copy-start | bytes 1540
  4.9 7.4 %copy-start.9 = (f32[128]{0:T(128)S(1)}, f32[128]{0:T(128)}, u32[]{:S(2)}) copy-start(f32[128]{0:T(128)} %param.17) | copy-start | bytes 1540
  4.9 61.9 %all-to-all-start = ((bf16[32,96,384]{2,1,0:T(8,128)(2,1)}), bf16[32,96,384]{2,1,0:T(8,128)(2,1)S(1)}, u32[]{:S(2)}, u32[]{:S(2)}) async-start(bf16[32,96,384]{2,1,0:T(8,128)(2,1)} %bitcast.20), calls=%async_computation | async-start | bytes 4718592 | tf_op jit(solution)/shard_map/all_to_all | solution.py:256
  12.3 0.9 copy-start.3
  13.2 0.8 copy-start.5
  17.3 1.0 %copy-start.1 = (bf16[12,384,128]{2,1,0:T(8,128)(2,1)}, bf16[12,384,128]{2,1,0:T(8,128)(2,1)S(1)}, u32[]{:S(2)}) copy-start(bf16[12,384,128]{2,1,0:T(8,128)(2,1)S(1)} %get-tuple-element.42.gate_ref) | copy-start | bytes 3538948
  18.3 3.7 %collective-permute-start = (bf16[96,384]{1,0:T(8,128)(2,1)S(1)}, bf16[96,384]{1,0:T(8,128)(2,1)S(1)}, u32[]{:S(2)}, u32[]{:S(2)}) collective-permute-start(bf16[96,384]{1,0:T(8,128)(2,1)S(1)} %get-tuple-element.25), channel_id=1, source_target_pairs={{0,1},{1,0},{2,3},{3,2},{4,5},{5,4},{6,7},{7,6},{8,9},{9,8},{10,11... | collective-permute-start | bytes 221192 | tf_op jit(solution)/shard_map/ppermute | solution.py:260
  18.6 13.2 %collective-permute-start.1 = (bf16[96,384]{1,0:T(8,128)(2,1)S(1)}, bf16[96,384]{1,0:T(8,128)(2,1)S(1)}, u32[]{:S(2)}, u32[]{:S(2)}) collective-permute-start(bf16[96,384]{1,0:T(8,128)(2,1)S(1)} %get-tuple-element.26), channel_id=1, source_target_pairs={{0,2},{1,3},{2,0},{3,1},{4,6},{5,7},{6,4},{7,5},{8,10},{9,11},{10,... | collective-permute-start | bytes 221192 | tf_op jit(solution)/shard_map/ppermute | solution.py:260
  20.3 12.3 %collective-permute-start.2 = (bf16[96,384]{1,0:T(8,128)(2,1)S(1)}, bf16[96,384]{1,0:T(8,128)(2,1)S(1)}, u32[]{:S(2)}, u32[]{:S(2)}) collective-permute-start(bf16[96,384]{1,0:T(8,128)(2,1)S(1)} %get-tuple-element.27), channel_id=1, source_target_pairs={{0,3},{1,2},{2,1},{3,0},{4,7},{5,6},{6,5},{7,4},{8,11},{9,10},{10,... | collective-permute-start | bytes 221192 | tf_op jit(solution)/shard_map/ppermute | solution.py:260
  20.3 12.6 %collective-permute-start.3 = (bf16[96,384]{1,0:T(8,128)(2,1)S(1)}, bf16[96,384]{1,0:T(8,128)(2,1)S(1)}, u32[]{:S(2)}, u32[]{:S(2)}) collective-permute-start(bf16[96,384]{1,0:T(8,128)(2,1)S(1)} %get-tuple-element.28), channel_id=1, source_target_pairs={{0,4},{1,5},{2,6},{3,7},{4,0},{5,1},{6,2},{7,3},{8,12},{9,13},{10,... | collective-permute-start | bytes 221192 | tf_op jit(solution)/shard_map/ppermute | solution.py:260
  22.0 13.2 %collective-permute-start.4 = (bf16[96,384]{1,0:T(8,128)(2,1)S(1)}, bf16[96,384]{1,0:T(8,128)(2,1)S(1)}, u32[]{:S(2)}, u32[]{:S(2)}) collective-permute-start(bf16[96,384]{1,0:T(8,128)(2,1)S(1)} %get-tuple-element.29), channel_id=1, source_target_pairs={{0,5},{1,4},{2,7},{3,6},{4,1},{5,0},{6,3},{7,2},{8,13},{9,12},{10,... | collective-permute-start | bytes 221192 | tf_op jit(solution)/shard_map/ppermute | solution.py:260
  22.1 20.2 %collective-permute-start.5 = (bf16[96,384]{1,0:T(8,128)(2,1)S(1)}, bf16[96,384]{1,0:T(8,128)(2,1)S(1)}, u32[]{:S(2)}, u32[]{:S(2)}) collective-permute-start(bf16[96,384]{1,0:T(8,128)(2,1)S(1)} %get-tuple-element.30), channel_id=1, source_target_pairs={{0,6},{1,7},{2,4},{3,5},{4,2},{5,3},{6,0},{7,1},{8,14},{9,15},{10,... | collective-permute-start | bytes 221192 | tf_op jit(solution)/shard_map/ppermute | solution.py:260
  31.8 11.3 %collective-permute-start.6 = (bf16[96,384]{1,0:T(8,128)(2,1)S(1)}, bf16[96,384]{1,0:T(8,128)(2,1)S(1)}, u32[]{:S(2)}, u32[]{:S(2)}) collective-permute-start(bf16[96,384]{1,0:T(8,128)(2,1)S(1)} %get-tuple-element.31), channel_id=1, source_target_pairs={{0,7},{1,6},{2,5},{3,4},{4,3},{5,2},{6,1},{7,0},{8,15},{9,14},{10,... | collective-permute-start | bytes 221192 | tf_op jit(solution)/shard_map/ppermute | solution.py:260
  32.6 20.9 %collective-permute-start.7 = (bf16[96,384]{1,0:T(8,128)(2,1)S(1)}, bf16[96,384]{1,0:T(8,128)(2,1)S(1)}, u32[]{:S(2)}, u32[]{:S(2)}) collective-permute-start(bf16[96,384]{1,0:T(8,128)(2,1)S(1)} %get-tuple-element.34), channel_id=1, source_target_pairs={{0,8},{1,9},{2,10},{3,11},{4,12},{5,13},{6,14},{7,15},{8,0},{9,1},... | collective-permute-start | bytes 221192 | tf_op jit(solution)/shard_map/ppermute | solution.py:260
  32.9 22.6 %collective-permute-start.8 = (bf16[96,384]{1,0:T(8,128)(2,1)S(1)}, bf16[96,384]{1,0:T(8,128)(2,1)S(1)}, u32[]{:S(2)}, u32[]{:S(2)}) collective-permute-start(bf16[96,384]{1,0:T(8,128)(2,1)S(1)} %get-tuple-element.35), channel_id=1, source_target_pairs={{0,9},{1,8},{2,11},{3,10},{4,13},{5,12},{6,15},{7,14},{8,1},{9,0},... | collective-permute-start | bytes 221192 | tf_op jit(solution)/shard_map/ppermute | solution.py:260
  35.1 23.1 %collective-permute-start.9 = (bf16[96,384]{1,0:T(8,128)(2,1)S(1)}, bf16[96,384]{1,0:T(8,128)(2,1)S(1)}, u32[]{:S(2)}, u32[]{:S(2)}) collective-permute-start(bf16[96,384]{1,0:T(8,128)(2,1)S(1)} %get-tuple-element.36), channel_id=1, source_target_pairs={{0,10},{1,11},{2,8},{3,9},{4,14},{5,15},{6,12},{7,13},{8,2},{9,3},... | collective-permute-start | bytes 221192 | tf_op jit(solution)/shard_map/ppermute | solution.py:260
  42.2 26.6 %collective-permute-start.10 = (bf16[96,384]{1,0:T(8,128)(2,1)}, bf16[96,384]{1,0:T(8,128)(2,1)S(1)}, u32[]{:S(2)}, u32[]{:S(2)}) collective-permute-start(bf16[96,384]{1,0:T(8,128)(2,1)} %get-tuple-element.37), channel_id=1, source_target_pairs={{0,11},{1,10},{2,9},{3,8},{4,15},{5,14},{6,13},{7,12},{8,3},{9,2},... | collective-permute-start | bytes 221192 | tf_op jit(solution)/shard_map/ppermute | solution.py:260
  43.1 25.8 %collective-permute-start.11 = (bf16[96,384]{1,0:T(8,128)(2,1)}, bf16[96,384]{1,0:T(8,128)(2,1)S(1)}, u32[]{:S(2)}, u32[]{:S(2)}) collective-permute-start(bf16[96,384]{1,0:T(8,128)(2,1)} %get-tuple-element.38), channel_id=1, source_target_pairs={{0,12},{1,13},{2,14},{3,15},{4,8},{5,9},{6,10},{7,11},{8,4},{9,5},... | collective-permute-start | bytes 221192 | tf_op jit(solution)/shard_map/ppermute | solution.py:260
  53.5 15.4 %collective-permute-start.12 = (bf16[96,384]{1,0:T(8,128)(2,1)}, bf16[96,384]{1,0:T(8,128)(2,1)S(1)}, u32[]{:S(2)}, u32[]{:S(2)}) collective-permute-start(bf16[96,384]{1,0:T(8,128)(2,1)} %get-tuple-element.39), channel_id=1, source_target_pairs={{0,13},{1,12},{2,15},{3,14},{4,9},{5,8},{6,11},{7,10},{8,5},{9,4},... | collective-permute-start | bytes 221192 | tf_op jit(solution)/shard_map/ppermute | solution.py:260
  55.4 13.4 %collective-permute-start.13 = (bf16[96,384]{1,0:T(8,128)(2,1)}, bf16[96,384]{1,0:T(8,128)(2,1)S(1)}, u32[]{:S(2)}, u32[]{:S(2)}) collective-permute-start(bf16[96,384]{1,0:T(8,128)(2,1)} %get-tuple-element.40), channel_id=1, source_target_pairs={{0,14},{1,15},{2,12},{3,13},{4,10},{5,11},{6,8},{7,9},{8,6},{9,7},... | collective-permute-start | bytes 221192 | tf_op jit(solution)/shard_map/ppermute | solution.py:260
  58.2 10.6 %collective-permute-start.14 = (bf16[96,384]{1,0:T(8,128)(2,1)}, bf16[96,384]{1,0:T(8,128)(2,1)S(1)}, u32[]{:S(2)}, u32[]{:S(2)}) collective-permute-start(bf16[96,384]{1,0:T(8,128)(2,1)} %get-tuple-element.41), channel_id=1, source_target_pairs={{0,15},{1,14},{2,13},{3,12},{4,11},{5,10},{6,9},{7,8},{8,7},{9,6},... | collective-permute-start | bytes 221192 | tf_op jit(solution)/shard_map/ppermute | solution.py:260
  71.2 21.1 %copy-start.2 = (bf16[12,384,128]{2,1,0:T(8,128)(2,1)S(1)}, bf16[12,384,128]{2,1,0:T(8,128)(2,1)}, u32[]{:S(2)}) copy-start(bf16[12,384,128]{2,1,0:T(8,128)(2,1)} %copy-done.1) | copy-start | bytes 3538948
  71.2 21.1 %copy-start.4 = (bf16[128,128]{1,0:T(8,128)(2,1)S(1)}, bf16[128,128]{1,0:T(8,128)(2,1)}, u32[]{:S(2)}) copy-start(bf16[128,128]{1,0:T(8,128)(2,1)} %w_ref.5) | copy-start | bytes 98308
  71.2 21.1 %copy-start.10 = (f32[128]{0:T(128)S(1)}, f32[128]{0:T(128)}, u32[]{:S(2)}) copy-start(f32[128]{0:T(128)} %param.18) | copy-start | bytes 1540
  71.2 21.1 %copy-start.11 = (f32[128]{0:T(128)S(1)}, f32[128]{0:T(128)}, u32[]{:S(2)}) copy-start(f32[128]{0:T(128)} %param.19) | copy-start | bytes 1540
  71.2 21.1 %copy-start.12 = (f32[128]{0:T(128)S(1)}, f32[128]{0:T(128)}, u32[]{:S(2)}) copy-start(f32[128]{0:T(128)} %param.21) | copy-start | bytes 1540

commit v18 on v16

--- a/solution.py
+++ b/solution.py
@@ -12,6 +12,7 @@
 CHANNELS = 128
 BLOCK = 8
 STEP = 4
+PAIRED = 2
 SIZE = 32
 LANES = 128
 GATHER = 32
@@ -64,23 +65,60 @@
     return sigmoid(both[:width]) * both[width:]
 
 
-def as_rows(values, k):
+def as_rows(values, k, step=STEP):
     hosts = values.shape[0] // BLOCK
     return jnp.concatenate(
-        [values[:, r * k : (r + 1) * k].reshape(hosts, BLOCK, k) for r in range(STEP)], axis=1
+        [values[:, r * k : (r + 1) * k].reshape(hosts, BLOCK, k) for r in range(step)], axis=1
     )
 
 
-def right_kernel(pair_ref, gain_ref, shift_ref, w_ref, b_ref, out_ref):
-    k, width = pair_ref.shape[1:]
-    half = w_ref.shape[1] // 2
-    x = pair_ref[...].astype(f32).reshape(STEP * k, width)
-    normed = normalize(x, gain_ref[...], shift_ref[...])
-    both = dot(normed, w_ref[...]) + b_ref[...]
-    values = sigmoid(both[:, :half]) * both[:, half:]
-    out = as_rows(values.T, k).astype(bf16)
-    for p in range(out_ref.shape[0]):
-        out_ref[p] = out
+def turns_of(rows):
+    cuts = [0, PAIRED, *range(PAIRED + STEP, rows - PAIRED + 1, STEP), rows]
+    return list(zip(cuts[:-1], (n - m for m, n in zip(cuts[:-1], cuts[1:]))))
+
+
+def right_kernel(
+    pair_ref, gain_ref, shift_ref, w_ref, b_ref, out_ref, pair, gain, shift, w, bias, made,
+    arrive, leave, sems,
+):
+    rows, k, width = pair.shape
+    half = w.shape[1]
+    turns = turns_of(rows)
+    loads = [
+        pltpu.make_async_copy(pair_ref.at[pl.ds(r, size)], pair.at[pl.ds(r, size)], arrive.at[n])
+        for n, (r, size) in enumerate(turns)
+    ]
+    small = [
+        pltpu.make_async_copy(ref, to, sems.at[n])
+        for n, (ref, to) in enumerate(
+            [
+                (w_ref.at[:, pl.ds(half, half)], w),
+                (b_ref.at[:, pl.ds(half, half)], bias),
+                (gain_ref, gain),
+                (shift_ref, shift),
+            ]
+        )
+    ]
+    for copy in loads[:1] + small + loads[1:]:
+        copy.start()
+    for copy in small:
+        copy.wait()
+    stores = []
+    for n, (r, size) in enumerate(turns):
+        loads[n].wait()
+        x = pair[r : r + size].astype(f32).reshape(size * k, width)
+        normed = normalize(x, gain[...], shift[...])
+        at = pl.ds(r * BLOCK, size * BLOCK)
+        both = dot(normed, w[...]) + bias[...]
+        values = sigmoid(both[:, : half // 2]) * both[:, half // 2 :]
+        made[:, at, :] = as_rows(values.T, k, size).astype(bf16)
+        for p in range(out_ref.shape[0]):
+            stores.append(
+                pltpu.make_async_copy(made.at[:, at, :], out_ref.at[p, :, at, :], leave.at[p, n])
+            )
+            stores[-1].start()
+    for store in stores:
+        store.wait()
 
 
 def left_kernel(pair_ref, gain_ref, shift_ref, w_ref, b_ref, gw_ref, gb_ref, *refs):
@@ -212,18 +250,23 @@
 
     vmem = pl.BlockSpec(memory_space=pltpu.VMEM)
     anywhere = pl.BlockSpec(memory_space=pl.ANY)
+    turns = len(turns_of(rows))
     right = pl.pallas_call(
         right_kernel,
-        grid=(steps,),
-        in_specs=[
-            row_block,
-            whole((1, width)),
-            whole((1, width)),
-            pl.BlockSpec((width, 2 * hidden), lambda s: (0, 1)),
-            pl.BlockSpec((1, 2 * hidden), lambda s: (0, 1)),
+        in_specs=[anywhere] * 5,
+        out_specs=anywhere,
+        out_shape=bfloat(parts, hosts, tall, k),
+        scratch_shapes=[
+            pltpu.VMEM((rows, k, width), bf16),
+            pltpu.VMEM((1, width), f32),
+            pltpu.VMEM((1, width), f32),
+            pltpu.VMEM((width, 2 * hidden), bf16),
+            pltpu.VMEM((1, 2 * hidden), f32),
+            pltpu.VMEM((hosts, tall, k), bf16),
+            pltpu.SemaphoreType.DMA((turns,)),
+            pltpu.SemaphoreType.DMA((parts, turns)),
+            pltpu.SemaphoreType.DMA((4,)),
         ],
-        out_specs=pl.BlockSpec((parts, hosts, STEP * BLOCK, k), lambda s: (0, 0, s, 0)),
-        out_shape=bfloat(parts, hosts, tall, k),
         compiler_params=params(60),
         cost_estimate=cost(4 * work * hidden, 6 * work),
         name="right_factor",

time: 93.3 us -> 94.1 us (level)
  no operation moved by 1% of the time
where the time goes in v18:
time: 94.1 us; the launch traced here: 93.8 us
  waiting for transfers between devices  29.1 us (31%)
  starting transfers between devices  26.4 us (28%)
  blocking collectives  21.1 us (22%)
  Pallas kernels  14.3 us (15%)
  local copies, waits for them, and re-layouts  2.73 us (3%)
    ppermute x15, waiting for transfers between devices, send(): return lax.ppermute(values, everywhere, pairs)  22.2 us
    all_to_all x1, blocking collectives, shards(): product = lax.all_to_all(product, in_part, 0, 0, tiled=True)  21.1 us
    ppermute x15, starting transfers between devices, send(): return lax.ppermute(values, everywhere, pairs)  19 us
    all_to_all x1, starting transfers between devices, shards(): lax.all_to_all(right.reshape(devices, tall, k), everywhere, 0, 0, tiled=T...  7.3 us
    all_to_all x1, waiting for transfers between devices, shards(): lax.all_to_all(right.reshape(devices, tall, k), everywhere, 0, 0, tiled=T...  6.88 us
    pallas_call x1, Pallas kernels, shards(): pl.pallas_call(right_kernel, in_specs=[anywhere] * 5, out_specs=anywhere,...  5.76 us
    pallas_call x1, Pallas kernels, shards(): pl.pallas_call(left_kernel, grid=(steps,), in_specs=[row_block, whole((1,...  3.39 us
    unnamed x26, local copies, waits for them, and re-layouts  2.73 us
  transfers between devices with their start and end apart: 16, of which 6 were waited for; matrix products, arithmetic and copies ran while one was open for 0% of the time, Pallas kernels for 5%

profile of v18, /device:TPU:0, one launch (start us, length us, event | category | flops | bytes accessed | tf_op | source)
XLA Modules:
  0.0 93.8 jit_solution(5201981234295290546)
XLA Ops:
  0.0 5.8 %right_factor.1 = bf16[2,16,96,384]{3,2,1,0:T(8,128)(2,1)} custom-call(bf16[12,384,128]{2,1,0:T(8,128)(2,1)} %pair_ref.3, f32[1,128]{1,0:T(1,128)} %bitcast.12, f32[1,128]{1,0:T(1,128)} %bitcast.14, bf16[128,512]{1,0:T(8,128)(2,1)} %w_ref.4, f32[1,512]{1,0:T(1,128)} %bitcast.10), custom_call_target="tpu_custom_call" | custom-call | flops 301989888 | bytes 3538944 | tf_op jit(solution)/shard_map/right_factor/pallas_call | solution.py:254
  5.8 0.0 copy-start
  5.8 0.0 copy-start.6
  5.8 0.0 copy-start.7
  5.8 0.0 copy-start.8
  5.8 0.0 copy-start.9
  5.8 7.3 %all-to-all-start = ((bf16[32,96,384]{2,1,0:T(8,128)(2,1)}), bf16[32,96,384]{2,1,0:T(8,128)(2,1)S(1)}, u32[]{:S(2)}, u32[]{:S(2)}) async-start(bf16[32,96,384]{2,1,0:T(8,128)(2,1)} %bitcast.20), calls=%async_computation | async-start | bytes 4718592 | tf_op jit(solution)/shard_map/all_to_all | solution.py:274
  13.2 0.0 copy-start.3
  13.2 0.9 copy-done.3
  14.1 0.8 copy-done.5
  14.9 3.4 %left_factor.1 = (bf16[96,384]{1,0:T(8,128)(2,1)S(1)}, bf16[96,384]{1,0:T(8,128)(2,1)S(1)}, bf16[96,384]{1,0:T(8,128)(2,1)S(1)}, bf16[96,384]{1,0:T(8,128)(2,1)S...) custom-call(bf16[12,384,128]{2,1,0:T(8,128)(2,1)S(1)} %copy-done, ...), custom_call_target="tpu_custom_call" | custom-call | flops 301989888 | bytes 3538944 | tf_op jit(solution)/shard_map/left_factor/pallas_call | solution.py:280
  18.3 1.0 %copy-done.1 = bf16[12,384,128]{2,1,0:T(8,128)(2,1)} copy-done((bf16[12,384,128]{2,1,0:T(8,128)(2,1)}, bf16[12,384,128]{2,1,0:T(8,128)(2,1)S(1)}, u32[]{:S(2)}) %copy-start.1) | copy-done | bytes 1179672
  19.3 0.2 collective-permute-start
  19.5 1.7 %collective-permute-start.1 = (bf16[96,384]{1,0:T(8,128)(2,1)S(1)}, bf16[96,384]{1,0:T(8,128)(2,1)S(1)}, u32[]{:S(2)}, u32[]{:S(2)}) collective-permute-start(bf16[96,384]{1,0:T(8,128)(2,1)S(1)} %get-tuple-element.24), channel_id=1, source_target_pairs={{0,2},{1,3},{2,0},{3,1},{4,6},{5,7},{6,4},{7,5},{8,10},{9,11},{10,... | collective-permute-start | bytes 221192 | tf_op jit(solution)/shard_map/ppermute | solution.py:278
  21.2 0.0 collective-permute-start.2
  21.2 1.7 %collective-permute-start.3 = (bf16[96,384]{1,0:T(8,128)(2,1)S(1)}, bf16[96,384]{1,0:T(8,128)(2,1)S(1)}, u32[]{:S(2)}, u32[]{:S(2)}) collective-permute-start(bf16[96,384]{1,0:T(8,128)(2,1)S(1)} %get-tuple-element.26), channel_id=1, source_target_pairs={{0,4},{1,5},{2,6},{3,7},{4,0},{5,1},{6,2},{7,3},{8,12},{9,13},{10,... | collective-permute-start | bytes 221192 | tf_op jit(solution)/shard_map/ppermute | solution.py:278
  22.9 0.1 collective-permute-start.4
  23.0 0.0 collective-permute-done.refs_1_
  23.0 2.6 %collective-permute-start.5 = (bf16[96,384]{1,0:T(8,128)(2,1)S(1)}, bf16[96,384]{1,0:T(8,128)(2,1)S(1)}, u32[]{:S(2)}, u32[]{:S(2)}) collective-permute-start(bf16[96,384]{1,0:T(8,128)(2,1)S(1)} %get-tuple-element.28), channel_id=1, source_target_pairs={{0,6},{1,7},{2,4},{3,5},{4,2},{5,3},{6,0},{7,1},{8,14},{9,15},{10,... | collective-permute-start | bytes 221192 | tf_op jit(solution)/shard_map/ppermute | solution.py:278
  25.6 7.1 %collective-permute-done.1.refs_2_ = bf16[96,384]{1,0:T(8,128)(2,1)S(1)} collective-permute-done((bf16[96,384]{1,0:T(8,128)(2,1)S(1)}, bf16[96,384]{1,0:T(8,128)(2,1)S(1)}, u32[]{:S(2)}, u32[]{:S(2)}) %collective-permute-start.1) | collective-permute-done | bytes 73760 | tf_op jit(solution)/shard_map/ppermute | solution.py:278
  32.7 0.6 collective-permute-start.6
  33.3 0.2 collective-permute-done.2.refs_3_
  33.5 0.3 collective-permute-start.7
  33.8 2.3 %collective-permute-start.8 = (bf16[96,384]{1,0:T(8,128)(2,1)S(1)}, bf16[96,384]{1,0:T(8,128)(2,1)S(1)}, u32[]{:S(2)}, u32[]{:S(2)}) collective-permute-start(bf16[96,384]{1,0:T(8,128)(2,1)S(1)} %get-tuple-element.31), channel_id=1, source_target_pairs={{0,9},{1,8},{2,11},{3,10},{4,13},{5,12},{6,15},{7,14},{8,1},{9,0},... | collective-permute-start | bytes 221192 | tf_op jit(solution)/shard_map/ppermute | solution.py:278
  36.1 0.0 collective-permute-done.4.refs_5_
  36.1 3.2 %collective-permute-start.9 = (bf16[96,384]{1,0:T(8,128)(2,1)S(1)}, bf16[96,384]{1,0:T(8,128)(2,1)S(1)}, u32[]{:S(2)}, u32[]{:S(2)}) collective-permute-start(bf16[96,384]{1,0:T(8,128)(2,1)S(1)} %get-tuple-element.32), channel_id=1, source_target_pairs={{0,10},{1,11},{2,8},{3,9},{4,14},{5,15},{6,12},{7,13},{8,2},{9,3},... | collective-permute-start | bytes 221192 | tf_op jit(solution)/shard_map/ppermute | solution.py:278
  39.2 3.9 %collective-permute-done.5.refs_6_ = bf16[96,384]{1,0:T(8,128)(2,1)S(1)} collective-permute-done((bf16[96,384]{1,0:T(8,128)(2,1)S(1)}, bf16[96,384]{1,0:T(8,128)(2,1)S(1)}, u32[]{:S(2)}, u32[]{:S(2)}) %collective-permute-start.5) | collective-permute-done | bytes 73760 | tf_op jit(solution)/shard_map/ppermute | solution.py:278
  43.2 0.0 collective-permute-start.10
  43.2 0.8 collective-permute-done.6.refs_7_
  44.0 0.0 collective-permute-start.11
  44.0 0.4 regroup_left.1.near
  44.3 10.1 %collective-permute-done.7.refs_0_ = bf16[96,384]{1,0:T(8,128)(2,1)S(1)} collective-permute-done((bf16[96,384]{1,0:T(8,128)(2,1)S(1)}, bf16[96,384]{1,0:T(8,128)(2,1)S(1)}, u32[]{:S(2)}, u32[]{:S(2)}) %collective-permute-start.7) | collective-permute-done | bytes 73760 | tf_op jit(solution)/shard_map/ppermute | solution.py:278
  54.4 1.9 %collective-permute-start.12 = (bf16[96,384]{1,0:T(8,128)(2,1)}, bf16[96,384]{1,0:T(8,128)(2,1)S(1)}, u32[]{:S(2)}, u32[]{:S(2)}) collective-permute-start(bf16[96,384]{1,0:T(8,128)(2,1)} %get-tuple-element.35), channel_id=1, source_target_pairs={{0,13},{1,12},{2,15},{3,14},{4,9},{5,8},{6,11},{7,10},{8,5},{9,4},... | collective-permute-start | bytes 221192 | tf_op jit(solution)/shard_map/ppermute | solution.py:278
  56.4 2.8 %collective-permute-start.13 = (bf16[96,384]{1,0:T(8,128)(2,1)}, bf16[96,384]{1,0:T(8,128)(2,1)S(1)}, u32[]{:S(2)}, u32[]{:S(2)}) collective-permute-start(bf16[96,384]{1,0:T(8,128)(2,1)} %get-tuple-element.36), channel_id=1, source_target_pairs={{0,14},{1,15},{2,12},{3,13},{4,10},{5,11},{6,8},{7,9},{8,6},{9,7},... | collective-permute-start | bytes 221192 | tf_op jit(solution)/shard_map/ppermute | solution.py:278
  59.2 1.7 %collective-permute-start.14 = (bf16[96,384]{1,0:T(8,128)(2,1)}, bf16[96,384]{1,0:T(8,128)(2,1)S(1)}, u32[]{:S(2)}, u32[]{:S(2)}) collective-permute-start(bf16[96,384]{1,0:T(8,128)(2,1)} %get-tuple-element.37), channel_id=1, source_target_pairs={{0,15},{1,14},{2,13},{3,12},{4,11},{5,10},{6,9},{7,8},{8,7},{9,6},... | collective-permute-start | bytes 221192 | tf_op jit(solution)/shard_map/ppermute | solution.py:278
  60.9 6.9 %all-to-all-done = bf16[32,96,384]{2,1,0:T(8,128)(2,1)S(1)} async-done(((bf16[32,96,384]{2,1,0:T(8,128)(2,1)}), bf16[32,96,384]{2,1,0:T(8,128)(2,1)S(1)}, u32[]{:S(2)}, u32[]{:S(2)}) %all-to-all-start) | async-done | bytes 2359328 | tf_op jit(solution)/shard_map/all_to_all | solution.py:274
  67.7 1.0 %regroup_right.1.right = bf16[8,384,384]{2,1,0:T(8,128)(2,1)S(1)} custom-call(bf16[3072,384]{1,0:T(8,128)(2,1)S(1)} %bitcast.9), custom_call_target="tpu_custom_call" | custom-call | flops 137438953472 | bytes 4718592 | tf_op jit(solution)/shard_map/regroup_right/pallas_call | solution.py:344
  68.7 0.0 collective-permute-done.11.refs_4_
  68.7 0.0 collective-permute-done.12.refs_5_
  68.8 0.0 collective-permute-done.14.refs_7_
  68.8 1.8 %products.1 = bf16[16,96,384]{2,1,0:T(8,128)(2,1)S(1)} custom-call(bf16[8,384,384]{2,1,0:T(8,128)(2,1)S(1)} %regroup_right.1.right, bf16[8,96,384]{2,1,0:T(8,128)(2,1)S(1)} %regroup_left.1.near, bf16[96,384]{1,0:T(8,128)(2,1)S(1)} %collective-permute-done.7.refs_0_, bf16[96,384]{1,0:T(8,128)(2,1)S(1)} %collective-permute-done.8.refs_1_, ...), custom_call_target="tpu_custom_call" | custom-call | flops 226492416 | bytes 3538944 | tf_op jit(solution)/shard_map/products/pallas_call | solution.py:352
  70.5 0.0 copy-start.2
  70.5 0.0 copy-start.4
  70.6 0.0 copy-start.10
  70.6 0.0 copy-start.11
  70.6 0.0 copy-start.12
  70.6 21.1 %all_to_all.10.x_ref = bf16[16,96,384]{2,1,0:T(8,128)(2,1)S(1)} all-to-all(bf16[16,96,384]{2,1,0:T(8,128)(2,1)S(1)} %products.1), channel_id=1, replica_groups=mesh['groups'=1,'part'=2,'chan'=8,'quarter'=2] {'chan','quarter'}, dimensions={0} | all-to-all | bytes 2359296 | tf_op jit(solution)/shard_map/all_to_all | solution.py:364
  91.7 2.1 %update.1 = bf16[12,384,128]{2,1,0:T(8,128)(2,1)} custom-call(bf16[16,96,384]{2,1,0:T(8,128)(2,1)S(1)} %all_to_all.10.x_ref, bf16[12,384,128]{2,1,0:T(8,128)(2,1)S(1)} %copy-done.2, f32[1,128]{1,0:T(1,128)S(1)} %bitcast.17, f32[1,128]{1,0:T(1,128)S(1)} %bitcast.18, bf16[128,128]{1,0:T(8,128)(2,1)S(1)} %copy-done.4, f32[1,128]{1,0:T(1,128)S(1)} %bitcast.19), custom_call_target="tpu_custom_call" | custom-call | flops 150994944 | bytes 3538944 | tf_op jit(solution)/shard_map/update/pallas_call | solution.py:366
  (17 shorter events, 0.0 us)
Async XLA Ops:
  5.8 7.4 %copy-start = (bf16[12,384,128]{2,1,0:T(8,128)(2,1)S(1)}, bf16[12,384,128]{2,1,0:T(8,128)(2,1)}, u32[]{:S(2)}) copy-start(bf16[12,384,128]{2,1,0:T(8,128)(2,1)} %pair_ref.3) | copy-start | bytes 3538948
  5.8 7.4 %copy-start.6 = (f32[512]{0:T(512)S(1)}, f32[512]{0:T(512)}, u32[]{:S(2)}) copy-start(f32[512]{0:T(512)} %param.15) | copy-start | bytes 6148
  5.8 7.4 %copy-start.7 = (f32[128]{0:T(128)S(1)}, f32[128]{0:T(128)}, u32[]{:S(2)}) copy-start(f32[128]{0:T(128)} %param.12) | copy-start | bytes 1540
  5.8 7.4 %copy-start.8 = (f32[128]{0:T(128)S(1)}, f32[128]{0:T(128)}, u32[]{:S(2)}) copy-start(f32[128]{0:T(128)} %param.13) | copy-start | bytes 1540
  5.8 7.4 %copy-start.9 = (f32[128]{0:T(128)S(1)}, f32[128]{0:T(128)}, u32[]{:S(2)}) copy-start(f32[128]{0:T(128)} %param.17) | copy-start | bytes 1540
  5.8 61.9 %all-to-all-start = ((bf16[32,96,384]{2,1,0:T(8,128)(2,1)}), bf16[32,96,384]{2,1,0:T(8,128)(2,1)S(1)}, u32[]{:S(2)}, u32[]{:S(2)}) async-start(bf16[32,96,384]{2,1,0:T(8,128)(2,1)} %bitcast.20), calls=%async_computation | async-start | bytes 4718592 | tf_op jit(solution)/shard_map/all_to_all | solution.py:274
  13.2 0.9 copy-start.3
  14.1 0.8 copy-start.5
  18.2 1.0 %copy-start.1 = (bf16[12,384,128]{2,1,0:T(8,128)(2,1)}, bf16[12,384,128]{2,1,0:T(8,128)(2,1)S(1)}, u32[]{:S(2)}) copy-start(bf16[12,384,128]{2,1,0:T(8,128)(2,1)S(1)} %get-tuple-element.38.gate_ref) | copy-start | bytes 3538948
  19.3 3.7 %collective-permute-start = (bf16[96,384]{1,0:T(8,128)(2,1)S(1)}, bf16[96,384]{1,0:T(8,128)(2,1)S(1)}, u32[]{:S(2)}, u32[]{:S(2)}) collective-permute-start(bf16[96,384]{1,0:T(8,128)(2,1)S(1)} %get-tuple-element.23), channel_id=1, source_target_pairs={{0,1},{1,0},{2,3},{3,2},{4,5},{5,4},{6,7},{7,6},{8,9},{9,8},{10,11... | collective-permute-start | bytes 221192 | tf_op jit(solution)/shard_map/ppermute | solution.py:278
  19.5 13.2 %collective-permute-start.1 = (bf16[96,384]{1,0:T(8,128)(2,1)S(1)}, bf16[96,384]{1,0:T(8,128)(2,1)S(1)}, u32[]{:S(2)}, u32[]{:S(2)}) collective-permute-start(bf16[96,384]{1,0:T(8,128)(2,1)S(1)} %get-tuple-element.24), channel_id=1, source_target_pairs={{0,2},{1,3},{2,0},{3,1},{4,6},{5,7},{6,4},{7,5},{8,10},{9,11},{10,... | collective-permute-start | bytes 221192 | tf_op jit(solution)/shard_map/ppermute | solution.py:278
  21.2 12.3 %collective-permute-start.2 = (bf16[96,384]{1,0:T(8,128)(2,1)S(1)}, bf16[96,384]{1,0:T(8,128)(2,1)S(1)}, u32[]{:S(2)}, u32[]{:S(2)}) collective-permute-start(bf16[96,384]{1,0:T(8,128)(2,1)S(1)} %get-tuple-element.25), channel_id=1, source_target_pairs={{0,3},{1,2},{2,1},{3,0},{4,7},{5,6},{6,5},{7,4},{8,11},{9,10},{10,... | collective-permute-start | bytes 221192 | tf_op jit(solution)/shard_map/ppermute | solution.py:278
  21.2 12.6 %collective-permute-start.3 = (bf16[96,384]{1,0:T(8,128)(2,1)S(1)}, bf16[96,384]{1,0:T(8,128)(2,1)S(1)}, u32[]{:S(2)}, u32[]{:S(2)}) collective-permute-start(bf16[96,384]{1,0:T(8,128)(2,1)S(1)} %get-tuple-element.26), channel_id=1, source_target_pairs={{0,4},{1,5},{2,6},{3,7},{4,0},{5,1},{6,2},{7,3},{8,12},{9,13},{10,... | collective-permute-start | bytes 221192 | tf_op jit(solution)/shard_map/ppermute | solution.py:278
  22.9 13.2 %collective-permute-start.4 = (bf16[96,384]{1,0:T(8,128)(2,1)S(1)}, bf16[96,384]{1,0:T(8,128)(2,1)S(1)}, u32[]{:S(2)}, u32[]{:S(2)}) collective-permute-start(bf16[96,384]{1,0:T(8,128)(2,1)S(1)} %get-tuple-element.27), channel_id=1, source_target_pairs={{0,5},{1,4},{2,7},{3,6},{4,1},{5,0},{6,3},{7,2},{8,13},{9,12},{10,... | collective-permute-start | bytes 221192 | tf_op jit(solution)/shard_map/ppermute | solution.py:278
  23.0 20.2 %collective-permute-start.5 = (bf16[96,384]{1,0:T(8,128)(2,1)S(1)}, bf16[96,384]{1,0:T(8,128)(2,1)S(1)}, u32[]{:S(2)}, u32[]{:S(2)}) collective-permute-start(bf16[96,384]{1,0:T(8,128)(2,1)S(1)} %get-tuple-element.28), channel_id=1, source_target_pairs={{0,6},{1,7},{2,4},{3,5},{4,2},{5,3},{6,0},{7,1},{8,14},{9,15},{10,... | collective-permute-start | bytes 221192 | tf_op jit(solution)/shard_map/ppermute | solution.py:278
  32.7 11.3 %collective-permute-start.6 = (bf16[96,384]{1,0:T(8,128)(2,1)S(1)}, bf16[96,384]{1,0:T(8,128)(2,1)S(1)}, u32[]{:S(2)}, u32[]{:S(2)}) collective-permute-start(bf16[96,384]{1,0:T(8,128)(2,1)S(1)} %get-tuple-element.29), channel_id=1, source_target_pairs={{0,7},{1,6},{2,5},{3,4},{4,3},{5,2},{6,1},{7,0},{8,15},{9,14},{10,... | collective-permute-start | bytes 221192 | tf_op jit(solution)/shard_map/ppermute | solution.py:278
  33.5 20.9 %collective-permute-start.7 = (bf16[96,384]{1,0:T(8,128)(2,1)S(1)}, bf16[96,384]{1,0:T(8,128)(2,1)S(1)}, u32[]{:S(2)}, u32[]{:S(2)}) collective-permute-start(bf16[96,384]{1,0:T(8,128)(2,1)S(1)} %get-tuple-element.30), channel_id=1, source_target_pairs={{0,8},{1,9},{2,10},{3,11},{4,12},{5,13},{6,14},{7,15},{8,0},{9,1},... | collective-permute-start | bytes 221192 | tf_op jit(solution)/shard_map/ppermute | solution.py:278
  33.8 22.6 %collective-permute-start.8 = (bf16[96,384]{1,0:T(8,128)(2,1)S(1)}, bf16[96,384]{1,0:T(8,128)(2,1)S(1)}, u32[]{:S(2)}, u32[]{:S(2)}) collective-permute-start(bf16[96,384]{1,0:T(8,128)(2,1)S(1)} %get-tuple-element.31), channel_id=1, source_target_pairs={{0,9},{1,8},{2,11},{3,10},{4,13},{5,12},{6,15},{7,14},{8,1},{9,0},... | collective-permute-start | bytes 221192 | tf_op jit(solution)/shard_map/ppermute | solution.py:278
  36.1 23.1 %collective-permute-start.9 = (bf16[96,384]{1,0:T(8,128)(2,1)S(1)}, bf16[96,384]{1,0:T(8,128)(2,1)S(1)}, u32[]{:S(2)}, u32[]{:S(2)}) collective-permute-start(bf16[96,384]{1,0:T(8,128)(2,1)S(1)} %get-tuple-element.32), channel_id=1, source_target_pairs={{0,10},{1,11},{2,8},{3,9},{4,14},{5,15},{6,12},{7,13},{8,2},{9,3},... | collective-permute-start | bytes 221192 | tf_op jit(solution)/shard_map/ppermute | solution.py:278
  43.2 25.5 %collective-permute-start.10 = (bf16[96,384]{1,0:T(8,128)(2,1)}, bf16[96,384]{1,0:T(8,128)(2,1)S(1)}, u32[]{:S(2)}, u32[]{:S(2)}) collective-permute-start(bf16[96,384]{1,0:T(8,128)(2,1)} %get-tuple-element.33), channel_id=1, source_target_pairs={{0,11},{1,10},{2,9},{3,8},{4,15},{5,14},{6,13},{7,12},{8,3},{9,2},... | collective-permute-start | bytes 221192 | tf_op jit(solution)/shard_map/ppermute | solution.py:278
  44.0 24.7 %collective-permute-start.11 = (bf16[96,384]{1,0:T(8,128)(2,1)}, bf16[96,384]{1,0:T(8,128)(2,1)S(1)}, u32[]{:S(2)}, u32[]{:S(2)}) collective-permute-start(bf16[96,384]{1,0:T(8,128)(2,1)} %get-tuple-element.34), channel_id=1, source_target_pairs={{0,12},{1,13},{2,14},{3,15},{4,8},{5,9},{6,10},{7,11},{8,4},{9,5},... | collective-permute-start | bytes 221192 | tf_op jit(solution)/shard_map/ppermute | solution.py:278
  54.4 14.3 %collective-permute-start.12 = (bf16[96,384]{1,0:T(8,128)(2,1)}, bf16[96,384]{1,0:T(8,128)(2,1)S(1)}, u32[]{:S(2)}, u32[]{:S(2)}) collective-permute-start(bf16[96,384]{1,0:T(8,128)(2,1)} %get-tuple-element.35), channel_id=1, source_target_pairs={{0,13},{1,12},{2,15},{3,14},{4,9},{5,8},{6,11},{7,10},{8,5},{9,4},... | collective-permute-start | bytes 221192 | tf_op jit(solution)/shard_map/ppermute | solution.py:278
  56.4 12.4 %collective-permute-start.13 = (bf16[96,384]{1,0:T(8,128)(2,1)}, bf16[96,384]{1,0:T(8,128)(2,1)S(1)}, u32[]{:S(2)}, u32[]{:S(2)}) collective-permute-start(bf16[96,384]{1,0:T(8,128)(2,1)} %get-tuple-element.36), channel_id=1, source_target_pairs={{0,14},{1,15},{2,12},{3,13},{4,10},{5,11},{6,8},{7,9},{8,6},{9,7},... | collective-permute-start | bytes 221192 | tf_op jit(solution)/shard_map/ppermute | solution.py:278
  59.2 9.6 %collective-permute-start.14 = (bf16[96,384]{1,0:T(8,128)(2,1)}, bf16[96,384]{1,0:T(8,128)(2,1)S(1)}, u32[]{:S(2)}, u32[]{:S(2)}) collective-permute-start(bf16[96,384]{1,0:T(8,128)(2,1)} %get-tuple-element.37), channel_id=1, source_target_pairs={{0,15},{1,14},{2,13},{3,12},{4,11},{5,10},{6,9},{7,8},{8,7},{9,6},... | collective-permute-start | bytes 221192 | tf_op jit(solution)/shard_map/ppermute | solution.py:278
  70.5 21.1 %copy-start.2 = (bf16[12,384,128]{2,1,0:T(8,128)(2,1)S(1)}, bf16[12,384,128]{2,1,0:T(8,128)(2,1)}, u32[]{:S(2)}) copy-start(bf16[12,384,128]{2,1,0:T(8,128)(2,1)} %copy-done.1) | copy-start | bytes 3538948
  70.5 21.1 %copy-start.4 = (bf16[128,128]{1,0:T(8,128)(2,1)S(1)}, bf16[128,128]{1,0:T(8,128)(2,1)}, u32[]{:S(2)}) copy-start(bf16[128,128]{1,0:T(8,128)(2,1)} %w_ref.5) | copy-start | bytes 98308
  70.6 21.1 %copy-start.10 = (f32[128]{0:T(128)S(1)}, f32[128]{0:T(128)}, u32[]{:S(2)}) copy-start(f32[128]{0:T(128)} %param.18) | copy-start | bytes 1540
  70.6 21.1 %copy-start.11 = (f32[128]{0:T(128)S(1)}, f32[128]{0:T(128)}, u32[]{:S(2)}) copy-start(f32[128]{0:T(128)} %param.19) | copy-start | bytes 1540
  70.6 21.1 %copy-start.12 = (f32[128]{0:T(128)S(1)}, f32[128]{0:T(128)}, u32[]{:S(2)}) copy-start(f32[128]{0:T(128)} %param.21) | copy-start | bytes 1540

commit v19 on v16

--- a/solution.py
+++ b/solution.py
@@ -12,6 +12,7 @@
 CHANNELS = 128
 BLOCK = 8
 STEP = 4
+PAIRED = 2
 SIZE = 32
 LANES = 128
 GATHER = 32
@@ -64,21 +65,21 @@
     return sigmoid(both[:width]) * both[width:]
 
 
-def as_rows(values, k):
+def as_rows(values, k, step=STEP):
     hosts = values.shape[0] // BLOCK
     return jnp.concatenate(
-        [values[:, r * k : (r + 1) * k].reshape(hosts, BLOCK, k) for r in range(STEP)], axis=1
+        [values[:, r * k : (r + 1) * k].reshape(hosts, BLOCK, k) for r in range(step)], axis=1
     )
 
 
 def right_kernel(pair_ref, gain_ref, shift_ref, w_ref, b_ref, out_ref):
     k, width = pair_ref.shape[1:]
     half = w_ref.shape[1] // 2
-    x = pair_ref[...].astype(f32).reshape(STEP * k, width)
+    x = pair_ref[...].astype(f32).reshape(PAIRED * k, width)
     normed = normalize(x, gain_ref[...], shift_ref[...])
     both = dot(normed, w_ref[...]) + b_ref[...]
     values = sigmoid(both[:, :half]) * both[:, half:]
-    out = as_rows(values.T, k).astype(bf16)
+    out = as_rows(values.T, k, PAIRED).astype(bf16)
     for p in range(out_ref.shape[0]):
         out_ref[p] = out
 
@@ -214,15 +215,15 @@
     anywhere = pl.BlockSpec(memory_space=pl.ANY)
     right = pl.pallas_call(
         right_kernel,
-        grid=(steps,),
+        grid=(rows // PAIRED,),
         in_specs=[
-            row_block,
+            pl.BlockSpec((PAIRED, k, width), lambda s: (s, 0, 0)),
             whole((1, width)),
             whole((1, width)),
             pl.BlockSpec((width, 2 * hidden), lambda s: (0, 1)),
             pl.BlockSpec((1, 2 * hidden), lambda s: (0, 1)),
         ],
-        out_specs=pl.BlockSpec((parts, hosts, STEP * BLOCK, k), lambda s: (0, 0, s, 0)),
+        out_specs=pl.BlockSpec((parts, hosts, PAIRED * BLOCK, k), lambda s: (0, 0, s, 0)),
         out_shape=bfloat(parts, hosts, tall, k),
         compiler_params=params(60),
         cost_estimate=cost(4 * work * hidden, 6 * work),

time: 93.3 us -> 94.7 us (1.015)
  Pallas kernels: 13.5 us -> 14.8 us
    pallas_call x1, Pallas kernels: 4.91 us -> 6.26 us  [shards(): pl.pallas_call(right_kernel, grid=(rows // PAIRED,), in_specs=[pl.BlockSp...]
where the time goes in v19:
time: 94.7 us; the launch traced here: 94.3 us
  waiting for transfers between devices  29.1 us (31%)
  starting transfers between devices  26.4 us (28%)
  blocking collectives  21.1 us (22%)
  Pallas kernels  14.8 us (16%)
  local copies, waits for them, and re-layouts  2.72 us (3%)
    ppermute x15, waiting for transfers between devices, send(): return lax.ppermute(values, everywhere, pairs)  22.2 us
    all_to_all x1, blocking collectives, shards(): product = lax.all_to_all(product, in_part, 0, 0, tiled=True)  21.1 us
    ppermute x15, starting transfers between devices, send(): return lax.ppermute(values, everywhere, pairs)  19.1 us
    all_to_all x1, starting transfers between devices, shards(): lax.all_to_all(right.reshape(devices, tall, k), everywhere, 0, 0, tiled=T...  7.3 us
    all_to_all x1, waiting for transfers between devices, shards(): lax.all_to_all(right.reshape(devices, tall, k), everywhere, 0, 0, tiled=T...  6.89 us
    pallas_call x1, Pallas kernels, shards(): pl.pallas_call(right_kernel, grid=(rows // PAIRED,), in_specs=[pl.BlockSp...  6.26 us
    pallas_call x1, Pallas kernels, shards(): pl.pallas_call(left_kernel, grid=(steps,), in_specs=[row_block, whole((1,...  3.39 us
    unnamed x26, local copies, waits for them, and re-layouts  2.72 us
  transfers between devices with their start and end apart: 16, of which 6 were waited for; matrix products, arithmetic and copies ran while one was open for 0% of the time, Pallas kernels for 5%

profile of v19, /device:TPU:0, one launch (start us, length us, event | category | flops | bytes accessed | tf_op | source)
XLA Modules:
  0.0 94.3 jit_solution(4854161233553252756)
XLA Ops:
  0.0 6.3 %right_factor.1 = bf16[2,16,96,384]{3,2,1,0:T(8,128)(2,1)} custom-call(bf16[12,384,128]{2,1,0:T(8,128)(2,1)} %pair_ref.3, f32[1,128]{1,0:T(1,128)} %bitcast.12, f32[1,128]{1,0:T(1,128)} %bitcast.14, bf16[128,512]{1,0:T(8,128)(2,1)} %w_ref.4, f32[1,512]{1,0:T(1,128)} %bitcast.10), custom_call_target="tpu_custom_call" | custom-call | flops 301989888 | bytes 3538944 | tf_op jit(solution)/shard_map/right_factor/pallas_call | solution.py:216
  6.3 0.0 copy-start.8
  6.3 0.0 copy-start.9
  6.3 7.3 %all-to-all-start = ((bf16[32,96,384]{2,1,0:T(8,128)(2,1)}), bf16[32,96,384]{2,1,0:T(8,128)(2,1)S(1)}, u32[]{:S(2)}, u32[]{:S(2)}) async-start(bf16[32,96,384]{2,1,0:T(8,128)(2,1)} %bitcast.20), calls=%async_computation | async-start | bytes 4718592 | tf_op jit(solution)/shard_map/all_to_all | solution.py:232
  13.7 0.0 copy-start.3
  13.7 0.9 copy-done.3
  14.6 0.8 copy-done.5
  15.3 3.4 %left_factor.1 = (bf16[96,384]{1,0:T(8,128)(2,1)S(1)}, bf16[96,384]{1,0:T(8,128)(2,1)S(1)}, bf16[96,384]{1,0:T(8,128)(2,1)S(1)}, bf16[96,384]{1,0:T(8,128)(2,1)S...) custom-call(bf16[12,384,128]{2,1,0:T(8,128)(2,1)S(1)} %copy-done, ...), custom_call_target="tpu_custom_call" | custom-call | flops 301989888 | bytes 3538944 | tf_op jit(solution)/shard_map/left_factor/pallas_call | solution.py:238
  18.7 1.0 %copy-done.1 = bf16[12,384,128]{2,1,0:T(8,128)(2,1)} copy-done((bf16[12,384,128]{2,1,0:T(8,128)(2,1)}, bf16[12,384,128]{2,1,0:T(8,128)(2,1)S(1)}, u32[]{:S(2)}) %copy-start.1) | copy-done | bytes 1179672
  19.7 0.3 collective-permute-start
  20.0 1.7 %collective-permute-start.1 = (bf16[96,384]{1,0:T(8,128)(2,1)S(1)}, bf16[96,384]{1,0:T(8,128)(2,1)S(1)}, u32[]{:S(2)}, u32[]{:S(2)}) collective-permute-start(bf16[96,384]{1,0:T(8,128)(2,1)S(1)} %get-tuple-element.24), channel_id=1, source_target_pairs={{0,2},{1,3},{2,0},{3,1},{4,6},{5,7},{6,4},{7,5},{8,10},{9,11},{10,... | collective-permute-start | bytes 221192 | tf_op jit(solution)/shard_map/ppermute | solution.py:236
  21.7 0.0 collective-permute-start.2
  21.7 1.7 %collective-permute-start.3 = (bf16[96,384]{1,0:T(8,128)(2,1)S(1)}, bf16[96,384]{1,0:T(8,128)(2,1)S(1)}, u32[]{:S(2)}, u32[]{:S(2)}) collective-permute-start(bf16[96,384]{1,0:T(8,128)(2,1)S(1)} %get-tuple-element.26), channel_id=1, source_target_pairs={{0,4},{1,5},{2,6},{3,7},{4,0},{5,1},{6,2},{7,3},{8,12},{9,13},{10,... | collective-permute-start | bytes 221192 | tf_op jit(solution)/shard_map/ppermute | solution.py:236
  23.4 0.1 collective-permute-start.4
  23.5 0.0 collective-permute-done.refs_1_
  23.5 2.6 %collective-permute-start.5 = (bf16[96,384]{1,0:T(8,128)(2,1)S(1)}, bf16[96,384]{1,0:T(8,128)(2,1)S(1)}, u32[]{:S(2)}, u32[]{:S(2)}) collective-permute-start(bf16[96,384]{1,0:T(8,128)(2,1)S(1)} %get-tuple-element.28), channel_id=1, source_target_pairs={{0,6},{1,7},{2,4},{3,5},{4,2},{5,3},{6,0},{7,1},{8,14},{9,15},{10,... | collective-permute-start | bytes 221192 | tf_op jit(solution)/shard_map/ppermute | solution.py:236
  26.1 7.1 %collective-permute-done.1.refs_2_ = bf16[96,384]{1,0:T(8,128)(2,1)S(1)} collective-permute-done((bf16[96,384]{1,0:T(8,128)(2,1)S(1)}, bf16[96,384]{1,0:T(8,128)(2,1)S(1)}, u32[]{:S(2)}, u32[]{:S(2)}) %collective-permute-start.1) | collective-permute-done | bytes 73760 | tf_op jit(solution)/shard_map/ppermute | solution.py:236
  33.2 0.6 collective-permute-start.6
  33.8 0.2 collective-permute-done.2.refs_3_
  34.0 0.3 collective-permute-start.7
  34.3 0.0 collective-permute-done.3.refs_4_
  34.3 2.3 %collective-permute-start.8 = (bf16[96,384]{1,0:T(8,128)(2,1)S(1)}, bf16[96,384]{1,0:T(8,128)(2,1)S(1)}, u32[]{:S(2)}, u32[]{:S(2)}) collective-permute-start(bf16[96,384]{1,0:T(8,128)(2,1)S(1)} %get-tuple-element.31), channel_id=1, source_target_pairs={{0,9},{1,8},{2,11},{3,10},{4,13},{5,12},{6,15},{7,14},{8,1},{9,0},... | collective-permute-start | bytes 221192 | tf_op jit(solution)/shard_map/ppermute | solution.py:236
  36.5 0.0 collective-permute-done.4.refs_5_
  36.5 3.2 %collective-permute-start.9 = (bf16[96,384]{1,0:T(8,128)(2,1)S(1)}, bf16[96,384]{1,0:T(8,128)(2,1)S(1)}, u32[]{:S(2)}, u32[]{:S(2)}) collective-permute-start(bf16[96,384]{1,0:T(8,128)(2,1)S(1)} %get-tuple-element.32), channel_id=1, source_target_pairs={{0,10},{1,11},{2,8},{3,9},{4,14},{5,15},{6,12},{7,13},{8,2},{9,3},... | collective-permute-start | bytes 221192 | tf_op jit(solution)/shard_map/ppermute | solution.py:236
  39.7 3.9 %collective-permute-done.5.refs_6_ = bf16[96,384]{1,0:T(8,128)(2,1)S(1)} collective-permute-done((bf16[96,384]{1,0:T(8,128)(2,1)S(1)}, bf16[96,384]{1,0:T(8,128)(2,1)S(1)}, u32[]{:S(2)}, u32[]{:S(2)}) %collective-permute-start.5) | collective-permute-done | bytes 73760 | tf_op jit(solution)/shard_map/ppermute | solution.py:236
  43.6 0.0 collective-permute-start.10
  43.7 0.8 collective-permute-done.6.refs_7_
  44.4 0.0 collective-permute-start.11
  44.5 0.4 regroup_left.1.near
  44.8 10.1 %collective-permute-done.7.refs_0_ = bf16[96,384]{1,0:T(8,128)(2,1)S(1)} collective-permute-done((bf16[96,384]{1,0:T(8,128)(2,1)S(1)}, bf16[96,384]{1,0:T(8,128)(2,1)S(1)}, u32[]{:S(2)}, u32[]{:S(2)}) %collective-permute-start.7) | collective-permute-done | bytes 73760 | tf_op jit(solution)/shard_map/ppermute | solution.py:236
  54.9 1.9 %collective-permute-start.12 = (bf16[96,384]{1,0:T(8,128)(2,1)}, bf16[96,384]{1,0:T(8,128)(2,1)S(1)}, u32[]{:S(2)}, u32[]{:S(2)}) collective-permute-start(bf16[96,384]{1,0:T(8,128)(2,1)} %get-tuple-element.35), channel_id=1, source_target_pairs={{0,13},{1,12},{2,15},{3,14},{4,9},{5,8},{6,11},{7,10},{8,5},{9,4},... | collective-permute-start | bytes 221192 | tf_op jit(solution)/shard_map/ppermute | solution.py:236
  56.8 0.0 collective-permute-done.8.refs_1_
  56.8 2.8 %collective-permute-start.13 = (bf16[96,384]{1,0:T(8,128)(2,1)}, bf16[96,384]{1,0:T(8,128)(2,1)S(1)}, u32[]{:S(2)}, u32[]{:S(2)}) collective-permute-start(bf16[96,384]{1,0:T(8,128)(2,1)} %get-tuple-element.36), channel_id=1, source_target_pairs={{0,14},{1,15},{2,12},{3,13},{4,10},{5,11},{6,8},{7,9},{8,6},{9,7},... | collective-permute-start | bytes 221192 | tf_op jit(solution)/shard_map/ppermute | solution.py:236
  59.6 0.0 collective-permute-done.9.refs_2_
  59.6 1.7 %collective-permute-start.14 = (bf16[96,384]{1,0:T(8,128)(2,1)}, bf16[96,384]{1,0:T(8,128)(2,1)S(1)}, u32[]{:S(2)}, u32[]{:S(2)}) collective-permute-start(bf16[96,384]{1,0:T(8,128)(2,1)} %get-tuple-element.37), channel_id=1, source_target_pairs={{0,15},{1,14},{2,13},{3,12},{4,11},{5,10},{6,9},{7,8},{8,7},{9,6},... | collective-permute-start | bytes 221192 | tf_op jit(solution)/shard_map/ppermute | solution.py:236
  61.3 6.9 %all-to-all-done = bf16[32,96,384]{2,1,0:T(8,128)(2,1)S(1)} async-done(((bf16[32,96,384]{2,1,0:T(8,128)(2,1)}), bf16[32,96,384]{2,1,0:T(8,128)(2,1)S(1)}, u32[]{:S(2)}, u32[]{:S(2)}) %all-to-all-start) | async-done | bytes 2359328 | tf_op jit(solution)/shard_map/all_to_all | solution.py:232
  68.2 1.0 %regroup_right.1.right = bf16[8,384,384]{2,1,0:T(8,128)(2,1)S(1)} custom-call(bf16[3072,384]{1,0:T(8,128)(2,1)S(1)} %bitcast.9), custom_call_target="tpu_custom_call" | custom-call | flops 137438953472 | bytes 4718592 | tf_op jit(solution)/shard_map/regroup_right/pallas_call | solution.py:302
  69.2 0.0 collective-permute-done.10.refs_3_
  69.2 0.0 collective-permute-done.12.refs_5_
  69.2 0.0 collective-permute-done.13.refs_6_
  69.2 1.8 %products.1 = bf16[16,96,384]{2,1,0:T(8,128)(2,1)S(1)} custom-call(bf16[8,384,384]{2,1,0:T(8,128)(2,1)S(1)} %regroup_right.1.right, bf16[8,96,384]{2,1,0:T(8,128)(2,1)S(1)} %regroup_left.1.near, bf16[96,384]{1,0:T(8,128)(2,1)S(1)} %collective-permute-done.7.refs_0_, bf16[96,384]{1,0:T(8,128)(2,1)S(1)} %collective-permute-done.8.refs_1_, ...), custom_call_target="tpu_custom_call" | custom-call | flops 226492416 | bytes 3538944 | tf_op jit(solution)/shard_map/products/pallas_call | solution.py:310
  71.0 0.0 copy-start.2
  71.0 0.0 copy-start.4
  71.0 0.0 copy-start.10
  71.0 0.0 copy-start.11
  71.1 0.0 copy-start.12
  71.1 21.1 %all_to_all.10.x_ref = bf16[16,96,384]{2,1,0:T(8,128)(2,1)S(1)} all-to-all(bf16[16,96,384]{2,1,0:T(8,128)(2,1)S(1)} %products.1), channel_id=1, replica_groups=mesh['groups'=1,'part'=2,'chan'=8,'quarter'=2] {'chan','quarter'}, dimensions={0} | all-to-all | bytes 2359296 | tf_op jit(solution)/shard_map/all_to_all | solution.py:322
  92.2 2.1 %update.1 = bf16[12,384,128]{2,1,0:T(8,128)(2,1)} custom-call(bf16[16,96,384]{2,1,0:T(8,128)(2,1)S(1)} %all_to_all.10.x_ref, bf16[12,384,128]{2,1,0:T(8,128)(2,1)S(1)} %copy-done.2, f32[1,128]{1,0:T(1,128)S(1)} %bitcast.17, f32[1,128]{1,0:T(1,128)S(1)} %bitcast.18, bf16[128,128]{1,0:T(8,128)(2,1)S(1)} %copy-done.4, f32[1,128]{1,0:T(1,128)S(1)} %bitcast.19), custom_call_target="tpu_custom_call" | custom-call | flops 150994944 | bytes 3538944 | tf_op jit(solution)/shard_map/update/pallas_call | solution.py:324
  (17 shorter events, 0.0 us)
Async XLA Ops:
  6.3 7.3 %copy-start = (bf16[12,384,128]{2,1,0:T(8,128)(2,1)S(1)}, bf16[12,384,128]{2,1,0:T(8,128)(2,1)}, u32[]{:S(2)}) copy-start(bf16[12,384,128]{2,1,0:T(8,128)(2,1)} %pair_ref.3) | copy-start | bytes 3538948
  6.3 7.4 %copy-start.6 = (f32[512]{0:T(512)S(1)}, f32[512]{0:T(512)}, u32[]{:S(2)}) copy-start(f32[512]{0:T(512)} %param.15) | copy-start | bytes 6148
  6.3 7.4 %copy-start.7 = (f32[128]{0:T(128)S(1)}, f32[128]{0:T(128)}, u32[]{:S(2)}) copy-start(f32[128]{0:T(128)} %param.12) | copy-start | bytes 1540
  6.3 7.4 %copy-start.8 = (f32[128]{0:T(128)S(1)}, f32[128]{0:T(128)}, u32[]{:S(2)}) copy-start(f32[128]{0:T(128)} %param.13) | copy-start | bytes 1540
  6.3 7.4 %copy-start.9 = (f32[128]{0:T(128)S(1)}, f32[128]{0:T(128)}, u32[]{:S(2)}) copy-start(f32[128]{0:T(128)} %param.17) | copy-start | bytes 1540
  6.3 61.9 %all-to-all-start = ((bf16[32,96,384]{2,1,0:T(8,128)(2,1)}), bf16[32,96,384]{2,1,0:T(8,128)(2,1)S(1)}, u32[]{:S(2)}, u32[]{:S(2)}) async-start(bf16[32,96,384]{2,1,0:T(8,128)(2,1)} %bitcast.20), calls=%async_computation | async-start | bytes 4718592 | tf_op jit(solution)/shard_map/all_to_all | solution.py:232
  13.7 0.9 copy-start.3
  14.6 0.8 copy-start.5
  18.7 1.0 %copy-start.1 = (bf16[12,384,128]{2,1,0:T(8,128)(2,1)}, bf16[12,384,128]{2,1,0:T(8,128)(2,1)S(1)}, u32[]{:S(2)}) copy-start(bf16[12,384,128]{2,1,0:T(8,128)(2,1)S(1)} %get-tuple-element.38.gate_ref) | copy-start | bytes 3538948
  19.7 3.7 %collective-permute-start = (bf16[96,384]{1,0:T(8,128)(2,1)S(1)}, bf16[96,384]{1,0:T(8,128)(2,1)S(1)}, u32[]{:S(2)}, u32[]{:S(2)}) collective-permute-start(bf16[96,384]{1,0:T(8,128)(2,1)S(1)} %get-tuple-element.23), channel_id=1, source_target_pairs={{0,1},{1,0},{2,3},{3,2},{4,5},{5,4},{6,7},{7,6},{8,9},{9,8},{10,11... | collective-permute-start | bytes 221192 | tf_op jit(solution)/shard_map/ppermute | solution.py:236
  20.0 13.2 %collective-permute-start.1 = (bf16[96,384]{1,0:T(8,128)(2,1)S(1)}, bf16[96,384]{1,0:T(8,128)(2,1)S(1)}, u32[]{:S(2)}, u32[]{:S(2)}) collective-permute-start(bf16[96,384]{1,0:T(8,128)(2,1)S(1)} %get-tuple-element.24), channel_id=1, source_target_pairs={{0,2},{1,3},{2,0},{3,1},{4,6},{5,7},{6,4},{7,5},{8,10},{9,11},{10,... | collective-permute-start | bytes 221192 | tf_op jit(solution)/shard_map/ppermute | solution.py:236
  21.7 12.3 %collective-permute-start.2 = (bf16[96,384]{1,0:T(8,128)(2,1)S(1)}, bf16[96,384]{1,0:T(8,128)(2,1)S(1)}, u32[]{:S(2)}, u32[]{:S(2)}) collective-permute-start(bf16[96,384]{1,0:T(8,128)(2,1)S(1)} %get-tuple-element.25), channel_id=1, source_target_pairs={{0,3},{1,2},{2,1},{3,0},{4,7},{5,6},{6,5},{7,4},{8,11},{9,10},{10,... | collective-permute-start | bytes 221192 | tf_op jit(solution)/shard_map/ppermute | solution.py:236
  21.7 12.6 %collective-permute-start.3 = (bf16[96,384]{1,0:T(8,128)(2,1)S(1)}, bf16[96,384]{1,0:T(8,128)(2,1)S(1)}, u32[]{:S(2)}, u32[]{:S(2)}) collective-permute-start(bf16[96,384]{1,0:T(8,128)(2,1)S(1)} %get-tuple-element.26), channel_id=1, source_target_pairs={{0,4},{1,5},{2,6},{3,7},{4,0},{5,1},{6,2},{7,3},{8,12},{9,13},{10,... | collective-permute-start | bytes 221192 | tf_op jit(solution)/shard_map/ppermute | solution.py:236
  23.4 13.2 %collective-permute-start.4 = (bf16[96,384]{1,0:T(8,128)(2,1)S(1)}, bf16[96,384]{1,0:T(8,128)(2,1)S(1)}, u32[]{:S(2)}, u32[]{:S(2)}) collective-permute-start(bf16[96,384]{1,0:T(8,128)(2,1)S(1)} %get-tuple-element.27), channel_id=1, source_target_pairs={{0,5},{1,4},{2,7},{3,6},{4,1},{5,0},{6,3},{7,2},{8,13},{9,12},{10,... | collective-permute-start | bytes 221192 | tf_op jit(solution)/shard_map/ppermute | solution.py:236
  23.5 20.2 %collective-permute-start.5 = (bf16[96,384]{1,0:T(8,128)(2,1)S(1)}, bf16[96,384]{1,0:T(8,128)(2,1)S(1)}, u32[]{:S(2)}, u32[]{:S(2)}) collective-permute-start(bf16[96,384]{1,0:T(8,128)(2,1)S(1)} %get-tuple-element.28), channel_id=1, source_target_pairs={{0,6},{1,7},{2,4},{3,5},{4,2},{5,3},{6,0},{7,1},{8,14},{9,15},{10,... | collective-permute-start | bytes 221192 | tf_op jit(solution)/shard_map/ppermute | solution.py:236
  33.2 11.3 %collective-permute-start.6 = (bf16[96,384]{1,0:T(8,128)(2,1)S(1)}, bf16[96,384]{1,0:T(8,128)(2,1)S(1)}, u32[]{:S(2)}, u32[]{:S(2)}) collective-permute-start(bf16[96,384]{1,0:T(8,128)(2,1)S(1)} %get-tuple-element.29), channel_id=1, source_target_pairs={{0,7},{1,6},{2,5},{3,4},{4,3},{5,2},{6,1},{7,0},{8,15},{9,14},{10,... | collective-permute-start | bytes 221192 | tf_op jit(solution)/shard_map/ppermute | solution.py:236
  34.0 20.9 %collective-permute-start.7 = (bf16[96,384]{1,0:T(8,128)(2,1)S(1)}, bf16[96,384]{1,0:T(8,128)(2,1)S(1)}, u32[]{:S(2)}, u32[]{:S(2)}) collective-permute-start(bf16[96,384]{1,0:T(8,128)(2,1)S(1)} %get-tuple-element.30), channel_id=1, source_target_pairs={{0,8},{1,9},{2,10},{3,11},{4,12},{5,13},{6,14},{7,15},{8,0},{9,1},... | collective-permute-start | bytes 221192 | tf_op jit(solution)/shard_map/ppermute | solution.py:236
  34.3 22.6 %collective-permute-start.8 = (bf16[96,384]{1,0:T(8,128)(2,1)S(1)}, bf16[96,384]{1,0:T(8,128)(2,1)S(1)}, u32[]{:S(2)}, u32[]{:S(2)}) collective-permute-start(bf16[96,384]{1,0:T(8,128)(2,1)S(1)} %get-tuple-element.31), channel_id=1, source_target_pairs={{0,9},{1,8},{2,11},{3,10},{4,13},{5,12},{6,15},{7,14},{8,1},{9,0},... | collective-permute-start | bytes 221192 | tf_op jit(solution)/shard_map/ppermute | solution.py:236
  36.5 23.1 %collective-permute-start.9 = (bf16[96,384]{1,0:T(8,128)(2,1)S(1)}, bf16[96,384]{1,0:T(8,128)(2,1)S(1)}, u32[]{:S(2)}, u32[]{:S(2)}) collective-permute-start(bf16[96,384]{1,0:T(8,128)(2,1)S(1)} %get-tuple-element.32), channel_id=1, source_target_pairs={{0,10},{1,11},{2,8},{3,9},{4,14},{5,15},{6,12},{7,13},{8,2},{9,3},... | collective-permute-start | bytes 221192 | tf_op jit(solution)/shard_map/ppermute | solution.py:236
  43.6 25.5 %collective-permute-start.10 = (bf16[96,384]{1,0:T(8,128)(2,1)}, bf16[96,384]{1,0:T(8,128)(2,1)S(1)}, u32[]{:S(2)}, u32[]{:S(2)}) collective-permute-start(bf16[96,384]{1,0:T(8,128)(2,1)} %get-tuple-element.33), channel_id=1, source_target_pairs={{0,11},{1,10},{2,9},{3,8},{4,15},{5,14},{6,13},{7,12},{8,3},{9,2},... | collective-permute-start | bytes 221192 | tf_op jit(solution)/shard_map/ppermute | solution.py:236
  44.4 24.8 %collective-permute-start.11 = (bf16[96,384]{1,0:T(8,128)(2,1)}, bf16[96,384]{1,0:T(8,128)(2,1)S(1)}, u32[]{:S(2)}, u32[]{:S(2)}) collective-permute-start(bf16[96,384]{1,0:T(8,128)(2,1)} %get-tuple-element.34), channel_id=1, source_target_pairs={{0,12},{1,13},{2,14},{3,15},{4,8},{5,9},{6,10},{7,11},{8,4},{9,5},... | collective-permute-start | bytes 221192 | tf_op jit(solution)/shard_map/ppermute | solution.py:236
  54.9 14.3 %collective-permute-start.12 = (bf16[96,384]{1,0:T(8,128)(2,1)}, bf16[96,384]{1,0:T(8,128)(2,1)S(1)}, u32[]{:S(2)}, u32[]{:S(2)}) collective-permute-start(bf16[96,384]{1,0:T(8,128)(2,1)} %get-tuple-element.35), channel_id=1, source_target_pairs={{0,13},{1,12},{2,15},{3,14},{4,9},{5,8},{6,11},{7,10},{8,5},{9,4},... | collective-permute-start | bytes 221192 | tf_op jit(solution)/shard_map/ppermute | solution.py:236
  56.8 12.4 %collective-permute-start.13 = (bf16[96,384]{1,0:T(8,128)(2,1)}, bf16[96,384]{1,0:T(8,128)(2,1)S(1)}, u32[]{:S(2)}, u32[]{:S(2)}) collective-permute-start(bf16[96,384]{1,0:T(8,128)(2,1)} %get-tuple-element.36), channel_id=1, source_target_pairs={{0,14},{1,15},{2,12},{3,13},{4,10},{5,11},{6,8},{7,9},{8,6},{9,7},... | collective-permute-start | bytes 221192 | tf_op jit(solution)/shard_map/ppermute | solution.py:236
  59.6 9.6 %collective-permute-start.14 = (bf16[96,384]{1,0:T(8,128)(2,1)}, bf16[96,384]{1,0:T(8,128)(2,1)S(1)}, u32[]{:S(2)}, u32[]{:S(2)}) collective-permute-start(bf16[96,384]{1,0:T(8,128)(2,1)} %get-tuple-element.37), channel_id=1, source_target_pairs={{0,15},{1,14},{2,13},{3,12},{4,11},{5,10},{6,9},{7,8},{8,7},{9,6},... | collective-permute-start | bytes 221192 | tf_op jit(solution)/shard_map/ppermute | solution.py:236
  71.0 21.1 %copy-start.2 = (bf16[12,384,128]{2,1,0:T(8,128)(2,1)S(1)}, bf16[12,384,128]{2,1,0:T(8,128)(2,1)}, u32[]{:S(2)}) copy-start(bf16[12,384,128]{2,1,0:T(8,128)(2,1)} %copy-done.1) | copy-start | bytes 3538948
  71.0 21.1 %copy-start.4 = (bf16[128,128]{1,0:T(8,128)(2,1)S(1)}, bf16[128,128]{1,0:T(8,128)(2,1)}, u32[]{:S(2)}) copy-start(bf16[128,128]{1,0:T(8,128)(2,1)} %w_ref.5) | copy-start | bytes 98308
  71.0 21.1 %copy-start.10 = (f32[128]{0:T(128)S(1)}, f32[128]{0:T(128)}, u32[]{:S(2)}) copy-start(f32[128]{0:T(128)} %param.18) | copy-start | bytes 1540
  71.0 21.1 %copy-start.11 = (f32[128]{0:T(128)S(1)}, f32[128]{0:T(128)}, u32[]{:S(2)}) copy-start(f32[128]{0:T(128)} %param.19) | copy-start | bytes 1540
  71.1 21.1 %copy-start.12 = (f32[128]{0:T(128)S(1)}, f32[128]{0:T(128)}, u32[]{:S(2)}) copy-start(f32[128]{0:T(128)} %param.21) | copy-start | bytes 1540

commit v20 on v19

--- a/solution.py
+++ b/solution.py
@@ -12,7 +12,7 @@
 CHANNELS = 128
 BLOCK = 8
 STEP = 4
-PAIRED = 2
+PAIRED = 6
 SIZE = 32
 LANES = 128
 GATHER = 32

time: 94.7 us -> 92.8 us (0.980)
  Pallas kernels: 14.8 us -> 13 us
    pallas_call x1, Pallas kernels: 6.26 us -> 4.45 us  [shards(): pl.pallas_call(right_kernel, grid=(rows // PAIRED,), in_specs=[pl.BlockSp...]
where the time goes in v20:
time: 92.8 us; the launch traced here: 92.5 us
  waiting for transfers between devices  29.1 us (31%)
  starting transfers between devices  26.4 us (28%)
  blocking collectives  21.1 us (23%)
  Pallas kernels  13 us (14%)
  local copies, waits for them, and re-layouts  2.72 us (3%)
    ppermute x15, waiting for transfers between devices, send(): return lax.ppermute(values, everywhere, pairs)  22.2 us
    all_to_all x1, blocking collectives, shards(): product = lax.all_to_all(product, in_part, 0, 0, tiled=True)  21.1 us
    ppermute x15, starting transfers between devices, send(): return lax.ppermute(values, everywhere, pairs)  19 us
    all_to_all x1, starting transfers between devices, shards(): lax.all_to_all(right.reshape(devices, tall, k), everywhere, 0, 0, tiled=T...  7.3 us
    all_to_all x1, waiting for transfers between devices, shards(): lax.all_to_all(right.reshape(devices, tall, k), everywhere, 0, 0, tiled=T...  6.88 us
    pallas_call x1, Pallas kernels, shards(): pl.pallas_call(right_kernel, grid=(rows // PAIRED,), in_specs=[pl.BlockSp...  4.45 us
    pallas_call x1, Pallas kernels, shards(): pl.pallas_call(left_kernel, grid=(steps,), in_specs=[row_block, whole((1,...  3.39 us
    unnamed x26, local copies, waits for them, and re-layouts  2.72 us
  transfers between devices with their start and end apart: 16, of which 6 were waited for; matrix products, arithmetic and copies ran while one was open for 0% of the time, Pallas kernels for 5%

profile of v20, /device:TPU:0, one launch (start us, length us, event | category | flops | bytes accessed | tf_op | source)
XLA Modules:
  0.0 92.5 jit_solution(9892772378129723834)
XLA Ops:
  0.0 4.5 %right_factor.1 = bf16[2,16,96,384]{3,2,1,0:T(8,128)(2,1)} custom-call(bf16[12,384,128]{2,1,0:T(8,128)(2,1)} %pair_ref.3, f32[1,128]{1,0:T(1,128)} %bitcast.12, f32[1,128]{1,0:T(1,128)} %bitcast.14, bf16[128,512]{1,0:T(8,128)(2,1)} %w_ref.4, f32[1,512]{1,0:T(1,128)} %bitcast.10), custom_call_target="tpu_custom_call" | custom-call | flops 301989888 | bytes 3538944 | tf_op jit(solution)/shard_map/right_factor/pallas_call | solution.py:216
  4.5 0.0 copy-start.8
  4.5 0.0 copy-start.9
  4.5 7.3 %all-to-all-start = ((bf16[32,96,384]{2,1,0:T(8,128)(2,1)}), bf16[32,96,384]{2,1,0:T(8,128)(2,1)S(1)}, u32[]{:S(2)}, u32[]{:S(2)}) async-start(bf16[32,96,384]{2,1,0:T(8,128)(2,1)} %bitcast.20), calls=%async_computation | async-start | bytes 4718592 | tf_op jit(solution)/shard_map/all_to_all | solution.py:232
  11.9 0.0 copy-start.3
  11.9 0.9 copy-done.3
  12.8 0.8 copy-done.5
  13.5 3.4 %left_factor.1 = (bf16[96,384]{1,0:T(8,128)(2,1)S(1)}, bf16[96,384]{1,0:T(8,128)(2,1)S(1)}, bf16[96,384]{1,0:T(8,128)(2,1)S(1)}, bf16[96,384]{1,0:T(8,128)(2,1)S...) custom-call(bf16[12,384,128]{2,1,0:T(8,128)(2,1)S(1)} %copy-done, ...), custom_call_target="tpu_custom_call" | custom-call | flops 301989888 | bytes 3538944 | tf_op jit(solution)/shard_map/left_factor/pallas_call | solution.py:238
  16.9 1.0 %copy-done.1 = bf16[12,384,128]{2,1,0:T(8,128)(2,1)} copy-done((bf16[12,384,128]{2,1,0:T(8,128)(2,1)}, bf16[12,384,128]{2,1,0:T(8,128)(2,1)S(1)}, u32[]{:S(2)}) %copy-start.1) | copy-done | bytes 1179672
  17.9 0.2 collective-permute-start
  18.2 1.7 %collective-permute-start.1 = (bf16[96,384]{1,0:T(8,128)(2,1)S(1)}, bf16[96,384]{1,0:T(8,128)(2,1)S(1)}, u32[]{:S(2)}, u32[]{:S(2)}) collective-permute-start(bf16[96,384]{1,0:T(8,128)(2,1)S(1)} %get-tuple-element.24), channel_id=1, source_target_pairs={{0,2},{1,3},{2,0},{3,1},{4,6},{5,7},{6,4},{7,5},{8,10},{9,11},{10,... | collective-permute-start | bytes 221192 | tf_op jit(solution)/shard_map/ppermute | solution.py:236
  19.9 0.0 collective-permute-start.2
  19.9 1.7 %collective-permute-start.3 = (bf16[96,384]{1,0:T(8,128)(2,1)S(1)}, bf16[96,384]{1,0:T(8,128)(2,1)S(1)}, u32[]{:S(2)}, u32[]{:S(2)}) collective-permute-start(bf16[96,384]{1,0:T(8,128)(2,1)S(1)} %get-tuple-element.26), channel_id=1, source_target_pairs={{0,4},{1,5},{2,6},{3,7},{4,0},{5,1},{6,2},{7,3},{8,12},{9,13},{10,... | collective-permute-start | bytes 221192 | tf_op jit(solution)/shard_map/ppermute | solution.py:236
  21.6 0.1 collective-permute-start.4
  21.7 0.0 collective-permute-done.refs_1_
  21.7 2.6 %collective-permute-start.5 = (bf16[96,384]{1,0:T(8,128)(2,1)S(1)}, bf16[96,384]{1,0:T(8,128)(2,1)S(1)}, u32[]{:S(2)}, u32[]{:S(2)}) collective-permute-start(bf16[96,384]{1,0:T(8,128)(2,1)S(1)} %get-tuple-element.28), channel_id=1, source_target_pairs={{0,6},{1,7},{2,4},{3,5},{4,2},{5,3},{6,0},{7,1},{8,14},{9,15},{10,... | collective-permute-start | bytes 221192 | tf_op jit(solution)/shard_map/ppermute | solution.py:236
  24.3 7.1 %collective-permute-done.1.refs_2_ = bf16[96,384]{1,0:T(8,128)(2,1)S(1)} collective-permute-done((bf16[96,384]{1,0:T(8,128)(2,1)S(1)}, bf16[96,384]{1,0:T(8,128)(2,1)S(1)}, u32[]{:S(2)}, u32[]{:S(2)}) %collective-permute-start.1) | collective-permute-done | bytes 73760 | tf_op jit(solution)/shard_map/ppermute | solution.py:236
  31.4 0.6 collective-permute-start.6
  32.0 0.2 collective-permute-done.2.refs_3_
  32.2 0.3 collective-permute-start.7
  32.4 0.0 collective-permute-done.3.refs_4_
  32.5 2.3 %collective-permute-start.8 = (bf16[96,384]{1,0:T(8,128)(2,1)S(1)}, bf16[96,384]{1,0:T(8,128)(2,1)S(1)}, u32[]{:S(2)}, u32[]{:S(2)}) collective-permute-start(bf16[96,384]{1,0:T(8,128)(2,1)S(1)} %get-tuple-element.31), channel_id=1, source_target_pairs={{0,9},{1,8},{2,11},{3,10},{4,13},{5,12},{6,15},{7,14},{8,1},{9,0},... | collective-permute-start | bytes 221192 | tf_op jit(solution)/shard_map/ppermute | solution.py:236
  34.7 0.0 collective-permute-done.4.refs_5_
  34.7 3.2 %collective-permute-start.9 = (bf16[96,384]{1,0:T(8,128)(2,1)S(1)}, bf16[96,384]{1,0:T(8,128)(2,1)S(1)}, u32[]{:S(2)}, u32[]{:S(2)}) collective-permute-start(bf16[96,384]{1,0:T(8,128)(2,1)S(1)} %get-tuple-element.32), channel_id=1, source_target_pairs={{0,10},{1,11},{2,8},{3,9},{4,14},{5,15},{6,12},{7,13},{8,2},{9,3},... | collective-permute-start | bytes 221192 | tf_op jit(solution)/shard_map/ppermute | solution.py:236
  37.9 3.9 %collective-permute-done.5.refs_6_ = bf16[96,384]{1,0:T(8,128)(2,1)S(1)} collective-permute-done((bf16[96,384]{1,0:T(8,128)(2,1)S(1)}, bf16[96,384]{1,0:T(8,128)(2,1)S(1)}, u32[]{:S(2)}, u32[]{:S(2)}) %collective-permute-start.5) | collective-permute-done | bytes 73760 | tf_op jit(solution)/shard_map/ppermute | solution.py:236
  41.8 0.0 collective-permute-start.10
  41.8 0.8 collective-permute-done.6.refs_7_
  42.6 0.0 collective-permute-start.11
  42.6 0.4 regroup_left.1.near
  43.0 10.1 %collective-permute-done.7.refs_0_ = bf16[96,384]{1,0:T(8,128)(2,1)S(1)} collective-permute-done((bf16[96,384]{1,0:T(8,128)(2,1)S(1)}, bf16[96,384]{1,0:T(8,128)(2,1)S(1)}, u32[]{:S(2)}, u32[]{:S(2)}) %collective-permute-start.7) | collective-permute-done | bytes 73760 | tf_op jit(solution)/shard_map/ppermute | solution.py:236
  53.1 1.9 %collective-permute-start.12 = (bf16[96,384]{1,0:T(8,128)(2,1)}, bf16[96,384]{1,0:T(8,128)(2,1)S(1)}, u32[]{:S(2)}, u32[]{:S(2)}) collective-permute-start(bf16[96,384]{1,0:T(8,128)(2,1)} %get-tuple-element.35), channel_id=1, source_target_pairs={{0,13},{1,12},{2,15},{3,14},{4,9},{5,8},{6,11},{7,10},{8,5},{9,4},... | collective-permute-start | bytes 221192 | tf_op jit(solution)/shard_map/ppermute | solution.py:236
  55.0 2.8 %collective-permute-start.13 = (bf16[96,384]{1,0:T(8,128)(2,1)}, bf16[96,384]{1,0:T(8,128)(2,1)S(1)}, u32[]{:S(2)}, u32[]{:S(2)}) collective-permute-start(bf16[96,384]{1,0:T(8,128)(2,1)} %get-tuple-element.36), channel_id=1, source_target_pairs={{0,14},{1,15},{2,12},{3,13},{4,10},{5,11},{6,8},{7,9},{8,6},{9,7},... | collective-permute-start | bytes 221192 | tf_op jit(solution)/shard_map/ppermute | solution.py:236
  57.8 0.0 collective-permute-done.9.refs_2_
  57.8 1.7 %collective-permute-start.14 = (bf16[96,384]{1,0:T(8,128)(2,1)}, bf16[96,384]{1,0:T(8,128)(2,1)S(1)}, u32[]{:S(2)}, u32[]{:S(2)}) collective-permute-start(bf16[96,384]{1,0:T(8,128)(2,1)} %get-tuple-element.37), channel_id=1, source_target_pairs={{0,15},{1,14},{2,13},{3,12},{4,11},{5,10},{6,9},{7,8},{8,7},{9,6},... | collective-permute-start | bytes 221192 | tf_op jit(solution)/shard_map/ppermute | solution.py:236
  59.5 6.9 %all-to-all-done = bf16[32,96,384]{2,1,0:T(8,128)(2,1)S(1)} async-done(((bf16[32,96,384]{2,1,0:T(8,128)(2,1)}), bf16[32,96,384]{2,1,0:T(8,128)(2,1)S(1)}, u32[]{:S(2)}, u32[]{:S(2)}) %all-to-all-start) | async-done | bytes 2359328 | tf_op jit(solution)/shard_map/all_to_all | solution.py:232
  66.4 1.0 %regroup_right.1.right = bf16[8,384,384]{2,1,0:T(8,128)(2,1)S(1)} custom-call(bf16[3072,384]{1,0:T(8,128)(2,1)S(1)} %bitcast.9), custom_call_target="tpu_custom_call" | custom-call | flops 137438953472 | bytes 4718592 | tf_op jit(solution)/shard_map/regroup_right/pallas_call | solution.py:302
  67.4 0.0 collective-permute-done.10.refs_3_
  67.4 0.0 collective-permute-done.11.refs_4_
  67.4 0.0 collective-permute-done.13.refs_6_
  67.4 0.0 collective-permute-done.14.refs_7_
  67.4 1.8 %products.1 = bf16[16,96,384]{2,1,0:T(8,128)(2,1)S(1)} custom-call(bf16[8,384,384]{2,1,0:T(8,128)(2,1)S(1)} %regroup_right.1.right, bf16[8,96,384]{2,1,0:T(8,128)(2,1)S(1)} %regroup_left.1.near, bf16[96,384]{1,0:T(8,128)(2,1)S(1)} %collective-permute-done.7.refs_0_, bf16[96,384]{1,0:T(8,128)(2,1)S(1)} %collective-permute-done.8.refs_1_, ...), custom_call_target="tpu_custom_call" | custom-call | flops 226492416 | bytes 3538944 | tf_op jit(solution)/shard_map/products/pallas_call | solution.py:310
  69.2 0.0 copy-start.2
  69.2 0.0 copy-start.4
  69.2 0.0 copy-start.10
  69.2 0.0 copy-start.11
  69.2 0.0 copy-start.12
  69.3 21.1 %all_to_all.10.x_ref = bf16[16,96,384]{2,1,0:T(8,128)(2,1)S(1)} all-to-all(bf16[16,96,384]{2,1,0:T(8,128)(2,1)S(1)} %products.1), channel_id=1, replica_groups=mesh['groups'=1,'part'=2,'chan'=8,'quarter'=2] {'chan','quarter'}, dimensions={0} | all-to-all | bytes 2359296 | tf_op jit(solution)/shard_map/all_to_all | solution.py:322
  90.4 2.1 %update.1 = bf16[12,384,128]{2,1,0:T(8,128)(2,1)} custom-call(bf16[16,96,384]{2,1,0:T(8,128)(2,1)S(1)} %all_to_all.10.x_ref, bf16[12,384,128]{2,1,0:T(8,128)(2,1)S(1)} %copy-done.2, f32[1,128]{1,0:T(1,128)S(1)} %bitcast.17, f32[1,128]{1,0:T(1,128)S(1)} %bitcast.18, bf16[128,128]{1,0:T(8,128)(2,1)S(1)} %copy-done.4, f32[1,128]{1,0:T(1,128)S(1)} %bitcast.19), custom_call_target="tpu_custom_call" | custom-call | flops 150994944 | bytes 3538944 | tf_op jit(solution)/shard_map/update/pallas_call | solution.py:324
  (17 shorter events, 0.0 us)
Async XLA Ops:
  4.5 7.3 %copy-start = (bf16[12,384,128]{2,1,0:T(8,128)(2,1)S(1)}, bf16[12,384,128]{2,1,0:T(8,128)(2,1)}, u32[]{:S(2)}) copy-start(bf16[12,384,128]{2,1,0:T(8,128)(2,1)} %pair_ref.3) | copy-start | bytes 3538948
  4.5 7.4 %copy-start.6 = (f32[512]{0:T(512)S(1)}, f32[512]{0:T(512)}, u32[]{:S(2)}) copy-start(f32[512]{0:T(512)} %param.15) | copy-start | bytes 6148
  4.5 7.4 %copy-start.7 = (f32[128]{0:T(128)S(1)}, f32[128]{0:T(128)}, u32[]{:S(2)}) copy-start(f32[128]{0:T(128)} %param.12) | copy-start | bytes 1540
  4.5 7.4 %copy-start.8 = (f32[128]{0:T(128)S(1)}, f32[128]{0:T(128)}, u32[]{:S(2)}) copy-start(f32[128]{0:T(128)} %param.13) | copy-start | bytes 1540
  4.5 7.4 %copy-start.9 = (f32[128]{0:T(128)S(1)}, f32[128]{0:T(128)}, u32[]{:S(2)}) copy-start(f32[128]{0:T(128)} %param.17) | copy-start | bytes 1540
  4.5 61.9 %all-to-all-start = ((bf16[32,96,384]{2,1,0:T(8,128)(2,1)}), bf16[32,96,384]{2,1,0:T(8,128)(2,1)S(1)}, u32[]{:S(2)}, u32[]{:S(2)}) async-start(bf16[32,96,384]{2,1,0:T(8,128)(2,1)} %bitcast.20), calls=%async_computation | async-start | bytes 4718592 | tf_op jit(solution)/shard_map/all_to_all | solution.py:232
  11.9 0.9 copy-start.3
  12.8 0.8 copy-start.5
  16.9 1.0 %copy-start.1 = (bf16[12,384,128]{2,1,0:T(8,128)(2,1)}, bf16[12,384,128]{2,1,0:T(8,128)(2,1)S(1)}, u32[]{:S(2)}) copy-start(bf16[12,384,128]{2,1,0:T(8,128)(2,1)S(1)} %get-tuple-element.38.gate_ref) | copy-start | bytes 3538948
  17.9 3.7 %collective-permute-start = (bf16[96,384]{1,0:T(8,128)(2,1)S(1)}, bf16[96,384]{1,0:T(8,128)(2,1)S(1)}, u32[]{:S(2)}, u32[]{:S(2)}) collective-permute-start(bf16[96,384]{1,0:T(8,128)(2,1)S(1)} %get-tuple-element.23), channel_id=1, source_target_pairs={{0,1},{1,0},{2,3},{3,2},{4,5},{5,4},{6,7},{7,6},{8,9},{9,8},{10,11... | collective-permute-start | bytes 221192 | tf_op jit(solution)/shard_map/ppermute | solution.py:236
  18.2 13.2 %collective-permute-start.1 = (bf16[96,384]{1,0:T(8,128)(2,1)S(1)}, bf16[96,384]{1,0:T(8,128)(2,1)S(1)}, u32[]{:S(2)}, u32[]{:S(2)}) collective-permute-start(bf16[96,384]{1,0:T(8,128)(2,1)S(1)} %get-tuple-element.24), channel_id=1, source_target_pairs={{0,2},{1,3},{2,0},{3,1},{4,6},{5,7},{6,4},{7,5},{8,10},{9,11},{10,... | collective-permute-start | bytes 221192 | tf_op jit(solution)/shard_map/ppermute | solution.py:236
  19.9 12.3 %collective-permute-start.2 = (bf16[96,384]{1,0:T(8,128)(2,1)S(1)}, bf16[96,384]{1,0:T(8,128)(2,1)S(1)}, u32[]{:S(2)}, u32[]{:S(2)}) collective-permute-start(bf16[96,384]{1,0:T(8,128)(2,1)S(1)} %get-tuple-element.25), channel_id=1, source_target_pairs={{0,3},{1,2},{2,1},{3,0},{4,7},{5,6},{6,5},{7,4},{8,11},{9,10},{10,... | collective-permute-start | bytes 221192 | tf_op jit(solution)/shard_map/ppermute | solution.py:236
  19.9 12.6 %collective-permute-start.3 = (bf16[96,384]{1,0:T(8,128)(2,1)S(1)}, bf16[96,384]{1,0:T(8,128)(2,1)S(1)}, u32[]{:S(2)}, u32[]{:S(2)}) collective-permute-start(bf16[96,384]{1,0:T(8,128)(2,1)S(1)} %get-tuple-element.26), channel_id=1, source_target_pairs={{0,4},{1,5},{2,6},{3,7},{4,0},{5,1},{6,2},{7,3},{8,12},{9,13},{10,... | collective-permute-start | bytes 221192 | tf_op jit(solution)/shard_map/ppermute | solution.py:236
  21.6 13.2 %collective-permute-start.4 = (bf16[96,384]{1,0:T(8,128)(2,1)S(1)}, bf16[96,384]{1,0:T(8,128)(2,1)S(1)}, u32[]{:S(2)}, u32[]{:S(2)}) collective-permute-start(bf16[96,384]{1,0:T(8,128)(2,1)S(1)} %get-tuple-element.27), channel_id=1, source_target_pairs={{0,5},{1,4},{2,7},{3,6},{4,1},{5,0},{6,3},{7,2},{8,13},{9,12},{10,... | collective-permute-start | bytes 221192 | tf_op jit(solution)/shard_map/ppermute | solution.py:236
  21.7 20.2 %collective-permute-start.5 = (bf16[96,384]{1,0:T(8,128)(2,1)S(1)}, bf16[96,384]{1,0:T(8,128)(2,1)S(1)}, u32[]{:S(2)}, u32[]{:S(2)}) collective-permute-start(bf16[96,384]{1,0:T(8,128)(2,1)S(1)} %get-tuple-element.28), channel_id=1, source_target_pairs={{0,6},{1,7},{2,4},{3,5},{4,2},{5,3},{6,0},{7,1},{8,14},{9,15},{10,... | collective-permute-start | bytes 221192 | tf_op jit(solution)/shard_map/ppermute | solution.py:236
  31.4 11.3 %collective-permute-start.6 = (bf16[96,384]{1,0:T(8,128)(2,1)S(1)}, bf16[96,384]{1,0:T(8,128)(2,1)S(1)}, u32[]{:S(2)}, u32[]{:S(2)}) collective-permute-start(bf16[96,384]{1,0:T(8,128)(2,1)S(1)} %get-tuple-element.29), channel_id=1, source_target_pairs={{0,7},{1,6},{2,5},{3,4},{4,3},{5,2},{6,1},{7,0},{8,15},{9,14},{10,... | collective-permute-start | bytes 221192 | tf_op jit(solution)/shard_map/ppermute | solution.py:236
  32.2 20.9 %collective-permute-start.7 = (bf16[96,384]{1,0:T(8,128)(2,1)S(1)}, bf16[96,384]{1,0:T(8,128)(2,1)S(1)}, u32[]{:S(2)}, u32[]{:S(2)}) collective-permute-start(bf16[96,384]{1,0:T(8,128)(2,1)S(1)} %get-tuple-element.30), channel_id=1, source_target_pairs={{0,8},{1,9},{2,10},{3,11},{4,12},{5,13},{6,14},{7,15},{8,0},{9,1},... | collective-permute-start | bytes 221192 | tf_op jit(solution)/shard_map/ppermute | solution.py:236
  32.5 22.6 %collective-permute-start.8 = (bf16[96,384]{1,0:T(8,128)(2,1)S(1)}, bf16[96,384]{1,0:T(8,128)(2,1)S(1)}, u32[]{:S(2)}, u32[]{:S(2)}) collective-permute-start(bf16[96,384]{1,0:T(8,128)(2,1)S(1)} %get-tuple-element.31), channel_id=1, source_target_pairs={{0,9},{1,8},{2,11},{3,10},{4,13},{5,12},{6,15},{7,14},{8,1},{9,0},... | collective-permute-start | bytes 221192 | tf_op jit(solution)/shard_map/ppermute | solution.py:236
  34.7 23.1 %collective-permute-start.9 = (bf16[96,384]{1,0:T(8,128)(2,1)S(1)}, bf16[96,384]{1,0:T(8,128)(2,1)S(1)}, u32[]{:S(2)}, u32[]{:S(2)}) collective-permute-start(bf16[96,384]{1,0:T(8,128)(2,1)S(1)} %get-tuple-element.32), channel_id=1, source_target_pairs={{0,10},{1,11},{2,8},{3,9},{4,14},{5,15},{6,12},{7,13},{8,2},{9,3},... | collective-permute-start | bytes 221192 | tf_op jit(solution)/shard_map/ppermute | solution.py:236
  41.8 25.5 %collective-permute-start.10 = (bf16[96,384]{1,0:T(8,128)(2,1)}, bf16[96,384]{1,0:T(8,128)(2,1)S(1)}, u32[]{:S(2)}, u32[]{:S(2)}) collective-permute-start(bf16[96,384]{1,0:T(8,128)(2,1)} %get-tuple-element.33), channel_id=1, source_target_pairs={{0,11},{1,10},{2,9},{3,8},{4,15},{5,14},{6,13},{7,12},{8,3},{9,2},... | collective-permute-start | bytes 221192 | tf_op jit(solution)/shard_map/ppermute | solution.py:236
  42.6 24.7 %collective-permute-start.11 = (bf16[96,384]{1,0:T(8,128)(2,1)}, bf16[96,384]{1,0:T(8,128)(2,1)S(1)}, u32[]{:S(2)}, u32[]{:S(2)}) collective-permute-start(bf16[96,384]{1,0:T(8,128)(2,1)} %get-tuple-element.34), channel_id=1, source_target_pairs={{0,12},{1,13},{2,14},{3,15},{4,8},{5,9},{6,10},{7,11},{8,4},{9,5},... | collective-permute-start | bytes 221192 | tf_op jit(solution)/shard_map/ppermute | solution.py:236
  53.1 14.3 %collective-permute-start.12 = (bf16[96,384]{1,0:T(8,128)(2,1)}, bf16[96,384]{1,0:T(8,128)(2,1)S(1)}, u32[]{:S(2)}, u32[]{:S(2)}) collective-permute-start(bf16[96,384]{1,0:T(8,128)(2,1)} %get-tuple-element.35), channel_id=1, source_target_pairs={{0,13},{1,12},{2,15},{3,14},{4,9},{5,8},{6,11},{7,10},{8,5},{9,4},... | collective-permute-start | bytes 221192 | tf_op jit(solution)/shard_map/ppermute | solution.py:236
  55.0 12.4 %collective-permute-start.13 = (bf16[96,384]{1,0:T(8,128)(2,1)}, bf16[96,384]{1,0:T(8,128)(2,1)S(1)}, u32[]{:S(2)}, u32[]{:S(2)}) collective-permute-start(bf16[96,384]{1,0:T(8,128)(2,1)} %get-tuple-element.36), channel_id=1, source_target_pairs={{0,14},{1,15},{2,12},{3,13},{4,10},{5,11},{6,8},{7,9},{8,6},{9,7},... | collective-permute-start | bytes 221192 | tf_op jit(solution)/shard_map/ppermute | solution.py:236
  57.8 9.6 %collective-permute-start.14 = (bf16[96,384]{1,0:T(8,128)(2,1)}, bf16[96,384]{1,0:T(8,128)(2,1)S(1)}, u32[]{:S(2)}, u32[]{:S(2)}) collective-permute-start(bf16[96,384]{1,0:T(8,128)(2,1)} %get-tuple-element.37), channel_id=1, source_target_pairs={{0,15},{1,14},{2,13},{3,12},{4,11},{5,10},{6,9},{7,8},{8,7},{9,6},... | collective-permute-start | bytes 221192 | tf_op jit(solution)/shard_map/ppermute | solution.py:236
  69.2 21.1 %copy-start.2 = (bf16[12,384,128]{2,1,0:T(8,128)(2,1)S(1)}, bf16[12,384,128]{2,1,0:T(8,128)(2,1)}, u32[]{:S(2)}) copy-start(bf16[12,384,128]{2,1,0:T(8,128)(2,1)} %copy-done.1) | copy-start | bytes 3538948
  69.2 21.1 %copy-start.4 = (bf16[128,128]{1,0:T(8,128)(2,1)S(1)}, bf16[128,128]{1,0:T(8,128)(2,1)}, u32[]{:S(2)}) copy-start(bf16[128,128]{1,0:T(8,128)(2,1)} %w_ref.5) | copy-start | bytes 98308
  69.2 21.1 %copy-start.10 = (f32[128]{0:T(128)S(1)}, f32[128]{0:T(128)}, u32[]{:S(2)}) copy-start(f32[128]{0:T(128)} %param.18) | copy-start | bytes 1540
  69.2 21.1 %copy-start.11 = (f32[128]{0:T(128)S(1)}, f32[128]{0:T(128)}, u32[]{:S(2)}) copy-start(f32[128]{0:T(128)} %param.19) | copy-start | bytes 1540
  69.2 21.1 %copy-start.12 = (f32[128]{0:T(128)S(1)}, f32[128]{0:T(128)}, u32[]{:S(2)}) copy-start(f32[128]{0:T(128)} %param.21) | copy-start | bytes 1540
